TPU v7x, 32 devices: a whole 2x2x4 slice. The times are simulated.
32 devices in a mesh: tm: 8 (over z, x), dp: 4 (over y, core).
Axes of the slice: x: 2, y: 2, z: 4, core: 2. Of those that a mesh axis runs over, the one named last changes fastest.
Arguments:
- inputs: bfloat16 [4, 4096, 256], P('dp', 'tm'), may hold values from -6 to 6
- grad_stream_out: bfloat16 [4, 4096, 256], P('dp', 'tm'), may hold values from -6 to 6
- grad_skip_out: bfloat16 [4, 4096, 256], P('dp', 'tm'), may hold values from -6 to 6
- sample_weight: float32 [4, 4096], P('dp', 'tm'), may hold values from 0.5 to 6, as said below
- conv_weight: bfloat16 [6, 512, 512], replicated, may hold values from -0.25 to 0.25
- out_weight: bfloat16 [6, 256, 512], replicated, may hold values from -0.375 to 0.375
Outputs:
- grad_inputs: float32 [4, 4096, 256], P('dp', 'tm')
- grad_conv: float32 [6, 512, 512], P(None, 'tm', 'dp')
- grad_out: float32 [6, 256, 512], P(None, 'tm', 'dp')
Inputs may be any that keep to these rules, and one draw needn't show every extreme that they name: `sample_weight`: positive loss weights of each sample.
All inputs are finite; a program needn't handle non-finite values.
Results may differ from a plain program's by a relative error of at most 0.02.
Values may be sent and summed in bfloat16 or wider, within the bound.
No kernel may reach another device: no remote copies, remote signals or barrier semaphores. Data moves between devices by JAX's collectives and lax.ppermute only.
A program may use at most 128 MiB of HBM per device.

v0:
```python
import jax
import jax.numpy as jnp
from jax import lax
from jax.sharding import PartitionSpec as P


def shifted(x, axis, by):
    count = lax.axis_size(axis)
    pairs = [(i, i + by) for i in range(count) if 0 <= i + by < count]
    return lax.ppermute(x, axis, pairs)


def project(operand, matrix):
    return jnp.einsum("btc,cd->btd", operand, matrix, preferred_element_type=jnp.float32)


def project_back(operand, matrix):
    return jnp.einsum("btd,cd->btc", operand, matrix, preferred_element_type=jnp.float32)


def outer_sum(left_op, right_op):
    return jnp.einsum("btc,btd->cd", left_op, right_op, preferred_element_type=jnp.float32)


def gated_layer(present, earlier, conv_layer, out_layer, channels):
    preact = project(present, conv_layer[:channels]) + project(earlier, conv_layer[channels:])
    gated = (jnp.tanh(preact[..., :channels]) * jax.nn.sigmoid(preact[..., channels:])).astype(
        jnp.bfloat16
    )
    projected = project(gated, out_layer)
    return (preact, gated, projected)


def body(inputs, grad_stream_out, grad_skip_out, sample_weight, conv_weight, out_weight):
    channels = inputs.shape[2]
    length = inputs.shape[1]
    layers = conv_weight.shape[0]
    weight_sum = lax.psum(jnp.sum(sample_weight), ("tm", "dp"))
    samples_all = sample_weight.size * lax.axis_size("tm") * lax.axis_size("dp")
    weighting = sample_weight * (samples_all / weight_sum)
    stored = []
    stream = inputs.astype(jnp.float32)
    for layer_index in range(layers):
        dilation = 2**layer_index
        present = stream.astype(jnp.bfloat16)
        border = shifted(present[:, length - dilation :], "tm", 1)
        earlier = jnp.concatenate([border, present[:, : length - dilation]], axis=1)
        preact, gated, projected = gated_layer(
            present, earlier, conv_weight[layer_index], out_weight[layer_index], channels
        )
        stream = stream + projected[..., :channels]
        stored.append((present, earlier, preact, gated))
    grad_stream = grad_stream_out.astype(jnp.float32) * weighting[..., None]
    grad_skips = grad_skip_out.astype(jnp.float32) * weighting[..., None]
    conv_grads = [None] * layers
    out_grads = [None] * layers
    for layer_index in reversed(range(layers)):
        dilation = 2**layer_index
        present, earlier, preact, gated = stored[layer_index]
        grad_proj = jnp.concatenate([grad_stream, grad_skips], axis=-1).astype(jnp.bfloat16)
        out_grads[layer_index] = outer_sum(gated, grad_proj)
        grad_gated = project_back(grad_proj, out_weight[layer_index])
        filtered = jnp.tanh(preact[..., :channels])
        opening = jax.nn.sigmoid(preact[..., channels:])
        grad_preact = jnp.concatenate(
            [
                grad_gated * opening * (1.0 - filtered * filtered),
                grad_gated * filtered * opening * (1.0 - opening),
            ],
            axis=-1,
        ).astype(jnp.bfloat16)
        conv_grads[layer_index] = jnp.concatenate(
            [outer_sum(present, grad_preact), outer_sum(earlier, grad_preact)], axis=0
        )
        incoming = shifted(grad_preact[:, :dilation], "tm", -1)
        later_rows = jnp.concatenate([grad_preact[:, dilation:], incoming], axis=1)
        grad_stream = (
            grad_stream
            + project_back(grad_preact, conv_weight[layer_index, :channels])
            + project_back(later_rows, conv_weight[layer_index, channels:])
        )
    conv_all = jnp.stack(conv_grads)
    out_all = jnp.stack(out_grads)
    partial_grads = (
        lax.psum_scatter(
            conv_all.astype(jnp.bfloat16), "dp", scatter_dimension=2, tiled=True
        ).astype(jnp.float32),
        lax.psum_scatter(
            out_all.astype(jnp.bfloat16), "dp", scatter_dimension=2, tiled=True
        ).astype(jnp.float32),
    )
    summed = (
        lax.psum_scatter(partial_grads[0], "tm", scatter_dimension=1, tiled=True),
        lax.psum_scatter(partial_grads[1], "tm", scatter_dimension=1, tiled=True),
    )
    return (grad_stream, summed[0], summed[1])


def solution(mesh):
    placed = (
        P("dp", "tm", None),
        P("dp", "tm", None),
        P("dp", "tm", None),
        P("dp", "tm"),
        P(),
        P(),
    )
    return jax.shard_map(
        body,
        mesh=mesh,
        in_specs=placed,
        out_specs=(P("dp", "tm", None), P(None, "tm", "dp"), P(None, "tm", "dp")),
        check_vma=False,
    )
```

profile of v0, /device:TPU:0, one launch (start us, length us, event | category | flops | bytes accessed | tf_op | source)
XLA Modules:
  0.0 369.2 jit_solution(12791991202593908510)
XLA Ops:
  7.2 0.8 slice.263
  8.1 1.4 reduce_sum.9
  9.5 4.8 %collective-permute-start = (bf16[1,1,256]{2,1,0:T(2,128)(2,1)S(1)}, bf16[1,1,256]{2,1,0:T(2,128)(2,1)S(1)}, u32[]{:S(2)}, u32[]{:S(2)}) collective-permute-start(bf16[1,1,256]{2,1,0:T(2,128)(2,1)S(1)} %slice.263), channel_id=1, source_target_pairs={{0,4},{4,8},{8,12},{12,16},{16,20},{20,24},{24,28},{1,5},{5,9},{9,... | collective-permute-start | bytes 1544 | tf_op jit(solution)/shard_map/ppermute | solution.py:10
  14.3 40.8 %psum.7 = f32[]{:T(128)} all-reduce(f32[]{:T(128)} %reduce_sum.9), channel_id=1, replica_groups=mesh['tm'=8,'dp'=4] {'tm','dp'}, use_global_device_ids=true, to_apply=%region_1.0 | all-reduce | flops 1 | bytes 8 | tf_op jit(solution)/shard_map/psum | solution.py:38
  56.5 1.8 copy.14
  58.3 1.8 copy.15
  60.1 1.5 fusion.127
  61.6 1.1 fusion.70
  63.8 4.2 %collective-permute-start.1 = (bf16[1,2,256]{2,1,0:T(2,128)(2,1)S(1)}, bf16[1,2,256]{2,1,0:T(2,128)(2,1)S(1)}, u32[]{:S(2)}, u32[]{:S(2)}) collective-permute-start(bf16[1,2,256]{2,1,0:T(2,128)(2,1)S(1)} %slice.334), channel_id=1, source_target_pairs={{0,4},{4,8},{8,12},{12,16},{16,20},{20,24},{24,28},{1,5},{5,9},{9,... | collective-permute-start | bytes 3080 | tf_op jit(solution)/shard_map/ppermute | solution.py:10
  68.3 0.9 collective-permute-done.1
  70.4 4.2 %collective-permute-start.2 = (bf16[1,4,256]{2,1,0:T(4,128)(2,1)S(1)}, bf16[1,4,256]{2,1,0:T(4,128)(2,1)S(1)}, u32[]{:S(2)}, u32[]{:S(2)}) collective-permute-start(bf16[1,4,256]{2,1,0:T(4,128)(2,1)S(1)} %slice.339), channel_id=1, source_target_pairs={{0,4},{4,8},{8,12},{12,16},{16,20},{20,24},{24,28},{1,5},{5,9},{9,... | collective-permute-start | bytes 6152 | tf_op jit(solution)/shard_map/ppermute | solution.py:10
  74.9 1.0 collective-permute-done.2
  76.9 4.2 %collective-permute-start.3 = (bf16[1,8,256]{2,1,0:T(8,128)(2,1)S(1)}, bf16[1,8,256]{2,1,0:T(8,128)(2,1)S(1)}, u32[]{:S(2)}, u32[]{:S(2)}) collective-permute-start(bf16[1,8,256]{2,1,0:T(8,128)(2,1)S(1)} %slice.344), channel_id=1, source_target_pairs={{0,4},{4,8},{8,12},{12,16},{16,20},{20,24},{24,28},{1,5},{5,9},{9,... | collective-permute-start | bytes 12296 | tf_op jit(solution)/shard_map/ppermute | solution.py:10
  81.5 0.9 collective-permute-done.3
  83.5 4.2 %collective-permute-start.4 = (bf16[1,16,256]{2,1,0:T(8,128)(2,1)S(1)}, bf16[1,16,256]{2,1,0:T(8,128)(2,1)S(1)}, u32[]{:S(2)}, u32[]{:S(2)}) collective-permute-start(bf16[1,16,256]{2,1,0:T(8,128)(2,1)S(1)} %slice.349), channel_id=1, source_target_pairs={{0,4},{4,8},{8,12},{12,16},{16,20},{20,24},{24,28},{1,5},{5,9},{9,... | collective-permute-start | bytes 24584 | tf_op jit(solution)/shard_map/ppermute | solution.py:10
  88.1 1.0 collective-permute-done.4
  90.2 4.6 %collective-permute-start.5 = (bf16[1,32,256]{2,1,0:T(8,128)(2,1)S(1)}, bf16[1,32,256]{2,1,0:T(8,128)(2,1)S(1)}, u32[]{:S(2)}, u32[]{:S(2)}) collective-permute-start(bf16[1,32,256]{2,1,0:T(8,128)(2,1)S(1)} %slice.354), channel_id=1, source_target_pairs={{0,4},{4,8},{8,12},{12,16},{16,20},{20,24},{24,28},{1,5},{5,9},{9,... | collective-permute-start | bytes 49160 | tf_op jit(solution)/shard_map/ppermute | solution.py:10
  95.2 1.0 collective-permute-done.5
  97.2 1.3 collective-permute-start.6
  99.1 7.0 %collective-permute-done.6 = bf16[1,32,512]{1,2,0:T(8,128)(2,1)S(1)} collective-permute-done((bf16[1,32,512]{1,2,0:T(8,128)(2,1)S(1)}, bf16[1,32,512]{1,2,0:T(8,128)(2,1)S(1)}, u32[]{:S(2)}, u32[]{:S(2)}) %collective-permute-start.6) | collective-permute-done | bytes 32800 | tf_op jit(solution)/shard_map/ppermute | solution.py:10
  107.0 1.3 collective-permute-start.7
  108.9 7.4 %collective-permute-done.7 = bf16[1,16,512]{1,2,0:T(8,128)(2,1)S(1)} collective-permute-done((bf16[1,16,512]{1,2,0:T(8,128)(2,1)S(1)}, bf16[1,16,512]{1,2,0:T(8,128)(2,1)S(1)}, u32[]{:S(2)}, u32[]{:S(2)}) %collective-permute-start.7) | collective-permute-done | bytes 16416 | tf_op jit(solution)/shard_map/ppermute | solution.py:10
  117.3 1.5 collective-permute-start.8
  119.3 5.4 %collective-permute-done.8 = bf16[1,8,512]{1,2,0:T(8,128)(2,1)S(1)} collective-permute-done((bf16[1,8,512]{1,2,0:T(8,128)(2,1)S(1)}, bf16[1,8,512]{1,2,0:T(8,128)(2,1)S(1)}, u32[]{:S(2)}, u32[]{:S(2)}) %collective-permute-start.8) | collective-permute-done | bytes 8224 | tf_op jit(solution)/shard_map/ppermute | solution.py:10
  125.7 1.3 collective-permute-start.9
  127.6 5.9 %collective-permute-done.9 = bf16[1,4,512]{1,2,0:T(8,128)(2,1)S(1)} collective-permute-done((bf16[1,4,512]{1,2,0:T(8,128)(2,1)S(1)}, bf16[1,4,512]{1,2,0:T(8,128)(2,1)S(1)}, u32[]{:S(2)}, u32[]{:S(2)}) %collective-permute-start.9) | collective-permute-done | bytes 4128 | tf_op jit(solution)/shard_map/ppermute | solution.py:10
  134.4 1.3 collective-permute-start.10
  136.3 5.9 %collective-permute-done.10 = bf16[1,2,512]{1,2,0:T(8,128)(2,1)S(1)} collective-permute-done((bf16[1,2,512]{1,2,0:T(8,128)(2,1)S(1)}, bf16[1,2,512]{1,2,0:T(8,128)(2,1)S(1)}, u32[]{:S(2)}, u32[]{:S(2)}) %collective-permute-start.10) | collective-permute-done | bytes 2080 | tf_op jit(solution)/shard_map/ppermute | solution.py:10
  142.6 1.1 fusion.20
  143.7 1.0 fusion.22
  144.7 1.1 fusion.24
  145.8 1.0 fusion.26
  146.8 1.0 fusion.28
  147.9 1.1 fusion.30
  148.9 4.4 %copy.23 = bf16[6,256,512]{1,0,2:T(8,128)(2,1)} copy(bf16[6,256,512]{2,1,0:T(8,128)(2,1)} %fusion.30) | data formatting | bytes 3145728
  153.3 3.2 copy.26
  156.7 1.6 convolution_convert_fusion.6
  158.3 1.5 convolution_convert_fusion.7
  159.8 1.6 convolution_convert_fusion.8
  164.1 1.4 multiply_convert_fusion.2
  166.3 0.8 fusion.62
  167.1 0.9 fusion.63
  168.0 0.8 fusion.64
  168.8 0.8 fusion.65
  170.5 0.8 fusion.67
  171.3 7.9 %copy.21 = bf16[6,512,512]{1,0,2:T(8,128)(2,1)} copy(bf16[6,512,512]{2,1,0:T(8,128)(2,1)} %fusion.67) | data formatting | bytes 6291456
  179.2 5.5 %copy.25 = bf16[64,8,6,512]{3,1,2,0:T(8,128)(2,1)} copy(bf16[64,8,6,512]{3,2,1,0:T(8,128)(2,1)} %bitcast.365) | data formatting | bytes 6291456
  185.1 1.0 reduce-scatter.15.cloned.1.call-done
  186.1 2.2 reshape.521
  188.3 1.4 copy.24
  189.7 0.9 convert_element_type.168
  190.7 36.0 %reduce-scatter.13.cloned.1.call-done = bf16[128,3072]{1,0:T(8,128)(2,1)} async-done(((bf16[512,3072]{1,0:T(8,128)(2,1)}), bf16[128,3072]{1,0:T(8,128)(2,1)}) %reduce-scatter.13.cloned.1.call-update) | async-done | bytes 786448
  226.8 2.8 reshape.519
  229.5 2.5 copy.22
  232.0 2.4 convert_element_type.166
  234.5 0.9 pad_maximum_fusion.42
  235.3 1.3 collective-permute-start.11
  236.6 1.4 fusion.16
  238.0 1.2 slice_maximum_fusion
  239.3 4.2 %collective-permute-done.11 = bf16[1,1,512]{1,2,0:T(8,128)(2,1)S(1)} collective-permute-done((bf16[1,1,512]{1,2,0:T(8,128)(2,1)S(1)}, bf16[1,1,512]{1,2,0:T(8,128)(2,1)S(1)}, u32[]{:S(2)}, u32[]{:S(2)}) %collective-permute-start.11) | collective-permute-done | bytes 1056 | tf_op jit(solution)/shard_map/ppermute | solution.py:10
  243.5 1.2 fusion.17
  244.7 2.0 copy.18
  246.7 47.2 %reduce-scatter.11.cloned.1.call-done = f32[6,32,128]{2,1,0:T(8,128)} async-done(((f32[6,256,128]{2,1,0:T(8,128)}), f32[6,32,128]{2,1,0:T(8,128)}) %reduce-scatter.11.cloned.1.call-update) | async-done | bytes 98320 | tf_op jit(solution)/shard_map/reduce_scatter | solution.py:94
  293.9 68.7 %reduce-scatter.9.cloned.1.call-done = f32[6,64,128]{2,1,0:T(8,128)} async-done(((f32[6,512,128]{2,1,0:T(8,128)}), f32[6,64,128]{2,1,0:T(8,128)}) %reduce-scatter.9.cloned.1.call-update) | async-done | bytes 196624 | tf_op jit(solution)/shard_map/reduce_scatter | solution.py:93
  (174 shorter events, 19.7 us)
Async XLA Ops:
  7.2 55.6 %copy-start.2 = (bf16[1,512,256]{2,1,0:T(8,128)(2,1)S(1)}, bf16[1,512,256]{2,1,0:T(8,128)(2,1)}, u32[]{:S(2)}) copy-start(bf16[1,512,256]{2,1,0:T(8,128)(2,1)} %param.6) | copy-start | bytes 786436
  7.2 55.6 %copy-start = (bf16[6,512,512]{2,1,0:T(8,128)(2,1)S(1)}, bf16[6,512,512]{2,1,0:T(8,128)(2,1)}, u32[]{:S(2)}) copy-start(bf16[6,512,512]{2,1,0:T(8,128)(2,1)} %param.10) | copy-start | bytes 9437188
  7.2 178.9 %reduce-scatter.15.cloned.1.call-start = ((), (), s32[]{:S(2)}) async-start(), calls=%async_computation.7 | async-start | bytes 1966080
  9.5 53.2 %collective-permute-start = (bf16[1,1,256]{2,1,0:T(2,128)(2,1)S(1)}, bf16[1,1,256]{2,1,0:T(2,128)(2,1)S(1)}, u32[]{:S(2)}, u32[]{:S(2)}) collective-permute-start(bf16[1,1,256]{2,1,0:T(2,128)(2,1)S(1)} %slice.263), channel_id=1, source_target_pairs={{0,4},{4,8},{8,12},{12,16},{16,20},{20,24},{24,28},{1,5},{5,9},{9,... | collective-permute-start | bytes 1544 | tf_op jit(solution)/shard_map/ppermute | solution.py:10
  60.1 3.2 copy-start.33
  62.7 85.1 %copy-start.43 = (bf16[512,256]{0,1:T(8,128)(2,1)}, bf16[512,256]{0,1:T(8,128)(2,1)S(1)}, u32[]{:S(2)}) copy-start(bf16[512,256]{0,1:T(8,128)(2,1)S(1)} %get-tuple-element.24) | copy-start | bytes 786436
  63.1 6.5 %copy-start.3 = (f32[1,512,512]{1,2,0:T(8,128)}, f32[1,512,512]{1,2,0:T(8,128)S(1)}, u32[]{:S(2)}) copy-start(f32[1,512,512]{1,2,0:T(8,128)S(1)} %fusion.5) | copy-start | bytes 3145732
  63.8 6.4 %copy-start.7 = (bf16[1,512,256]{2,1,0:T(8,128)(2,1)}, bf16[1,512,256]{2,1,0:T(8,128)(2,1)S(1)}, u32[]{:S(2)}) copy-start(bf16[1,512,256]{2,1,0:T(8,128)(2,1)S(1)} %fusion.69) | copy-start | bytes 786436
  63.8 5.5 %collective-permute-start.1 = (bf16[1,2,256]{2,1,0:T(2,128)(2,1)S(1)}, bf16[1,2,256]{2,1,0:T(2,128)(2,1)S(1)}, u32[]{:S(2)}, u32[]{:S(2)}) collective-permute-start(bf16[1,2,256]{2,1,0:T(2,128)(2,1)S(1)} %slice.334), channel_id=1, source_target_pairs={{0,4},{4,8},{8,12},{12,16},{16,20},{20,24},{24,28},{1,5},{5,9},{9,... | collective-permute-start | bytes 3080 | tf_op jit(solution)/shard_map/ppermute | solution.py:10
  70.4 6.4 %copy-start.5 = (bf16[1,512,256]{2,1,0:T(8,128)(2,1)}, bf16[1,512,256]{2,1,0:T(8,128)(2,1)S(1)}, u32[]{:S(2)}) copy-start(bf16[1,512,256]{2,1,0:T(8,128)(2,1)S(1)} %get-tuple-element.9) | copy-start | bytes 786436
  70.4 5.5 %collective-permute-start.2 = (bf16[1,4,256]{2,1,0:T(4,128)(2,1)S(1)}, bf16[1,4,256]{2,1,0:T(4,128)(2,1)S(1)}, u32[]{:S(2)}, u32[]{:S(2)}) collective-permute-start(bf16[1,4,256]{2,1,0:T(4,128)(2,1)S(1)} %slice.339), channel_id=1, source_target_pairs={{0,4},{4,8},{8,12},{12,16},{16,20},{20,24},{24,28},{1,5},{5,9},{9,... | collective-permute-start | bytes 6152 | tf_op jit(solution)/shard_map/ppermute | solution.py:10
  76.9 6.1 %copy-start.31 = (bf16[1,512,256]{2,1,0:T(8,128)(2,1)}, bf16[1,512,256]{2,1,0:T(8,128)(2,1)S(1)}, u32[]{:S(2)}) copy-start(bf16[1,512,256]{2,1,0:T(8,128)(2,1)S(1)} %fusion.167) | copy-start | bytes 786436
  76.9 5.5 %collective-permute-start.3 = (bf16[1,8,256]{2,1,0:T(8,128)(2,1)S(1)}, bf16[1,8,256]{2,1,0:T(8,128)(2,1)S(1)}, u32[]{:S(2)}, u32[]{:S(2)}) collective-permute-start(bf16[1,8,256]{2,1,0:T(8,128)(2,1)S(1)} %slice.344), channel_id=1, source_target_pairs={{0,4},{4,8},{8,12},{12,16},{16,20},{20,24},{24,28},{1,5},{5,9},{9,... | collective-permute-start | bytes 12296 | tf_op jit(solution)/shard_map/ppermute | solution.py:10
  81.5 2.0 copy-start.37
  83.5 5.9 %copy-start.9 = (bf16[1,512,256]{2,1,0:T(8,128)(2,1)}, bf16[1,512,256]{2,1,0:T(8,128)(2,1)S(1)}, u32[]{:S(2)}) copy-start(bf16[1,512,256]{2,1,0:T(8,128)(2,1)S(1)} %fusion.210) | copy-start | bytes 786436
  83.5 5.5 %collective-permute-start.4 = (bf16[1,16,256]{2,1,0:T(8,128)(2,1)S(1)}, bf16[1,16,256]{2,1,0:T(8,128)(2,1)S(1)}, u32[]{:S(2)}, u32[]{:S(2)}) collective-permute-start(bf16[1,16,256]{2,1,0:T(8,128)(2,1)S(1)} %slice.349), channel_id=1, source_target_pairs={{0,4},{4,8},{8,12},{12,16},{16,20},{20,24},{24,28},{1,5},{5,9},{9,... | collective-permute-start | bytes 24584 | tf_op jit(solution)/shard_map/ppermute | solution.py:10
  88.1 1.6 copy-start.39
  90.2 6.9 %copy-start.11 = (bf16[1,512,256]{2,1,0:T(8,128)(2,1)}, bf16[1,512,256]{2,1,0:T(8,128)(2,1)S(1)}, u32[]{:S(2)}) copy-start(bf16[1,512,256]{2,1,0:T(8,128)(2,1)S(1)} %fusion.34) | copy-start | bytes 786436
  90.2 6.0 %collective-permute-start.5 = (bf16[1,32,256]{2,1,0:T(8,128)(2,1)S(1)}, bf16[1,32,256]{2,1,0:T(8,128)(2,1)S(1)}, u32[]{:S(2)}, u32[]{:S(2)}) collective-permute-start(bf16[1,32,256]{2,1,0:T(8,128)(2,1)S(1)} %slice.354), channel_id=1, source_target_pairs={{0,4},{4,8},{8,12},{12,16},{16,20},{20,24},{24,28},{1,5},{5,9},{9,... | collective-permute-start | bytes 49160 | tf_op jit(solution)/shard_map/ppermute | solution.py:10
  95.2 1.9 copy-start.40
  96.6 1.9 copy-start.36
  97.1 1.9 copy-start.34
  97.1 1.9 copy-start.35
  97.2 8.9 %collective-permute-start.6 = (bf16[1,32,512]{1,2,0:T(8,128)(2,1)S(1)}, bf16[1,32,512]{1,2,0:T(8,128)(2,1)S(1)}, u32[]{:S(2)}, u32[]{:S(2)}) collective-permute-start(bf16[1,32,512]{1,2,0:T(8,128)(2,1)S(1)} %pad_maximum_fusion.47), channel_id=1, source_target_pairs={{4,0},{8,4},{12,8},{16,12},{20,16},{24,20},{28,24},{5,1},{9,5},{13... | collective-permute-start | bytes 98312 | tf_op jit(solution)/shard_map/ppermute | solution.py:10
  107.0 9.7 %copy-start.12 = (bf16[1,512,256]{1,2,0:T(8,128)(2,1)}, bf16[1,512,256]{1,2,0:T(8,128)(2,1)S(1)}, u32[]{:S(2)}) copy-start(bf16[1,512,256]{1,2,0:T(8,128)(2,1)S(1)} %get-tuple-element.19) | copy-start | bytes 786436
  107.0 9.7 %copy-start.14 = (bf16[1,512,256]{1,2,0:T(8,128)(2,1)}, bf16[1,512,256]{1,2,0:T(8,128)(2,1)S(1)}, u32[]{:S(2)}) copy-start(bf16[1,512,256]{1,2,0:T(8,128)(2,1)S(1)} %get-tuple-element.20) | copy-start | bytes 786436
  107.0 9.3 %collective-permute-start.7 = (bf16[1,16,512]{1,2,0:T(8,128)(2,1)S(1)}, bf16[1,16,512]{1,2,0:T(8,128)(2,1)S(1)}, u32[]{:S(2)}, u32[]{:S(2)}) collective-permute-start(bf16[1,16,512]{1,2,0:T(8,128)(2,1)S(1)} %pad_maximum_fusion.46), channel_id=1, source_target_pairs={{4,0},{8,4},{12,8},{16,12},{20,16},{24,20},{28,24},{5,1},{9,5},{13... | collective-permute-start | bytes 49160 | tf_op jit(solution)/shard_map/ppermute | solution.py:10
  117.2 7.9 %copy-start.16 = (bf16[1,512,256]{1,2,0:T(8,128)(2,1)}, bf16[1,512,256]{1,2,0:T(8,128)(2,1)S(1)}, u32[]{:S(2)}) copy-start(bf16[1,512,256]{1,2,0:T(8,128)(2,1)S(1)} %get-tuple-element.17) | copy-start | bytes 786436
  117.2 7.9 %copy-start.18 = (bf16[1,512,256]{1,2,0:T(8,128)(2,1)}, bf16[1,512,256]{1,2,0:T(8,128)(2,1)S(1)}, u32[]{:S(2)}) copy-start(bf16[1,512,256]{1,2,0:T(8,128)(2,1)S(1)} %get-tuple-element.18) | copy-start | bytes 786436
  117.3 7.5 %collective-permute-start.8 = (bf16[1,8,512]{1,2,0:T(8,128)(2,1)S(1)}, bf16[1,8,512]{1,2,0:T(8,128)(2,1)S(1)}, u32[]{:S(2)}, u32[]{:S(2)}) collective-permute-start(bf16[1,8,512]{1,2,0:T(8,128)(2,1)S(1)} %pad_maximum_fusion.45), channel_id=1, source_target_pairs={{4,0},{8,4},{12,8},{16,12},{20,16},{24,20},{28,24},{5,1},{9,5},{13... | collective-permute-start | bytes 24584 | tf_op jit(solution)/shard_map/ppermute | solution.py:10
  125.7 8.2 %copy-start.20 = (bf16[1,512,256]{1,2,0:T(8,128)(2,1)}, bf16[1,512,256]{1,2,0:T(8,128)(2,1)S(1)}, u32[]{:S(2)}) copy-start(bf16[1,512,256]{1,2,0:T(8,128)(2,1)S(1)} %get-tuple-element.15) | copy-start | bytes 786436
  125.7 8.2 %copy-start.22 = (bf16[1,512,256]{1,2,0:T(8,128)(2,1)}, bf16[1,512,256]{1,2,0:T(8,128)(2,1)S(1)}, u32[]{:S(2)}) copy-start(bf16[1,512,256]{1,2,0:T(8,128)(2,1)S(1)} %get-tuple-element.16) | copy-start | bytes 786436
  125.7 7.8 %collective-permute-start.9 = (bf16[1,4,512]{1,2,0:T(8,128)(2,1)S(1)}, bf16[1,4,512]{1,2,0:T(8,128)(2,1)S(1)}, u32[]{:S(2)}, u32[]{:S(2)}) collective-permute-start(bf16[1,4,512]{1,2,0:T(8,128)(2,1)S(1)} %pad_maximum_fusion.44), channel_id=1, source_target_pairs={{4,0},{8,4},{12,8},{16,12},{20,16},{24,20},{28,24},{5,1},{9,5},{13... | collective-permute-start | bytes 12296 | tf_op jit(solution)/shard_map/ppermute | solution.py:10
  134.4 8.2 %copy-start.27 = (bf16[1,512,256]{1,2,0:T(8,128)(2,1)}, bf16[1,512,256]{1,2,0:T(8,128)(2,1)S(1)}, u32[]{:S(2)}) copy-start(bf16[1,512,256]{1,2,0:T(8,128)(2,1)S(1)} %get-tuple-element.13) | copy-start | bytes 786436
  134.4 8.2 %copy-start.29 = (bf16[1,512,256]{1,2,0:T(8,128)(2,1)}, bf16[1,512,256]{1,2,0:T(8,128)(2,1)S(1)}, u32[]{:S(2)}) copy-start(bf16[1,512,256]{1,2,0:T(8,128)(2,1)S(1)} %get-tuple-element.14) | copy-start | bytes 786436
  134.4 7.8 %collective-permute-start.10 = (bf16[1,2,512]{1,2,0:T(8,128)(2,1)S(1)}, bf16[1,2,512]{1,2,0:T(8,128)(2,1)S(1)}, u32[]{:S(2)}, u32[]{:S(2)}) collective-permute-start(bf16[1,2,512]{1,2,0:T(8,128)(2,1)S(1)} %pad_maximum_fusion.43), channel_id=1, source_target_pairs={{4,0},{8,4},{12,8},{16,12},{20,16},{24,20},{28,24},{5,1},{9,5},{13... | collective-permute-start | bytes 6152 | tf_op jit(solution)/shard_map/ppermute | solution.py:10
  142.5 4.3 %copy-start.1 = (f32[1,512,256]{1,2,0:T(8,128)}, f32[1,512,256]{1,2,0:T(8,128)S(1)}, u32[]{:S(2)}) copy-start(f32[1,512,256]{1,2,0:T(8,128)S(1)} %fusion.15) | copy-start | bytes 1572868
  142.6 5.2 %copy-start.41 = (bf16[512,256]{0,1:T(8,128)(2,1)}, bf16[512,256]{0,1:T(8,128)(2,1)S(1)}, u32[]{:S(2)}) copy-start(bf16[512,256]{0,1:T(8,128)(2,1)S(1)} %convert_bitcast_fusion) | copy-start | bytes 786436
  156.6 70.2 %reduce-scatter.13.cloned.1.call-start = ((), (), s32[]{:S(2)}) async-start(), calls=%async_computation.6 | async-start | bytes 3932160
  156.6 4.8 %copy-start.10 = (bf16[1,512,256]{2,1,0:T(8,128)(2,1)S(1)}, bf16[1,512,256]{2,1,0:T(8,128)(2,1)}, u32[]{:S(2)}) copy-start(bf16[1,512,256]{2,1,0:T(8,128)(2,1)} %copy-done.9) | copy-start | bytes 786436
  156.6 4.8 %copy-start.13 = (bf16[1,512,256]{1,2,0:T(8,128)(2,1)S(1)}, bf16[1,512,256]{1,2,0:T(8,128)(2,1)}, u32[]{:S(2)}) copy-start(bf16[1,512,256]{1,2,0:T(8,128)(2,1)} %copy-done.12) | copy-start | bytes 786436
  156.6 4.8 %copy-start.15 = (bf16[1,512,256]{1,2,0:T(8,128)(2,1)S(1)}, bf16[1,512,256]{1,2,0:T(8,128)(2,1)}, u32[]{:S(2)}) copy-start(bf16[1,512,256]{1,2,0:T(8,128)(2,1)} %copy-done.14) | copy-start | bytes 786436
  156.6 5.2 %copy-start.17 = (bf16[1,512,256]{1,2,0:T(8,128)(2,1)S(1)}, bf16[1,512,256]{1,2,0:T(8,128)(2,1)}, u32[]{:S(2)}) copy-start(bf16[1,512,256]{1,2,0:T(8,128)(2,1)} %copy-done.16) | copy-start | bytes 786436
  156.7 5.2 %copy-start.19 = (bf16[1,512,256]{1,2,0:T(8,128)(2,1)S(1)}, bf16[1,512,256]{1,2,0:T(8,128)(2,1)}, u32[]{:S(2)}) copy-start(bf16[1,512,256]{1,2,0:T(8,128)(2,1)} %copy-done.18) | copy-start | bytes 786436
  156.7 5.2 %copy-start.38 = (bf16[1,504,256]{2,1,0:T(8,128)(2,1)S(1)}, bf16[1,504,256]{2,1,0:T(8,128)(2,1)}, u32[]{:S(2)}) copy-start(bf16[1,504,256]{2,1,0:T(8,128)(2,1)} %copy-done.37) | copy-start | bytes 774148
  158.3 3.9 %copy-start.32 = (bf16[1,512,256]{2,1,0:T(8,128)(2,1)S(1)}, bf16[1,512,256]{2,1,0:T(8,128)(2,1)}, u32[]{:S(2)}) copy-start(bf16[1,512,256]{2,1,0:T(8,128)(2,1)} %copy-done.31) | copy-start | bytes 786436
  159.8 2.8 copy-start.6
  159.8 2.8 copy-start.21
  159.8 2.8 copy-start.23
  161.8 1.5 copy-start.8
  161.8 1.5 copy-start.28
  161.8 1.5 copy-start.30
  162.6 1.5 copy-start.4
  162.6 1.5 copy-start.42
  162.6 1.5 copy-start.44
  165.6 4.1 %copy-start.24 = (bf16[1,512,256]{1,2,0:T(8,128)(2,1)}, bf16[1,512,256]{1,2,0:T(8,128)(2,1)S(1)}, u32[]{:S(2)}) copy-start(bf16[1,512,256]{1,2,0:T(8,128)(2,1)S(1)} %get-tuple-element.11) | copy-start | bytes 786436
  165.6 4.1 %copy-start.26 = (bf16[1,512,256]{1,2,0:T(8,128)(2,1)}, bf16[1,512,256]{1,2,0:T(8,128)(2,1)S(1)}, u32[]{:S(2)}) copy-start(bf16[1,512,256]{1,2,0:T(8,128)(2,1)S(1)} %get-tuple-element.12) | copy-start | bytes 786436
  184.8 109.1 %reduce-scatter.11.cloned.1.call-start = ((), (), s32[]{:S(2)}) async-start(), calls=%async_computation.5 | async-start | bytes 884736 | tf_op jit(solution)/shard_map/reduce_scatter | solution.py:94
  190.7 172.0 %reduce-scatter.9.cloned.1.call-start = ((), (), s32[]{:S(2)}) async-start(), calls=%async_computation.4 | async-start | bytes 1769472 | tf_op jit(solution)/shard_map/reduce_scatter | solution.py:93
  229.5 4.9 %copy-start.25 = (bf16[1,512,256]{1,2,0:T(8,128)(2,1)S(1)}, bf16[1,512,256]{1,2,0:T(8,128)(2,1)}, u32[]{:S(2)}) copy-start(bf16[1,512,256]{1,2,0:T(8,128)(2,1)} %copy-done.24) | copy-start | bytes 786436
  235.3 8.2 %collective-permute-start.11 = (bf16[1,1,512]{1,2,0:T(8,128)(2,1)S(1)}, bf16[1,1,512]{1,2,0:T(8,128)(2,1)S(1)}, u32[]{:S(2)}, u32[]{:S(2)}) collective-permute-start(bf16[1,1,512]{1,2,0:T(8,128)(2,1)S(1)} %pad_maximum_fusion.42), channel_id=1, source_target_pairs={{4,0},{8,4},{12,8},{16,12},{20,16},{24,20},{28,24},{5,1},{9,5},{13... | collective-permute-start | bytes 3080 | tf_op jit(solution)/shard_map/ppermute | solution.py:10
Sparse Core Ops, SparseCore 0:
  156.7 29.3 reduce-scatter.14
  188.8 37.9 reduce-scatter.12
  230.7 63.2 reduce-scatter.10
  298.2 64.4 reduce-scatter.8
where the time goes:
time: 371 us; the launch traced here: 369 us
  waiting for transfers between devices  194 us (52%)
  blocking collectives  40.8 us (11%)
  local copies, waits for them, and re-layouts  36.6 us (10%)
  starting transfers between devices  34.5 us (9%)
  matrix products  30.6 us (8%)
  other arithmetic  17.1 us (5%)
  between operations  15.8 us (4%)
    reduce_scatter x1, waiting for transfers between devices, body(): lax.psum_scatter(partial_grads[0], 'tm', scatter_dimension=1, tiled=True)  68.7 us
    reduce_scatter x1, waiting for transfers between devices, body(): lax.psum_scatter(partial_grads[1], 'tm', scatter_dimension=1, tiled=True)  47.2 us
    psum x1, blocking collectives, body(): weight_sum = lax.psum(jnp.sum(sample_weight), ('tm', 'dp'))  40.8 us
    ppermute x12, waiting for transfers between devices, shifted(): return lax.ppermute(x, axis, pairs)  40.7 us
    unnamed x6, waiting for transfers between devices  37.1 us
    unnamed x101, local copies, waits for them, and re-layouts  35.7 us
    ppermute x12, starting transfers between devices, shifted(): return lax.ppermute(x, axis, pairs)  34.1 us
    dot_general x18, matrix products, outer_sum(): jnp.einsum('btc,btd->cd', left_op, right_op, preferred_element_type=jnp.f...  14.1 us
  transfers between devices with their start and end apart: 16, of which 15 were waited for; matrix products, arithmetic and copies ran while one was open for 16% of the time, Pallas kernels for 0%

commit v1 on v0

v1 whole, which is shorter than its diff:
```python
import functools

import jax
import jax.numpy as jnp
from jax import lax
from jax.experimental import pallas as pl
from jax.experimental.pallas import tpu as pltpu
from jax.sharding import PartitionSpec as P

LANES = 128
VMEM_BYTES = 56 * 1024 * 1024
NN = (((1,), (0,)), ((), ()))
NT = (((1,), (1,)), ((), ()))
TN = (((0,), (0,)), ((), ()))


def dot(left, right, dims):
    return lax.dot_general(left, right, dims, preferred_element_type=jnp.float32)


def shifted(x, axis, by):
    count = lax.axis_size(axis)
    pairs = [(i, i + by) for i in range(count) if 0 <= i + by < count]
    return lax.ppermute(x, axis, pairs)


def column(row, rows):
    return jnp.broadcast_to(row, (LANES, rows)).T


def pack_kernel(head_x, tail_x, head_gs, head_gk, weight, to_next, to_prev):
    halo, channels = tail_x.shape
    to_next[...] = tail_x[...]
    by_row = column(weight[...][:, :LANES], LANES)[:halo]
    by_row = jnp.concatenate([by_row] * (channels // LANES), axis=1)
    to_prev[0:halo] = head_x[...]
    to_prev[halo : 2 * halo] = (head_gs[...].astype(jnp.float32) * by_row).astype(jnp.bfloat16)
    to_prev[2 * halo : 3 * halo] = (head_gk[...].astype(jnp.float32) * by_row).astype(jnp.bfloat16)


def pack(halo, x, grad_stream_out, grad_skip_out, weight):
    length, channels = x.shape
    first = pl.BlockSpec((halo, channels), lambda i: (0, 0))
    last = pl.BlockSpec((halo, channels), lambda i: (length // halo - 1, 0))
    return pl.pallas_call(
        pack_kernel,
        grid=(1,),
        in_specs=[first, last, first, first, pl.BlockSpec((1, length), lambda i: (0, 0))],
        out_specs=[
            pl.BlockSpec((halo, channels), lambda i: (0, 0)),
            pl.BlockSpec((3 * halo, channels), lambda i: (0, 0)),
        ],
        out_shape=[
            jax.ShapeDtypeStruct((halo, channels), jnp.bfloat16),
            jax.ShapeDtypeStruct((3 * halo, channels), jnp.bfloat16),
        ],
        name="pack_borders",
    )(x, x, grad_stream_out, grad_skip_out, weight)


def split_rows(total):
    high = total.astype(jnp.bfloat16).astype(jnp.float32)
    middle = (total - high).astype(jnp.bfloat16).astype(jnp.float32)
    low = total - high - middle
    row = lax.broadcasted_iota(jnp.int32, (16, LANES), 0)
    rows = jnp.where(row == 0, high, jnp.where(row == 1, middle, jnp.where(row == 2, low, 0.0)))
    return rows.astype(jnp.bfloat16)


def joined_rows(rows):
    return jnp.sum(rows.astype(jnp.float32), axis=0, keepdims=True)


def layer_kernel(
    plan, prev_x, own_x, next_rows, own_gs, own_gk, weight, conv_w, out_w,
    grad_in, *rest,
):
    grad_parts = rest[:-8]
    stream, operands, factors, gates, grad_proj, grad_stream, past_part, total = rest[-8:]
    halo, (length, channels) = plan["halo"], own_x.shape
    layers = conv_w.shape[0]
    pad = 2 ** (layers - 1)
    extent = length + 2 * halo
    stream[0:pad] = jnp.zeros((pad, channels), jnp.float32)
    stream[pad : pad + halo] = prev_x[...].astype(jnp.float32)
    stream[pad + halo : pad + halo + length] = own_x[...].astype(jnp.float32)
    stream[pad + halo + length :] = next_rows[0:halo].astype(jnp.float32)
    by_row = column(weight[...], length)
    by_row = jnp.concatenate([by_row] * (channels // LANES), axis=1)
    grad_stream[0:length] = own_gs[...].astype(jnp.float32) * by_row
    grad_stream[length:] = next_rows[halo : 2 * halo].astype(jnp.float32)
    grad_proj[0:length, channels:] = (own_gk[...].astype(jnp.float32) * by_row).astype(jnp.bfloat16)
    grad_proj[length:, channels:] = next_rows[2 * halo : 3 * halo]

    for index in range(layers):
        dilation = 2**index
        start = plan["starts"][index]
        operands[index, start:, :channels] = stream[pad + start :].astype(jnp.bfloat16)
        operands[index, start:, channels:] = stream[
            pad + start - dilation : pad + extent - dilation
        ].astype(jnp.bfloat16)
        preact = dot(operands[index, start:], conv_w[index], NN)
        filtered = jnp.tanh(preact[:, :channels])
        opening = 0.5 + 0.5 * jnp.tanh(0.5 * preact[:, channels:])
        product = filtered * opening
        gates[index, start:] = product.astype(jnp.bfloat16)
        factors[index, start:, :channels] = opening - filtered * product
        factors[index, start:, channels:] = product * (1.0 - opening)
        if index < layers - 1:
            stream[pad + start :] += dot(gates[index, start:], out_w[index, :, :channels], NN)

    for index in reversed(range(layers)):
        dilation = 2**index
        count = plan["counts"][index]
        grad_proj[0:count, :channels] = grad_stream[0:count].astype(jnp.bfloat16)
        grad_gated = dot(grad_proj[0:count], out_w[index], NT)
        own = slice(halo, halo + length)
        total[0:channels] = dot(gates[index, own], grad_proj[0:length], TN)
        plan["store"](total, channels, index, grad_parts, True)
        both = factors[index, halo : halo + count]
        grad_preact = jnp.concatenate(
            [grad_gated * both[:, :channels], grad_gated * both[:, channels:]], axis=1
        ).astype(jnp.bfloat16)
        spread = dot(grad_preact, conv_w[index], NT)
        past_part[0:count] = spread[:, channels:]
        rows = plan["counts"][index - 1] if index else length
        grad_stream[0:rows] += spread[0:rows, :channels] + past_part[dilation : dilation + rows]
        total[...] = dot(operands[index, own], grad_preact[0:length], TN)
        plan["store"](total, 2 * channels, index, grad_parts, False)
    grad_in[...] = grad_stream[0:length]
    plan["finish"](weight, grad_parts)


def store_whole(total, height, index, grad_parts, is_out):
    grad_parts[int(is_out)][index] = total[0:height].astype(jnp.bfloat16)


def finish_whole(weight, grad_parts):
    pass


def finish_shards(weight, grad_parts):
    keep, send = grad_parts[:2]
    own_sum = jnp.broadcast_to(jnp.sum(weight[...], axis=1, keepdims=True), (1, LANES))
    slab = split_rows(own_sum)
    first = keep.shape[2] - 16
    for a in range(keep.shape[0]):
        for b in range(keep.shape[1]):
            keep[a, b, first:] = slab
            send[a, b, first:] = slab


def store_shards(tm, dp, total, height, index, grad_parts, is_out):
    keep, send = grad_parts[2:] if is_out else grad_parts[:2]
    t_at, d_at = lax.axis_index("tm"), lax.axis_index("dp")
    x_at, y_at, z_at, core_at = lax.rem(t_at, 2), lax.div(d_at, 2), lax.div(t_at, 2), lax.rem(d_at, 2)
    depth, rows = tm // 2, height // tm
    at = pl.ds(index * rows, rows)
    for y in range(dp // 2):
        near = total[0 : rows * tm, (2 * y) * LANES : (2 * y + 1) * LANES]
        far = total[0 : rows * tm, (2 * y + 1) * LANES : (2 * y + 2) * LANES]
        mine = jnp.where(core_at == 0, near, far).astype(jnp.bfloat16)
        other = jnp.where(core_at == 0, far, near).astype(jnp.bfloat16)
        y_off = lax.rem(y - y_at + dp // 2, dp // 2)
        for t in range(tm):
            z, x = divmod(t, 2)
            plane = lax.rem(x - x_at + 2, 2) * (dp // 2) + y_off
            along = lax.rem(z - z_at + depth, depth)
            lead = (along, plane) if is_out else (plane, along)
            keep[lead[0], lead[1], at] = mine[t * rows : (t + 1) * rows]
            send[lead[0], lead[1], at] = other[t * rows : (t + 1) * rows]


def run_layers(in_shards, tm, dp, halo, arrays, weight, conv_w, out_w):
    prev_x, own_x, next_rows, own_gs, own_gk = arrays
    length, channels = own_x.shape
    layers = conv_w.shape[0]
    extent = length + 2 * halo
    starts = []
    for index in range(layers):
        need = halo if index == layers - 1 else 2 ** (index + 1)
        starts.append(need // 16 * 16)
    counts = [-(-(length + 2 ** (index + 1) - 1) // 16) * 16 for index in range(layers)]
    plan = {"halo": halo, "starts": starts, "counts": counts}
    if in_shards:
        plan["store"], plan["finish"] = functools.partial(store_shards, tm, dp), finish_shards
        conv_rows, out_rows = layers * 2 * channels // tm + 16, layers * channels // tm
        shapes = 2 * [(dp, tm // 2, conv_rows, LANES)] + 2 * [(tm // 2, dp, out_rows, LANES)]
    else:
        plan["store"], plan["finish"] = store_whole, finish_whole
        shapes = [conv_w.shape, out_w.shape]
    vmem = pl.BlockSpec(memory_space=pltpu.VMEM)
    return pl.pallas_call(
        functools.partial(layer_kernel, plan),
        in_specs=[vmem] * 8,
        out_specs=[vmem] * (1 + len(shapes)),
        out_shape=[jax.ShapeDtypeStruct((length, channels), jnp.float32)]
        + [jax.ShapeDtypeStruct(shape, jnp.bfloat16) for shape in shapes],
        scratch_shapes=[
            pltpu.VMEM((2 ** (layers - 1) + extent, channels), jnp.float32),
            pltpu.VMEM((layers, extent, 2 * channels), jnp.bfloat16),
            pltpu.VMEM((layers, extent, 2 * channels), jnp.float32),
            pltpu.VMEM((layers, extent, channels), jnp.bfloat16),
            pltpu.VMEM((length + halo, 2 * channels), jnp.bfloat16),
            pltpu.VMEM((length + halo, channels), jnp.float32),
            pltpu.VMEM((length + halo, channels), jnp.float32),
            pltpu.VMEM((2 * channels, 2 * channels), jnp.float32),
        ],
        compiler_params=pltpu.CompilerParams(vmem_limit_bytes=VMEM_BYTES),
        name="layers_both_ways",
    )(prev_x, own_x, next_rows, own_gs, own_gk, weight, conv_w, out_w)


def add_kernel(terms, slab_at, *refs):
    outs = refs[sum(len(t) for t in terms) :]
    at = 0
    for out, term in zip(outs, terms):
        parts = refs[at : at + len(term)]
        at += len(term)
        rows = out.shape[-2]
        body = rows if slab_at is None else slab_at
        lead = (slice(None),) * (len(out.shape) - 2)
        value = parts[0][lead + (slice(0, body),)].astype(jnp.float32)
        for part in parts[1:]:
            value = value + part[lead + (slice(0, body),)].astype(jnp.float32)
        out[lead + (slice(0, body),)] = value.astype(out.dtype)
        if slab_at is not None:
            first = (0,) * (len(out.shape) - 2)
            total = joined_rows(parts[0][first + (slice(body, rows),)])
            for part in parts[1:]:
                total = total + joined_rows(part[first + (slice(body, rows),)])
            slab = split_rows(total)
            if len(out.shape) == 2:
                out[body:rows] = slab
            else:
                for i in range(out.shape[0]):
                    out[i, body:rows] = slab


def lead_block(array, index):
    shape = array.shape[1:]
    return pl.BlockSpec((None,) + shape, lambda i: (index,) + (0,) * len(shape))


def add_up(groups, shape, slab_at, name):
    operands = [a for group in groups for a, _ in group]
    specs = [lead_block(a, i) for group in groups for a, i in group]
    zero = (0,) * len(shape)
    return pl.pallas_call(
        functools.partial(add_kernel, [[None] * len(g) for g in groups], slab_at),
        grid=(1,),
        in_specs=specs,
        out_specs=[pl.BlockSpec(shape, lambda i: zero) for _ in groups],
        out_shape=[jax.ShapeDtypeStruct(shape, jnp.bfloat16) for _ in groups],
        compiler_params=pltpu.CompilerParams(vmem_limit_bytes=VMEM_BYTES),
        name=name,
    )(*operands)


def last_kernel(conv_count, out_count, samples_all, *refs):
    conv_parts, refs = refs[:conv_count], refs[conv_count:]
    out_parts, refs = refs[:out_count], refs[out_count:]
    grad_in, grad_inputs, grad_conv, grad_out = refs
    layers, conv_rows, _ = grad_conv.shape
    slab_at = layers * conv_rows
    total = joined_rows(conv_parts[0][slab_at:])
    for part in conv_parts[1:]:
        total = total + joined_rows(part[slab_at:])
    scale = samples_all / total
    for parts, out in ((conv_parts, grad_conv), (out_parts, grad_out)):
        rows = out.shape[1]
        for index in range(layers):
            at = slice(index * rows, (index + 1) * rows)
            value = parts[0][at].astype(jnp.float32)
            for part in parts[1:]:
                value = value + part[at].astype(jnp.float32)
            out[index] = value * scale
    for first in range(0, grad_in.shape[1], LANES):
        grad_inputs[:, first : first + LANES] = grad_in[:, first : first + LANES] * scale


def reduce_shards(tm, dp, keep_conv, send_conv, keep_out, send_out):
    depth, wide = tm // 2, dp // 2
    axes = ("tm", "dp")

    def moved(x, core=0, xs=0, ys=0, zs=0):
        pairs = []
        for t in range(tm):
            for d in range(dp):
                z, a = divmod(t, 2)
                y, c = divmod(d, 2)
                to_t = (z + zs) % depth * 2 + (a + xs) % 2
                to_d = (y + ys) % wide * 2 + (c + core) % 2
                pairs.append((t * dp + d, to_t * dp + to_d))
        return lax.ppermute(x, axes, pairs)

    def plane(x, step):
        return moved(x, xs=step // wide, ys=step % wide)

    def along(x, step):
        return moved(x, zs=step)

    out_there = moved(send_out, core=1)
    conv_there = moved(send_conv, core=1)
    conv_slab = keep_conv.shape[2] - 16
    steps_z, steps_p = range(1, depth), range(1, 2 * wide)
    out_first = add_up(
        [[(keep_out, r), (out_there, r)] for r in steps_z], keep_out.shape[1:], None, "add_out_cores"
    )
    out_z = [along(x, r) for x, r in zip(out_first, steps_z)]
    conv_first = add_up(
        [[(keep_conv, r), (conv_there, r)] for r in steps_p], keep_conv.shape[1:], conv_slab, "add_conv_cores"
    )
    conv_p = [plane(x, r) for x, r in zip(conv_first, steps_p)]
    out_second = add_up(
        [
            [(keep_out.reshape((-1,) + keep_out.shape[2:]), r), (out_there.reshape((-1,) + keep_out.shape[2:]), r)]
            + [(x, r) for x in out_z]
            for r in range(2 * wide)
        ],
        keep_out.shape[2:], None, "add_out_along",
    )
    out_p = [plane(x, r) for x, r in zip(out_second[1:], steps_p)]
    conv_second = add_up(
        [
            [(keep_conv.reshape((-1,) + keep_conv.shape[2:]), r), (conv_there.reshape((-1,) + keep_conv.shape[2:]), r)]
            + [(x, r) for x in conv_p]
            for r in range(depth)
        ],
        keep_conv.shape[2:], conv_slab, "add_conv_plane",
    )
    conv_z = [along(x, r) for x, r in zip(conv_second[1:], steps_z)]
    return [conv_second[0]] + conv_z, [out_second[0]] + out_p


def scattered(part):
    columns = lax.psum_scatter(part, "dp", scatter_dimension=2, tiled=True).astype(jnp.float32)
    return lax.psum_scatter(columns, "tm", scatter_dimension=1, tiled=True)


def body(inputs, grad_stream_out, grad_skip_out, sample_weight, conv_weight, out_weight):
    tm, dp = lax.axis_size("tm"), lax.axis_size("dp")
    batch, length, channels = inputs.shape
    layers = conv_weight.shape[0]
    halo = 2**layers
    samples_all = batch * length * tm * dp
    x, gs, gk = inputs[0], grad_stream_out[0], grad_skip_out[0]
    to_next, to_prev = pack(halo, x, gs, gk, sample_weight)
    prev_x = shifted(to_next, "tm", 1)
    next_rows = shifted(to_prev, "tm", -1)
    in_shards = dp == 4 and tm % 2 == 0 and channels // tm % 16 == 0 and 2 * channels == dp * LANES
    grad_in, *parts = run_layers(
        in_shards, tm, dp, halo, (prev_x, x, next_rows, gs, gk), sample_weight, conv_weight, out_weight
    )
    if not in_shards:
        scale = samples_all / lax.psum(jnp.sum(sample_weight), ("tm", "dp"))
        grad_conv, grad_out = (scattered(part) * scale for part in parts)
        return (grad_in * scale)[None], grad_conv, grad_out
    conv_terms, out_terms = reduce_shards(tm, dp, *parts)
    conv_rows, out_rows = 2 * channels // tm, channels // tm
    grad_inputs, grad_conv, grad_out = pl.pallas_call(
        functools.partial(last_kernel, len(conv_terms), len(out_terms), float(samples_all)),
        out_shape=[
            jax.ShapeDtypeStruct((length, channels), jnp.float32),
            jax.ShapeDtypeStruct((layers, conv_rows, LANES), jnp.float32),
            jax.ShapeDtypeStruct((layers, out_rows, LANES), jnp.float32),
        ],
        name="scale_all",
    )(*conv_terms, *out_terms, grad_in)
    return grad_inputs[None], grad_conv, grad_out


def solution(mesh):
    placed = (
        P("dp", "tm", None),
        P("dp", "tm", None),
        P("dp", "tm", None),
        P("dp", "tm"),
        P(),
        P(),
    )
    return jax.shard_map(
        body,
        mesh=mesh,
        in_specs=placed,
        out_specs=(P("dp", "tm", None), P(None, "tm", "dp"), P(None, "tm", "dp")),
        check_vma=False,
    )
```

time: 371 us -> 82 us (0.22)
  waiting for transfers between devices: 194 us -> 16.3 us
  blocking collectives: 40.8 us -> 0 us
  local copies, waits for them, and re-layouts: 36.6 us -> 5.48 us
  matrix products: 30.6 us -> 0 us
  Pallas kernels: 0 us -> 26.4 us
  other arithmetic: 17.1 us -> 0 us
  between operations: 15.8 us -> 0.74 us
    reduce_scatter x2 -> x0, waiting for transfers between devices: 116 us -> none  [the longest x1 68.7 us: body(): lax.psum_scatter(partial_grads[0], 'tm', scatter_dimension=1, tiled=True)]
    psum x1 -> x0, blocking collectives: 40.8 us -> none  [body(): weight_sum = lax.psum(jnp.sum(sample_weight), ('tm', 'dp'))]
    ppermute x12 -> x2, waiting for transfers between devices: 40.7 us -> 2.06 us  [shifted(): return lax.ppermute(x, axis, pairs)]
    unnamed x6 -> x0, waiting for transfers between devices: 37.1 us -> none
    dot_general x53 -> x0, matrix products: 30.6 us -> none  [the longest x18 14.1 us: outer_sum(): jnp.einsum('btc,btd->cd', left_op, right_op, preferred_element_type=jnp.f...]
    unnamed x101 -> x32, local copies, waits for them, and re-layouts: 35.7 us -> 5.48 us
    ppermute x12 -> x2, starting transfers between devices: 34.1 us -> 6.75 us  [shifted(): return lax.ppermute(x, axis, pairs)]
    pallas_call x0 -> x7, Pallas kernels: none -> 26.4 us  [the longest x1 13.1 us: run_layers(): pl.pallas_call(functools.partial(layer_kernel, plan), in_specs=[vmem] * 8...]
  transfers between devices with their start and end apart: 16 -> 16, of which waited for: 15 -> 6; matrix products, arithmetic and copies ran while one was open for 16% -> 0% of each run, Pallas kernels for 0% -> 12%
where the time goes in v1:
time: 82 us; the launch traced here: 81.6 us
  starting transfers between devices  32.7 us (40%)
  Pallas kernels  26.4 us (32%)
  waiting for transfers between devices  16.3 us (20%)
  local copies, waits for them, and re-layouts  5.48 us (7%)
    ppermute x14, starting transfers between devices, moved(): return lax.ppermute(x, axes, pairs)  26 us
    ppermute x14, waiting for transfers between devices, moved(): return lax.ppermute(x, axes, pairs)  14.2 us
    pallas_call x1, Pallas kernels, run_layers(): pl.pallas_call(functools.partial(layer_kernel, plan), in_specs=[vmem] * 8...  13.1 us
    pallas_call x4, Pallas kernels, add_up(): pl.pallas_call(functools.partial(add_kernel, [[None] * len(g) for g in gr...  9.4 us
    ppermute x2, starting transfers between devices, shifted(): return lax.ppermute(x, axis, pairs)  6.75 us
    unnamed x32, local copies, waits for them, and re-layouts  5.48 us
    pallas_call x1, Pallas kernels, body(): pl.pallas_call(functools.partial(last_kernel, len(conv_terms), len(out_te...  2.29 us
    ppermute x2, waiting for transfers between devices, shifted(): return lax.ppermute(x, axis, pairs)  2.06 us
  transfers between devices with their start and end apart: 16, of which 6 were waited for; matrix products, arithmetic and copies ran while one was open for 0% of the time, Pallas kernels for 12%

profile of v1, /device:TPU:0, one launch (start us, length us, event | category | flops | bytes accessed | tf_op | source)
XLA Modules:
  0.0 81.6 jit_solution(14812485574495275619)
XLA Ops:
  0.6 1.5 %pack_borders.1 = (bf16[64,256]{1,0:T(8,128)(2,1)}, bf16[192,256]{1,0:T(8,128)(2,1)}) custom-call(bf16[512,256]{1,0:T(8,128)(2,1)} %bitcast.24, bf16[512,256]{1,0:T(8,128)(2,1)} %bitcast.25, bf16[512,256]{1,0:T(8,128)(2,1)} %bitcast.27, bf16[512,256]{1,0:T(8,128)(2,1)} %bitcast.29, f32[1,512]{1,0:T(1,128)} %weight.3), custom_call_target="tpu_custom_call" | custom-call | tf_op jit(solution)/shard_map/pack_borders/pallas_call | solution.py:45
  2.2 1.3 %collective-permute-start.1 = (bf16[192,256]{1,0:T(8,128)(2,1)}, bf16[192,256]{1,0:T(8,128)(2,1)S(1)}, u32[]{:S(2)}, u32[]{:S(2)}) collective-permute-start(bf16[192,256]{1,0:T(8,128)(2,1)} %get-tuple-element.28), channel_id=1, source_target_pairs={{4,0},{8,4},{12,8},{16,12},{20,16},{24,20},{28,24},{5,1},{9,5},{13... | collective-permute-start | bytes 294920 | tf_op jit(solution)/shard_map/ppermute | solution.py:24
  3.5 5.5 %collective-permute-start = (bf16[64,256]{1,0:T(8,128)(2,1)}, bf16[64,256]{1,0:T(8,128)(2,1)S(1)}, u32[]{:S(2)}, u32[]{:S(2)}) collective-permute-start(bf16[64,256]{1,0:T(8,128)(2,1)} %get-tuple-element.27), channel_id=1, source_target_pairs={{0,4},{4,8},{8,12},{12,16},{16,20},{20,24},{24,28},{1,5},{5,9},{9,... | collective-permute-start | bytes 98312 | tf_op jit(solution)/shard_map/ppermute | solution.py:24
  8.9 2.1 %collective-permute-done.prev_x = bf16[64,256]{1,0:T(8,128)(2,1)S(1)} collective-permute-done((bf16[64,256]{1,0:T(8,128)(2,1)}, bf16[64,256]{1,0:T(8,128)(2,1)S(1)}, u32[]{:S(2)}, u32[]{:S(2)}) %collective-permute-start) | collective-permute-done | bytes 32800 | tf_op jit(solution)/shard_map/ppermute | solution.py:24
  11.0 0.0 copy-start.15
  11.0 0.0 collective-permute-done.1.next_rows
  11.0 0.6 copy-done.15
  11.6 0.0 copy-start.11
  11.6 0.6 copy-done.11
  12.3 13.1 %layers_both_ways.1 = (f32[512,256]{1,0:T(8,128)}, bf16[4,4,400,128]{3,2,1,0:T(8,128)(2,1)}, bf16[4,4,400,128]{3,2,1,0:T(8,128)(2,1)}, bf16[4,4,192,128]{3,2,1,0:T(8,128)(2,1)}, bf16[4,4,192,128]{3,2,1,0:T(8,128)(2,1)}) custom-call(bf16[64,256]{1,0:T(8,128)(2,1)} %copy-done.15, bf16[512,256]{1,0:T(8,128)(2,1)} %bitcast.26, bf16[192,256]{1,0:T(8,128)(2,1)} %copy-done.11, ...), custom_call_target="tpu_custom_call" | custom-call | tf_op jit(solution)/shard_map/layers_both_ways/pallas_call | solution.py:193
  25.4 0.0 collective-permute-start.2
  25.4 0.5 collective-permute-start.9
  25.9 3.2 %collective-permute-done.2.refs_1_.refs_3_.refs_5_ = bf16[4,4,400,128]{3,2,1,0:T(8,128)(2,1)S(1)} collective-permute-done((bf16[4,4,400,128]{3,2,1,0:T(8,128)(2,1)}, bf16[4,4,400,128]{3,2,1,0:T(8,128)(2,1)S(1)}, u32[]{:S(2)}, u32[]{:S(2)}) %collective-permute-start.2) | collective-permute-done | bytes 1638432 | tf_op jit(solution)/shard_map/ppermute | solution.py:295
  29.1 0.0 copy-start
  29.1 1.2 %copy-done = bf16[4,4,400,128]{3,2,1,0:T(8,128)(2,1)} copy-done((bf16[4,4,400,128]{3,2,1,0:T(8,128)(2,1)}, bf16[4,4,400,128]{3,2,1,0:T(8,128)(2,1)S(1)}, u32[]{:S(2)}) %copy-start) | copy-done | bytes 1638424
  30.3 2.7 %add_conv_cores.1 = (bf16[4,400,128]{2,1,0:T(8,128)(2,1)}, bf16[4,400,128]{2,1,0:T(8,128)(2,1)}, bf16[4,400,128]{2,1,0:T(8,128)(2,1)}) custom-call(bf16[4,4,400,128]{3,2,1,0:T(8,128)(2,1)} %get-tuple-element.29.refs_0_.refs_2_.refs_4_, bf16[4,4,400,128]{3,2,1,0:T(8,128)(2,1)} %copy-done, bf16[4,4,400,128]{3,2,1,0:T(8,128)(2,1)} %get-tuple-element.29.refs_0_.refs_2_.refs_4_, ...), custom_call_target="tpu_custom_call" | custom-call | tf_op jit(solution)/shard_map/add_conv_cores/pallas_call | solution.py:249
  33.0 1.9 %collective-permute-start.3 = (bf16[4,400,128]{2,1,0:T(8,128)(2,1)}, bf16[4,400,128]{2,1,0:T(8,128)(2,1)S(1)}, u32[]{:S(2)}, u32[]{:S(2)}) collective-permute-start(bf16[4,400,128]{2,1,0:T(8,128)(2,1)} %get-tuple-element.31), channel_id=1, source_target_pairs={{0,2},{1,3},{2,0},{3,1},{4,6},{5,7},{6,4},{7,5},{8,10},{9,11},{10,... | collective-permute-start | bytes 1228808 | tf_op jit(solution)/shard_map/ppermute | solution.py:295
  34.9 2.4 %collective-permute-start.4 = (bf16[4,400,128]{2,1,0:T(8,128)(2,1)}, bf16[4,400,128]{2,1,0:T(8,128)(2,1)S(1)}, u32[]{:S(2)}, u32[]{:S(2)}) collective-permute-start(bf16[4,400,128]{2,1,0:T(8,128)(2,1)} %get-tuple-element.32), channel_id=1, source_target_pairs={{0,4},{1,5},{2,6},{3,7},{4,0},{5,1},{6,2},{7,3},{8,12},{9,13},{10,... | collective-permute-start | bytes 1228808 | tf_op jit(solution)/shard_map/ppermute | solution.py:295
  37.3 0.0 collective-permute-start.5
  37.3 0.0 collective-permute-done.9.refs_1_.refs_3_.refs_5_
  37.3 0.0 copy-start.1
  37.3 0.9 %copy-done.1 = bf16[4,4,192,128]{3,2,1,0:T(8,128)(2,1)} copy-done((bf16[4,4,192,128]{3,2,1,0:T(8,128)(2,1)}, bf16[4,4,192,128]{3,2,1,0:T(8,128)(2,1)S(1)}, u32[]{:S(2)}) %copy-start.1) | copy-done | bytes 786456
  38.2 2.2 %add_out_cores.1 = (bf16[4,192,128]{2,1,0:T(8,128)(2,1)}, bf16[4,192,128]{2,1,0:T(8,128)(2,1)}, bf16[4,192,128]{2,1,0:T(8,128)(2,1)}) custom-call(bf16[4,4,192,128]{3,2,1,0:T(8,128)(2,1)} %get-tuple-element.38.refs_0_.refs_2_.refs_4_, bf16[4,4,192,128]{3,2,1,0:T(8,128)(2,1)} %copy-done.1, bf16[4,4,192,128]{3,2,1,0:T(8,128)(2,1)} %get-tuple-element.38.refs_0_.refs_2_.refs_4_, ...), custom_call_target="tpu_custom_call" | custom-call | tf_op jit(solution)/shard_map/add_out_cores/pallas_call | solution.py:249
  40.4 3.6 %collective-permute-start.10 = (bf16[4,192,128]{2,1,0:T(8,128)(2,1)}, bf16[4,192,128]{2,1,0:T(8,128)(2,1)S(1)}, u32[]{:S(2)}, u32[]{:S(2)}) collective-permute-start(bf16[4,192,128]{2,1,0:T(8,128)(2,1)} %get-tuple-element.40), channel_id=1, source_target_pairs={{0,8},{1,9},{2,10},{3,11},{4,12},{5,13},{6,14},{7,15},{8,16},{9,17... | collective-permute-start | bytes 589832 | tf_op jit(solution)/shard_map/ppermute | solution.py:295
  44.0 2.6 %collective-permute-start.11 = (bf16[4,192,128]{2,1,0:T(8,128)(2,1)}, bf16[4,192,128]{2,1,0:T(8,128)(2,1)S(1)}, u32[]{:S(2)}, u32[]{:S(2)}) collective-permute-start(bf16[4,192,128]{2,1,0:T(8,128)(2,1)} %get-tuple-element.41), channel_id=1, source_target_pairs={{0,16},{1,17},{2,18},{3,19},{4,20},{5,21},{6,22},{7,23},{8,24},{9,... | collective-permute-start | bytes 589832 | tf_op jit(solution)/shard_map/ppermute | solution.py:295
  46.6 0.0 collective-permute-done.3.refs_2_.refs_7_.refs_12_.refs_17_
  46.6 0.0 copy-start.2
  46.6 4.6 %collective-permute-start.12 = (bf16[4,192,128]{2,1,0:T(8,128)(2,1)}, bf16[4,192,128]{2,1,0:T(8,128)(2,1)S(1)}, u32[]{:S(2)}, u32[]{:S(2)}) collective-permute-start(bf16[4,192,128]{2,1,0:T(8,128)(2,1)} %get-tuple-element.42), channel_id=1, source_target_pairs={{0,24},{1,25},{2,26},{3,27},{4,28},{5,29},{6,30},{7,31},{8,0},{9,1... | collective-permute-start | bytes 589832 | tf_op jit(solution)/shard_map/ppermute | solution.py:295
  51.2 0.0 collective-permute-done.4.refs_3_.refs_8_.refs_13_.refs_18_
  51.2 0.0 copy-start.3
  51.2 4.5 %collective-permute-done.5.refs_4_.refs_9_.refs_14_.refs_19_ = bf16[4,400,128]{2,1,0:T(8,128)(2,1)S(1)} collective-permute-done((bf16[4,400,128]{2,1,0:T(8,128)(2,1)}, bf16[4,400,128]{2,1,0:T(8,128)(2,1)S(1)}, u32[]{:S(2)}, u32[]{:S(2)}) %collective-permute-start.5) | collective-permute-done | bytes 409632 | tf_op jit(solution)/shard_map/ppermute | solution.py:295
  55.7 0.0 copy-done.2
  55.7 0.0 copy-done.3
  55.7 0.7 copy-done.4
  56.5 2.5 %add_conv_plane.1 = (bf16[400,128]{1,0:T(8,128)(2,1)}, bf16[400,128]{1,0:T(8,128)(2,1)}, bf16[400,128]{1,0:T(8,128)(2,1)}, bf16[400,128]{1,0:T(8,128)(2,1)}) custom-call(bf16[16,400,128]{2,1,0:T(8,128)(2,1)} %bitcast.8, bf16[16,400,128]{2,1,0:T(8,128)(2,1)} %bitcast.12, bf16[4,400,128]{2,1,0:T(8,128)(2,1)} %copy-done.2, bf16[4,400,128]{2,1,0:T(8,128)(2,1)} %copy-done.3, ...), custom_call_target="tpu_custom_call" | custom-call | tf_op jit(solution)/shard_map/add_conv_plane/pallas_call | solution.py:249
  59.0 3.4 %collective-permute-start.6 = (bf16[400,128]{1,0:T(8,128)(2,1)}, bf16[400,128]{1,0:T(8,128)(2,1)S(1)}, u32[]{:S(2)}, u32[]{:S(2)}) collective-permute-start(bf16[400,128]{1,0:T(8,128)(2,1)} %get-tuple-element.35), channel_id=1, source_target_pairs={{0,8},{1,9},{2,10},{3,11},{4,12},{5,13},{6,14},{7,15},{8,16},{9,17... | collective-permute-start | bytes 307208 | tf_op jit(solution)/shard_map/ppermute | solution.py:295
  62.4 2.6 %collective-permute-start.7 = (bf16[400,128]{1,0:T(8,128)(2,1)}, bf16[400,128]{1,0:T(8,128)(2,1)S(1)}, u32[]{:S(2)}, u32[]{:S(2)}) collective-permute-start(bf16[400,128]{1,0:T(8,128)(2,1)} %get-tuple-element.36), channel_id=1, source_target_pairs={{0,16},{1,17},{2,18},{3,19},{4,20},{5,21},{6,22},{7,23},{8,24},{9,... | collective-permute-start | bytes 307208 | tf_op jit(solution)/shard_map/ppermute | solution.py:295
  65.0 0.0 collective-permute-done.10.refs_2_.refs_7_.refs_12_.refs_17_
  65.0 1.4 %collective-permute-start.8 = (bf16[400,128]{1,0:T(8,128)(2,1)}, bf16[400,128]{1,0:T(8,128)(2,1)S(1)}, u32[]{:S(2)}, u32[]{:S(2)}) collective-permute-start(bf16[400,128]{1,0:T(8,128)(2,1)} %get-tuple-element.37), channel_id=1, source_target_pairs={{0,24},{1,25},{2,26},{3,27},{4,28},{5,29},{6,30},{7,31},{8,0},{9,1... | collective-permute-start | bytes 307208 | tf_op jit(solution)/shard_map/ppermute | solution.py:295
  66.3 0.0 collective-permute-done.11.refs_3_.refs_8_.refs_13_.refs_18_
  66.4 0.0 collective-permute-done.12.refs_4_.refs_9_.refs_14_.refs_19_
  66.4 0.0 copy-start.7
  66.4 0.0 copy-done.5
  66.4 0.6 copy-done.6
  67.0 0.1 copy-done.7
  67.1 1.9 %add_out_along.1 = (bf16[192,128]{1,0:T(8,128)(2,1)}, bf16[192,128]{1,0:T(8,128)(2,1)}, bf16[192,128]{1,0:T(8,128)(2,1)}, bf16[192,128]{1,0:T(8,128)(2,1)}) custom-call(bf16[16,192,128]{2,1,0:T(8,128)(2,1)} %bitcast.16, bf16[16,192,128]{2,1,0:T(8,128)(2,1)} %bitcast.20, bf16[4,192,128]{2,1,0:T(8,128)(2,1)} %copy-done.5, bf16[4,192,128]{2,1,0:T(8,128)(2,1)} %copy-done.6, ...), custom_call_target="tpu_custom_call" | custom-call | tf_op jit(solution)/shard_map/add_out_along/pallas_call | solution.py:249
  69.0 1.6 %collective-permute-start.13 = (bf16[192,128]{1,0:T(8,128)(2,1)}, bf16[192,128]{1,0:T(8,128)(2,1)S(1)}, u32[]{:S(2)}, u32[]{:S(2)}) collective-permute-start(bf16[192,128]{1,0:T(8,128)(2,1)} %get-tuple-element.44), channel_id=1, source_target_pairs={{0,2},{1,3},{2,0},{3,1},{4,6},{5,7},{6,4},{7,5},{8,10},{9,11},{10,... | collective-permute-start | bytes 147464 | tf_op jit(solution)/shard_map/ppermute | solution.py:295
  70.6 0.3 collective-permute-start.14
  70.9 2.5 %collective-permute-done.13.refs_5_ = bf16[192,128]{1,0:T(8,128)(2,1)S(1)} collective-permute-done((bf16[192,128]{1,0:T(8,128)(2,1)}, bf16[192,128]{1,0:T(8,128)(2,1)S(1)}, u32[]{:S(2)}, u32[]{:S(2)}) %collective-permute-start.13) | collective-permute-done | bytes 49184 | tf_op jit(solution)/shard_map/ppermute | solution.py:295
  73.4 1.2 %collective-permute-start.15 = (bf16[192,128]{1,0:T(8,128)(2,1)}, bf16[192,128]{1,0:T(8,128)(2,1)S(1)}, u32[]{:S(2)}, u32[]{:S(2)}) collective-permute-start(bf16[192,128]{1,0:T(8,128)(2,1)} %get-tuple-element.46), channel_id=1, source_target_pairs={{0,6},{1,7},{2,4},{3,5},{4,2},{5,3},{6,0},{7,1},{8,14},{9,15},{10,... | collective-permute-start | bytes 147464 | tf_op jit(solution)/shard_map/ppermute | solution.py:295
  74.6 0.7 collective-permute-done.14.refs_6_
  75.3 3.2 %collective-permute-done.15.refs_7_ = bf16[192,128]{1,0:T(8,128)(2,1)S(1)} collective-permute-done((bf16[192,128]{1,0:T(8,128)(2,1)}, bf16[192,128]{1,0:T(8,128)(2,1)S(1)}, u32[]{:S(2)}, u32[]{:S(2)}) %collective-permute-start.15) | collective-permute-done | bytes 49184 | tf_op jit(solution)/shard_map/ppermute | solution.py:295
  78.6 0.0 collective-permute-done.6.refs_1_
  78.6 0.0 collective-permute-done.7.refs_2_
  78.6 0.0 copy-start.9
  78.6 0.0 collective-permute-done.8.refs_3_
  78.6 0.0 copy-start.10
  78.6 0.0 copy-done.12
  78.6 0.0 copy-done.13
  78.6 0.5 copy-done.14
  79.2 0.1 copy-done.8
  79.2 0.0 copy-done.9
  79.3 0.0 copy-done.10
  79.3 2.3 %scale_all.1 = (f32[512,256]{1,0:T(8,128)}, f32[6,64,128]{2,1,0:T(8,128)}, f32[6,32,128]{2,1,0:T(8,128)}) custom-call(bf16[400,128]{1,0:T(8,128)(2,1)} %get-tuple-element.34.refs_0_, bf16[400,128]{1,0:T(8,128)(2,1)} %copy-done.8, bf16[400,128]{1,0:T(8,128)(2,1)} %copy-done.9, bf16[400,128]{1,0:T(8,128)(2,1)} %copy-done.10, ...), custom_call_target="tpu_custom_call" | custom-call | tf_op jit(solution)/shard_map/scale_all/pallas_call | solution.py:361
  (7 shorter events, 0.0 us)
Async XLA Ops:
  2.2 8.8 %collective-permute-start.1 = (bf16[192,256]{1,0:T(8,128)(2,1)}, bf16[192,256]{1,0:T(8,128)(2,1)S(1)}, u32[]{:S(2)}, u32[]{:S(2)}) collective-permute-start(bf16[192,256]{1,0:T(8,128)(2,1)} %get-tuple-element.28), channel_id=1, source_target_pairs={{4,0},{8,4},{12,8},{16,12},{20,16},{24,20},{28,24},{5,1},{9,5},{13... | collective-permute-start | bytes 294920 | tf_op jit(solution)/shard_map/ppermute | solution.py:24
  3.5 7.5 %collective-permute-start = (bf16[64,256]{1,0:T(8,128)(2,1)}, bf16[64,256]{1,0:T(8,128)(2,1)S(1)}, u32[]{:S(2)}, u32[]{:S(2)}) collective-permute-start(bf16[64,256]{1,0:T(8,128)(2,1)} %get-tuple-element.27), channel_id=1, source_target_pairs={{0,4},{4,8},{8,12},{12,16},{16,20},{20,24},{24,28},{1,5},{5,9},{9,... | collective-permute-start | bytes 98312 | tf_op jit(solution)/shard_map/ppermute | solution.py:24
  11.0 0.6 copy-start.15
  11.6 0.6 copy-start.11
  25.4 3.7 %collective-permute-start.2 = (bf16[4,4,400,128]{3,2,1,0:T(8,128)(2,1)}, bf16[4,4,400,128]{3,2,1,0:T(8,128)(2,1)S(1)}, u32[]{:S(2)}, u32[]{:S(2)}) collective-permute-start(bf16[4,4,400,128]{3,2,1,0:T(8,128)(2,1)} %get-tuple-element.30), channel_id=1, source_target_pairs={{0,1},{1,0},{2,3},{3,2},{4,5},{5,4},{6,7},{7,6},{8,9},{9,8},{10,11... | collective-permute-start | bytes 4915208 | tf_op jit(solution)/shard_map/ppermute | solution.py:295
  25.4 11.9 %collective-permute-start.9 = (bf16[4,4,192,128]{3,2,1,0:T(8,128)(2,1)}, bf16[4,4,192,128]{3,2,1,0:T(8,128)(2,1)S(1)}, u32[]{:S(2)}, u32[]{:S(2)}) collective-permute-start(bf16[4,4,192,128]{3,2,1,0:T(8,128)(2,1)} %get-tuple-element.39), channel_id=1, source_target_pairs={{0,1},{1,0},{2,3},{3,2},{4,5},{5,4},{6,7},{7,6},{8,9},{9,8},{10,11... | collective-permute-start | bytes 2359304 | tf_op jit(solution)/shard_map/ppermute | solution.py:295
  29.1 1.2 %copy-start = (bf16[4,4,400,128]{3,2,1,0:T(8,128)(2,1)}, bf16[4,4,400,128]{3,2,1,0:T(8,128)(2,1)S(1)}, u32[]{:S(2)}) copy-start(bf16[4,4,400,128]{3,2,1,0:T(8,128)(2,1)S(1)} %collective-permute-done.2.refs_1_.refs_3_.refs_5_) | copy-start | bytes 4915204
  33.0 13.6 %collective-permute-start.3 = (bf16[4,400,128]{2,1,0:T(8,128)(2,1)}, bf16[4,400,128]{2,1,0:T(8,128)(2,1)S(1)}, u32[]{:S(2)}, u32[]{:S(2)}) collective-permute-start(bf16[4,400,128]{2,1,0:T(8,128)(2,1)} %get-tuple-element.31), channel_id=1, source_target_pairs={{0,2},{1,3},{2,0},{3,1},{4,6},{5,7},{6,4},{7,5},{8,10},{9,11},{10,... | collective-permute-start | bytes 1228808 | tf_op jit(solution)/shard_map/ppermute | solution.py:295
  34.9 16.3 %collective-permute-start.4 = (bf16[4,400,128]{2,1,0:T(8,128)(2,1)}, bf16[4,400,128]{2,1,0:T(8,128)(2,1)S(1)}, u32[]{:S(2)}, u32[]{:S(2)}) collective-permute-start(bf16[4,400,128]{2,1,0:T(8,128)(2,1)} %get-tuple-element.32), channel_id=1, source_target_pairs={{0,4},{1,5},{2,6},{3,7},{4,0},{5,1},{6,2},{7,3},{8,12},{9,13},{10,... | collective-permute-start | bytes 1228808 | tf_op jit(solution)/shard_map/ppermute | solution.py:295
  37.3 18.4 %collective-permute-start.5 = (bf16[4,400,128]{2,1,0:T(8,128)(2,1)}, bf16[4,400,128]{2,1,0:T(8,128)(2,1)S(1)}, u32[]{:S(2)}, u32[]{:S(2)}) collective-permute-start(bf16[4,400,128]{2,1,0:T(8,128)(2,1)} %get-tuple-element.33), channel_id=1, source_target_pairs={{0,6},{1,7},{2,4},{3,5},{4,2},{5,3},{6,0},{7,1},{8,14},{9,15},{10,... | collective-permute-start | bytes 1228808 | tf_op jit(solution)/shard_map/ppermute | solution.py:295
  37.3 0.9 %copy-start.1 = (bf16[4,4,192,128]{3,2,1,0:T(8,128)(2,1)}, bf16[4,4,192,128]{3,2,1,0:T(8,128)(2,1)S(1)}, u32[]{:S(2)}) copy-start(bf16[4,4,192,128]{3,2,1,0:T(8,128)(2,1)S(1)} %collective-permute-done.9.refs_1_.refs_3_.refs_5_) | copy-start | bytes 2359300
  40.4 24.6 %collective-permute-start.10 = (bf16[4,192,128]{2,1,0:T(8,128)(2,1)}, bf16[4,192,128]{2,1,0:T(8,128)(2,1)S(1)}, u32[]{:S(2)}, u32[]{:S(2)}) collective-permute-start(bf16[4,192,128]{2,1,0:T(8,128)(2,1)} %get-tuple-element.40), channel_id=1, source_target_pairs={{0,8},{1,9},{2,10},{3,11},{4,12},{5,13},{6,14},{7,15},{8,16},{9,17... | collective-permute-start | bytes 589832 | tf_op jit(solution)/shard_map/ppermute | solution.py:295
  44.0 22.3 %collective-permute-start.11 = (bf16[4,192,128]{2,1,0:T(8,128)(2,1)}, bf16[4,192,128]{2,1,0:T(8,128)(2,1)S(1)}, u32[]{:S(2)}, u32[]{:S(2)}) collective-permute-start(bf16[4,192,128]{2,1,0:T(8,128)(2,1)} %get-tuple-element.41), channel_id=1, source_target_pairs={{0,16},{1,17},{2,18},{3,19},{4,20},{5,21},{6,22},{7,23},{8,24},{9,... | collective-permute-start | bytes 589832 | tf_op jit(solution)/shard_map/ppermute | solution.py:295
  46.6 9.1 %copy-start.2 = (bf16[4,400,128]{2,1,0:T(8,128)(2,1)}, bf16[4,400,128]{2,1,0:T(8,128)(2,1)S(1)}, u32[]{:S(2)}) copy-start(bf16[4,400,128]{2,1,0:T(8,128)(2,1)S(1)} %collective-permute-done.3.refs_2_.refs_7_.refs_12_.refs_17_) | copy-start | bytes 1228804
  46.6 19.8 %collective-permute-start.12 = (bf16[4,192,128]{2,1,0:T(8,128)(2,1)}, bf16[4,192,128]{2,1,0:T(8,128)(2,1)S(1)}, u32[]{:S(2)}, u32[]{:S(2)}) collective-permute-start(bf16[4,192,128]{2,1,0:T(8,128)(2,1)} %get-tuple-element.42), channel_id=1, source_target_pairs={{0,24},{1,25},{2,26},{3,27},{4,28},{5,29},{6,30},{7,31},{8,0},{9,1... | collective-permute-start | bytes 589832 | tf_op jit(solution)/shard_map/ppermute | solution.py:295
  51.2 4.5 %copy-start.3 = (bf16[4,400,128]{2,1,0:T(8,128)(2,1)}, bf16[4,400,128]{2,1,0:T(8,128)(2,1)S(1)}, u32[]{:S(2)}) copy-start(bf16[4,400,128]{2,1,0:T(8,128)(2,1)S(1)} %collective-permute-done.4.refs_3_.refs_8_.refs_13_.refs_18_) | copy-start | bytes 1228804
  55.7 0.7 copy-start.4
  59.0 19.6 %collective-permute-start.6 = (bf16[400,128]{1,0:T(8,128)(2,1)}, bf16[400,128]{1,0:T(8,128)(2,1)S(1)}, u32[]{:S(2)}, u32[]{:S(2)}) collective-permute-start(bf16[400,128]{1,0:T(8,128)(2,1)} %get-tuple-element.35), channel_id=1, source_target_pairs={{0,8},{1,9},{2,10},{3,11},{4,12},{5,13},{6,14},{7,15},{8,16},{9,17... | collective-permute-start | bytes 307208 | tf_op jit(solution)/shard_map/ppermute | solution.py:295
  62.4 16.2 %collective-permute-start.7 = (bf16[400,128]{1,0:T(8,128)(2,1)}, bf16[400,128]{1,0:T(8,128)(2,1)S(1)}, u32[]{:S(2)}, u32[]{:S(2)}) collective-permute-start(bf16[400,128]{1,0:T(8,128)(2,1)} %get-tuple-element.36), channel_id=1, source_target_pairs={{0,16},{1,17},{2,18},{3,19},{4,20},{5,21},{6,22},{7,23},{8,24},{9,... | collective-permute-start | bytes 307208 | tf_op jit(solution)/shard_map/ppermute | solution.py:295
  65.0 1.4 %copy-start.5 = (bf16[4,192,128]{2,1,0:T(8,128)(2,1)}, bf16[4,192,128]{2,1,0:T(8,128)(2,1)S(1)}, u32[]{:S(2)}) copy-start(bf16[4,192,128]{2,1,0:T(8,128)(2,1)S(1)} %collective-permute-done.10.refs_2_.refs_7_.refs_12_.refs_17_) | copy-start | bytes 589828
  65.0 13.6 %collective-permute-start.8 = (bf16[400,128]{1,0:T(8,128)(2,1)}, bf16[400,128]{1,0:T(8,128)(2,1)S(1)}, u32[]{:S(2)}, u32[]{:S(2)}) collective-permute-start(bf16[400,128]{1,0:T(8,128)(2,1)} %get-tuple-element.37), channel_id=1, source_target_pairs={{0,24},{1,25},{2,26},{3,27},{4,28},{5,29},{6,30},{7,31},{8,0},{9,1... | collective-permute-start | bytes 307208 | tf_op jit(solution)/shard_map/ppermute | solution.py:295
  66.4 0.7 copy-start.6
  66.4 0.7 copy-start.7
  69.0 4.4 %collective-permute-start.13 = (bf16[192,128]{1,0:T(8,128)(2,1)}, bf16[192,128]{1,0:T(8,128)(2,1)S(1)}, u32[]{:S(2)}, u32[]{:S(2)}) collective-permute-start(bf16[192,128]{1,0:T(8,128)(2,1)} %get-tuple-element.44), channel_id=1, source_target_pairs={{0,2},{1,3},{2,0},{3,1},{4,6},{5,7},{6,4},{7,5},{8,10},{9,11},{10,... | collective-permute-start | bytes 147464 | tf_op jit(solution)/shard_map/ppermute | solution.py:295
  70.6 4.8 %collective-permute-start.14 = (bf16[192,128]{1,0:T(8,128)(2,1)}, bf16[192,128]{1,0:T(8,128)(2,1)S(1)}, u32[]{:S(2)}, u32[]{:S(2)}) collective-permute-start(bf16[192,128]{1,0:T(8,128)(2,1)} %get-tuple-element.45), channel_id=1, source_target_pairs={{0,4},{1,5},{2,6},{3,7},{4,0},{5,1},{6,2},{7,3},{8,12},{9,13},{10,... | collective-permute-start | bytes 147464 | tf_op jit(solution)/shard_map/ppermute | solution.py:295
  73.4 5.2 %copy-start.12 = (bf16[192,128]{1,0:T(8,128)(2,1)}, bf16[192,128]{1,0:T(8,128)(2,1)S(1)}, u32[]{:S(2)}) copy-start(bf16[192,128]{1,0:T(8,128)(2,1)S(1)} %collective-permute-done.13.refs_5_) | copy-start | bytes 147460
  73.4 5.2 %collective-permute-start.15 = (bf16[192,128]{1,0:T(8,128)(2,1)}, bf16[192,128]{1,0:T(8,128)(2,1)S(1)}, u32[]{:S(2)}, u32[]{:S(2)}) collective-permute-start(bf16[192,128]{1,0:T(8,128)(2,1)} %get-tuple-element.46), channel_id=1, source_target_pairs={{0,6},{1,7},{2,4},{3,5},{4,2},{5,3},{6,0},{7,1},{8,14},{9,15},{10,... | collective-permute-start | bytes 147464 | tf_op jit(solution)/shard_map/ppermute | solution.py:295
  75.3 3.3 %copy-start.13 = (bf16[192,128]{1,0:T(8,128)(2,1)}, bf16[192,128]{1,0:T(8,128)(2,1)S(1)}, u32[]{:S(2)}) copy-start(bf16[192,128]{1,0:T(8,128)(2,1)S(1)} %collective-permute-done.14.refs_6_) | copy-start | bytes 147460
  78.6 0.6 copy-start.14
  78.6 0.7 copy-start.8
  78.6 0.7 copy-start.9
  78.6 0.7 copy-start.10

commit v2 on v1

--- a/solution.py
+++ b/solution.py
@@ -8,7 +8,8 @@
 from jax.sharding import PartitionSpec as P
 
 LANES = 128
-VMEM_BYTES = 56 * 1024 * 1024
+VMEM_BYTES = 36 * 1024 * 1024
+ADD_BYTES = 8 * 1024 * 1024
 NN = (((1,), (0,)), ((), ()))
 NT = (((1,), (1,)), ((), ()))
 TN = (((0,), (0,)), ((), ()))
@@ -16,6 +17,10 @@
 
 def dot(left, right, dims):
     return lax.dot_general(left, right, dims, preferred_element_type=jnp.float32)
+
+
+def held(arrays, space=pltpu.VMEM):
+    return [pltpu.with_memory_space_constraint(x, space) for x in arrays]
 
 
 def shifted(x, axis, by):
@@ -54,8 +59,9 @@
             jax.ShapeDtypeStruct((halo, channels), jnp.bfloat16),
             jax.ShapeDtypeStruct((3 * halo, channels), jnp.bfloat16),
         ],
+        compiler_params=pltpu.CompilerParams(vmem_limit_bytes=ADD_BYTES),
         name="pack_borders",
-    )(x, x, grad_stream_out, grad_skip_out, weight)
+    )(*held((x, x, grad_stream_out, grad_skip_out), pltpu.HBM), weight)
 
 
 def split_rows(total):
@@ -194,8 +200,7 @@
         functools.partial(layer_kernel, plan),
         in_specs=[vmem] * 8,
         out_specs=[vmem] * (1 + len(shapes)),
-        out_shape=[jax.ShapeDtypeStruct((length, channels), jnp.float32)]
-        + [jax.ShapeDtypeStruct(shape, jnp.bfloat16) for shape in shapes],
+        out_shape=[pltpu.VMEM((length, channels), jnp.float32)] + [pltpu.VMEM(shape, jnp.bfloat16) for shape in shapes],
         scratch_shapes=[
             pltpu.VMEM((2 ** (layers - 1) + extent, channels), jnp.float32),
             pltpu.VMEM((layers, extent, 2 * channels), jnp.bfloat16),
@@ -208,53 +213,38 @@
         ],
         compiler_params=pltpu.CompilerParams(vmem_limit_bytes=VMEM_BYTES),
         name="layers_both_ways",
-    )(prev_x, own_x, next_rows, own_gs, own_gk, weight, conv_w, out_w)
-
-
-def add_kernel(terms, slab_at, *refs):
-    outs = refs[sum(len(t) for t in terms) :]
-    at = 0
-    for out, term in zip(outs, terms):
-        parts = refs[at : at + len(term)]
-        at += len(term)
-        rows = out.shape[-2]
+    )(*held([prev_x]), own_x, *held([next_rows]), own_gs, own_gk, weight, conv_w, out_w)
+
+
+def add_kernel(count, groups, slab_at, *refs):
+    arrays, outs = refs[:count], refs[-len(groups) :]
+    for out, group in zip(outs, groups):
+        rows, lead = out.shape[-2], (slice(None),) * (len(out.shape) - 2)
         body = rows if slab_at is None else slab_at
-        lead = (slice(None),) * (len(out.shape) - 2)
-        value = parts[0][lead + (slice(0, body),)].astype(jnp.float32)
-        for part in parts[1:]:
-            value = value + part[lead + (slice(0, body),)].astype(jnp.float32)
+        value = 0.0
+        for array, at in group:
+            value = value + arrays[array][at + lead + (slice(0, body),)].astype(jnp.float32)
         out[lead + (slice(0, body),)] = value.astype(out.dtype)
         if slab_at is not None:
-            first = (0,) * (len(out.shape) - 2)
-            total = joined_rows(parts[0][first + (slice(body, rows),)])
-            for part in parts[1:]:
-                total = total + joined_rows(part[first + (slice(body, rows),)])
+            first = (0,) * len(lead) + (slice(body, rows),)
+            total = 0.0
+            for array, at in group:
+                total = total + joined_rows(arrays[array][at + first])
             slab = split_rows(total)
-            if len(out.shape) == 2:
-                out[body:rows] = slab
-            else:
-                for i in range(out.shape[0]):
-                    out[i, body:rows] = slab
-
-
-def lead_block(array, index):
-    shape = array.shape[1:]
-    return pl.BlockSpec((None,) + shape, lambda i: (index,) + (0,) * len(shape))
-
-
-def add_up(groups, shape, slab_at, name):
-    operands = [a for group in groups for a, _ in group]
-    specs = [lead_block(a, i) for group in groups for a, i in group]
-    zero = (0,) * len(shape)
+            for i in range(out.shape[0]) if lead else (None,):
+                out[(() if i is None else (i,)) + (slice(body, rows),)] = slab
+
+
+def add_up(arrays, groups, shape, slab_at, after, name):
+    vmem = pl.BlockSpec(memory_space=pltpu.VMEM)
     return pl.pallas_call(
-        functools.partial(add_kernel, [[None] * len(g) for g in groups], slab_at),
-        grid=(1,),
-        in_specs=specs,
-        out_specs=[pl.BlockSpec(shape, lambda i: zero) for _ in groups],
-        out_shape=[jax.ShapeDtypeStruct(shape, jnp.bfloat16) for _ in groups],
-        compiler_params=pltpu.CompilerParams(vmem_limit_bytes=VMEM_BYTES),
+        functools.partial(add_kernel, len(arrays), groups, slab_at),
+        in_specs=[vmem] * len(arrays) + [pl.BlockSpec(memory_space=pl.ANY)] * len(after),
+        out_specs=[vmem] * len(groups),
+        out_shape=[pltpu.VMEM(shape, jnp.bfloat16) for _ in groups],
+        compiler_params=pltpu.CompilerParams(vmem_limit_bytes=ADD_BYTES),
         name=name,
-    )(*operands)
+    )(*held(arrays), *held(after))
 
 
 def last_kernel(conv_count, out_count, samples_all, *refs):
@@ -305,29 +295,25 @@
     conv_slab = keep_conv.shape[2] - 16
     steps_z, steps_p = range(1, depth), range(1, 2 * wide)
     out_first = add_up(
-        [[(keep_out, r), (out_there, r)] for r in steps_z], keep_out.shape[1:], None, "add_out_cores"
+        [keep_out, out_there], [[(0, (r,)), (1, (r,))] for r in steps_z], keep_out.shape[1:], None, [],
+        "add_out_cores",
     )
     out_z = [along(x, r) for x, r in zip(out_first, steps_z)]
     conv_first = add_up(
-        [[(keep_conv, r), (conv_there, r)] for r in steps_p], keep_conv.shape[1:], conv_slab, "add_conv_cores"
+        [keep_conv, conv_there], [[(0, (r,)), (1, (r,))] for r in steps_p], keep_conv.shape[1:], conv_slab,
+        out_first[:1], "add_conv_cores",
     )
     conv_p = [plane(x, r) for x, r in zip(conv_first, steps_p)]
     out_second = add_up(
-        [
-            [(keep_out.reshape((-1,) + keep_out.shape[2:]), r), (out_there.reshape((-1,) + keep_out.shape[2:]), r)]
-            + [(x, r) for x in out_z]
-            for r in range(2 * wide)
-        ],
-        keep_out.shape[2:], None, "add_out_along",
+        [keep_out, out_there] + out_z,
+        [[(0, (0, r)), (1, (0, r))] + [(2 + i, (r,)) for i in range(len(out_z))] for r in range(2 * wide)],
+        keep_out.shape[2:], None, [], "add_out_along",
     )
     out_p = [plane(x, r) for x, r in zip(out_second[1:], steps_p)]
     conv_second = add_up(
-        [
-            [(keep_conv.reshape((-1,) + keep_conv.shape[2:]), r), (conv_there.reshape((-1,) + keep_conv.shape[2:]), r)]
-            + [(x, r) for x in conv_p]
-            for r in range(depth)
-        ],
-        keep_conv.shape[2:], conv_slab, "add_conv_plane",
+        [keep_conv, conv_there] + conv_p,
+        [[(0, (0, r)), (1, (0, r))] + [(2 + i, (r,)) for i in range(len(conv_p))] for r in range(depth)],
+        keep_conv.shape[2:], conv_slab, out_second[:1], "add_conv_plane",
     )
     conv_z = [along(x, r) for x, r in zip(conv_second[1:], steps_z)]
     return [conv_second[0]] + conv_z, [out_second[0]] + out_p
@@ -365,8 +351,9 @@
             jax.ShapeDtypeStruct((layers, conv_rows, LANES), jnp.float32),
             jax.ShapeDtypeStruct((layers, out_rows, LANES), jnp.float32),
         ],
+        compiler_params=pltpu.CompilerParams(vmem_limit_bytes=ADD_BYTES),
         name="scale_all",
-    )(*conv_terms, *out_terms, grad_in)
+    )(*held(conv_terms), *held(out_terms), *held([grad_in]))
     return grad_inputs[None], grad_conv, grad_out
 
 

time: 82 us -> 76.5 us (0.933)
  Pallas kernels: 26.4 us -> 11.2 us
  waiting for transfers between devices: 16.3 us -> 28.3 us
  starting transfers between devices: 32.7 us -> 28.4 us
  local copies, waits for them, and re-layouts: 5.48 us -> 7.5 us
    ppermute x14, waiting for transfers between devices: 14.2 us -> 26.5 us  [moved(): return lax.ppermute(x, axes, pairs)]
    pallas_call x4, Pallas kernels: 9.4 us -> 0.85 us  [add_up(): pl.pallas_call(functools.partial(add_kernel, len(arrays), groups, slab_at...]
    pallas_call x1, Pallas kernels: 13.1 us -> 8.49 us  [run_layers(): pl.pallas_call(functools.partial(layer_kernel, plan), in_specs=[vmem] * 8...]
    ppermute x14, starting transfers between devices: 26 us -> 21.6 us  [moved(): return lax.ppermute(x, axes, pairs)]
    unnamed x32 -> x14, local copies, waits for them, and re-layouts: 5.48 us -> 7.5 us
    pallas_call x1, Pallas kernels: 2.29 us -> 0.96 us  [body(): pl.pallas_call(functools.partial(last_kernel, len(conv_terms), len(out_te...]
  transfers between devices with their start and end apart: 16 -> 16, of which waited for: 6 -> 7; matrix products, arithmetic and copies ran while one was open for 0% -> 0% of each run, Pallas kernels for 12% -> 0%
where the time goes in v2:
time: 76.5 us; the launch traced here: 76.1 us
  starting transfers between devices  28.4 us (37%)
  waiting for transfers between devices  28.3 us (37%)
  Pallas kernels  11.2 us (15%)
  local copies, waits for them, and re-layouts  7.5 us (10%)
    ppermute x14, waiting for transfers between devices, moved(): return lax.ppermute(x, axes, pairs)  26.5 us
    ppermute x14, starting transfers between devices, moved(): return lax.ppermute(x, axes, pairs)  21.6 us
    pallas_call x1, Pallas kernels, run_layers(): pl.pallas_call(functools.partial(layer_kernel, plan), in_specs=[vmem] * 8...  8.49 us
    unnamed x14, local copies, waits for them, and re-layouts  7.5 us
    ppermute x2, starting transfers between devices, shifted(): return lax.ppermute(x, axis, pairs)  6.76 us
    ppermute x2, waiting for transfers between devices, shifted(): return lax.ppermute(x, axis, pairs)  1.74 us
  transfers between devices with their start and end apart: 16, of which 7 were waited for; matrix products, arithmetic and copies ran while one was open for 0% of the time, Pallas kernels for 0%

profile of v2, /device:TPU:0, one launch (start us, length us, event | category | flops | bytes accessed | tf_op | source)
XLA Modules:
  0.0 76.1 jit_solution(3356028844995745715)
XLA Ops:
  0.6 0.0 copy-start.5
  0.6 0.7 copy-done.5
  1.3 0.9 %pack_borders.1 = (bf16[64,256]{1,0:T(8,128)(2,1)S(1)}, bf16[192,256]{1,0:T(8,128)(2,1)S(1)}) custom-call(bf16[512,256]{1,0:T(8,128)(2,1)} %bitcast.4, bf16[512,256]{1,0:T(8,128)(2,1)} %bitcast.5, bf16[512,256]{1,0:T(8,128)(2,1)} %bitcast.7, bf16[512,256]{1,0:T(8,128)(2,1)} %bitcast.9, f32[1,512]{1,0:T(1,128)S(1)} %copy-done.5), custom_call_target="tpu_custom_call" | custom-call | tf_op jit(solution)/shard_map/pack_borders/pallas_call | solution.py:50
  2.2 1.3 %collective-permute-start.1 = (bf16[192,256]{1,0:T(8,128)(2,1)S(1)}, bf16[192,256]{1,0:T(8,128)(2,1)S(1)}, u32[]{:S(2)}, u32[]{:S(2)}) collective-permute-start(bf16[192,256]{1,0:T(8,128)(2,1)S(1)} %get-tuple-element.28), channel_id=1, source_target_pairs={{4,0},{8,4},{12,8},{16,12},{20,16},{24,20},{28,24},{5,1},{9,5},{13... | collective-permute-start | bytes 294920 | tf_op jit(solution)/shard_map/ppermute | solution.py:29
  3.5 5.5 %collective-permute-start = (bf16[64,256]{1,0:T(8,128)(2,1)S(1)}, bf16[64,256]{1,0:T(8,128)(2,1)S(1)}, u32[]{:S(2)}, u32[]{:S(2)}) collective-permute-start(bf16[64,256]{1,0:T(8,128)(2,1)S(1)} %get-tuple-element.27), channel_id=1, source_target_pairs={{0,4},{4,8},{8,12},{12,16},{16,20},{20,24},{24,28},{1,5},{5,9},{9,... | collective-permute-start | bytes 98312 | tf_op jit(solution)/shard_map/ppermute | solution.py:29
  9.0 1.7 %collective-permute-done.prev_x = bf16[64,256]{1,0:T(8,128)(2,1)S(1)} collective-permute-done((bf16[64,256]{1,0:T(8,128)(2,1)S(1)}, bf16[64,256]{1,0:T(8,128)(2,1)S(1)}, u32[]{:S(2)}, u32[]{:S(2)}) %collective-permute-start) | collective-permute-done | bytes 32800 | tf_op jit(solution)/shard_map/ppermute | solution.py:29
  10.7 0.0 collective-permute-done.1.next_rows
  10.7 0.0 copy-start
  10.7 1.9 %copy-done = bf16[6,512,512]{2,1,0:T(8,128)(2,1)S(1)} copy-done((bf16[6,512,512]{2,1,0:T(8,128)(2,1)S(1)}, bf16[6,512,512]{2,1,0:T(8,128)(2,1)}, u32[]{:S(2)}) %copy-start) | copy-done | bytes 3145752
  12.6 0.0 copy-start.1
  12.6 0.9 %copy-done.1 = bf16[1,512,256]{2,1,0:T(8,128)(2,1)S(1)} copy-done((bf16[1,512,256]{2,1,0:T(8,128)(2,1)S(1)}, bf16[1,512,256]{2,1,0:T(8,128)(2,1)}, u32[]{:S(2)}) %copy-start.1) | copy-done | bytes 262168
  13.6 0.0 copy-start.2
  13.6 1.4 %copy-done.2 = bf16[6,256,512]{2,1,0:T(8,128)(2,1)S(1)} copy-done((bf16[6,256,512]{2,1,0:T(8,128)(2,1)S(1)}, bf16[6,256,512]{2,1,0:T(8,128)(2,1)}, u32[]{:S(2)}) %copy-start.2) | copy-done | bytes 1572888
  15.0 0.0 copy-start.3
  15.0 0.9 %copy-done.3 = bf16[1,512,256]{2,1,0:T(8,128)(2,1)S(1)} copy-done((bf16[1,512,256]{2,1,0:T(8,128)(2,1)S(1)}, bf16[1,512,256]{2,1,0:T(8,128)(2,1)}, u32[]{:S(2)}) %copy-start.3) | copy-done | bytes 262168
  15.9 0.0 copy-start.4
  15.9 0.9 %copy-done.4 = bf16[1,512,256]{2,1,0:T(8,128)(2,1)S(1)} copy-done((bf16[1,512,256]{2,1,0:T(8,128)(2,1)S(1)}, bf16[1,512,256]{2,1,0:T(8,128)(2,1)}, u32[]{:S(2)}) %copy-start.4) | copy-done | bytes 262168
  16.9 0.0 copy-start.6
  16.9 0.7 copy-done.6
  17.6 8.5 %layers_both_ways.1 = (f32[512,256]{1,0:T(8,128)S(1)}, bf16[4,4,400,128]{3,2,1,0:T(8,128)(2,1)S(1)}, bf16[4,4,400,128]{3,2,1,0:T(8,128)(2,1)S(1)}, bf16[4,4,192,...) custom-call(bf16[64,256]{1,0:T(8,128)(2,1)S(1)} %collective-permute-done.prev_x, bf16[512,256]{1,0:T(8,128)(2,1)S(1)} %bitcast.6, ...), custom_call_target="tpu_custom_call" | custom-call | tf_op jit(solution)/shard_map/layers_both_ways/pallas_call | solution.py:199
  26.1 0.1 collective-permute-start.2
  26.2 0.5 collective-permute-start.3
  26.6 4.1 %collective-permute-done.3.refs_1_ = bf16[4,4,192,128]{3,2,1,0:T(8,128)(2,1)S(1)} collective-permute-done((bf16[4,4,192,128]{3,2,1,0:T(8,128)(2,1)S(1)}, bf16[4,4,192,128]{3,2,1,0:T(8,128)(2,1)S(1)}, u32[]{:S(2)}, u32[]{:S(2)}) %collective-permute-start.3) | collective-permute-done | bytes 786464 | tf_op jit(solution)/shard_map/ppermute | solution.py:285
  30.8 0.1 add_out_cores.1
  30.9 0.0 collective-permute-done.2.refs_1_
  30.9 0.3 add_conv_cores.1
  31.2 1.9 %collective-permute-start.4 = (bf16[4,400,128]{2,1,0:T(8,128)(2,1)S(1)}, bf16[4,400,128]{2,1,0:T(8,128)(2,1)S(1)}, u32[]{:S(2)}, u32[]{:S(2)}) collective-permute-start(bf16[4,400,128]{2,1,0:T(8,128)(2,1)S(1)} %get-tuple-element.34), channel_id=1, source_target_pairs={{0,2},{1,3},{2,0},{3,1},{4,6},{5,7},{6,4},{7,5},{8,10},{9,11},{10,... | collective-permute-start | bytes 1228808 | tf_op jit(solution)/shard_map/ppermute | solution.py:285
  33.2 2.4 %collective-permute-start.5 = (bf16[4,400,128]{2,1,0:T(8,128)(2,1)S(1)}, bf16[4,400,128]{2,1,0:T(8,128)(2,1)S(1)}, u32[]{:S(2)}, u32[]{:S(2)}) collective-permute-start(bf16[4,400,128]{2,1,0:T(8,128)(2,1)S(1)} %get-tuple-element.35), channel_id=1, source_target_pairs={{0,4},{1,5},{2,6},{3,7},{4,0},{5,1},{6,2},{7,3},{8,12},{9,13},{10,... | collective-permute-start | bytes 1228808 | tf_op jit(solution)/shard_map/ppermute | solution.py:285
  35.6 0.0 collective-permute-start.6
  35.6 4.7 %collective-permute-start.8 = (bf16[4,192,128]{2,1,0:T(8,128)(2,1)S(1)}, bf16[4,192,128]{2,1,0:T(8,128)(2,1)S(1)}, u32[]{:S(2)}, u32[]{:S(2)}) collective-permute-start(bf16[4,192,128]{2,1,0:T(8,128)(2,1)S(1)} %get-tuple-element.37), channel_id=1, source_target_pairs={{0,16},{1,17},{2,18},{3,19},{4,20},{5,21},{6,22},{7,23},{8,24},{9,... | collective-permute-start | bytes 589832 | tf_op jit(solution)/shard_map/ppermute | solution.py:285
  40.3 1.3 %collective-permute-start.9 = (bf16[4,192,128]{2,1,0:T(8,128)(2,1)S(1)}, bf16[4,192,128]{2,1,0:T(8,128)(2,1)S(1)}, u32[]{:S(2)}, u32[]{:S(2)}) collective-permute-start(bf16[4,192,128]{2,1,0:T(8,128)(2,1)S(1)} %get-tuple-element.38), channel_id=1, source_target_pairs={{0,24},{1,25},{2,26},{3,27},{4,28},{5,29},{6,30},{7,31},{8,0},{9,1... | collective-permute-start | bytes 589832 | tf_op jit(solution)/shard_map/ppermute | solution.py:285
  41.6 8.4 %collective-permute-done.8.refs_3_ = bf16[4,192,128]{2,1,0:T(8,128)(2,1)S(1)} collective-permute-done((bf16[4,192,128]{2,1,0:T(8,128)(2,1)S(1)}, bf16[4,192,128]{2,1,0:T(8,128)(2,1)S(1)}, u32[]{:S(2)}, u32[]{:S(2)}) %collective-permute-start.8) | collective-permute-done | bytes 196640 | tf_op jit(solution)/shard_map/ppermute | solution.py:285
  50.1 3.7 %collective-permute-start.7 = (bf16[4,192,128]{2,1,0:T(8,128)(2,1)S(1)}, bf16[4,192,128]{2,1,0:T(8,128)(2,1)S(1)}, u32[]{:S(2)}, u32[]{:S(2)}) collective-permute-start(bf16[4,192,128]{2,1,0:T(8,128)(2,1)S(1)} %get-tuple-element.33.refs_2_), channel_id=1, source_target_pairs={{0,8},{1,9},{2,10},{3,11},{4,12},{5,13},{6,14},{7,15},{8,16},{9,17... | collective-permute-start | bytes 589832 | tf_op jit(solution)/shard_map/ppermute | solution.py:285
  53.8 0.0 collective-permute-done.9.refs_4_
  53.8 7.9 %collective-permute-done.7.refs_2_ = bf16[4,192,128]{2,1,0:T(8,128)(2,1)S(1)} collective-permute-done((bf16[4,192,128]{2,1,0:T(8,128)(2,1)S(1)}, bf16[4,192,128]{2,1,0:T(8,128)(2,1)S(1)}, u32[]{:S(2)}, u32[]{:S(2)}) %collective-permute-start.7) | collective-permute-done | bytes 196640 | tf_op jit(solution)/shard_map/ppermute | solution.py:285
  61.7 0.1 add_out_along.1
  61.8 0.0 collective-permute-done.4.refs_2_
  61.8 0.0 collective-permute-done.5.refs_3_
  61.8 0.0 collective-permute-done.6.refs_4_
  61.9 0.3 add_conv_plane.1
  62.1 0.1 collective-permute-start.10
  62.2 2.3 %collective-permute-start.11 = (bf16[400,128]{1,0:T(8,128)(2,1)S(1)}, bf16[400,128]{1,0:T(8,128)(2,1)S(1)}, u32[]{:S(2)}, u32[]{:S(2)}) collective-permute-start(bf16[400,128]{1,0:T(8,128)(2,1)S(1)} %get-tuple-element.42), channel_id=1, source_target_pairs={{0,16},{1,17},{2,18},{3,19},{4,20},{5,21},{6,22},{7,23},{8,24},{9,... | collective-permute-start | bytes 307208 | tf_op jit(solution)/shard_map/ppermute | solution.py:285
  64.5 1.5 %collective-permute-start.12 = (bf16[400,128]{1,0:T(8,128)(2,1)S(1)}, bf16[400,128]{1,0:T(8,128)(2,1)S(1)}, u32[]{:S(2)}, u32[]{:S(2)}) collective-permute-start(bf16[400,128]{1,0:T(8,128)(2,1)S(1)} %get-tuple-element.43), channel_id=1, source_target_pairs={{0,24},{1,25},{2,26},{3,27},{4,28},{5,29},{6,30},{7,31},{8,0},{9,1... | collective-permute-start | bytes 307208 | tf_op jit(solution)/shard_map/ppermute | solution.py:285
  66.0 1.5 %collective-permute-start.13 = (bf16[192,128]{1,0:T(8,128)(2,1)S(1)}, bf16[192,128]{1,0:T(8,128)(2,1)S(1)}, u32[]{:S(2)}, u32[]{:S(2)}) collective-permute-start(bf16[192,128]{1,0:T(8,128)(2,1)S(1)} %get-tuple-element.44), channel_id=1, source_target_pairs={{0,2},{1,3},{2,0},{3,1},{4,6},{5,7},{6,4},{7,5},{8,10},{9,11},{10,... | collective-permute-start | bytes 147464 | tf_op jit(solution)/shard_map/ppermute | solution.py:285
  67.5 0.3 collective-permute-start.14
  67.8 2.3 %collective-permute-done.13.refs_5_ = bf16[192,128]{1,0:T(8,128)(2,1)S(1)} collective-permute-done((bf16[192,128]{1,0:T(8,128)(2,1)S(1)}, bf16[192,128]{1,0:T(8,128)(2,1)S(1)}, u32[]{:S(2)}, u32[]{:S(2)}) %collective-permute-start.13) | collective-permute-done | bytes 49184 | tf_op jit(solution)/shard_map/ppermute | solution.py:285
  70.1 1.2 %collective-permute-start.15 = (bf16[192,128]{1,0:T(8,128)(2,1)S(1)}, bf16[192,128]{1,0:T(8,128)(2,1)S(1)}, u32[]{:S(2)}, u32[]{:S(2)}) collective-permute-start(bf16[192,128]{1,0:T(8,128)(2,1)S(1)} %get-tuple-element.46), channel_id=1, source_target_pairs={{0,6},{1,7},{2,4},{3,5},{4,2},{5,3},{6,0},{7,1},{8,14},{9,15},{10,... | collective-permute-start | bytes 147464 | tf_op jit(solution)/shard_map/ppermute | solution.py:285
  71.4 0.3 collective-permute-done.14.refs_6_
  71.6 3.5 %collective-permute-done.15.refs_7_ = bf16[192,128]{1,0:T(8,128)(2,1)S(1)} collective-permute-done((bf16[192,128]{1,0:T(8,128)(2,1)S(1)}, bf16[192,128]{1,0:T(8,128)(2,1)S(1)}, u32[]{:S(2)}, u32[]{:S(2)}) %collective-permute-start.15) | collective-permute-done | bytes 49184 | tf_op jit(solution)/shard_map/ppermute | solution.py:285
  75.1 0.0 collective-permute-done.10.refs_1_
  75.1 0.0 collective-permute-done.11.refs_2_
  75.1 0.0 collective-permute-done.12.refs_3_
  75.1 1.0 %scale_all.1 = (f32[512,256]{1,0:T(8,128)}, f32[6,64,128]{2,1,0:T(8,128)}, f32[6,32,128]{2,1,0:T(8,128)}) custom-call(bf16[400,128]{1,0:T(8,128)(2,1)S(1)} %get-tuple-element.40.refs_0_, bf16[400,128]{1,0:T(8,128)(2,1)S(1)} %collective-permute-done.10.refs_1_, bf16[400,128]{1,0:T(8,128)(2,1)S(1)} %collective-permute-done.11.refs_2_, ...), custom_call_target="tpu_custom_call" | custom-call | tf_op jit(solution)/shard_map/scale_all/pallas_call | solution.py:347
Async XLA Ops:
  0.6 0.7 copy-start.5
  2.2 8.5 %collective-permute-start.1 = (bf16[192,256]{1,0:T(8,128)(2,1)S(1)}, bf16[192,256]{1,0:T(8,128)(2,1)S(1)}, u32[]{:S(2)}, u32[]{:S(2)}) collective-permute-start(bf16[192,256]{1,0:T(8,128)(2,1)S(1)} %get-tuple-element.28), channel_id=1, source_target_pairs={{4,0},{8,4},{12,8},{16,12},{20,16},{24,20},{28,24},{5,1},{9,5},{13... | collective-permute-start | bytes 294920 | tf_op jit(solution)/shard_map/ppermute | solution.py:29
  3.5 7.2 %collective-permute-start = (bf16[64,256]{1,0:T(8,128)(2,1)S(1)}, bf16[64,256]{1,0:T(8,128)(2,1)S(1)}, u32[]{:S(2)}, u32[]{:S(2)}) collective-permute-start(bf16[64,256]{1,0:T(8,128)(2,1)S(1)} %get-tuple-element.27), channel_id=1, source_target_pairs={{0,4},{4,8},{8,12},{12,16},{16,20},{20,24},{24,28},{1,5},{5,9},{9,... | collective-permute-start | bytes 98312 | tf_op jit(solution)/shard_map/ppermute | solution.py:29
  10.7 1.9 %copy-start = (bf16[6,512,512]{2,1,0:T(8,128)(2,1)S(1)}, bf16[6,512,512]{2,1,0:T(8,128)(2,1)}, u32[]{:S(2)}) copy-start(bf16[6,512,512]{2,1,0:T(8,128)(2,1)} %conv_w.1) | copy-start | bytes 9437188
  12.6 0.9 %copy-start.1 = (bf16[1,512,256]{2,1,0:T(8,128)(2,1)S(1)}, bf16[1,512,256]{2,1,0:T(8,128)(2,1)}, u32[]{:S(2)}) copy-start(bf16[1,512,256]{2,1,0:T(8,128)(2,1)} %param.6) | copy-start | bytes 786436
  13.6 1.4 %copy-start.2 = (bf16[6,256,512]{2,1,0:T(8,128)(2,1)S(1)}, bf16[6,256,512]{2,1,0:T(8,128)(2,1)}, u32[]{:S(2)}) copy-start(bf16[6,256,512]{2,1,0:T(8,128)(2,1)} %out_w.1) | copy-start | bytes 4718596
  15.0 0.9 %copy-start.3 = (bf16[1,512,256]{2,1,0:T(8,128)(2,1)S(1)}, bf16[1,512,256]{2,1,0:T(8,128)(2,1)}, u32[]{:S(2)}) copy-start(bf16[1,512,256]{2,1,0:T(8,128)(2,1)} %param.7) | copy-start | bytes 786436
  15.9 0.9 %copy-start.4 = (bf16[1,512,256]{2,1,0:T(8,128)(2,1)S(1)}, bf16[1,512,256]{2,1,0:T(8,128)(2,1)}, u32[]{:S(2)}) copy-start(bf16[1,512,256]{2,1,0:T(8,128)(2,1)} %param.8) | copy-start | bytes 786436
  16.9 0.7 copy-start.6
  26.1 4.8 %collective-permute-start.2 = (bf16[4,4,400,128]{3,2,1,0:T(8,128)(2,1)S(1)}, bf16[4,4,400,128]{3,2,1,0:T(8,128)(2,1)S(1)}, u32[]{:S(2)}, u32[]{:S(2)}) collective-permute-start(bf16[4,4,400,128]{3,2,1,0:T(8,128)(2,1)S(1)} %get-tuple-element.30), channel_id=1, source_target_pairs={{0,1},{1,0},{2,3},{3,2},{4,5},{5,4},{6,7},{7,6},{8,9},{9,8},{10,11... | collective-permute-start | bytes 4915208 | tf_op jit(solution)/shard_map/ppermute | solution.py:285
  26.2 4.6 %collective-permute-start.3 = (bf16[4,4,192,128]{3,2,1,0:T(8,128)(2,1)S(1)}, bf16[4,4,192,128]{3,2,1,0:T(8,128)(2,1)S(1)}, u32[]{:S(2)}, u32[]{:S(2)}) collective-permute-start(bf16[4,4,192,128]{3,2,1,0:T(8,128)(2,1)S(1)} %get-tuple-element.32), channel_id=1, source_target_pairs={{0,1},{1,0},{2,3},{3,2},{4,5},{5,4},{6,7},{7,6},{8,9},{9,8},{10,11... | collective-permute-start | bytes 2359304 | tf_op jit(solution)/shard_map/ppermute | solution.py:285
  31.2 30.6 %collective-permute-start.4 = (bf16[4,400,128]{2,1,0:T(8,128)(2,1)S(1)}, bf16[4,400,128]{2,1,0:T(8,128)(2,1)S(1)}, u32[]{:S(2)}, u32[]{:S(2)}) collective-permute-start(bf16[4,400,128]{2,1,0:T(8,128)(2,1)S(1)} %get-tuple-element.34), channel_id=1, source_target_pairs={{0,2},{1,3},{2,0},{3,1},{4,6},{5,7},{6,4},{7,5},{8,10},{9,11},{10,... | collective-permute-start | bytes 1228808 | tf_op jit(solution)/shard_map/ppermute | solution.py:285
  33.2 28.7 %collective-permute-start.5 = (bf16[4,400,128]{2,1,0:T(8,128)(2,1)S(1)}, bf16[4,400,128]{2,1,0:T(8,128)(2,1)S(1)}, u32[]{:S(2)}, u32[]{:S(2)}) collective-permute-start(bf16[4,400,128]{2,1,0:T(8,128)(2,1)S(1)} %get-tuple-element.35), channel_id=1, source_target_pairs={{0,4},{1,5},{2,6},{3,7},{4,0},{5,1},{6,2},{7,3},{8,12},{9,13},{10,... | collective-permute-start | bytes 1228808 | tf_op jit(solution)/shard_map/ppermute | solution.py:285
  35.6 26.3 %collective-permute-start.6 = (bf16[4,400,128]{2,1,0:T(8,128)(2,1)S(1)}, bf16[4,400,128]{2,1,0:T(8,128)(2,1)S(1)}, u32[]{:S(2)}, u32[]{:S(2)}) collective-permute-start(bf16[4,400,128]{2,1,0:T(8,128)(2,1)S(1)} %get-tuple-element.36), channel_id=1, source_target_pairs={{0,6},{1,7},{2,4},{3,5},{4,2},{5,3},{6,0},{7,1},{8,14},{9,15},{10,... | collective-permute-start | bytes 1228808 | tf_op jit(solution)/shard_map/ppermute | solution.py:285
  35.6 14.5 %collective-permute-start.8 = (bf16[4,192,128]{2,1,0:T(8,128)(2,1)S(1)}, bf16[4,192,128]{2,1,0:T(8,128)(2,1)S(1)}, u32[]{:S(2)}, u32[]{:S(2)}) collective-permute-start(bf16[4,192,128]{2,1,0:T(8,128)(2,1)S(1)} %get-tuple-element.37), channel_id=1, source_target_pairs={{0,16},{1,17},{2,18},{3,19},{4,20},{5,21},{6,22},{7,23},{8,24},{9,... | collective-permute-start | bytes 589832 | tf_op jit(solution)/shard_map/ppermute | solution.py:285
  40.3 13.5 %collective-permute-start.9 = (bf16[4,192,128]{2,1,0:T(8,128)(2,1)S(1)}, bf16[4,192,128]{2,1,0:T(8,128)(2,1)S(1)}, u32[]{:S(2)}, u32[]{:S(2)}) collective-permute-start(bf16[4,192,128]{2,1,0:T(8,128)(2,1)S(1)} %get-tuple-element.38), channel_id=1, source_target_pairs={{0,24},{1,25},{2,26},{3,27},{4,28},{5,29},{6,30},{7,31},{8,0},{9,1... | collective-permute-start | bytes 589832 | tf_op jit(solution)/shard_map/ppermute | solution.py:285
  50.1 11.6 %collective-permute-start.7 = (bf16[4,192,128]{2,1,0:T(8,128)(2,1)S(1)}, bf16[4,192,128]{2,1,0:T(8,128)(2,1)S(1)}, u32[]{:S(2)}, u32[]{:S(2)}) collective-permute-start(bf16[4,192,128]{2,1,0:T(8,128)(2,1)S(1)} %get-tuple-element.33.refs_2_), channel_id=1, source_target_pairs={{0,8},{1,9},{2,10},{3,11},{4,12},{5,13},{6,14},{7,15},{8,16},{9,17... | collective-permute-start | bytes 589832 | tf_op jit(solution)/shard_map/ppermute | solution.py:285
  62.1 13.0 %collective-permute-start.10 = (bf16[400,128]{1,0:T(8,128)(2,1)S(1)}, bf16[400,128]{1,0:T(8,128)(2,1)S(1)}, u32[]{:S(2)}, u32[]{:S(2)}) collective-permute-start(bf16[400,128]{1,0:T(8,128)(2,1)S(1)} %get-tuple-element.41), channel_id=1, source_target_pairs={{0,8},{1,9},{2,10},{3,11},{4,12},{5,13},{6,14},{7,15},{8,16},{9,17... | collective-permute-start | bytes 307208 | tf_op jit(solution)/shard_map/ppermute | solution.py:285
  62.2 12.9 %collective-permute-start.11 = (bf16[400,128]{1,0:T(8,128)(2,1)S(1)}, bf16[400,128]{1,0:T(8,128)(2,1)S(1)}, u32[]{:S(2)}, u32[]{:S(2)}) collective-permute-start(bf16[400,128]{1,0:T(8,128)(2,1)S(1)} %get-tuple-element.42), channel_id=1, source_target_pairs={{0,16},{1,17},{2,18},{3,19},{4,20},{5,21},{6,22},{7,23},{8,24},{9,... | collective-permute-start | bytes 307208 | tf_op jit(solution)/shard_map/ppermute | solution.py:285
  64.5 10.6 %collective-permute-start.12 = (bf16[400,128]{1,0:T(8,128)(2,1)S(1)}, bf16[400,128]{1,0:T(8,128)(2,1)S(1)}, u32[]{:S(2)}, u32[]{:S(2)}) collective-permute-start(bf16[400,128]{1,0:T(8,128)(2,1)S(1)} %get-tuple-element.43), channel_id=1, source_target_pairs={{0,24},{1,25},{2,26},{3,27},{4,28},{5,29},{6,30},{7,31},{8,0},{9,1... | collective-permute-start | bytes 307208 | tf_op jit(solution)/shard_map/ppermute | solution.py:285
  66.0 4.1 %collective-permute-start.13 = (bf16[192,128]{1,0:T(8,128)(2,1)S(1)}, bf16[192,128]{1,0:T(8,128)(2,1)S(1)}, u32[]{:S(2)}, u32[]{:S(2)}) collective-permute-start(bf16[192,128]{1,0:T(8,128)(2,1)S(1)} %get-tuple-element.44), channel_id=1, source_target_pairs={{0,2},{1,3},{2,0},{3,1},{4,6},{5,7},{6,4},{7,5},{8,10},{9,11},{10,... | collective-permute-start | bytes 147464 | tf_op jit(solution)/shard_map/ppermute | solution.py:285
  67.5 4.1 %collective-permute-start.14 = (bf16[192,128]{1,0:T(8,128)(2,1)S(1)}, bf16[192,128]{1,0:T(8,128)(2,1)S(1)}, u32[]{:S(2)}, u32[]{:S(2)}) collective-permute-start(bf16[192,128]{1,0:T(8,128)(2,1)S(1)} %get-tuple-element.45), channel_id=1, source_target_pairs={{0,4},{1,5},{2,6},{3,7},{4,0},{5,1},{6,2},{7,3},{8,12},{9,13},{10,... | collective-permute-start | bytes 147464 | tf_op jit(solution)/shard_map/ppermute | solution.py:285
  70.1 5.0 %collective-permute-start.15 = (bf16[192,128]{1,0:T(8,128)(2,1)S(1)}, bf16[192,128]{1,0:T(8,128)(2,1)S(1)}, u32[]{:S(2)}, u32[]{:S(2)}) collective-permute-start(bf16[192,128]{1,0:T(8,128)(2,1)S(1)} %get-tuple-element.46), channel_id=1, source_target_pairs={{0,6},{1,7},{2,4},{3,5},{4,2},{5,3},{6,0},{7,1},{8,14},{9,15},{10,... | collective-permute-start | bytes 147464 | tf_op jit(solution)/shard_map/ppermute | solution.py:285

commit v3 on v2

v3 whole, which is shorter than its diff:
```python
import functools

import jax
import jax.numpy as jnp
from jax import lax
from jax.experimental import pallas as pl
from jax.experimental.pallas import tpu as pltpu
from jax.sharding import PartitionSpec as P

LANES = 128
VMEM_BYTES = 24 * 1024 * 1024
ADD_BYTES = 8 * 1024 * 1024
NN = (((1,), (0,)), ((), ()))
NT = (((1,), (1,)), ((), ()))
TN = (((0,), (0,)), ((), ()))


def dot(left, right, dims):
    return lax.dot_general(left, right, dims, preferred_element_type=jnp.float32)


def held(arrays, space=pltpu.VMEM):
    return [pltpu.with_memory_space_constraint(x, space) for x in arrays]


def shifted(x, axis, by):
    count = lax.axis_size(axis)
    pairs = [(i, i + by) for i in range(count) if 0 <= i + by < count]
    return lax.ppermute(x, axis, pairs)


def column(row, rows):
    return jnp.broadcast_to(row, (LANES, rows)).T


def cost(flops, moved):
    return pl.CostEstimate(flops=flops, bytes_accessed=moved, transcendentals=0)


def pack_kernel(head_x, tail_x, head_gs, head_gk, weight, to_next, to_prev):
    halo, channels = tail_x.shape
    to_next[...] = tail_x[...]
    by_row = column(weight[...], LANES)[:halo]
    by_row = jnp.concatenate([by_row] * (channels // LANES), axis=1)
    to_prev[0:halo] = head_x[...]
    to_prev[halo : 2 * halo] = (head_gs[...].astype(jnp.float32) * by_row).astype(jnp.bfloat16)
    to_prev[2 * halo : 3 * halo] = (head_gk[...].astype(jnp.float32) * by_row).astype(jnp.bfloat16)


def pack(halo, x, grad_stream_out, grad_skip_out, weight):
    length, channels = x.shape
    first = pl.BlockSpec((halo, channels), lambda i: (0, 0))
    last = pl.BlockSpec((halo, channels), lambda i: (length // halo - 1, 0))
    return pl.pallas_call(
        pack_kernel,
        grid=(1,),
        in_specs=[first, last, first, first, pl.BlockSpec((1, LANES), lambda i: (0, 0))],
        out_specs=[
            pl.BlockSpec((halo, channels), lambda i: (0, 0)),
            pl.BlockSpec((3 * halo, channels), lambda i: (0, 0)),
        ],
        out_shape=[
            jax.ShapeDtypeStruct((halo, channels), jnp.bfloat16),
            jax.ShapeDtypeStruct((3 * halo, channels), jnp.bfloat16),
        ],
        compiler_params=pltpu.CompilerParams(vmem_limit_bytes=ADD_BYTES),
        name="pack_borders",
    )(*held((x, x, grad_stream_out, grad_skip_out, weight), pltpu.HBM))


def load_kernel(
    x, gs, gk, weight, conv_w, out_w, _, x_here, grad_stream, grad_skip, sums, conv_here, out_here,
    gs_raw, gk_raw, weight_here, sems,
):
    pairs = ((weight, weight_here), (gs, gs_raw), (gk, gk_raw), (x, x_here), (conv_w, conv_here), (out_w, out_here))
    copies = [pltpu.make_async_copy(a, b, sems.at[i]) for i, (a, b) in enumerate(pairs)]
    for copy in copies:
        copy.start()
    for copy in copies[:3]:
        copy.wait()
    length, channels = x_here.shape
    by_row = column(weight_here[...], length)
    by_row = jnp.concatenate([by_row] * (channels // LANES), axis=1)
    grad_stream[...] = gs_raw[...].astype(jnp.float32) * by_row
    grad_skip[...] = (gk_raw[...].astype(jnp.float32) * by_row).astype(jnp.bfloat16)
    own_sum = jnp.broadcast_to(jnp.sum(weight_here[...], axis=1, keepdims=True), (1, LANES))
    sums[...] = split_rows(own_sum)
    for copy in copies[3:]:
        copy.wait()


def load_all(x, gs, gk, weight, conv_w, out_w, after):
    shape = x.shape
    vmem, anywhere = pl.BlockSpec(memory_space=pltpu.VMEM), pl.BlockSpec(memory_space=pl.ANY)
    return pl.pallas_call(
        load_kernel,
        in_specs=[anywhere] * 7,
        out_specs=[vmem] * 6,
        out_shape=[
            pltpu.VMEM(shape, jnp.bfloat16),
            pltpu.VMEM(shape, jnp.float32),
            pltpu.VMEM(shape, jnp.bfloat16),
            pltpu.VMEM((16, LANES), jnp.bfloat16),
            pltpu.VMEM(conv_w.shape, jnp.bfloat16),
            pltpu.VMEM(out_w.shape, jnp.bfloat16),
        ],
        scratch_shapes=[
            pltpu.VMEM(shape, jnp.bfloat16),
            pltpu.VMEM(shape, jnp.bfloat16),
            pltpu.VMEM(weight.shape, jnp.float32),
            pltpu.SemaphoreType.DMA((6,)),
        ],
        compiler_params=pltpu.CompilerParams(vmem_limit_bytes=ADD_BYTES),
        cost_estimate=cost(10**7, 6 * 10**6),
        name="load_all",
    )(*held((x, gs, gk, weight, conv_w, out_w), pltpu.HBM), *held([after]))


def split_rows(total):
    high = total.astype(jnp.bfloat16).astype(jnp.float32)
    middle = (total - high).astype(jnp.bfloat16).astype(jnp.float32)
    low = total - high - middle
    row = lax.broadcasted_iota(jnp.int32, (16, LANES), 0)
    rows = jnp.where(row == 0, high, jnp.where(row == 1, middle, jnp.where(row == 2, low, 0.0)))
    return rows.astype(jnp.bfloat16)


def joined_rows(rows):
    return jnp.sum(rows.astype(jnp.float32), axis=0, keepdims=True)


def backward(plan, layers, refs_of, conv_w, out_w, grad_proj, grad_stream, past_part, total, grad_parts):
    halo, length, channels = plan["halo"], plan["length"], plan["channels"]
    own = slice(halo, halo + length)
    for place, index in enumerate(layers):
        dilation, count = 2**index, plan["counts"][index]
        operands, factors, gates = refs_of(index)
        grad_proj[0:count, :channels] = grad_stream[0:count].astype(jnp.bfloat16)
        grad_gated = dot(grad_proj[0:count], out_w[index], NT)
        total[0:channels] = dot(gates[own], grad_proj[0:length], TN)
        plan["store"](total, channels, place, grad_parts, True)
        both = factors[halo : halo + count]
        grad_preact = jnp.concatenate(
            [grad_gated * both[:, :channels], grad_gated * both[:, channels:]], axis=1
        ).astype(jnp.bfloat16)
        spread = dot(grad_preact, conv_w[index], NT)
        past_part[0:count] = spread[:, channels:]
        rows = plan["counts"][index - 1] if index else length
        grad_stream[0:rows] += spread[0:rows, :channels] + past_part[dilation : dilation + rows]
        total[...] = dot(operands[own], grad_preact[0:length], TN)
        plan["store"](total, 2 * channels, place, grad_parts, False)


def first_kernel(
    plan, prev_x, next_rows, own_x, own_grad, own_skip, conv_w, out_w,
    low_operands, low_factors, low_gates, grad_stream, grad_skip, *rest,
):
    grad_parts = rest[:-7]
    stream, operands, factors, gates, grad_proj, past_part, total = rest[-7:]
    halo, (length, channels) = plan["halo"], own_x.shape
    layers, low = conv_w.shape[0], low_gates.shape[0]
    pad = 2 ** (layers - 1)
    extent = length + 2 * halo
    stream[0:pad] = jnp.zeros((pad, channels), jnp.float32)
    stream[pad : pad + halo] = prev_x[...].astype(jnp.float32)
    stream[pad + halo : pad + halo + length] = own_x[...].astype(jnp.float32)
    stream[pad + halo + length :] = next_rows[0:halo].astype(jnp.float32)

    def refs_of(index):
        if index < low:
            return low_operands.at[index], low_factors.at[index], low_gates.at[index]
        return operands.at[index - low], factors.at[index - low], gates.at[index - low]

    for index in range(layers):
        dilation, start = 2**index, plan["starts"][index]
        operand, factor, gate = refs_of(index)
        operand[start:, :channels] = stream[pad + start :].astype(jnp.bfloat16)
        operand[start:, channels:] = stream[pad + start - dilation : pad + extent - dilation].astype(jnp.bfloat16)
        preact = dot(operand[start:], conv_w[index], NN)
        filtered = jnp.tanh(preact[:, :channels])
        opening = 0.5 + 0.5 * jnp.tanh(0.5 * preact[:, channels:])
        product = filtered * opening
        gate[start:] = product.astype(jnp.bfloat16)
        factor[start:, :channels] = opening - filtered * product
        factor[start:, channels:] = product * (1.0 - opening)
        if index < layers - 1:
            stream[pad + start :] += dot(gate[start:], out_w[index, :, :channels], NN)

    grad_stream[0:length] = own_grad[...]
    grad_stream[length:] = next_rows[halo : 2 * halo].astype(jnp.float32)
    grad_skip[0:length] = own_skip[...]
    grad_skip[length:] = next_rows[2 * halo : 3 * halo]
    grad_proj[:, channels:] = grad_skip[...]
    backward(
        plan, list(reversed(range(low, layers))), refs_of, conv_w, out_w,
        grad_proj, grad_stream, past_part, total, grad_parts,
    )


def second_kernel(
    plan, low_operands, low_factors, low_gates, grad_before, grad_skip, sums, conv_w, out_w, grad_in, *rest
):
    grad_parts = rest[:-4]
    grad_stream, grad_proj, past_part, total = rest[-4:]
    channels, low = plan["channels"], low_gates.shape[0]
    grad_stream[...] = grad_before[...]
    grad_proj[:, channels:] = grad_skip[...]

    def refs_of(index):
        return low_operands.at[index], low_factors.at[index], low_gates.at[index]

    backward(
        plan, list(reversed(range(low))), refs_of, conv_w, out_w, grad_proj, grad_stream, past_part, total, grad_parts
    )
    grad_in[...] = grad_stream[0 : plan["length"]]
    plan["finish"](sums, grad_parts)


def store_whole(total, height, place, grad_parts, is_out):
    grad_parts[int(is_out)][place] = total[0:height].astype(jnp.bfloat16)


def finish_whole(sums, grad_parts):
    pass


def finish_shards(sums, grad_parts):
    for part in grad_parts:
        for a in range(part.shape[0]):
            for b in range(part.shape[1]):
                for c in range(part.shape[2]):
                    part[a, b, c, part.shape[3] - 16 :] = sums[...]


def lead_of_high(place, x, y, z):
    return z, x, y


def lead_of_low(half, place, x, y, z):
    return (x, y, z) if place < half else (y, x, z)


def store_shards(tm, dp, lead_of, total, height, place, grad_parts, is_out):
    keep, send = grad_parts
    t_at, d_at = lax.axis_index("tm"), lax.axis_index("dp")
    x_at, y_at, z_at, core_at = lax.rem(t_at, 2), lax.div(d_at, 2), lax.div(t_at, 2), lax.rem(d_at, 2)
    channels = total.shape[0] // 2
    depth, rows = tm // 2, height // tm
    at = pl.ds(place * 3 * channels // tm + (2 * channels // tm if is_out else 0), rows)
    for y in range(dp // 2):
        near = total[0:height, (2 * y) * LANES : (2 * y + 1) * LANES]
        far = total[0:height, (2 * y + 1) * LANES : (2 * y + 2) * LANES]
        mine = jnp.where(core_at == 0, near, far).astype(jnp.bfloat16)
        other = jnp.where(core_at == 0, far, near).astype(jnp.bfloat16)
        y_off = lax.rem(y - y_at + dp // 2, dp // 2)
        for t in range(tm):
            z, x = divmod(t, 2)
            lead = lead_of(place, lax.rem(x - x_at + 2, 2), y_off, lax.rem(z - z_at + depth, depth))
            keep[lead[0], lead[1], lead[2], at] = mine[t * rows : (t + 1) * rows]
            send[lead[0], lead[1], lead[2], at] = other[t * rows : (t + 1) * rows]


def run_layers(in_shards, tm, dp, halo, prev_x, next_rows, loaded):
    own_x, own_grad, own_skip, sums, conv_w, out_w = loaded
    length, channels = own_x.shape
    layers = conv_w.shape[0]
    low = layers - layers // 3
    extent = length + 2 * halo
    starts = []
    for index in range(layers):
        need = halo if index == layers - 1 else 2 ** (index + 1)
        starts.append(need // 16 * 16)
    counts = [-(-(length + 2 ** (index + 1) - 1) // 16) * 16 for index in range(layers)]
    plan = {"halo": halo, "starts": starts, "counts": counts, "length": length, "channels": channels}
    if in_shards:
        rows = 3 * channels // tm
        high_plan = plan | {"store": functools.partial(store_shards, tm, dp, lead_of_high)}
        low_plan = plan | {
            "store": functools.partial(store_shards, tm, dp, functools.partial(lead_of_low, low // 2)),
            "finish": finish_shards,
        }
        high_shapes = 2 * [(tm // 2, 2, dp // 2, (layers - low) * rows, LANES)]
        low_shapes = 2 * [(2, 2, tm // 2, low * rows + 16, LANES)]
    else:
        high_plan = plan | {"store": store_whole}
        low_plan = high_plan | {"finish": finish_whole}
        high_shapes = [(layers - low,) + conv_w.shape[1:], (layers - low,) + out_w.shape[1:]]
        low_shapes = [(low,) + conv_w.shape[1:], (low,) + out_w.shape[1:]]
    vmem = pl.BlockSpec(memory_space=pltpu.VMEM)
    weight_bytes = 2 * (conv_w.size + out_w.size)
    flops = 2 * length * channels * channels
    border = length + halo
    *kept, grad_stream, grad_skip, a, b = pl.pallas_call(
        functools.partial(first_kernel, high_plan),
        in_specs=[vmem] * 7,
        out_specs=[vmem] * 7,
        out_shape=[
            pltpu.VMEM((low, extent, 2 * channels), jnp.bfloat16),
            pltpu.VMEM((low, extent, 2 * channels), jnp.float32),
            pltpu.VMEM((low, extent, channels), jnp.bfloat16),
            pltpu.VMEM((border, channels), jnp.float32),
            pltpu.VMEM((border, channels), jnp.bfloat16),
        ]
        + [pltpu.VMEM(shape, jnp.bfloat16) for shape in high_shapes],
        scratch_shapes=[
            pltpu.VMEM((2 ** (layers - 1) + extent, channels), jnp.float32),
            pltpu.VMEM((layers - low, extent, 2 * channels), jnp.bfloat16),
            pltpu.VMEM((layers - low, extent, 2 * channels), jnp.float32),
            pltpu.VMEM((layers - low, extent, channels), jnp.bfloat16),
            pltpu.VMEM((border, 2 * channels), jnp.bfloat16),
            pltpu.VMEM((border, channels), jnp.float32),
            pltpu.VMEM((2 * channels, 2 * channels), jnp.float32),
        ],
        compiler_params=pltpu.CompilerParams(vmem_limit_bytes=VMEM_BYTES),
        cost_estimate=cost(flops * (5 * layers + 12 * (layers - low)), weight_bytes),
        name="forward_and_last_layers",
    )(*held((prev_x, next_rows, own_x, own_grad, own_skip, conv_w, out_w)))
    grad_in, *rest = pl.pallas_call(
        functools.partial(second_kernel, low_plan),
        in_specs=[vmem] * 8,
        out_specs=[vmem] * 3,
        out_shape=[pltpu.VMEM((length, channels), jnp.float32)]
        + [pltpu.VMEM(shape, jnp.bfloat16) for shape in low_shapes],
        scratch_shapes=[
            pltpu.VMEM((border, channels), jnp.float32),
            pltpu.VMEM((border, 2 * channels), jnp.bfloat16),
            pltpu.VMEM((border, channels), jnp.float32),
            pltpu.VMEM((2 * channels, 2 * channels), jnp.float32),
        ],
        compiler_params=pltpu.CompilerParams(vmem_limit_bytes=VMEM_BYTES),
        cost_estimate=cost(flops * 12 * low, weight_bytes),
        name="first_layers",
    )(*held((*kept, grad_stream, grad_skip, sums, conv_w, out_w)))
    return grad_in, (a, b), rest


def add_kernel(count, groups, *refs):
    arrays, outs = refs[:count], refs[-len(groups) :]
    for out, pieces in zip(outs, groups):
        lead = (slice(None),) * (len(out.shape) - 2)
        for first, rows, with_total, terms in pieces:
            body = rows - 16 if with_total else rows
            value = 0.0
            for array, at, begin in terms:
                value = value + arrays[array][at + lead + (slice(begin, begin + body),)].astype(jnp.float32)
            out[lead + (slice(first, first + body),)] = value.astype(out.dtype)
            if with_total:
                total = 0.0
                for array, at, begin in terms:
                    rows_at = slice(begin + body, begin + rows)
                    total = total + joined_rows(arrays[array][at + (0,) * len(lead) + (rows_at,)])
                slab = split_rows(total)
                out[lead + (slice(first + body, first + rows),)] = jnp.broadcast_to(slab, out.shape[:-2] + slab.shape)


def add_up(arrays, groups, shapes, after, name):
    vmem = pl.BlockSpec(memory_space=pltpu.VMEM)
    return pl.pallas_call(
        functools.partial(add_kernel, len(arrays), groups),
        in_specs=[vmem] * len(arrays) + [pl.BlockSpec(memory_space=pl.ANY)] * len(after),
        out_specs=[vmem] * len(groups),
        out_shape=[pltpu.VMEM(shape, jnp.bfloat16) for shape in shapes],
        compiler_params=pltpu.CompilerParams(vmem_limit_bytes=ADD_BYTES),
        name=name,
    )(*held(arrays), *held(after))


def last_kernel(low_count, high_count, samples_all, low, *refs):
    low_parts, refs = refs[:low_count], refs[low_count:]
    high_parts, refs = refs[:high_count], refs[high_count:]
    grad_in, grad_inputs, grad_conv, grad_out = refs
    layers, conv_rows, _ = grad_conv.shape
    out_rows = grad_out.shape[1]
    rows = conv_rows + out_rows
    total = 0.0
    for part in low_parts:
        total = total + joined_rows(part[low * rows :])
    scale = samples_all / total
    for index in range(layers):
        parts, place = (low_parts, low - 1 - index) if index < low else (high_parts, layers - 1 - index)
        for out, at in ((grad_conv, 0), (grad_out, conv_rows)):
            first = place * rows + at
            value = 0.0
            for part in parts:
                value = value + part[first : first + out.shape[1]].astype(jnp.float32)
            out[index] = value * scale
    for first in range(0, grad_in.shape[1], LANES):
        grad_inputs[:, first : first + LANES] = grad_in[:, first : first + LANES] * scale


def reduce_shards(tm, dp, layers, high_parts, low_parts):
    depth, wide = tm // 2, dp // 2
    axes = ("tm", "dp")

    def moved(x, core=0, xs=0, ys=0, zs=0):
        pairs = []
        for t in range(tm):
            for d in range(dp):
                z, a = divmod(t, 2)
                y, c = divmod(d, 2)
                to_t = (z + zs) % depth * 2 + (a + xs) % 2
                to_d = (y + ys) % wide * 2 + (c + core) % 2
                pairs.append((t * dp + d, to_t * dp + to_d))
        return lax.ppermute(x, axes, pairs)

    (keep_high, send_high), (keep_low, send_low) = high_parts, low_parts
    high_rows, low_rows = keep_high.shape[3], keep_low.shape[3]
    half = (low_rows - 16) // 2
    steps_z = range(1, depth)
    steps_p = [(x, y) for x in range(2) for y in range(wide)][1:]

    high_there = moved(send_high, core=1)
    low_there = moved(send_low, core=1)
    high_first = add_up(
        [keep_high, high_there], [[(0, high_rows, False, [(0, (r,), 0), (1, (r,), 0)])] for r in steps_z],
        [keep_high.shape[1:]] * len(steps_z), [], "add_last_cores",
    )
    high_z = [moved(x, zs=r) for x, r in zip(high_first, steps_z)]
    a_rows, b_rows = half, low_rows - half
    send_a, send_b = add_up(
        [keep_low, low_there],
        [
            [(0, a_rows, False, [(0, (1,), 0), (1, (1,), 0)])],
            [(0, b_rows, True, [(0, (1,), half), (1, (1,), half)])],
        ],
        [(2, depth, a_rows, LANES), (2, depth, b_rows, LANES)], high_first[:1], "add_first_cores",
    )
    a_x, b_y = moved(send_a, xs=1), moved(send_b, ys=1)
    send_a, send_b = add_up(
        [keep_low, low_there, a_x, b_y],
        [
            [(0, a_rows, False, [(0, (0, 1), 0), (1, (0, 1), 0), (2, (1,), 0)])],
            [(0, b_rows, True, [(0, (0, 1), half), (1, (0, 1), half), (3, (1,), 0)])],
        ],
        [(depth, a_rows, LANES), (depth, b_rows, LANES)], [], "add_first_halves",
    )
    a_y, b_x = moved(send_a, ys=1), moved(send_b, xs=1)
    high_second = add_up(
        [keep_high, high_there] + high_z,
        [
            [(0, high_rows, False, [(0, (0, x, y), 0), (1, (0, x, y), 0)] + [(2 + i, (x, y), 0) for i in range(len(high_z))])]
            for x, y in [(0, 0)] + steps_p
        ],
        [(high_rows, LANES)] * (2 * wide), [send_a], "add_last_along",
    )
    high_p = [moved(v, xs=x, ys=y) for v, (x, y) in zip(high_second[1:], steps_p)]
    low_third = add_up(
        [keep_low, low_there, a_x, b_y, a_y, b_x],
        [
            [
                (0, a_rows, False, [(0, (0, 0, r), 0), (1, (0, 0, r), 0), (2, (0, r), 0), (4, (r,), 0)]),
                (half, b_rows, True, [(0, (0, 0, r), half), (1, (0, 0, r), half), (3, (0, r), 0), (5, (r,), 0)]),
            ]
            for r in range(depth)
        ],
        [(low_rows, LANES)] * depth, high_second[:1], "add_first_quarters",
    )
    low_z = [moved(v, zs=r) for v, r in zip(low_third[1:], steps_z)]
    return [low_third[0]] + low_z, [high_second[0]] + high_p


def scattered(part):
    columns = lax.psum_scatter(part, "dp", scatter_dimension=2, tiled=True).astype(jnp.float32)
    return lax.psum_scatter(columns, "tm", scatter_dimension=1, tiled=True)


def body(inputs, grad_stream_out, grad_skip_out, sample_weight, conv_weight, out_weight):
    tm, dp = lax.axis_size("tm"), lax.axis_size("dp")
    batch, length, channels = inputs.shape
    layers = conv_weight.shape[0]
    low = layers - layers // 3
    halo = 2**layers
    samples_all = batch * length * tm * dp
    x, gs, gk = inputs[0], grad_stream_out[0], grad_skip_out[0]
    to_next, to_prev = pack(halo, x, gs, gk, sample_weight)
    prev_x = shifted(to_next, "tm", 1)
    next_rows = shifted(to_prev, "tm", -1)
    loaded = load_all(x, gs, gk, sample_weight, conv_weight, out_weight, to_next)
    in_shards = dp == 4 and tm % 2 == 0 and channels // tm % 16 == 0 and 2 * channels == dp * LANES and low % 2 == 0
    grad_in, high_parts, low_parts = run_layers(in_shards, tm, dp, halo, prev_x, next_rows, loaded)
    if not in_shards:
        scale = samples_all / lax.psum(jnp.sum(sample_weight), ("tm", "dp"))
        grad_conv, grad_out = (
            scattered(jnp.concatenate([first[::-1], last[::-1]])) * scale for first, last in zip(low_parts, high_parts)
        )
        return (grad_in * scale)[None], grad_conv, grad_out
    low_terms, high_terms = reduce_shards(tm, dp, layers, high_parts, low_parts)
    conv_rows, out_rows = 2 * channels // tm, channels // tm
    grad_inputs, grad_conv, grad_out = pl.pallas_call(
        functools.partial(last_kernel, len(low_terms), len(high_terms), float(samples_all), low),
        out_shape=[
            jax.ShapeDtypeStruct((length, channels), jnp.float32),
            jax.ShapeDtypeStruct((layers, conv_rows, LANES), jnp.float32),
            jax.ShapeDtypeStruct((layers, out_rows, LANES), jnp.float32),
        ],
        compiler_params=pltpu.CompilerParams(vmem_limit_bytes=ADD_BYTES),
        name="scale_all",
    )(*held(low_terms), *held(high_terms), *held([grad_in]))
    return grad_inputs[None], grad_conv, grad_out


def solution(mesh):
    placed = (
        P("dp", "tm", None),
        P("dp", "tm", None),
        P("dp", "tm", None),
        P("dp", "tm"),
        P(),
        P(),
    )
    return jax.shard_map(
        body,
        mesh=mesh,
        in_specs=placed,
        out_specs=(P("dp", "tm", None), P(None, "tm", "dp"), P(None, "tm", "dp")),
        check_vma=False,
    )
```

time: 76.5 us -> 75.5 us (0.987)
  local copies, waits for them, and re-layouts: 7.5 us -> 0 us
  starting transfers between devices: 28.4 us -> 32.3 us
  Pallas kernels: 11.2 us -> 14.2 us
    unnamed x14 -> x0, local copies, waits for them, and re-layouts: 7.5 us -> none
    ppermute x14 -> x15, starting transfers between devices: 21.6 us -> 25.6 us  [moved(): return lax.ppermute(x, axes, pairs)]
    pallas_call x6 -> x9, Pallas kernels: 10.3 us -> 13.2 us  [the longest x1 5.16 us: run_layers(): pl.pallas_call(functools.partial(first_kernel, high_plan), in_specs=[vmem...]
    ppermute x2, waiting for transfers between devices: 1.74 us -> 0.01 us  [shifted(): return lax.ppermute(x, axis, pairs)]
    ppermute x14 -> x15, waiting for transfers between devices: 26.5 us -> 28 us  [moved(): return lax.ppermute(x, axes, pairs)]
  transfers between devices with their start and end apart: 16 -> 17, of which waited for: 7 -> 5; matrix products, arithmetic and copies ran while one was open for 0% -> 0% of each run, Pallas kernels for 0% -> 4%
where the time goes in v3:
time: 75.5 us; the launch traced here: 75.3 us
  starting transfers between devices  32.3 us (43%)
  waiting for transfers between devices  28 us (37%)
  Pallas kernels  14.2 us (19%)
    ppermute x15, waiting for transfers between devices, moved(): return lax.ppermute(x, axes, pairs)  28 us
    ppermute x15, starting transfers between devices, moved(): return lax.ppermute(x, axes, pairs)  25.6 us
    ppermute x2, starting transfers between devices, shifted(): return lax.ppermute(x, axis, pairs)  6.76 us
    pallas_call x1, Pallas kernels, run_layers(): pl.pallas_call(functools.partial(first_kernel, high_plan), in_specs=[vmem...  5.16 us
    pallas_call x1, Pallas kernels, run_layers(): pl.pallas_call(functools.partial(second_kernel, low_plan), in_specs=[vmem...  3.6 us
    pallas_call x1, Pallas kernels, load_all(): pl.pallas_call(load_kernel, in_specs=[anywhere] * 7, out_specs=[vmem] * 6...  2.68 us
  transfers between devices with their start and end apart: 17, of which 5 were waited for; matrix products, arithmetic and copies ran while one was open for 0% of the time, Pallas kernels for 4%

profile of v3, /device:TPU:0, one launch (start us, length us, event | category | flops | bytes accessed | tf_op | source)
XLA Modules:
  0.0 75.3 jit_solution(18123209732747278472)
XLA Ops:
  0.6 0.9 %pack_borders.1 = (bf16[64,256]{1,0:T(8,128)(2,1)S(1)}, bf16[192,256]{1,0:T(8,128)(2,1)S(1)}) custom-call(bf16[512,256]{1,0:T(8,128)(2,1)} %bitcast.4, bf16[512,256]{1,0:T(8,128)(2,1)} %bitcast.5, bf16[512,256]{1,0:T(8,128)(2,1)} %bitcast.7, bf16[512,256]{1,0:T(8,128)(2,1)} %bitcast.9, f32[1,512]{1,0:T(1,128)} %weight.3), custom_call_target="tpu_custom_call" | custom-call | tf_op jit(solution)/shard_map/pack_borders/pallas_call | solution.py:54
  1.5 1.3 %collective-permute-start.1 = (bf16[192,256]{1,0:T(8,128)(2,1)S(1)}, bf16[192,256]{1,0:T(8,128)(2,1)S(1)}, u32[]{:S(2)}, u32[]{:S(2)}) collective-permute-start(bf16[192,256]{1,0:T(8,128)(2,1)S(1)} %get-tuple-element.40), channel_id=1, source_target_pairs={{4,0},{8,4},{12,8},{16,12},{20,16},{24,20},{28,24},{5,1},{9,5},{13... | collective-permute-start | bytes 294920 | tf_op jit(solution)/shard_map/ppermute | solution.py:29
  2.8 5.5 %collective-permute-start = (bf16[64,256]{1,0:T(8,128)(2,1)S(1)}, bf16[64,256]{1,0:T(8,128)(2,1)S(1)}, u32[]{:S(2)}, u32[]{:S(2)}) collective-permute-start(bf16[64,256]{1,0:T(8,128)(2,1)S(1)} %get-tuple-element.39._), channel_id=1, source_target_pairs={{0,4},{4,8},{8,12},{12,16},{16,20},{20,24},{24,28},{1,5},{5,9},{9,... | collective-permute-start | bytes 98312 | tf_op jit(solution)/shard_map/ppermute | solution.py:29
  8.3 2.7 %load_all.1 = (bf16[512,256]{1,0:T(8,128)(2,1)S(1)}, f32[512,256]{1,0:T(8,128)S(1)}, bf16[512,256]{1,0:T(8,128)(2,1)S(1)}, bf16[16,128]{1,0:T(8,128)(2,1)S(1)}, ...) custom-call(bf16[512,256]{1,0:T(8,128)(2,1)} %bitcast.6, bf16[512,256]{1,0:T(8,128)(2,1)} %bitcast.8, ...), custom_call_target="tpu_custom_call" | custom-call | flops 10000000 | bytes 6000000 | tf_op jit(solution)/shard_map/load_all/pallas_call | solution.py:95
  11.0 0.0 collective-permute-done.prev_x
  11.0 0.0 collective-permute-done.1.next_rows
  11.0 5.2 %forward_and_last_layers.1 = (bf16[4,640,512]{2,1,0:T(8,128)(2,1)S(1)}, f32[4,640,512]{2,1,0:T(8,128)S(1)}, bf16[4,640,256]{2,1,0:T(8,128)(2,1)S(1)}, f32[576,25...) custom-call(bf16[64,256]{1,0:T(8,128)(2,1)S(1)} %collective-permute-, ...), custom_call_target="tpu_custom_call" | custom-call | flops 3623878656 | bytes 4718592 | tf_op jit(solution)/shard_map/forward_and_last_layers/pallas_call | solution.py:293
  16.2 3.6 %first_layers.1 = (f32[512,256]{1,0:T(8,128)S(1)}, bf16[2,2,4,400,128]{4,3,2,1,0:T(8,128)(2,1)S(1)}, bf16[2,2,4,400,128]{4,3,2,1,0:T(8,128)(2,1)S(1)}) custom-call(bf16[4,640,512]{2,1,0:T(8,128)(2,1)S(1)} %get-tuple-element.46.low_operands, f32[4,640,512]{2,1,0:T(8,128)S(1)} %get-tuple-element.47.low_factors, ...), custom_call_target="tpu_custom_call" | custom-call | flops 3221225472 | bytes 4718592 | tf_op jit(solution)/shard_map/first_layers/pallas_call | solution.py:318
  19.8 0.1 collective-permute-start.2
  19.9 0.5 collective-permute-start.3
  20.4 4.1 %collective-permute-done.3.refs_1_ = bf16[4,2,2,192,128]{4,3,2,1,0:T(8,128)(2,1)S(1)} collective-permute-done((bf16[4,2,2,192,128]{4,3,2,1,0:T(8,128)(2,1)S(1)}, bf16[4,2,2,192,128]{4,3,2,1,0:T(8,128)(2,1)S(1)}, u32[]{:S(2)}, u32[]{:S(2)}) %collective-permute-start.3) | collective-permute-done | bytes 786464 | tf_op jit(solution)/shard_map/ppermute | solution.py:404
  24.5 0.1 add_last_cores.1
  24.6 0.0 collective-permute-done.2.refs_1_
  24.6 0.2 add_first_cores.1
  24.8 2.1 %collective-permute-start.5 = (bf16[2,4,208,128]{3,2,1,0:T(8,128)(2,1)S(1)}, bf16[2,4,208,128]{3,2,1,0:T(8,128)(2,1)S(1)}, u32[]{:S(2)}, u32[]{:S(2)}) collective-permute-start(bf16[2,4,208,128]{3,2,1,0:T(8,128)(2,1)S(1)} %get-tuple-element.58), channel_id=1, source_target_pairs={{0,2},{1,3},{2,0},{3,1},{4,6},{5,7},{6,4},{7,5},{8,10},{9,11},{10,... | collective-permute-start | bytes 1277960 | tf_op jit(solution)/shard_map/ppermute | solution.py:404
  27.0 2.4 %collective-permute-start.4 = (bf16[2,4,192,128]{3,2,1,0:T(8,128)(2,1)S(1)}, bf16[2,4,192,128]{3,2,1,0:T(8,128)(2,1)S(1)}, u32[]{:S(2)}, u32[]{:S(2)}) collective-permute-start(bf16[2,4,192,128]{3,2,1,0:T(8,128)(2,1)S(1)} %get-tuple-element.57), channel_id=1, source_target_pairs={{0,4},{1,5},{2,6},{3,7},{4,0},{5,1},{6,2},{7,3},{8,12},{9,13},{10,... | collective-permute-start | bytes 1179656 | tf_op jit(solution)/shard_map/ppermute | solution.py:404
  29.3 9.1 %collective-permute-done.4.refs_2_ = bf16[2,4,192,128]{3,2,1,0:T(8,128)(2,1)S(1)} collective-permute-done((bf16[2,4,192,128]{3,2,1,0:T(8,128)(2,1)S(1)}, bf16[2,4,192,128]{3,2,1,0:T(8,128)(2,1)S(1)}, u32[]{:S(2)}, u32[]{:S(2)}) %collective-permute-start.4) | collective-permute-done | bytes 393248 | tf_op jit(solution)/shard_map/ppermute | solution.py:404
  38.5 0.0 collective-permute-done.5.refs_3_
  38.5 0.2 add_first_halves.1
  38.6 1.8 %collective-permute-start.7 = (bf16[4,208,128]{2,1,0:T(8,128)(2,1)S(1)}, bf16[4,208,128]{2,1,0:T(8,128)(2,1)S(1)}, u32[]{:S(2)}, u32[]{:S(2)}) collective-permute-start(bf16[4,208,128]{2,1,0:T(8,128)(2,1)S(1)} %get-tuple-element.60), channel_id=1, source_target_pairs={{0,4},{1,5},{2,6},{3,7},{4,0},{5,1},{6,2},{7,3},{8,12},{9,13},{10,... | collective-permute-start | bytes 638984 | tf_op jit(solution)/shard_map/ppermute | solution.py:404
  40.5 2.6 %collective-permute-start.9 = (bf16[2,2,192,128]{3,2,1,0:T(8,128)(2,1)S(1)}, bf16[2,2,192,128]{3,2,1,0:T(8,128)(2,1)S(1)}, u32[]{:S(2)}, u32[]{:S(2)}) collective-permute-start(bf16[2,2,192,128]{3,2,1,0:T(8,128)(2,1)S(1)} %get-tuple-element.61), channel_id=1, source_target_pairs={{0,16},{1,17},{2,18},{3,19},{4,20},{5,21},{6,22},{7,23},{8,24},{9,... | collective-permute-start | bytes 589832 | tf_op jit(solution)/shard_map/ppermute | solution.py:404
  43.0 1.4 %collective-permute-start.10 = (bf16[2,2,192,128]{3,2,1,0:T(8,128)(2,1)S(1)}, bf16[2,2,192,128]{3,2,1,0:T(8,128)(2,1)S(1)}, u32[]{:S(2)}, u32[]{:S(2)}) collective-permute-start(bf16[2,2,192,128]{3,2,1,0:T(8,128)(2,1)S(1)} %get-tuple-element.62), channel_id=1, source_target_pairs={{0,24},{1,25},{2,26},{3,27},{4,28},{5,29},{6,30},{7,31},{8,0},{9,1... | collective-permute-start | bytes 589832 | tf_op jit(solution)/shard_map/ppermute | solution.py:404
  44.4 0.7 collective-permute-start.8
  45.1 1.0 %collective-permute-start.6 = (bf16[4,192,128]{2,1,0:T(8,128)(2,1)S(1)}, bf16[4,192,128]{2,1,0:T(8,128)(2,1)S(1)}, u32[]{:S(2)}, u32[]{:S(2)}) collective-permute-start(bf16[4,192,128]{2,1,0:T(8,128)(2,1)S(1)} %get-tuple-element.59.refs_5_), channel_id=1, source_target_pairs={{0,2},{1,3},{2,0},{3,1},{4,6},{5,7},{6,4},{7,5},{8,10},{9,11},{10,... | collective-permute-start | bytes 589832 | tf_op jit(solution)/shard_map/ppermute | solution.py:404
  46.0 10.4 %collective-permute-done.9.refs_3_ = bf16[2,2,192,128]{3,2,1,0:T(8,128)(2,1)S(1)} collective-permute-done((bf16[2,2,192,128]{3,2,1,0:T(8,128)(2,1)S(1)}, bf16[2,2,192,128]{3,2,1,0:T(8,128)(2,1)S(1)}, u32[]{:S(2)}, u32[]{:S(2)}) %collective-permute-start.9) | collective-permute-done | bytes 196640 | tf_op jit(solution)/shard_map/ppermute | solution.py:404
  56.5 0.0 collective-permute-done.10.refs_4_
  56.5 0.0 collective-permute-done.8.refs_2_
  56.5 0.1 add_last_along.1
  56.6 0.0 collective-permute-done.6.refs_4_
  56.6 0.0 collective-permute-done.7.refs_5_
  56.6 0.2 add_first_quarters.1
  56.9 3.7 %collective-permute-start.11 = (bf16[400,128]{1,0:T(8,128)(2,1)S(1)}, bf16[400,128]{1,0:T(8,128)(2,1)S(1)}, u32[]{:S(2)}, u32[]{:S(2)}) collective-permute-start(bf16[400,128]{1,0:T(8,128)(2,1)S(1)} %get-tuple-element.65), channel_id=1, source_target_pairs={{0,8},{1,9},{2,10},{3,11},{4,12},{5,13},{6,14},{7,15},{8,16},{9,17... | collective-permute-start | bytes 307208 | tf_op jit(solution)/shard_map/ppermute | solution.py:404
  60.5 1.9 %collective-permute-start.12 = (bf16[400,128]{1,0:T(8,128)(2,1)S(1)}, bf16[400,128]{1,0:T(8,128)(2,1)S(1)}, u32[]{:S(2)}, u32[]{:S(2)}) collective-permute-start(bf16[400,128]{1,0:T(8,128)(2,1)S(1)} %get-tuple-element.66), channel_id=1, source_target_pairs={{0,16},{1,17},{2,18},{3,19},{4,20},{5,21},{6,22},{7,23},{8,24},{9,... | collective-permute-start | bytes 307208 | tf_op jit(solution)/shard_map/ppermute | solution.py:404
  62.4 2.8 %collective-permute-start.13 = (bf16[400,128]{1,0:T(8,128)(2,1)S(1)}, bf16[400,128]{1,0:T(8,128)(2,1)S(1)}, u32[]{:S(2)}, u32[]{:S(2)}) collective-permute-start(bf16[400,128]{1,0:T(8,128)(2,1)S(1)} %get-tuple-element.67), channel_id=1, source_target_pairs={{0,24},{1,25},{2,26},{3,27},{4,28},{5,29},{6,30},{7,31},{8,0},{9,1... | collective-permute-start | bytes 307208 | tf_op jit(solution)/shard_map/ppermute | solution.py:404
  65.2 1.1 %collective-permute-start.14 = (bf16[192,128]{1,0:T(8,128)(2,1)S(1)}, bf16[192,128]{1,0:T(8,128)(2,1)S(1)}, u32[]{:S(2)}, u32[]{:S(2)}) collective-permute-start(bf16[192,128]{1,0:T(8,128)(2,1)S(1)} %get-tuple-element.68), channel_id=1, source_target_pairs={{0,2},{1,3},{2,0},{3,1},{4,6},{5,7},{6,4},{7,5},{8,10},{9,11},{10,... | collective-permute-start | bytes 147464 | tf_op jit(solution)/shard_map/ppermute | solution.py:404
  66.3 1.6 %collective-permute-start.15 = (bf16[192,128]{1,0:T(8,128)(2,1)S(1)}, bf16[192,128]{1,0:T(8,128)(2,1)S(1)}, u32[]{:S(2)}, u32[]{:S(2)}) collective-permute-start(bf16[192,128]{1,0:T(8,128)(2,1)S(1)} %get-tuple-element.69), channel_id=1, source_target_pairs={{0,4},{1,5},{2,6},{3,7},{4,0},{5,1},{6,2},{7,3},{8,12},{9,13},{10,... | collective-permute-start | bytes 147464 | tf_op jit(solution)/shard_map/ppermute | solution.py:404
  67.9 1.4 %collective-permute-done.14.refs_5_ = bf16[192,128]{1,0:T(8,128)(2,1)S(1)} collective-permute-done((bf16[192,128]{1,0:T(8,128)(2,1)S(1)}, bf16[192,128]{1,0:T(8,128)(2,1)S(1)}, u32[]{:S(2)}, u32[]{:S(2)}) %collective-permute-start.14) | collective-permute-done | bytes 49184 | tf_op jit(solution)/shard_map/ppermute | solution.py:404
  69.3 2.1 %collective-permute-start.16 = (bf16[192,128]{1,0:T(8,128)(2,1)S(1)}, bf16[192,128]{1,0:T(8,128)(2,1)S(1)}, u32[]{:S(2)}, u32[]{:S(2)}) collective-permute-start(bf16[192,128]{1,0:T(8,128)(2,1)S(1)} %get-tuple-element.70), channel_id=1, source_target_pairs={{0,6},{1,7},{2,4},{3,5},{4,2},{5,3},{6,0},{7,1},{8,14},{9,15},{10,... | collective-permute-start | bytes 147464 | tf_op jit(solution)/shard_map/ppermute | solution.py:404
  71.4 0.0 collective-permute-done.15.refs_6_
  71.4 2.9 %collective-permute-done.16.refs_7_ = bf16[192,128]{1,0:T(8,128)(2,1)S(1)} collective-permute-done((bf16[192,128]{1,0:T(8,128)(2,1)S(1)}, bf16[192,128]{1,0:T(8,128)(2,1)S(1)}, u32[]{:S(2)}, u32[]{:S(2)}) %collective-permute-start.16) | collective-permute-done | bytes 49184 | tf_op jit(solution)/shard_map/ppermute | solution.py:404
  74.3 0.0 collective-permute-done.11.refs_1_
  74.3 0.0 collective-permute-done.12.refs_2_
  74.3 0.0 collective-permute-done.13.refs_3_
  74.3 1.0 %scale_all.1 = (f32[512,256]{1,0:T(8,128)}, f32[6,64,128]{2,1,0:T(8,128)}, f32[6,32,128]{2,1,0:T(8,128)}) custom-call(bf16[400,128]{1,0:T(8,128)(2,1)S(1)} %get-tuple-element.64.refs_0_, bf16[400,128]{1,0:T(8,128)(2,1)S(1)} %collective-permute-done.11.refs_1_, bf16[400,128]{1,0:T(8,128)(2,1)S(1)} %collective-permute-done.12.refs_2_, ...), custom_call_target="tpu_custom_call" | custom-call | tf_op jit(solution)/shard_map/scale_all/pallas_call | solution.py:489
Async XLA Ops:
  1.5 9.5 %collective-permute-start.1 = (bf16[192,256]{1,0:T(8,128)(2,1)S(1)}, bf16[192,256]{1,0:T(8,128)(2,1)S(1)}, u32[]{:S(2)}, u32[]{:S(2)}) collective-permute-start(bf16[192,256]{1,0:T(8,128)(2,1)S(1)} %get-tuple-element.40), channel_id=1, source_target_pairs={{4,0},{8,4},{12,8},{16,12},{20,16},{24,20},{28,24},{5,1},{9,5},{13... | collective-permute-start | bytes 294920 | tf_op jit(solution)/shard_map/ppermute | solution.py:29
  2.8 8.2 %collective-permute-start = (bf16[64,256]{1,0:T(8,128)(2,1)S(1)}, bf16[64,256]{1,0:T(8,128)(2,1)S(1)}, u32[]{:S(2)}, u32[]{:S(2)}) collective-permute-start(bf16[64,256]{1,0:T(8,128)(2,1)S(1)} %get-tuple-element.39._), channel_id=1, source_target_pairs={{0,4},{4,8},{8,12},{12,16},{16,20},{20,24},{24,28},{1,5},{5,9},{9,... | collective-permute-start | bytes 98312 | tf_op jit(solution)/shard_map/ppermute | solution.py:29
  19.8 4.8 %collective-permute-start.2 = (bf16[2,2,4,400,128]{4,3,2,1,0:T(8,128)(2,1)S(1)}, bf16[2,2,4,400,128]{4,3,2,1,0:T(8,128)(2,1)S(1)}, u32[]{:S(2)}, u32[]{:S(2)}) collective-permute-start(bf16[2,2,4,400,128]{4,3,2,1,0:T(8,128)(2,1)S(1)} %get-tuple-element.53), channel_id=1, source_target_pairs={{0,1},{1,0},{2,3},{3,2},{4,5},{5,4},{6,7},{7,6},{8,9},{9,8},{10,11... | collective-permute-start | bytes 4915208 | tf_op jit(solution)/shard_map/ppermute | solution.py:404
  19.9 4.6 %collective-permute-start.3 = (bf16[4,2,2,192,128]{4,3,2,1,0:T(8,128)(2,1)S(1)}, bf16[4,2,2,192,128]{4,3,2,1,0:T(8,128)(2,1)S(1)}, u32[]{:S(2)}, u32[]{:S(2)}) collective-permute-start(bf16[4,2,2,192,128]{4,3,2,1,0:T(8,128)(2,1)S(1)} %get-tuple-element.55), channel_id=1, source_target_pairs={{0,1},{1,0},{2,3},{3,2},{4,5},{5,4},{6,7},{7,6},{8,9},{9,8},{10,11... | collective-permute-start | bytes 2359304 | tf_op jit(solution)/shard_map/ppermute | solution.py:404
  24.8 13.6 %collective-permute-start.5 = (bf16[2,4,208,128]{3,2,1,0:T(8,128)(2,1)S(1)}, bf16[2,4,208,128]{3,2,1,0:T(8,128)(2,1)S(1)}, u32[]{:S(2)}, u32[]{:S(2)}) collective-permute-start(bf16[2,4,208,128]{3,2,1,0:T(8,128)(2,1)S(1)} %get-tuple-element.58), channel_id=1, source_target_pairs={{0,2},{1,3},{2,0},{3,1},{4,6},{5,7},{6,4},{7,5},{8,10},{9,11},{10,... | collective-permute-start | bytes 1277960 | tf_op jit(solution)/shard_map/ppermute | solution.py:404
  27.0 11.5 %collective-permute-start.4 = (bf16[2,4,192,128]{3,2,1,0:T(8,128)(2,1)S(1)}, bf16[2,4,192,128]{3,2,1,0:T(8,128)(2,1)S(1)}, u32[]{:S(2)}, u32[]{:S(2)}) collective-permute-start(bf16[2,4,192,128]{3,2,1,0:T(8,128)(2,1)S(1)} %get-tuple-element.57), channel_id=1, source_target_pairs={{0,4},{1,5},{2,6},{3,7},{4,0},{5,1},{6,2},{7,3},{8,12},{9,13},{10,... | collective-permute-start | bytes 1179656 | tf_op jit(solution)/shard_map/ppermute | solution.py:404
  38.6 18.0 %collective-permute-start.7 = (bf16[4,208,128]{2,1,0:T(8,128)(2,1)S(1)}, bf16[4,208,128]{2,1,0:T(8,128)(2,1)S(1)}, u32[]{:S(2)}, u32[]{:S(2)}) collective-permute-start(bf16[4,208,128]{2,1,0:T(8,128)(2,1)S(1)} %get-tuple-element.60), channel_id=1, source_target_pairs={{0,4},{1,5},{2,6},{3,7},{4,0},{5,1},{6,2},{7,3},{8,12},{9,13},{10,... | collective-permute-start | bytes 638984 | tf_op jit(solution)/shard_map/ppermute | solution.py:404
  40.5 16.0 %collective-permute-start.9 = (bf16[2,2,192,128]{3,2,1,0:T(8,128)(2,1)S(1)}, bf16[2,2,192,128]{3,2,1,0:T(8,128)(2,1)S(1)}, u32[]{:S(2)}, u32[]{:S(2)}) collective-permute-start(bf16[2,2,192,128]{3,2,1,0:T(8,128)(2,1)S(1)} %get-tuple-element.61), channel_id=1, source_target_pairs={{0,16},{1,17},{2,18},{3,19},{4,20},{5,21},{6,22},{7,23},{8,24},{9,... | collective-permute-start | bytes 589832 | tf_op jit(solution)/shard_map/ppermute | solution.py:404
  43.0 13.4 %collective-permute-start.10 = (bf16[2,2,192,128]{3,2,1,0:T(8,128)(2,1)S(1)}, bf16[2,2,192,128]{3,2,1,0:T(8,128)(2,1)S(1)}, u32[]{:S(2)}, u32[]{:S(2)}) collective-permute-start(bf16[2,2,192,128]{3,2,1,0:T(8,128)(2,1)S(1)} %get-tuple-element.62), channel_id=1, source_target_pairs={{0,24},{1,25},{2,26},{3,27},{4,28},{5,29},{6,30},{7,31},{8,0},{9,1... | collective-permute-start | bytes 589832 | tf_op jit(solution)/shard_map/ppermute | solution.py:404
  44.4 12.1 %collective-permute-start.8 = (bf16[2,2,192,128]{3,2,1,0:T(8,128)(2,1)S(1)}, bf16[2,2,192,128]{3,2,1,0:T(8,128)(2,1)S(1)}, u32[]{:S(2)}, u32[]{:S(2)}) collective-permute-start(bf16[2,2,192,128]{3,2,1,0:T(8,128)(2,1)S(1)} %get-tuple-element.56.refs_2_), channel_id=1, source_target_pairs={{0,8},{1,9},{2,10},{3,11},{4,12},{5,13},{6,14},{7,15},{8,16},{9,17... | collective-permute-start | bytes 589832 | tf_op jit(solution)/shard_map/ppermute | solution.py:404
  45.1 11.5 %collective-permute-start.6 = (bf16[4,192,128]{2,1,0:T(8,128)(2,1)S(1)}, bf16[4,192,128]{2,1,0:T(8,128)(2,1)S(1)}, u32[]{:S(2)}, u32[]{:S(2)}) collective-permute-start(bf16[4,192,128]{2,1,0:T(8,128)(2,1)S(1)} %get-tuple-element.59.refs_5_), channel_id=1, source_target_pairs={{0,2},{1,3},{2,0},{3,1},{4,6},{5,7},{6,4},{7,5},{8,10},{9,11},{10,... | collective-permute-start | bytes 589832 | tf_op jit(solution)/shard_map/ppermute | solution.py:404
  56.9 17.4 %collective-permute-start.11 = (bf16[400,128]{1,0:T(8,128)(2,1)S(1)}, bf16[400,128]{1,0:T(8,128)(2,1)S(1)}, u32[]{:S(2)}, u32[]{:S(2)}) collective-permute-start(bf16[400,128]{1,0:T(8,128)(2,1)S(1)} %get-tuple-element.65), channel_id=1, source_target_pairs={{0,8},{1,9},{2,10},{3,11},{4,12},{5,13},{6,14},{7,15},{8,16},{9,17... | collective-permute-start | bytes 307208 | tf_op jit(solution)/shard_map/ppermute | solution.py:404
  60.5 13.8 %collective-permute-start.12 = (bf16[400,128]{1,0:T(8,128)(2,1)S(1)}, bf16[400,128]{1,0:T(8,128)(2,1)S(1)}, u32[]{:S(2)}, u32[]{:S(2)}) collective-permute-start(bf16[400,128]{1,0:T(8,128)(2,1)S(1)} %get-tuple-element.66), channel_id=1, source_target_pairs={{0,16},{1,17},{2,18},{3,19},{4,20},{5,21},{6,22},{7,23},{8,24},{9,... | collective-permute-start | bytes 307208 | tf_op jit(solution)/shard_map/ppermute | solution.py:404
  62.4 11.9 %collective-permute-start.13 = (bf16[400,128]{1,0:T(8,128)(2,1)S(1)}, bf16[400,128]{1,0:T(8,128)(2,1)S(1)}, u32[]{:S(2)}, u32[]{:S(2)}) collective-permute-start(bf16[400,128]{1,0:T(8,128)(2,1)S(1)} %get-tuple-element.67), channel_id=1, source_target_pairs={{0,24},{1,25},{2,26},{3,27},{4,28},{5,29},{6,30},{7,31},{8,0},{9,1... | collective-permute-start | bytes 307208 | tf_op jit(solution)/shard_map/ppermute | solution.py:404
  65.2 4.1 %collective-permute-start.14 = (bf16[192,128]{1,0:T(8,128)(2,1)S(1)}, bf16[192,128]{1,0:T(8,128)(2,1)S(1)}, u32[]{:S(2)}, u32[]{:S(2)}) collective-permute-start(bf16[192,128]{1,0:T(8,128)(2,1)S(1)} %get-tuple-element.68), channel_id=1, source_target_pairs={{0,2},{1,3},{2,0},{3,1},{4,6},{5,7},{6,4},{7,5},{8,10},{9,11},{10,... | collective-permute-start | bytes 147464 | tf_op jit(solution)/shard_map/ppermute | solution.py:404
  66.3 5.1 %collective-permute-start.15 = (bf16[192,128]{1,0:T(8,128)(2,1)S(1)}, bf16[192,128]{1,0:T(8,128)(2,1)S(1)}, u32[]{:S(2)}, u32[]{:S(2)}) collective-permute-start(bf16[192,128]{1,0:T(8,128)(2,1)S(1)} %get-tuple-element.69), channel_id=1, source_target_pairs={{0,4},{1,5},{2,6},{3,7},{4,0},{5,1},{6,2},{7,3},{8,12},{9,13},{10,... | collective-permute-start | bytes 147464 | tf_op jit(solution)/shard_map/ppermute | solution.py:404
  69.3 5.0 %collective-permute-start.16 = (bf16[192,128]{1,0:T(8,128)(2,1)S(1)}, bf16[192,128]{1,0:T(8,128)(2,1)S(1)}, u32[]{:S(2)}, u32[]{:S(2)}) collective-permute-start(bf16[192,128]{1,0:T(8,128)(2,1)S(1)} %get-tuple-element.70), channel_id=1, source_target_pairs={{0,6},{1,7},{2,4},{3,5},{4,2},{5,3},{6,0},{7,1},{8,14},{9,15},{10,... | collective-permute-start | bytes 147464 | tf_op jit(solution)/shard_map/ppermute | solution.py:404

commit v4 on v3

v4 whole, which is shorter than its diff:
```python
import functools

import jax
import jax.numpy as jnp
from jax import lax
from jax.experimental import pallas as pl
from jax.experimental.pallas import tpu as pltpu
from jax.sharding import PartitionSpec as P

LANES = 128
VMEM_BYTES = 24 * 1024 * 1024
ADD_BYTES = 8 * 1024 * 1024
EXTRA = (32, 16, 0)
CHAINS = (("x", "y", "z0", "z1"), ("y", "z0", "x", "z1"), ("z0", "x", "y", "z1"))
NN = (((1,), (0,)), ((), ()))
NT = (((1,), (1,)), ((), ()))
TN = (((0,), (0,)), ((), ()))


def dot(left, right, dims):
    return lax.dot_general(left, right, dims, preferred_element_type=jnp.float32)


def held(arrays, space=pltpu.VMEM):
    return [pltpu.with_memory_space_constraint(x, space) for x in arrays]


def shifted(x, axis, by):
    count = lax.axis_size(axis)
    pairs = [(i, i + by) for i in range(count) if 0 <= i + by < count]
    return lax.ppermute(x, axis, pairs)


def column(row, rows):
    return jnp.broadcast_to(row, (LANES, rows)).T


def cost(flops, moved):
    return pl.CostEstimate(flops=flops, bytes_accessed=moved, transcendentals=0)


def pack_kernel(head_x, tail_x, head_gs, head_gk, weight, to_next, to_prev):
    halo, channels = tail_x.shape
    to_next[...] = tail_x[...]
    by_row = column(weight[...], LANES)[:halo]
    by_row = jnp.concatenate([by_row] * (channels // LANES), axis=1)
    to_prev[0:halo] = head_x[...]
    to_prev[halo : 2 * halo] = (head_gs[...].astype(jnp.float32) * by_row).astype(jnp.bfloat16)
    to_prev[2 * halo : 3 * halo] = (head_gk[...].astype(jnp.float32) * by_row).astype(jnp.bfloat16)


def pack(halo, x, grad_stream_out, grad_skip_out, weight):
    length, channels = x.shape
    first = pl.BlockSpec((halo, channels), lambda i: (0, 0))
    last = pl.BlockSpec((halo, channels), lambda i: (length // halo - 1, 0))
    return pl.pallas_call(
        pack_kernel,
        grid=(1,),
        in_specs=[first, last, first, first, pl.BlockSpec((1, LANES), lambda i: (0, 0))],
        out_specs=[
            pl.BlockSpec((halo, channels), lambda i: (0, 0)),
            pl.BlockSpec((3 * halo, channels), lambda i: (0, 0)),
        ],
        out_shape=[
            jax.ShapeDtypeStruct((halo, channels), jnp.bfloat16),
            jax.ShapeDtypeStruct((3 * halo, channels), jnp.bfloat16),
        ],
        compiler_params=pltpu.CompilerParams(vmem_limit_bytes=ADD_BYTES),
        name="pack_borders",
    )(*held((x, x, grad_stream_out, grad_skip_out, weight), pltpu.HBM))


def load_kernel(
    x, gs, gk, weight, conv_w, out_w, _, x_here, grad_stream, grad_skip, sums, conv_here, out_here,
    gs_raw, gk_raw, weight_here, sems,
):
    some = pl.ds(0, conv_here.shape[0])
    pairs = (
        (weight, weight_here), (gs, gs_raw), (gk, gk_raw), (x, x_here),
        (conv_w.at[some], conv_here), (out_w.at[some], out_here),
    )
    copies = [pltpu.make_async_copy(a, b, sems.at[i]) for i, (a, b) in enumerate(pairs)]
    for copy in copies:
        copy.start()
    for copy in copies[:3]:
        copy.wait()
    length, channels = x_here.shape
    by_row = column(weight_here[...], length)
    by_row = jnp.concatenate([by_row] * (channels // LANES), axis=1)
    grad_stream[...] = gs_raw[...].astype(jnp.float32) * by_row
    grad_skip[...] = (gk_raw[...].astype(jnp.float32) * by_row).astype(jnp.bfloat16)
    own_sum = jnp.broadcast_to(jnp.sum(weight_here[...], axis=1, keepdims=True), (1, LANES))
    sums[...] = split_rows(own_sum)
    for copy in copies[3:]:
        copy.wait()


def load_some(third, x, gs, gk, weight, conv_w, out_w, after):
    shape = x.shape
    vmem, anywhere = pl.BlockSpec(memory_space=pltpu.VMEM), pl.BlockSpec(memory_space=pl.ANY)
    return pl.pallas_call(
        load_kernel,
        in_specs=[anywhere] * 7,
        out_specs=[vmem] * 6,
        out_shape=[
            pltpu.VMEM(shape, jnp.bfloat16),
            pltpu.VMEM(shape, jnp.float32),
            pltpu.VMEM(shape, jnp.bfloat16),
            pltpu.VMEM((16, LANES), jnp.bfloat16),
            pltpu.VMEM((third,) + conv_w.shape[1:], jnp.bfloat16),
            pltpu.VMEM((third,) + out_w.shape[1:], jnp.bfloat16),
        ],
        scratch_shapes=[
            pltpu.VMEM(shape, jnp.bfloat16),
            pltpu.VMEM(shape, jnp.bfloat16),
            pltpu.VMEM(weight.shape, jnp.float32),
            pltpu.SemaphoreType.DMA((6,)),
        ],
        compiler_params=pltpu.CompilerParams(vmem_limit_bytes=ADD_BYTES),
        cost_estimate=cost(10**7, 4 * 10**6),
        name="load_some",
    )(*held((x, gs, gk, weight, conv_w, out_w), pltpu.HBM), *held([after]))


def split_rows(total):
    high = total.astype(jnp.bfloat16).astype(jnp.float32)
    middle = (total - high).astype(jnp.bfloat16).astype(jnp.float32)
    low = total - high - middle
    row = lax.broadcasted_iota(jnp.int32, (16, LANES), 0)
    rows = jnp.where(row == 0, high, jnp.where(row == 1, middle, jnp.where(row == 2, low, 0.0)))
    return rows.astype(jnp.bfloat16)


def joined_rows(rows):
    return jnp.sum(rows.astype(jnp.float32), axis=0, keepdims=True)


def backward(plan, layers, refs_of, weights_of, grad_proj, grad_stream, past_part, total, grad_parts):
    halo, length, channels = plan["halo"], plan["length"], plan["channels"]
    own = slice(halo, halo + length)
    for place, index in enumerate(layers):
        dilation, count = 2**index, plan["counts"][index]
        operands, factors, gates = refs_of(index)
        conv_layer, out_layer = weights_of(index)
        grad_proj[0:count, :channels] = grad_stream[0:count].astype(jnp.bfloat16)
        grad_gated = dot(grad_proj[0:count], out_layer[...], NT)
        total[0:channels] = dot(gates[own], grad_proj[0:length], TN)
        plan["store"](total, channels, place, grad_parts, True)
        both = factors[halo : halo + count]
        grad_preact = jnp.concatenate(
            [grad_gated * both[:, :channels], grad_gated * both[:, channels:]], axis=1
        ).astype(jnp.bfloat16)
        spread = dot(grad_preact, conv_layer[...], NT)
        past_part[0:count] = spread[:, channels:]
        rows = plan["counts"][index - 1] if index else length
        grad_stream[0:rows] += spread[0:rows, :channels] + past_part[dilation : dilation + rows]
        total[...] = dot(operands[own], grad_preact[0:length], TN)
        plan["store"](total, 2 * channels, place, grad_parts, False)


def first_kernel(
    plan, prev_x, next_rows, own_x, own_grad, own_skip, sums, conv_low, out_low, conv_w, out_w,
    low_operands, low_factors, low_gates, grad_stream, grad_skip, conv_high, out_high, *rest,
):
    grad_parts = rest[:-8]
    stream, operands, factors, gates, grad_proj, past_part, total, sems = rest[-8:]
    halo, (length, channels) = plan["halo"], own_x.shape
    layers, low, third = conv_w.shape[0], low_gates.shape[0], conv_low.shape[0]
    copies = {}
    for index in range(third, layers):
        at = 2 * (index - third)
        copies[index] = (
            pltpu.make_async_copy(conv_w.at[index], conv_high.at[index - third], sems.at[at]),
            pltpu.make_async_copy(out_w.at[index], out_high.at[index - third], sems.at[at + 1]),
        )
        for copy in copies[index]:
            copy.start()
    pad = 2 ** (layers - 1)
    extent = length + 2 * halo
    stream[0:pad] = jnp.zeros((pad, channels), jnp.float32)
    stream[pad : pad + halo] = prev_x[...].astype(jnp.float32)
    stream[pad + halo : pad + halo + length] = own_x[...].astype(jnp.float32)
    stream[pad + halo + length :] = next_rows[0:halo].astype(jnp.float32)

    def refs_of(index):
        if index < low:
            return low_operands.at[index], low_factors.at[index], low_gates.at[index]
        return operands.at[index - low], factors.at[index - low], gates.at[index - low]

    def weights_of(index):
        if index < third:
            return conv_low.at[index], out_low.at[index]
        return conv_high.at[index - third], out_high.at[index - third]

    for index in range(layers):
        dilation, start = 2**index, plan["starts"][index]
        operand, factor, gate = refs_of(index)
        conv_layer, out_layer = weights_of(index)
        operand[start:, :channels] = stream[pad + start :].astype(jnp.bfloat16)
        operand[start:, channels:] = stream[pad + start - dilation : pad + extent - dilation].astype(jnp.bfloat16)
        for copy in copies.get(index, ()):
            copy.wait()
        preact = dot(operand[start:], conv_layer[...], NN)
        filtered = jnp.tanh(preact[:, :channels])
        opening = 0.5 + 0.5 * jnp.tanh(0.5 * preact[:, channels:])
        product = filtered * opening
        gate[start:] = product.astype(jnp.bfloat16)
        factor[start:, :channels] = opening - filtered * product
        factor[start:, channels:] = product * (1.0 - opening)
        if index < layers - 1:
            stream[pad + start :] += dot(gate[start:], out_layer[:, :channels], NN)

    grad_stream[0:length] = own_grad[...]
    grad_stream[length:] = next_rows[halo : 2 * halo].astype(jnp.float32)
    grad_skip[0:length] = own_skip[...]
    grad_skip[length:] = next_rows[2 * halo : 3 * halo]
    grad_proj[:, channels:] = grad_skip[...]
    backward(
        plan, list(reversed(range(low, layers))), refs_of, weights_of,
        grad_proj, grad_stream, past_part, total, grad_parts,
    )
    plan["finish"](sums, grad_parts)


def later_kernel(
    plan, first, third, low_operands, low_factors, low_gates, grad_before, grad_skip, sums, conv_w, out_w, *rest
):
    grad_after, *grad_parts, grad_stream, grad_proj, past_part, total = rest[-7:]
    channels = plan["channels"]
    grad_stream[...] = grad_before[...]
    grad_proj[:, channels:] = grad_skip[...]

    def refs_of(index):
        return low_operands.at[index], low_factors.at[index], low_gates.at[index]

    def weights_of(index):
        return conv_w.at[index - first], out_w.at[index - first]

    backward(
        plan, list(reversed(range(first, first + third))), refs_of, weights_of,
        grad_proj, grad_stream, past_part, total, grad_parts,
    )
    grad_after[...] = grad_stream[0 : grad_after.shape[0]]
    plan["finish"](sums, grad_parts)


def store_whole(total, height, place, grad_parts, is_out):
    grad_parts[int(is_out)][place] = total[0:height].astype(jnp.bfloat16)


def finish_whole(sums, grad_parts):
    pass


def finish_shards(extra, sums, grad_parts):
    for part in grad_parts:
        lead, rows = part.shape[:-2], part.shape[-2]
        for first in range(rows - extra, rows, 16):
            part[(slice(None),) * len(lead) + (slice(first, first + 16),)] = jnp.broadcast_to(
                sums[...], lead + sums.shape
            )


def store_shards(tm, dp, order, total, height, place, grad_parts, is_out):
    keep, send = grad_parts
    t_at, d_at = lax.axis_index("tm"), lax.axis_index("dp")
    core_at = lax.rem(d_at, 2)
    channels = total.shape[0] // 2
    rows = height // tm
    at = pl.ds(place * 3 * channels // tm + (2 * channels // tm if is_out else 0), rows)
    at_bits = bits_of(t_at, d_at, lax.rem, lax.div)
    for y in range(dp // 2):
        near = total[0:height, (2 * y) * LANES : (2 * y + 1) * LANES]
        far = total[0:height, (2 * y + 1) * LANES : (2 * y + 2) * LANES]
        mine = jnp.where(core_at == 0, near, far).astype(jnp.bfloat16)
        other = jnp.where(core_at == 0, far, near).astype(jnp.bfloat16)
        for t in range(tm):
            bits = bits_of(t, 2 * y, lambda a, b: a % b, lambda a, b: a // b)
            lead = tuple(lax.rem(bits[name] + at_bits[name], 2) for name in order)
            keep[lead + (at,)] = mine[t * rows : (t + 1) * rows]
            send[lead + (at,)] = other[t * rows : (t + 1) * rows]


def bits_of(t, d, rem, div):
    return {"x": rem(t, 2), "z0": rem(div(t, 2), 2), "z1": div(t, 4), "y": div(d, 2)}


def run_layers(in_shards, tm, dp, halo, prev_x, next_rows, loaded, conv_w, out_w):
    own_x, own_grad, own_skip, sums, conv_low, out_low = loaded
    length, channels = own_x.shape
    layers, third = conv_w.shape[0], conv_low.shape[0]
    low = layers - third
    extent, border = length + 2 * halo, length + halo
    starts = []
    for index in range(layers):
        need = halo if index == layers - 1 else 2 ** (index + 1)
        starts.append(need // 16 * 16)
    counts = [-(-(length + 2 ** (index + 1) - 1) // 16) * 16 for index in range(layers)]
    plan = {"halo": halo, "starts": starts, "counts": counts, "length": length, "channels": channels}
    if in_shards:
        rows = third * 3 * channels // tm
        plans = [
            plan
            | {
                "store": functools.partial(store_shards, tm, dp, order),
                "finish": functools.partial(finish_shards, extra),
            }
            for order, extra in zip(CHAINS, EXTRA)
        ]
        shapes = [2 * [(2,) * len(order) + (rows + extra, LANES)] for order, extra in zip(CHAINS, EXTRA)]
    else:
        plans = [plan | {"store": store_whole, "finish": finish_whole}] * len(CHAINS)
        shapes = [[(third,) + conv_w.shape[1:], (third,) + out_w.shape[1:]]] * len(CHAINS)
    vmem, anywhere = pl.BlockSpec(memory_space=pltpu.VMEM), pl.BlockSpec(memory_space=pl.ANY)
    weight_bytes = 2 * (conv_w.size + out_w.size)
    flops = 2 * length * channels * channels
    *kept, grad_stream, grad_skip, conv_high, out_high, keep, send = pl.pallas_call(
        functools.partial(first_kernel, plans[0]),
        in_specs=[vmem] * 8 + [anywhere] * 2,
        out_specs=[vmem] * 9,
        out_shape=[
            pltpu.VMEM((low, extent, 2 * channels), jnp.bfloat16),
            pltpu.VMEM((low, extent, 2 * channels), jnp.float32),
            pltpu.VMEM((low, extent, channels), jnp.bfloat16),
            pltpu.VMEM((border, channels), jnp.float32),
            pltpu.VMEM((border, channels), jnp.bfloat16),
            pltpu.VMEM((low,) + conv_w.shape[1:], jnp.bfloat16),
            pltpu.VMEM((low,) + out_w.shape[1:], jnp.bfloat16),
        ]
        + [pltpu.VMEM(shape, jnp.bfloat16) for shape in shapes[0]],
        scratch_shapes=[
            pltpu.VMEM((2 ** (layers - 1) + extent, channels), jnp.float32),
            pltpu.VMEM((third, extent, 2 * channels), jnp.bfloat16),
            pltpu.VMEM((third, extent, 2 * channels), jnp.float32),
            pltpu.VMEM((third, extent, channels), jnp.bfloat16),
            pltpu.VMEM((border, 2 * channels), jnp.bfloat16),
            pltpu.VMEM((border, channels), jnp.float32),
            pltpu.VMEM((2 * channels, 2 * channels), jnp.float32),
            pltpu.SemaphoreType.DMA((2 * low,)),
        ],
        compiler_params=pltpu.CompilerParams(vmem_limit_bytes=VMEM_BYTES),
        cost_estimate=cost(flops * (5 * layers + 12 * third), weight_bytes),
        name="forward_and_last_third",
    )(
        *held((prev_x, next_rows, own_x, own_grad, own_skip, sums, conv_low, out_low)),
        *held((conv_w, out_w), pltpu.HBM),
    )
    parts = [Chunk(tm, dp, 0, keep, send) if in_shards else (keep, send)]
    for step in (1, 2):
        first = layers - (step + 1) * third
        last = step == 2
        weights = (conv_low, out_low) if last else (conv_high, out_high)
        after = [parts[0].next_message()] if last and in_shards else []
        grad_stream, keep, send = pl.pallas_call(
            functools.partial(later_kernel, plans[step], first, third),
            in_specs=[vmem] * 8 + [anywhere] * len(after),
            out_specs=[vmem] * 3,
            out_shape=[pltpu.VMEM((length if last else border, channels), jnp.float32)]
            + [pltpu.VMEM(shape, jnp.bfloat16) for shape in shapes[step]],
            scratch_shapes=[
                pltpu.VMEM((border, channels), jnp.float32),
                pltpu.VMEM((border, 2 * channels), jnp.bfloat16),
                pltpu.VMEM((border, channels), jnp.float32),
                pltpu.VMEM((2 * channels, 2 * channels), jnp.float32),
            ],
            compiler_params=pltpu.CompilerParams(vmem_limit_bytes=VMEM_BYTES),
            cost_estimate=cost(flops * 12 * third, weight_bytes),
            name="first_third" if last else "middle_third",
        )(*held((*kept, grad_stream, grad_skip, sums, *weights, *after)))
        parts.append(Chunk(tm, dp, step, keep, send) if in_shards else (keep, send))
    return grad_stream, parts


def add_kernel(count, groups, *refs):
    arrays, outs = refs[:count], refs[-len(groups) :]
    for out, pieces in zip(outs, groups):
        lead = (slice(None),) * (len(out.shape) - 2)
        for first, rows, with_total, terms in pieces:
            body = rows - 16 if with_total else rows
            value = 0.0
            for array, at, begin in terms:
                value = value + arrays[array][at + lead + (slice(begin, begin + body),)].astype(jnp.float32)
            out[lead + (slice(first, first + body),)] = value.astype(out.dtype)
            if with_total:
                total = 0.0
                for array, at, begin in terms:
                    rows_at = slice(begin + body, begin + rows)
                    total = total + joined_rows(arrays[array][at + (0,) * len(lead) + (rows_at,)])
                slab = split_rows(total)
                out[lead + (slice(first + body, first + rows),)] = jnp.broadcast_to(slab, out.shape[:-2] + slab.shape)


def add_up(arrays, groups, shapes, after, name):
    vmem = pl.BlockSpec(memory_space=pltpu.VMEM)
    return pl.pallas_call(
        functools.partial(add_kernel, len(arrays), groups),
        in_specs=[vmem] * len(arrays) + [pl.BlockSpec(memory_space=pl.ANY)] * len(after),
        out_specs=[vmem] * len(groups),
        out_shape=[pltpu.VMEM(shape, jnp.bfloat16) for shape in shapes],
        compiler_params=pltpu.CompilerParams(vmem_limit_bytes=ADD_BYTES),
        name=name,
    )(*held(arrays), *held(after))


def last_kernel(counts, samples_all, third, *refs):
    parts = []
    for count in counts:
        parts.append(refs[:count])
        refs = refs[count:]
    grad_in, grad_inputs, grad_conv, grad_out = refs
    layers, conv_rows, _ = grad_conv.shape
    out_rows = grad_out.shape[1]
    rows = conv_rows + out_rows
    total = 0.0
    for part in parts[0]:
        total = total + joined_rows(part[(0,) * (len(part.shape) - 2) + (slice(part.shape[-2] - 16, part.shape[-2]),)])
    scale = samples_all / total
    for chunk, terms in enumerate(parts):
        for place in range(third):
            index = layers - 1 - chunk * third - place
            for out, at in ((grad_conv, place * rows), (grad_out, place * rows + conv_rows)):
                value = 0.0
                for part in terms:
                    own = (0,) * (len(part.shape) - 2) + (slice(at, at + out.shape[1]),)
                    value = value + part[own].astype(jnp.float32)
                out[index] = value * scale
    for first in range(0, grad_in.shape[1], LANES):
        grad_inputs[:, first : first + LANES] = grad_in[:, first : first + LANES] * scale


class Chunk:
    def __init__(self, tm, dp, chunk, keep, send):
        self.tm, self.dp, self.chunk, self.rows = tm, dp, chunk, keep.shape[-2]
        self.message = None
        self.terms = [keep, self.swapped(send, "core")]

    def swapped(self, value, name):
        over_t, over_d = {"core": (0, 1), "y": (0, 2), "x": (1, 0), "z0": (2, 0), "z1": (4, 0)}[name]
        tm, dp = self.tm, self.dp
        pairs = [(t * dp + d, (t ^ over_t) * dp + (d ^ over_d)) for t in range(tm) for d in range(dp)]
        return lax.ppermute(value, ("tm", "dp"), pairs)

    def next_message(self):
        if self.message is None:
            left = len(CHAINS[self.chunk]) + 2 - len(self.terms)
            leads = [(0,) * (len(v.shape) - 2 - left) + (1,) for v in self.terms]
            pieces = [(0, self.rows, self.chunk == 0, [(i, at, 0) for i, at in enumerate(leads)])]
            (self.message,) = add_up(
                self.terms, [pieces], [(2,) * (left - 1) + (self.rows, LANES)], [],
                "add_chunk%d_step%d" % (self.chunk, len(self.terms) - 1),
            )
        return self.message

    def finished(self):
        for name in CHAINS[self.chunk]:
            self.terms.append(self.swapped(self.next_message(), name))
            self.message = None
        return self.terms


def scattered(part):
    columns = lax.psum_scatter(part, "dp", scatter_dimension=2, tiled=True).astype(jnp.float32)
    return lax.psum_scatter(columns, "tm", scatter_dimension=1, tiled=True)


def body(inputs, grad_stream_out, grad_skip_out, sample_weight, conv_weight, out_weight):
    tm, dp = lax.axis_size("tm"), lax.axis_size("dp")
    batch, length, channels = inputs.shape
    layers = conv_weight.shape[0]
    third = layers // len(CHAINS)
    halo = 2**layers
    samples_all = batch * length * tm * dp
    x, gs, gk = inputs[0], grad_stream_out[0], grad_skip_out[0]
    to_next, to_prev = pack(halo, x, gs, gk, sample_weight)
    prev_x = shifted(to_next, "tm", 1)
    next_rows = shifted(to_prev, "tm", -1)
    loaded = load_some(third, x, gs, gk, sample_weight, conv_weight, out_weight, to_next)
    in_shards = tm == 8 and dp == 4 and channels // tm % 16 == 0 and 2 * channels == dp * LANES
    grad_in, parts = run_layers(in_shards, tm, dp, halo, prev_x, next_rows, loaded, conv_weight, out_weight)
    if not in_shards:
        scale = samples_all / lax.psum(jnp.sum(sample_weight), ("tm", "dp"))
        grad_conv, grad_out = (
            scattered(jnp.concatenate([part[i][::-1] for part in reversed(parts)])) * scale for i in range(2)
        )
        return (grad_in * scale)[None], grad_conv, grad_out
    terms = [part.finished() for part in parts]
    conv_rows, out_rows = 2 * channels // tm, channels // tm
    grad_inputs, grad_conv, grad_out = pl.pallas_call(
        functools.partial(last_kernel, [len(group) for group in terms], float(samples_all), third),
        out_shape=[
            jax.ShapeDtypeStruct((length, channels), jnp.float32),
            jax.ShapeDtypeStruct((layers, conv_rows, LANES), jnp.float32),
            jax.ShapeDtypeStruct((layers, out_rows, LANES), jnp.float32),
        ],
        compiler_params=pltpu.CompilerParams(vmem_limit_bytes=ADD_BYTES),
        name="scale_all",
    )(*held([value for group in terms for value in group]), *held([grad_in]))
    return grad_inputs[None], grad_conv, grad_out


def solution(mesh):
    placed = (
        P("dp", "tm", None),
        P("dp", "tm", None),
        P("dp", "tm", None),
        P("dp", "tm"),
        P(),
        P(),
    )
    return jax.shard_map(
        body,
        mesh=mesh,
        in_specs=placed,
        out_specs=(P("dp", "tm", None), P(None, "tm", "dp"), P(None, "tm", "dp")),
        check_vma=False,
    )
```

time: 75.5 us -> 60.6 us (0.80)
  waiting for transfers between devices: 28 us -> 13.7 us
  starting transfers between devices: 32.3 us -> 31.1 us
    ppermute x15, waiting for transfers between devices: 28 us -> 13.7 us  [swapped(): return lax.ppermute(value, ('tm', 'dp'), pairs)]
    ppermute x15, starting transfers between devices: 25.6 us -> 24.3 us  [swapped(): return lax.ppermute(value, ('tm', 'dp'), pairs)]
    pallas_call x4 -> x5, Pallas kernels: 12.4 us -> 13.1 us  [the longest x1 6.54 us: run_layers(): pl.pallas_call(functools.partial(first_kernel, plans[0]), in_specs=[vmem]...]
  transfers between devices with their start and end apart: 17 -> 17, of which waited for: 5 -> 6; matrix products, arithmetic and copies ran while one was open for 0% -> 0% of each run, Pallas kernels for 4% -> 11%
where the time goes in v4:
time: 60.6 us; the launch traced here: 60.4 us
  starting transfers between devices  31.1 us (51%)
  Pallas kernels  14.8 us (24%)
  waiting for transfers between devices  13.7 us (23%)
  between operations  0.74 us (1%)
    ppermute x15, starting transfers between devices, swapped(): return lax.ppermute(value, ('tm', 'dp'), pairs)  24.3 us
    ppermute x15, waiting for transfers between devices, swapped(): return lax.ppermute(value, ('tm', 'dp'), pairs)  13.7 us
    ppermute x2, starting transfers between devices, shifted(): return lax.ppermute(x, axis, pairs)  6.76 us
    pallas_call x1, Pallas kernels, run_layers(): pl.pallas_call(functools.partial(first_kernel, plans[0]), in_specs=[vmem]...  6.54 us
    pallas_call x2, Pallas kernels, run_layers(): pl.pallas_call(functools.partial(later_kernel, plans[step], first, third)...  3.87 us
    pallas_call x1, Pallas kernels, load_some(): pl.pallas_call(load_kernel, in_specs=[anywhere] * 7, out_specs=[vmem] * 6...  1.67 us
  transfers between devices with their start and end apart: 17, of which 6 were waited for; matrix products, arithmetic and copies ran while one was open for 0% of the time, Pallas kernels for 11%

profile of v4, /device:TPU:0, one launch (start us, length us, event | category | flops | bytes accessed | tf_op | source)
XLA Modules:
  0.0 60.4 jit_solution(9272415591425204770)
XLA Ops:
  0.6 0.9 %pack_borders.1 = (bf16[64,256]{1,0:T(8,128)(2,1)S(1)}, bf16[192,256]{1,0:T(8,128)(2,1)S(1)}) custom-call(bf16[512,256]{1,0:T(8,128)(2,1)} %bitcast.4, bf16[512,256]{1,0:T(8,128)(2,1)} %bitcast.5, bf16[512,256]{1,0:T(8,128)(2,1)} %bitcast.7, bf16[512,256]{1,0:T(8,128)(2,1)} %bitcast.9, f32[1,512]{1,0:T(1,128)} %weight.3), custom_call_target="tpu_custom_call" | custom-call | tf_op jit(solution)/shard_map/pack_borders/pallas_call | solution.py:56
  1.5 1.3 %collective-permute-start.1 = (bf16[192,256]{1,0:T(8,128)(2,1)S(1)}, bf16[192,256]{1,0:T(8,128)(2,1)S(1)}, u32[]{:S(2)}, u32[]{:S(2)}) collective-permute-start(bf16[192,256]{1,0:T(8,128)(2,1)S(1)} %get-tuple-element.30), channel_id=1, source_target_pairs={{4,0},{8,4},{12,8},{16,12},{20,16},{24,20},{28,24},{5,1},{9,5},{13... | collective-permute-start | bytes 294920 | tf_op jit(solution)/shard_map/ppermute | solution.py:31
  2.8 5.5 %collective-permute-start = (bf16[64,256]{1,0:T(8,128)(2,1)S(1)}, bf16[64,256]{1,0:T(8,128)(2,1)S(1)}, u32[]{:S(2)}, u32[]{:S(2)}) collective-permute-start(bf16[64,256]{1,0:T(8,128)(2,1)S(1)} %get-tuple-element.29._), channel_id=1, source_target_pairs={{0,4},{4,8},{8,12},{12,16},{16,20},{20,24},{24,28},{1,5},{5,9},{9,... | collective-permute-start | bytes 98312 | tf_op jit(solution)/shard_map/ppermute | solution.py:31
  8.3 1.7 %load_some.1 = (bf16[512,256]{1,0:T(8,128)(2,1)S(1)}, f32[512,256]{1,0:T(8,128)S(1)}, bf16[512,256]{1,0:T(8,128)(2,1)S(1)}, bf16[16,128]{1,0:T(8,128)(2,1)S(1)},...) custom-call(bf16[512,256]{1,0:T(8,128)(2,1)} %bitcast.6, bf16[512,256]{1,0:T(8,128)(2,1)} %bitcast.8, ...), custom_call_target="tpu_custom_call" | custom-call | flops 10000000 | bytes 4000000 | tf_op jit(solution)/shard_map/load_some/pallas_call | solution.py:101
  10.0 0.1 collective-permute-done.prev_x
  10.1 0.0 collective-permute-done.1.next_rows
  10.1 6.5 %forward_and_last_third.1 = (bf16[4,640,512]{2,1,0:T(8,128)(2,1)S(1)}, f32[4,640,512]{2,1,0:T(8,128)S(1)}, bf16[4,640,256]{2,1,0:T(8,128)(2,1)S(1)}, f32[576,256...) custom-call(bf16[64,256]{1,0:T(8,128)(2,1)S(1)} %collective-permute-, ...), custom_call_target="tpu_custom_call" | custom-call | flops 3623878656 | bytes 4718592 | tf_op jit(solution)/shard_map/forward_and_last_third/pallas_call | solution.py:317
  16.6 0.1 collective-permute-start.2
  16.7 1.9 %middle_third.1 = (f32[576,256]{1,0:T(8,128)S(1)}, bf16[2,2,2,2,208,128]{5,4,3,2,1,0:T(8,128)(2,1)S(1)}, bf16[2,2,2,2,208,128]{5,4,3,2,1,0:T(8,128)(2,1)S(1)}) custom-call(bf16[4,640,512]{2,1,0:T(8,128)(2,1)S(1)} %get-tuple-element.39.low_operands, f32[4,640,512]{2,1,0:T(8,128)S(1)} %get-tuple-element.40.low_factors, ...), custom_call_target="tpu_custom_call" | custom-call | flops 1610612736 | bytes 4718592 | tf_op jit(solution)/shard_map/middle_third/pallas_call | solution.py:354
  18.6 0.6 collective-permute-start.7
  19.2 0.0 collective-permute-done.2.refs_1_
  19.2 0.1 add_chunk0_step1.1.rest_0_
  19.3 1.9 %first_third.1 = (f32[512,256]{1,0:T(8,128)S(1)}, bf16[2,2,2,2,192,128]{5,4,3,2,1,0:T(8,128)(2,1)S(1)}, bf16[2,2,2,2,192,128]{5,4,3,2,1,0:T(8,128)(2,1)S(1)}) custom-call(bf16[4,640,512]{2,1,0:T(8,128)(2,1)S(1)} %get-tuple-element.39.low_operands, f32[4,640,512]{2,1,0:T(8,128)S(1)} %get-tuple-element.40.low_factors, ...), custom_call_target="tpu_custom_call" | custom-call | flops 1610612736 | bytes 4718592 | tf_op jit(solution)/shard_map/first_third/pallas_call | solution.py:354
  21.3 0.1 collective-permute-start.12
  21.4 2.9 %collective-permute-start.3 = (bf16[2,2,2,224,128]{4,3,2,1,0:T(8,128)(2,1)S(1)}, bf16[2,2,2,224,128]{4,3,2,1,0:T(8,128)(2,1)S(1)}, u32[]{:S(2)}, u32[]{:S(2)}) collective-permute-start(bf16[2,2,2,224,128]{4,3,2,1,0:T(8,128)(2,1)S(1)} %add_chunk0_step1.1.rest_0_), channel_id=1, source_target_pairs={{0,4},{1,5},{2,6},{3,7},{4,0},{5,1},{6,2},{7,3},{8,12},{9,13},{10,... | collective-permute-start | bytes 1376264 | tf_op jit(solution)/shard_map/ppermute | solution.py:441
  24.3 0.0 collective-permute-done.7.refs_1_.refs_7_
  24.3 0.1 add_chunk1_step1.1
  24.4 1.6 %collective-permute-start.8 = (bf16[2,2,2,208,128]{4,3,2,1,0:T(8,128)(2,1)S(1)}, bf16[2,2,2,208,128]{4,3,2,1,0:T(8,128)(2,1)S(1)}, u32[]{:S(2)}, u32[]{:S(2)}) collective-permute-start(bf16[2,2,2,208,128]{4,3,2,1,0:T(8,128)(2,1)S(1)} %add_chunk1_step1.1), channel_id=1, source_target_pairs={{0,2},{1,3},{2,0},{3,1},{4,6},{5,7},{6,4},{7,5},{8,10},{9,11},{10,... | collective-permute-start | bytes 1277960 | tf_op jit(solution)/shard_map/ppermute | solution.py:441
  26.0 0.0 collective-permute-done.12.refs_1_.refs_13_
  26.0 0.1 add_chunk2_step1.1
  26.1 2.2 %collective-permute-start.13 = (bf16[2,2,2,192,128]{4,3,2,1,0:T(8,128)(2,1)S(1)}, bf16[2,2,2,192,128]{4,3,2,1,0:T(8,128)(2,1)S(1)}, u32[]{:S(2)}, u32[]{:S(2)}) collective-permute-start(bf16[2,2,2,192,128]{4,3,2,1,0:T(8,128)(2,1)S(1)} %add_chunk2_step1.1), channel_id=1, source_target_pairs={{0,8},{1,9},{2,10},{3,11},{4,12},{5,13},{6,14},{7,15},{8,0},{9,1},... | collective-permute-start | bytes 1179656 | tf_op jit(solution)/shard_map/ppermute | solution.py:441
  28.3 7.1 %collective-permute-done.3.refs_2_ = bf16[2,2,2,224,128]{4,3,2,1,0:T(8,128)(2,1)S(1)} collective-permute-done((bf16[2,2,2,224,128]{4,3,2,1,0:T(8,128)(2,1)S(1)}, bf16[2,2,2,224,128]{4,3,2,1,0:T(8,128)(2,1)S(1)}, u32[]{:S(2)}, u32[]{:S(2)}) %collective-permute-start.3) | collective-permute-done | bytes 458784 | tf_op jit(solution)/shard_map/ppermute | solution.py:441
  35.4 0.1 add_chunk0_step2.1
  35.5 1.6 %collective-permute-start.4 = (bf16[2,2,224,128]{3,2,1,0:T(8,128)(2,1)S(1)}, bf16[2,2,224,128]{3,2,1,0:T(8,128)(2,1)S(1)}, u32[]{:S(2)}, u32[]{:S(2)}) collective-permute-start(bf16[2,2,224,128]{3,2,1,0:T(8,128)(2,1)S(1)} %add_chunk0_step2.1), channel_id=1, source_target_pairs={{0,2},{1,3},{2,0},{3,1},{4,6},{5,7},{6,4},{7,5},{8,10},{9,11},{10,... | collective-permute-start | bytes 688136 | tf_op jit(solution)/shard_map/ppermute | solution.py:441
  37.1 0.0 collective-permute-done.8.refs_2_.refs_8_
  37.1 0.1 add_chunk1_step2.1
  37.2 3.5 %collective-permute-start.9 = (bf16[2,2,208,128]{3,2,1,0:T(8,128)(2,1)S(1)}, bf16[2,2,208,128]{3,2,1,0:T(8,128)(2,1)S(1)}, u32[]{:S(2)}, u32[]{:S(2)}) collective-permute-start(bf16[2,2,208,128]{3,2,1,0:T(8,128)(2,1)S(1)} %add_chunk1_step2.1), channel_id=1, source_target_pairs={{0,8},{1,9},{2,10},{3,11},{4,12},{5,13},{6,14},{7,15},{8,0},{9,1},... | collective-permute-start | bytes 638984 | tf_op jit(solution)/shard_map/ppermute | solution.py:441
  40.6 0.0 collective-permute-done.13.refs_2_.refs_14_
  40.6 0.1 add_chunk2_step2.1
  40.7 0.3 collective-permute-start.14
  41.0 1.9 %collective-permute-done.4.refs_3_ = bf16[2,2,224,128]{3,2,1,0:T(8,128)(2,1)S(1)} collective-permute-done((bf16[2,2,224,128]{3,2,1,0:T(8,128)(2,1)S(1)}, bf16[2,2,224,128]{3,2,1,0:T(8,128)(2,1)S(1)}, u32[]{:S(2)}, u32[]{:S(2)}) %collective-permute-start.4) | collective-permute-done | bytes 229408 | tf_op jit(solution)/shard_map/ppermute | solution.py:441
  42.9 0.1 add_chunk0_step3.1
  43.0 3.3 %collective-permute-start.5 = (bf16[2,224,128]{2,1,0:T(8,128)(2,1)S(1)}, bf16[2,224,128]{2,1,0:T(8,128)(2,1)S(1)}, u32[]{:S(2)}, u32[]{:S(2)}) collective-permute-start(bf16[2,224,128]{2,1,0:T(8,128)(2,1)S(1)} %add_chunk0_step3.1), channel_id=1, source_target_pairs={{0,8},{1,9},{2,10},{3,11},{4,12},{5,13},{6,14},{7,15},{8,0},{9,1},... | collective-permute-start | bytes 344072 | tf_op jit(solution)/shard_map/ppermute | solution.py:441
  46.2 0.0 collective-permute-done.9.refs_3_.refs_9_
  46.2 0.1 add_chunk1_step3.1
  46.3 0.5 collective-permute-start.10
  46.8 0.0 collective-permute-done.14.refs_3_.refs_15_
  46.8 0.1 add_chunk2_step3.1
  46.9 1.6 %collective-permute-start.15 = (bf16[2,192,128]{2,1,0:T(8,128)(2,1)S(1)}, bf16[2,192,128]{2,1,0:T(8,128)(2,1)S(1)}, u32[]{:S(2)}, u32[]{:S(2)}) collective-permute-start(bf16[2,192,128]{2,1,0:T(8,128)(2,1)S(1)} %add_chunk2_step3.1), channel_id=1, source_target_pairs={{0,2},{1,3},{2,0},{3,1},{4,6},{5,7},{6,4},{7,5},{8,10},{9,11},{10,... | collective-permute-start | bytes 294920 | tf_op jit(solution)/shard_map/ppermute | solution.py:441
  48.5 0.5 collective-permute-done.5.refs_4_
  49.0 0.1 add_chunk0_step4.1
  49.1 3.1 %collective-permute-start.6 = (bf16[224,128]{1,0:T(8,128)(2,1)S(1)}, bf16[224,128]{1,0:T(8,128)(2,1)S(1)}, u32[]{:S(2)}, u32[]{:S(2)}) collective-permute-start(bf16[224,128]{1,0:T(8,128)(2,1)S(1)} %add_chunk0_step4.1), channel_id=1, source_target_pairs={{0,16},{1,17},{2,18},{3,19},{4,20},{5,21},{6,22},{7,23},{8,24},{9,... | collective-permute-start | bytes 172040 | tf_op jit(solution)/shard_map/ppermute | solution.py:441
  52.2 0.0 collective-permute-done.10.refs_4_.refs_10_
  52.2 1.6 %collective-permute-start.11 = (bf16[208,128]{1,0:T(8,128)(2,1)S(1)}, bf16[208,128]{1,0:T(8,128)(2,1)S(1)}, u32[]{:S(2)}, u32[]{:S(2)}) collective-permute-start(bf16[208,128]{1,0:T(8,128)(2,1)S(1)} %add_chunk1_step4.1), channel_id=1, source_target_pairs={{0,16},{1,17},{2,18},{3,19},{4,20},{5,21},{6,22},{7,23},{8,24},{9,... | collective-permute-start | bytes 159752 | tf_op jit(solution)/shard_map/ppermute | solution.py:441
  53.8 0.0 collective-permute-done.15.refs_4_.refs_16_
  53.8 1.5 %collective-permute-start.16 = (bf16[192,128]{1,0:T(8,128)(2,1)S(1)}, bf16[192,128]{1,0:T(8,128)(2,1)S(1)}, u32[]{:S(2)}, u32[]{:S(2)}) collective-permute-start(bf16[192,128]{1,0:T(8,128)(2,1)S(1)} %add_chunk2_step4.1), channel_id=1, source_target_pairs={{0,16},{1,17},{2,18},{3,19},{4,20},{5,21},{6,22},{7,23},{8,24},{9,... | collective-permute-start | bytes 147464 | tf_op jit(solution)/shard_map/ppermute | solution.py:441
  55.3 2.0 %collective-permute-done.11.refs_11_ = bf16[208,128]{1,0:T(8,128)(2,1)S(1)} collective-permute-done((bf16[208,128]{1,0:T(8,128)(2,1)S(1)}, bf16[208,128]{1,0:T(8,128)(2,1)S(1)}, u32[]{:S(2)}, u32[]{:S(2)}) %collective-permute-start.11) | collective-permute-done | bytes 53280 | tf_op jit(solution)/shard_map/ppermute | solution.py:441
  57.3 0.0 collective-permute-done.6.refs_5_
  57.3 2.1 %collective-permute-done.16.refs_17_ = bf16[192,128]{1,0:T(8,128)(2,1)S(1)} collective-permute-done((bf16[192,128]{1,0:T(8,128)(2,1)S(1)}, bf16[192,128]{1,0:T(8,128)(2,1)S(1)}, u32[]{:S(2)}, u32[]{:S(2)}) %collective-permute-start.16) | collective-permute-done | bytes 49184 | tf_op jit(solution)/shard_map/ppermute | solution.py:441
  59.4 1.0 %scale_all.1 = (f32[512,256]{1,0:T(8,128)}, f32[6,64,128]{2,1,0:T(8,128)}, f32[6,32,128]{2,1,0:T(8,128)}) custom-call(bf16[2,2,2,2,224,128]{5,4,3,2,1,0:T(8,128)(2,1)S(1)} %get-tuple-element.37.refs_0_, bf16[2,2,2,2,224,128]{5,4,3,2,1,0:T(8,128)(2,1)S(1)} %collective-permute-done.2.refs_1_, bf16[2,2,2,224,128]{4,3,2,1,0:T(8,128)(2,1)S(1)} %collective-permute-done.3.refs_2_, ...), custom_call_target="tpu_custom_call" | custom-call | tf_op jit(solution)/shard_map/scale_all/pallas_call | solution.py:488
  (2 shorter events, 0.1 us)
Async XLA Ops:
  1.5 8.5 %collective-permute-start.1 = (bf16[192,256]{1,0:T(8,128)(2,1)S(1)}, bf16[192,256]{1,0:T(8,128)(2,1)S(1)}, u32[]{:S(2)}, u32[]{:S(2)}) collective-permute-start(bf16[192,256]{1,0:T(8,128)(2,1)S(1)} %get-tuple-element.30), channel_id=1, source_target_pairs={{4,0},{8,4},{12,8},{16,12},{20,16},{24,20},{28,24},{5,1},{9,5},{13... | collective-permute-start | bytes 294920 | tf_op jit(solution)/shard_map/ppermute | solution.py:31
  2.8 7.2 %collective-permute-start = (bf16[64,256]{1,0:T(8,128)(2,1)S(1)}, bf16[64,256]{1,0:T(8,128)(2,1)S(1)}, u32[]{:S(2)}, u32[]{:S(2)}) collective-permute-start(bf16[64,256]{1,0:T(8,128)(2,1)S(1)} %get-tuple-element.29._), channel_id=1, source_target_pairs={{0,4},{4,8},{8,12},{12,16},{16,20},{20,24},{24,28},{1,5},{5,9},{9,... | collective-permute-start | bytes 98312 | tf_op jit(solution)/shard_map/ppermute | solution.py:31
  16.6 2.6 %collective-permute-start.2 = (bf16[2,2,2,2,224,128]{5,4,3,2,1,0:T(8,128)(2,1)S(1)}, bf16[2,2,2,2,224,128]{5,4,3,2,1,0:T(8,128)(2,1)S(1)}, u32[]{:S(2)}, u32[]{:S(2)}) collective-permute-start(bf16[2,2,2,2,224,128]{5,4,3,2,1,0:T(8,128)(2,1)S(1)} %get-tuple-element.38), channel_id=1, source_target_pairs={{0,1},{1,0},{2,3},{3,2},{4,5},{5,4},{6,7},{7,6},{8,9},{9,8},{10,11... | collective-permute-start | bytes 2752520 | tf_op jit(solution)/shard_map/ppermute | solution.py:441
  18.6 5.6 %collective-permute-start.7 = (bf16[2,2,2,2,208,128]{5,4,3,2,1,0:T(8,128)(2,1)S(1)}, bf16[2,2,2,2,208,128]{5,4,3,2,1,0:T(8,128)(2,1)S(1)}, u32[]{:S(2)}, u32[]{:S(2)}) collective-permute-start(bf16[2,2,2,2,208,128]{5,4,3,2,1,0:T(8,128)(2,1)S(1)} %get-tuple-element.47), channel_id=1, source_target_pairs={{0,1},{1,0},{2,3},{3,2},{4,5},{5,4},{6,7},{7,6},{8,9},{9,8},{10,11... | collective-permute-start | bytes 2555912 | tf_op jit(solution)/shard_map/ppermute | solution.py:441
  21.3 4.7 %collective-permute-start.12 = (bf16[2,2,2,2,192,128]{5,4,3,2,1,0:T(8,128)(2,1)S(1)}, bf16[2,2,2,2,192,128]{5,4,3,2,1,0:T(8,128)(2,1)S(1)}, u32[]{:S(2)}, u32[]{:S(2)}) collective-permute-start(bf16[2,2,2,2,192,128]{5,4,3,2,1,0:T(8,128)(2,1)S(1)} %get-tuple-element.50), channel_id=1, source_target_pairs={{0,1},{1,0},{2,3},{3,2},{4,5},{5,4},{6,7},{7,6},{8,9},{9,8},{10,11... | collective-permute-start | bytes 2359304 | tf_op jit(solution)/shard_map/ppermute | solution.py:441
  21.4 14.0 %collective-permute-start.3 = (bf16[2,2,2,224,128]{4,3,2,1,0:T(8,128)(2,1)S(1)}, bf16[2,2,2,224,128]{4,3,2,1,0:T(8,128)(2,1)S(1)}, u32[]{:S(2)}, u32[]{:S(2)}) collective-permute-start(bf16[2,2,2,224,128]{4,3,2,1,0:T(8,128)(2,1)S(1)} %add_chunk0_step1.1.rest_0_), channel_id=1, source_target_pairs={{0,4},{1,5},{2,6},{3,7},{4,0},{5,1},{6,2},{7,3},{8,12},{9,13},{10,... | collective-permute-start | bytes 1376264 | tf_op jit(solution)/shard_map/ppermute | solution.py:441
  24.4 12.7 %collective-permute-start.8 = (bf16[2,2,2,208,128]{4,3,2,1,0:T(8,128)(2,1)S(1)}, bf16[2,2,2,208,128]{4,3,2,1,0:T(8,128)(2,1)S(1)}, u32[]{:S(2)}, u32[]{:S(2)}) collective-permute-start(bf16[2,2,2,208,128]{4,3,2,1,0:T(8,128)(2,1)S(1)} %add_chunk1_step1.1), channel_id=1, source_target_pairs={{0,2},{1,3},{2,0},{3,1},{4,6},{5,7},{6,4},{7,5},{8,10},{9,11},{10,... | collective-permute-start | bytes 1277960 | tf_op jit(solution)/shard_map/ppermute | solution.py:441
  26.1 14.5 %collective-permute-start.13 = (bf16[2,2,2,192,128]{4,3,2,1,0:T(8,128)(2,1)S(1)}, bf16[2,2,2,192,128]{4,3,2,1,0:T(8,128)(2,1)S(1)}, u32[]{:S(2)}, u32[]{:S(2)}) collective-permute-start(bf16[2,2,2,192,128]{4,3,2,1,0:T(8,128)(2,1)S(1)} %add_chunk2_step1.1), channel_id=1, source_target_pairs={{0,8},{1,9},{2,10},{3,11},{4,12},{5,13},{6,14},{7,15},{8,0},{9,1},... | collective-permute-start | bytes 1179656 | tf_op jit(solution)/shard_map/ppermute | solution.py:441
  35.5 7.4 %collective-permute-start.4 = (bf16[2,2,224,128]{3,2,1,0:T(8,128)(2,1)S(1)}, bf16[2,2,224,128]{3,2,1,0:T(8,128)(2,1)S(1)}, u32[]{:S(2)}, u32[]{:S(2)}) collective-permute-start(bf16[2,2,224,128]{3,2,1,0:T(8,128)(2,1)S(1)} %add_chunk0_step2.1), channel_id=1, source_target_pairs={{0,2},{1,3},{2,0},{3,1},{4,6},{5,7},{6,4},{7,5},{8,10},{9,11},{10,... | collective-permute-start | bytes 688136 | tf_op jit(solution)/shard_map/ppermute | solution.py:441
  37.2 9.1 %collective-permute-start.9 = (bf16[2,2,208,128]{3,2,1,0:T(8,128)(2,1)S(1)}, bf16[2,2,208,128]{3,2,1,0:T(8,128)(2,1)S(1)}, u32[]{:S(2)}, u32[]{:S(2)}) collective-permute-start(bf16[2,2,208,128]{3,2,1,0:T(8,128)(2,1)S(1)} %add_chunk1_step2.1), channel_id=1, source_target_pairs={{0,8},{1,9},{2,10},{3,11},{4,12},{5,13},{6,14},{7,15},{8,0},{9,1},... | collective-permute-start | bytes 638984 | tf_op jit(solution)/shard_map/ppermute | solution.py:441
  40.7 6.1 %collective-permute-start.14 = (bf16[2,2,192,128]{3,2,1,0:T(8,128)(2,1)S(1)}, bf16[2,2,192,128]{3,2,1,0:T(8,128)(2,1)S(1)}, u32[]{:S(2)}, u32[]{:S(2)}) collective-permute-start(bf16[2,2,192,128]{3,2,1,0:T(8,128)(2,1)S(1)} %add_chunk2_step2.1), channel_id=1, source_target_pairs={{0,4},{1,5},{2,6},{3,7},{4,0},{5,1},{6,2},{7,3},{8,12},{9,13},{10,... | collective-permute-start | bytes 589832 | tf_op jit(solution)/shard_map/ppermute | solution.py:441
  43.0 6.0 %collective-permute-start.5 = (bf16[2,224,128]{2,1,0:T(8,128)(2,1)S(1)}, bf16[2,224,128]{2,1,0:T(8,128)(2,1)S(1)}, u32[]{:S(2)}, u32[]{:S(2)}) collective-permute-start(bf16[2,224,128]{2,1,0:T(8,128)(2,1)S(1)} %add_chunk0_step3.1), channel_id=1, source_target_pairs={{0,8},{1,9},{2,10},{3,11},{4,12},{5,13},{6,14},{7,15},{8,0},{9,1},... | collective-permute-start | bytes 344072 | tf_op jit(solution)/shard_map/ppermute | solution.py:441
  46.3 5.9 %collective-permute-start.10 = (bf16[2,208,128]{2,1,0:T(8,128)(2,1)S(1)}, bf16[2,208,128]{2,1,0:T(8,128)(2,1)S(1)}, u32[]{:S(2)}, u32[]{:S(2)}) collective-permute-start(bf16[2,208,128]{2,1,0:T(8,128)(2,1)S(1)} %add_chunk1_step3.1), channel_id=1, source_target_pairs={{0,4},{1,5},{2,6},{3,7},{4,0},{5,1},{6,2},{7,3},{8,12},{9,13},{10,... | collective-permute-start | bytes 319496 | tf_op jit(solution)/shard_map/ppermute | solution.py:441
  46.9 6.9 %collective-permute-start.15 = (bf16[2,192,128]{2,1,0:T(8,128)(2,1)S(1)}, bf16[2,192,128]{2,1,0:T(8,128)(2,1)S(1)}, u32[]{:S(2)}, u32[]{:S(2)}) collective-permute-start(bf16[2,192,128]{2,1,0:T(8,128)(2,1)S(1)} %add_chunk2_step3.1), channel_id=1, source_target_pairs={{0,2},{1,3},{2,0},{3,1},{4,6},{5,7},{6,4},{7,5},{8,10},{9,11},{10,... | collective-permute-start | bytes 294920 | tf_op jit(solution)/shard_map/ppermute | solution.py:441
  49.1 8.2 %collective-permute-start.6 = (bf16[224,128]{1,0:T(8,128)(2,1)S(1)}, bf16[224,128]{1,0:T(8,128)(2,1)S(1)}, u32[]{:S(2)}, u32[]{:S(2)}) collective-permute-start(bf16[224,128]{1,0:T(8,128)(2,1)S(1)} %add_chunk0_step4.1), channel_id=1, source_target_pairs={{0,16},{1,17},{2,18},{3,19},{4,20},{5,21},{6,22},{7,23},{8,24},{9,... | collective-permute-start | bytes 172040 | tf_op jit(solution)/shard_map/ppermute | solution.py:441
  52.2 5.1 %collective-permute-start.11 = (bf16[208,128]{1,0:T(8,128)(2,1)S(1)}, bf16[208,128]{1,0:T(8,128)(2,1)S(1)}, u32[]{:S(2)}, u32[]{:S(2)}) collective-permute-start(bf16[208,128]{1,0:T(8,128)(2,1)S(1)} %add_chunk1_step4.1), channel_id=1, source_target_pairs={{0,16},{1,17},{2,18},{3,19},{4,20},{5,21},{6,22},{7,23},{8,24},{9,... | collective-permute-start | bytes 159752 | tf_op jit(solution)/shard_map/ppermute | solution.py:441
  53.8 5.6 %collective-permute-start.16 = (bf16[192,128]{1,0:T(8,128)(2,1)S(1)}, bf16[192,128]{1,0:T(8,128)(2,1)S(1)}, u32[]{:S(2)}, u32[]{:S(2)}) collective-permute-start(bf16[192,128]{1,0:T(8,128)(2,1)S(1)} %add_chunk2_step4.1), channel_id=1, source_target_pairs={{0,16},{1,17},{2,18},{3,19},{4,20},{5,21},{6,22},{7,23},{8,24},{9,... | collective-permute-start | bytes 147464 | tf_op jit(solution)/shard_map/ppermute | solution.py:441

commit v5 on v4

v5 whole, which is shorter than its diff:
```python
import functools

import jax
import jax.numpy as jnp
from jax import lax
from jax.experimental import pallas as pl
from jax.experimental.pallas import tpu as pltpu
from jax.sharding import PartitionSpec as P

LANES = 128
VMEM_BYTES = 24 * 1024 * 1024
ADD_BYTES = 8 * 1024 * 1024
CHAINS = (("x", "y", "z0", "z1"), ("y", "z0", "x", "z1"), ("z0", "x", "y", "z1"))
EXTRA = (16, 0, 0)
NN = (((1,), (0,)), ((), ()))
NT = (((1,), (1,)), ((), ()))
TN = (((0,), (0,)), ((), ()))


def dot(left, right, dims):
    return lax.dot_general(left, right, dims, preferred_element_type=jnp.float32)


def held(arrays, space=pltpu.VMEM):
    return [pltpu.with_memory_space_constraint(x, space) for x in arrays]


def around(x, axis, by):
    count = lax.axis_size(axis)
    return lax.ppermute(x, axis, [(i, (i + by) % count) for i in range(count)])


def column(row, rows):
    return jnp.broadcast_to(row, (LANES, rows)).T


def cost(flops, moved):
    return pl.CostEstimate(flops=flops, bytes_accessed=moved, transcendentals=0)


def pack_kernel(tail_x, tail_gs, tail_gk, weight, message):
    halo, channels = tail_gs.shape
    by_row = column(weight[...], LANES)[LANES - halo :]
    by_row = jnp.concatenate([by_row] * (channels // LANES), axis=1)
    message[0 : 2 * halo] = tail_x[...]
    message[2 * halo : 3 * halo] = (tail_gs[...].astype(jnp.float32) * by_row).astype(jnp.bfloat16)
    message[3 * halo :] = (tail_gk[...].astype(jnp.float32) * by_row).astype(jnp.bfloat16)


def pack(halo, x, grad_stream_out, grad_skip_out, weight):
    length, channels = x.shape

    def last(rows):
        return pl.BlockSpec((rows, channels), lambda i: (length // rows - 1, 0))

    return pl.pallas_call(
        pack_kernel,
        grid=(1,),
        in_specs=[last(2 * halo), last(halo), last(halo), pl.BlockSpec((1, LANES), lambda i: (0, length // LANES - 1))],
        out_specs=pl.BlockSpec((4 * halo, channels), lambda i: (0, 0)),
        out_shape=jax.ShapeDtypeStruct((4 * halo, channels), jnp.bfloat16),
        compiler_params=pltpu.CompilerParams(vmem_limit_bytes=ADD_BYTES),
        name="pack_borders",
    )(*held((x, grad_stream_out, grad_skip_out, weight), pltpu.HBM))


def load_kernel(
    x, gs, gk, weight, conv_w, out_w, _, x_here, grad_stream, grad_skip, sums, conv_here, out_here,
    gs_raw, gk_raw, weight_here, sems,
):
    some = pl.ds(0, conv_here.shape[0])
    pairs = (
        (weight, weight_here), (gs, gs_raw), (gk, gk_raw), (x, x_here),
        (conv_w.at[some], conv_here), (out_w.at[some], out_here),
    )
    copies = [pltpu.make_async_copy(a, b, sems.at[i]) for i, (a, b) in enumerate(pairs)]
    for copy in copies:
        copy.start()
    for copy in copies[:3]:
        copy.wait()
    length, channels = x_here.shape
    by_row = column(weight_here[...], length)
    by_row = jnp.concatenate([by_row] * (channels // LANES), axis=1)
    grad_stream[...] = gs_raw[...].astype(jnp.float32) * by_row
    grad_skip[...] = (gk_raw[...].astype(jnp.float32) * by_row).astype(jnp.bfloat16)
    own_sum = jnp.broadcast_to(jnp.sum(weight_here[...], axis=1, keepdims=True), (1, LANES))
    sums[...] = split_rows(own_sum)
    for copy in copies[3:]:
        copy.wait()


def load_some(low, x, gs, gk, weight, conv_w, out_w, after):
    shape = x.shape
    vmem, anywhere = pl.BlockSpec(memory_space=pltpu.VMEM), pl.BlockSpec(memory_space=pl.ANY)
    return pl.pallas_call(
        load_kernel,
        in_specs=[anywhere] * 7,
        out_specs=[vmem] * 6,
        out_shape=[
            pltpu.VMEM(shape, jnp.bfloat16),
            pltpu.VMEM(shape, jnp.float32),
            pltpu.VMEM(shape, jnp.bfloat16),
            pltpu.VMEM((16, LANES), jnp.bfloat16),
            pltpu.VMEM((low,) + conv_w.shape[1:], jnp.bfloat16),
            pltpu.VMEM((low,) + out_w.shape[1:], jnp.bfloat16),
        ],
        scratch_shapes=[
            pltpu.VMEM(shape, jnp.bfloat16),
            pltpu.VMEM(shape, jnp.bfloat16),
            pltpu.VMEM(weight.shape, jnp.float32),
            pltpu.SemaphoreType.DMA((6,)),
        ],
        compiler_params=pltpu.CompilerParams(vmem_limit_bytes=ADD_BYTES),
        cost_estimate=cost(10**7, 5 * 10**6),
        name="load_some",
    )(*held((x, gs, gk, weight, conv_w, out_w), pltpu.HBM), *held([after]))


def split_rows(total):
    high = total.astype(jnp.bfloat16).astype(jnp.float32)
    middle = (total - high).astype(jnp.bfloat16).astype(jnp.float32)
    low = total - high - middle
    row = lax.broadcasted_iota(jnp.int32, (16, LANES), 0)
    rows = jnp.where(row == 0, high, jnp.where(row == 1, middle, jnp.where(row == 2, low, 0.0)))
    return rows.astype(jnp.bfloat16)


def joined_rows(rows):
    return jnp.sum(rows.astype(jnp.float32), axis=0, keepdims=True)


def cut_off(rows, dilation):
    row = lax.broadcasted_iota(jnp.int32, rows.shape, 0)
    return jnp.where(jnp.logical_and(row < dilation, lax.axis_index("tm") == 0), 0.0, rows)


def items_of(layers, chunk):
    third = layers // len(CHAINS)
    high = layers - chunk * third
    items = []
    for index in reversed(range(high - third, high)):
        items.append((index, False))
        if chunk == 0 or index < high - 1:
            items.append((index, True))
    return items + ([(high - third - 1, True)] if high > third else [])


def backward(plan, layers, refs_of, weights_of, grad_proj, grad_stream, past_part, total, grad_parts):
    halo, length, channels = plan["halo"], plan["length"], plan["channels"]
    own = slice(halo, halo + length)
    items = plan["items"]

    def out_grad(index):
        if (index, True) in items:
            total[0:channels] = dot(refs_of(index)[2][own], grad_proj[0:length], TN)
            plan["store"](total, channels, items.index((index, True)), grad_parts)

    for index in layers:
        dilation, count = 2**index, plan["counts"][index]
        operands, factors, _ = refs_of(index)
        conv_layer, out_layer = weights_of(index)
        grad_proj[0:count, :channels] = grad_stream[0:count].astype(jnp.bfloat16)
        grad_gated = dot(grad_proj[0:count], out_layer[...], NT)
        out_grad(index)
        both = factors[halo : halo + count]
        grad_preact = jnp.concatenate(
            [grad_gated * both[:, :channels], grad_gated * both[:, channels:]], axis=1
        ).astype(jnp.bfloat16)
        spread = dot(grad_preact, conv_layer[...], NT)
        past_part[0:count] = spread[:, channels:]
        cut = slice(halo, halo + max(dilation, 8))
        past_part[cut] = cut_off(past_part[cut], dilation)
        rows = plan["counts"][index - 1] if index else length
        grad_stream[0:rows] += spread[0:rows, :channels] + past_part[dilation : dilation + rows]
        total[...] = dot(operands[own], grad_preact[0:length], TN)
        plan["store"](total, 2 * channels, items.index((index, False)), grad_parts)
    after = layers[-1] - 1
    if (after, True) in items:
        grad_proj[0:length, :channels] = grad_stream[0:length].astype(jnp.bfloat16)
        out_grad(after)


def first_kernel(
    plan, prev_rows, own_x, own_grad, own_skip, sums, conv_low, out_low, conv_w, out_w,
    low_operands, low_factors, low_gates, grad_stream, grad_skip, *rest,
):
    grad_parts = rest[:-10]
    stream, operands, factors, gates, grad_proj, past_part, total, conv_high, out_high, sems = rest[-10:]
    halo, (length, channels) = plan["halo"], own_x.shape
    layers, low = conv_w.shape[0], low_gates.shape[0]
    copies = {}
    for index in range(low, layers):
        at = 2 * (index - low)
        copies[index] = (
            pltpu.make_async_copy(conv_w.at[index], conv_high.at[index - low], sems.at[at]),
            pltpu.make_async_copy(out_w.at[index], out_high.at[index - low], sems.at[at + 1]),
        )
        for copy in copies[index]:
            copy.start()
    pad = 2 ** (layers - 1)
    extent = length + 2 * halo
    begin = 2 * halo
    stream[0:pad] = jnp.zeros((pad, channels), jnp.float32)
    stream[pad : pad + begin] = prev_rows[0:begin].astype(jnp.float32)
    stream[pad + begin :] = own_x[...].astype(jnp.float32)

    def refs_of(index):
        if index < low:
            return low_operands.at[index], low_factors.at[index], low_gates.at[index]
        return operands.at[index - low], factors.at[index - low], gates.at[index - low]

    def weights_of(index):
        if index < low:
            return conv_low.at[index], out_low.at[index]
        return conv_high.at[index - low], out_high.at[index - low]

    for index in range(layers):
        dilation, start = 2**index, plan["starts"][index]
        operand, factor, gate = refs_of(index)
        conv_layer, out_layer = weights_of(index)
        operand[start:, :channels] = stream[pad + start :].astype(jnp.bfloat16)
        operand[start:, channels:] = stream[pad + start - dilation : pad + extent - dilation].astype(jnp.bfloat16)
        slab = max(dilation, 16)
        earlier = stream[pad + begin - dilation : pad + begin - dilation + slab]
        operand[begin : begin + slab, channels:] = cut_off(earlier, dilation).astype(jnp.bfloat16)
        for copy in copies.get(index, ()):
            copy.wait()
        preact = dot(operand[start:], conv_layer[...], NN)
        filtered = jnp.tanh(preact[:, :channels])
        opening = 0.5 + 0.5 * jnp.tanh(0.5 * preact[:, channels:])
        product = filtered * opening
        gate[start:] = product.astype(jnp.bfloat16)
        factor[start:, :channels] = opening - filtered * product
        factor[start:, channels:] = product * (1.0 - opening)
        if index < layers - 1:
            stream[pad + start :] += dot(gate[start:], out_layer[:, :channels], NN)

    grad_stream[0:halo] = prev_rows[2 * halo : 3 * halo].astype(jnp.float32)
    grad_stream[halo:] = own_grad[...]
    grad_skip[0:halo] = prev_rows[3 * halo :]
    grad_skip[halo:] = own_skip[...]
    grad_proj[:, channels:] = grad_skip[...]
    backward(
        plan, list(reversed(range(low, layers))), refs_of, weights_of,
        grad_proj, grad_stream, past_part, total, grad_parts,
    )
    plan["finish"](sums, grad_parts)


def later_kernel(
    plan, first, third, low_operands, low_factors, low_gates, grad_before, grad_skip, conv_w, out_w, *rest
):
    *outs, keep, send, grad_stream, grad_proj, past_part, total = rest[plan["unused"] :]
    channels = plan["channels"]
    grad_stream[...] = grad_before[...]
    grad_proj[:, channels:] = grad_skip[...]

    def refs_of(index):
        return low_operands.at[index], low_factors.at[index], low_gates.at[index]

    def weights_of(index):
        return conv_w.at[index], out_w.at[index]

    backward(
        plan, list(reversed(range(first, first + third))), refs_of, weights_of,
        grad_proj, grad_stream, past_part, total, (keep, send),
    )
    at = 0
    for out in outs:
        out[...] = grad_stream[at : at + out.shape[0]]
        at += out.shape[0]


def store_whole(items, total, height, item, grad_parts):
    is_out = items[item][1]
    place = sum(kind == is_out for _, kind in items[:item])
    grad_parts[int(is_out)][place] = total[0:height].astype(jnp.bfloat16)


def finish_whole(sums, grad_parts):
    pass


def finish_shards(extra, sums, grad_parts):
    for part in grad_parts:
        lead, rows = part.shape[:-2], part.shape[-2]
        for first in range(rows - extra, rows, 16):
            part[(slice(None),) * len(lead) + (slice(first, first + 16),)] = jnp.broadcast_to(
                sums[...], lead + sums.shape
            )


def store_shards(tm, dp, order, bases, total, height, item, grad_parts):
    keep, send = grad_parts
    t_at, d_at = lax.axis_index("tm"), lax.axis_index("dp")
    core_at = lax.rem(d_at, 2)
    rows = height // tm
    at = pl.ds(bases[item], rows)
    at_bits = bits_of(t_at, d_at, lax.rem, lax.div)
    for y in range(dp // 2):
        near = total[0:height, (2 * y) * LANES : (2 * y + 1) * LANES]
        far = total[0:height, (2 * y + 1) * LANES : (2 * y + 2) * LANES]
        mine = jnp.where(core_at == 0, near, far).astype(jnp.bfloat16)
        other = jnp.where(core_at == 0, far, near).astype(jnp.bfloat16)
        for t in range(tm):
            bits = bits_of(t, 2 * y, lambda a, b: a % b, lambda a, b: a // b)
            lead = tuple(lax.rem(bits[name] + at_bits[name], 2) for name in order)
            keep[lead + (at,)] = mine[t * rows : (t + 1) * rows]
            send[lead + (at,)] = other[t * rows : (t + 1) * rows]


def bits_of(t, d, rem, div):
    return {"x": rem(t, 2), "z0": rem(div(t, 2), 2), "z1": div(t, 4), "y": div(d, 2)}


def bases_of(items, tm, channels):
    ends = [0]
    for _, is_out in items:
        ends.append(ends[-1] + (1 if is_out else 2) * channels // tm)
    return ends[:-1], ends[-1]


def run_layers(in_shards, tm, dp, halo, prev_rows, loaded, conv_w, out_w):
    own_x, own_grad, own_skip, sums, conv_low, out_low = loaded
    length, channels = own_x.shape
    layers, low = conv_w.shape[0], conv_low.shape[0]
    third = layers - low
    extent, border = length + 2 * halo, length + halo
    starts = []
    for index in range(layers):
        need = halo if index == layers - 1 else 2 ** (index + 1)
        starts.append(need // 16 * 16)
    counts = [-(-(length + 2 ** (index + 1) - 1) // 16) * 16 for index in range(layers)]
    plan = {"halo": halo, "starts": starts, "counts": counts, "length": length, "channels": channels, "unused": 0}
    plans, shapes = [], []
    for chunk, order in enumerate(CHAINS):
        items = items_of(layers, chunk)
        bases, rows = bases_of(items, tm, channels)
        if in_shards:
            store = functools.partial(store_shards, tm, dp, order, bases)
            finish = functools.partial(finish_shards, EXTRA[chunk])
            shapes.append(2 * [(2,) * len(order) + (rows + EXTRA[chunk], LANES)])
        else:
            store, finish = functools.partial(store_whole, items), finish_whole
            outs = sum(is_out for _, is_out in items)
            shapes.append([(len(items) - outs,) + conv_w.shape[1:], (outs,) + out_w.shape[1:]])
        plans.append(plan | {"items": items, "store": store, "finish": finish})
    vmem, anywhere = pl.BlockSpec(memory_space=pltpu.VMEM), pl.BlockSpec(memory_space=pl.ANY)
    weight_bytes = 2 * (conv_w.size + out_w.size)
    flops = 2 * length * channels * channels
    *kept, grad_stream, grad_skip, keep, send = pl.pallas_call(
        functools.partial(first_kernel, plans[0]),
        in_specs=[vmem] * 7 + [anywhere] * 2,
        out_specs=[vmem] * 7,
        out_shape=[
            pltpu.VMEM((low, extent, 2 * channels), jnp.bfloat16),
            pltpu.VMEM((low, extent, 2 * channels), jnp.float32),
            pltpu.VMEM((low, extent, channels), jnp.bfloat16),
            pltpu.VMEM((border, channels), jnp.float32),
            pltpu.VMEM((border, channels), jnp.bfloat16),
        ]
        + [pltpu.VMEM(shape, jnp.bfloat16) for shape in shapes[0]],
        scratch_shapes=[
            pltpu.VMEM((2 ** (layers - 1) + extent, channels), jnp.float32),
            pltpu.VMEM((third, extent, 2 * channels), jnp.bfloat16),
            pltpu.VMEM((third, extent, 2 * channels), jnp.float32),
            pltpu.VMEM((third, extent, channels), jnp.bfloat16),
            pltpu.VMEM((border, 2 * channels), jnp.bfloat16),
            pltpu.VMEM((border, channels), jnp.float32),
            pltpu.VMEM((2 * channels, 2 * channels), jnp.float32),
            pltpu.VMEM((third,) + conv_w.shape[1:], jnp.bfloat16),
            pltpu.VMEM((third,) + out_w.shape[1:], jnp.bfloat16),
            pltpu.SemaphoreType.DMA((2 * third,)),
        ],
        compiler_params=pltpu.CompilerParams(vmem_limit_bytes=VMEM_BYTES),
        cost_estimate=cost(flops * (5 * layers + 12 * third), weight_bytes),
        name="forward_and_last_third",
    )(*held((prev_rows, own_x, own_grad, own_skip, sums, conv_low, out_low)), *held((conv_w, out_w), pltpu.HBM))

    def later(step, outs, after):
        return pl.pallas_call(
            functools.partial(later_kernel, plans[step] | {"unused": len(after)}, layers - (step + 1) * third, third),
            in_specs=[vmem] * 7 + [anywhere] * len(after),
            out_specs=[vmem] * (len(outs) + 2),
            out_shape=[pltpu.VMEM((rows, channels), jnp.float32) for rows in outs]
            + [pltpu.VMEM(shape, jnp.bfloat16) for shape in shapes[step]],
            scratch_shapes=[
                pltpu.VMEM((border, channels), jnp.float32),
                pltpu.VMEM((border, 2 * channels), jnp.bfloat16),
                pltpu.VMEM((border, channels), jnp.float32),
                pltpu.VMEM((2 * channels, 2 * channels), jnp.float32),
            ],
            compiler_params=pltpu.CompilerParams(vmem_limit_bytes=VMEM_BYTES),
            cost_estimate=cost(flops * 12 * third, weight_bytes),
            name="middle_third" if step == 1 else "first_third",
        )(*held((*kept, grad_stream, grad_skip, conv_low, out_low, *after)))

    parts = [(keep, send)]
    if in_shards:
        parts[0] = Chunk(tm, dp, 0, keep, send)
    grad_stream, *middle = later(1, [border], [])
    other, own, *last = later(2, [halo, length - halo], [parts[0].next_message()] if in_shards else [])
    parts += [middle, last]
    if in_shards:
        for step in (1, 2):
            parts[step] = Chunk(tm, dp, step, *parts[step])
    return other, own, parts


def add_kernel(count, groups, *refs):
    arrays, outs = refs[:count], refs[-len(groups) :]
    for out, pieces in zip(outs, groups):
        lead = (slice(None),) * (len(out.shape) - 2)
        for first, rows, with_total, terms in pieces:
            body = rows - 16 if with_total else rows
            value = 0.0
            for array, at, begin in terms:
                value = value + arrays[array][at + lead + (slice(begin, begin + body),)].astype(jnp.float32)
            out[lead + (slice(first, first + body),)] = value.astype(out.dtype)
            if with_total:
                total = 0.0
                for array, at, begin in terms:
                    rows_at = slice(begin + body, begin + rows)
                    total = total + joined_rows(arrays[array][at + (0,) * len(lead) + (rows_at,)])
                slab = split_rows(total)
                out[lead + (slice(first + body, first + rows),)] = jnp.broadcast_to(slab, out.shape[:-2] + slab.shape)


def add_up(arrays, groups, shapes, after, name):
    vmem = pl.BlockSpec(memory_space=pltpu.VMEM)
    return pl.pallas_call(
        functools.partial(add_kernel, len(arrays), groups),
        in_specs=[vmem] * len(arrays) + [pl.BlockSpec(memory_space=pl.ANY)] * len(after),
        out_specs=[vmem] * len(groups),
        out_shape=[pltpu.VMEM(shape, jnp.bfloat16) for shape in shapes],
        compiler_params=pltpu.CompilerParams(vmem_limit_bytes=ADD_BYTES),
        name=name,
    )(*held(arrays), *held(after))


def first_block(array, first, rows):
    return array[(0,) * (len(array.shape) - 2) + (slice(first, first + rows),)].astype(jnp.float32)


def first_block(array, first, rows):
    return array[(0,) * (len(array.shape) - 2) + (slice(first, first + rows),)].astype(jnp.float32)


def last_kernel(counts, samples_all, tm, *refs):
    chunks = []
    for count in counts:
        chunks.append(refs[:count])
        refs = refs[count:]
    other, own, grad_inputs, grad_conv, grad_out = refs
    layers, channels = grad_conv.shape[0], own.shape[1]
    total = 0.0
    for term in chunks[0]:
        total = total + jnp.sum(first_block(term, term.shape[-2] - 16, 16), axis=0, keepdims=True)
    scale = samples_all / total
    for chunk, terms in enumerate(chunks):
        items = items_of(layers, chunk)
        for (index, is_out), base in zip(items, bases_of(items, tm, channels)[0]):
            out = grad_out if is_out else grad_conv
            value = 0.0
            for term in terms:
                value = value + first_block(term, base, out.shape[1])
            out[index] = value * scale
    for first in range(0, channels, LANES):
        lanes = slice(first, first + LANES)
        grad_inputs[0 : own.shape[0], lanes] = own[:, lanes] * scale
        grad_inputs[own.shape[0] :, lanes] = other[:, lanes] * scale


class Chunk:
    def __init__(self, tm, dp, chunk, keep, send):
        self.tm, self.dp, self.chunk, self.rows = tm, dp, chunk, keep.shape[-2]
        self.message = None
        self.terms = [keep, swapped(tm, dp, send, "core")]

    def next_message(self, after=()):
        if self.message is None:
            left = len(CHAINS[self.chunk]) + 2 - len(self.terms)
            pieces = []
            for i, v in enumerate(self.terms):
                pieces.append((i, (0,) * (len(v.shape) - 2 - left) + (1,), 0))
            (self.message,) = add_up(
                self.terms, [[(0, self.rows, self.chunk == 0, pieces)]], [(2,) * (left - 1) + (self.rows, LANES)], after,
                "add_chunk%d_step%d" % (self.chunk, len(self.terms) - 1),
            )
        return self.message

    def run_chain(self, after=()):
        for step, name in enumerate(CHAINS[self.chunk]):
            self.terms.append(swapped(self.tm, self.dp, self.next_message(after if step == 1 else ()), name))
            self.message = None
        return self.terms


def swapped(tm, dp, value, name):
    over_t, over_d = {"core": (0, 1), "y": (0, 2), "x": (1, 0), "z0": (2, 0), "z1": (4, 0)}[name]
    pairs = [(t * dp + d, (t ^ over_t) * dp + (d ^ over_d)) for t in range(tm) for d in range(dp)]
    return lax.ppermute(value, ("tm", "dp"), pairs)


def scattered(part):
    columns = lax.psum_scatter(part, "dp", scatter_dimension=2, tiled=True).astype(jnp.float32)
    return lax.psum_scatter(columns, "tm", scatter_dimension=1, tiled=True)


def body(inputs, grad_stream_out, grad_skip_out, sample_weight, conv_weight, out_weight):
    tm, dp = lax.axis_size("tm"), lax.axis_size("dp")
    batch, length, channels = inputs.shape
    layers = conv_weight.shape[0]
    third = layers // len(CHAINS)
    halo = 2**layers
    samples_all = batch * length * tm * dp
    x, gs, gk = inputs[0], grad_stream_out[0], grad_skip_out[0]
    message = pack(halo, x, gs, gk, sample_weight)
    prev_rows = around(message, "tm", 1)
    loaded = load_some(layers - third, x, gs, gk, sample_weight, conv_weight, out_weight, message)
    in_shards = tm == 8 and dp == 4 and channels // tm % 16 == 0 and 2 * channels == dp * LANES
    other, own, parts = run_layers(in_shards, tm, dp, halo, prev_rows, loaded, conv_weight, out_weight)
    other = around(other, "tm", -1)
    if not in_shards:
        scale = samples_all / lax.psum(jnp.sum(sample_weight), ("tm", "dp"))
        found = {}
        for chunk, part in enumerate(parts):
            items = items_of(layers, chunk)
            for is_out in (False, True):
                for place, item in enumerate(item for item in items if item[1] == is_out):
                    found[item] = part[int(is_out)][place]
        grad_conv, grad_out = (
            scattered(jnp.stack([found[index, is_out] for index in range(layers)])) * scale for is_out in (False, True)
        )
        return (jnp.concatenate([own, other]) * scale)[None], grad_conv, grad_out
    chunks = [part.run_chain([other] if part is parts[0] else ()) for part in parts]
    conv_rows, out_rows = 2 * channels // tm, channels // tm
    grad_inputs, grad_conv, grad_out = pl.pallas_call(
        functools.partial(last_kernel, [len(terms) for terms in chunks], float(samples_all), tm),
        out_shape=[
            jax.ShapeDtypeStruct((length, channels), jnp.float32),
            jax.ShapeDtypeStruct((layers, conv_rows, LANES), jnp.float32),
            jax.ShapeDtypeStruct((layers, out_rows, LANES), jnp.float32),
        ],
        compiler_params=pltpu.CompilerParams(vmem_limit_bytes=ADD_BYTES),
        name="scale_all",
    )(*held([term for terms in chunks for term in terms]), *held([other, own]))
    return grad_inputs[None], grad_conv, grad_out


def solution(mesh):
    placed = (
        P("dp", "tm", None),
        P("dp", "tm", None),
        P("dp", "tm", None),
        P("dp", "tm"),
        P(),
        P(),
    )
    return jax.shard_map(
        body,
        mesh=mesh,
        in_specs=placed,
        out_specs=(P("dp", "tm", None), P(None, "tm", "dp"), P(None, "tm", "dp")),
        check_vma=False,
    )
```

time: 60.6 us -> 60 us (0.990)
  starting transfers between devices: 31.1 us -> 16.5 us
  waiting for transfers between devices: 13.7 us -> 26.6 us
  Pallas kernels: 14.8 us -> 15.9 us
    ppermute x15, starting transfers between devices: 24.3 us -> 10.3 us  [swapped(): return lax.ppermute(value, ('tm', 'dp'), pairs)]
    ppermute x2, waiting for transfers between devices: 0.07 us -> 13.9 us  [around(): return lax.ppermute(x, axis, [(i, (i + by) % count) for i in range(count)])]
    ppermute x15, waiting for transfers between devices: 13.7 us -> 12.7 us  [swapped(): return lax.ppermute(value, ('tm', 'dp'), pairs)]
  transfers between devices with their start and end apart: 17 -> 17, of which waited for: 6 -> 8; matrix products, arithmetic and copies ran while one was open for 0% -> 0% of each run, Pallas kernels for 11% -> 12%
where the time goes in v5:
time: 60 us; the launch traced here: 59.8 us
  waiting for transfers between devices  26.6 us (44%)
  starting transfers between devices  16.5 us (28%)
  Pallas kernels  15.9 us (26%)
  between operations  0.77 us (1%)
    ppermute x2, waiting for transfers between devices, around(): return lax.ppermute(x, axis, [(i, (i + by) % count) for i in range(count)])  13.9 us
    ppermute x15, waiting for transfers between devices, swapped(): return lax.ppermute(value, ('tm', 'dp'), pairs)  12.7 us
    ppermute x15, starting transfers between devices, swapped(): return lax.ppermute(value, ('tm', 'dp'), pairs)  10.3 us
    pallas_call x1, Pallas kernels, run_layers(): pl.pallas_call(functools.partial(first_kernel, plans[0]), in_specs=[vmem]...  6.79 us
    ppermute x2, starting transfers between devices, around(): return lax.ppermute(x, axis, [(i, (i + by) % count) for i in range(count)])  6.27 us
    pallas_call x2, Pallas kernels, later(): pl.pallas_call(functools.partial(later_kernel, plans[step] | {'unused': l...  4.15 us
    pallas_call x1, Pallas kernels, load_some(): pl.pallas_call(load_kernel, in_specs=[anywhere] * 7, out_specs=[vmem] * 6...  2.16 us
  transfers between devices with their start and end apart: 17, of which 8 were waited for; matrix products, arithmetic and copies ran while one was open for 0% of the time, Pallas kernels for 12%

profile of v5, /device:TPU:0, one launch (start us, length us, event | category | flops | bytes accessed | tf_op | source)
XLA Modules:
  0.0 59.8 jit_solution(13783409500301999223)
XLA Ops:
  0.6 1.0 %pack_borders.1._ = bf16[256,256]{1,0:T(8,128)(2,1)S(1)} custom-call(bf16[512,256]{1,0:T(8,128)(2,1)} %bitcast.4, bf16[512,256]{1,0:T(8,128)(2,1)} %bitcast.6, bf16[512,256]{1,0:T(8,128)(2,1)} %bitcast.8, f32[1,512]{1,0:T(1,128)} %weight.3), custom_call_target="tpu_custom_call" | custom-call | tf_op jit(solution)/shard_map/pack_borders/pallas_call | solution.py:56
  1.6 3.0 %collective-permute-start = (bf16[256,256]{1,0:T(8,128)(2,1)S(1)}, bf16[256,256]{1,0:T(8,128)(2,1)S(1)}, u32[]{:S(2)}, u32[]{:S(2)}) collective-permute-start(bf16[256,256]{1,0:T(8,128)(2,1)S(1)} %pack_borders.1._), channel_id=1, source_target_pairs={{0,4},{4,8},{8,12},{12,16},{16,20},{20,24},{24,28},{28,0},{1,5},{5... | collective-permute-start | bytes 393224 | tf_op jit(solution)/shard_map/ppermute | solution.py:30
  4.6 2.2 %load_some.1 = (bf16[512,256]{1,0:T(8,128)(2,1)S(1)}, f32[512,256]{1,0:T(8,128)S(1)}, bf16[512,256]{1,0:T(8,128)(2,1)S(1)}, bf16[16,128]{1,0:T(8,128)(2,1)S(1)},...) custom-call(bf16[512,256]{1,0:T(8,128)(2,1)} %bitcast.5, bf16[512,256]{1,0:T(8,128)(2,1)} %bitcast.7, ...), custom_call_target="tpu_custom_call" | custom-call | flops 10000000 | bytes 5000000 | tf_op jit(solution)/shard_map/load_some/pallas_call | solution.py:95
  6.8 4.4 %collective-permute-done.prev_rows = bf16[256,256]{1,0:T(8,128)(2,1)S(1)} collective-permute-done((bf16[256,256]{1,0:T(8,128)(2,1)S(1)}, bf16[256,256]{1,0:T(8,128)(2,1)S(1)}, u32[]{:S(2)}, u32[]{:S(2)}) %collective-permute-start) | collective-permute-done | bytes 131104 | tf_op jit(solution)/shard_map/ppermute | solution.py:30
  11.1 6.8 %forward_and_last_third.1 = (bf16[4,640,512]{2,1,0:T(8,128)(2,1)S(1)}, f32[4,640,512]{2,1,0:T(8,128)S(1)}, bf16[4,640,256]{2,1,0:T(8,128)(2,1)S(1)}, f32[576,256...) custom-call(bf16[256,256]{1,0:T(8,128)(2,1)S(1)} %collective-permute, ...), custom_call_target="tpu_custom_call" | custom-call | flops 3623878656 | bytes 4718592 | tf_op jit(solution)/shard_map/forward_and_last_third/pallas_call | solution.py:351
  17.9 0.1 collective-permute-start.1
  18.0 2.2 %middle_third.1 = (f32[576,256]{1,0:T(8,128)S(1)}, bf16[2,2,2,2,192,128]{5,4,3,2,1,0:T(8,128)(2,1)S(1)}, bf16[2,2,2,2,192,128]{5,4,3,2,1,0:T(8,128)(2,1)S(1)}) custom-call(bf16[4,640,512]{2,1,0:T(8,128)(2,1)S(1)} %get-tuple-element.34.low_operands, f32[4,640,512]{2,1,0:T(8,128)S(1)} %get-tuple-element.35.low_factors, ...), custom_call_target="tpu_custom_call" | custom-call | flops 1610612736 | bytes 4718592 | tf_op jit(solution)/shard_map/middle_third/pallas_call | solution.py:381
  20.2 0.6 collective-permute-start.7
  20.7 0.0 collective-permute-done.1.refs_1_
  20.7 0.1 add_chunk0_step1.1.rest_0_
  20.9 2.0 %first_third.1 = (f32[64,256]{1,0:T(8,128)S(1)}, f32[448,256]{1,0:T(8,128)S(1)}, bf16[2,2,2,2,160,128]{5,4,3,2,1,0:T(8,128)(2,1)S(1)}, bf16[2,2,2,2,160,128]{5,4,3,2,1,0:T(8,128)(2,1)S(1)}) custom-call(bf16[4,640,512]{2,1,0:T(8,128)(2,1)S(1)} %get-tuple-element.34.low_operands, f32[4,640,512]{2,1,0:T(8,128)S(1)} %get-tuple-element.35.low_factors, ...), custom_call_target="tpu_custom_call" | custom-call | flops 1610612736 | bytes 4718592 | tf_op jit(solution)/shard_map/first_third/pallas_call | solution.py:381
  22.9 0.1 collective-permute-start.12
  23.0 0.1 collective-permute-start.2
  23.0 0.0 collective-permute-done.7.refs_1_.refs_7_
  23.0 0.1 add_chunk1_step1.1
  23.1 1.6 %collective-permute-start.8 = (bf16[2,2,2,192,128]{4,3,2,1,0:T(8,128)(2,1)S(1)}, bf16[2,2,2,192,128]{4,3,2,1,0:T(8,128)(2,1)S(1)}, u32[]{:S(2)}, u32[]{:S(2)}) collective-permute-start(bf16[2,2,2,192,128]{4,3,2,1,0:T(8,128)(2,1)S(1)} %add_chunk1_step1.1), channel_id=1, source_target_pairs={{0,2},{1,3},{2,0},{3,1},{4,6},{5,7},{6,4},{7,5},{8,10},{9,11},{10,... | collective-permute-start | bytes 1179656 | tf_op jit(solution)/shard_map/ppermute | solution.py:502
  24.7 0.3 collective-permute-done.12.refs_1_.refs_13_
  25.0 0.1 add_chunk2_step1.1
  25.1 0.1 collective-permute-start.13
  25.2 3.3 %collective-permute-start.3 = (f32[64,256]{1,0:T(8,128)S(1)}, f32[64,256]{1,0:T(8,128)S(1)}, u32[]{:S(2)}, u32[]{:S(2)}) collective-permute-start(f32[64,256]{1,0:T(8,128)S(1)} %get-tuple-element.40), channel_id=1, source_target_pairs={{0,28},{4,0},{8,4},{12,8},{16,12},{20,16},{24,20},{28,24},{1,29},{... | collective-permute-start | bytes 196616 | tf_op jit(solution)/shard_map/ppermute | solution.py:30
  28.5 9.5 %collective-permute-done.3.refs_3_.refs_18_ = f32[64,256]{1,0:T(8,128)S(1)} collective-permute-done((f32[64,256]{1,0:T(8,128)S(1)}, f32[64,256]{1,0:T(8,128)S(1)}, u32[]{:S(2)}, u32[]{:S(2)}) %collective-permute-start.3) | collective-permute-done | bytes 65568 | tf_op jit(solution)/shard_map/ppermute | solution.py:30
  38.0 0.0 collective-permute-done.2.refs_2_
  38.0 0.1 add_chunk0_step2.1
  38.1 1.6 %collective-permute-start.4 = (bf16[2,2,240,128]{3,2,1,0:T(8,128)(2,1)S(1)}, bf16[2,2,240,128]{3,2,1,0:T(8,128)(2,1)S(1)}, u32[]{:S(2)}, u32[]{:S(2)}) collective-permute-start(bf16[2,2,240,128]{3,2,1,0:T(8,128)(2,1)S(1)} %add_chunk0_step2.1), channel_id=1, source_target_pairs={{0,2},{1,3},{2,0},{3,1},{4,6},{5,7},{6,4},{7,5},{8,10},{9,11},{10,... | collective-permute-start | bytes 737288 | tf_op jit(solution)/shard_map/ppermute | solution.py:502
  39.7 0.0 collective-permute-done.8.refs_2_.refs_8_
  39.7 0.1 add_chunk1_step2.1
  39.8 0.1 collective-permute-start.9
  39.8 0.0 collective-permute-done.13.refs_2_.refs_14_
  39.9 0.1 add_chunk2_step2.1
  39.9 0.3 collective-permute-start.14
  40.3 5.4 %collective-permute-done.4.refs_3_ = bf16[2,2,240,128]{3,2,1,0:T(8,128)(2,1)S(1)} collective-permute-done((bf16[2,2,240,128]{3,2,1,0:T(8,128)(2,1)S(1)}, bf16[2,2,240,128]{3,2,1,0:T(8,128)(2,1)S(1)}, u32[]{:S(2)}, u32[]{:S(2)}) %collective-permute-start.4) | collective-permute-done | bytes 245792 | tf_op jit(solution)/shard_map/ppermute | solution.py:502
  45.7 0.1 add_chunk0_step3.1
  45.8 0.1 collective-permute-start.5
  45.8 0.2 collective-permute-done.9.refs_3_.refs_9_
  46.0 0.1 add_chunk1_step3.1
  46.1 0.5 collective-permute-start.10
  46.6 0.0 collective-permute-done.14.refs_3_.refs_15_
  46.6 1.4 %collective-permute-start.15 = (bf16[2,160,128]{2,1,0:T(8,128)(2,1)S(1)}, bf16[2,160,128]{2,1,0:T(8,128)(2,1)S(1)}, u32[]{:S(2)}, u32[]{:S(2)}) collective-permute-start(bf16[2,160,128]{2,1,0:T(8,128)(2,1)S(1)} %add_chunk2_step3.1), channel_id=1, source_target_pairs={{0,2},{1,3},{2,0},{3,1},{4,6},{5,7},{6,4},{7,5},{8,10},{9,11},{10,... | collective-permute-start | bytes 245768 | tf_op jit(solution)/shard_map/ppermute | solution.py:502
  48.1 2.6 %collective-permute-done.5.refs_4_ = bf16[2,240,128]{2,1,0:T(8,128)(2,1)S(1)} collective-permute-done((bf16[2,240,128]{2,1,0:T(8,128)(2,1)S(1)}, bf16[2,240,128]{2,1,0:T(8,128)(2,1)S(1)}, u32[]{:S(2)}, u32[]{:S(2)}) %collective-permute-start.5) | collective-permute-done | bytes 122912 | tf_op jit(solution)/shard_map/ppermute | solution.py:502
  50.7 0.1 add_chunk0_step4.1
  50.8 0.8 %collective-permute-start.6 = (bf16[240,128]{1,0:T(8,128)(2,1)S(1)}, bf16[240,128]{1,0:T(8,128)(2,1)S(1)}, u32[]{:S(2)}, u32[]{:S(2)}) collective-permute-start(bf16[240,128]{1,0:T(8,128)(2,1)S(1)} %add_chunk0_step4.1), channel_id=1, source_target_pairs={{0,16},{1,17},{2,18},{3,19},{4,20},{5,21},{6,22},{7,23},{8,24},{9,... | collective-permute-start | bytes 184328 | tf_op jit(solution)/shard_map/ppermute | solution.py:502
  51.5 0.0 collective-permute-done.10.refs_4_.refs_10_
  51.6 2.3 %collective-permute-start.11 = (bf16[192,128]{1,0:T(8,128)(2,1)S(1)}, bf16[192,128]{1,0:T(8,128)(2,1)S(1)}, u32[]{:S(2)}, u32[]{:S(2)}) collective-permute-start(bf16[192,128]{1,0:T(8,128)(2,1)S(1)} %add_chunk1_step4.1), channel_id=1, source_target_pairs={{0,16},{1,17},{2,18},{3,19},{4,20},{5,21},{6,22},{7,23},{8,24},{9,... | collective-permute-start | bytes 147464 | tf_op jit(solution)/shard_map/ppermute | solution.py:502
  53.9 0.0 collective-permute-done.15.refs_4_.refs_16_
  53.9 0.8 %collective-permute-start.16 = (bf16[160,128]{1,0:T(8,128)(2,1)S(1)}, bf16[160,128]{1,0:T(8,128)(2,1)S(1)}, u32[]{:S(2)}, u32[]{:S(2)}) collective-permute-start(bf16[160,128]{1,0:T(8,128)(2,1)S(1)} %add_chunk2_step4.1), channel_id=1, source_target_pairs={{0,16},{1,17},{2,18},{3,19},{4,20},{5,21},{6,22},{7,23},{8,24},{9,... | collective-permute-start | bytes 122888 | tf_op jit(solution)/shard_map/ppermute | solution.py:502
  54.7 2.3 %collective-permute-done.11.refs_11_ = bf16[192,128]{1,0:T(8,128)(2,1)S(1)} collective-permute-done((bf16[192,128]{1,0:T(8,128)(2,1)S(1)}, bf16[192,128]{1,0:T(8,128)(2,1)S(1)}, u32[]{:S(2)}, u32[]{:S(2)}) %collective-permute-start.11) | collective-permute-done | bytes 49184 | tf_op jit(solution)/shard_map/ppermute | solution.py:502
  56.9 0.0 collective-permute-done.6.refs_5_
  57.0 1.9 %collective-permute-done.16.refs_17_ = bf16[160,128]{1,0:T(8,128)(2,1)S(1)} collective-permute-done((bf16[160,128]{1,0:T(8,128)(2,1)S(1)}, bf16[160,128]{1,0:T(8,128)(2,1)S(1)}, u32[]{:S(2)}, u32[]{:S(2)}) %collective-permute-start.16) | collective-permute-done | bytes 40992 | tf_op jit(solution)/shard_map/ppermute | solution.py:502
  58.9 1.0 %scale_all.1 = (f32[512,256]{1,0:T(8,128)}, f32[6,64,128]{2,1,0:T(8,128)}, f32[6,32,128]{2,1,0:T(8,128)}) custom-call(bf16[2,2,2,2,240,128]{5,4,3,2,1,0:T(8,128)(2,1)S(1)} %get-tuple-element.32.refs_0_, bf16[2,2,2,2,240,128]{5,4,3,2,1,0:T(8,128)(2,1)S(1)} %collective-permute-done.1.refs_1_, bf16[2,2,2,240,128]{4,3,2,1,0:T(8,128)(2,1)S(1)} %collective-permute-done.2.refs_2_, ...), custom_call_target="tpu_custom_call" | custom-call | tf_op jit(solution)/shard_map/scale_all/pallas_call | solution.py:538
  (3 shorter events, 0.1 us)
Async XLA Ops:
  1.6 9.5 %collective-permute-start = (bf16[256,256]{1,0:T(8,128)(2,1)S(1)}, bf16[256,256]{1,0:T(8,128)(2,1)S(1)}, u32[]{:S(2)}, u32[]{:S(2)}) collective-permute-start(bf16[256,256]{1,0:T(8,128)(2,1)S(1)} %pack_borders.1._), channel_id=1, source_target_pairs={{0,4},{4,8},{8,12},{12,16},{16,20},{20,24},{24,28},{28,0},{1,5},{5... | collective-permute-start | bytes 393224 | tf_op jit(solution)/shard_map/ppermute | solution.py:30
  17.9 2.8 %collective-permute-start.1 = (bf16[2,2,2,2,240,128]{5,4,3,2,1,0:T(8,128)(2,1)S(1)}, bf16[2,2,2,2,240,128]{5,4,3,2,1,0:T(8,128)(2,1)S(1)}, u32[]{:S(2)}, u32[]{:S(2)}) collective-permute-start(bf16[2,2,2,2,240,128]{5,4,3,2,1,0:T(8,128)(2,1)S(1)} %get-tuple-element.33), channel_id=1, source_target_pairs={{0,1},{1,0},{2,3},{3,2},{4,5},{5,4},{6,7},{7,6},{8,9},{9,8},{10,11... | collective-permute-start | bytes 2949128 | tf_op jit(solution)/shard_map/ppermute | solution.py:502
  20.2 2.9 %collective-permute-start.7 = (bf16[2,2,2,2,192,128]{5,4,3,2,1,0:T(8,128)(2,1)S(1)}, bf16[2,2,2,2,192,128]{5,4,3,2,1,0:T(8,128)(2,1)S(1)}, u32[]{:S(2)}, u32[]{:S(2)}) collective-permute-start(bf16[2,2,2,2,192,128]{5,4,3,2,1,0:T(8,128)(2,1)S(1)} %get-tuple-element.42), channel_id=1, source_target_pairs={{0,1},{1,0},{2,3},{3,2},{4,5},{5,4},{6,7},{7,6},{8,9},{9,8},{10,11... | collective-permute-start | bytes 2359304 | tf_op jit(solution)/shard_map/ppermute | solution.py:502
  22.9 2.2 %collective-permute-start.12 = (bf16[2,2,2,2,160,128]{5,4,3,2,1,0:T(8,128)(2,1)S(1)}, bf16[2,2,2,2,160,128]{5,4,3,2,1,0:T(8,128)(2,1)S(1)}, u32[]{:S(2)}, u32[]{:S(2)}) collective-permute-start(bf16[2,2,2,2,160,128]{5,4,3,2,1,0:T(8,128)(2,1)S(1)} %get-tuple-element.44), channel_id=1, source_target_pairs={{0,1},{1,0},{2,3},{3,2},{4,5},{5,4},{6,7},{7,6},{8,9},{9,8},{10,11... | collective-permute-start | bytes 1966088 | tf_op jit(solution)/shard_map/ppermute | solution.py:502
  23.0 15.0 %collective-permute-start.2 = (bf16[2,2,2,240,128]{4,3,2,1,0:T(8,128)(2,1)S(1)}, bf16[2,2,2,240,128]{4,3,2,1,0:T(8,128)(2,1)S(1)}, u32[]{:S(2)}, u32[]{:S(2)}) collective-permute-start(bf16[2,2,2,240,128]{4,3,2,1,0:T(8,128)(2,1)S(1)} %add_chunk0_step1.1.rest_0_), channel_id=1, source_target_pairs={{0,4},{1,5},{2,6},{3,7},{4,0},{5,1},{6,2},{7,3},{8,12},{9,13},{10,... | collective-permute-start | bytes 1474568 | tf_op jit(solution)/shard_map/ppermute | solution.py:502
  23.1 16.6 %collective-permute-start.8 = (bf16[2,2,2,192,128]{4,3,2,1,0:T(8,128)(2,1)S(1)}, bf16[2,2,2,192,128]{4,3,2,1,0:T(8,128)(2,1)S(1)}, u32[]{:S(2)}, u32[]{:S(2)}) collective-permute-start(bf16[2,2,2,192,128]{4,3,2,1,0:T(8,128)(2,1)S(1)} %add_chunk1_step1.1), channel_id=1, source_target_pairs={{0,2},{1,3},{2,0},{3,1},{4,6},{5,7},{6,4},{7,5},{8,10},{9,11},{10,... | collective-permute-start | bytes 1179656 | tf_op jit(solution)/shard_map/ppermute | solution.py:502
  25.1 14.7 %collective-permute-start.13 = (bf16[2,2,2,160,128]{4,3,2,1,0:T(8,128)(2,1)S(1)}, bf16[2,2,2,160,128]{4,3,2,1,0:T(8,128)(2,1)S(1)}, u32[]{:S(2)}, u32[]{:S(2)}) collective-permute-start(bf16[2,2,2,160,128]{4,3,2,1,0:T(8,128)(2,1)S(1)} %add_chunk2_step1.1), channel_id=1, source_target_pairs={{0,8},{1,9},{2,10},{3,11},{4,12},{5,13},{6,14},{7,15},{8,0},{9,1},... | collective-permute-start | bytes 983048 | tf_op jit(solution)/shard_map/ppermute | solution.py:502
  25.2 12.8 %collective-permute-start.3 = (f32[64,256]{1,0:T(8,128)S(1)}, f32[64,256]{1,0:T(8,128)S(1)}, u32[]{:S(2)}, u32[]{:S(2)}) collective-permute-start(f32[64,256]{1,0:T(8,128)S(1)} %get-tuple-element.40), channel_id=1, source_target_pairs={{0,28},{4,0},{8,4},{12,8},{16,12},{20,16},{24,20},{28,24},{1,29},{... | collective-permute-start | bytes 196616 | tf_op jit(solution)/shard_map/ppermute | solution.py:30
  38.1 7.6 %collective-permute-start.4 = (bf16[2,2,240,128]{3,2,1,0:T(8,128)(2,1)S(1)}, bf16[2,2,240,128]{3,2,1,0:T(8,128)(2,1)S(1)}, u32[]{:S(2)}, u32[]{:S(2)}) collective-permute-start(bf16[2,2,240,128]{3,2,1,0:T(8,128)(2,1)S(1)} %add_chunk0_step2.1), channel_id=1, source_target_pairs={{0,2},{1,3},{2,0},{3,1},{4,6},{5,7},{6,4},{7,5},{8,10},{9,11},{10,... | collective-permute-start | bytes 737288 | tf_op jit(solution)/shard_map/ppermute | solution.py:502
  39.8 6.3 %collective-permute-start.9 = (bf16[2,2,192,128]{3,2,1,0:T(8,128)(2,1)S(1)}, bf16[2,2,192,128]{3,2,1,0:T(8,128)(2,1)S(1)}, u32[]{:S(2)}, u32[]{:S(2)}) collective-permute-start(bf16[2,2,192,128]{3,2,1,0:T(8,128)(2,1)S(1)} %add_chunk1_step2.1), channel_id=1, source_target_pairs={{0,8},{1,9},{2,10},{3,11},{4,12},{5,13},{6,14},{7,15},{8,0},{9,1},... | collective-permute-start | bytes 589832 | tf_op jit(solution)/shard_map/ppermute | solution.py:502
  39.9 6.7 %collective-permute-start.14 = (bf16[2,2,160,128]{3,2,1,0:T(8,128)(2,1)S(1)}, bf16[2,2,160,128]{3,2,1,0:T(8,128)(2,1)S(1)}, u32[]{:S(2)}, u32[]{:S(2)}) collective-permute-start(bf16[2,2,160,128]{3,2,1,0:T(8,128)(2,1)S(1)} %add_chunk2_step2.1), channel_id=1, source_target_pairs={{0,4},{1,5},{2,6},{3,7},{4,0},{5,1},{6,2},{7,3},{8,12},{9,13},{10,... | collective-permute-start | bytes 491528 | tf_op jit(solution)/shard_map/ppermute | solution.py:502
  45.8 4.9 %collective-permute-start.5 = (bf16[2,240,128]{2,1,0:T(8,128)(2,1)S(1)}, bf16[2,240,128]{2,1,0:T(8,128)(2,1)S(1)}, u32[]{:S(2)}, u32[]{:S(2)}) collective-permute-start(bf16[2,240,128]{2,1,0:T(8,128)(2,1)S(1)} %add_chunk0_step3.1), channel_id=1, source_target_pairs={{0,8},{1,9},{2,10},{3,11},{4,12},{5,13},{6,14},{7,15},{8,0},{9,1},... | collective-permute-start | bytes 368648 | tf_op jit(solution)/shard_map/ppermute | solution.py:502
  46.1 5.4 %collective-permute-start.10 = (bf16[2,192,128]{2,1,0:T(8,128)(2,1)S(1)}, bf16[2,192,128]{2,1,0:T(8,128)(2,1)S(1)}, u32[]{:S(2)}, u32[]{:S(2)}) collective-permute-start(bf16[2,192,128]{2,1,0:T(8,128)(2,1)S(1)} %add_chunk1_step3.1), channel_id=1, source_target_pairs={{0,4},{1,5},{2,6},{3,7},{4,0},{5,1},{6,2},{7,3},{8,12},{9,13},{10,... | collective-permute-start | bytes 294920 | tf_op jit(solution)/shard_map/ppermute | solution.py:502
  46.6 7.2 %collective-permute-start.15 = (bf16[2,160,128]{2,1,0:T(8,128)(2,1)S(1)}, bf16[2,160,128]{2,1,0:T(8,128)(2,1)S(1)}, u32[]{:S(2)}, u32[]{:S(2)}) collective-permute-start(bf16[2,160,128]{2,1,0:T(8,128)(2,1)S(1)} %add_chunk2_step3.1), channel_id=1, source_target_pairs={{0,2},{1,3},{2,0},{3,1},{4,6},{5,7},{6,4},{7,5},{8,10},{9,11},{10,... | collective-permute-start | bytes 245768 | tf_op jit(solution)/shard_map/ppermute | solution.py:502
  50.8 6.2 %collective-permute-start.6 = (bf16[240,128]{1,0:T(8,128)(2,1)S(1)}, bf16[240,128]{1,0:T(8,128)(2,1)S(1)}, u32[]{:S(2)}, u32[]{:S(2)}) collective-permute-start(bf16[240,128]{1,0:T(8,128)(2,1)S(1)} %add_chunk0_step4.1), channel_id=1, source_target_pairs={{0,16},{1,17},{2,18},{3,19},{4,20},{5,21},{6,22},{7,23},{8,24},{9,... | collective-permute-start | bytes 184328 | tf_op jit(solution)/shard_map/ppermute | solution.py:502
  51.6 5.4 %collective-permute-start.11 = (bf16[192,128]{1,0:T(8,128)(2,1)S(1)}, bf16[192,128]{1,0:T(8,128)(2,1)S(1)}, u32[]{:S(2)}, u32[]{:S(2)}) collective-permute-start(bf16[192,128]{1,0:T(8,128)(2,1)S(1)} %add_chunk1_step4.1), channel_id=1, source_target_pairs={{0,16},{1,17},{2,18},{3,19},{4,20},{5,21},{6,22},{7,23},{8,24},{9,... | collective-permute-start | bytes 147464 | tf_op jit(solution)/shard_map/ppermute | solution.py:502
  53.9 5.0 %collective-permute-start.16 = (bf16[160,128]{1,0:T(8,128)(2,1)S(1)}, bf16[160,128]{1,0:T(8,128)(2,1)S(1)}, u32[]{:S(2)}, u32[]{:S(2)}) collective-permute-start(bf16[160,128]{1,0:T(8,128)(2,1)S(1)} %add_chunk2_step4.1), channel_id=1, source_target_pairs={{0,16},{1,17},{2,18},{3,19},{4,20},{5,21},{6,22},{7,23},{8,24},{9,... | collective-permute-start | bytes 122888 | tf_op jit(solution)/shard_map/ppermute | solution.py:502

commit v6 on v5

--- a/solution.py
+++ b/solution.py
@@ -25,9 +25,13 @@
     return [pltpu.with_memory_space_constraint(x, space) for x in arrays]
 
 
-def around(x, axis, by):
+def shifted(x, axis, by):
     count = lax.axis_size(axis)
-    return lax.ppermute(x, axis, [(i, (i + by) % count) for i in range(count)])
+    return lax.ppermute(x, axis, [(i, i + by) for i in range(count) if 0 <= i + by < count])
+
+
+def is_last():
+    return lax.axis_index("tm") == lax.axis_size("tm") - 1
 
 
 def column(row, rows):
@@ -68,11 +72,7 @@
     x, gs, gk, weight, conv_w, out_w, _, x_here, grad_stream, grad_skip, sums, conv_here, out_here,
     gs_raw, gk_raw, weight_here, sems,
 ):
-    some = pl.ds(0, conv_here.shape[0])
-    pairs = (
-        (weight, weight_here), (gs, gs_raw), (gk, gk_raw), (x, x_here),
-        (conv_w.at[some], conv_here), (out_w.at[some], out_here),
-    )
+    pairs = ((weight, weight_here), (gs, gs_raw), (gk, gk_raw), (x, x_here), (conv_w, conv_here), (out_w, out_here))
     copies = [pltpu.make_async_copy(a, b, sems.at[i]) for i, (a, b) in enumerate(pairs)]
     for copy in copies:
         copy.start()
@@ -89,7 +89,7 @@
         copy.wait()
 
 
-def load_some(low, x, gs, gk, weight, conv_w, out_w, after):
+def load_all(x, gs, gk, weight, conv_w, out_w, after):
     shape = x.shape
     vmem, anywhere = pl.BlockSpec(memory_space=pltpu.VMEM), pl.BlockSpec(memory_space=pl.ANY)
     return pl.pallas_call(
@@ -101,8 +101,8 @@
             pltpu.VMEM(shape, jnp.float32),
             pltpu.VMEM(shape, jnp.bfloat16),
             pltpu.VMEM((16, LANES), jnp.bfloat16),
-            pltpu.VMEM((low,) + conv_w.shape[1:], jnp.bfloat16),
-            pltpu.VMEM((low,) + out_w.shape[1:], jnp.bfloat16),
+            pltpu.VMEM(conv_w.shape, jnp.bfloat16),
+            pltpu.VMEM(out_w.shape, jnp.bfloat16),
         ],
         scratch_shapes=[
             pltpu.VMEM(shape, jnp.bfloat16),
@@ -111,8 +111,8 @@
             pltpu.SemaphoreType.DMA((6,)),
         ],
         compiler_params=pltpu.CompilerParams(vmem_limit_bytes=ADD_BYTES),
-        cost_estimate=cost(10**7, 5 * 10**6),
-        name="load_some",
+        cost_estimate=cost(10**7, 6 * 10**6),
+        name="load_all",
     )(*held((x, gs, gk, weight, conv_w, out_w), pltpu.HBM), *held([after]))
 
 
@@ -127,11 +127,6 @@
 
 def joined_rows(rows):
     return jnp.sum(rows.astype(jnp.float32), axis=0, keepdims=True)
-
-
-def cut_off(rows, dilation):
-    row = lax.broadcasted_iota(jnp.int32, rows.shape, 0)
-    return jnp.where(jnp.logical_and(row < dilation, lax.axis_index("tm") == 0), 0.0, rows)
 
 
 def items_of(layers, chunk):
@@ -145,58 +140,63 @@
     return items + ([(high - third - 1, True)] if high > third else [])
 
 
-def backward(plan, layers, refs_of, weights_of, grad_proj, grad_stream, past_part, total, grad_parts):
+def backward(plan, layers, refs_of, conv_w, out_w, grad_stream, scratch, grad_parts):
+    grad_proj, grad_preact, past_part, conv_total, *out_totals = scratch
     halo, length, channels = plan["halo"], plan["length"], plan["channels"]
-    own = slice(halo, halo + length)
+    border = length + halo
     items = plan["items"]
-
-    def out_grad(index):
-        if (index, True) in items:
-            total[0:channels] = dot(refs_of(index)[2][own], grad_proj[0:length], TN)
-            plan["store"](total, channels, items.index((index, True)), grad_parts)
+    past_part[border:] = jnp.zeros((past_part.shape[0] - border, channels), jnp.float32)
+    grad_proj[:, :channels] = grad_stream[...].astype(jnp.bfloat16)
+
+    def add_rows(at, to, index):
+        rows = slice(halo + at, halo + to)
+        operands, _, gates = refs_of(index)
+        yield conv_total, (index, False), operands[rows], grad_preact[at:to]
+        if (index - 1, True) in items:
+            yield out_totals[0], (index - 1, True), refs_of(index - 1)[2][rows], grad_proj[at:to]
 
     for index in layers:
-        dilation, count = 2**index, plan["counts"][index]
-        operands, factors, _ = refs_of(index)
-        conv_layer, out_layer = weights_of(index)
-        grad_proj[0:count, :channels] = grad_stream[0:count].astype(jnp.bfloat16)
-        grad_gated = dot(grad_proj[0:count], out_layer[...], NT)
-        out_grad(index)
-        both = factors[halo : halo + count]
-        grad_preact = jnp.concatenate(
+        dilation = 2**index
+        _, factors, gates = refs_of(index)
+        grad_gated = dot(grad_proj[...], out_w[index], NT)
+        first = index == layers[0] and (index, True) in items
+        if first:
+            out_totals[1][...] = dot(gates[halo:border], grad_proj[0:length], TN)
+
+            @pl.when(is_last())
+            def _():
+                out_totals[1][...] += dot(gates[border:], grad_proj[length:], TN)
+
+            plan["store"](out_totals[1], items.index((index, True)), grad_parts)
+        both = factors[halo:]
+        grad_preact[...] = jnp.concatenate(
             [grad_gated * both[:, :channels], grad_gated * both[:, channels:]], axis=1
         ).astype(jnp.bfloat16)
-        spread = dot(grad_preact, conv_layer[...], NT)
-        past_part[0:count] = spread[:, channels:]
-        cut = slice(halo, halo + max(dilation, 8))
-        past_part[cut] = cut_off(past_part[cut], dilation)
-        rows = plan["counts"][index - 1] if index else length
-        grad_stream[0:rows] += spread[0:rows, :channels] + past_part[dilation : dilation + rows]
-        total[...] = dot(operands[own], grad_preact[0:length], TN)
-        plan["store"](total, 2 * channels, items.index((index, False)), grad_parts)
-    after = layers[-1] - 1
-    if (after, True) in items:
-        grad_proj[0:length, :channels] = grad_stream[0:length].astype(jnp.bfloat16)
-        out_grad(after)
+        spread = dot(grad_preact[...], conv_w[index], NT)
+        past_part[0:border] = spread[:, channels:]
+        grad_stream[...] += spread[:, :channels] + past_part[dilation : dilation + border]
+        if index:
+            grad_proj[:, :channels] = grad_stream[...].astype(jnp.bfloat16)
+        for total, _, left, right in add_rows(0, length, index):
+            total[...] = dot(left, right, TN)
+
+        @pl.when(is_last())
+        def _():
+            for total, _, left, right in add_rows(length, border, index):
+                total[...] += dot(left, right, TN)
+
+        for total, item, _, _ in add_rows(0, 0, index):
+            plan["store"](total, items.index(item), grad_parts)
 
 
 def first_kernel(
-    plan, prev_rows, own_x, own_grad, own_skip, sums, conv_low, out_low, conv_w, out_w,
+    plan, prev_rows, own_x, own_grad, own_skip, sums, conv_w, out_w,
     low_operands, low_factors, low_gates, grad_stream, grad_skip, *rest,
 ):
-    grad_parts = rest[:-10]
-    stream, operands, factors, gates, grad_proj, past_part, total, conv_high, out_high, sems = rest[-10:]
+    *grad_parts, stream, operands, factors, gates = rest[: 4 + 2]
+    scratch = rest[6:]
     halo, (length, channels) = plan["halo"], own_x.shape
     layers, low = conv_w.shape[0], low_gates.shape[0]
-    copies = {}
-    for index in range(low, layers):
-        at = 2 * (index - low)
-        copies[index] = (
-            pltpu.make_async_copy(conv_w.at[index], conv_high.at[index - low], sems.at[at]),
-            pltpu.make_async_copy(out_w.at[index], out_high.at[index - low], sems.at[at + 1]),
-        )
-        for copy in copies[index]:
-            copy.start()
     pad = 2 ** (layers - 1)
     extent = length + 2 * halo
     begin = 2 * halo
@@ -209,23 +209,12 @@
             return low_operands.at[index], low_factors.at[index], low_gates.at[index]
         return operands.at[index - low], factors.at[index - low], gates.at[index - low]
 
-    def weights_of(index):
-        if index < low:
-            return conv_low.at[index], out_low.at[index]
-        return conv_high.at[index - low], out_high.at[index - low]
-
     for index in range(layers):
         dilation, start = 2**index, plan["starts"][index]
         operand, factor, gate = refs_of(index)
-        conv_layer, out_layer = weights_of(index)
         operand[start:, :channels] = stream[pad + start :].astype(jnp.bfloat16)
         operand[start:, channels:] = stream[pad + start - dilation : pad + extent - dilation].astype(jnp.bfloat16)
-        slab = max(dilation, 16)
-        earlier = stream[pad + begin - dilation : pad + begin - dilation + slab]
-        operand[begin : begin + slab, channels:] = cut_off(earlier, dilation).astype(jnp.bfloat16)
-        for copy in copies.get(index, ()):
-            copy.wait()
-        preact = dot(operand[start:], conv_layer[...], NN)
+        preact = dot(operand[start:], conv_w[index], NN)
         filtered = jnp.tanh(preact[:, :channels])
         opening = 0.5 + 0.5 * jnp.tanh(0.5 * preact[:, channels:])
         product = filtered * opening
@@ -233,48 +222,40 @@
         factor[start:, :channels] = opening - filtered * product
         factor[start:, channels:] = product * (1.0 - opening)
         if index < layers - 1:
-            stream[pad + start :] += dot(gate[start:], out_layer[:, :channels], NN)
+            stream[pad + start :] += dot(gate[start:], out_w[index, :, :channels], NN)
 
     grad_stream[0:halo] = prev_rows[2 * halo : 3 * halo].astype(jnp.float32)
     grad_stream[halo:] = own_grad[...]
     grad_skip[0:halo] = prev_rows[3 * halo :]
     grad_skip[halo:] = own_skip[...]
-    grad_proj[:, channels:] = grad_skip[...]
-    backward(
-        plan, list(reversed(range(low, layers))), refs_of, weights_of,
-        grad_proj, grad_stream, past_part, total, grad_parts,
-    )
+    scratch[0][:, channels:] = grad_skip[...]
+    backward(plan, list(reversed(range(low, layers))), refs_of, conv_w, out_w, grad_stream, scratch, grad_parts)
     plan["finish"](sums, grad_parts)
 
 
 def later_kernel(
     plan, first, third, low_operands, low_factors, low_gates, grad_before, grad_skip, conv_w, out_w, *rest
 ):
-    *outs, keep, send, grad_stream, grad_proj, past_part, total = rest[plan["unused"] :]
-    channels = plan["channels"]
+    outs = rest[plan["unused"] : plan["unused"] + plan["outs"]]
+    keep, send, grad_stream, *scratch = rest[plan["unused"] + plan["outs"] :]
     grad_stream[...] = grad_before[...]
-    grad_proj[:, channels:] = grad_skip[...]
+    scratch[0][:, plan["channels"] :] = grad_skip[...]
 
     def refs_of(index):
         return low_operands.at[index], low_factors.at[index], low_gates.at[index]
 
-    def weights_of(index):
-        return conv_w.at[index], out_w.at[index]
-
-    backward(
-        plan, list(reversed(range(first, first + third))), refs_of, weights_of,
-        grad_proj, grad_stream, past_part, total, (keep, send),
-    )
+    layers = list(reversed(range(first, first + third)))
+    backward(plan, layers, refs_of, conv_w, out_w, grad_stream, scratch, (keep, send))
     at = 0
     for out in outs:
         out[...] = grad_stream[at : at + out.shape[0]]
         at += out.shape[0]
 
 
-def store_whole(items, total, height, item, grad_parts):
+def store_whole(items, total, item, grad_parts):
     is_out = items[item][1]
     place = sum(kind == is_out for _, kind in items[:item])
-    grad_parts[int(is_out)][place] = total[0:height].astype(jnp.bfloat16)
+    grad_parts[int(is_out)][place] = total[...].astype(jnp.bfloat16)
 
 
 def finish_whole(sums, grad_parts):
@@ -290,16 +271,16 @@
             )
 
 
-def store_shards(tm, dp, order, bases, total, height, item, grad_parts):
+def store_shards(tm, dp, order, bases, total, item, grad_parts):
     keep, send = grad_parts
     t_at, d_at = lax.axis_index("tm"), lax.axis_index("dp")
     core_at = lax.rem(d_at, 2)
-    rows = height // tm
+    rows = total.shape[0] // tm
     at = pl.ds(bases[item], rows)
     at_bits = bits_of(t_at, d_at, lax.rem, lax.div)
     for y in range(dp // 2):
-        near = total[0:height, (2 * y) * LANES : (2 * y + 1) * LANES]
-        far = total[0:height, (2 * y + 1) * LANES : (2 * y + 2) * LANES]
+        near = total[:, (2 * y) * LANES : (2 * y + 1) * LANES]
+        far = total[:, (2 * y + 1) * LANES : (2 * y + 2) * LANES]
         mine = jnp.where(core_at == 0, near, far).astype(jnp.bfloat16)
         other = jnp.where(core_at == 0, far, near).astype(jnp.bfloat16)
         for t in range(tm):
@@ -320,18 +301,18 @@
     return ends[:-1], ends[-1]
 
 
-def run_layers(in_shards, tm, dp, halo, prev_rows, loaded, conv_w, out_w):
-    own_x, own_grad, own_skip, sums, conv_low, out_low = loaded
+def run_layers(in_shards, tm, dp, halo, prev_rows, loaded):
+    own_x, own_grad, own_skip, sums, conv_w, out_w = loaded
     length, channels = own_x.shape
-    layers, low = conv_w.shape[0], conv_low.shape[0]
-    third = layers - low
+    layers = conv_w.shape[0]
+    third = layers // len(CHAINS)
+    low = layers - third
     extent, border = length + 2 * halo, length + halo
     starts = []
     for index in range(layers):
         need = halo if index == layers - 1 else 2 ** (index + 1)
         starts.append(need // 16 * 16)
-    counts = [-(-(length + 2 ** (index + 1) - 1) // 16) * 16 for index in range(layers)]
-    plan = {"halo": halo, "starts": starts, "counts": counts, "length": length, "channels": channels, "unused": 0}
+    plan = {"halo": halo, "starts": starts, "length": length, "channels": channels}
     plans, shapes = [], []
     for chunk, order in enumerate(CHAINS):
         items = items_of(layers, chunk)
@@ -348,9 +329,17 @@
     vmem, anywhere = pl.BlockSpec(memory_space=pltpu.VMEM), pl.BlockSpec(memory_space=pl.ANY)
     weight_bytes = 2 * (conv_w.size + out_w.size)
     flops = 2 * length * channels * channels
+    scratch = [
+        pltpu.VMEM((border, 2 * channels), jnp.bfloat16),
+        pltpu.VMEM((border, 2 * channels), jnp.bfloat16),
+        pltpu.VMEM((border + 2 ** (layers - 1), channels), jnp.float32),
+        pltpu.VMEM((2 * channels, 2 * channels), jnp.float32),
+        pltpu.VMEM((channels, 2 * channels), jnp.float32),
+        pltpu.VMEM((channels, 2 * channels), jnp.float32),
+    ]
     *kept, grad_stream, grad_skip, keep, send = pl.pallas_call(
         functools.partial(first_kernel, plans[0]),
-        in_specs=[vmem] * 7 + [anywhere] * 2,
+        in_specs=[vmem] * 7,
         out_specs=[vmem] * 7,
         out_shape=[
             pltpu.VMEM((low, extent, 2 * channels), jnp.bfloat16),
@@ -365,46 +354,37 @@
             pltpu.VMEM((third, extent, 2 * channels), jnp.bfloat16),
             pltpu.VMEM((third, extent, 2 * channels), jnp.float32),
             pltpu.VMEM((third, extent, channels), jnp.bfloat16),
-            pltpu.VMEM((border, 2 * channels), jnp.bfloat16),
-            pltpu.VMEM((border, channels), jnp.float32),
-            pltpu.VMEM((2 * channels, 2 * channels), jnp.float32),
-            pltpu.VMEM((third,) + conv_w.shape[1:], jnp.bfloat16),
-            pltpu.VMEM((third,) + out_w.shape[1:], jnp.bfloat16),
-            pltpu.SemaphoreType.DMA((2 * third,)),
-        ],
+        ]
+        + scratch,
         compiler_params=pltpu.CompilerParams(vmem_limit_bytes=VMEM_BYTES),
         cost_estimate=cost(flops * (5 * layers + 12 * third), weight_bytes),
         name="forward_and_last_third",
-    )(*held((prev_rows, own_x, own_grad, own_skip, sums, conv_low, out_low)), *held((conv_w, out_w), pltpu.HBM))
+    )(*held((prev_rows, *loaded)))
 
     def later(step, outs, after):
+        more = {"unused": len(after), "outs": len(outs)}
         return pl.pallas_call(
-            functools.partial(later_kernel, plans[step] | {"unused": len(after)}, layers - (step + 1) * third, third),
+            functools.partial(later_kernel, plans[step] | more, layers - (step + 1) * third, third),
             in_specs=[vmem] * 7 + [anywhere] * len(after),
             out_specs=[vmem] * (len(outs) + 2),
             out_shape=[pltpu.VMEM((rows, channels), jnp.float32) for rows in outs]
             + [pltpu.VMEM(shape, jnp.bfloat16) for shape in shapes[step]],
-            scratch_shapes=[
-                pltpu.VMEM((border, channels), jnp.float32),
-                pltpu.VMEM((border, 2 * channels), jnp.bfloat16),
-                pltpu.VMEM((border, channels), jnp.float32),
-                pltpu.VMEM((2 * channels, 2 * channels), jnp.float32),
-            ],
+            scratch_shapes=[pltpu.VMEM((border, channels), jnp.float32)] + scratch,
             compiler_params=pltpu.CompilerParams(vmem_limit_bytes=VMEM_BYTES),
             cost_estimate=cost(flops * 12 * third, weight_bytes),
             name="middle_third" if step == 1 else "first_third",
-        )(*held((*kept, grad_stream, grad_skip, conv_low, out_low, *after)))
+        )(*held((*kept, grad_stream, grad_skip, conv_w, out_w, *after)))
 
     parts = [(keep, send)]
     if in_shards:
         parts[0] = Chunk(tm, dp, 0, keep, send)
     grad_stream, *middle = later(1, [border], [])
-    other, own, *last = later(2, [halo, length - halo], [parts[0].next_message()] if in_shards else [])
+    other, own, tail, *last = later(2, [halo, length - halo, halo], [parts[0].next_message()] if in_shards else [])
     parts += [middle, last]
     if in_shards:
         for step in (1, 2):
             parts[step] = Chunk(tm, dp, step, *parts[step])
-    return other, own, parts
+    return other, own, tail, parts
 
 
 def add_kernel(count, groups, *refs):
@@ -451,7 +431,7 @@
     for count in counts:
         chunks.append(refs[:count])
         refs = refs[count:]
-    other, own, grad_inputs, grad_conv, grad_out = refs
+    other, own, tail, grad_inputs, grad_conv, grad_out = refs
     layers, channels = grad_conv.shape[0], own.shape[1]
     total = 0.0
     for term in chunks[0]:
@@ -468,7 +448,7 @@
     for first in range(0, channels, LANES):
         lanes = slice(first, first + LANES)
         grad_inputs[0 : own.shape[0], lanes] = own[:, lanes] * scale
-        grad_inputs[own.shape[0] :, lanes] = other[:, lanes] * scale
+        grad_inputs[own.shape[0] :, lanes] = jnp.where(is_last(), tail[:, lanes], other[:, lanes]) * scale
 
 
 class Chunk:
@@ -516,11 +496,11 @@
     samples_all = batch * length * tm * dp
     x, gs, gk = inputs[0], grad_stream_out[0], grad_skip_out[0]
     message = pack(halo, x, gs, gk, sample_weight)
-    prev_rows = around(message, "tm", 1)
-    loaded = load_some(layers - third, x, gs, gk, sample_weight, conv_weight, out_weight, message)
+    prev_rows = shifted(message, "tm", 1)
+    loaded = load_all(x, gs, gk, sample_weight, conv_weight, out_weight, message)
     in_shards = tm == 8 and dp == 4 and channels // tm % 16 == 0 and 2 * channels == dp * LANES
-    other, own, parts = run_layers(in_shards, tm, dp, halo, prev_rows, loaded, conv_weight, out_weight)
-    other = around(other, "tm", -1)
+    other, own, tail, parts = run_layers(in_shards, tm, dp, halo, prev_rows, loaded)
+    other = shifted(other, "tm", -1)
     if not in_shards:
         scale = samples_all / lax.psum(jnp.sum(sample_weight), ("tm", "dp"))
         found = {}
@@ -532,7 +512,8 @@
         grad_conv, grad_out = (
             scattered(jnp.stack([found[index, is_out] for index in range(layers)])) * scale for is_out in (False, True)
         )
-        return (jnp.concatenate([own, other]) * scale)[None], grad_conv, grad_out
+        ends = jnp.where(is_last(), tail, other)
+        return (jnp.concatenate([own, ends]) * scale)[None], grad_conv, grad_out
     chunks = [part.run_chain([other] if part is parts[0] else ()) for part in parts]
     conv_rows, out_rows = 2 * channels // tm, channels // tm
     grad_inputs, grad_conv, grad_out = pl.pallas_call(
@@ -544,7 +525,7 @@
         ],
         compiler_params=pltpu.CompilerParams(vmem_limit_bytes=ADD_BYTES),
         name="scale_all",
-    )(*held([term for terms in chunks for term in terms]), *held([other, own]))
+    )(*held([term for terms in chunks for term in terms]), *held([other, own, tail]))
     return grad_inputs[None], grad_conv, grad_out
 
 

time: 60 us -> 64 us (1.067)
  starting transfers between devices: 16.5 us -> 29.6 us
  waiting for transfers between devices: 26.6 us -> 16 us
  Pallas kernels: 15.9 us -> 17.5 us
    ppermute x15, starting transfers between devices: 10.3 us -> 23.4 us  [swapped(): return lax.ppermute(value, ('tm', 'dp'), pairs)]
    ppermute x15, waiting for transfers between devices: 12.7 us -> 7.41 us  [swapped(): return lax.ppermute(value, ('tm', 'dp'), pairs)]
    ppermute x2, waiting for transfers between devices: 13.9 us -> 8.57 us  [shifted(): lax.ppermute(x, axis, [(i, i + by) for i in range(count) if 0 <= i + by <...]
    pallas_call x3, Pallas kernels: 6.32 us -> 8.18 us  [the longest x2 5.5 us: later(): pl.pallas_call(functools.partial(later_kernel, plans[step] | more, layers...]
  transfers between devices with their start and end apart: 17 -> 17, of which waited for: 8 -> 5; matrix products, arithmetic and copies ran while one was open for 0% -> 0% of each run, Pallas kernels for 12% -> 14%
where the time goes in v6:
time: 64 us; the launch traced here: 63.8 us
  starting transfers between devices  29.6 us (46%)
  Pallas kernels  17.5 us (27%)
  waiting for transfers between devices  16 us (25%)
  between operations  0.74 us (1%)
    ppermute x15, starting transfers between devices, swapped(): return lax.ppermute(value, ('tm', 'dp'), pairs)  23.4 us
    ppermute x2, waiting for transfers between devices, shifted(): lax.ppermute(x, axis, [(i, i + by) for i in range(count) if 0 <= i + by <...  8.57 us
    ppermute x15, waiting for transfers between devices, swapped(): return lax.ppermute(value, ('tm', 'dp'), pairs)  7.41 us
    pallas_call x1, Pallas kernels, run_layers(): pl.pallas_call(functools.partial(first_kernel, plans[0]), in_specs=[vmem]...  6.5 us
    ppermute x2, starting transfers between devices, shifted(): lax.ppermute(x, axis, [(i, i + by) for i in range(count) if 0 <= i + by <...  6.13 us
    pallas_call x2, Pallas kernels, later(): pl.pallas_call(functools.partial(later_kernel, plans[step] | more, layers...  5.5 us
    pallas_call x1, Pallas kernels, load_all(): pl.pallas_call(load_kernel, in_specs=[anywhere] * 7, out_specs=[vmem] * 6...  2.68 us
  transfers between devices with their start and end apart: 17, of which 5 were waited for; matrix products, arithmetic and copies ran while one was open for 0% of the time, Pallas kernels for 14%

profile of v6, /device:TPU:0, one launch (start us, length us, event | category | flops | bytes accessed | tf_op | source)
XLA Modules:
  0.0 63.8 jit_solution(17323979867979492030)
XLA Ops:
  0.6 1.0 %pack_borders.1._ = bf16[256,256]{1,0:T(8,128)(2,1)S(1)} custom-call(bf16[512,256]{1,0:T(8,128)(2,1)} %bitcast.4, bf16[512,256]{1,0:T(8,128)(2,1)} %bitcast.6, bf16[512,256]{1,0:T(8,128)(2,1)} %bitcast.8, f32[1,512]{1,0:T(1,128)} %weight.3), custom_call_target="tpu_custom_call" | custom-call | tf_op jit(solution)/shard_map/pack_borders/pallas_call | solution.py:60
  1.6 4.8 %collective-permute-start = (bf16[256,256]{1,0:T(8,128)(2,1)S(1)}, bf16[256,256]{1,0:T(8,128)(2,1)S(1)}, u32[]{:S(2)}, u32[]{:S(2)}) collective-permute-start(bf16[256,256]{1,0:T(8,128)(2,1)S(1)} %pack_borders.1._), channel_id=1, source_target_pairs={{0,4},{4,8},{8,12},{12,16},{16,20},{20,24},{24,28},{1,5},{5,9},{9,... | collective-permute-start | bytes 393224 | tf_op jit(solution)/shard_map/ppermute | solution.py:30
  6.5 2.7 %load_all.1 = (bf16[512,256]{1,0:T(8,128)(2,1)S(1)}, f32[512,256]{1,0:T(8,128)S(1)}, bf16[512,256]{1,0:T(8,128)(2,1)S(1)}, bf16[16,128]{1,0:T(8,128)(2,1)S(1)}, ...) custom-call(bf16[512,256]{1,0:T(8,128)(2,1)} %bitcast.5, bf16[512,256]{1,0:T(8,128)(2,1)} %bitcast.7, ...), custom_call_target="tpu_custom_call" | custom-call | flops 10000000 | bytes 6000000 | tf_op jit(solution)/shard_map/load_all/pallas_call | solution.py:95
  9.2 0.0 collective-permute-done.prev_rows
  9.2 6.5 %forward_and_last_third.1 = (bf16[4,640,512]{2,1,0:T(8,128)(2,1)S(1)}, f32[4,640,512]{2,1,0:T(8,128)S(1)}, bf16[4,640,256]{2,1,0:T(8,128)(2,1)S(1)}, f32[576,256...) custom-call(bf16[256,256]{1,0:T(8,128)(2,1)S(1)} %collective-permute, ...), custom_call_target="tpu_custom_call" | custom-call | flops 3623878656 | bytes 4718592 | tf_op jit(solution)/shard_map/forward_and_last_third/pallas_call | solution.py:340
  15.7 0.1 collective-permute-start.1
  15.8 2.8 %middle_third.1 = (f32[576,256]{1,0:T(8,128)S(1)}, bf16[2,2,2,2,192,128]{5,4,3,2,1,0:T(8,128)(2,1)S(1)}, bf16[2,2,2,2,192,128]{5,4,3,2,1,0:T(8,128)(2,1)S(1)}) custom-call(bf16[4,640,512]{2,1,0:T(8,128)(2,1)S(1)} %get-tuple-element.35.low_operands, f32[4,640,512]{2,1,0:T(8,128)S(1)} %get-tuple-element.36.low_factors, ...), custom_call_target="tpu_custom_call" | custom-call | flops 1610612736 | bytes 4718592 | tf_op jit(solution)/shard_map/middle_third/pallas_call | solution.py:366
  18.6 0.6 collective-permute-start.7
  19.2 0.0 collective-permute-done.1.refs_1_
  19.2 0.1 add_chunk0_step1.1.rest_0_
  19.3 2.7 %first_third.1 = (f32[64,256]{1,0:T(8,128)S(1)}, f32[448,256]{1,0:T(8,128)S(1)}, f32[64,256]{1,0:T(8,128)S(1)}, bf16[2,2,2,2,160,128]{5,4,3,2,1,0:T(8,128)(2,1)S(1)}, bf16[2,2,2,2,160,128]{5,4,3,2,1,0:T(8,128)(2,1)S(1)}) custom-call(bf16[4,640,512]{2,1,0:T(8,128)(2,1)S(1)} %get-tuple-element.35.low_operands, ...), custom_call_target="tpu_custom_call" | custom-call | flops 1610612736 | bytes 4718592 | tf_op jit(solution)/shard_map/first_third/pallas_call | solution.py:366
  22.0 0.1 collective-permute-start.12
  22.1 2.5 %collective-permute-start.2 = (bf16[2,2,2,240,128]{4,3,2,1,0:T(8,128)(2,1)S(1)}, bf16[2,2,2,240,128]{4,3,2,1,0:T(8,128)(2,1)S(1)}, u32[]{:S(2)}, u32[]{:S(2)}) collective-permute-start(bf16[2,2,2,240,128]{4,3,2,1,0:T(8,128)(2,1)S(1)} %add_chunk0_step1.1.rest_0_), channel_id=1, source_target_pairs={{0,4},{1,5},{2,6},{3,7},{4,0},{5,1},{6,2},{7,3},{8,12},{9,13},{10,... | collective-permute-start | bytes 1474568 | tf_op jit(solution)/shard_map/ppermute | solution.py:482
  24.6 0.0 collective-permute-done.7.refs_1_.refs_7_
  24.6 0.1 add_chunk1_step1.1
  24.7 1.6 %collective-permute-start.8 = (bf16[2,2,2,192,128]{4,3,2,1,0:T(8,128)(2,1)S(1)}, bf16[2,2,2,192,128]{4,3,2,1,0:T(8,128)(2,1)S(1)}, u32[]{:S(2)}, u32[]{:S(2)}) collective-permute-start(bf16[2,2,2,192,128]{4,3,2,1,0:T(8,128)(2,1)S(1)} %add_chunk1_step1.1), channel_id=1, source_target_pairs={{0,2},{1,3},{2,0},{3,1},{4,6},{5,7},{6,4},{7,5},{8,10},{9,11},{10,... | collective-permute-start | bytes 1179656 | tf_op jit(solution)/shard_map/ppermute | solution.py:482
  26.3 0.0 collective-permute-done.12.refs_1_.refs_13_
  26.3 0.1 add_chunk2_step1.1
  26.4 1.6 %collective-permute-start.13 = (bf16[2,2,2,160,128]{4,3,2,1,0:T(8,128)(2,1)S(1)}, bf16[2,2,2,160,128]{4,3,2,1,0:T(8,128)(2,1)S(1)}, u32[]{:S(2)}, u32[]{:S(2)}) collective-permute-start(bf16[2,2,2,160,128]{4,3,2,1,0:T(8,128)(2,1)S(1)} %add_chunk2_step1.1), channel_id=1, source_target_pairs={{0,8},{1,9},{2,10},{3,11},{4,12},{5,13},{6,14},{7,15},{8,0},{9,1},... | collective-permute-start | bytes 983048 | tf_op jit(solution)/shard_map/ppermute | solution.py:482
  28.0 1.3 %collective-permute-start.3 = (f32[64,256]{1,0:T(8,128)S(1)}, f32[64,256]{1,0:T(8,128)S(1)}, u32[]{:S(2)}, u32[]{:S(2)}) collective-permute-start(f32[64,256]{1,0:T(8,128)S(1)} %get-tuple-element.41), channel_id=1, source_target_pairs={{4,0},{8,4},{12,8},{16,12},{20,16},{24,20},{28,24},{5,1},{9,5},{13... | collective-permute-start | bytes 196616 | tf_op jit(solution)/shard_map/ppermute | solution.py:30
  29.3 8.5 %collective-permute-done.3.refs_3_.refs_18_ = f32[64,256]{1,0:T(8,128)S(1)} collective-permute-done((f32[64,256]{1,0:T(8,128)S(1)}, f32[64,256]{1,0:T(8,128)S(1)}, u32[]{:S(2)}, u32[]{:S(2)}) %collective-permute-start.3) | collective-permute-done | bytes 65568 | tf_op jit(solution)/shard_map/ppermute | solution.py:30
  37.8 0.0 collective-permute-done.2.refs_2_
  37.8 0.1 add_chunk0_step2.1
  37.9 1.6 %collective-permute-start.4 = (bf16[2,2,240,128]{3,2,1,0:T(8,128)(2,1)S(1)}, bf16[2,2,240,128]{3,2,1,0:T(8,128)(2,1)S(1)}, u32[]{:S(2)}, u32[]{:S(2)}) collective-permute-start(bf16[2,2,240,128]{3,2,1,0:T(8,128)(2,1)S(1)} %add_chunk0_step2.1), channel_id=1, source_target_pairs={{0,2},{1,3},{2,0},{3,1},{4,6},{5,7},{6,4},{7,5},{8,10},{9,11},{10,... | collective-permute-start | bytes 737288 | tf_op jit(solution)/shard_map/ppermute | solution.py:482
  39.5 0.0 collective-permute-done.8.refs_2_.refs_8_
  39.5 0.1 add_chunk1_step2.1
  39.6 2.8 %collective-permute-start.9 = (bf16[2,2,192,128]{3,2,1,0:T(8,128)(2,1)S(1)}, bf16[2,2,192,128]{3,2,1,0:T(8,128)(2,1)S(1)}, u32[]{:S(2)}, u32[]{:S(2)}) collective-permute-start(bf16[2,2,192,128]{3,2,1,0:T(8,128)(2,1)S(1)} %add_chunk1_step2.1), channel_id=1, source_target_pairs={{0,8},{1,9},{2,10},{3,11},{4,12},{5,13},{6,14},{7,15},{8,0},{9,1},... | collective-permute-start | bytes 589832 | tf_op jit(solution)/shard_map/ppermute | solution.py:482
  42.4 0.0 collective-permute-done.13.refs_2_.refs_14_
  42.4 0.1 add_chunk2_step2.1
  42.5 0.7 %collective-permute-start.14 = (bf16[2,2,160,128]{3,2,1,0:T(8,128)(2,1)S(1)}, bf16[2,2,160,128]{3,2,1,0:T(8,128)(2,1)S(1)}, u32[]{:S(2)}, u32[]{:S(2)}) collective-permute-start(bf16[2,2,160,128]{3,2,1,0:T(8,128)(2,1)S(1)} %add_chunk2_step2.1), channel_id=1, source_target_pairs={{0,4},{1,5},{2,6},{3,7},{4,0},{5,1},{6,2},{7,3},{8,12},{9,13},{10,... | collective-permute-start | bytes 491528 | tf_op jit(solution)/shard_map/ppermute | solution.py:482
  43.1 2.6 %collective-permute-done.4.refs_3_ = bf16[2,2,240,128]{3,2,1,0:T(8,128)(2,1)S(1)} collective-permute-done((bf16[2,2,240,128]{3,2,1,0:T(8,128)(2,1)S(1)}, bf16[2,2,240,128]{3,2,1,0:T(8,128)(2,1)S(1)}, u32[]{:S(2)}, u32[]{:S(2)}) %collective-permute-start.4) | collective-permute-done | bytes 245792 | tf_op jit(solution)/shard_map/ppermute | solution.py:482
  45.7 0.1 add_chunk0_step3.1
  45.8 2.6 %collective-permute-start.5 = (bf16[2,240,128]{2,1,0:T(8,128)(2,1)S(1)}, bf16[2,240,128]{2,1,0:T(8,128)(2,1)S(1)}, u32[]{:S(2)}, u32[]{:S(2)}) collective-permute-start(bf16[2,240,128]{2,1,0:T(8,128)(2,1)S(1)} %add_chunk0_step3.1), channel_id=1, source_target_pairs={{0,8},{1,9},{2,10},{3,11},{4,12},{5,13},{6,14},{7,15},{8,0},{9,1},... | collective-permute-start | bytes 368648 | tf_op jit(solution)/shard_map/ppermute | solution.py:482
  48.4 0.0 collective-permute-done.9.refs_3_.refs_9_
  48.4 0.1 add_chunk1_step3.1
  48.5 0.7 %collective-permute-start.10 = (bf16[2,192,128]{2,1,0:T(8,128)(2,1)S(1)}, bf16[2,192,128]{2,1,0:T(8,128)(2,1)S(1)}, u32[]{:S(2)}, u32[]{:S(2)}) collective-permute-start(bf16[2,192,128]{2,1,0:T(8,128)(2,1)S(1)} %add_chunk1_step3.1), channel_id=1, source_target_pairs={{0,4},{1,5},{2,6},{3,7},{4,0},{5,1},{6,2},{7,3},{8,12},{9,13},{10,... | collective-permute-start | bytes 294920 | tf_op jit(solution)/shard_map/ppermute | solution.py:482
  49.1 0.0 collective-permute-done.14.refs_3_.refs_15_
  49.2 1.6 %collective-permute-start.15 = (bf16[2,160,128]{2,1,0:T(8,128)(2,1)S(1)}, bf16[2,160,128]{2,1,0:T(8,128)(2,1)S(1)}, u32[]{:S(2)}, u32[]{:S(2)}) collective-permute-start(bf16[2,160,128]{2,1,0:T(8,128)(2,1)S(1)} %add_chunk2_step3.1), channel_id=1, source_target_pairs={{0,2},{1,3},{2,0},{3,1},{4,6},{5,7},{6,4},{7,5},{8,10},{9,11},{10,... | collective-permute-start | bytes 245768 | tf_op jit(solution)/shard_map/ppermute | solution.py:482
  50.8 0.5 collective-permute-done.5.refs_4_
  51.3 0.1 add_chunk0_step4.1
  51.3 4.0 %collective-permute-start.6 = (bf16[240,128]{1,0:T(8,128)(2,1)S(1)}, bf16[240,128]{1,0:T(8,128)(2,1)S(1)}, u32[]{:S(2)}, u32[]{:S(2)}) collective-permute-start(bf16[240,128]{1,0:T(8,128)(2,1)S(1)} %add_chunk0_step4.1), channel_id=1, source_target_pairs={{0,16},{1,17},{2,18},{3,19},{4,20},{5,21},{6,22},{7,23},{8,24},{9,... | collective-permute-start | bytes 184328 | tf_op jit(solution)/shard_map/ppermute | solution.py:482
  55.3 0.0 collective-permute-done.10.refs_4_.refs_10_
  55.4 1.8 %collective-permute-start.11 = (bf16[192,128]{1,0:T(8,128)(2,1)S(1)}, bf16[192,128]{1,0:T(8,128)(2,1)S(1)}, u32[]{:S(2)}, u32[]{:S(2)}) collective-permute-start(bf16[192,128]{1,0:T(8,128)(2,1)S(1)} %add_chunk1_step4.1), channel_id=1, source_target_pairs={{0,16},{1,17},{2,18},{3,19},{4,20},{5,21},{6,22},{7,23},{8,24},{9,... | collective-permute-start | bytes 147464 | tf_op jit(solution)/shard_map/ppermute | solution.py:482
  57.2 0.0 collective-permute-done.15.refs_4_.refs_16_
  57.2 1.2 %collective-permute-start.16 = (bf16[160,128]{1,0:T(8,128)(2,1)S(1)}, bf16[160,128]{1,0:T(8,128)(2,1)S(1)}, u32[]{:S(2)}, u32[]{:S(2)}) collective-permute-start(bf16[160,128]{1,0:T(8,128)(2,1)S(1)} %add_chunk2_step4.1), channel_id=1, source_target_pairs={{0,16},{1,17},{2,18},{3,19},{4,20},{5,21},{6,22},{7,23},{8,24},{9,... | collective-permute-start | bytes 122888 | tf_op jit(solution)/shard_map/ppermute | solution.py:482
  58.5 2.1 %collective-permute-done.11.refs_11_ = bf16[192,128]{1,0:T(8,128)(2,1)S(1)} collective-permute-done((bf16[192,128]{1,0:T(8,128)(2,1)S(1)}, bf16[192,128]{1,0:T(8,128)(2,1)S(1)}, u32[]{:S(2)}, u32[]{:S(2)}) %collective-permute-start.11) | collective-permute-done | bytes 49184 | tf_op jit(solution)/shard_map/ppermute | solution.py:482
  60.5 0.0 collective-permute-done.6.refs_5_
  60.5 2.2 %collective-permute-done.16.refs_17_ = bf16[160,128]{1,0:T(8,128)(2,1)S(1)} collective-permute-done((bf16[160,128]{1,0:T(8,128)(2,1)S(1)}, bf16[160,128]{1,0:T(8,128)(2,1)S(1)}, u32[]{:S(2)}, u32[]{:S(2)}) %collective-permute-start.16) | collective-permute-done | bytes 40992 | tf_op jit(solution)/shard_map/ppermute | solution.py:482
  62.8 1.0 %scale_all.1 = (f32[512,256]{1,0:T(8,128)}, f32[6,64,128]{2,1,0:T(8,128)}, f32[6,32,128]{2,1,0:T(8,128)}) custom-call(bf16[2,2,2,2,240,128]{5,4,3,2,1,0:T(8,128)(2,1)S(1)} %get-tuple-element.33.refs_0_, bf16[2,2,2,2,240,128]{5,4,3,2,1,0:T(8,128)(2,1)S(1)} %collective-permute-done.1.refs_1_, bf16[2,2,2,240,128]{4,3,2,1,0:T(8,128)(2,1)S(1)} %collective-permute-done.2.refs_2_, ...), custom_call_target="tpu_custom_call" | custom-call | tf_op jit(solution)/shard_map/scale_all/pallas_call | solution.py:519
  (3 shorter events, 0.1 us)
Async XLA Ops:
  1.6 7.6 %collective-permute-start = (bf16[256,256]{1,0:T(8,128)(2,1)S(1)}, bf16[256,256]{1,0:T(8,128)(2,1)S(1)}, u32[]{:S(2)}, u32[]{:S(2)}) collective-permute-start(bf16[256,256]{1,0:T(8,128)(2,1)S(1)} %pack_borders.1._), channel_id=1, source_target_pairs={{0,4},{4,8},{8,12},{12,16},{16,20},{20,24},{24,28},{1,5},{5,9},{9,... | collective-permute-start | bytes 393224 | tf_op jit(solution)/shard_map/ppermute | solution.py:30
  15.7 3.5 %collective-permute-start.1 = (bf16[2,2,2,2,240,128]{5,4,3,2,1,0:T(8,128)(2,1)S(1)}, bf16[2,2,2,2,240,128]{5,4,3,2,1,0:T(8,128)(2,1)S(1)}, u32[]{:S(2)}, u32[]{:S(2)}) collective-permute-start(bf16[2,2,2,2,240,128]{5,4,3,2,1,0:T(8,128)(2,1)S(1)} %get-tuple-element.34), channel_id=1, source_target_pairs={{0,1},{1,0},{2,3},{3,2},{4,5},{5,4},{6,7},{7,6},{8,9},{9,8},{10,11... | collective-permute-start | bytes 2949128 | tf_op jit(solution)/shard_map/ppermute | solution.py:482
  18.6 6.0 %collective-permute-start.7 = (bf16[2,2,2,2,192,128]{5,4,3,2,1,0:T(8,128)(2,1)S(1)}, bf16[2,2,2,2,192,128]{5,4,3,2,1,0:T(8,128)(2,1)S(1)}, u32[]{:S(2)}, u32[]{:S(2)}) collective-permute-start(bf16[2,2,2,2,192,128]{5,4,3,2,1,0:T(8,128)(2,1)S(1)} %get-tuple-element.43), channel_id=1, source_target_pairs={{0,1},{1,0},{2,3},{3,2},{4,5},{5,4},{6,7},{7,6},{8,9},{9,8},{10,11... | collective-permute-start | bytes 2359304 | tf_op jit(solution)/shard_map/ppermute | solution.py:482
  22.0 4.3 %collective-permute-start.12 = (bf16[2,2,2,2,160,128]{5,4,3,2,1,0:T(8,128)(2,1)S(1)}, bf16[2,2,2,2,160,128]{5,4,3,2,1,0:T(8,128)(2,1)S(1)}, u32[]{:S(2)}, u32[]{:S(2)}) collective-permute-start(bf16[2,2,2,2,160,128]{5,4,3,2,1,0:T(8,128)(2,1)S(1)} %get-tuple-element.45), channel_id=1, source_target_pairs={{0,1},{1,0},{2,3},{3,2},{4,5},{5,4},{6,7},{7,6},{8,9},{9,8},{10,11... | collective-permute-start | bytes 1966088 | tf_op jit(solution)/shard_map/ppermute | solution.py:482
  22.1 15.8 %collective-permute-start.2 = (bf16[2,2,2,240,128]{4,3,2,1,0:T(8,128)(2,1)S(1)}, bf16[2,2,2,240,128]{4,3,2,1,0:T(8,128)(2,1)S(1)}, u32[]{:S(2)}, u32[]{:S(2)}) collective-permute-start(bf16[2,2,2,240,128]{4,3,2,1,0:T(8,128)(2,1)S(1)} %add_chunk0_step1.1.rest_0_), channel_id=1, source_target_pairs={{0,4},{1,5},{2,6},{3,7},{4,0},{5,1},{6,2},{7,3},{8,12},{9,13},{10,... | collective-permute-start | bytes 1474568 | tf_op jit(solution)/shard_map/ppermute | solution.py:482
  24.7 14.8 %collective-permute-start.8 = (bf16[2,2,2,192,128]{4,3,2,1,0:T(8,128)(2,1)S(1)}, bf16[2,2,2,192,128]{4,3,2,1,0:T(8,128)(2,1)S(1)}, u32[]{:S(2)}, u32[]{:S(2)}) collective-permute-start(bf16[2,2,2,192,128]{4,3,2,1,0:T(8,128)(2,1)S(1)} %add_chunk1_step1.1), channel_id=1, source_target_pairs={{0,2},{1,3},{2,0},{3,1},{4,6},{5,7},{6,4},{7,5},{8,10},{9,11},{10,... | collective-permute-start | bytes 1179656 | tf_op jit(solution)/shard_map/ppermute | solution.py:482
  26.4 16.0 %collective-permute-start.13 = (bf16[2,2,2,160,128]{4,3,2,1,0:T(8,128)(2,1)S(1)}, bf16[2,2,2,160,128]{4,3,2,1,0:T(8,128)(2,1)S(1)}, u32[]{:S(2)}, u32[]{:S(2)}) collective-permute-start(bf16[2,2,2,160,128]{4,3,2,1,0:T(8,128)(2,1)S(1)} %add_chunk2_step1.1), channel_id=1, source_target_pairs={{0,8},{1,9},{2,10},{3,11},{4,12},{5,13},{6,14},{7,15},{8,0},{9,1},... | collective-permute-start | bytes 983048 | tf_op jit(solution)/shard_map/ppermute | solution.py:482
  28.0 9.8 %collective-permute-start.3 = (f32[64,256]{1,0:T(8,128)S(1)}, f32[64,256]{1,0:T(8,128)S(1)}, u32[]{:S(2)}, u32[]{:S(2)}) collective-permute-start(f32[64,256]{1,0:T(8,128)S(1)} %get-tuple-element.41), channel_id=1, source_target_pairs={{4,0},{8,4},{12,8},{16,12},{20,16},{24,20},{28,24},{5,1},{9,5},{13... | collective-permute-start | bytes 196616 | tf_op jit(solution)/shard_map/ppermute | solution.py:30
  37.9 7.8 %collective-permute-start.4 = (bf16[2,2,240,128]{3,2,1,0:T(8,128)(2,1)S(1)}, bf16[2,2,240,128]{3,2,1,0:T(8,128)(2,1)S(1)}, u32[]{:S(2)}, u32[]{:S(2)}) collective-permute-start(bf16[2,2,240,128]{3,2,1,0:T(8,128)(2,1)S(1)} %add_chunk0_step2.1), channel_id=1, source_target_pairs={{0,2},{1,3},{2,0},{3,1},{4,6},{5,7},{6,4},{7,5},{8,10},{9,11},{10,... | collective-permute-start | bytes 737288 | tf_op jit(solution)/shard_map/ppermute | solution.py:482
  39.6 8.8 %collective-permute-start.9 = (bf16[2,2,192,128]{3,2,1,0:T(8,128)(2,1)S(1)}, bf16[2,2,192,128]{3,2,1,0:T(8,128)(2,1)S(1)}, u32[]{:S(2)}, u32[]{:S(2)}) collective-permute-start(bf16[2,2,192,128]{3,2,1,0:T(8,128)(2,1)S(1)} %add_chunk1_step2.1), channel_id=1, source_target_pairs={{0,8},{1,9},{2,10},{3,11},{4,12},{5,13},{6,14},{7,15},{8,0},{9,1},... | collective-permute-start | bytes 589832 | tf_op jit(solution)/shard_map/ppermute | solution.py:482
  42.5 6.6 %collective-permute-start.14 = (bf16[2,2,160,128]{3,2,1,0:T(8,128)(2,1)S(1)}, bf16[2,2,160,128]{3,2,1,0:T(8,128)(2,1)S(1)}, u32[]{:S(2)}, u32[]{:S(2)}) collective-permute-start(bf16[2,2,160,128]{3,2,1,0:T(8,128)(2,1)S(1)} %add_chunk2_step2.1), channel_id=1, source_target_pairs={{0,4},{1,5},{2,6},{3,7},{4,0},{5,1},{6,2},{7,3},{8,12},{9,13},{10,... | collective-permute-start | bytes 491528 | tf_op jit(solution)/shard_map/ppermute | solution.py:482
  45.8 5.5 %collective-permute-start.5 = (bf16[2,240,128]{2,1,0:T(8,128)(2,1)S(1)}, bf16[2,240,128]{2,1,0:T(8,128)(2,1)S(1)}, u32[]{:S(2)}, u32[]{:S(2)}) collective-permute-start(bf16[2,240,128]{2,1,0:T(8,128)(2,1)S(1)} %add_chunk0_step3.1), channel_id=1, source_target_pairs={{0,8},{1,9},{2,10},{3,11},{4,12},{5,13},{6,14},{7,15},{8,0},{9,1},... | collective-permute-start | bytes 368648 | tf_op jit(solution)/shard_map/ppermute | solution.py:482
  48.5 6.9 %collective-permute-start.10 = (bf16[2,192,128]{2,1,0:T(8,128)(2,1)S(1)}, bf16[2,192,128]{2,1,0:T(8,128)(2,1)S(1)}, u32[]{:S(2)}, u32[]{:S(2)}) collective-permute-start(bf16[2,192,128]{2,1,0:T(8,128)(2,1)S(1)} %add_chunk1_step3.1), channel_id=1, source_target_pairs={{0,4},{1,5},{2,6},{3,7},{4,0},{5,1},{6,2},{7,3},{8,12},{9,13},{10,... | collective-permute-start | bytes 294920 | tf_op jit(solution)/shard_map/ppermute | solution.py:482
  49.2 8.0 %collective-permute-start.15 = (bf16[2,160,128]{2,1,0:T(8,128)(2,1)S(1)}, bf16[2,160,128]{2,1,0:T(8,128)(2,1)S(1)}, u32[]{:S(2)}, u32[]{:S(2)}) collective-permute-start(bf16[2,160,128]{2,1,0:T(8,128)(2,1)S(1)} %add_chunk2_step3.1), channel_id=1, source_target_pairs={{0,2},{1,3},{2,0},{3,1},{4,6},{5,7},{6,4},{7,5},{8,10},{9,11},{10,... | collective-permute-start | bytes 245768 | tf_op jit(solution)/shard_map/ppermute | solution.py:482
  51.3 9.2 %collective-permute-start.6 = (bf16[240,128]{1,0:T(8,128)(2,1)S(1)}, bf16[240,128]{1,0:T(8,128)(2,1)S(1)}, u32[]{:S(2)}, u32[]{:S(2)}) collective-permute-start(bf16[240,128]{1,0:T(8,128)(2,1)S(1)} %add_chunk0_step4.1), channel_id=1, source_target_pairs={{0,16},{1,17},{2,18},{3,19},{4,20},{5,21},{6,22},{7,23},{8,24},{9,... | collective-permute-start | bytes 184328 | tf_op jit(solution)/shard_map/ppermute | solution.py:482
  55.4 5.2 %collective-permute-start.11 = (bf16[192,128]{1,0:T(8,128)(2,1)S(1)}, bf16[192,128]{1,0:T(8,128)(2,1)S(1)}, u32[]{:S(2)}, u32[]{:S(2)}) collective-permute-start(bf16[192,128]{1,0:T(8,128)(2,1)S(1)} %add_chunk1_step4.1), channel_id=1, source_target_pairs={{0,16},{1,17},{2,18},{3,19},{4,20},{5,21},{6,22},{7,23},{8,24},{9,... | collective-permute-start | bytes 147464 | tf_op jit(solution)/shard_map/ppermute | solution.py:482
  57.2 5.5 %collective-permute-start.16 = (bf16[160,128]{1,0:T(8,128)(2,1)S(1)}, bf16[160,128]{1,0:T(8,128)(2,1)S(1)}, u32[]{:S(2)}, u32[]{:S(2)}) collective-permute-start(bf16[160,128]{1,0:T(8,128)(2,1)S(1)} %add_chunk2_step4.1), channel_id=1, source_target_pairs={{0,16},{1,17},{2,18},{3,19},{4,20},{5,21},{6,22},{7,23},{8,24},{9,... | collective-permute-start | bytes 122888 | tf_op jit(solution)/shard_map/ppermute | solution.py:482

commit v7 on v6

--- a/solution.py
+++ b/solution.py
@@ -25,13 +25,13 @@
     return [pltpu.with_memory_space_constraint(x, space) for x in arrays]
 
 
-def shifted(x, axis, by):
+def neighbours_swapped(x, axis, even_first):
     count = lax.axis_size(axis)
-    return lax.ppermute(x, axis, [(i, i + by) for i in range(count) if 0 <= i + by < count])
-
-
-def is_last():
-    return lax.axis_index("tm") == lax.axis_size("tm") - 1
+    pairs = []
+    for i in range(count):
+        j = i + 1 if i % 2 == (0 if even_first else 1) else i - 1
+        pairs.append((i, j if 0 <= j < count else i))
+    return lax.ppermute(x, axis, pairs)
 
 
 def column(row, rows):
@@ -42,30 +42,35 @@
     return pl.CostEstimate(flops=flops, bytes_accessed=moved, transcendentals=0)
 
 
-def pack_kernel(tail_x, tail_gs, tail_gk, weight, message):
-    halo, channels = tail_gs.shape
-    by_row = column(weight[...], LANES)[LANES - halo :]
+def pack_kernel(head_x, tail_x, head_gs, head_gk, weight, message_a, message_b):
+    halo, channels = head_x.shape
+    by_row = column(weight[...], LANES)[:halo]
     by_row = jnp.concatenate([by_row] * (channels // LANES), axis=1)
-    message[0 : 2 * halo] = tail_x[...]
-    message[2 * halo : 3 * halo] = (tail_gs[...].astype(jnp.float32) * by_row).astype(jnp.bfloat16)
-    message[3 * halo :] = (tail_gk[...].astype(jnp.float32) * by_row).astype(jnp.bfloat16)
+    for_prev = jnp.concatenate([
+        head_x[...],
+        (head_gs[...].astype(jnp.float32) * by_row).astype(jnp.bfloat16),
+        (head_gk[...].astype(jnp.float32) * by_row).astype(jnp.bfloat16),
+    ])
+    for_next = jnp.concatenate([tail_x[...], jnp.zeros((2 * halo, channels), jnp.bfloat16)])
+    odd = lax.rem(lax.axis_index("tm"), 2) == 1
+    message_a[...] = jnp.where(odd, for_prev, for_next)
+    message_b[...] = jnp.where(odd, for_next, for_prev)
 
 
 def pack(halo, x, grad_stream_out, grad_skip_out, weight):
     length, channels = x.shape
-
-    def last(rows):
-        return pl.BlockSpec((rows, channels), lambda i: (length // rows - 1, 0))
-
+    first = pl.BlockSpec((halo, channels), lambda i: (0, 0))
+    last = pl.BlockSpec((halo, channels), lambda i: (length // halo - 1, 0))
+    message = jax.ShapeDtypeStruct((3 * halo, channels), jnp.bfloat16)
     return pl.pallas_call(
         pack_kernel,
         grid=(1,),
-        in_specs=[last(2 * halo), last(halo), last(halo), pl.BlockSpec((1, LANES), lambda i: (0, length // LANES - 1))],
-        out_specs=pl.BlockSpec((4 * halo, channels), lambda i: (0, 0)),
-        out_shape=jax.ShapeDtypeStruct((4 * halo, channels), jnp.bfloat16),
+        in_specs=[first, last, first, first, pl.BlockSpec((1, LANES), lambda i: (0, 0))],
+        out_specs=[pl.BlockSpec(message.shape, lambda i: (0, 0))] * 2,
+        out_shape=[message] * 2,
         compiler_params=pltpu.CompilerParams(vmem_limit_bytes=ADD_BYTES),
         name="pack_borders",
-    )(*held((x, grad_stream_out, grad_skip_out, weight), pltpu.HBM))
+    )(*held((x, x, grad_stream_out, grad_skip_out, weight), pltpu.HBM))
 
 
 def load_kernel(
@@ -141,68 +146,63 @@
 
 
 def backward(plan, layers, refs_of, conv_w, out_w, grad_stream, scratch, grad_parts):
-    grad_proj, grad_preact, past_part, conv_total, *out_totals = scratch
+    grad_proj, past_part, total = scratch
     halo, length, channels = plan["halo"], plan["length"], plan["channels"]
-    border = length + halo
+    own = slice(halo, halo + length)
     items = plan["items"]
-    past_part[border:] = jnp.zeros((past_part.shape[0] - border, channels), jnp.float32)
-    grad_proj[:, :channels] = grad_stream[...].astype(jnp.bfloat16)
-
-    def add_rows(at, to, index):
-        rows = slice(halo + at, halo + to)
-        operands, _, gates = refs_of(index)
-        yield conv_total, (index, False), operands[rows], grad_preact[at:to]
-        if (index - 1, True) in items:
-            yield out_totals[0], (index - 1, True), refs_of(index - 1)[2][rows], grad_proj[at:to]
+
+    def out_grad(index):
+        if (index, True) in items:
+            total[0:channels] = dot(refs_of(index)[2][own], grad_proj[0:length], TN)
+            plan["store"](total, items.index((index, True)), grad_parts)
 
     for index in layers:
-        dilation = 2**index
-        _, factors, gates = refs_of(index)
-        grad_gated = dot(grad_proj[...], out_w[index], NT)
-        first = index == layers[0] and (index, True) in items
-        if first:
-            out_totals[1][...] = dot(gates[halo:border], grad_proj[0:length], TN)
-
-            @pl.when(is_last())
-            def _():
-                out_totals[1][...] += dot(gates[border:], grad_proj[length:], TN)
-
-            plan["store"](out_totals[1], items.index((index, True)), grad_parts)
-        both = factors[halo:]
-        grad_preact[...] = jnp.concatenate(
+        dilation, count = 2**index, plan["counts"][index]
+        operands, factors, _ = refs_of(index)
+        grad_proj[0:count, :channels] = grad_stream[0:count].astype(jnp.bfloat16)
+        grad_gated = dot(grad_proj[0:count], out_w[index], NT)
+        out_grad(index)
+        both = factors[halo : halo + count]
+        grad_preact = jnp.concatenate(
             [grad_gated * both[:, :channels], grad_gated * both[:, channels:]], axis=1
         ).astype(jnp.bfloat16)
-        spread = dot(grad_preact[...], conv_w[index], NT)
-        past_part[0:border] = spread[:, channels:]
-        grad_stream[...] += spread[:, :channels] + past_part[dilation : dilation + border]
-        if index:
-            grad_proj[:, :channels] = grad_stream[...].astype(jnp.bfloat16)
-        for total, _, left, right in add_rows(0, length, index):
-            total[...] = dot(left, right, TN)
-
-        @pl.when(is_last())
-        def _():
-            for total, _, left, right in add_rows(length, border, index):
-                total[...] += dot(left, right, TN)
-
-        for total, item, _, _ in add_rows(0, 0, index):
-            plan["store"](total, items.index(item), grad_parts)
+        spread = dot(grad_preact, conv_w[index], NT)
+        past_part[0:count] = spread[:, channels:]
+        rows = plan["counts"][index - 1] if index else length
+        grad_stream[0:rows] += spread[0:rows, :channels] + past_part[dilation : dilation + rows]
+        total[...] = dot(operands[own], grad_preact[0:length], TN)
+        plan["store"](total, items.index((index, False)), grad_parts)
+    after = layers[-1] - 1
+    if (after, True) in items:
+        grad_proj[0:length, :channels] = grad_stream[0:length].astype(jnp.bfloat16)
+        out_grad(after)
 
 
 def first_kernel(
-    plan, prev_rows, own_x, own_grad, own_skip, sums, conv_w, out_w,
+    plan, message_a, message_b, own_x, own_grad, own_skip, sums, conv_w, out_w,
     low_operands, low_factors, low_gates, grad_stream, grad_skip, *rest,
 ):
-    *grad_parts, stream, operands, factors, gates = rest[: 4 + 2]
+    *grad_parts, stream, operands, factors, gates = rest[:6]
     scratch = rest[6:]
     halo, (length, channels) = plan["halo"], own_x.shape
     layers, low = conv_w.shape[0], low_gates.shape[0]
     pad = 2 ** (layers - 1)
     extent = length + 2 * halo
-    begin = 2 * halo
+    at = lax.axis_index("tm")
+    odd, is_first, is_last = lax.rem(at, 2) == 1, at == 0, at == lax.axis_size("tm") - 1
+
+    def from_prev(rows):
+        chosen = jnp.where(odd, message_a[rows], message_b[rows])
+        return jnp.where(is_first, jnp.zeros_like(chosen), chosen)
+
+    def from_next(rows):
+        chosen = jnp.where(odd, message_b[rows], message_a[rows])
+        return jnp.where(is_last, jnp.zeros_like(chosen), chosen)
+
     stream[0:pad] = jnp.zeros((pad, channels), jnp.float32)
-    stream[pad : pad + begin] = prev_rows[0:begin].astype(jnp.float32)
-    stream[pad + begin :] = own_x[...].astype(jnp.float32)
+    stream[pad : pad + halo] = from_prev(slice(0, halo)).astype(jnp.float32)
+    stream[pad + halo : pad + halo + length] = own_x[...].astype(jnp.float32)
+    stream[pad + halo + length :] = from_next(slice(0, halo)).astype(jnp.float32)
 
     def refs_of(index):
         if index < low:
@@ -224,10 +224,10 @@
         if index < layers - 1:
             stream[pad + start :] += dot(gate[start:], out_w[index, :, :channels], NN)
 
-    grad_stream[0:halo] = prev_rows[2 * halo : 3 * halo].astype(jnp.float32)
-    grad_stream[halo:] = own_grad[...]
-    grad_skip[0:halo] = prev_rows[3 * halo :]
-    grad_skip[halo:] = own_skip[...]
+    grad_stream[0:length] = own_grad[...]
+    grad_stream[length:] = from_next(slice(halo, 2 * halo)).astype(jnp.float32)
+    grad_skip[0:length] = own_skip[...]
+    grad_skip[length:] = from_next(slice(2 * halo, 3 * halo))
     scratch[0][:, channels:] = grad_skip[...]
     backward(plan, list(reversed(range(low, layers))), refs_of, conv_w, out_w, grad_stream, scratch, grad_parts)
     plan["finish"](sums, grad_parts)
@@ -236,8 +236,7 @@
 def later_kernel(
     plan, first, third, low_operands, low_factors, low_gates, grad_before, grad_skip, conv_w, out_w, *rest
 ):
-    outs = rest[plan["unused"] : plan["unused"] + plan["outs"]]
-    keep, send, grad_stream, *scratch = rest[plan["unused"] + plan["outs"] :]
+    grad_after, keep, send, grad_stream, *scratch = rest[plan["unused"] :]
     grad_stream[...] = grad_before[...]
     scratch[0][:, plan["channels"] :] = grad_skip[...]
 
@@ -246,16 +245,14 @@
 
     layers = list(reversed(range(first, first + third)))
     backward(plan, layers, refs_of, conv_w, out_w, grad_stream, scratch, (keep, send))
-    at = 0
-    for out in outs:
-        out[...] = grad_stream[at : at + out.shape[0]]
-        at += out.shape[0]
+    grad_after[...] = grad_stream[0 : grad_after.shape[0]]
 
 
 def store_whole(items, total, item, grad_parts):
     is_out = items[item][1]
     place = sum(kind == is_out for _, kind in items[:item])
-    grad_parts[int(is_out)][place] = total[...].astype(jnp.bfloat16)
+    part = grad_parts[int(is_out)]
+    part[place] = total[0 : part.shape[1]].astype(jnp.bfloat16)
 
 
 def finish_whole(sums, grad_parts):
@@ -271,16 +268,17 @@
             )
 
 
-def store_shards(tm, dp, order, bases, total, item, grad_parts):
+def store_shards(tm, dp, order, items, bases, total, item, grad_parts):
     keep, send = grad_parts
     t_at, d_at = lax.axis_index("tm"), lax.axis_index("dp")
     core_at = lax.rem(d_at, 2)
-    rows = total.shape[0] // tm
+    height = total.shape[0] // (2 if items[item][1] else 1)
+    rows = height // tm
     at = pl.ds(bases[item], rows)
     at_bits = bits_of(t_at, d_at, lax.rem, lax.div)
     for y in range(dp // 2):
-        near = total[:, (2 * y) * LANES : (2 * y + 1) * LANES]
-        far = total[:, (2 * y + 1) * LANES : (2 * y + 2) * LANES]
+        near = total[0:height, (2 * y) * LANES : (2 * y + 1) * LANES]
+        far = total[0:height, (2 * y + 1) * LANES : (2 * y + 2) * LANES]
         mine = jnp.where(core_at == 0, near, far).astype(jnp.bfloat16)
         other = jnp.where(core_at == 0, far, near).astype(jnp.bfloat16)
         for t in range(tm):
@@ -301,7 +299,7 @@
     return ends[:-1], ends[-1]
 
 
-def run_layers(in_shards, tm, dp, halo, prev_rows, loaded):
+def run_layers(in_shards, tm, dp, halo, messages, loaded):
     own_x, own_grad, own_skip, sums, conv_w, out_w = loaded
     length, channels = own_x.shape
     layers = conv_w.shape[0]
@@ -312,13 +310,14 @@
     for index in range(layers):
         need = halo if index == layers - 1 else 2 ** (index + 1)
         starts.append(need // 16 * 16)
-    plan = {"halo": halo, "starts": starts, "length": length, "channels": channels}
+    counts = [-(-(length + 2 ** (index + 1) - 1) // 16) * 16 for index in range(layers)]
+    plan = {"halo": halo, "starts": starts, "counts": counts, "length": length, "channels": channels}
     plans, shapes = [], []
     for chunk, order in enumerate(CHAINS):
         items = items_of(layers, chunk)
         bases, rows = bases_of(items, tm, channels)
         if in_shards:
-            store = functools.partial(store_shards, tm, dp, order, bases)
+            store = functools.partial(store_shards, tm, dp, order, items, bases)
             finish = functools.partial(finish_shards, EXTRA[chunk])
             shapes.append(2 * [(2,) * len(order) + (rows + EXTRA[chunk], LANES)])
         else:
@@ -331,15 +330,12 @@
     flops = 2 * length * channels * channels
     scratch = [
         pltpu.VMEM((border, 2 * channels), jnp.bfloat16),
-        pltpu.VMEM((border, 2 * channels), jnp.bfloat16),
-        pltpu.VMEM((border + 2 ** (layers - 1), channels), jnp.float32),
+        pltpu.VMEM((border, channels), jnp.float32),
         pltpu.VMEM((2 * channels, 2 * channels), jnp.float32),
-        pltpu.VMEM((channels, 2 * channels), jnp.float32),
-        pltpu.VMEM((channels, 2 * channels), jnp.float32),
     ]
     *kept, grad_stream, grad_skip, keep, send = pl.pallas_call(
         functools.partial(first_kernel, plans[0]),
-        in_specs=[vmem] * 7,
+        in_specs=[vmem] * 8,
         out_specs=[vmem] * 7,
         out_shape=[
             pltpu.VMEM((low, extent, 2 * channels), jnp.bfloat16),
@@ -359,15 +355,15 @@
         compiler_params=pltpu.CompilerParams(vmem_limit_bytes=VMEM_BYTES),
         cost_estimate=cost(flops * (5 * layers + 12 * third), weight_bytes),
         name="forward_and_last_third",
-    )(*held((prev_rows, *loaded)))
-
-    def later(step, outs, after):
-        more = {"unused": len(after), "outs": len(outs)}
+    )(*held((*messages, *loaded)))
+
+    def later(step, rows, after):
+        more = {"unused": len(after)}
         return pl.pallas_call(
             functools.partial(later_kernel, plans[step] | more, layers - (step + 1) * third, third),
             in_specs=[vmem] * 7 + [anywhere] * len(after),
-            out_specs=[vmem] * (len(outs) + 2),
-            out_shape=[pltpu.VMEM((rows, channels), jnp.float32) for rows in outs]
+            out_specs=[vmem] * 3,
+            out_shape=[pltpu.VMEM((rows, channels), jnp.float32)]
             + [pltpu.VMEM(shape, jnp.bfloat16) for shape in shapes[step]],
             scratch_shapes=[pltpu.VMEM((border, channels), jnp.float32)] + scratch,
             compiler_params=pltpu.CompilerParams(vmem_limit_bytes=VMEM_BYTES),
@@ -378,13 +374,13 @@
     parts = [(keep, send)]
     if in_shards:
         parts[0] = Chunk(tm, dp, 0, keep, send)
-    grad_stream, *middle = later(1, [border], [])
-    other, own, tail, *last = later(2, [halo, length - halo, halo], [parts[0].next_message()] if in_shards else [])
+    grad_stream, *middle = later(1, border, [])
+    grad_in, *last = later(2, length, [parts[0].next_message()] if in_shards else [])
     parts += [middle, last]
     if in_shards:
         for step in (1, 2):
             parts[step] = Chunk(tm, dp, step, *parts[step])
-    return other, own, tail, parts
+    return grad_in, parts
 
 
 def add_kernel(count, groups, *refs):
@@ -406,16 +402,16 @@
                 out[lead + (slice(first + body, first + rows),)] = jnp.broadcast_to(slab, out.shape[:-2] + slab.shape)
 
 
-def add_up(arrays, groups, shapes, after, name):
+def add_up(arrays, groups, shapes, name):
     vmem = pl.BlockSpec(memory_space=pltpu.VMEM)
     return pl.pallas_call(
         functools.partial(add_kernel, len(arrays), groups),
-        in_specs=[vmem] * len(arrays) + [pl.BlockSpec(memory_space=pl.ANY)] * len(after),
+        in_specs=[vmem] * len(arrays),
         out_specs=[vmem] * len(groups),
         out_shape=[pltpu.VMEM(shape, jnp.bfloat16) for shape in shapes],
         compiler_params=pltpu.CompilerParams(vmem_limit_bytes=ADD_BYTES),
         name=name,
-    )(*held(arrays), *held(after))
+    )(*held(arrays))
 
 
 def first_block(array, first, rows):
@@ -431,8 +427,8 @@
     for count in counts:
         chunks.append(refs[:count])
         refs = refs[count:]
-    other, own, tail, grad_inputs, grad_conv, grad_out = refs
-    layers, channels = grad_conv.shape[0], own.shape[1]
+    grad_in, grad_inputs, grad_conv, grad_out = refs
+    layers, channels = grad_conv.shape[0], grad_in.shape[1]
     total = 0.0
     for term in chunks[0]:
         total = total + jnp.sum(first_block(term, term.shape[-2] - 16, 16), axis=0, keepdims=True)
@@ -447,8 +443,7 @@
             out[index] = value * scale
     for first in range(0, channels, LANES):
         lanes = slice(first, first + LANES)
-        grad_inputs[0 : own.shape[0], lanes] = own[:, lanes] * scale
-        grad_inputs[own.shape[0] :, lanes] = jnp.where(is_last(), tail[:, lanes], other[:, lanes]) * scale
+        grad_inputs[:, lanes] = grad_in[:, lanes] * scale
 
 
 class Chunk:
@@ -457,21 +452,21 @@
         self.message = None
         self.terms = [keep, swapped(tm, dp, send, "core")]
 
-    def next_message(self, after=()):
+    def next_message(self):
         if self.message is None:
             left = len(CHAINS[self.chunk]) + 2 - len(self.terms)
             pieces = []
             for i, v in enumerate(self.terms):
                 pieces.append((i, (0,) * (len(v.shape) - 2 - left) + (1,), 0))
             (self.message,) = add_up(
-                self.terms, [[(0, self.rows, self.chunk == 0, pieces)]], [(2,) * (left - 1) + (self.rows, LANES)], after,
+                self.terms, [[(0, self.rows, self.chunk == 0, pieces)]], [(2,) * (left - 1) + (self.rows, LANES)],
                 "add_chunk%d_step%d" % (self.chunk, len(self.terms) - 1),
             )
         return self.message
 
-    def run_chain(self, after=()):
-        for step, name in enumerate(CHAINS[self.chunk]):
-            self.terms.append(swapped(self.tm, self.dp, self.next_message(after if step == 1 else ()), name))
+    def run_chain(self):
+        for name in CHAINS[self.chunk]:
+            self.terms.append(swapped(self.tm, self.dp, self.next_message(), name))
             self.message = None
         return self.terms
 
@@ -495,12 +490,11 @@
     halo = 2**layers
     samples_all = batch * length * tm * dp
     x, gs, gk = inputs[0], grad_stream_out[0], grad_skip_out[0]
-    message = pack(halo, x, gs, gk, sample_weight)
-    prev_rows = shifted(message, "tm", 1)
-    loaded = load_all(x, gs, gk, sample_weight, conv_weight, out_weight, message)
+    message_a, message_b = pack(halo, x, gs, gk, sample_weight)
+    messages = [neighbours_swapped(message_a, "tm", True), neighbours_swapped(message_b, "tm", False)]
+    loaded = load_all(x, gs, gk, sample_weight, conv_weight, out_weight, message_a)
     in_shards = tm == 8 and dp == 4 and channels // tm % 16 == 0 and 2 * channels == dp * LANES
-    other, own, tail, parts = run_layers(in_shards, tm, dp, halo, prev_rows, loaded)
-    other = shifted(other, "tm", -1)
+    grad_in, parts = run_layers(in_shards, tm, dp, halo, messages, loaded)
     if not in_shards:
         scale = samples_all / lax.psum(jnp.sum(sample_weight), ("tm", "dp"))
         found = {}
@@ -512,9 +506,8 @@
         grad_conv, grad_out = (
             scattered(jnp.stack([found[index, is_out] for index in range(layers)])) * scale for is_out in (False, True)
         )
-        ends = jnp.where(is_last(), tail, other)
-        return (jnp.concatenate([own, ends]) * scale)[None], grad_conv, grad_out
-    chunks = [part.run_chain([other] if part is parts[0] else ()) for part in parts]
+        return (grad_in * scale)[None], grad_conv, grad_out
+    chunks = [part.run_chain() for part in parts]
     conv_rows, out_rows = 2 * channels // tm, channels // tm
     grad_inputs, grad_conv, grad_out = pl.pallas_call(
         functools.partial(last_kernel, [len(terms) for terms in chunks], float(samples_all), tm),
@@ -525,7 +518,7 @@
         ],
         compiler_params=pltpu.CompilerParams(vmem_limit_bytes=ADD_BYTES),
         name="scale_all",
-    )(*held([term for terms in chunks for term in terms]), *held([other, own, tail]))
+    )(*held([term for terms in chunks for term in terms]), *held([grad_in]))
     return grad_inputs[None], grad_conv, grad_out
 
 

time: 64 us -> 59.7 us (0.933)
  Pallas kernels: 17.5 us -> 15.1 us
  waiting for transfers between devices: 16 us -> 14.9 us
  starting transfers between devices: 29.6 us -> 28.7 us
    ppermute x2, waiting for transfers between devices: 8.57 us -> 0.01 us  [neighbours_swapped(): return lax.ppermute(x, axis, pairs)]
    ppermute x15, waiting for transfers between devices: 7.41 us -> 14.9 us  [swapped(): return lax.ppermute(value, ('tm', 'dp'), pairs)]
    ppermute x2, starting transfers between devices: 6.13 us -> 3.66 us  [neighbours_swapped(): return lax.ppermute(x, axis, pairs)]
    ppermute x15, starting transfers between devices: 23.4 us -> 25.1 us  [swapped(): return lax.ppermute(value, ('tm', 'dp'), pairs)]
    pallas_call x2, Pallas kernels: 5.5 us -> 4.19 us  [later(): pl.pallas_call(functools.partial(later_kernel, plans[step] | more, layers...]
    pallas_call x1, Pallas kernels: 6.5 us -> 5.49 us  [run_layers(): pl.pallas_call(functools.partial(first_kernel, plans[0]), in_specs=[vmem]...]
  transfers between devices with their start and end apart: 17 -> 17, of which waited for: 5 -> 5; matrix products, arithmetic and copies ran while one was open for 0% -> 0% of each run, Pallas kernels for 14% -> 13%
where the time goes in v7:
time: 59.7 us; the launch traced here: 59.5 us
  starting transfers between devices  28.7 us (48%)
  Pallas kernels  15.1 us (25%)
  waiting for transfers between devices  14.9 us (25%)
  between operations  0.74 us (1%)
    ppermute x15, starting transfers between devices, swapped(): return lax.ppermute(value, ('tm', 'dp'), pairs)  25.1 us
    ppermute x15, waiting for transfers between devices, swapped(): return lax.ppermute(value, ('tm', 'dp'), pairs)  14.9 us
    pallas_call x1, Pallas kernels, run_layers(): pl.pallas_call(functools.partial(first_kernel, plans[0]), in_specs=[vmem]...  5.49 us
    pallas_call x2, Pallas kernels, later(): pl.pallas_call(functools.partial(later_kernel, plans[step] | more, layers...  4.19 us
    ppermute x2, starting transfers between devices, neighbours_swapped(): return lax.ppermute(x, axis, pairs)  3.66 us
    pallas_call x1, Pallas kernels, load_all(): pl.pallas_call(load_kernel, in_specs=[anywhere] * 7, out_specs=[vmem] * 6...  2.68 us
  transfers between devices with their start and end apart: 17, of which 5 were waited for; matrix products, arithmetic and copies ran while one was open for 0% of the time, Pallas kernels for 13%

profile of v7, /device:TPU:0, one launch (start us, length us, event | category | flops | bytes accessed | tf_op | source)
XLA Modules:
  0.0 59.5 jit_solution(4938968614150923502)
XLA Ops:
  0.6 0.9 %pack_borders.1 = (bf16[192,256]{1,0:T(8,128)(2,1)S(1)}, bf16[192,256]{1,0:T(8,128)(2,1)S(1)}) custom-call(bf16[512,256]{1,0:T(8,128)(2,1)} %bitcast.4, bf16[512,256]{1,0:T(8,128)(2,1)} %bitcast.5, bf16[512,256]{1,0:T(8,128)(2,1)} %bitcast.7, bf16[512,256]{1,0:T(8,128)(2,1)} %bitcast.9, f32[1,512]{1,0:T(1,128)} %weight.3), custom_call_target="tpu_custom_call" | custom-call | tf_op jit(solution)/shard_map/pack_borders/pallas_call | solution.py:65
  1.5 3.0 %collective-permute-start = (bf16[192,256]{1,0:T(8,128)(2,1)S(1)}, bf16[192,256]{1,0:T(8,128)(2,1)S(1)}, u32[]{:S(2)}, u32[]{:S(2)}) collective-permute-start(bf16[192,256]{1,0:T(8,128)(2,1)S(1)} %get-tuple-element.27._), channel_id=1, source_target_pairs={{0,4},{4,0},{8,12},{12,8},{16,20},{20,16},{24,28},{28,24},{1,5},{5... | collective-permute-start | bytes 294920 | tf_op jit(solution)/shard_map/ppermute | solution.py:34
  4.5 0.7 %collective-permute-start.1 = (bf16[192,256]{1,0:T(8,128)(2,1)S(1)}, bf16[192,256]{1,0:T(8,128)(2,1)S(1)}, u32[]{:S(2)}, u32[]{:S(2)}) collective-permute-start(bf16[192,256]{1,0:T(8,128)(2,1)S(1)} %get-tuple-element.28), channel_id=1, source_target_pairs={{0,0},{4,8},{8,4},{12,16},{16,12},{20,24},{24,20},{28,28},{1,1},{5... | collective-permute-start | bytes 294920 | tf_op jit(solution)/shard_map/ppermute | solution.py:34
  5.2 2.7 %load_all.1 = (bf16[512,256]{1,0:T(8,128)(2,1)S(1)}, f32[512,256]{1,0:T(8,128)S(1)}, bf16[512,256]{1,0:T(8,128)(2,1)S(1)}, bf16[16,128]{1,0:T(8,128)(2,1)S(1)}, ...) custom-call(bf16[512,256]{1,0:T(8,128)(2,1)} %bitcast.6, bf16[512,256]{1,0:T(8,128)(2,1)} %bitcast.8, ...), custom_call_target="tpu_custom_call" | custom-call | flops 10000000 | bytes 6000000 | tf_op jit(solution)/shard_map/load_all/pallas_call | solution.py:100
  7.9 0.0 collective-permute-done.message_a
  7.9 0.0 collective-permute-done.1.message_b
  7.9 5.5 %forward_and_last_third.1 = (bf16[4,640,512]{2,1,0:T(8,128)(2,1)S(1)}, f32[4,640,512]{2,1,0:T(8,128)S(1)}, bf16[4,640,256]{2,1,0:T(8,128)(2,1)S(1)}, f32[576,256...) custom-call(bf16[192,256]{1,0:T(8,128)(2,1)S(1)} %collective-permute, ...), custom_call_target="tpu_custom_call" | custom-call | flops 3623878656 | bytes 4718592 | tf_op jit(solution)/shard_map/forward_and_last_third/pallas_call | solution.py:336
  13.4 0.1 collective-permute-start.2
  13.5 2.2 %middle_third.1 = (f32[576,256]{1,0:T(8,128)S(1)}, bf16[2,2,2,2,192,128]{5,4,3,2,1,0:T(8,128)(2,1)S(1)}, bf16[2,2,2,2,192,128]{5,4,3,2,1,0:T(8,128)(2,1)S(1)}) custom-call(bf16[4,640,512]{2,1,0:T(8,128)(2,1)S(1)} %get-tuple-element.37.low_operands, f32[4,640,512]{2,1,0:T(8,128)S(1)} %get-tuple-element.38.low_factors, ...), custom_call_target="tpu_custom_call" | custom-call | flops 1610612736 | bytes 4718592 | tf_op jit(solution)/shard_map/middle_third/pallas_call | solution.py:362
  15.7 0.6 collective-permute-start.7
  16.2 0.0 collective-permute-done.2.refs_1_
  16.2 0.1 add_chunk0_step1.1.rest_0_
  16.3 2.0 %first_third.1 = (f32[512,256]{1,0:T(8,128)S(1)}, bf16[2,2,2,2,160,128]{5,4,3,2,1,0:T(8,128)(2,1)S(1)}, bf16[2,2,2,2,160,128]{5,4,3,2,1,0:T(8,128)(2,1)S(1)}) custom-call(bf16[4,640,512]{2,1,0:T(8,128)(2,1)S(1)} %get-tuple-element.37.low_operands, f32[4,640,512]{2,1,0:T(8,128)S(1)} %get-tuple-element.38.low_factors, ...), custom_call_target="tpu_custom_call" | custom-call | flops 1610612736 | bytes 4718592 | tf_op jit(solution)/shard_map/first_third/pallas_call | solution.py:362
  18.4 0.1 collective-permute-start.12
  18.5 4.3 %collective-permute-start.3 = (bf16[2,2,2,240,128]{4,3,2,1,0:T(8,128)(2,1)S(1)}, bf16[2,2,2,240,128]{4,3,2,1,0:T(8,128)(2,1)S(1)}, u32[]{:S(2)}, u32[]{:S(2)}) collective-permute-start(bf16[2,2,2,240,128]{4,3,2,1,0:T(8,128)(2,1)S(1)} %add_chunk0_step1.1.rest_0_), channel_id=1, source_target_pairs={{0,4},{1,5},{2,6},{3,7},{4,0},{5,1},{6,2},{7,3},{8,12},{9,13},{10,... | collective-permute-start | bytes 1474568 | tf_op jit(solution)/shard_map/ppermute | solution.py:477
  22.8 0.0 collective-permute-done.7.refs_1_.refs_7_
  22.8 0.1 add_chunk1_step1.1
  22.9 1.9 %collective-permute-start.8 = (bf16[2,2,2,192,128]{4,3,2,1,0:T(8,128)(2,1)S(1)}, bf16[2,2,2,192,128]{4,3,2,1,0:T(8,128)(2,1)S(1)}, u32[]{:S(2)}, u32[]{:S(2)}) collective-permute-start(bf16[2,2,2,192,128]{4,3,2,1,0:T(8,128)(2,1)S(1)} %add_chunk1_step1.1), channel_id=1, source_target_pairs={{0,2},{1,3},{2,0},{3,1},{4,6},{5,7},{6,4},{7,5},{8,10},{9,11},{10,... | collective-permute-start | bytes 1179656 | tf_op jit(solution)/shard_map/ppermute | solution.py:477
  24.8 0.0 collective-permute-done.12.refs_1_.refs_13_
  24.8 0.1 add_chunk2_step1.1
  24.8 1.6 %collective-permute-start.13 = (bf16[2,2,2,160,128]{4,3,2,1,0:T(8,128)(2,1)S(1)}, bf16[2,2,2,160,128]{4,3,2,1,0:T(8,128)(2,1)S(1)}, u32[]{:S(2)}, u32[]{:S(2)}) collective-permute-start(bf16[2,2,2,160,128]{4,3,2,1,0:T(8,128)(2,1)S(1)} %add_chunk2_step1.1), channel_id=1, source_target_pairs={{0,8},{1,9},{2,10},{3,11},{4,12},{5,13},{6,14},{7,15},{8,0},{9,1},... | collective-permute-start | bytes 983048 | tf_op jit(solution)/shard_map/ppermute | solution.py:477
  26.5 8.1 %collective-permute-done.3.refs_2_ = bf16[2,2,2,240,128]{4,3,2,1,0:T(8,128)(2,1)S(1)} collective-permute-done((bf16[2,2,2,240,128]{4,3,2,1,0:T(8,128)(2,1)S(1)}, bf16[2,2,2,240,128]{4,3,2,1,0:T(8,128)(2,1)S(1)}, u32[]{:S(2)}, u32[]{:S(2)}) %collective-permute-start.3) | collective-permute-done | bytes 491552 | tf_op jit(solution)/shard_map/ppermute | solution.py:477
  34.6 0.1 add_chunk0_step2.1
  34.7 1.9 %collective-permute-start.4 = (bf16[2,2,240,128]{3,2,1,0:T(8,128)(2,1)S(1)}, bf16[2,2,240,128]{3,2,1,0:T(8,128)(2,1)S(1)}, u32[]{:S(2)}, u32[]{:S(2)}) collective-permute-start(bf16[2,2,240,128]{3,2,1,0:T(8,128)(2,1)S(1)} %add_chunk0_step2.1), channel_id=1, source_target_pairs={{0,2},{1,3},{2,0},{3,1},{4,6},{5,7},{6,4},{7,5},{8,10},{9,11},{10,... | collective-permute-start | bytes 737288 | tf_op jit(solution)/shard_map/ppermute | solution.py:477
  36.6 0.0 collective-permute-done.8.refs_2_.refs_8_
  36.6 0.1 add_chunk1_step2.1
  36.7 2.9 %collective-permute-start.9 = (bf16[2,2,192,128]{3,2,1,0:T(8,128)(2,1)S(1)}, bf16[2,2,192,128]{3,2,1,0:T(8,128)(2,1)S(1)}, u32[]{:S(2)}, u32[]{:S(2)}) collective-permute-start(bf16[2,2,192,128]{3,2,1,0:T(8,128)(2,1)S(1)} %add_chunk1_step2.1), channel_id=1, source_target_pairs={{0,8},{1,9},{2,10},{3,11},{4,12},{5,13},{6,14},{7,15},{8,0},{9,1},... | collective-permute-start | bytes 589832 | tf_op jit(solution)/shard_map/ppermute | solution.py:477
  39.5 0.0 collective-permute-done.13.refs_2_.refs_14_
  39.5 0.1 add_chunk2_step2.1
  39.6 0.6 collective-permute-start.14
  40.2 2.4 %collective-permute-done.4.refs_3_ = bf16[2,2,240,128]{3,2,1,0:T(8,128)(2,1)S(1)} collective-permute-done((bf16[2,2,240,128]{3,2,1,0:T(8,128)(2,1)S(1)}, bf16[2,2,240,128]{3,2,1,0:T(8,128)(2,1)S(1)}, u32[]{:S(2)}, u32[]{:S(2)}) %collective-permute-start.4) | collective-permute-done | bytes 245792 | tf_op jit(solution)/shard_map/ppermute | solution.py:477
  42.6 0.1 add_chunk0_step3.1
  42.6 2.9 %collective-permute-start.5 = (bf16[2,240,128]{2,1,0:T(8,128)(2,1)S(1)}, bf16[2,240,128]{2,1,0:T(8,128)(2,1)S(1)}, u32[]{:S(2)}, u32[]{:S(2)}) collective-permute-start(bf16[2,240,128]{2,1,0:T(8,128)(2,1)S(1)} %add_chunk0_step3.1), channel_id=1, source_target_pairs={{0,8},{1,9},{2,10},{3,11},{4,12},{5,13},{6,14},{7,15},{8,0},{9,1},... | collective-permute-start | bytes 368648 | tf_op jit(solution)/shard_map/ppermute | solution.py:477
  45.5 0.0 collective-permute-done.9.refs_3_.refs_9_
  45.5 0.1 add_chunk1_step3.1
  45.6 0.6 collective-permute-start.10
  46.2 0.0 collective-permute-done.14.refs_3_.refs_15_
  46.2 1.6 %collective-permute-start.15 = (bf16[2,160,128]{2,1,0:T(8,128)(2,1)S(1)}, bf16[2,160,128]{2,1,0:T(8,128)(2,1)S(1)}, u32[]{:S(2)}, u32[]{:S(2)}) collective-permute-start(bf16[2,160,128]{2,1,0:T(8,128)(2,1)S(1)} %add_chunk2_step3.1), channel_id=1, source_target_pairs={{0,2},{1,3},{2,0},{3,1},{4,6},{5,7},{6,4},{7,5},{8,10},{9,11},{10,... | collective-permute-start | bytes 245768 | tf_op jit(solution)/shard_map/ppermute | solution.py:477
  47.8 0.6 collective-permute-done.5.refs_4_
  48.4 0.1 add_chunk0_step4.1
  48.4 3.1 %collective-permute-start.6 = (bf16[240,128]{1,0:T(8,128)(2,1)S(1)}, bf16[240,128]{1,0:T(8,128)(2,1)S(1)}, u32[]{:S(2)}, u32[]{:S(2)}) collective-permute-start(bf16[240,128]{1,0:T(8,128)(2,1)S(1)} %add_chunk0_step4.1), channel_id=1, source_target_pairs={{0,16},{1,17},{2,18},{3,19},{4,20},{5,21},{6,22},{7,23},{8,24},{9,... | collective-permute-start | bytes 184328 | tf_op jit(solution)/shard_map/ppermute | solution.py:477
  51.5 0.0 collective-permute-done.10.refs_4_.refs_10_
  51.6 1.4 %collective-permute-start.11 = (bf16[192,128]{1,0:T(8,128)(2,1)S(1)}, bf16[192,128]{1,0:T(8,128)(2,1)S(1)}, u32[]{:S(2)}, u32[]{:S(2)}) collective-permute-start(bf16[192,128]{1,0:T(8,128)(2,1)S(1)} %add_chunk1_step4.1), channel_id=1, source_target_pairs={{0,16},{1,17},{2,18},{3,19},{4,20},{5,21},{6,22},{7,23},{8,24},{9,... | collective-permute-start | bytes 147464 | tf_op jit(solution)/shard_map/ppermute | solution.py:477
  53.0 0.0 collective-permute-done.15.refs_4_.refs_16_
  53.0 1.7 %collective-permute-start.16 = (bf16[160,128]{1,0:T(8,128)(2,1)S(1)}, bf16[160,128]{1,0:T(8,128)(2,1)S(1)}, u32[]{:S(2)}, u32[]{:S(2)}) collective-permute-start(bf16[160,128]{1,0:T(8,128)(2,1)S(1)} %add_chunk2_step4.1), channel_id=1, source_target_pairs={{0,16},{1,17},{2,18},{3,19},{4,20},{5,21},{6,22},{7,23},{8,24},{9,... | collective-permute-start | bytes 122888 | tf_op jit(solution)/shard_map/ppermute | solution.py:477
  54.7 2.0 %collective-permute-done.11.refs_11_ = bf16[192,128]{1,0:T(8,128)(2,1)S(1)} collective-permute-done((bf16[192,128]{1,0:T(8,128)(2,1)S(1)}, bf16[192,128]{1,0:T(8,128)(2,1)S(1)}, u32[]{:S(2)}, u32[]{:S(2)}) %collective-permute-start.11) | collective-permute-done | bytes 49184 | tf_op jit(solution)/shard_map/ppermute | solution.py:477
  56.6 0.0 collective-permute-done.6.refs_5_
  56.6 1.9 %collective-permute-done.16.refs_17_ = bf16[160,128]{1,0:T(8,128)(2,1)S(1)} collective-permute-done((bf16[160,128]{1,0:T(8,128)(2,1)S(1)}, bf16[160,128]{1,0:T(8,128)(2,1)S(1)}, u32[]{:S(2)}, u32[]{:S(2)}) %collective-permute-start.16) | collective-permute-done | bytes 40992 | tf_op jit(solution)/shard_map/ppermute | solution.py:477
  58.5 1.0 %scale_all.1 = (f32[512,256]{1,0:T(8,128)}, f32[6,64,128]{2,1,0:T(8,128)}, f32[6,32,128]{2,1,0:T(8,128)}) custom-call(bf16[2,2,2,2,240,128]{5,4,3,2,1,0:T(8,128)(2,1)S(1)} %get-tuple-element.35.refs_0_, bf16[2,2,2,2,240,128]{5,4,3,2,1,0:T(8,128)(2,1)S(1)} %collective-permute-done.2.refs_1_, bf16[2,2,2,240,128]{4,3,2,1,0:T(8,128)(2,1)S(1)} %collective-permute-done.3.refs_2_, ...), custom_call_target="tpu_custom_call" | custom-call | tf_op jit(solution)/shard_map/scale_all/pallas_call | solution.py:512
  (3 shorter events, 0.1 us)
Async XLA Ops:
  1.5 6.4 %collective-permute-start = (bf16[192,256]{1,0:T(8,128)(2,1)S(1)}, bf16[192,256]{1,0:T(8,128)(2,1)S(1)}, u32[]{:S(2)}, u32[]{:S(2)}) collective-permute-start(bf16[192,256]{1,0:T(8,128)(2,1)S(1)} %get-tuple-element.27._), channel_id=1, source_target_pairs={{0,4},{4,0},{8,12},{12,8},{16,20},{20,16},{24,28},{28,24},{1,5},{5... | collective-permute-start | bytes 294920 | tf_op jit(solution)/shard_map/ppermute | solution.py:34
  4.5 3.4 %collective-permute-start.1 = (bf16[192,256]{1,0:T(8,128)(2,1)S(1)}, bf16[192,256]{1,0:T(8,128)(2,1)S(1)}, u32[]{:S(2)}, u32[]{:S(2)}) collective-permute-start(bf16[192,256]{1,0:T(8,128)(2,1)S(1)} %get-tuple-element.28), channel_id=1, source_target_pairs={{0,0},{4,8},{8,4},{12,16},{16,12},{20,24},{24,20},{28,28},{1,1},{5... | collective-permute-start | bytes 294920 | tf_op jit(solution)/shard_map/ppermute | solution.py:34
  13.4 2.8 %collective-permute-start.2 = (bf16[2,2,2,2,240,128]{5,4,3,2,1,0:T(8,128)(2,1)S(1)}, bf16[2,2,2,2,240,128]{5,4,3,2,1,0:T(8,128)(2,1)S(1)}, u32[]{:S(2)}, u32[]{:S(2)}) collective-permute-start(bf16[2,2,2,2,240,128]{5,4,3,2,1,0:T(8,128)(2,1)S(1)} %get-tuple-element.36), channel_id=1, source_target_pairs={{0,1},{1,0},{2,3},{3,2},{4,5},{5,4},{6,7},{7,6},{8,9},{9,8},{10,11... | collective-permute-start | bytes 2949128 | tf_op jit(solution)/shard_map/ppermute | solution.py:477
  15.7 7.1 %collective-permute-start.7 = (bf16[2,2,2,2,192,128]{5,4,3,2,1,0:T(8,128)(2,1)S(1)}, bf16[2,2,2,2,192,128]{5,4,3,2,1,0:T(8,128)(2,1)S(1)}, u32[]{:S(2)}, u32[]{:S(2)}) collective-permute-start(bf16[2,2,2,2,192,128]{5,4,3,2,1,0:T(8,128)(2,1)S(1)} %get-tuple-element.43), channel_id=1, source_target_pairs={{0,1},{1,0},{2,3},{3,2},{4,5},{5,4},{6,7},{7,6},{8,9},{9,8},{10,11... | collective-permute-start | bytes 2359304 | tf_op jit(solution)/shard_map/ppermute | solution.py:477
  18.4 6.4 %collective-permute-start.12 = (bf16[2,2,2,2,160,128]{5,4,3,2,1,0:T(8,128)(2,1)S(1)}, bf16[2,2,2,2,160,128]{5,4,3,2,1,0:T(8,128)(2,1)S(1)}, u32[]{:S(2)}, u32[]{:S(2)}) collective-permute-start(bf16[2,2,2,2,160,128]{5,4,3,2,1,0:T(8,128)(2,1)S(1)} %get-tuple-element.46), channel_id=1, source_target_pairs={{0,1},{1,0},{2,3},{3,2},{4,5},{5,4},{6,7},{7,6},{8,9},{9,8},{10,11... | collective-permute-start | bytes 1966088 | tf_op jit(solution)/shard_map/ppermute | solution.py:477
  18.5 16.1 %collective-permute-start.3 = (bf16[2,2,2,240,128]{4,3,2,1,0:T(8,128)(2,1)S(1)}, bf16[2,2,2,240,128]{4,3,2,1,0:T(8,128)(2,1)S(1)}, u32[]{:S(2)}, u32[]{:S(2)}) collective-permute-start(bf16[2,2,2,240,128]{4,3,2,1,0:T(8,128)(2,1)S(1)} %add_chunk0_step1.1.rest_0_), channel_id=1, source_target_pairs={{0,4},{1,5},{2,6},{3,7},{4,0},{5,1},{6,2},{7,3},{8,12},{9,13},{10,... | collective-permute-start | bytes 1474568 | tf_op jit(solution)/shard_map/ppermute | solution.py:477
  22.9 13.7 %collective-permute-start.8 = (bf16[2,2,2,192,128]{4,3,2,1,0:T(8,128)(2,1)S(1)}, bf16[2,2,2,192,128]{4,3,2,1,0:T(8,128)(2,1)S(1)}, u32[]{:S(2)}, u32[]{:S(2)}) collective-permute-start(bf16[2,2,2,192,128]{4,3,2,1,0:T(8,128)(2,1)S(1)} %add_chunk1_step1.1), channel_id=1, source_target_pairs={{0,2},{1,3},{2,0},{3,1},{4,6},{5,7},{6,4},{7,5},{8,10},{9,11},{10,... | collective-permute-start | bytes 1179656 | tf_op jit(solution)/shard_map/ppermute | solution.py:477
  24.8 14.7 %collective-permute-start.13 = (bf16[2,2,2,160,128]{4,3,2,1,0:T(8,128)(2,1)S(1)}, bf16[2,2,2,160,128]{4,3,2,1,0:T(8,128)(2,1)S(1)}, u32[]{:S(2)}, u32[]{:S(2)}) collective-permute-start(bf16[2,2,2,160,128]{4,3,2,1,0:T(8,128)(2,1)S(1)} %add_chunk2_step1.1), channel_id=1, source_target_pairs={{0,8},{1,9},{2,10},{3,11},{4,12},{5,13},{6,14},{7,15},{8,0},{9,1},... | collective-permute-start | bytes 983048 | tf_op jit(solution)/shard_map/ppermute | solution.py:477
  34.7 7.8 %collective-permute-start.4 = (bf16[2,2,240,128]{3,2,1,0:T(8,128)(2,1)S(1)}, bf16[2,2,240,128]{3,2,1,0:T(8,128)(2,1)S(1)}, u32[]{:S(2)}, u32[]{:S(2)}) collective-permute-start(bf16[2,2,240,128]{3,2,1,0:T(8,128)(2,1)S(1)} %add_chunk0_step2.1), channel_id=1, source_target_pairs={{0,2},{1,3},{2,0},{3,1},{4,6},{5,7},{6,4},{7,5},{8,10},{9,11},{10,... | collective-permute-start | bytes 737288 | tf_op jit(solution)/shard_map/ppermute | solution.py:477
  36.7 8.9 %collective-permute-start.9 = (bf16[2,2,192,128]{3,2,1,0:T(8,128)(2,1)S(1)}, bf16[2,2,192,128]{3,2,1,0:T(8,128)(2,1)S(1)}, u32[]{:S(2)}, u32[]{:S(2)}) collective-permute-start(bf16[2,2,192,128]{3,2,1,0:T(8,128)(2,1)S(1)} %add_chunk1_step2.1), channel_id=1, source_target_pairs={{0,8},{1,9},{2,10},{3,11},{4,12},{5,13},{6,14},{7,15},{8,0},{9,1},... | collective-permute-start | bytes 589832 | tf_op jit(solution)/shard_map/ppermute | solution.py:477
  39.6 6.6 %collective-permute-start.14 = (bf16[2,2,160,128]{3,2,1,0:T(8,128)(2,1)S(1)}, bf16[2,2,160,128]{3,2,1,0:T(8,128)(2,1)S(1)}, u32[]{:S(2)}, u32[]{:S(2)}) collective-permute-start(bf16[2,2,160,128]{3,2,1,0:T(8,128)(2,1)S(1)} %add_chunk2_step2.1), channel_id=1, source_target_pairs={{0,4},{1,5},{2,6},{3,7},{4,0},{5,1},{6,2},{7,3},{8,12},{9,13},{10,... | collective-permute-start | bytes 491528 | tf_op jit(solution)/shard_map/ppermute | solution.py:477
  42.6 5.8 %collective-permute-start.5 = (bf16[2,240,128]{2,1,0:T(8,128)(2,1)S(1)}, bf16[2,240,128]{2,1,0:T(8,128)(2,1)S(1)}, u32[]{:S(2)}, u32[]{:S(2)}) collective-permute-start(bf16[2,240,128]{2,1,0:T(8,128)(2,1)S(1)} %add_chunk0_step3.1), channel_id=1, source_target_pairs={{0,8},{1,9},{2,10},{3,11},{4,12},{5,13},{6,14},{7,15},{8,0},{9,1},... | collective-permute-start | bytes 368648 | tf_op jit(solution)/shard_map/ppermute | solution.py:477
  45.6 6.0 %collective-permute-start.10 = (bf16[2,192,128]{2,1,0:T(8,128)(2,1)S(1)}, bf16[2,192,128]{2,1,0:T(8,128)(2,1)S(1)}, u32[]{:S(2)}, u32[]{:S(2)}) collective-permute-start(bf16[2,192,128]{2,1,0:T(8,128)(2,1)S(1)} %add_chunk1_step3.1), channel_id=1, source_target_pairs={{0,4},{1,5},{2,6},{3,7},{4,0},{5,1},{6,2},{7,3},{8,12},{9,13},{10,... | collective-permute-start | bytes 294920 | tf_op jit(solution)/shard_map/ppermute | solution.py:477
  46.2 6.7 %collective-permute-start.15 = (bf16[2,160,128]{2,1,0:T(8,128)(2,1)S(1)}, bf16[2,160,128]{2,1,0:T(8,128)(2,1)S(1)}, u32[]{:S(2)}, u32[]{:S(2)}) collective-permute-start(bf16[2,160,128]{2,1,0:T(8,128)(2,1)S(1)} %add_chunk2_step3.1), channel_id=1, source_target_pairs={{0,2},{1,3},{2,0},{3,1},{4,6},{5,7},{6,4},{7,5},{8,10},{9,11},{10,... | collective-permute-start | bytes 245768 | tf_op jit(solution)/shard_map/ppermute | solution.py:477
  48.4 8.2 %collective-permute-start.6 = (bf16[240,128]{1,0:T(8,128)(2,1)S(1)}, bf16[240,128]{1,0:T(8,128)(2,1)S(1)}, u32[]{:S(2)}, u32[]{:S(2)}) collective-permute-start(bf16[240,128]{1,0:T(8,128)(2,1)S(1)} %add_chunk0_step4.1), channel_id=1, source_target_pairs={{0,16},{1,17},{2,18},{3,19},{4,20},{5,21},{6,22},{7,23},{8,24},{9,... | collective-permute-start | bytes 184328 | tf_op jit(solution)/shard_map/ppermute | solution.py:477
  51.6 5.1 %collective-permute-start.11 = (bf16[192,128]{1,0:T(8,128)(2,1)S(1)}, bf16[192,128]{1,0:T(8,128)(2,1)S(1)}, u32[]{:S(2)}, u32[]{:S(2)}) collective-permute-start(bf16[192,128]{1,0:T(8,128)(2,1)S(1)} %add_chunk1_step4.1), channel_id=1, source_target_pairs={{0,16},{1,17},{2,18},{3,19},{4,20},{5,21},{6,22},{7,23},{8,24},{9,... | collective-permute-start | bytes 147464 | tf_op jit(solution)/shard_map/ppermute | solution.py:477
  53.0 5.5 %collective-permute-start.16 = (bf16[160,128]{1,0:T(8,128)(2,1)S(1)}, bf16[160,128]{1,0:T(8,128)(2,1)S(1)}, u32[]{:S(2)}, u32[]{:S(2)}) collective-permute-start(bf16[160,128]{1,0:T(8,128)(2,1)S(1)} %add_chunk2_step4.1), channel_id=1, source_target_pairs={{0,16},{1,17},{2,18},{3,19},{4,20},{5,21},{6,22},{7,23},{8,24},{9,... | collective-permute-start | bytes 122888 | tf_op jit(solution)/shard_map/ppermute | solution.py:477

commit v8 on v5

--- a/solution.py
+++ b/solution.py
@@ -11,7 +11,7 @@
 VMEM_BYTES = 24 * 1024 * 1024
 ADD_BYTES = 8 * 1024 * 1024
 CHAINS = (("x", "y", "z0", "z1"), ("y", "z0", "x", "z1"), ("z0", "x", "y", "z1"))
-EXTRA = (16, 0, 0)
+EXTRA = (0, 0, 16)
 NN = (((1,), (0,)), ((), ()))
 NT = (((1,), (1,)), ((), ()))
 TN = (((0,), (0,)), ((), ()))
@@ -68,11 +68,7 @@
     x, gs, gk, weight, conv_w, out_w, _, x_here, grad_stream, grad_skip, sums, conv_here, out_here,
     gs_raw, gk_raw, weight_here, sems,
 ):
-    some = pl.ds(0, conv_here.shape[0])
-    pairs = (
-        (weight, weight_here), (gs, gs_raw), (gk, gk_raw), (x, x_here),
-        (conv_w.at[some], conv_here), (out_w.at[some], out_here),
-    )
+    pairs = ((weight, weight_here), (gs, gs_raw), (gk, gk_raw), (x, x_here), (conv_w, conv_here), (out_w, out_here))
     copies = [pltpu.make_async_copy(a, b, sems.at[i]) for i, (a, b) in enumerate(pairs)]
     for copy in copies:
         copy.start()
@@ -89,7 +85,7 @@
         copy.wait()
 
 
-def load_some(low, x, gs, gk, weight, conv_w, out_w, after):
+def load_all(x, gs, gk, weight, conv_w, out_w, after):
     shape = x.shape
     vmem, anywhere = pl.BlockSpec(memory_space=pltpu.VMEM), pl.BlockSpec(memory_space=pl.ANY)
     return pl.pallas_call(
@@ -101,8 +97,8 @@
             pltpu.VMEM(shape, jnp.float32),
             pltpu.VMEM(shape, jnp.bfloat16),
             pltpu.VMEM((16, LANES), jnp.bfloat16),
-            pltpu.VMEM((low,) + conv_w.shape[1:], jnp.bfloat16),
-            pltpu.VMEM((low,) + out_w.shape[1:], jnp.bfloat16),
+            pltpu.VMEM(conv_w.shape, jnp.bfloat16),
+            pltpu.VMEM(out_w.shape, jnp.bfloat16),
         ],
         scratch_shapes=[
             pltpu.VMEM(shape, jnp.bfloat16),
@@ -111,8 +107,8 @@
             pltpu.SemaphoreType.DMA((6,)),
         ],
         compiler_params=pltpu.CompilerParams(vmem_limit_bytes=ADD_BYTES),
-        cost_estimate=cost(10**7, 5 * 10**6),
-        name="load_some",
+        cost_estimate=cost(10**7, 6 * 10**6),
+        name="load_all",
     )(*held((x, gs, gk, weight, conv_w, out_w), pltpu.HBM), *held([after]))
 
 
@@ -145,7 +141,7 @@
     return items + ([(high - third - 1, True)] if high > third else [])
 
 
-def backward(plan, layers, refs_of, weights_of, grad_proj, grad_stream, past_part, total, grad_parts):
+def backward(plan, layers, refs_of, conv_w, out_w, grad_proj, grad_stream, past_part, total, grad_parts):
     halo, length, channels = plan["halo"], plan["length"], plan["channels"]
     own = slice(halo, halo + length)
     items = plan["items"]
@@ -158,15 +154,14 @@
     for index in layers:
         dilation, count = 2**index, plan["counts"][index]
         operands, factors, _ = refs_of(index)
-        conv_layer, out_layer = weights_of(index)
         grad_proj[0:count, :channels] = grad_stream[0:count].astype(jnp.bfloat16)
-        grad_gated = dot(grad_proj[0:count], out_layer[...], NT)
+        grad_gated = dot(grad_proj[0:count], out_w[index], NT)
         out_grad(index)
         both = factors[halo : halo + count]
         grad_preact = jnp.concatenate(
             [grad_gated * both[:, :channels], grad_gated * both[:, channels:]], axis=1
         ).astype(jnp.bfloat16)
-        spread = dot(grad_preact, conv_layer[...], NT)
+        spread = dot(grad_preact, conv_w[index], NT)
         past_part[0:count] = spread[:, channels:]
         cut = slice(halo, halo + max(dilation, 8))
         past_part[cut] = cut_off(past_part[cut], dilation)
@@ -181,22 +176,12 @@
 
 
 def first_kernel(
-    plan, prev_rows, own_x, own_grad, own_skip, sums, conv_low, out_low, conv_w, out_w,
+    plan, prev_rows, own_x, own_grad, own_skip, conv_w, out_w,
     low_operands, low_factors, low_gates, grad_stream, grad_skip, *rest,
 ):
-    grad_parts = rest[:-10]
-    stream, operands, factors, gates, grad_proj, past_part, total, conv_high, out_high, sems = rest[-10:]
+    *grad_parts, stream, operands, factors, gates, grad_proj, past_part, total = rest
     halo, (length, channels) = plan["halo"], own_x.shape
     layers, low = conv_w.shape[0], low_gates.shape[0]
-    copies = {}
-    for index in range(low, layers):
-        at = 2 * (index - low)
-        copies[index] = (
-            pltpu.make_async_copy(conv_w.at[index], conv_high.at[index - low], sems.at[at]),
-            pltpu.make_async_copy(out_w.at[index], out_high.at[index - low], sems.at[at + 1]),
-        )
-        for copy in copies[index]:
-            copy.start()
     pad = 2 ** (layers - 1)
     extent = length + 2 * halo
     begin = 2 * halo
@@ -209,23 +194,15 @@
             return low_operands.at[index], low_factors.at[index], low_gates.at[index]
         return operands.at[index - low], factors.at[index - low], gates.at[index - low]
 
-    def weights_of(index):
-        if index < low:
-            return conv_low.at[index], out_low.at[index]
-        return conv_high.at[index - low], out_high.at[index - low]
-
     for index in range(layers):
         dilation, start = 2**index, plan["starts"][index]
         operand, factor, gate = refs_of(index)
-        conv_layer, out_layer = weights_of(index)
         operand[start:, :channels] = stream[pad + start :].astype(jnp.bfloat16)
         operand[start:, channels:] = stream[pad + start - dilation : pad + extent - dilation].astype(jnp.bfloat16)
         slab = max(dilation, 16)
         earlier = stream[pad + begin - dilation : pad + begin - dilation + slab]
         operand[begin : begin + slab, channels:] = cut_off(earlier, dilation).astype(jnp.bfloat16)
-        for copy in copies.get(index, ()):
-            copy.wait()
-        preact = dot(operand[start:], conv_layer[...], NN)
+        preact = dot(operand[start:], conv_w[index], NN)
         filtered = jnp.tanh(preact[:, :channels])
         opening = 0.5 + 0.5 * jnp.tanh(0.5 * preact[:, channels:])
         product = filtered * opening
@@ -233,7 +210,7 @@
         factor[start:, :channels] = opening - filtered * product
         factor[start:, channels:] = product * (1.0 - opening)
         if index < layers - 1:
-            stream[pad + start :] += dot(gate[start:], out_layer[:, :channels], NN)
+            stream[pad + start :] += dot(gate[start:], out_w[index, :, :channels], NN)
 
     grad_stream[0:halo] = prev_rows[2 * halo : 3 * halo].astype(jnp.float32)
     grad_stream[halo:] = own_grad[...]
@@ -241,14 +218,13 @@
     grad_skip[halo:] = own_skip[...]
     grad_proj[:, channels:] = grad_skip[...]
     backward(
-        plan, list(reversed(range(low, layers))), refs_of, weights_of,
+        plan, list(reversed(range(low, layers))), refs_of, conv_w, out_w,
         grad_proj, grad_stream, past_part, total, grad_parts,
     )
-    plan["finish"](sums, grad_parts)
 
 
 def later_kernel(
-    plan, first, third, low_operands, low_factors, low_gates, grad_before, grad_skip, conv_w, out_w, *rest
+    plan, first, third, low_operands, low_factors, low_gates, grad_before, grad_skip, sums, conv_w, out_w, *rest
 ):
     *outs, keep, send, grad_stream, grad_proj, past_part, total = rest[plan["unused"] :]
     channels = plan["channels"]
@@ -258,17 +234,15 @@
     def refs_of(index):
         return low_operands.at[index], low_factors.at[index], low_gates.at[index]
 
-    def weights_of(index):
-        return conv_w.at[index], out_w.at[index]
-
     backward(
-        plan, list(reversed(range(first, first + third))), refs_of, weights_of,
+        plan, list(reversed(range(first, first + third))), refs_of, conv_w, out_w,
         grad_proj, grad_stream, past_part, total, (keep, send),
     )
     at = 0
     for out in outs:
         out[...] = grad_stream[at : at + out.shape[0]]
         at += out.shape[0]
+    plan["finish"](sums, (keep, send))
 
 
 def store_whole(items, total, height, item, grad_parts):
@@ -320,11 +294,12 @@
     return ends[:-1], ends[-1]
 
 
-def run_layers(in_shards, tm, dp, halo, prev_rows, loaded, conv_w, out_w):
-    own_x, own_grad, own_skip, sums, conv_low, out_low = loaded
+def run_layers(in_shards, tm, dp, halo, prev_rows, loaded):
+    own_x, own_grad, own_skip, sums, conv_w, out_w = loaded
     length, channels = own_x.shape
-    layers, low = conv_w.shape[0], conv_low.shape[0]
-    third = layers - low
+    layers = conv_w.shape[0]
+    third = layers // len(CHAINS)
+    low = layers - third
     extent, border = length + 2 * halo, length + halo
     starts = []
     for index in range(layers):
@@ -350,7 +325,7 @@
     flops = 2 * length * channels * channels
     *kept, grad_stream, grad_skip, keep, send = pl.pallas_call(
         functools.partial(first_kernel, plans[0]),
-        in_specs=[vmem] * 7 + [anywhere] * 2,
+        in_specs=[vmem] * 6,
         out_specs=[vmem] * 7,
         out_shape=[
             pltpu.VMEM((low, extent, 2 * channels), jnp.bfloat16),
@@ -368,19 +343,16 @@
             pltpu.VMEM((border, 2 * channels), jnp.bfloat16),
             pltpu.VMEM((border, channels), jnp.float32),
             pltpu.VMEM((2 * channels, 2 * channels), jnp.float32),
-            pltpu.VMEM((third,) + conv_w.shape[1:], jnp.bfloat16),
-            pltpu.VMEM((third,) + out_w.shape[1:], jnp.bfloat16),
-            pltpu.SemaphoreType.DMA((2 * third,)),
         ],
         compiler_params=pltpu.CompilerParams(vmem_limit_bytes=VMEM_BYTES),
         cost_estimate=cost(flops * (5 * layers + 12 * third), weight_bytes),
         name="forward_and_last_third",
-    )(*held((prev_rows, own_x, own_grad, own_skip, sums, conv_low, out_low)), *held((conv_w, out_w), pltpu.HBM))
+    )(*held((prev_rows, own_x, own_grad, own_skip, conv_w, out_w)))
 
     def later(step, outs, after):
         return pl.pallas_call(
             functools.partial(later_kernel, plans[step] | {"unused": len(after)}, layers - (step + 1) * third, third),
-            in_specs=[vmem] * 7 + [anywhere] * len(after),
+            in_specs=[vmem] * 8 + [anywhere] * len(after),
             out_specs=[vmem] * (len(outs) + 2),
             out_shape=[pltpu.VMEM((rows, channels), jnp.float32) for rows in outs]
             + [pltpu.VMEM(shape, jnp.bfloat16) for shape in shapes[step]],
@@ -393,7 +365,7 @@
             compiler_params=pltpu.CompilerParams(vmem_limit_bytes=VMEM_BYTES),
             cost_estimate=cost(flops * 12 * third, weight_bytes),
             name="middle_third" if step == 1 else "first_third",
-        )(*held((*kept, grad_stream, grad_skip, conv_low, out_low, *after)))
+        )(*held((*kept, grad_stream, grad_skip, sums, conv_w, out_w, *after)))
 
     parts = [(keep, send)]
     if in_shards:
@@ -454,7 +426,7 @@
     other, own, grad_inputs, grad_conv, grad_out = refs
     layers, channels = grad_conv.shape[0], own.shape[1]
     total = 0.0
-    for term in chunks[0]:
+    for term in chunks[-1]:
         total = total + jnp.sum(first_block(term, term.shape[-2] - 16, 16), axis=0, keepdims=True)
     scale = samples_all / total
     for chunk, terms in enumerate(chunks):
@@ -484,14 +456,14 @@
             for i, v in enumerate(self.terms):
                 pieces.append((i, (0,) * (len(v.shape) - 2 - left) + (1,), 0))
             (self.message,) = add_up(
-                self.terms, [[(0, self.rows, self.chunk == 0, pieces)]], [(2,) * (left - 1) + (self.rows, LANES)], after,
+                self.terms, [[(0, self.rows, EXTRA[self.chunk] > 0, pieces)]], [(2,) * (left - 1) + (self.rows, LANES)], after,
                 "add_chunk%d_step%d" % (self.chunk, len(self.terms) - 1),
             )
         return self.message
 
     def run_chain(self, after=()):
         for step, name in enumerate(CHAINS[self.chunk]):
-            self.terms.append(swapped(self.tm, self.dp, self.next_message(after if step == 1 else ()), name))
+            self.terms.append(swapped(self.tm, self.dp, self.next_message(after if step == 2 else ()), name))
             self.message = None
         return self.terms
 
@@ -517,9 +489,9 @@
     x, gs, gk = inputs[0], grad_stream_out[0], grad_skip_out[0]
     message = pack(halo, x, gs, gk, sample_weight)
     prev_rows = around(message, "tm", 1)
-    loaded = load_some(layers - third, x, gs, gk, sample_weight, conv_weight, out_weight, message)
+    loaded = load_all(x, gs, gk, sample_weight, conv_weight, out_weight, message)
     in_shards = tm == 8 and dp == 4 and channels // tm % 16 == 0 and 2 * channels == dp * LANES
-    other, own, parts = run_layers(in_shards, tm, dp, halo, prev_rows, loaded, conv_weight, out_weight)
+    other, own, parts = run_layers(in_shards, tm, dp, halo, prev_rows, loaded)
     other = around(other, "tm", -1)
     if not in_shards:
         scale = samples_all / lax.psum(jnp.sum(sample_weight), ("tm", "dp"))

time: 60 us -> 58.1 us (0.968)
  waiting for transfers between devices: 26.6 us -> 23.4 us
  starting transfers between devices: 16.5 us -> 18.6 us
  Pallas kernels: 15.9 us -> 15.1 us
    ppermute x2, waiting for transfers between devices: 13.9 us -> 7.5 us  [around(): return lax.ppermute(x, axis, [(i, (i + by) % count) for i in range(count)])]
    ppermute x15, waiting for transfers between devices: 12.7 us -> 15.9 us  [swapped(): return lax.ppermute(value, ('tm', 'dp'), pairs)]
    ppermute x15, starting transfers between devices: 10.3 us -> 12.3 us  [swapped(): return lax.ppermute(value, ('tm', 'dp'), pairs)]
    pallas_call x1, Pallas kernels: 6.79 us -> 5.46 us  [run_layers(): pl.pallas_call(functools.partial(first_kernel, plans[0]), in_specs=[vmem]...]
  transfers between devices with their start and end apart: 17 -> 17, of which waited for: 8 -> 7; matrix products, arithmetic and copies ran while one was open for 0% -> 0% of each run, Pallas kernels for 12% -> 13%
where the time goes in v8:
time: 58.1 us; the launch traced here: 57.9 us
  waiting for transfers between devices  23.4 us (40%)
  starting transfers between devices  18.6 us (32%)
  Pallas kernels  15.1 us (26%)
  between operations  0.77 us (1%)
    ppermute x15, waiting for transfers between devices, swapped(): return lax.ppermute(value, ('tm', 'dp'), pairs)  15.9 us
    ppermute x15, starting transfers between devices, swapped(): return lax.ppermute(value, ('tm', 'dp'), pairs)  12.3 us
    ppermute x2, waiting for transfers between devices, around(): return lax.ppermute(x, axis, [(i, (i + by) % count) for i in range(count)])  7.5 us
    ppermute x2, starting transfers between devices, around(): return lax.ppermute(x, axis, [(i, (i + by) % count) for i in range(count)])  6.32 us
    pallas_call x1, Pallas kernels, run_layers(): pl.pallas_call(functools.partial(first_kernel, plans[0]), in_specs=[vmem]...  5.46 us
    pallas_call x2, Pallas kernels, later(): pl.pallas_call(functools.partial(later_kernel, plans[step] | {'unused': l...  4.21 us
    pallas_call x1, Pallas kernels, load_all(): pl.pallas_call(load_kernel, in_specs=[anywhere] * 7, out_specs=[vmem] * 6...  2.67 us
  transfers between devices with their start and end apart: 17, of which 7 were waited for; matrix products, arithmetic and copies ran while one was open for 0% of the time, Pallas kernels for 13%

profile of v8, /device:TPU:0, one launch (start us, length us, event | category | flops | bytes accessed | tf_op | source)
XLA Modules:
  0.0 57.9 jit_solution(8953325349554896787)
XLA Ops:
  0.6 1.0 %pack_borders.1._ = bf16[256,256]{1,0:T(8,128)(2,1)S(1)} custom-call(bf16[512,256]{1,0:T(8,128)(2,1)} %bitcast.4, bf16[512,256]{1,0:T(8,128)(2,1)} %bitcast.6, bf16[512,256]{1,0:T(8,128)(2,1)} %bitcast.8, f32[1,512]{1,0:T(1,128)} %weight.3), custom_call_target="tpu_custom_call" | custom-call | tf_op jit(solution)/shard_map/pack_borders/pallas_call | solution.py:56
  1.6 3.0 %collective-permute-start = (bf16[256,256]{1,0:T(8,128)(2,1)S(1)}, bf16[256,256]{1,0:T(8,128)(2,1)S(1)}, u32[]{:S(2)}, u32[]{:S(2)}) collective-permute-start(bf16[256,256]{1,0:T(8,128)(2,1)S(1)} %pack_borders.1._), channel_id=1, source_target_pairs={{0,4},{4,8},{8,12},{12,16},{16,20},{20,24},{24,28},{28,0},{1,5},{5... | collective-permute-start | bytes 393224 | tf_op jit(solution)/shard_map/ppermute | solution.py:30
  4.6 2.7 %load_all.1 = (bf16[512,256]{1,0:T(8,128)(2,1)S(1)}, f32[512,256]{1,0:T(8,128)S(1)}, bf16[512,256]{1,0:T(8,128)(2,1)S(1)}, bf16[16,128]{1,0:T(8,128)(2,1)S(1)}, ...) custom-call(bf16[512,256]{1,0:T(8,128)(2,1)} %bitcast.5, bf16[512,256]{1,0:T(8,128)(2,1)} %bitcast.7, ...), custom_call_target="tpu_custom_call" | custom-call | flops 10000000 | bytes 6000000 | tf_op jit(solution)/shard_map/load_all/pallas_call | solution.py:91
  7.3 3.9 %collective-permute-done.prev_rows = bf16[256,256]{1,0:T(8,128)(2,1)S(1)} collective-permute-done((bf16[256,256]{1,0:T(8,128)(2,1)S(1)}, bf16[256,256]{1,0:T(8,128)(2,1)S(1)}, u32[]{:S(2)}, u32[]{:S(2)}) %collective-permute-start) | collective-permute-done | bytes 131104 | tf_op jit(solution)/shard_map/ppermute | solution.py:30
  11.1 5.5 %forward_and_last_third.1 = (bf16[4,640,512]{2,1,0:T(8,128)(2,1)S(1)}, f32[4,640,512]{2,1,0:T(8,128)S(1)}, bf16[4,640,256]{2,1,0:T(8,128)(2,1)S(1)}, f32[576,256...) custom-call(bf16[256,256]{1,0:T(8,128)(2,1)S(1)} %collective-permute, ...), custom_call_target="tpu_custom_call" | custom-call | flops 3623878656 | bytes 4718592 | tf_op jit(solution)/shard_map/forward_and_last_third/pallas_call | solution.py:326
  16.6 0.1 collective-permute-start.1
  16.7 2.2 %middle_third.1 = (f32[576,256]{1,0:T(8,128)S(1)}, bf16[2,2,2,2,192,128]{5,4,3,2,1,0:T(8,128)(2,1)S(1)}, bf16[2,2,2,2,192,128]{5,4,3,2,1,0:T(8,128)(2,1)S(1)}) custom-call(bf16[4,640,512]{2,1,0:T(8,128)(2,1)S(1)} %get-tuple-element.33.low_operands, f32[4,640,512]{2,1,0:T(8,128)S(1)} %get-tuple-element.34.low_factors, ...), custom_call_target="tpu_custom_call" | custom-call | flops 1610612736 | bytes 4718592 | tf_op jit(solution)/shard_map/middle_third/pallas_call | solution.py:353
  18.9 0.6 collective-permute-start.7
  19.4 0.0 collective-permute-done.1.refs_1_
  19.4 0.1 add_chunk0_step1.1.rest_0_
  19.5 2.0 %first_third.1 = (f32[64,256]{1,0:T(8,128)S(1)}, f32[448,256]{1,0:T(8,128)S(1)}, bf16[2,2,2,2,176,128]{5,4,3,2,1,0:T(8,128)(2,1)S(1)}, bf16[2,2,2,2,176,128]{5,4,3,2,1,0:T(8,128)(2,1)S(1)}) custom-call(bf16[4,640,512]{2,1,0:T(8,128)(2,1)S(1)} %get-tuple-element.33.low_operands, f32[4,640,512]{2,1,0:T(8,128)S(1)} %get-tuple-element.34.low_factors, ...), custom_call_target="tpu_custom_call" | custom-call | flops 1610612736 | bytes 4718592 | tf_op jit(solution)/shard_map/first_third/pallas_call | solution.py:353
  21.6 0.1 collective-permute-start.12
  21.7 0.1 collective-permute-start.2
  21.7 0.0 collective-permute-done.7.refs_1_.refs_7_
  21.7 0.1 add_chunk1_step1.1
  21.8 1.6 %collective-permute-start.8 = (bf16[2,2,2,192,128]{4,3,2,1,0:T(8,128)(2,1)S(1)}, bf16[2,2,2,192,128]{4,3,2,1,0:T(8,128)(2,1)S(1)}, u32[]{:S(2)}, u32[]{:S(2)}) collective-permute-start(bf16[2,2,2,192,128]{4,3,2,1,0:T(8,128)(2,1)S(1)} %add_chunk1_step1.1), channel_id=1, source_target_pairs={{0,2},{1,3},{2,0},{3,1},{4,6},{5,7},{6,4},{7,5},{8,10},{9,11},{10,... | collective-permute-start | bytes 1179656 | tf_op jit(solution)/shard_map/ppermute | solution.py:474
  23.4 0.4 collective-permute-done.12.refs_1_.refs_13_
  23.8 0.1 add_chunk2_step1.1
  23.9 0.1 collective-permute-start.13
  24.0 10.6 %collective-permute-done.2.refs_2_ = bf16[2,2,2,224,128]{4,3,2,1,0:T(8,128)(2,1)S(1)} collective-permute-done((bf16[2,2,2,224,128]{4,3,2,1,0:T(8,128)(2,1)S(1)}, bf16[2,2,2,224,128]{4,3,2,1,0:T(8,128)(2,1)S(1)}, u32[]{:S(2)}, u32[]{:S(2)}) %collective-permute-start.2) | collective-permute-done | bytes 458784 | tf_op jit(solution)/shard_map/ppermute | solution.py:474
  34.6 0.1 add_chunk0_step2.1
  34.7 1.6 %collective-permute-start.3 = (bf16[2,2,224,128]{3,2,1,0:T(8,128)(2,1)S(1)}, bf16[2,2,224,128]{3,2,1,0:T(8,128)(2,1)S(1)}, u32[]{:S(2)}, u32[]{:S(2)}) collective-permute-start(bf16[2,2,224,128]{3,2,1,0:T(8,128)(2,1)S(1)} %add_chunk0_step2.1), channel_id=1, source_target_pairs={{0,2},{1,3},{2,0},{3,1},{4,6},{5,7},{6,4},{7,5},{8,10},{9,11},{10,... | collective-permute-start | bytes 688136 | tf_op jit(solution)/shard_map/ppermute | solution.py:474
  36.3 0.0 collective-permute-done.8.refs_2_.refs_8_
  36.3 0.1 add_chunk1_step2.1
  36.3 0.1 collective-permute-start.9
  36.4 0.0 collective-permute-done.13.refs_2_.refs_14_
  36.4 0.1 add_chunk2_step2.1
  36.5 0.3 collective-permute-start.14
  36.9 3.3 %collective-permute-start.4 = (f32[64,256]{1,0:T(8,128)S(1)}, f32[64,256]{1,0:T(8,128)S(1)}, u32[]{:S(2)}, u32[]{:S(2)}) collective-permute-start(f32[64,256]{1,0:T(8,128)S(1)} %get-tuple-element.40), channel_id=1, source_target_pairs={{0,28},{4,0},{8,4},{12,8},{16,12},{20,16},{24,20},{28,24},{1,29},{... | collective-permute-start | bytes 196616 | tf_op jit(solution)/shard_map/ppermute | solution.py:30
  40.2 3.6 %collective-permute-done.4.refs_4_.refs_18_ = f32[64,256]{1,0:T(8,128)S(1)} collective-permute-done((f32[64,256]{1,0:T(8,128)S(1)}, f32[64,256]{1,0:T(8,128)S(1)}, u32[]{:S(2)}, u32[]{:S(2)}) %collective-permute-start.4) | collective-permute-done | bytes 65568 | tf_op jit(solution)/shard_map/ppermute | solution.py:30
  43.8 0.0 collective-permute-done.3.refs_3_
  43.8 0.1 add_chunk0_step3.1
  43.9 1.8 %collective-permute-start.5 = (bf16[2,224,128]{2,1,0:T(8,128)(2,1)S(1)}, bf16[2,224,128]{2,1,0:T(8,128)(2,1)S(1)}, u32[]{:S(2)}, u32[]{:S(2)}) collective-permute-start(bf16[2,224,128]{2,1,0:T(8,128)(2,1)S(1)} %add_chunk0_step3.1), channel_id=1, source_target_pairs={{0,8},{1,9},{2,10},{3,11},{4,12},{5,13},{6,14},{7,15},{8,0},{9,1},... | collective-permute-start | bytes 344072 | tf_op jit(solution)/shard_map/ppermute | solution.py:474
  45.7 0.0 collective-permute-done.9.refs_3_.refs_9_
  45.7 0.1 add_chunk1_step3.1
  45.7 0.4 collective-permute-start.10
  46.1 0.0 collective-permute-done.14.refs_3_.refs_15_
  46.1 0.1 add_chunk2_step3.1
  46.2 0.6 collective-permute-start.15
  46.8 2.0 %collective-permute-done.5.refs_4_ = bf16[2,224,128]{2,1,0:T(8,128)(2,1)S(1)} collective-permute-done((bf16[2,224,128]{2,1,0:T(8,128)(2,1)S(1)}, bf16[2,224,128]{2,1,0:T(8,128)(2,1)S(1)}, u32[]{:S(2)}, u32[]{:S(2)}) %collective-permute-start.5) | collective-permute-done | bytes 114720 | tf_op jit(solution)/shard_map/ppermute | solution.py:474
  48.8 2.0 %collective-permute-start.6 = (bf16[224,128]{1,0:T(8,128)(2,1)S(1)}, bf16[224,128]{1,0:T(8,128)(2,1)S(1)}, u32[]{:S(2)}, u32[]{:S(2)}) collective-permute-start(bf16[224,128]{1,0:T(8,128)(2,1)S(1)} %add_chunk0_step4.1), channel_id=1, source_target_pairs={{0,16},{1,17},{2,18},{3,19},{4,20},{5,21},{6,22},{7,23},{8,24},{9,... | collective-permute-start | bytes 172040 | tf_op jit(solution)/shard_map/ppermute | solution.py:474
  50.8 0.0 collective-permute-done.10.refs_4_.refs_10_
  50.9 1.0 %collective-permute-start.11 = (bf16[192,128]{1,0:T(8,128)(2,1)S(1)}, bf16[192,128]{1,0:T(8,128)(2,1)S(1)}, u32[]{:S(2)}, u32[]{:S(2)}) collective-permute-start(bf16[192,128]{1,0:T(8,128)(2,1)S(1)} %add_chunk1_step4.1), channel_id=1, source_target_pairs={{0,16},{1,17},{2,18},{3,19},{4,20},{5,21},{6,22},{7,23},{8,24},{9,... | collective-permute-start | bytes 147464 | tf_op jit(solution)/shard_map/ppermute | solution.py:474
  51.9 0.0 collective-permute-done.15.refs_4_.refs_16_
  51.9 2.0 %collective-permute-start.16 = (bf16[176,128]{1,0:T(8,128)(2,1)S(1)}, bf16[176,128]{1,0:T(8,128)(2,1)S(1)}, u32[]{:S(2)}, u32[]{:S(2)}) collective-permute-start(bf16[176,128]{1,0:T(8,128)(2,1)S(1)} %add_chunk2_step4.1), channel_id=1, source_target_pairs={{0,16},{1,17},{2,18},{3,19},{4,20},{5,21},{6,22},{7,23},{8,24},{9,... | collective-permute-start | bytes 135176 | tf_op jit(solution)/shard_map/ppermute | solution.py:474
  54.0 2.4 %collective-permute-done.11.refs_11_ = bf16[192,128]{1,0:T(8,128)(2,1)S(1)} collective-permute-done((bf16[192,128]{1,0:T(8,128)(2,1)S(1)}, bf16[192,128]{1,0:T(8,128)(2,1)S(1)}, u32[]{:S(2)}, u32[]{:S(2)}) %collective-permute-start.11) | collective-permute-done | bytes 49184 | tf_op jit(solution)/shard_map/ppermute | solution.py:474
  56.3 0.0 collective-permute-done.6.refs_5_
  56.3 0.6 %collective-permute-done.16.refs_17_ = bf16[176,128]{1,0:T(8,128)(2,1)S(1)} collective-permute-done((bf16[176,128]{1,0:T(8,128)(2,1)S(1)}, bf16[176,128]{1,0:T(8,128)(2,1)S(1)}, u32[]{:S(2)}, u32[]{:S(2)}) %collective-permute-start.16) | collective-permute-done | bytes 45088 | tf_op jit(solution)/shard_map/ppermute | solution.py:474
  57.0 1.0 %scale_all.1 = (f32[512,256]{1,0:T(8,128)}, f32[6,64,128]{2,1,0:T(8,128)}, f32[6,32,128]{2,1,0:T(8,128)}) custom-call(bf16[2,2,2,2,224,128]{5,4,3,2,1,0:T(8,128)(2,1)S(1)} %get-tuple-element.31.refs_0_, bf16[2,2,2,2,224,128]{5,4,3,2,1,0:T(8,128)(2,1)S(1)} %collective-permute-done.1.refs_1_, bf16[2,2,2,224,128]{4,3,2,1,0:T(8,128)(2,1)S(1)} %collective-permute-done.2.refs_2_, ...), custom_call_target="tpu_custom_call" | custom-call | tf_op jit(solution)/shard_map/scale_all/pallas_call | solution.py:510
  (3 shorter events, 0.1 us)
Async XLA Ops:
  1.6 9.5 %collective-permute-start = (bf16[256,256]{1,0:T(8,128)(2,1)S(1)}, bf16[256,256]{1,0:T(8,128)(2,1)S(1)}, u32[]{:S(2)}, u32[]{:S(2)}) collective-permute-start(bf16[256,256]{1,0:T(8,128)(2,1)S(1)} %pack_borders.1._), channel_id=1, source_target_pairs={{0,4},{4,8},{8,12},{12,16},{16,20},{20,24},{24,28},{28,0},{1,5},{5... | collective-permute-start | bytes 393224 | tf_op jit(solution)/shard_map/ppermute | solution.py:30
  16.6 2.8 %collective-permute-start.1 = (bf16[2,2,2,2,224,128]{5,4,3,2,1,0:T(8,128)(2,1)S(1)}, bf16[2,2,2,2,224,128]{5,4,3,2,1,0:T(8,128)(2,1)S(1)}, u32[]{:S(2)}, u32[]{:S(2)}) collective-permute-start(bf16[2,2,2,2,224,128]{5,4,3,2,1,0:T(8,128)(2,1)S(1)} %get-tuple-element.32), channel_id=1, source_target_pairs={{0,1},{1,0},{2,3},{3,2},{4,5},{5,4},{6,7},{7,6},{8,9},{9,8},{10,11... | collective-permute-start | bytes 2752520 | tf_op jit(solution)/shard_map/ppermute | solution.py:474
  18.9 2.9 %collective-permute-start.7 = (bf16[2,2,2,2,192,128]{5,4,3,2,1,0:T(8,128)(2,1)S(1)}, bf16[2,2,2,2,192,128]{5,4,3,2,1,0:T(8,128)(2,1)S(1)}, u32[]{:S(2)}, u32[]{:S(2)}) collective-permute-start(bf16[2,2,2,2,192,128]{5,4,3,2,1,0:T(8,128)(2,1)S(1)} %get-tuple-element.42), channel_id=1, source_target_pairs={{0,1},{1,0},{2,3},{3,2},{4,5},{5,4},{6,7},{7,6},{8,9},{9,8},{10,11... | collective-permute-start | bytes 2359304 | tf_op jit(solution)/shard_map/ppermute | solution.py:474
  21.6 2.3 %collective-permute-start.12 = (bf16[2,2,2,2,176,128]{5,4,3,2,1,0:T(8,128)(2,1)S(1)}, bf16[2,2,2,2,176,128]{5,4,3,2,1,0:T(8,128)(2,1)S(1)}, u32[]{:S(2)}, u32[]{:S(2)}) collective-permute-start(bf16[2,2,2,2,176,128]{5,4,3,2,1,0:T(8,128)(2,1)S(1)} %get-tuple-element.44), channel_id=1, source_target_pairs={{0,1},{1,0},{2,3},{3,2},{4,5},{5,4},{6,7},{7,6},{8,9},{9,8},{10,11... | collective-permute-start | bytes 2162696 | tf_op jit(solution)/shard_map/ppermute | solution.py:474
  21.7 12.9 %collective-permute-start.2 = (bf16[2,2,2,224,128]{4,3,2,1,0:T(8,128)(2,1)S(1)}, bf16[2,2,2,224,128]{4,3,2,1,0:T(8,128)(2,1)S(1)}, u32[]{:S(2)}, u32[]{:S(2)}) collective-permute-start(bf16[2,2,2,224,128]{4,3,2,1,0:T(8,128)(2,1)S(1)} %add_chunk0_step1.1.rest_0_), channel_id=1, source_target_pairs={{0,4},{1,5},{2,6},{3,7},{4,0},{5,1},{6,2},{7,3},{8,12},{9,13},{10,... | collective-permute-start | bytes 1376264 | tf_op jit(solution)/shard_map/ppermute | solution.py:474
  21.8 14.4 %collective-permute-start.8 = (bf16[2,2,2,192,128]{4,3,2,1,0:T(8,128)(2,1)S(1)}, bf16[2,2,2,192,128]{4,3,2,1,0:T(8,128)(2,1)S(1)}, u32[]{:S(2)}, u32[]{:S(2)}) collective-permute-start(bf16[2,2,2,192,128]{4,3,2,1,0:T(8,128)(2,1)S(1)} %add_chunk1_step1.1), channel_id=1, source_target_pairs={{0,2},{1,3},{2,0},{3,1},{4,6},{5,7},{6,4},{7,5},{8,10},{9,11},{10,... | collective-permute-start | bytes 1179656 | tf_op jit(solution)/shard_map/ppermute | solution.py:474
  23.9 12.5 %collective-permute-start.13 = (bf16[2,2,2,176,128]{4,3,2,1,0:T(8,128)(2,1)S(1)}, bf16[2,2,2,176,128]{4,3,2,1,0:T(8,128)(2,1)S(1)}, u32[]{:S(2)}, u32[]{:S(2)}) collective-permute-start(bf16[2,2,2,176,128]{4,3,2,1,0:T(8,128)(2,1)S(1)} %add_chunk2_step1.1), channel_id=1, source_target_pairs={{0,8},{1,9},{2,10},{3,11},{4,12},{5,13},{6,14},{7,15},{8,0},{9,1},... | collective-permute-start | bytes 1081352 | tf_op jit(solution)/shard_map/ppermute | solution.py:474
  34.7 9.1 %collective-permute-start.3 = (bf16[2,2,224,128]{3,2,1,0:T(8,128)(2,1)S(1)}, bf16[2,2,224,128]{3,2,1,0:T(8,128)(2,1)S(1)}, u32[]{:S(2)}, u32[]{:S(2)}) collective-permute-start(bf16[2,2,224,128]{3,2,1,0:T(8,128)(2,1)S(1)} %add_chunk0_step2.1), channel_id=1, source_target_pairs={{0,2},{1,3},{2,0},{3,1},{4,6},{5,7},{6,4},{7,5},{8,10},{9,11},{10,... | collective-permute-start | bytes 688136 | tf_op jit(solution)/shard_map/ppermute | solution.py:474
  36.3 9.3 %collective-permute-start.9 = (bf16[2,2,192,128]{3,2,1,0:T(8,128)(2,1)S(1)}, bf16[2,2,192,128]{3,2,1,0:T(8,128)(2,1)S(1)}, u32[]{:S(2)}, u32[]{:S(2)}) collective-permute-start(bf16[2,2,192,128]{3,2,1,0:T(8,128)(2,1)S(1)} %add_chunk1_step2.1), channel_id=1, source_target_pairs={{0,8},{1,9},{2,10},{3,11},{4,12},{5,13},{6,14},{7,15},{8,0},{9,1},... | collective-permute-start | bytes 589832 | tf_op jit(solution)/shard_map/ppermute | solution.py:474
  36.5 9.6 %collective-permute-start.14 = (bf16[2,2,176,128]{3,2,1,0:T(8,128)(2,1)S(1)}, bf16[2,2,176,128]{3,2,1,0:T(8,128)(2,1)S(1)}, u32[]{:S(2)}, u32[]{:S(2)}) collective-permute-start(bf16[2,2,176,128]{3,2,1,0:T(8,128)(2,1)S(1)} %add_chunk2_step2.1), channel_id=1, source_target_pairs={{0,4},{1,5},{2,6},{3,7},{4,0},{5,1},{6,2},{7,3},{8,12},{9,13},{10,... | collective-permute-start | bytes 540680 | tf_op jit(solution)/shard_map/ppermute | solution.py:474
  36.9 7.0 %collective-permute-start.4 = (f32[64,256]{1,0:T(8,128)S(1)}, f32[64,256]{1,0:T(8,128)S(1)}, u32[]{:S(2)}, u32[]{:S(2)}) collective-permute-start(f32[64,256]{1,0:T(8,128)S(1)} %get-tuple-element.40), channel_id=1, source_target_pairs={{0,28},{4,0},{8,4},{12,8},{16,12},{20,16},{24,20},{28,24},{1,29},{... | collective-permute-start | bytes 196616 | tf_op jit(solution)/shard_map/ppermute | solution.py:30
  43.9 4.9 %collective-permute-start.5 = (bf16[2,224,128]{2,1,0:T(8,128)(2,1)S(1)}, bf16[2,224,128]{2,1,0:T(8,128)(2,1)S(1)}, u32[]{:S(2)}, u32[]{:S(2)}) collective-permute-start(bf16[2,224,128]{2,1,0:T(8,128)(2,1)S(1)} %add_chunk0_step3.1), channel_id=1, source_target_pairs={{0,8},{1,9},{2,10},{3,11},{4,12},{5,13},{6,14},{7,15},{8,0},{9,1},... | collective-permute-start | bytes 344072 | tf_op jit(solution)/shard_map/ppermute | solution.py:474
  45.7 5.1 %collective-permute-start.10 = (bf16[2,192,128]{2,1,0:T(8,128)(2,1)S(1)}, bf16[2,192,128]{2,1,0:T(8,128)(2,1)S(1)}, u32[]{:S(2)}, u32[]{:S(2)}) collective-permute-start(bf16[2,192,128]{2,1,0:T(8,128)(2,1)S(1)} %add_chunk1_step3.1), channel_id=1, source_target_pairs={{0,4},{1,5},{2,6},{3,7},{4,0},{5,1},{6,2},{7,3},{8,12},{9,13},{10,... | collective-permute-start | bytes 294920 | tf_op jit(solution)/shard_map/ppermute | solution.py:474
  46.2 5.7 %collective-permute-start.15 = (bf16[2,176,128]{2,1,0:T(8,128)(2,1)S(1)}, bf16[2,176,128]{2,1,0:T(8,128)(2,1)S(1)}, u32[]{:S(2)}, u32[]{:S(2)}) collective-permute-start(bf16[2,176,128]{2,1,0:T(8,128)(2,1)S(1)} %add_chunk2_step3.1), channel_id=1, source_target_pairs={{0,2},{1,3},{2,0},{3,1},{4,6},{5,7},{6,4},{7,5},{8,10},{9,11},{10,... | collective-permute-start | bytes 270344 | tf_op jit(solution)/shard_map/ppermute | solution.py:474
  48.8 7.5 %collective-permute-start.6 = (bf16[224,128]{1,0:T(8,128)(2,1)S(1)}, bf16[224,128]{1,0:T(8,128)(2,1)S(1)}, u32[]{:S(2)}, u32[]{:S(2)}) collective-permute-start(bf16[224,128]{1,0:T(8,128)(2,1)S(1)} %add_chunk0_step4.1), channel_id=1, source_target_pairs={{0,16},{1,17},{2,18},{3,19},{4,20},{5,21},{6,22},{7,23},{8,24},{9,... | collective-permute-start | bytes 172040 | tf_op jit(solution)/shard_map/ppermute | solution.py:474
  50.9 5.5 %collective-permute-start.11 = (bf16[192,128]{1,0:T(8,128)(2,1)S(1)}, bf16[192,128]{1,0:T(8,128)(2,1)S(1)}, u32[]{:S(2)}, u32[]{:S(2)}) collective-permute-start(bf16[192,128]{1,0:T(8,128)(2,1)S(1)} %add_chunk1_step4.1), channel_id=1, source_target_pairs={{0,16},{1,17},{2,18},{3,19},{4,20},{5,21},{6,22},{7,23},{8,24},{9,... | collective-permute-start | bytes 147464 | tf_op jit(solution)/shard_map/ppermute | solution.py:474
  51.9 5.0 %collective-permute-start.16 = (bf16[176,128]{1,0:T(8,128)(2,1)S(1)}, bf16[176,128]{1,0:T(8,128)(2,1)S(1)}, u32[]{:S(2)}, u32[]{:S(2)}) collective-permute-start(bf16[176,128]{1,0:T(8,128)(2,1)S(1)} %add_chunk2_step4.1), channel_id=1, source_target_pairs={{0,16},{1,17},{2,18},{3,19},{4,20},{5,21},{6,22},{7,23},{8,24},{9,... | collective-permute-start | bytes 135176 | tf_op jit(solution)/shard_map/ppermute | solution.py:474

commit v9 on v8

--- a/solution.py
+++ b/solution.py
@@ -10,7 +10,7 @@
 LANES = 128
 VMEM_BYTES = 24 * 1024 * 1024
 ADD_BYTES = 8 * 1024 * 1024
-CHAINS = (("x", "y", "z0", "z1"), ("y", "z0", "x", "z1"), ("z0", "x", "y", "z1"))
+CHAINS = (("y", "x", "z0", "z1"), ("x", "z0", "y", "z1"), ("z0", "y", "x", "z1"))
 EXTRA = (0, 0, 16)
 NN = (((1,), (0,)), ((), ()))
 NT = (((1,), (1,)), ((), ()))
@@ -141,23 +141,29 @@
     return items + ([(high - third - 1, True)] if high > third else [])
 
 
-def backward(plan, layers, refs_of, conv_w, out_w, grad_proj, grad_stream, past_part, total, grad_parts):
+def earlier_rows(plan, index, present, first, last):
+    dilation, begin = 2**index, 2 * plan["halo"]
+    cut = cut_off(present[begin - dilation : begin], dilation)
+    return jnp.concatenate([present[first - dilation : begin - dilation], cut, present[begin : last - dilation]])
+
+
+def backward(plan, layers, refs_of, conv_w, out_w, grad_proj, grad_stream, past_part, grad_parts):
     halo, length, channels = plan["halo"], plan["length"], plan["channels"]
     own = slice(halo, halo + length)
     items = plan["items"]
 
     def out_grad(index):
         if (index, True) in items:
-            total[0:channels] = dot(refs_of(index)[2][own], grad_proj[0:length], TN)
-            plan["store"](total, channels, items.index((index, True)), grad_parts)
+            total = dot(refs_of(index)[3][own], grad_proj[0:length], TN)
+            plan["store"](total, items.index((index, True)), grad_parts)
 
     for index in layers:
         dilation, count = 2**index, plan["counts"][index]
-        operands, factors, _ = refs_of(index)
+        present, earlier, factors, _ = refs_of(index)
         grad_proj[0:count, :channels] = grad_stream[0:count].astype(jnp.bfloat16)
         grad_gated = dot(grad_proj[0:count], out_w[index], NT)
         out_grad(index)
-        both = factors[halo : halo + count]
+        both = factors[halo : halo + count].astype(jnp.float32)
         grad_preact = jnp.concatenate(
             [grad_gated * both[:, :channels], grad_gated * both[:, channels:]], axis=1
         ).astype(jnp.bfloat16)
@@ -167,8 +173,9 @@
         past_part[cut] = cut_off(past_part[cut], dilation)
         rows = plan["counts"][index - 1] if index else length
         grad_stream[0:rows] += spread[0:rows, :channels] + past_part[dilation : dilation + rows]
-        total[...] = dot(operands[own], grad_preact[0:length], TN)
-        plan["store"](total, 2 * channels, items.index((index, False)), grad_parts)
+        past = earlier_rows(plan, index, present, halo, halo + length) if earlier is None else earlier[own]
+        total = dot(jnp.concatenate([present[own], past], axis=1), grad_preact[0:length], TN)
+        plan["store"](total, items.index((index, False)), grad_parts)
     after = layers[-1] - 1
     if (after, True) in items:
         grad_proj[0:length, :channels] = grad_stream[0:length].astype(jnp.bfloat16)
@@ -177,9 +184,9 @@
 
 def first_kernel(
     plan, prev_rows, own_x, own_grad, own_skip, conv_w, out_w,
-    low_operands, low_factors, low_gates, grad_stream, grad_skip, *rest,
+    low_present, low_earlier, low_factors, low_gates, grad_stream, grad_skip, *rest,
 ):
-    *grad_parts, stream, operands, factors, gates, grad_proj, past_part, total = rest
+    *grad_parts, stream, high_present, high_factors, high_gates, grad_proj, past_part = rest
     halo, (length, channels) = plan["halo"], own_x.shape
     layers, low = conv_w.shape[0], low_gates.shape[0]
     pad = 2 ** (layers - 1)
@@ -191,26 +198,35 @@
 
     def refs_of(index):
         if index < low:
-            return low_operands.at[index], low_factors.at[index], low_gates.at[index]
-        return operands.at[index - low], factors.at[index - low], gates.at[index - low]
-
+            return low_present.at[index], low_earlier.at[index], low_factors.at[index], low_gates.at[index]
+        at = index - low
+        return high_present.at[at], None, high_factors.at[at], high_gates.at[at]
+
+    refs_of(0)[0][0:begin] = prev_rows[0:begin]
+    refs_of(0)[0][begin:] = own_x[...]
     for index in range(layers):
         dilation, start = 2**index, plan["starts"][index]
-        operand, factor, gate = refs_of(index)
-        operand[start:, :channels] = stream[pad + start :].astype(jnp.bfloat16)
-        operand[start:, channels:] = stream[pad + start - dilation : pad + extent - dilation].astype(jnp.bfloat16)
-        slab = max(dilation, 16)
-        earlier = stream[pad + begin - dilation : pad + begin - dilation + slab]
-        operand[begin : begin + slab, channels:] = cut_off(earlier, dilation).astype(jnp.bfloat16)
-        preact = dot(operand[start:], conv_w[index], NN)
+        present, earlier, factor, gate = refs_of(index)
+        if earlier is None:
+            past = earlier_rows(plan, index, present, start, extent)
+        else:
+            past = stream[pad + start - dilation : pad + extent - dilation]
+            cut = cut_off(past[begin - start : begin - start + 16], dilation)
+            past = jnp.concatenate([past[: begin - start], cut, past[begin - start + 16 :]]).astype(jnp.bfloat16)
+            earlier[start:] = past
+        preact = dot(jnp.concatenate([present[start:], past], axis=1), conv_w[index], NN)
         filtered = jnp.tanh(preact[:, :channels])
         opening = 0.5 + 0.5 * jnp.tanh(0.5 * preact[:, channels:])
         product = filtered * opening
-        gate[start:] = product.astype(jnp.bfloat16)
-        factor[start:, :channels] = opening - filtered * product
-        factor[start:, channels:] = product * (1.0 - opening)
+        gated = product.astype(jnp.bfloat16)
+        gate[start:] = gated
+        factor[start:, :channels] = (opening - filtered * product).astype(jnp.bfloat16)
+        factor[start:, channels:] = (product * (1.0 - opening)).astype(jnp.bfloat16)
         if index < layers - 1:
-            stream[pad + start :] += dot(gate[start:], out_w[index, :, :channels], NN)
+            after = stream[pad + start :] + dot(gated, out_w[index, :, :channels], NN)
+            refs_of(index + 1)[0][start:] = after.astype(jnp.bfloat16)
+            if index < layers - 2:
+                stream[pad + start :] = after
 
     grad_stream[0:halo] = prev_rows[2 * halo : 3 * halo].astype(jnp.float32)
     grad_stream[halo:] = own_grad[...]
@@ -218,37 +234,36 @@
     grad_skip[halo:] = own_skip[...]
     grad_proj[:, channels:] = grad_skip[...]
     backward(
-        plan, list(reversed(range(low, layers))), refs_of, conv_w, out_w,
-        grad_proj, grad_stream, past_part, total, grad_parts,
+        plan, list(reversed(range(low, layers))), refs_of, conv_w, out_w, grad_proj, grad_stream, past_part, grad_parts
     )
 
 
 def later_kernel(
-    plan, first, third, low_operands, low_factors, low_gates, grad_before, grad_skip, sums, conv_w, out_w, *rest
+    plan, first, third, present, earlier, factors, gates, grad_before, grad_skip, sums, conv_w, out_w, *rest
 ):
-    *outs, keep, send, grad_stream, grad_proj, past_part, total = rest[plan["unused"] :]
+    *outs, keep, send, grad_stream, grad_proj, past_part = rest[plan["unused"] :]
     channels = plan["channels"]
     grad_stream[...] = grad_before[...]
     grad_proj[:, channels:] = grad_skip[...]
 
     def refs_of(index):
-        return low_operands.at[index], low_factors.at[index], low_gates.at[index]
+        return present.at[index], earlier.at[index], factors.at[index], gates.at[index]
 
     backward(
         plan, list(reversed(range(first, first + third))), refs_of, conv_w, out_w,
-        grad_proj, grad_stream, past_part, total, (keep, send),
+        grad_proj, grad_stream, past_part, (keep, send),
     )
     at = 0
     for out in outs:
-        out[...] = grad_stream[at : at + out.shape[0]]
+        out[...] = grad_stream[at : at + out.shape[0]].astype(out.dtype)
         at += out.shape[0]
     plan["finish"](sums, (keep, send))
 
 
-def store_whole(items, total, height, item, grad_parts):
+def store_whole(items, total, item, grad_parts):
     is_out = items[item][1]
     place = sum(kind == is_out for _, kind in items[:item])
-    grad_parts[int(is_out)][place] = total[0:height].astype(jnp.bfloat16)
+    grad_parts[int(is_out)][place] = total.astype(jnp.bfloat16)
 
 
 def finish_whole(sums, grad_parts):
@@ -264,16 +279,16 @@
             )
 
 
-def store_shards(tm, dp, order, bases, total, height, item, grad_parts):
+def store_shards(tm, dp, order, bases, total, item, grad_parts):
     keep, send = grad_parts
     t_at, d_at = lax.axis_index("tm"), lax.axis_index("dp")
     core_at = lax.rem(d_at, 2)
-    rows = height // tm
+    rows = total.shape[0] // tm
     at = pl.ds(bases[item], rows)
     at_bits = bits_of(t_at, d_at, lax.rem, lax.div)
     for y in range(dp // 2):
-        near = total[0:height, (2 * y) * LANES : (2 * y + 1) * LANES]
-        far = total[0:height, (2 * y + 1) * LANES : (2 * y + 2) * LANES]
+        near = total[:, (2 * y) * LANES : (2 * y + 1) * LANES]
+        far = total[:, (2 * y + 1) * LANES : (2 * y + 2) * LANES]
         mine = jnp.where(core_at == 0, near, far).astype(jnp.bfloat16)
         other = jnp.where(core_at == 0, far, near).astype(jnp.bfloat16)
         for t in range(tm):
@@ -326,10 +341,11 @@
     *kept, grad_stream, grad_skip, keep, send = pl.pallas_call(
         functools.partial(first_kernel, plans[0]),
         in_specs=[vmem] * 6,
-        out_specs=[vmem] * 7,
+        out_specs=[vmem] * 8,
         out_shape=[
+            pltpu.VMEM((low, extent, channels), jnp.bfloat16),
+            pltpu.VMEM((low, extent, channels), jnp.bfloat16),
             pltpu.VMEM((low, extent, 2 * channels), jnp.bfloat16),
-            pltpu.VMEM((low, extent, 2 * channels), jnp.float32),
             pltpu.VMEM((low, extent, channels), jnp.bfloat16),
             pltpu.VMEM((border, channels), jnp.float32),
             pltpu.VMEM((border, channels), jnp.bfloat16),
@@ -337,12 +353,11 @@
         + [pltpu.VMEM(shape, jnp.bfloat16) for shape in shapes[0]],
         scratch_shapes=[
             pltpu.VMEM((2 ** (layers - 1) + extent, channels), jnp.float32),
+            pltpu.VMEM((third, extent, channels), jnp.bfloat16),
             pltpu.VMEM((third, extent, 2 * channels), jnp.bfloat16),
-            pltpu.VMEM((third, extent, 2 * channels), jnp.float32),
             pltpu.VMEM((third, extent, channels), jnp.bfloat16),
             pltpu.VMEM((border, 2 * channels), jnp.bfloat16),
             pltpu.VMEM((border, channels), jnp.float32),
-            pltpu.VMEM((2 * channels, 2 * channels), jnp.float32),
         ],
         compiler_params=pltpu.CompilerParams(vmem_limit_bytes=VMEM_BYTES),
         cost_estimate=cost(flops * (5 * layers + 12 * third), weight_bytes),
@@ -352,15 +367,14 @@
     def later(step, outs, after):
         return pl.pallas_call(
             functools.partial(later_kernel, plans[step] | {"unused": len(after)}, layers - (step + 1) * third, third),
-            in_specs=[vmem] * 8 + [anywhere] * len(after),
+            in_specs=[vmem] * 9 + [anywhere] * len(after),
             out_specs=[vmem] * (len(outs) + 2),
-            out_shape=[pltpu.VMEM((rows, channels), jnp.float32) for rows in outs]
+            out_shape=[pltpu.VMEM((rows, channels), kind) for rows, kind in outs]
             + [pltpu.VMEM(shape, jnp.bfloat16) for shape in shapes[step]],
             scratch_shapes=[
                 pltpu.VMEM((border, channels), jnp.float32),
                 pltpu.VMEM((border, 2 * channels), jnp.bfloat16),
                 pltpu.VMEM((border, channels), jnp.float32),
-                pltpu.VMEM((2 * channels, 2 * channels), jnp.float32),
             ],
             compiler_params=pltpu.CompilerParams(vmem_limit_bytes=VMEM_BYTES),
             cost_estimate=cost(flops * 12 * third, weight_bytes),
@@ -370,8 +384,10 @@
     parts = [(keep, send)]
     if in_shards:
         parts[0] = Chunk(tm, dp, 0, keep, send)
-    grad_stream, *middle = later(1, [border], [])
-    other, own, *last = later(2, [halo, length - halo], [parts[0].next_message()] if in_shards else [])
+    grad_stream, *middle = later(1, [(border, jnp.float32)], [])
+    other, own, *last = later(
+        2, [(halo, jnp.bfloat16), (length - halo, jnp.float32)], [parts[0].next_message()] if in_shards else []
+    )
     parts += [middle, last]
     if in_shards:
         for step in (1, 2):
@@ -440,7 +456,7 @@
     for first in range(0, channels, LANES):
         lanes = slice(first, first + LANES)
         grad_inputs[0 : own.shape[0], lanes] = own[:, lanes] * scale
-        grad_inputs[own.shape[0] :, lanes] = other[:, lanes] * scale
+        grad_inputs[own.shape[0] :, lanes] = other[:, lanes].astype(jnp.float32) * scale
 
 
 class Chunk:
@@ -463,7 +479,7 @@
 
     def run_chain(self, after=()):
         for step, name in enumerate(CHAINS[self.chunk]):
-            self.terms.append(swapped(self.tm, self.dp, self.next_message(after if step == 2 else ()), name))
+            self.terms.append(swapped(self.tm, self.dp, self.next_message(after if step == 1 else ()), name))
             self.message = None
         return self.terms
 

time: 58.1 us -> 56.5 us (0.972)
  waiting for transfers between devices: 23.4 us -> 22.2 us
    ppermute x15, waiting for transfers between devices: 15.9 us -> 10.2 us  [swapped(): return lax.ppermute(value, ('tm', 'dp'), pairs)]
    ppermute x2, waiting for transfers between devices: 7.5 us -> 12 us  [around(): return lax.ppermute(x, axis, [(i, (i + by) % count) for i in range(count)])]
  transfers between devices with their start and end apart: 17 -> 17, of which waited for: 7 -> 8; matrix products, arithmetic and copies ran while one was open for 0% -> 0% of each run, Pallas kernels for 13% -> 14%
where the time goes in v9:
time: 56.5 us; the launch traced here: 56.4 us
  waiting for transfers between devices  22.2 us (39%)
  starting transfers between devices  18.3 us (32%)
  Pallas kernels  15.1 us (27%)
  between operations  0.76 us (1%)
    ppermute x15, starting transfers between devices, swapped(): return lax.ppermute(value, ('tm', 'dp'), pairs)  12.2 us
    ppermute x2, waiting for transfers between devices, around(): return lax.ppermute(x, axis, [(i, (i + by) % count) for i in range(count)])  12 us
    ppermute x15, waiting for transfers between devices, swapped(): return lax.ppermute(value, ('tm', 'dp'), pairs)  10.2 us
    ppermute x2, starting transfers between devices, around(): return lax.ppermute(x, axis, [(i, (i + by) % count) for i in range(count)])  6.17 us
    pallas_call x1, Pallas kernels, run_layers(): pl.pallas_call(functools.partial(first_kernel, plans[0]), in_specs=[vmem]...  5.48 us
    pallas_call x2, Pallas kernels, later(): pl.pallas_call(functools.partial(later_kernel, plans[step] | {'unused': l...  4.14 us
    pallas_call x1, Pallas kernels, load_all(): pl.pallas_call(load_kernel, in_specs=[anywhere] * 7, out_specs=[vmem] * 6...  2.67 us
  transfers between devices with their start and end apart: 17, of which 8 were waited for; matrix products, arithmetic and copies ran while one was open for 0% of the time, Pallas kernels for 14%

profile of v9, /device:TPU:0, one launch (start us, length us, event | category | flops | bytes accessed | tf_op | source)
XLA Modules:
  0.0 56.4 jit_solution(7721427923430255807)
XLA Ops:
  0.6 1.0 %pack_borders.1._ = bf16[256,256]{1,0:T(8,128)(2,1)S(1)} custom-call(bf16[512,256]{1,0:T(8,128)(2,1)} %bitcast.4, bf16[512,256]{1,0:T(8,128)(2,1)} %bitcast.6, bf16[512,256]{1,0:T(8,128)(2,1)} %bitcast.8, f32[1,512]{1,0:T(1,128)} %weight.3), custom_call_target="tpu_custom_call" | custom-call | tf_op jit(solution)/shard_map/pack_borders/pallas_call | solution.py:56
  1.6 3.0 %collective-permute-start = (bf16[256,256]{1,0:T(8,128)(2,1)S(1)}, bf16[256,256]{1,0:T(8,128)(2,1)S(1)}, u32[]{:S(2)}, u32[]{:S(2)}) collective-permute-start(bf16[256,256]{1,0:T(8,128)(2,1)S(1)} %pack_borders.1._), channel_id=1, source_target_pairs={{0,4},{4,8},{8,12},{12,16},{16,20},{20,24},{24,28},{28,0},{1,5},{5... | collective-permute-start | bytes 393224 | tf_op jit(solution)/shard_map/ppermute | solution.py:30
  4.6 2.7 %load_all.1 = (bf16[512,256]{1,0:T(8,128)(2,1)S(1)}, f32[512,256]{1,0:T(8,128)S(1)}, bf16[512,256]{1,0:T(8,128)(2,1)S(1)}, bf16[16,128]{1,0:T(8,128)(2,1)S(1)}, ...) custom-call(bf16[512,256]{1,0:T(8,128)(2,1)} %bitcast.5, bf16[512,256]{1,0:T(8,128)(2,1)} %bitcast.7, ...), custom_call_target="tpu_custom_call" | custom-call | flops 10000000 | bytes 6000000 | tf_op jit(solution)/shard_map/load_all/pallas_call | solution.py:91
  7.3 3.9 %collective-permute-done.prev_rows = bf16[256,256]{1,0:T(8,128)(2,1)S(1)} collective-permute-done((bf16[256,256]{1,0:T(8,128)(2,1)S(1)}, bf16[256,256]{1,0:T(8,128)(2,1)S(1)}, u32[]{:S(2)}, u32[]{:S(2)}) %collective-permute-start) | collective-permute-done | bytes 131104 | tf_op jit(solution)/shard_map/ppermute | solution.py:30
  11.1 5.5 %forward_and_last_third.1 = (bf16[4,640,256]{2,1,0:T(8,128)(2,1)S(1)}, bf16[4,640,256]{2,1,0:T(8,128)(2,1)S(1)}, bf16[4,640,512]{2,1,0:T(8,128)(2,1)S(1)}, bf16[...) custom-call(bf16[256,256]{1,0:T(8,128)(2,1)S(1)} %collective-permute, ...), custom_call_target="tpu_custom_call" | custom-call | flops 3623878656 | bytes 4718592 | tf_op jit(solution)/shard_map/forward_and_last_third/pallas_call | solution.py:341
  16.6 0.1 collective-permute-start.1
  16.7 2.1 %middle_third.1 = (f32[576,256]{1,0:T(8,128)S(1)}, bf16[2,2,2,2,192,128]{5,4,3,2,1,0:T(8,128)(2,1)S(1)}, bf16[2,2,2,2,192,128]{5,4,3,2,1,0:T(8,128)(2,1)S(1)}) custom-call(bf16[4,640,256]{2,1,0:T(8,128)(2,1)S(1)} %get-tuple-element.34.present, bf16[4,640,256]{2,1,0:T(8,128)(2,1)S(1)} %get-tuple-element.35.earlier, ...), custom_call_target="tpu_custom_call" | custom-call | flops 1610612736 | bytes 4718592 | tf_op jit(solution)/shard_map/middle_third/pallas_call | solution.py:368
  18.8 0.6 collective-permute-start.7
  19.4 0.0 collective-permute-done.1.refs_1_
  19.4 0.1 add_chunk0_step1.1.rest_0_
  19.5 2.0 %first_third.1 = (bf16[64,256]{1,0:T(8,128)(2,1)S(1)}, f32[448,256]{1,0:T(8,128)S(1)}, bf16[2,2,2,2,176,128]{5,4,3,2,1,0:T(8,128)(2,1)S(1)}, bf16[2,2,2,2,176,128]{5,4,3,2,1,0:T(8,128)(2,1)S(1)}) custom-call(bf16[4,640,256]{2,1,0:T(8,128)(2,1)S(1)} %get-tuple-element.34.present, bf16[4,640,256]{2,1,0:T(8,128)(2,1)S(1)} %get-tuple-element.35.earlier, ...), custom_call_target="tpu_custom_call" | custom-call | flops 1610612736 | bytes 4718592 | tf_op jit(solution)/shard_map/first_third/pallas_call | solution.py:368
  21.5 0.1 collective-permute-start.12
  21.6 1.6 %collective-permute-start.2 = (bf16[2,2,2,224,128]{4,3,2,1,0:T(8,128)(2,1)S(1)}, bf16[2,2,2,224,128]{4,3,2,1,0:T(8,128)(2,1)S(1)}, u32[]{:S(2)}, u32[]{:S(2)}) collective-permute-start(bf16[2,2,2,224,128]{4,3,2,1,0:T(8,128)(2,1)S(1)} %add_chunk0_step1.1.rest_0_), channel_id=1, source_target_pairs={{0,2},{1,3},{2,0},{3,1},{4,6},{5,7},{6,4},{7,5},{8,10},{9,11},{10,... | collective-permute-start | bytes 1376264 | tf_op jit(solution)/shard_map/ppermute | solution.py:490
  23.2 0.0 collective-permute-done.7.refs_1_.refs_7_
  23.2 0.1 add_chunk1_step1.1
  23.3 0.1 collective-permute-start.8
  23.4 0.4 collective-permute-done.12.refs_1_.refs_13_
  23.8 0.1 add_chunk2_step1.1
  23.9 0.1 collective-permute-start.13
  24.0 3.2 %collective-permute-start.3 = (bf16[64,256]{1,0:T(8,128)(2,1)S(1)}, bf16[64,256]{1,0:T(8,128)(2,1)S(1)}, u32[]{:S(2)}, u32[]{:S(2)}) collective-permute-start(bf16[64,256]{1,0:T(8,128)(2,1)S(1)} %get-tuple-element.42), channel_id=1, source_target_pairs={{0,28},{4,0},{8,4},{12,8},{16,12},{20,16},{24,20},{28,24},{1,29},{... | collective-permute-start | bytes 98312 | tf_op jit(solution)/shard_map/ppermute | solution.py:30
  27.1 8.1 %collective-permute-done.3.refs_3_.refs_18_ = bf16[64,256]{1,0:T(8,128)(2,1)S(1)} collective-permute-done((bf16[64,256]{1,0:T(8,128)(2,1)S(1)}, bf16[64,256]{1,0:T(8,128)(2,1)S(1)}, u32[]{:S(2)}, u32[]{:S(2)}) %collective-permute-start.3) | collective-permute-done | bytes 32800 | tf_op jit(solution)/shard_map/ppermute | solution.py:30
  35.3 0.0 collective-permute-done.2.refs_2_
  35.3 0.1 add_chunk0_step2.1
  35.3 1.4 %collective-permute-start.4 = (bf16[2,2,224,128]{3,2,1,0:T(8,128)(2,1)S(1)}, bf16[2,2,224,128]{3,2,1,0:T(8,128)(2,1)S(1)}, u32[]{:S(2)}, u32[]{:S(2)}) collective-permute-start(bf16[2,2,224,128]{3,2,1,0:T(8,128)(2,1)S(1)} %add_chunk0_step2.1), channel_id=1, source_target_pairs={{0,4},{1,5},{2,6},{3,7},{4,0},{5,1},{6,2},{7,3},{8,12},{9,13},{10,... | collective-permute-start | bytes 688136 | tf_op jit(solution)/shard_map/ppermute | solution.py:490
  36.7 0.0 collective-permute-done.8.refs_2_.refs_8_
  36.7 0.1 add_chunk1_step2.1
  36.8 0.1 collective-permute-start.9
  36.9 0.0 collective-permute-done.13.refs_2_.refs_14_
  36.9 0.1 add_chunk2_step2.1
  37.0 1.6 %collective-permute-start.14 = (bf16[2,2,176,128]{3,2,1,0:T(8,128)(2,1)S(1)}, bf16[2,2,176,128]{3,2,1,0:T(8,128)(2,1)S(1)}, u32[]{:S(2)}, u32[]{:S(2)}) collective-permute-start(bf16[2,2,176,128]{3,2,1,0:T(8,128)(2,1)S(1)} %add_chunk2_step2.1), channel_id=1, source_target_pairs={{0,2},{1,3},{2,0},{3,1},{4,6},{5,7},{6,4},{7,5},{8,10},{9,11},{10,... | collective-permute-start | bytes 540680 | tf_op jit(solution)/shard_map/ppermute | solution.py:490
  38.6 3.7 %collective-permute-done.4.refs_3_ = bf16[2,2,224,128]{3,2,1,0:T(8,128)(2,1)S(1)} collective-permute-done((bf16[2,2,224,128]{3,2,1,0:T(8,128)(2,1)S(1)}, bf16[2,2,224,128]{3,2,1,0:T(8,128)(2,1)S(1)}, u32[]{:S(2)}, u32[]{:S(2)}) %collective-permute-start.4) | collective-permute-done | bytes 229408 | tf_op jit(solution)/shard_map/ppermute | solution.py:490
  42.3 0.1 add_chunk0_step3.1
  42.3 0.1 collective-permute-start.5
  42.4 0.1 collective-permute-done.9.refs_3_.refs_9_
  42.5 0.1 add_chunk1_step3.1
  42.6 1.6 %collective-permute-start.10 = (bf16[2,192,128]{2,1,0:T(8,128)(2,1)S(1)}, bf16[2,192,128]{2,1,0:T(8,128)(2,1)S(1)}, u32[]{:S(2)}, u32[]{:S(2)}) collective-permute-start(bf16[2,192,128]{2,1,0:T(8,128)(2,1)S(1)} %add_chunk1_step3.1), channel_id=1, source_target_pairs={{0,2},{1,3},{2,0},{3,1},{4,6},{5,7},{6,4},{7,5},{8,10},{9,11},{10,... | collective-permute-start | bytes 294920 | tf_op jit(solution)/shard_map/ppermute | solution.py:490
  44.2 0.0 collective-permute-done.14.refs_3_.refs_15_
  44.2 0.1 add_chunk2_step3.1
  44.3 0.9 %collective-permute-start.15 = (bf16[2,176,128]{2,1,0:T(8,128)(2,1)S(1)}, bf16[2,176,128]{2,1,0:T(8,128)(2,1)S(1)}, u32[]{:S(2)}, u32[]{:S(2)}) collective-permute-start(bf16[2,176,128]{2,1,0:T(8,128)(2,1)S(1)} %add_chunk2_step3.1), channel_id=1, source_target_pairs={{0,4},{1,5},{2,6},{3,7},{4,0},{5,1},{6,2},{7,3},{8,12},{9,13},{10,... | collective-permute-start | bytes 270344 | tf_op jit(solution)/shard_map/ppermute | solution.py:490
  45.2 2.0 %collective-permute-done.5.refs_4_ = bf16[2,224,128]{2,1,0:T(8,128)(2,1)S(1)} collective-permute-done((bf16[2,224,128]{2,1,0:T(8,128)(2,1)S(1)}, bf16[2,224,128]{2,1,0:T(8,128)(2,1)S(1)}, u32[]{:S(2)}, u32[]{:S(2)}) %collective-permute-start.5) | collective-permute-done | bytes 114720 | tf_op jit(solution)/shard_map/ppermute | solution.py:490
  47.2 1.0 %collective-permute-start.6 = (bf16[224,128]{1,0:T(8,128)(2,1)S(1)}, bf16[224,128]{1,0:T(8,128)(2,1)S(1)}, u32[]{:S(2)}, u32[]{:S(2)}) collective-permute-start(bf16[224,128]{1,0:T(8,128)(2,1)S(1)} %add_chunk0_step4.1), channel_id=1, source_target_pairs={{0,16},{1,17},{2,18},{3,19},{4,20},{5,21},{6,22},{7,23},{8,24},{9,... | collective-permute-start | bytes 172040 | tf_op jit(solution)/shard_map/ppermute | solution.py:490
  48.2 0.0 collective-permute-done.10.refs_4_.refs_10_
  48.3 2.0 %collective-permute-start.11 = (bf16[192,128]{1,0:T(8,128)(2,1)S(1)}, bf16[192,128]{1,0:T(8,128)(2,1)S(1)}, u32[]{:S(2)}, u32[]{:S(2)}) collective-permute-start(bf16[192,128]{1,0:T(8,128)(2,1)S(1)} %add_chunk1_step4.1), channel_id=1, source_target_pairs={{0,16},{1,17},{2,18},{3,19},{4,20},{5,21},{6,22},{7,23},{8,24},{9,... | collective-permute-start | bytes 147464 | tf_op jit(solution)/shard_map/ppermute | solution.py:490
  50.3 0.0 collective-permute-done.15.refs_4_.refs_16_
  50.4 1.0 %collective-permute-start.16 = (bf16[176,128]{1,0:T(8,128)(2,1)S(1)}, bf16[176,128]{1,0:T(8,128)(2,1)S(1)}, u32[]{:S(2)}, u32[]{:S(2)}) collective-permute-start(bf16[176,128]{1,0:T(8,128)(2,1)S(1)} %add_chunk2_step4.1), channel_id=1, source_target_pairs={{0,16},{1,17},{2,18},{3,19},{4,20},{5,21},{6,22},{7,23},{8,24},{9,... | collective-permute-start | bytes 135176 | tf_op jit(solution)/shard_map/ppermute | solution.py:490
  51.4 1.9 %collective-permute-done.11.refs_11_ = bf16[192,128]{1,0:T(8,128)(2,1)S(1)} collective-permute-done((bf16[192,128]{1,0:T(8,128)(2,1)S(1)}, bf16[192,128]{1,0:T(8,128)(2,1)S(1)}, u32[]{:S(2)}, u32[]{:S(2)}) %collective-permute-start.11) | collective-permute-done | bytes 49184 | tf_op jit(solution)/shard_map/ppermute | solution.py:490
  53.3 0.0 collective-permute-done.6.refs_5_
  53.3 2.0 %collective-permute-done.16.refs_17_ = bf16[176,128]{1,0:T(8,128)(2,1)S(1)} collective-permute-done((bf16[176,128]{1,0:T(8,128)(2,1)S(1)}, bf16[176,128]{1,0:T(8,128)(2,1)S(1)}, u32[]{:S(2)}, u32[]{:S(2)}) %collective-permute-start.16) | collective-permute-done | bytes 45088 | tf_op jit(solution)/shard_map/ppermute | solution.py:490
  55.4 1.0 %scale_all.1 = (f32[512,256]{1,0:T(8,128)}, f32[6,64,128]{2,1,0:T(8,128)}, f32[6,32,128]{2,1,0:T(8,128)}) custom-call(bf16[2,2,2,2,224,128]{5,4,3,2,1,0:T(8,128)(2,1)S(1)} %get-tuple-element.32.refs_0_, bf16[2,2,2,2,224,128]{5,4,3,2,1,0:T(8,128)(2,1)S(1)} %collective-permute-done.1.refs_1_, bf16[2,2,2,224,128]{4,3,2,1,0:T(8,128)(2,1)S(1)} %collective-permute-done.2.refs_2_, ...), custom_call_target="tpu_custom_call" | custom-call | tf_op jit(solution)/shard_map/scale_all/pallas_call | solution.py:526
  (3 shorter events, 0.1 us)
Async XLA Ops:
  1.6 9.5 %collective-permute-start = (bf16[256,256]{1,0:T(8,128)(2,1)S(1)}, bf16[256,256]{1,0:T(8,128)(2,1)S(1)}, u32[]{:S(2)}, u32[]{:S(2)}) collective-permute-start(bf16[256,256]{1,0:T(8,128)(2,1)S(1)} %pack_borders.1._), channel_id=1, source_target_pairs={{0,4},{4,8},{8,12},{12,16},{16,20},{20,24},{24,28},{28,0},{1,5},{5... | collective-permute-start | bytes 393224 | tf_op jit(solution)/shard_map/ppermute | solution.py:30
  16.6 2.8 %collective-permute-start.1 = (bf16[2,2,2,2,224,128]{5,4,3,2,1,0:T(8,128)(2,1)S(1)}, bf16[2,2,2,2,224,128]{5,4,3,2,1,0:T(8,128)(2,1)S(1)}, u32[]{:S(2)}, u32[]{:S(2)}) collective-permute-start(bf16[2,2,2,2,224,128]{5,4,3,2,1,0:T(8,128)(2,1)S(1)} %get-tuple-element.33), channel_id=1, source_target_pairs={{0,1},{1,0},{2,3},{3,2},{4,5},{5,4},{6,7},{7,6},{8,9},{9,8},{10,11... | collective-permute-start | bytes 2752520 | tf_op jit(solution)/shard_map/ppermute | solution.py:490
  18.8 4.4 %collective-permute-start.7 = (bf16[2,2,2,2,192,128]{5,4,3,2,1,0:T(8,128)(2,1)S(1)}, bf16[2,2,2,2,192,128]{5,4,3,2,1,0:T(8,128)(2,1)S(1)}, u32[]{:S(2)}, u32[]{:S(2)}) collective-permute-start(bf16[2,2,2,2,192,128]{5,4,3,2,1,0:T(8,128)(2,1)S(1)} %get-tuple-element.44), channel_id=1, source_target_pairs={{0,1},{1,0},{2,3},{3,2},{4,5},{5,4},{6,7},{7,6},{8,9},{9,8},{10,11... | collective-permute-start | bytes 2359304 | tf_op jit(solution)/shard_map/ppermute | solution.py:490
  21.5 2.3 %collective-permute-start.12 = (bf16[2,2,2,2,176,128]{5,4,3,2,1,0:T(8,128)(2,1)S(1)}, bf16[2,2,2,2,176,128]{5,4,3,2,1,0:T(8,128)(2,1)S(1)}, u32[]{:S(2)}, u32[]{:S(2)}) collective-permute-start(bf16[2,2,2,2,176,128]{5,4,3,2,1,0:T(8,128)(2,1)S(1)} %get-tuple-element.46), channel_id=1, source_target_pairs={{0,1},{1,0},{2,3},{3,2},{4,5},{5,4},{6,7},{7,6},{8,9},{9,8},{10,11... | collective-permute-start | bytes 2162696 | tf_op jit(solution)/shard_map/ppermute | solution.py:490
  21.6 13.6 %collective-permute-start.2 = (bf16[2,2,2,224,128]{4,3,2,1,0:T(8,128)(2,1)S(1)}, bf16[2,2,2,224,128]{4,3,2,1,0:T(8,128)(2,1)S(1)}, u32[]{:S(2)}, u32[]{:S(2)}) collective-permute-start(bf16[2,2,2,224,128]{4,3,2,1,0:T(8,128)(2,1)S(1)} %add_chunk0_step1.1.rest_0_), channel_id=1, source_target_pairs={{0,2},{1,3},{2,0},{3,1},{4,6},{5,7},{6,4},{7,5},{8,10},{9,11},{10,... | collective-permute-start | bytes 1376264 | tf_op jit(solution)/shard_map/ppermute | solution.py:490
  23.3 13.4 %collective-permute-start.8 = (bf16[2,2,2,192,128]{4,3,2,1,0:T(8,128)(2,1)S(1)}, bf16[2,2,2,192,128]{4,3,2,1,0:T(8,128)(2,1)S(1)}, u32[]{:S(2)}, u32[]{:S(2)}) collective-permute-start(bf16[2,2,2,192,128]{4,3,2,1,0:T(8,128)(2,1)S(1)} %add_chunk1_step1.1), channel_id=1, source_target_pairs={{0,4},{1,5},{2,6},{3,7},{4,0},{5,1},{6,2},{7,3},{8,12},{9,13},{10,... | collective-permute-start | bytes 1179656 | tf_op jit(solution)/shard_map/ppermute | solution.py:490
  23.9 13.0 %collective-permute-start.13 = (bf16[2,2,2,176,128]{4,3,2,1,0:T(8,128)(2,1)S(1)}, bf16[2,2,2,176,128]{4,3,2,1,0:T(8,128)(2,1)S(1)}, u32[]{:S(2)}, u32[]{:S(2)}) collective-permute-start(bf16[2,2,2,176,128]{4,3,2,1,0:T(8,128)(2,1)S(1)} %add_chunk2_step1.1), channel_id=1, source_target_pairs={{0,8},{1,9},{2,10},{3,11},{4,12},{5,13},{6,14},{7,15},{8,0},{9,1},... | collective-permute-start | bytes 1081352 | tf_op jit(solution)/shard_map/ppermute | solution.py:490
  24.0 11.3 %collective-permute-start.3 = (bf16[64,256]{1,0:T(8,128)(2,1)S(1)}, bf16[64,256]{1,0:T(8,128)(2,1)S(1)}, u32[]{:S(2)}, u32[]{:S(2)}) collective-permute-start(bf16[64,256]{1,0:T(8,128)(2,1)S(1)} %get-tuple-element.42), channel_id=1, source_target_pairs={{0,28},{4,0},{8,4},{12,8},{16,12},{20,16},{24,20},{28,24},{1,29},{... | collective-permute-start | bytes 98312 | tf_op jit(solution)/shard_map/ppermute | solution.py:30
  35.3 6.9 %collective-permute-start.4 = (bf16[2,2,224,128]{3,2,1,0:T(8,128)(2,1)S(1)}, bf16[2,2,224,128]{3,2,1,0:T(8,128)(2,1)S(1)}, u32[]{:S(2)}, u32[]{:S(2)}) collective-permute-start(bf16[2,2,224,128]{3,2,1,0:T(8,128)(2,1)S(1)} %add_chunk0_step2.1), channel_id=1, source_target_pairs={{0,4},{1,5},{2,6},{3,7},{4,0},{5,1},{6,2},{7,3},{8,12},{9,13},{10,... | collective-permute-start | bytes 688136 | tf_op jit(solution)/shard_map/ppermute | solution.py:490
  36.8 5.7 %collective-permute-start.9 = (bf16[2,2,192,128]{3,2,1,0:T(8,128)(2,1)S(1)}, bf16[2,2,192,128]{3,2,1,0:T(8,128)(2,1)S(1)}, u32[]{:S(2)}, u32[]{:S(2)}) collective-permute-start(bf16[2,2,192,128]{3,2,1,0:T(8,128)(2,1)S(1)} %add_chunk1_step2.1), channel_id=1, source_target_pairs={{0,8},{1,9},{2,10},{3,11},{4,12},{5,13},{6,14},{7,15},{8,0},{9,1},... | collective-permute-start | bytes 589832 | tf_op jit(solution)/shard_map/ppermute | solution.py:490
  37.0 7.2 %collective-permute-start.14 = (bf16[2,2,176,128]{3,2,1,0:T(8,128)(2,1)S(1)}, bf16[2,2,176,128]{3,2,1,0:T(8,128)(2,1)S(1)}, u32[]{:S(2)}, u32[]{:S(2)}) collective-permute-start(bf16[2,2,176,128]{3,2,1,0:T(8,128)(2,1)S(1)} %add_chunk2_step2.1), channel_id=1, source_target_pairs={{0,2},{1,3},{2,0},{3,1},{4,6},{5,7},{6,4},{7,5},{8,10},{9,11},{10,... | collective-permute-start | bytes 540680 | tf_op jit(solution)/shard_map/ppermute | solution.py:490
  42.3 4.9 %collective-permute-start.5 = (bf16[2,224,128]{2,1,0:T(8,128)(2,1)S(1)}, bf16[2,224,128]{2,1,0:T(8,128)(2,1)S(1)}, u32[]{:S(2)}, u32[]{:S(2)}) collective-permute-start(bf16[2,224,128]{2,1,0:T(8,128)(2,1)S(1)} %add_chunk0_step3.1), channel_id=1, source_target_pairs={{0,8},{1,9},{2,10},{3,11},{4,12},{5,13},{6,14},{7,15},{8,0},{9,1},... | collective-permute-start | bytes 344072 | tf_op jit(solution)/shard_map/ppermute | solution.py:490
  42.6 5.6 %collective-permute-start.10 = (bf16[2,192,128]{2,1,0:T(8,128)(2,1)S(1)}, bf16[2,192,128]{2,1,0:T(8,128)(2,1)S(1)}, u32[]{:S(2)}, u32[]{:S(2)}) collective-permute-start(bf16[2,192,128]{2,1,0:T(8,128)(2,1)S(1)} %add_chunk1_step3.1), channel_id=1, source_target_pairs={{0,2},{1,3},{2,0},{3,1},{4,6},{5,7},{6,4},{7,5},{8,10},{9,11},{10,... | collective-permute-start | bytes 294920 | tf_op jit(solution)/shard_map/ppermute | solution.py:490
  44.3 6.1 %collective-permute-start.15 = (bf16[2,176,128]{2,1,0:T(8,128)(2,1)S(1)}, bf16[2,176,128]{2,1,0:T(8,128)(2,1)S(1)}, u32[]{:S(2)}, u32[]{:S(2)}) collective-permute-start(bf16[2,176,128]{2,1,0:T(8,128)(2,1)S(1)} %add_chunk2_step3.1), channel_id=1, source_target_pairs={{0,4},{1,5},{2,6},{3,7},{4,0},{5,1},{6,2},{7,3},{8,12},{9,13},{10,... | collective-permute-start | bytes 270344 | tf_op jit(solution)/shard_map/ppermute | solution.py:490
  47.2 6.1 %collective-permute-start.6 = (bf16[224,128]{1,0:T(8,128)(2,1)S(1)}, bf16[224,128]{1,0:T(8,128)(2,1)S(1)}, u32[]{:S(2)}, u32[]{:S(2)}) collective-permute-start(bf16[224,128]{1,0:T(8,128)(2,1)S(1)} %add_chunk0_step4.1), channel_id=1, source_target_pairs={{0,16},{1,17},{2,18},{3,19},{4,20},{5,21},{6,22},{7,23},{8,24},{9,... | collective-permute-start | bytes 172040 | tf_op jit(solution)/shard_map/ppermute | solution.py:490
  48.3 5.1 %collective-permute-start.11 = (bf16[192,128]{1,0:T(8,128)(2,1)S(1)}, bf16[192,128]{1,0:T(8,128)(2,1)S(1)}, u32[]{:S(2)}, u32[]{:S(2)}) collective-permute-start(bf16[192,128]{1,0:T(8,128)(2,1)S(1)} %add_chunk1_step4.1), channel_id=1, source_target_pairs={{0,16},{1,17},{2,18},{3,19},{4,20},{5,21},{6,22},{7,23},{8,24},{9,... | collective-permute-start | bytes 147464 | tf_op jit(solution)/shard_map/ppermute | solution.py:490
  50.4 5.0 %collective-permute-start.16 = (bf16[176,128]{1,0:T(8,128)(2,1)S(1)}, bf16[176,128]{1,0:T(8,128)(2,1)S(1)}, u32[]{:S(2)}, u32[]{:S(2)}) collective-permute-start(bf16[176,128]{1,0:T(8,128)(2,1)S(1)} %add_chunk2_step4.1), channel_id=1, source_target_pairs={{0,16},{1,17},{2,18},{3,19},{4,20},{5,21},{6,22},{7,23},{8,24},{9,... | collective-permute-start | bytes 135176 | tf_op jit(solution)/shard_map/ppermute | solution.py:490

commit v10 on v9

--- a/solution.py
+++ b/solution.py
@@ -243,6 +243,8 @@
 ):
     *outs, keep, send, grad_stream, grad_proj, past_part = rest[plan["unused"] :]
     channels = plan["channels"]
+    halves = outs[plan["outs"] :]
+    outs = outs[: plan["outs"]]
     grad_stream[...] = grad_before[...]
     grad_proj[:, channels:] = grad_skip[...]
 
@@ -258,6 +260,8 @@
         out[...] = grad_stream[at : at + out.shape[0]].astype(out.dtype)
         at += out.shape[0]
     plan["finish"](sums, (keep, send))
+    for i, half in enumerate(halves):
+        half[...] = send[i]
 
 
 def store_whole(items, total, item, grad_parts):
@@ -365,13 +369,18 @@
     )(*held((prev_rows, own_x, own_grad, own_skip, conv_w, out_w)))
 
     def later(step, outs, after):
+        more = {"unused": len(after), "outs": len(outs)}
+        split = in_shards and step == len(CHAINS) - 1
+        keep, send = (pltpu.VMEM(shape, jnp.bfloat16) for shape in shapes[step])
+        halves = [pltpu.VMEM(shapes[step][1][1:], jnp.bfloat16)] * 2
         return pl.pallas_call(
-            functools.partial(later_kernel, plans[step] | {"unused": len(after)}, layers - (step + 1) * third, third),
+            functools.partial(later_kernel, plans[step] | more, layers - (step + 1) * third, third),
             in_specs=[vmem] * 9 + [anywhere] * len(after),
-            out_specs=[vmem] * (len(outs) + 2),
+            out_specs=[vmem] * (len(outs) + (3 if split else 2)),
             out_shape=[pltpu.VMEM((rows, channels), kind) for rows, kind in outs]
-            + [pltpu.VMEM(shape, jnp.bfloat16) for shape in shapes[step]],
-            scratch_shapes=[
+            + (halves + [keep] if split else [keep, send]),
+            scratch_shapes=([send] if split else [])
+            + [
                 pltpu.VMEM((border, channels), jnp.float32),
                 pltpu.VMEM((border, 2 * channels), jnp.bfloat16),
                 pltpu.VMEM((border, channels), jnp.float32),
@@ -383,15 +392,15 @@
 
     parts = [(keep, send)]
     if in_shards:
-        parts[0] = Chunk(tm, dp, 0, keep, send)
+        parts[0] = Chunk(tm, dp, 0, keep, [send])
     grad_stream, *middle = later(1, [(border, jnp.float32)], [])
     other, own, *last = later(
         2, [(halo, jnp.bfloat16), (length - halo, jnp.float32)], [parts[0].next_message()] if in_shards else []
     )
     parts += [middle, last]
     if in_shards:
-        for step in (1, 2):
-            parts[step] = Chunk(tm, dp, step, *parts[step])
+        parts[1] = Chunk(tm, dp, 1, middle[0], middle[1:])
+        parts[2] = Chunk(tm, dp, 2, last[-1], last[:-1])
     return other, own, parts
 
 
@@ -460,19 +469,23 @@
 
 
 class Chunk:
-    def __init__(self, tm, dp, chunk, keep, send):
+    def __init__(self, tm, dp, chunk, keep, sends):
         self.tm, self.dp, self.chunk, self.rows = tm, dp, chunk, keep.shape[-2]
         self.message = None
-        self.terms = [keep, swapped(tm, dp, send, "core")]
+        there = [swapped(tm, dp, send, "core") for send in reversed(sends)]
+        self.terms = [keep, there[-1]]
+        self.first_terms = [keep, there[0]]
 
     def next_message(self, after=()):
         if self.message is None:
             left = len(CHAINS[self.chunk]) + 2 - len(self.terms)
+            terms = self.first_terms if len(self.terms) == 2 else self.terms
             pieces = []
-            for i, v in enumerate(self.terms):
-                pieces.append((i, (0,) * (len(v.shape) - 2 - left) + (1,), 0))
+            for i, v in enumerate(terms):
+                more = len(v.shape) - 2 - left
+                pieces.append((i, () if more < 0 else (0,) * more + (1,), 0))
             (self.message,) = add_up(
-                self.terms, [[(0, self.rows, EXTRA[self.chunk] > 0, pieces)]], [(2,) * (left - 1) + (self.rows, LANES)], after,
+                terms, [[(0, self.rows, EXTRA[self.chunk] > 0, pieces)]], [(2,) * (left - 1) + (self.rows, LANES)], after,
                 "add_chunk%d_step%d" % (self.chunk, len(self.terms) - 1),
             )
         return self.message

time: 56.5 us -> 56.9 us (level)
  waiting for transfers between devices: 22.2 us -> 23.2 us
  starting transfers between devices: 18.3 us -> 17.7 us
    ppermute x15 -> x16, waiting for transfers between devices: 10.2 us -> 11.2 us  [swapped(): return lax.ppermute(value, ('tm', 'dp'), pairs)]
    ppermute x15 -> x16, starting transfers between devices: 12.2 us -> 11.4 us  [swapped(): return lax.ppermute(value, ('tm', 'dp'), pairs)]
  transfers between devices with their start and end apart: 17 -> 18, of which waited for: 8 -> 7; matrix products, arithmetic and copies ran while one was open for 0% -> 0% of each run, Pallas kernels for 14% -> 14%
where the time goes in v10:
time: 56.9 us; the launch traced here: 56.8 us
  waiting for transfers between devices  23.2 us (41%)
  starting transfers between devices  17.7 us (31%)
  Pallas kernels  15.1 us (27%)
  between operations  0.76 us (1%)
    ppermute x2, waiting for transfers between devices, around(): return lax.ppermute(x, axis, [(i, (i + by) % count) for i in range(count)])  12 us
    ppermute x16, starting transfers between devices, swapped(): return lax.ppermute(value, ('tm', 'dp'), pairs)  11.4 us
    ppermute x16, waiting for transfers between devices, swapped(): return lax.ppermute(value, ('tm', 'dp'), pairs)  11.2 us
    ppermute x2, starting transfers between devices, around(): return lax.ppermute(x, axis, [(i, (i + by) % count) for i in range(count)])  6.33 us
    pallas_call x1, Pallas kernels, run_layers(): pl.pallas_call(functools.partial(first_kernel, plans[0]), in_specs=[vmem]...  5.48 us
    pallas_call x2, Pallas kernels, later(): pl.pallas_call(functools.partial(later_kernel, plans[step] | more, layers...  4.18 us
    pallas_call x1, Pallas kernels, load_all(): pl.pallas_call(load_kernel, in_specs=[anywhere] * 7, out_specs=[vmem] * 6...  2.67 us
  transfers between devices with their start and end apart: 18, of which 7 were waited for; matrix products, arithmetic and copies ran while one was open for 0% of the time, Pallas kernels for 14%

profile of v10, /device:TPU:0, one launch (start us, length us, event | category | flops | bytes accessed | tf_op | source)
XLA Modules:
  0.0 56.8 jit_solution(1362156999442298533)
XLA Ops:
  0.6 1.0 %pack_borders.1._ = bf16[256,256]{1,0:T(8,128)(2,1)S(1)} custom-call(bf16[512,256]{1,0:T(8,128)(2,1)} %bitcast.4, bf16[512,256]{1,0:T(8,128)(2,1)} %bitcast.6, bf16[512,256]{1,0:T(8,128)(2,1)} %bitcast.8, f32[1,512]{1,0:T(1,128)} %weight.3), custom_call_target="tpu_custom_call" | custom-call | tf_op jit(solution)/shard_map/pack_borders/pallas_call | solution.py:56
  1.6 3.0 %collective-permute-start = (bf16[256,256]{1,0:T(8,128)(2,1)S(1)}, bf16[256,256]{1,0:T(8,128)(2,1)S(1)}, u32[]{:S(2)}, u32[]{:S(2)}) collective-permute-start(bf16[256,256]{1,0:T(8,128)(2,1)S(1)} %pack_borders.1._), channel_id=1, source_target_pairs={{0,4},{4,8},{8,12},{12,16},{16,20},{20,24},{24,28},{28,0},{1,5},{5... | collective-permute-start | bytes 393224 | tf_op jit(solution)/shard_map/ppermute | solution.py:30
  4.6 2.7 %load_all.1 = (bf16[512,256]{1,0:T(8,128)(2,1)S(1)}, f32[512,256]{1,0:T(8,128)S(1)}, bf16[512,256]{1,0:T(8,128)(2,1)S(1)}, bf16[16,128]{1,0:T(8,128)(2,1)S(1)}, ...) custom-call(bf16[512,256]{1,0:T(8,128)(2,1)} %bitcast.5, bf16[512,256]{1,0:T(8,128)(2,1)} %bitcast.7, ...), custom_call_target="tpu_custom_call" | custom-call | flops 10000000 | bytes 6000000 | tf_op jit(solution)/shard_map/load_all/pallas_call | solution.py:91
  7.3 3.9 %collective-permute-done.prev_rows = bf16[256,256]{1,0:T(8,128)(2,1)S(1)} collective-permute-done((bf16[256,256]{1,0:T(8,128)(2,1)S(1)}, bf16[256,256]{1,0:T(8,128)(2,1)S(1)}, u32[]{:S(2)}, u32[]{:S(2)}) %collective-permute-start) | collective-permute-done | bytes 131104 | tf_op jit(solution)/shard_map/ppermute | solution.py:30
  11.1 5.5 %forward_and_last_third.1 = (bf16[4,640,256]{2,1,0:T(8,128)(2,1)S(1)}, bf16[4,640,256]{2,1,0:T(8,128)(2,1)S(1)}, bf16[4,640,512]{2,1,0:T(8,128)(2,1)S(1)}, bf16[...) custom-call(bf16[256,256]{1,0:T(8,128)(2,1)S(1)} %collective-permute, ...), custom_call_target="tpu_custom_call" | custom-call | flops 3623878656 | bytes 4718592 | tf_op jit(solution)/shard_map/forward_and_last_third/pallas_call | solution.py:345
  16.6 0.1 collective-permute-start.1
  16.7 2.1 %middle_third.1 = (f32[576,256]{1,0:T(8,128)S(1)}, bf16[2,2,2,2,192,128]{5,4,3,2,1,0:T(8,128)(2,1)S(1)}, bf16[2,2,2,2,192,128]{5,4,3,2,1,0:T(8,128)(2,1)S(1)}) custom-call(bf16[4,640,256]{2,1,0:T(8,128)(2,1)S(1)} %get-tuple-element.35.present, bf16[4,640,256]{2,1,0:T(8,128)(2,1)S(1)} %get-tuple-element.36.earlier, ...), custom_call_target="tpu_custom_call" | custom-call | flops 1610612736 | bytes 4718592 | tf_op jit(solution)/shard_map/middle_third/pallas_call | solution.py:376
  18.8 0.6 collective-permute-start.7
  19.4 0.0 collective-permute-done.1.refs_1_
  19.4 0.1 add_chunk0_step1.1.rest_0_
  19.5 2.1 %first_third.1 = (bf16[64,256]{1,0:T(8,128)(2,1)S(1)}, f32[448,256]{1,0:T(8,128)S(1)}, bf16[2,2,2,176,128]{4,3,2,1,0:T(8,128)(2,1)S(1)}, bf16[2,2,2,176,128]{4,3...) custom-call(bf16[4,640,256]{2,1,0:T(8,128)(2,1)S(1)} %get-tuple-element.35.present, ...), custom_call_target="tpu_custom_call" | custom-call | flops 1610612736 | bytes 4718592 | tf_op jit(solution)/shard_map/first_third/pallas_call | solution.py:376
  21.6 0.1 collective-permute-start.13
  21.7 1.6 %collective-permute-start.2 = (bf16[2,2,2,224,128]{4,3,2,1,0:T(8,128)(2,1)S(1)}, bf16[2,2,2,224,128]{4,3,2,1,0:T(8,128)(2,1)S(1)}, u32[]{:S(2)}, u32[]{:S(2)}) collective-permute-start(bf16[2,2,2,224,128]{4,3,2,1,0:T(8,128)(2,1)S(1)} %add_chunk0_step1.1.rest_0_), channel_id=1, source_target_pairs={{0,2},{1,3},{2,0},{3,1},{4,6},{5,7},{6,4},{7,5},{8,10},{9,11},{10,... | collective-permute-start | bytes 1376264 | tf_op jit(solution)/shard_map/ppermute | solution.py:503
  23.2 0.0 collective-permute-done.7.refs_1_.refs_7_
  23.3 0.1 add_chunk1_step1.1
  23.3 0.1 collective-permute-start.8
  23.4 0.2 collective-permute-start.12
  23.7 0.0 collective-permute-done.13.refs_1_
  23.7 0.1 add_chunk2_step1.1
  23.8 0.1 collective-permute-start.14
  23.9 3.3 %collective-permute-start.3 = (bf16[64,256]{1,0:T(8,128)(2,1)S(1)}, bf16[64,256]{1,0:T(8,128)(2,1)S(1)}, u32[]{:S(2)}, u32[]{:S(2)}) collective-permute-start(bf16[64,256]{1,0:T(8,128)(2,1)S(1)} %get-tuple-element.43), channel_id=1, source_target_pairs={{0,28},{4,0},{8,4},{12,8},{16,12},{20,16},{24,20},{28,24},{1,29},{... | collective-permute-start | bytes 98312 | tf_op jit(solution)/shard_map/ppermute | solution.py:30
  27.2 8.1 %collective-permute-done.3.refs_3_.refs_18_ = bf16[64,256]{1,0:T(8,128)(2,1)S(1)} collective-permute-done((bf16[64,256]{1,0:T(8,128)(2,1)S(1)}, bf16[64,256]{1,0:T(8,128)(2,1)S(1)}, u32[]{:S(2)}, u32[]{:S(2)}) %collective-permute-start.3) | collective-permute-done | bytes 32800 | tf_op jit(solution)/shard_map/ppermute | solution.py:30
  35.3 0.0 collective-permute-done.2.refs_2_
  35.3 0.1 add_chunk0_step2.1
  35.4 1.4 %collective-permute-start.4 = (bf16[2,2,224,128]{3,2,1,0:T(8,128)(2,1)S(1)}, bf16[2,2,224,128]{3,2,1,0:T(8,128)(2,1)S(1)}, u32[]{:S(2)}, u32[]{:S(2)}) collective-permute-start(bf16[2,2,224,128]{3,2,1,0:T(8,128)(2,1)S(1)} %add_chunk0_step2.1), channel_id=1, source_target_pairs={{0,4},{1,5},{2,6},{3,7},{4,0},{5,1},{6,2},{7,3},{8,12},{9,13},{10,... | collective-permute-start | bytes 688136 | tf_op jit(solution)/shard_map/ppermute | solution.py:503
  36.8 0.0 collective-permute-done.8.refs_2_.refs_8_
  36.8 0.1 add_chunk1_step2.1
  36.9 0.1 collective-permute-start.9
  37.0 0.0 collective-permute-done.12.refs_1_.refs_13_
  37.0 0.0 collective-permute-done.14.refs_2_.refs_14_
  37.0 0.1 add_chunk2_step2.1
  37.1 1.0 %collective-permute-start.15 = (bf16[2,2,176,128]{3,2,1,0:T(8,128)(2,1)S(1)}, bf16[2,2,176,128]{3,2,1,0:T(8,128)(2,1)S(1)}, u32[]{:S(2)}, u32[]{:S(2)}) collective-permute-start(bf16[2,2,176,128]{3,2,1,0:T(8,128)(2,1)S(1)} %add_chunk2_step2.1), channel_id=1, source_target_pairs={{0,2},{1,3},{2,0},{3,1},{4,6},{5,7},{6,4},{7,5},{8,10},{9,11},{10,... | collective-permute-start | bytes 540680 | tf_op jit(solution)/shard_map/ppermute | solution.py:503
  38.1 4.2 %collective-permute-done.4.refs_3_ = bf16[2,2,224,128]{3,2,1,0:T(8,128)(2,1)S(1)} collective-permute-done((bf16[2,2,224,128]{3,2,1,0:T(8,128)(2,1)S(1)}, bf16[2,2,224,128]{3,2,1,0:T(8,128)(2,1)S(1)}, u32[]{:S(2)}, u32[]{:S(2)}) %collective-permute-start.4) | collective-permute-done | bytes 229408 | tf_op jit(solution)/shard_map/ppermute | solution.py:503
  42.3 0.1 add_chunk0_step3.1
  42.4 0.1 collective-permute-start.5
  42.5 0.3 collective-permute-done.9.refs_3_.refs_9_
  42.7 0.1 add_chunk1_step3.1
  42.8 0.9 %collective-permute-start.10 = (bf16[2,192,128]{2,1,0:T(8,128)(2,1)S(1)}, bf16[2,192,128]{2,1,0:T(8,128)(2,1)S(1)}, u32[]{:S(2)}, u32[]{:S(2)}) collective-permute-start(bf16[2,192,128]{2,1,0:T(8,128)(2,1)S(1)} %add_chunk1_step3.1), channel_id=1, source_target_pairs={{0,2},{1,3},{2,0},{3,1},{4,6},{5,7},{6,4},{7,5},{8,10},{9,11},{10,... | collective-permute-start | bytes 294920 | tf_op jit(solution)/shard_map/ppermute | solution.py:503
  43.7 0.0 collective-permute-done.15.refs_3_.refs_15_
  43.7 0.1 add_chunk2_step3.1
  43.8 1.1 %collective-permute-start.16 = (bf16[2,176,128]{2,1,0:T(8,128)(2,1)S(1)}, bf16[2,176,128]{2,1,0:T(8,128)(2,1)S(1)}, u32[]{:S(2)}, u32[]{:S(2)}) collective-permute-start(bf16[2,176,128]{2,1,0:T(8,128)(2,1)S(1)} %add_chunk2_step3.1), channel_id=1, source_target_pairs={{0,4},{1,5},{2,6},{3,7},{4,0},{5,1},{6,2},{7,3},{8,12},{9,13},{10,... | collective-permute-start | bytes 270344 | tf_op jit(solution)/shard_map/ppermute | solution.py:503
  44.9 2.3 %collective-permute-done.5.refs_4_ = bf16[2,224,128]{2,1,0:T(8,128)(2,1)S(1)} collective-permute-done((bf16[2,224,128]{2,1,0:T(8,128)(2,1)S(1)}, bf16[2,224,128]{2,1,0:T(8,128)(2,1)S(1)}, u32[]{:S(2)}, u32[]{:S(2)}) %collective-permute-start.5) | collective-permute-done | bytes 114720 | tf_op jit(solution)/shard_map/ppermute | solution.py:503
  47.3 1.0 %collective-permute-start.6 = (bf16[224,128]{1,0:T(8,128)(2,1)S(1)}, bf16[224,128]{1,0:T(8,128)(2,1)S(1)}, u32[]{:S(2)}, u32[]{:S(2)}) collective-permute-start(bf16[224,128]{1,0:T(8,128)(2,1)S(1)} %add_chunk0_step4.1), channel_id=1, source_target_pairs={{0,16},{1,17},{2,18},{3,19},{4,20},{5,21},{6,22},{7,23},{8,24},{9,... | collective-permute-start | bytes 172040 | tf_op jit(solution)/shard_map/ppermute | solution.py:503
  48.2 0.0 collective-permute-done.10.refs_4_.refs_10_
  48.3 2.1 %collective-permute-start.11 = (bf16[192,128]{1,0:T(8,128)(2,1)S(1)}, bf16[192,128]{1,0:T(8,128)(2,1)S(1)}, u32[]{:S(2)}, u32[]{:S(2)}) collective-permute-start(bf16[192,128]{1,0:T(8,128)(2,1)S(1)} %add_chunk1_step4.1), channel_id=1, source_target_pairs={{0,16},{1,17},{2,18},{3,19},{4,20},{5,21},{6,22},{7,23},{8,24},{9,... | collective-permute-start | bytes 147464 | tf_op jit(solution)/shard_map/ppermute | solution.py:503
  50.4 0.0 collective-permute-done.16.refs_4_.refs_16_
  50.4 1.0 %collective-permute-start.17 = (bf16[176,128]{1,0:T(8,128)(2,1)S(1)}, bf16[176,128]{1,0:T(8,128)(2,1)S(1)}, u32[]{:S(2)}, u32[]{:S(2)}) collective-permute-start(bf16[176,128]{1,0:T(8,128)(2,1)S(1)} %add_chunk2_step4.1), channel_id=1, source_target_pairs={{0,16},{1,17},{2,18},{3,19},{4,20},{5,21},{6,22},{7,23},{8,24},{9,... | collective-permute-start | bytes 135176 | tf_op jit(solution)/shard_map/ppermute | solution.py:503
  51.4 2.5 %collective-permute-done.11.refs_11_ = bf16[192,128]{1,0:T(8,128)(2,1)S(1)} collective-permute-done((bf16[192,128]{1,0:T(8,128)(2,1)S(1)}, bf16[192,128]{1,0:T(8,128)(2,1)S(1)}, u32[]{:S(2)}, u32[]{:S(2)}) %collective-permute-start.11) | collective-permute-done | bytes 49184 | tf_op jit(solution)/shard_map/ppermute | solution.py:503
  53.9 0.0 collective-permute-done.6.refs_5_
  53.9 1.9 %collective-permute-done.17.refs_17_ = bf16[176,128]{1,0:T(8,128)(2,1)S(1)} collective-permute-done((bf16[176,128]{1,0:T(8,128)(2,1)S(1)}, bf16[176,128]{1,0:T(8,128)(2,1)S(1)}, u32[]{:S(2)}, u32[]{:S(2)}) %collective-permute-start.17) | collective-permute-done | bytes 45088 | tf_op jit(solution)/shard_map/ppermute | solution.py:503
  55.8 1.0 %scale_all.1 = (f32[512,256]{1,0:T(8,128)}, f32[6,64,128]{2,1,0:T(8,128)}, f32[6,32,128]{2,1,0:T(8,128)}) custom-call(bf16[2,2,2,2,224,128]{5,4,3,2,1,0:T(8,128)(2,1)S(1)} %get-tuple-element.33.refs_0_, bf16[2,2,2,2,224,128]{5,4,3,2,1,0:T(8,128)(2,1)S(1)} %collective-permute-done.1.refs_1_, bf16[2,2,2,224,128]{4,3,2,1,0:T(8,128)(2,1)S(1)} %collective-permute-done.2.refs_2_, ...), custom_call_target="tpu_custom_call" | custom-call | tf_op jit(solution)/shard_map/scale_all/pallas_call | solution.py:539
  (3 shorter events, 0.1 us)
Async XLA Ops:
  1.6 9.5 %collective-permute-start = (bf16[256,256]{1,0:T(8,128)(2,1)S(1)}, bf16[256,256]{1,0:T(8,128)(2,1)S(1)}, u32[]{:S(2)}, u32[]{:S(2)}) collective-permute-start(bf16[256,256]{1,0:T(8,128)(2,1)S(1)} %pack_borders.1._), channel_id=1, source_target_pairs={{0,4},{4,8},{8,12},{12,16},{16,20},{20,24},{24,28},{28,0},{1,5},{5... | collective-permute-start | bytes 393224 | tf_op jit(solution)/shard_map/ppermute | solution.py:30
  16.6 2.8 %collective-permute-start.1 = (bf16[2,2,2,2,224,128]{5,4,3,2,1,0:T(8,128)(2,1)S(1)}, bf16[2,2,2,2,224,128]{5,4,3,2,1,0:T(8,128)(2,1)S(1)}, u32[]{:S(2)}, u32[]{:S(2)}) collective-permute-start(bf16[2,2,2,2,224,128]{5,4,3,2,1,0:T(8,128)(2,1)S(1)} %get-tuple-element.34), channel_id=1, source_target_pairs={{0,1},{1,0},{2,3},{3,2},{4,5},{5,4},{6,7},{7,6},{8,9},{9,8},{10,11... | collective-permute-start | bytes 2752520 | tf_op jit(solution)/shard_map/ppermute | solution.py:503
  18.8 4.4 %collective-permute-start.7 = (bf16[2,2,2,2,192,128]{5,4,3,2,1,0:T(8,128)(2,1)S(1)}, bf16[2,2,2,2,192,128]{5,4,3,2,1,0:T(8,128)(2,1)S(1)}, u32[]{:S(2)}, u32[]{:S(2)}) collective-permute-start(bf16[2,2,2,2,192,128]{5,4,3,2,1,0:T(8,128)(2,1)S(1)} %get-tuple-element.45), channel_id=1, source_target_pairs={{0,1},{1,0},{2,3},{3,2},{4,5},{5,4},{6,7},{7,6},{8,9},{9,8},{10,11... | collective-permute-start | bytes 2359304 | tf_op jit(solution)/shard_map/ppermute | solution.py:503
  21.6 2.1 %collective-permute-start.13 = (bf16[2,2,2,176,128]{4,3,2,1,0:T(8,128)(2,1)S(1)}, bf16[2,2,2,176,128]{4,3,2,1,0:T(8,128)(2,1)S(1)}, u32[]{:S(2)}, u32[]{:S(2)}) collective-permute-start(bf16[2,2,2,176,128]{4,3,2,1,0:T(8,128)(2,1)S(1)} %get-tuple-element.48), channel_id=1, source_target_pairs={{0,1},{1,0},{2,3},{3,2},{4,5},{5,4},{6,7},{7,6},{8,9},{9,8},{10,11... | collective-permute-start | bytes 1081352 | tf_op jit(solution)/shard_map/ppermute | solution.py:503
  21.7 13.6 %collective-permute-start.2 = (bf16[2,2,2,224,128]{4,3,2,1,0:T(8,128)(2,1)S(1)}, bf16[2,2,2,224,128]{4,3,2,1,0:T(8,128)(2,1)S(1)}, u32[]{:S(2)}, u32[]{:S(2)}) collective-permute-start(bf16[2,2,2,224,128]{4,3,2,1,0:T(8,128)(2,1)S(1)} %add_chunk0_step1.1.rest_0_), channel_id=1, source_target_pairs={{0,2},{1,3},{2,0},{3,1},{4,6},{5,7},{6,4},{7,5},{8,10},{9,11},{10,... | collective-permute-start | bytes 1376264 | tf_op jit(solution)/shard_map/ppermute | solution.py:503
  23.3 13.5 %collective-permute-start.8 = (bf16[2,2,2,192,128]{4,3,2,1,0:T(8,128)(2,1)S(1)}, bf16[2,2,2,192,128]{4,3,2,1,0:T(8,128)(2,1)S(1)}, u32[]{:S(2)}, u32[]{:S(2)}) collective-permute-start(bf16[2,2,2,192,128]{4,3,2,1,0:T(8,128)(2,1)S(1)} %add_chunk1_step1.1), channel_id=1, source_target_pairs={{0,4},{1,5},{2,6},{3,7},{4,0},{5,1},{6,2},{7,3},{8,12},{9,13},{10,... | collective-permute-start | bytes 1179656 | tf_op jit(solution)/shard_map/ppermute | solution.py:503
  23.4 13.5 %collective-permute-start.12 = (bf16[2,2,2,176,128]{4,3,2,1,0:T(8,128)(2,1)S(1)}, bf16[2,2,2,176,128]{4,3,2,1,0:T(8,128)(2,1)S(1)}, u32[]{:S(2)}, u32[]{:S(2)}) collective-permute-start(bf16[2,2,2,176,128]{4,3,2,1,0:T(8,128)(2,1)S(1)} %get-tuple-element.47), channel_id=1, source_target_pairs={{0,1},{1,0},{2,3},{3,2},{4,5},{5,4},{6,7},{7,6},{8,9},{9,8},{10,11... | collective-permute-start | bytes 1081352 | tf_op jit(solution)/shard_map/ppermute | solution.py:503
  23.8 13.2 %collective-permute-start.14 = (bf16[2,2,2,176,128]{4,3,2,1,0:T(8,128)(2,1)S(1)}, bf16[2,2,2,176,128]{4,3,2,1,0:T(8,128)(2,1)S(1)}, u32[]{:S(2)}, u32[]{:S(2)}) collective-permute-start(bf16[2,2,2,176,128]{4,3,2,1,0:T(8,128)(2,1)S(1)} %add_chunk2_step1.1), channel_id=1, source_target_pairs={{0,8},{1,9},{2,10},{3,11},{4,12},{5,13},{6,14},{7,15},{8,0},{9,1},... | collective-permute-start | bytes 1081352 | tf_op jit(solution)/shard_map/ppermute | solution.py:503
  23.9 11.4 %collective-permute-start.3 = (bf16[64,256]{1,0:T(8,128)(2,1)S(1)}, bf16[64,256]{1,0:T(8,128)(2,1)S(1)}, u32[]{:S(2)}, u32[]{:S(2)}) collective-permute-start(bf16[64,256]{1,0:T(8,128)(2,1)S(1)} %get-tuple-element.43), channel_id=1, source_target_pairs={{0,28},{4,0},{8,4},{12,8},{16,12},{20,16},{24,20},{28,24},{1,29},{... | collective-permute-start | bytes 98312 | tf_op jit(solution)/shard_map/ppermute | solution.py:30
  35.4 6.9 %collective-permute-start.4 = (bf16[2,2,224,128]{3,2,1,0:T(8,128)(2,1)S(1)}, bf16[2,2,224,128]{3,2,1,0:T(8,128)(2,1)S(1)}, u32[]{:S(2)}, u32[]{:S(2)}) collective-permute-start(bf16[2,2,224,128]{3,2,1,0:T(8,128)(2,1)S(1)} %add_chunk0_step2.1), channel_id=1, source_target_pairs={{0,4},{1,5},{2,6},{3,7},{4,0},{5,1},{6,2},{7,3},{8,12},{9,13},{10,... | collective-permute-start | bytes 688136 | tf_op jit(solution)/shard_map/ppermute | solution.py:503
  36.9 5.8 %collective-permute-start.9 = (bf16[2,2,192,128]{3,2,1,0:T(8,128)(2,1)S(1)}, bf16[2,2,192,128]{3,2,1,0:T(8,128)(2,1)S(1)}, u32[]{:S(2)}, u32[]{:S(2)}) collective-permute-start(bf16[2,2,192,128]{3,2,1,0:T(8,128)(2,1)S(1)} %add_chunk1_step2.1), channel_id=1, source_target_pairs={{0,8},{1,9},{2,10},{3,11},{4,12},{5,13},{6,14},{7,15},{8,0},{9,1},... | collective-permute-start | bytes 589832 | tf_op jit(solution)/shard_map/ppermute | solution.py:503
  37.1 6.7 %collective-permute-start.15 = (bf16[2,2,176,128]{3,2,1,0:T(8,128)(2,1)S(1)}, bf16[2,2,176,128]{3,2,1,0:T(8,128)(2,1)S(1)}, u32[]{:S(2)}, u32[]{:S(2)}) collective-permute-start(bf16[2,2,176,128]{3,2,1,0:T(8,128)(2,1)S(1)} %add_chunk2_step2.1), channel_id=1, source_target_pairs={{0,2},{1,3},{2,0},{3,1},{4,6},{5,7},{6,4},{7,5},{8,10},{9,11},{10,... | collective-permute-start | bytes 540680 | tf_op jit(solution)/shard_map/ppermute | solution.py:503
  42.4 4.9 %collective-permute-start.5 = (bf16[2,224,128]{2,1,0:T(8,128)(2,1)S(1)}, bf16[2,224,128]{2,1,0:T(8,128)(2,1)S(1)}, u32[]{:S(2)}, u32[]{:S(2)}) collective-permute-start(bf16[2,224,128]{2,1,0:T(8,128)(2,1)S(1)} %add_chunk0_step3.1), channel_id=1, source_target_pairs={{0,8},{1,9},{2,10},{3,11},{4,12},{5,13},{6,14},{7,15},{8,0},{9,1},... | collective-permute-start | bytes 344072 | tf_op jit(solution)/shard_map/ppermute | solution.py:503
  42.8 5.5 %collective-permute-start.10 = (bf16[2,192,128]{2,1,0:T(8,128)(2,1)S(1)}, bf16[2,192,128]{2,1,0:T(8,128)(2,1)S(1)}, u32[]{:S(2)}, u32[]{:S(2)}) collective-permute-start(bf16[2,192,128]{2,1,0:T(8,128)(2,1)S(1)} %add_chunk1_step3.1), channel_id=1, source_target_pairs={{0,2},{1,3},{2,0},{3,1},{4,6},{5,7},{6,4},{7,5},{8,10},{9,11},{10,... | collective-permute-start | bytes 294920 | tf_op jit(solution)/shard_map/ppermute | solution.py:503
  43.8 6.6 %collective-permute-start.16 = (bf16[2,176,128]{2,1,0:T(8,128)(2,1)S(1)}, bf16[2,176,128]{2,1,0:T(8,128)(2,1)S(1)}, u32[]{:S(2)}, u32[]{:S(2)}) collective-permute-start(bf16[2,176,128]{2,1,0:T(8,128)(2,1)S(1)} %add_chunk2_step3.1), channel_id=1, source_target_pairs={{0,4},{1,5},{2,6},{3,7},{4,0},{5,1},{6,2},{7,3},{8,12},{9,13},{10,... | collective-permute-start | bytes 270344 | tf_op jit(solution)/shard_map/ppermute | solution.py:503
  47.3 6.6 %collective-permute-start.6 = (bf16[224,128]{1,0:T(8,128)(2,1)S(1)}, bf16[224,128]{1,0:T(8,128)(2,1)S(1)}, u32[]{:S(2)}, u32[]{:S(2)}) collective-permute-start(bf16[224,128]{1,0:T(8,128)(2,1)S(1)} %add_chunk0_step4.1), channel_id=1, source_target_pairs={{0,16},{1,17},{2,18},{3,19},{4,20},{5,21},{6,22},{7,23},{8,24},{9,... | collective-permute-start | bytes 172040 | tf_op jit(solution)/shard_map/ppermute | solution.py:503
  48.3 5.6 %collective-permute-start.11 = (bf16[192,128]{1,0:T(8,128)(2,1)S(1)}, bf16[192,128]{1,0:T(8,128)(2,1)S(1)}, u32[]{:S(2)}, u32[]{:S(2)}) collective-permute-start(bf16[192,128]{1,0:T(8,128)(2,1)S(1)} %add_chunk1_step4.1), channel_id=1, source_target_pairs={{0,16},{1,17},{2,18},{3,19},{4,20},{5,21},{6,22},{7,23},{8,24},{9,... | collective-permute-start | bytes 147464 | tf_op jit(solution)/shard_map/ppermute | solution.py:503
  50.4 5.4 %collective-permute-start.17 = (bf16[176,128]{1,0:T(8,128)(2,1)S(1)}, bf16[176,128]{1,0:T(8,128)(2,1)S(1)}, u32[]{:S(2)}, u32[]{:S(2)}) collective-permute-start(bf16[176,128]{1,0:T(8,128)(2,1)S(1)} %add_chunk2_step4.1), channel_id=1, source_target_pairs={{0,16},{1,17},{2,18},{3,19},{4,20},{5,21},{6,22},{7,23},{8,24},{9,... | collective-permute-start | bytes 135176 | tf_op jit(solution)/shard_map/ppermute | solution.py:503

commit v11 on v9

--- a/solution.py
+++ b/solution.py
@@ -141,13 +141,20 @@
     return items + ([(high - third - 1, True)] if high > third else [])
 
 
+def row_blocks(first, last):
+    middle = first + (last - first) // 32 * 16
+    return ((middle, last), (first, middle))
+
+
 def earlier_rows(plan, index, present, first, last):
     dilation, begin = 2**index, 2 * plan["halo"]
+    if first >= begin + dilation or last <= begin:
+        return present[first - dilation : last - dilation]
     cut = cut_off(present[begin - dilation : begin], dilation)
     return jnp.concatenate([present[first - dilation : begin - dilation], cut, present[begin : last - dilation]])
 
 
-def backward(plan, layers, refs_of, conv_w, out_w, grad_proj, grad_stream, past_part, grad_parts):
+def backward(plan, layers, refs_of, conv_w, out_w, grad_proj, grad_preact, grad_stream, past_part, grad_parts):
     halo, length, channels = plan["halo"], plan["length"], plan["channels"]
     own = slice(halo, halo + length)
     items = plan["items"]
@@ -159,20 +166,23 @@
 
     for index in layers:
         dilation, count = 2**index, plan["counts"][index]
+        rows = plan["counts"][index - 1] if index else length
         present, earlier, factors, _ = refs_of(index)
-        grad_proj[0:count, :channels] = grad_stream[0:count].astype(jnp.bfloat16)
-        grad_gated = dot(grad_proj[0:count], out_w[index], NT)
+        for a, b in row_blocks(0, count):
+            grad_proj[a:b, :channels] = grad_stream[a:b].astype(jnp.bfloat16)
+            grad_gated = dot(grad_proj[a:b], out_w[index], NT)
+            both = factors[halo + a : halo + b].astype(jnp.float32)
+            grad_preact[a:b] = jnp.concatenate(
+                [grad_gated * both[:, :channels], grad_gated * both[:, channels:]], axis=1
+            ).astype(jnp.bfloat16)
+            spread = dot(grad_preact[a:b], conv_w[index], NT)
+            past_part[a:b] = spread[:, channels:]
+            if a <= halo < b:
+                cut = slice(halo, halo + max(dilation, 8))
+                past_part[cut] = cut_off(past_part[cut], dilation)
+            c = min(b, rows)
+            grad_stream[a:c] += spread[0 : c - a, :channels] + past_part[a + dilation : c + dilation]
         out_grad(index)
-        both = factors[halo : halo + count].astype(jnp.float32)
-        grad_preact = jnp.concatenate(
-            [grad_gated * both[:, :channels], grad_gated * both[:, channels:]], axis=1
-        ).astype(jnp.bfloat16)
-        spread = dot(grad_preact, conv_w[index], NT)
-        past_part[0:count] = spread[:, channels:]
-        cut = slice(halo, halo + max(dilation, 8))
-        past_part[cut] = cut_off(past_part[cut], dilation)
-        rows = plan["counts"][index - 1] if index else length
-        grad_stream[0:rows] += spread[0:rows, :channels] + past_part[dilation : dilation + rows]
         past = earlier_rows(plan, index, present, halo, halo + length) if earlier is None else earlier[own]
         total = dot(jnp.concatenate([present[own], past], axis=1), grad_preact[0:length], TN)
         plan["store"](total, items.index((index, False)), grad_parts)
@@ -186,7 +196,7 @@
     plan, prev_rows, own_x, own_grad, own_skip, conv_w, out_w,
     low_present, low_earlier, low_factors, low_gates, grad_stream, grad_skip, *rest,
 ):
-    *grad_parts, stream, high_present, high_factors, high_gates, grad_proj, past_part = rest
+    *grad_parts, stream, high_present, high_factors, high_gates, grad_proj, grad_preact, past_part = rest
     halo, (length, channels) = plan["halo"], own_x.shape
     layers, low = conv_w.shape[0], low_gates.shape[0]
     pad = 2 ** (layers - 1)
@@ -205,28 +215,31 @@
     refs_of(0)[0][0:begin] = prev_rows[0:begin]
     refs_of(0)[0][begin:] = own_x[...]
     for index in range(layers):
-        dilation, start = 2**index, plan["starts"][index]
+        dilation = 2**index
         present, earlier, factor, gate = refs_of(index)
-        if earlier is None:
-            past = earlier_rows(plan, index, present, start, extent)
-        else:
-            past = stream[pad + start - dilation : pad + extent - dilation]
-            cut = cut_off(past[begin - start : begin - start + 16], dilation)
-            past = jnp.concatenate([past[: begin - start], cut, past[begin - start + 16 :]]).astype(jnp.bfloat16)
-            earlier[start:] = past
-        preact = dot(jnp.concatenate([present[start:], past], axis=1), conv_w[index], NN)
-        filtered = jnp.tanh(preact[:, :channels])
-        opening = 0.5 + 0.5 * jnp.tanh(0.5 * preact[:, channels:])
-        product = filtered * opening
-        gated = product.astype(jnp.bfloat16)
-        gate[start:] = gated
-        factor[start:, :channels] = (opening - filtered * product).astype(jnp.bfloat16)
-        factor[start:, channels:] = (product * (1.0 - opening)).astype(jnp.bfloat16)
-        if index < layers - 1:
-            after = stream[pad + start :] + dot(gated, out_w[index, :, :channels], NN)
-            refs_of(index + 1)[0][start:] = after.astype(jnp.bfloat16)
-            if index < layers - 2:
-                stream[pad + start :] = after
+        for a, b in row_blocks(plan["starts"][index], extent):
+            if earlier is None:
+                past = earlier_rows(plan, index, present, a, b)
+            else:
+                past = stream[pad + a - dilation : pad + b - dilation]
+                if a <= begin < b:
+                    cut = cut_off(past[begin - a : begin - a + 16], dilation)
+                    past = jnp.concatenate([past[: begin - a], cut, past[begin - a + 16 :]])
+                past = past.astype(jnp.bfloat16)
+                earlier[a:b] = past
+            preact = dot(jnp.concatenate([present[a:b], past], axis=1), conv_w[index], NN)
+            filtered = jnp.tanh(preact[:, :channels])
+            opening = 0.5 + 0.5 * jnp.tanh(0.5 * preact[:, channels:])
+            product = filtered * opening
+            gated = product.astype(jnp.bfloat16)
+            gate[a:b] = gated
+            factor[a:b, :channels] = (opening - filtered * product).astype(jnp.bfloat16)
+            factor[a:b, channels:] = (product * (1.0 - opening)).astype(jnp.bfloat16)
+            if index < layers - 1:
+                after = stream[pad + a : pad + b] + dot(gated, out_w[index, :, :channels], NN)
+                refs_of(index + 1)[0][a:b] = after.astype(jnp.bfloat16)
+                if index < layers - 2:
+                    stream[pad + a : pad + b] = after
 
     grad_stream[0:halo] = prev_rows[2 * halo : 3 * halo].astype(jnp.float32)
     grad_stream[halo:] = own_grad[...]
@@ -234,14 +247,15 @@
     grad_skip[halo:] = own_skip[...]
     grad_proj[:, channels:] = grad_skip[...]
     backward(
-        plan, list(reversed(range(low, layers))), refs_of, conv_w, out_w, grad_proj, grad_stream, past_part, grad_parts
+        plan, list(reversed(range(low, layers))), refs_of, conv_w, out_w,
+        grad_proj, grad_preact, grad_stream, past_part, grad_parts,
     )
 
 
 def later_kernel(
     plan, first, third, present, earlier, factors, gates, grad_before, grad_skip, sums, conv_w, out_w, *rest
 ):
-    *outs, keep, send, grad_stream, grad_proj, past_part = rest[plan["unused"] :]
+    *outs, keep, send, grad_stream, grad_proj, grad_preact, past_part = rest[plan["unused"] :]
     channels = plan["channels"]
     grad_stream[...] = grad_before[...]
     grad_proj[:, channels:] = grad_skip[...]
@@ -251,7 +265,7 @@
 
     backward(
         plan, list(reversed(range(first, first + third))), refs_of, conv_w, out_w,
-        grad_proj, grad_stream, past_part, (keep, send),
+        grad_proj, grad_preact, grad_stream, past_part, (keep, send),
     )
     at = 0
     for out in outs:
@@ -357,6 +371,7 @@
             pltpu.VMEM((third, extent, 2 * channels), jnp.bfloat16),
             pltpu.VMEM((third, extent, channels), jnp.bfloat16),
             pltpu.VMEM((border, 2 * channels), jnp.bfloat16),
+            pltpu.VMEM((border, 2 * channels), jnp.bfloat16),
             pltpu.VMEM((border, channels), jnp.float32),
         ],
         compiler_params=pltpu.CompilerParams(vmem_limit_bytes=VMEM_BYTES),
@@ -373,6 +388,7 @@
             + [pltpu.VMEM(shape, jnp.bfloat16) for shape in shapes[step]],
             scratch_shapes=[
                 pltpu.VMEM((border, channels), jnp.float32),
+                pltpu.VMEM((border, 2 * channels), jnp.bfloat16),
                 pltpu.VMEM((border, 2 * channels), jnp.bfloat16),
                 pltpu.VMEM((border, channels), jnp.float32),
             ],

time: 56.5 us -> 58 us (1.027)
  Pallas kernels: 15.1 us -> 16.6 us
    pallas_call x1, Pallas kernels: 5.48 us -> 6.27 us  [run_layers(): pl.pallas_call(functools.partial(first_kernel, plans[0]), in_specs=[vmem]...]
    pallas_call x2, Pallas kernels: 4.14 us -> 4.86 us  [later(): pl.pallas_call(functools.partial(later_kernel, plans[step] | {'unused': l...]
where the time goes in v11:
time: 58 us; the launch traced here: 57.9 us
  waiting for transfers between devices  22.2 us (38%)
  starting transfers between devices  18.3 us (32%)
  Pallas kernels  16.6 us (29%)
  between operations  0.76 us (1%)
    ppermute x15, starting transfers between devices, swapped(): return lax.ppermute(value, ('tm', 'dp'), pairs)  12.1 us
    ppermute x2, waiting for transfers between devices, around(): return lax.ppermute(x, axis, [(i, (i + by) % count) for i in range(count)])  12 us
    ppermute x15, waiting for transfers between devices, swapped(): return lax.ppermute(value, ('tm', 'dp'), pairs)  10.3 us
    pallas_call x1, Pallas kernels, run_layers(): pl.pallas_call(functools.partial(first_kernel, plans[0]), in_specs=[vmem]...  6.27 us
    ppermute x2, starting transfers between devices, around(): return lax.ppermute(x, axis, [(i, (i + by) % count) for i in range(count)])  6.17 us
    pallas_call x2, Pallas kernels, later(): pl.pallas_call(functools.partial(later_kernel, plans[step] | {'unused': l...  4.86 us
    pallas_call x1, Pallas kernels, load_all(): pl.pallas_call(load_kernel, in_specs=[anywhere] * 7, out_specs=[vmem] * 6...  2.67 us
  transfers between devices with their start and end apart: 17, of which 8 were waited for; matrix products, arithmetic and copies ran while one was open for 0% of the time, Pallas kernels for 14%

profile of v11, /device:TPU:0, one launch (start us, length us, event | category | flops | bytes accessed | tf_op | source)
XLA Modules:
  0.0 57.9 jit_solution(933903930401839364)
XLA Ops:
  0.6 1.0 %pack_borders.1._ = bf16[256,256]{1,0:T(8,128)(2,1)S(1)} custom-call(bf16[512,256]{1,0:T(8,128)(2,1)} %bitcast.4, bf16[512,256]{1,0:T(8,128)(2,1)} %bitcast.6, bf16[512,256]{1,0:T(8,128)(2,1)} %bitcast.8, f32[1,512]{1,0:T(1,128)} %weight.3), custom_call_target="tpu_custom_call" | custom-call | tf_op jit(solution)/shard_map/pack_borders/pallas_call | solution.py:56
  1.6 3.0 %collective-permute-start = (bf16[256,256]{1,0:T(8,128)(2,1)S(1)}, bf16[256,256]{1,0:T(8,128)(2,1)S(1)}, u32[]{:S(2)}, u32[]{:S(2)}) collective-permute-start(bf16[256,256]{1,0:T(8,128)(2,1)S(1)} %pack_borders.1._), channel_id=1, source_target_pairs={{0,4},{4,8},{8,12},{12,16},{16,20},{20,24},{24,28},{28,0},{1,5},{5... | collective-permute-start | bytes 393224 | tf_op jit(solution)/shard_map/ppermute | solution.py:30
  4.6 2.7 %load_all.1 = (bf16[512,256]{1,0:T(8,128)(2,1)S(1)}, f32[512,256]{1,0:T(8,128)S(1)}, bf16[512,256]{1,0:T(8,128)(2,1)S(1)}, bf16[16,128]{1,0:T(8,128)(2,1)S(1)}, ...) custom-call(bf16[512,256]{1,0:T(8,128)(2,1)} %bitcast.5, bf16[512,256]{1,0:T(8,128)(2,1)} %bitcast.7, ...), custom_call_target="tpu_custom_call" | custom-call | flops 10000000 | bytes 6000000 | tf_op jit(solution)/shard_map/load_all/pallas_call | solution.py:91
  7.3 3.9 %collective-permute-done.prev_rows = bf16[256,256]{1,0:T(8,128)(2,1)S(1)} collective-permute-done((bf16[256,256]{1,0:T(8,128)(2,1)S(1)}, bf16[256,256]{1,0:T(8,128)(2,1)S(1)}, u32[]{:S(2)}, u32[]{:S(2)}) %collective-permute-start) | collective-permute-done | bytes 131104 | tf_op jit(solution)/shard_map/ppermute | solution.py:30
  11.1 6.3 %forward_and_last_third.1 = (bf16[4,640,256]{2,1,0:T(8,128)(2,1)S(1)}, bf16[4,640,256]{2,1,0:T(8,128)(2,1)S(1)}, bf16[4,640,512]{2,1,0:T(8,128)(2,1)S(1)}, bf16[...) custom-call(bf16[256,256]{1,0:T(8,128)(2,1)S(1)} %collective-permute, ...), custom_call_target="tpu_custom_call" | custom-call | flops 3623878656 | bytes 4718592 | tf_op jit(solution)/shard_map/forward_and_last_third/pallas_call | solution.py:355
  17.4 0.1 collective-permute-start.1
  17.5 2.5 %middle_third.1 = (f32[576,256]{1,0:T(8,128)S(1)}, bf16[2,2,2,2,192,128]{5,4,3,2,1,0:T(8,128)(2,1)S(1)}, bf16[2,2,2,2,192,128]{5,4,3,2,1,0:T(8,128)(2,1)S(1)}) custom-call(bf16[4,640,256]{2,1,0:T(8,128)(2,1)S(1)} %get-tuple-element.34.present, bf16[4,640,256]{2,1,0:T(8,128)(2,1)S(1)} %get-tuple-element.35.earlier, ...), custom_call_target="tpu_custom_call" | custom-call | flops 1610612736 | bytes 4718592 | tf_op jit(solution)/shard_map/middle_third/pallas_call | solution.py:383
  20.0 0.6 collective-permute-start.7
  20.5 0.0 collective-permute-done.1.refs_1_
  20.5 0.1 add_chunk0_step1.1.rest_0_
  20.7 2.4 %first_third.1 = (bf16[64,256]{1,0:T(8,128)(2,1)S(1)}, f32[448,256]{1,0:T(8,128)S(1)}, bf16[2,2,2,2,176,128]{5,4,3,2,1,0:T(8,128)(2,1)S(1)}, bf16[2,2,2,2,176,128]{5,4,3,2,1,0:T(8,128)(2,1)S(1)}) custom-call(bf16[4,640,256]{2,1,0:T(8,128)(2,1)S(1)} %get-tuple-element.34.present, bf16[4,640,256]{2,1,0:T(8,128)(2,1)S(1)} %get-tuple-element.35.earlier, ...), custom_call_target="tpu_custom_call" | custom-call | flops 1610612736 | bytes 4718592 | tf_op jit(solution)/shard_map/first_third/pallas_call | solution.py:383
  23.0 0.1 collective-permute-start.12
  23.1 1.6 %collective-permute-start.2 = (bf16[2,2,2,224,128]{4,3,2,1,0:T(8,128)(2,1)S(1)}, bf16[2,2,2,224,128]{4,3,2,1,0:T(8,128)(2,1)S(1)}, u32[]{:S(2)}, u32[]{:S(2)}) collective-permute-start(bf16[2,2,2,224,128]{4,3,2,1,0:T(8,128)(2,1)S(1)} %add_chunk0_step1.1.rest_0_), channel_id=1, source_target_pairs={{0,2},{1,3},{2,0},{3,1},{4,6},{5,7},{6,4},{7,5},{8,10},{9,11},{10,... | collective-permute-start | bytes 1376264 | tf_op jit(solution)/shard_map/ppermute | solution.py:506
  24.7 0.0 collective-permute-done.7.refs_1_.refs_7_
  24.7 0.1 add_chunk1_step1.1
  24.8 0.1 collective-permute-start.8
  24.9 0.4 collective-permute-done.12.refs_1_.refs_13_
  25.3 0.1 add_chunk2_step1.1
  25.4 0.1 collective-permute-start.13
  25.5 3.2 %collective-permute-start.3 = (bf16[64,256]{1,0:T(8,128)(2,1)S(1)}, bf16[64,256]{1,0:T(8,128)(2,1)S(1)}, u32[]{:S(2)}, u32[]{:S(2)}) collective-permute-start(bf16[64,256]{1,0:T(8,128)(2,1)S(1)} %get-tuple-element.42), channel_id=1, source_target_pairs={{0,28},{4,0},{8,4},{12,8},{16,12},{20,16},{24,20},{28,24},{1,29},{... | collective-permute-start | bytes 98312 | tf_op jit(solution)/shard_map/ppermute | solution.py:30
  28.7 8.1 %collective-permute-done.3.refs_3_.refs_18_ = bf16[64,256]{1,0:T(8,128)(2,1)S(1)} collective-permute-done((bf16[64,256]{1,0:T(8,128)(2,1)S(1)}, bf16[64,256]{1,0:T(8,128)(2,1)S(1)}, u32[]{:S(2)}, u32[]{:S(2)}) %collective-permute-start.3) | collective-permute-done | bytes 32800 | tf_op jit(solution)/shard_map/ppermute | solution.py:30
  36.7 0.0 collective-permute-done.2.refs_2_
  36.8 0.1 add_chunk0_step2.1
  36.8 1.4 %collective-permute-start.4 = (bf16[2,2,224,128]{3,2,1,0:T(8,128)(2,1)S(1)}, bf16[2,2,224,128]{3,2,1,0:T(8,128)(2,1)S(1)}, u32[]{:S(2)}, u32[]{:S(2)}) collective-permute-start(bf16[2,2,224,128]{3,2,1,0:T(8,128)(2,1)S(1)} %add_chunk0_step2.1), channel_id=1, source_target_pairs={{0,4},{1,5},{2,6},{3,7},{4,0},{5,1},{6,2},{7,3},{8,12},{9,13},{10,... | collective-permute-start | bytes 688136 | tf_op jit(solution)/shard_map/ppermute | solution.py:506
  38.2 0.0 collective-permute-done.8.refs_2_.refs_8_
  38.2 0.1 add_chunk1_step2.1
  38.3 0.1 collective-permute-start.9
  38.4 0.0 collective-permute-done.13.refs_2_.refs_14_
  38.4 0.1 add_chunk2_step2.1
  38.5 1.6 %collective-permute-start.14 = (bf16[2,2,176,128]{3,2,1,0:T(8,128)(2,1)S(1)}, bf16[2,2,176,128]{3,2,1,0:T(8,128)(2,1)S(1)}, u32[]{:S(2)}, u32[]{:S(2)}) collective-permute-start(bf16[2,2,176,128]{3,2,1,0:T(8,128)(2,1)S(1)} %add_chunk2_step2.1), channel_id=1, source_target_pairs={{0,2},{1,3},{2,0},{3,1},{4,6},{5,7},{6,4},{7,5},{8,10},{9,11},{10,... | collective-permute-start | bytes 540680 | tf_op jit(solution)/shard_map/ppermute | solution.py:506
  40.1 3.7 %collective-permute-done.4.refs_3_ = bf16[2,2,224,128]{3,2,1,0:T(8,128)(2,1)S(1)} collective-permute-done((bf16[2,2,224,128]{3,2,1,0:T(8,128)(2,1)S(1)}, bf16[2,2,224,128]{3,2,1,0:T(8,128)(2,1)S(1)}, u32[]{:S(2)}, u32[]{:S(2)}) %collective-permute-start.4) | collective-permute-done | bytes 229408 | tf_op jit(solution)/shard_map/ppermute | solution.py:506
  43.8 0.1 add_chunk0_step3.1
  43.8 0.1 collective-permute-start.5
  43.9 0.2 collective-permute-done.9.refs_3_.refs_9_
  44.0 0.1 add_chunk1_step3.1
  44.1 1.6 %collective-permute-start.10 = (bf16[2,192,128]{2,1,0:T(8,128)(2,1)S(1)}, bf16[2,192,128]{2,1,0:T(8,128)(2,1)S(1)}, u32[]{:S(2)}, u32[]{:S(2)}) collective-permute-start(bf16[2,192,128]{2,1,0:T(8,128)(2,1)S(1)} %add_chunk1_step3.1), channel_id=1, source_target_pairs={{0,2},{1,3},{2,0},{3,1},{4,6},{5,7},{6,4},{7,5},{8,10},{9,11},{10,... | collective-permute-start | bytes 294920 | tf_op jit(solution)/shard_map/ppermute | solution.py:506
  45.7 0.0 collective-permute-done.14.refs_3_.refs_15_
  45.7 0.1 add_chunk2_step3.1
  45.7 0.9 %collective-permute-start.15 = (bf16[2,176,128]{2,1,0:T(8,128)(2,1)S(1)}, bf16[2,176,128]{2,1,0:T(8,128)(2,1)S(1)}, u32[]{:S(2)}, u32[]{:S(2)}) collective-permute-start(bf16[2,176,128]{2,1,0:T(8,128)(2,1)S(1)} %add_chunk2_step3.1), channel_id=1, source_target_pairs={{0,4},{1,5},{2,6},{3,7},{4,0},{5,1},{6,2},{7,3},{8,12},{9,13},{10,... | collective-permute-start | bytes 270344 | tf_op jit(solution)/shard_map/ppermute | solution.py:506
  46.7 2.0 %collective-permute-done.5.refs_4_ = bf16[2,224,128]{2,1,0:T(8,128)(2,1)S(1)} collective-permute-done((bf16[2,224,128]{2,1,0:T(8,128)(2,1)S(1)}, bf16[2,224,128]{2,1,0:T(8,128)(2,1)S(1)}, u32[]{:S(2)}, u32[]{:S(2)}) %collective-permute-start.5) | collective-permute-done | bytes 114720 | tf_op jit(solution)/shard_map/ppermute | solution.py:506
  48.7 1.0 %collective-permute-start.6 = (bf16[224,128]{1,0:T(8,128)(2,1)S(1)}, bf16[224,128]{1,0:T(8,128)(2,1)S(1)}, u32[]{:S(2)}, u32[]{:S(2)}) collective-permute-start(bf16[224,128]{1,0:T(8,128)(2,1)S(1)} %add_chunk0_step4.1), channel_id=1, source_target_pairs={{0,16},{1,17},{2,18},{3,19},{4,20},{5,21},{6,22},{7,23},{8,24},{9,... | collective-permute-start | bytes 172040 | tf_op jit(solution)/shard_map/ppermute | solution.py:506
  49.7 0.0 collective-permute-done.10.refs_4_.refs_10_
  49.8 2.0 %collective-permute-start.11 = (bf16[192,128]{1,0:T(8,128)(2,1)S(1)}, bf16[192,128]{1,0:T(8,128)(2,1)S(1)}, u32[]{:S(2)}, u32[]{:S(2)}) collective-permute-start(bf16[192,128]{1,0:T(8,128)(2,1)S(1)} %add_chunk1_step4.1), channel_id=1, source_target_pairs={{0,16},{1,17},{2,18},{3,19},{4,20},{5,21},{6,22},{7,23},{8,24},{9,... | collective-permute-start | bytes 147464 | tf_op jit(solution)/shard_map/ppermute | solution.py:506
  51.8 0.0 collective-permute-done.15.refs_4_.refs_16_
  51.9 1.0 %collective-permute-start.16 = (bf16[176,128]{1,0:T(8,128)(2,1)S(1)}, bf16[176,128]{1,0:T(8,128)(2,1)S(1)}, u32[]{:S(2)}, u32[]{:S(2)}) collective-permute-start(bf16[176,128]{1,0:T(8,128)(2,1)S(1)} %add_chunk2_step4.1), channel_id=1, source_target_pairs={{0,16},{1,17},{2,18},{3,19},{4,20},{5,21},{6,22},{7,23},{8,24},{9,... | collective-permute-start | bytes 135176 | tf_op jit(solution)/shard_map/ppermute | solution.py:506
  52.9 1.9 %collective-permute-done.11.refs_11_ = bf16[192,128]{1,0:T(8,128)(2,1)S(1)} collective-permute-done((bf16[192,128]{1,0:T(8,128)(2,1)S(1)}, bf16[192,128]{1,0:T(8,128)(2,1)S(1)}, u32[]{:S(2)}, u32[]{:S(2)}) %collective-permute-start.11) | collective-permute-done | bytes 49184 | tf_op jit(solution)/shard_map/ppermute | solution.py:506
  54.8 0.0 collective-permute-done.6.refs_5_
  54.8 2.0 %collective-permute-done.16.refs_17_ = bf16[176,128]{1,0:T(8,128)(2,1)S(1)} collective-permute-done((bf16[176,128]{1,0:T(8,128)(2,1)S(1)}, bf16[176,128]{1,0:T(8,128)(2,1)S(1)}, u32[]{:S(2)}, u32[]{:S(2)}) %collective-permute-start.16) | collective-permute-done | bytes 45088 | tf_op jit(solution)/shard_map/ppermute | solution.py:506
  56.9 1.0 %scale_all.1 = (f32[512,256]{1,0:T(8,128)}, f32[6,64,128]{2,1,0:T(8,128)}, f32[6,32,128]{2,1,0:T(8,128)}) custom-call(bf16[2,2,2,2,224,128]{5,4,3,2,1,0:T(8,128)(2,1)S(1)} %get-tuple-element.32.refs_0_, bf16[2,2,2,2,224,128]{5,4,3,2,1,0:T(8,128)(2,1)S(1)} %collective-permute-done.1.refs_1_, bf16[2,2,2,224,128]{4,3,2,1,0:T(8,128)(2,1)S(1)} %collective-permute-done.2.refs_2_, ...), custom_call_target="tpu_custom_call" | custom-call | tf_op jit(solution)/shard_map/scale_all/pallas_call | solution.py:542
  (3 shorter events, 0.1 us)
Async XLA Ops:
  1.6 9.5 %collective-permute-start = (bf16[256,256]{1,0:T(8,128)(2,1)S(1)}, bf16[256,256]{1,0:T(8,128)(2,1)S(1)}, u32[]{:S(2)}, u32[]{:S(2)}) collective-permute-start(bf16[256,256]{1,0:T(8,128)(2,1)S(1)} %pack_borders.1._), channel_id=1, source_target_pairs={{0,4},{4,8},{8,12},{12,16},{16,20},{20,24},{24,28},{28,0},{1,5},{5... | collective-permute-start | bytes 393224 | tf_op jit(solution)/shard_map/ppermute | solution.py:30
  17.4 3.1 %collective-permute-start.1 = (bf16[2,2,2,2,224,128]{5,4,3,2,1,0:T(8,128)(2,1)S(1)}, bf16[2,2,2,2,224,128]{5,4,3,2,1,0:T(8,128)(2,1)S(1)}, u32[]{:S(2)}, u32[]{:S(2)}) collective-permute-start(bf16[2,2,2,2,224,128]{5,4,3,2,1,0:T(8,128)(2,1)S(1)} %get-tuple-element.33), channel_id=1, source_target_pairs={{0,1},{1,0},{2,3},{3,2},{4,5},{5,4},{6,7},{7,6},{8,9},{9,8},{10,11... | collective-permute-start | bytes 2752520 | tf_op jit(solution)/shard_map/ppermute | solution.py:506
  20.0 4.7 %collective-permute-start.7 = (bf16[2,2,2,2,192,128]{5,4,3,2,1,0:T(8,128)(2,1)S(1)}, bf16[2,2,2,2,192,128]{5,4,3,2,1,0:T(8,128)(2,1)S(1)}, u32[]{:S(2)}, u32[]{:S(2)}) collective-permute-start(bf16[2,2,2,2,192,128]{5,4,3,2,1,0:T(8,128)(2,1)S(1)} %get-tuple-element.44), channel_id=1, source_target_pairs={{0,1},{1,0},{2,3},{3,2},{4,5},{5,4},{6,7},{7,6},{8,9},{9,8},{10,11... | collective-permute-start | bytes 2359304 | tf_op jit(solution)/shard_map/ppermute | solution.py:506
  23.0 2.3 %collective-permute-start.12 = (bf16[2,2,2,2,176,128]{5,4,3,2,1,0:T(8,128)(2,1)S(1)}, bf16[2,2,2,2,176,128]{5,4,3,2,1,0:T(8,128)(2,1)S(1)}, u32[]{:S(2)}, u32[]{:S(2)}) collective-permute-start(bf16[2,2,2,2,176,128]{5,4,3,2,1,0:T(8,128)(2,1)S(1)} %get-tuple-element.46), channel_id=1, source_target_pairs={{0,1},{1,0},{2,3},{3,2},{4,5},{5,4},{6,7},{7,6},{8,9},{9,8},{10,11... | collective-permute-start | bytes 2162696 | tf_op jit(solution)/shard_map/ppermute | solution.py:506
  23.1 13.6 %collective-permute-start.2 = (bf16[2,2,2,224,128]{4,3,2,1,0:T(8,128)(2,1)S(1)}, bf16[2,2,2,224,128]{4,3,2,1,0:T(8,128)(2,1)S(1)}, u32[]{:S(2)}, u32[]{:S(2)}) collective-permute-start(bf16[2,2,2,224,128]{4,3,2,1,0:T(8,128)(2,1)S(1)} %add_chunk0_step1.1.rest_0_), channel_id=1, source_target_pairs={{0,2},{1,3},{2,0},{3,1},{4,6},{5,7},{6,4},{7,5},{8,10},{9,11},{10,... | collective-permute-start | bytes 1376264 | tf_op jit(solution)/shard_map/ppermute | solution.py:506
  24.8 13.4 %collective-permute-start.8 = (bf16[2,2,2,192,128]{4,3,2,1,0:T(8,128)(2,1)S(1)}, bf16[2,2,2,192,128]{4,3,2,1,0:T(8,128)(2,1)S(1)}, u32[]{:S(2)}, u32[]{:S(2)}) collective-permute-start(bf16[2,2,2,192,128]{4,3,2,1,0:T(8,128)(2,1)S(1)} %add_chunk1_step1.1), channel_id=1, source_target_pairs={{0,4},{1,5},{2,6},{3,7},{4,0},{5,1},{6,2},{7,3},{8,12},{9,13},{10,... | collective-permute-start | bytes 1179656 | tf_op jit(solution)/shard_map/ppermute | solution.py:506
  25.4 13.0 %collective-permute-start.13 = (bf16[2,2,2,176,128]{4,3,2,1,0:T(8,128)(2,1)S(1)}, bf16[2,2,2,176,128]{4,3,2,1,0:T(8,128)(2,1)S(1)}, u32[]{:S(2)}, u32[]{:S(2)}) collective-permute-start(bf16[2,2,2,176,128]{4,3,2,1,0:T(8,128)(2,1)S(1)} %add_chunk2_step1.1), channel_id=1, source_target_pairs={{0,8},{1,9},{2,10},{3,11},{4,12},{5,13},{6,14},{7,15},{8,0},{9,1},... | collective-permute-start | bytes 1081352 | tf_op jit(solution)/shard_map/ppermute | solution.py:506
  25.5 11.3 %collective-permute-start.3 = (bf16[64,256]{1,0:T(8,128)(2,1)S(1)}, bf16[64,256]{1,0:T(8,128)(2,1)S(1)}, u32[]{:S(2)}, u32[]{:S(2)}) collective-permute-start(bf16[64,256]{1,0:T(8,128)(2,1)S(1)} %get-tuple-element.42), channel_id=1, source_target_pairs={{0,28},{4,0},{8,4},{12,8},{16,12},{20,16},{24,20},{28,24},{1,29},{... | collective-permute-start | bytes 98312 | tf_op jit(solution)/shard_map/ppermute | solution.py:30
  36.8 6.9 %collective-permute-start.4 = (bf16[2,2,224,128]{3,2,1,0:T(8,128)(2,1)S(1)}, bf16[2,2,224,128]{3,2,1,0:T(8,128)(2,1)S(1)}, u32[]{:S(2)}, u32[]{:S(2)}) collective-permute-start(bf16[2,2,224,128]{3,2,1,0:T(8,128)(2,1)S(1)} %add_chunk0_step2.1), channel_id=1, source_target_pairs={{0,4},{1,5},{2,6},{3,7},{4,0},{5,1},{6,2},{7,3},{8,12},{9,13},{10,... | collective-permute-start | bytes 688136 | tf_op jit(solution)/shard_map/ppermute | solution.py:506
  38.3 5.7 %collective-permute-start.9 = (bf16[2,2,192,128]{3,2,1,0:T(8,128)(2,1)S(1)}, bf16[2,2,192,128]{3,2,1,0:T(8,128)(2,1)S(1)}, u32[]{:S(2)}, u32[]{:S(2)}) collective-permute-start(bf16[2,2,192,128]{3,2,1,0:T(8,128)(2,1)S(1)} %add_chunk1_step2.1), channel_id=1, source_target_pairs={{0,8},{1,9},{2,10},{3,11},{4,12},{5,13},{6,14},{7,15},{8,0},{9,1},... | collective-permute-start | bytes 589832 | tf_op jit(solution)/shard_map/ppermute | solution.py:506
  38.5 7.2 %collective-permute-start.14 = (bf16[2,2,176,128]{3,2,1,0:T(8,128)(2,1)S(1)}, bf16[2,2,176,128]{3,2,1,0:T(8,128)(2,1)S(1)}, u32[]{:S(2)}, u32[]{:S(2)}) collective-permute-start(bf16[2,2,176,128]{3,2,1,0:T(8,128)(2,1)S(1)} %add_chunk2_step2.1), channel_id=1, source_target_pairs={{0,2},{1,3},{2,0},{3,1},{4,6},{5,7},{6,4},{7,5},{8,10},{9,11},{10,... | collective-permute-start | bytes 540680 | tf_op jit(solution)/shard_map/ppermute | solution.py:506
  43.8 4.9 %collective-permute-start.5 = (bf16[2,224,128]{2,1,0:T(8,128)(2,1)S(1)}, bf16[2,224,128]{2,1,0:T(8,128)(2,1)S(1)}, u32[]{:S(2)}, u32[]{:S(2)}) collective-permute-start(bf16[2,224,128]{2,1,0:T(8,128)(2,1)S(1)} %add_chunk0_step3.1), channel_id=1, source_target_pairs={{0,8},{1,9},{2,10},{3,11},{4,12},{5,13},{6,14},{7,15},{8,0},{9,1},... | collective-permute-start | bytes 344072 | tf_op jit(solution)/shard_map/ppermute | solution.py:506
  44.1 5.6 %collective-permute-start.10 = (bf16[2,192,128]{2,1,0:T(8,128)(2,1)S(1)}, bf16[2,192,128]{2,1,0:T(8,128)(2,1)S(1)}, u32[]{:S(2)}, u32[]{:S(2)}) collective-permute-start(bf16[2,192,128]{2,1,0:T(8,128)(2,1)S(1)} %add_chunk1_step3.1), channel_id=1, source_target_pairs={{0,2},{1,3},{2,0},{3,1},{4,6},{5,7},{6,4},{7,5},{8,10},{9,11},{10,... | collective-permute-start | bytes 294920 | tf_op jit(solution)/shard_map/ppermute | solution.py:506
  45.7 6.1 %collective-permute-start.15 = (bf16[2,176,128]{2,1,0:T(8,128)(2,1)S(1)}, bf16[2,176,128]{2,1,0:T(8,128)(2,1)S(1)}, u32[]{:S(2)}, u32[]{:S(2)}) collective-permute-start(bf16[2,176,128]{2,1,0:T(8,128)(2,1)S(1)} %add_chunk2_step3.1), channel_id=1, source_target_pairs={{0,4},{1,5},{2,6},{3,7},{4,0},{5,1},{6,2},{7,3},{8,12},{9,13},{10,... | collective-permute-start | bytes 270344 | tf_op jit(solution)/shard_map/ppermute | solution.py:506
  48.7 6.1 %collective-permute-start.6 = (bf16[224,128]{1,0:T(8,128)(2,1)S(1)}, bf16[224,128]{1,0:T(8,128)(2,1)S(1)}, u32[]{:S(2)}, u32[]{:S(2)}) collective-permute-start(bf16[224,128]{1,0:T(8,128)(2,1)S(1)} %add_chunk0_step4.1), channel_id=1, source_target_pairs={{0,16},{1,17},{2,18},{3,19},{4,20},{5,21},{6,22},{7,23},{8,24},{9,... | collective-permute-start | bytes 172040 | tf_op jit(solution)/shard_map/ppermute | solution.py:506
  49.8 5.1 %collective-permute-start.11 = (bf16[192,128]{1,0:T(8,128)(2,1)S(1)}, bf16[192,128]{1,0:T(8,128)(2,1)S(1)}, u32[]{:S(2)}, u32[]{:S(2)}) collective-permute-start(bf16[192,128]{1,0:T(8,128)(2,1)S(1)} %add_chunk1_step4.1), channel_id=1, source_target_pairs={{0,16},{1,17},{2,18},{3,19},{4,20},{5,21},{6,22},{7,23},{8,24},{9,... | collective-permute-start | bytes 147464 | tf_op jit(solution)/shard_map/ppermute | solution.py:506
  51.9 5.0 %collective-permute-start.16 = (bf16[176,128]{1,0:T(8,128)(2,1)S(1)}, bf16[176,128]{1,0:T(8,128)(2,1)S(1)}, u32[]{:S(2)}, u32[]{:S(2)}) collective-permute-start(bf16[176,128]{1,0:T(8,128)(2,1)S(1)} %add_chunk2_step4.1), channel_id=1, source_target_pairs={{0,16},{1,17},{2,18},{3,19},{4,20},{5,21},{6,22},{7,23},{8,24},{9,... | collective-permute-start | bytes 135176 | tf_op jit(solution)/shard_map/ppermute | solution.py:506

commit v12 on v9

--- a/solution.py
+++ b/solution.py
@@ -11,7 +11,7 @@
 VMEM_BYTES = 24 * 1024 * 1024
 ADD_BYTES = 8 * 1024 * 1024
 CHAINS = (("y", "x", "z0", "z1"), ("x", "z0", "y", "z1"), ("z0", "y", "x", "z1"))
-EXTRA = (0, 0, 16)
+EXTRA = (16, 0, 0)
 NN = (((1,), (0,)), ((), ()))
 NT = (((1,), (1,)), ((), ()))
 TN = (((0,), (0,)), ((), ()))
@@ -133,12 +133,7 @@
 def items_of(layers, chunk):
     third = layers // len(CHAINS)
     high = layers - chunk * third
-    items = []
-    for index in reversed(range(high - third, high)):
-        items.append((index, False))
-        if chunk == 0 or index < high - 1:
-            items.append((index, True))
-    return items + ([(high - third - 1, True)] if high > third else [])
+    return [(index, is_out) for index in reversed(range(high - third, high)) for is_out in (False, True)]
 
 
 def earlier_rows(plan, index, present, first, last):
@@ -152,17 +147,13 @@
     own = slice(halo, halo + length)
     items = plan["items"]
 
-    def out_grad(index):
-        if (index, True) in items:
-            total = dot(refs_of(index)[3][own], grad_proj[0:length], TN)
-            plan["store"](total, items.index((index, True)), grad_parts)
-
     for index in layers:
         dilation, count = 2**index, plan["counts"][index]
-        present, earlier, factors, _ = refs_of(index)
+        present, earlier, factors, gates = refs_of(index)
         grad_proj[0:count, :channels] = grad_stream[0:count].astype(jnp.bfloat16)
         grad_gated = dot(grad_proj[0:count], out_w[index], NT)
-        out_grad(index)
+        total = dot(gates[own], grad_proj[0:length], TN)
+        plan["store"](total, items.index((index, True)), grad_parts)
         both = factors[halo : halo + count].astype(jnp.float32)
         grad_preact = jnp.concatenate(
             [grad_gated * both[:, :channels], grad_gated * both[:, channels:]], axis=1
@@ -176,14 +167,10 @@
         past = earlier_rows(plan, index, present, halo, halo + length) if earlier is None else earlier[own]
         total = dot(jnp.concatenate([present[own], past], axis=1), grad_preact[0:length], TN)
         plan["store"](total, items.index((index, False)), grad_parts)
-    after = layers[-1] - 1
-    if (after, True) in items:
-        grad_proj[0:length, :channels] = grad_stream[0:length].astype(jnp.bfloat16)
-        out_grad(after)
 
 
 def first_kernel(
-    plan, prev_rows, own_x, own_grad, own_skip, conv_w, out_w,
+    plan, prev_rows, own_x, own_grad, own_skip, sums, conv_w, out_w,
     low_present, low_earlier, low_factors, low_gates, grad_stream, grad_skip, *rest,
 ):
     *grad_parts, stream, high_present, high_factors, high_gates, grad_proj, past_part = rest
@@ -236,10 +223,11 @@
     backward(
         plan, list(reversed(range(low, layers))), refs_of, conv_w, out_w, grad_proj, grad_stream, past_part, grad_parts
     )
+    plan["finish"](sums, grad_parts)
 
 
 def later_kernel(
-    plan, first, third, present, earlier, factors, gates, grad_before, grad_skip, sums, conv_w, out_w, *rest
+    plan, first, third, present, earlier, factors, gates, grad_before, grad_skip, conv_w, out_w, *rest
 ):
     *outs, keep, send, grad_stream, grad_proj, past_part = rest[plan["unused"] :]
     channels = plan["channels"]
@@ -257,7 +245,6 @@
     for out in outs:
         out[...] = grad_stream[at : at + out.shape[0]].astype(out.dtype)
         at += out.shape[0]
-    plan["finish"](sums, (keep, send))
 
 
 def store_whole(items, total, item, grad_parts):
@@ -340,7 +327,7 @@
     flops = 2 * length * channels * channels
     *kept, grad_stream, grad_skip, keep, send = pl.pallas_call(
         functools.partial(first_kernel, plans[0]),
-        in_specs=[vmem] * 6,
+        in_specs=[vmem] * 7,
         out_specs=[vmem] * 8,
         out_shape=[
             pltpu.VMEM((low, extent, channels), jnp.bfloat16),
@@ -362,12 +349,12 @@
         compiler_params=pltpu.CompilerParams(vmem_limit_bytes=VMEM_BYTES),
         cost_estimate=cost(flops * (5 * layers + 12 * third), weight_bytes),
         name="forward_and_last_third",
-    )(*held((prev_rows, own_x, own_grad, own_skip, conv_w, out_w)))
+    )(*held((prev_rows, *loaded)))
 
     def later(step, outs, after):
         return pl.pallas_call(
             functools.partial(later_kernel, plans[step] | {"unused": len(after)}, layers - (step + 1) * third, third),
-            in_specs=[vmem] * 9 + [anywhere] * len(after),
+            in_specs=[vmem] * 8 + [anywhere] * len(after),
             out_specs=[vmem] * (len(outs) + 2),
             out_shape=[pltpu.VMEM((rows, channels), kind) for rows, kind in outs]
             + [pltpu.VMEM(shape, jnp.bfloat16) for shape in shapes[step]],
@@ -379,7 +366,7 @@
             compiler_params=pltpu.CompilerParams(vmem_limit_bytes=VMEM_BYTES),
             cost_estimate=cost(flops * 12 * third, weight_bytes),
             name="middle_third" if step == 1 else "first_third",
-        )(*held((*kept, grad_stream, grad_skip, sums, conv_w, out_w, *after)))
+        )(*held((*kept, grad_stream, grad_skip, conv_w, out_w, *after)))
 
     parts = [(keep, send)]
     if in_shards:
@@ -437,12 +424,12 @@
 def last_kernel(counts, samples_all, tm, *refs):
     chunks = []
     for count in counts:
-        chunks.append(refs[:count])
+        chunks.insert(0, refs[:count])
         refs = refs[count:]
     other, own, grad_inputs, grad_conv, grad_out = refs
     layers, channels = grad_conv.shape[0], own.shape[1]
     total = 0.0
-    for term in chunks[-1]:
+    for term in chunks[0]:
         total = total + jnp.sum(first_block(term, term.shape[-2] - 16, 16), axis=0, keepdims=True)
     scale = samples_all / total
     for chunk, terms in enumerate(chunks):
@@ -524,7 +511,7 @@
     chunks = [part.run_chain([other] if part is parts[0] else ()) for part in parts]
     conv_rows, out_rows = 2 * channels // tm, channels // tm
     grad_inputs, grad_conv, grad_out = pl.pallas_call(
-        functools.partial(last_kernel, [len(terms) for terms in chunks], float(samples_all), tm),
+        functools.partial(last_kernel, [len(terms) for terms in reversed(chunks)], float(samples_all), tm),
         out_shape=[
             jax.ShapeDtypeStruct((length, channels), jnp.float32),
             jax.ShapeDtypeStruct((layers, conv_rows, LANES), jnp.float32),
@@ -532,7 +519,7 @@
         ],
         compiler_params=pltpu.CompilerParams(vmem_limit_bytes=ADD_BYTES),
         name="scale_all",
-    )(*held([term for terms in chunks for term in terms]), *held([other, own]))
+    )(*held([term for terms in reversed(chunks) for term in terms]), *held([other, own]))
     return grad_inputs[None], grad_conv, grad_out
 
 

time: 56.5 us -> 55.9 us (0.989)
  waiting for transfers between devices: 22.2 us -> 20.9 us
  starting transfers between devices: 18.3 us -> 19.3 us
    ppermute x15, waiting for transfers between devices: 10.2 us -> 8.93 us  [swapped(): return lax.ppermute(value, ('tm', 'dp'), pairs)]
    ppermute x15, starting transfers between devices: 12.2 us -> 13.3 us  [swapped(): return lax.ppermute(value, ('tm', 'dp'), pairs)]
  transfers between devices with their start and end apart: 17 -> 17, of which waited for: 8 -> 8; matrix products, arithmetic and copies ran while one was open for 0% -> 0% of each run, Pallas kernels for 14% -> 13%
where the time goes in v12:
time: 55.9 us; the launch traced here: 55.7 us
  waiting for transfers between devices  20.9 us (37%)
  starting transfers between devices  19.3 us (35%)
  Pallas kernels  14.8 us (26%)
  between operations  0.75 us (1%)
    ppermute x15, starting transfers between devices, swapped(): return lax.ppermute(value, ('tm', 'dp'), pairs)  13.3 us
    ppermute x2, waiting for transfers between devices, around(): return lax.ppermute(x, axis, [(i, (i + by) % count) for i in range(count)])  12 us
    ppermute x15, waiting for transfers between devices, swapped(): return lax.ppermute(value, ('tm', 'dp'), pairs)  8.93 us
    ppermute x2, starting transfers between devices, around(): return lax.ppermute(x, axis, [(i, (i + by) % count) for i in range(count)])  6.07 us
    pallas_call x1, Pallas kernels, run_layers(): pl.pallas_call(functools.partial(first_kernel, plans[0]), in_specs=[vmem]...  5.45 us
    pallas_call x2, Pallas kernels, later(): pl.pallas_call(functools.partial(later_kernel, plans[step] | {'unused': l...  3.85 us
    pallas_call x1, Pallas kernels, load_all(): pl.pallas_call(load_kernel, in_specs=[anywhere] * 7, out_specs=[vmem] * 6...  2.67 us
  transfers between devices with their start and end apart: 17, of which 8 were waited for; matrix products, arithmetic and copies ran while one was open for 0% of the time, Pallas kernels for 13%

profile of v12, /device:TPU:0, one launch (start us, length us, event | category | flops | bytes accessed | tf_op | source)
XLA Modules:
  0.0 55.7 jit_solution(14966392369426051017)
XLA Ops:
  0.6 1.0 %pack_borders.1._ = bf16[256,256]{1,0:T(8,128)(2,1)S(1)} custom-call(bf16[512,256]{1,0:T(8,128)(2,1)} %bitcast.4, bf16[512,256]{1,0:T(8,128)(2,1)} %bitcast.6, bf16[512,256]{1,0:T(8,128)(2,1)} %bitcast.8, f32[1,512]{1,0:T(1,128)} %weight.3), custom_call_target="tpu_custom_call" | custom-call | tf_op jit(solution)/shard_map/pack_borders/pallas_call | solution.py:56
  1.6 3.0 %collective-permute-start = (bf16[256,256]{1,0:T(8,128)(2,1)S(1)}, bf16[256,256]{1,0:T(8,128)(2,1)S(1)}, u32[]{:S(2)}, u32[]{:S(2)}) collective-permute-start(bf16[256,256]{1,0:T(8,128)(2,1)S(1)} %pack_borders.1._), channel_id=1, source_target_pairs={{0,4},{4,8},{8,12},{12,16},{16,20},{20,24},{24,28},{28,0},{1,5},{5... | collective-permute-start | bytes 393224 | tf_op jit(solution)/shard_map/ppermute | solution.py:30
  4.6 2.7 %load_all.1 = (bf16[512,256]{1,0:T(8,128)(2,1)S(1)}, f32[512,256]{1,0:T(8,128)S(1)}, bf16[512,256]{1,0:T(8,128)(2,1)S(1)}, bf16[16,128]{1,0:T(8,128)(2,1)S(1)}, ...) custom-call(bf16[512,256]{1,0:T(8,128)(2,1)} %bitcast.5, bf16[512,256]{1,0:T(8,128)(2,1)} %bitcast.7, ...), custom_call_target="tpu_custom_call" | custom-call | flops 10000000 | bytes 6000000 | tf_op jit(solution)/shard_map/load_all/pallas_call | solution.py:91
  7.3 3.9 %collective-permute-done.prev_rows = bf16[256,256]{1,0:T(8,128)(2,1)S(1)} collective-permute-done((bf16[256,256]{1,0:T(8,128)(2,1)S(1)}, bf16[256,256]{1,0:T(8,128)(2,1)S(1)}, u32[]{:S(2)}, u32[]{:S(2)}) %collective-permute-start) | collective-permute-done | bytes 131104 | tf_op jit(solution)/shard_map/ppermute | solution.py:30
  11.1 5.5 %forward_and_last_third.1 = (bf16[4,640,256]{2,1,0:T(8,128)(2,1)S(1)}, bf16[4,640,256]{2,1,0:T(8,128)(2,1)S(1)}, bf16[4,640,512]{2,1,0:T(8,128)(2,1)S(1)}, bf16[...) custom-call(bf16[256,256]{1,0:T(8,128)(2,1)S(1)} %collective-permute, ...), custom_call_target="tpu_custom_call" | custom-call | flops 3623878656 | bytes 4718592 | tf_op jit(solution)/shard_map/forward_and_last_third/pallas_call | solution.py:328
  16.6 0.1 collective-permute-start.1
  16.7 1.9 %middle_third.1 = (f32[576,256]{1,0:T(8,128)S(1)}, bf16[2,2,2,2,192,128]{5,4,3,2,1,0:T(8,128)(2,1)S(1)}, bf16[2,2,2,2,192,128]{5,4,3,2,1,0:T(8,128)(2,1)S(1)}) custom-call(bf16[4,640,256]{2,1,0:T(8,128)(2,1)S(1)} %get-tuple-element.33.present, bf16[4,640,256]{2,1,0:T(8,128)(2,1)S(1)} %get-tuple-element.34.earlier, ...), custom_call_target="tpu_custom_call" | custom-call | flops 1610612736 | bytes 4718592 | tf_op jit(solution)/shard_map/middle_third/pallas_call | solution.py:355
  18.6 0.6 %collective-permute-start.7 = (bf16[2,2,2,2,192,128]{5,4,3,2,1,0:T(8,128)(2,1)S(1)}, bf16[2,2,2,2,192,128]{5,4,3,2,1,0:T(8,128)(2,1)S(1)}, u32[]{:S(2)}, u32[]{:S(2)}) collective-permute-start(bf16[2,2,2,2,192,128]{5,4,3,2,1,0:T(8,128)(2,1)S(1)} %get-tuple-element.45), channel_id=1, source_target_pairs={{0,1},{1,0},{2,3},{3,2},{4,5},{5,4},{6,7},{7,6},{8,9},{9,8},{10,11... | collective-permute-start | bytes 2359304 | tf_op jit(solution)/shard_map/ppermute | solution.py:477
  19.2 0.0 collective-permute-done.1.refs_1_.refs_13_
  19.2 0.1 add_chunk0_step1.1.rest_0_
  19.3 1.9 %first_third.1 = (bf16[64,256]{1,0:T(8,128)(2,1)S(1)}, f32[448,256]{1,0:T(8,128)S(1)}, bf16[2,2,2,2,192,128]{5,4,3,2,1,0:T(8,128)(2,1)S(1)}, bf16[2,2,2,2,192,128]{5,4,3,2,1,0:T(8,128)(2,1)S(1)}) custom-call(bf16[4,640,256]{2,1,0:T(8,128)(2,1)S(1)} %get-tuple-element.33.present, bf16[4,640,256]{2,1,0:T(8,128)(2,1)S(1)} %get-tuple-element.34.earlier, ...), custom_call_target="tpu_custom_call" | custom-call | flops 1610612736 | bytes 4718592 | tf_op jit(solution)/shard_map/first_third/pallas_call | solution.py:355
  21.2 0.1 collective-permute-start.2
  21.3 1.6 %collective-permute-start.12 = (bf16[2,2,2,208,128]{4,3,2,1,0:T(8,128)(2,1)S(1)}, bf16[2,2,2,208,128]{4,3,2,1,0:T(8,128)(2,1)S(1)}, u32[]{:S(2)}, u32[]{:S(2)}) collective-permute-start(bf16[2,2,2,208,128]{4,3,2,1,0:T(8,128)(2,1)S(1)} %add_chunk0_step1.1.rest_0_), channel_id=1, source_target_pairs={{0,2},{1,3},{2,0},{3,1},{4,6},{5,7},{6,4},{7,5},{8,10},{9,11},{10,... | collective-permute-start | bytes 1277960 | tf_op jit(solution)/shard_map/ppermute | solution.py:477
  22.9 0.0 collective-permute-done.7.refs_1_.refs_7_
  22.9 0.1 add_chunk1_step1.1
  23.0 0.1 collective-permute-start.8
  23.0 0.5 collective-permute-done.2.refs_1_
  23.6 0.1 add_chunk2_step1.1
  23.7 0.1 collective-permute-start.3
  23.7 3.1 %collective-permute-start.13 = (bf16[64,256]{1,0:T(8,128)(2,1)S(1)}, bf16[64,256]{1,0:T(8,128)(2,1)S(1)}, u32[]{:S(2)}, u32[]{:S(2)}) collective-permute-start(bf16[64,256]{1,0:T(8,128)(2,1)S(1)} %get-tuple-element.46), channel_id=1, source_target_pairs={{0,28},{4,0},{8,4},{12,8},{16,12},{20,16},{24,20},{28,24},{1,29},{... | collective-permute-start | bytes 98312 | tf_op jit(solution)/shard_map/ppermute | solution.py:30
  26.8 8.1 %collective-permute-done.13.refs_3_.refs_18_ = bf16[64,256]{1,0:T(8,128)(2,1)S(1)} collective-permute-done((bf16[64,256]{1,0:T(8,128)(2,1)S(1)}, bf16[64,256]{1,0:T(8,128)(2,1)S(1)}, u32[]{:S(2)}, u32[]{:S(2)}) %collective-permute-start.13) | collective-permute-done | bytes 32800 | tf_op jit(solution)/shard_map/ppermute | solution.py:30
  34.9 0.0 collective-permute-done.12.refs_2_.refs_14_
  34.9 0.1 add_chunk0_step2.1
  35.0 2.2 %collective-permute-start.14 = (bf16[2,2,208,128]{3,2,1,0:T(8,128)(2,1)S(1)}, bf16[2,2,208,128]{3,2,1,0:T(8,128)(2,1)S(1)}, u32[]{:S(2)}, u32[]{:S(2)}) collective-permute-start(bf16[2,2,208,128]{3,2,1,0:T(8,128)(2,1)S(1)} %add_chunk0_step2.1), channel_id=1, source_target_pairs={{0,4},{1,5},{2,6},{3,7},{4,0},{5,1},{6,2},{7,3},{8,12},{9,13},{10,... | collective-permute-start | bytes 638984 | tf_op jit(solution)/shard_map/ppermute | solution.py:477
  37.2 0.0 collective-permute-done.8.refs_2_.refs_8_
  37.2 0.1 add_chunk1_step2.1
  37.3 0.1 collective-permute-start.9
  37.4 0.0 collective-permute-done.3.refs_2_
  37.4 0.1 add_chunk2_step2.1
  37.5 1.6 %collective-permute-start.4 = (bf16[2,2,192,128]{3,2,1,0:T(8,128)(2,1)S(1)}, bf16[2,2,192,128]{3,2,1,0:T(8,128)(2,1)S(1)}, u32[]{:S(2)}, u32[]{:S(2)}) collective-permute-start(bf16[2,2,192,128]{3,2,1,0:T(8,128)(2,1)S(1)} %add_chunk2_step2.1), channel_id=1, source_target_pairs={{0,2},{1,3},{2,0},{3,1},{4,6},{5,7},{6,4},{7,5},{8,10},{9,11},{10,... | collective-permute-start | bytes 589832 | tf_op jit(solution)/shard_map/ppermute | solution.py:477
  39.0 2.6 %collective-permute-done.14.refs_3_.refs_15_ = bf16[2,2,208,128]{3,2,1,0:T(8,128)(2,1)S(1)} collective-permute-done((bf16[2,2,208,128]{3,2,1,0:T(8,128)(2,1)S(1)}, bf16[2,2,208,128]{3,2,1,0:T(8,128)(2,1)S(1)}, u32[]{:S(2)}, u32[]{:S(2)}) %collective-permute-start.14) | collective-permute-done | bytes 213024 | tf_op jit(solution)/shard_map/ppermute | solution.py:477
  41.6 0.1 add_chunk0_step3.1
  41.7 0.2 collective-permute-start.15
  41.9 1.4 %collective-permute-done.9.refs_3_.refs_9_ = bf16[2,2,192,128]{3,2,1,0:T(8,128)(2,1)S(1)} collective-permute-done((bf16[2,2,192,128]{3,2,1,0:T(8,128)(2,1)S(1)}, bf16[2,2,192,128]{3,2,1,0:T(8,128)(2,1)S(1)}, u32[]{:S(2)}, u32[]{:S(2)}) %collective-permute-start.9) | collective-permute-done | bytes 196640 | tf_op jit(solution)/shard_map/ppermute | solution.py:477
  43.2 0.1 add_chunk1_step3.1
  43.3 1.6 %collective-permute-start.10 = (bf16[2,192,128]{2,1,0:T(8,128)(2,1)S(1)}, bf16[2,192,128]{2,1,0:T(8,128)(2,1)S(1)}, u32[]{:S(2)}, u32[]{:S(2)}) collective-permute-start(bf16[2,192,128]{2,1,0:T(8,128)(2,1)S(1)} %add_chunk1_step3.1), channel_id=1, source_target_pairs={{0,2},{1,3},{2,0},{3,1},{4,6},{5,7},{6,4},{7,5},{8,10},{9,11},{10,... | collective-permute-start | bytes 294920 | tf_op jit(solution)/shard_map/ppermute | solution.py:477
  44.9 0.0 collective-permute-done.4.refs_3_
  44.9 0.1 add_chunk2_step3.1
  44.9 0.4 collective-permute-start.5
  45.3 1.2 %collective-permute-done.15.refs_4_.refs_16_ = bf16[2,208,128]{2,1,0:T(8,128)(2,1)S(1)} collective-permute-done((bf16[2,208,128]{2,1,0:T(8,128)(2,1)S(1)}, bf16[2,208,128]{2,1,0:T(8,128)(2,1)S(1)}, u32[]{:S(2)}, u32[]{:S(2)}) %collective-permute-start.15) | collective-permute-done | bytes 106528 | tf_op jit(solution)/shard_map/ppermute | solution.py:477
  46.5 0.1 add_chunk0_step4.1
  46.5 1.8 %collective-permute-start.16 = (bf16[208,128]{1,0:T(8,128)(2,1)S(1)}, bf16[208,128]{1,0:T(8,128)(2,1)S(1)}, u32[]{:S(2)}, u32[]{:S(2)}) collective-permute-start(bf16[208,128]{1,0:T(8,128)(2,1)S(1)} %add_chunk0_step4.1), channel_id=1, source_target_pairs={{0,16},{1,17},{2,18},{3,19},{4,20},{5,21},{6,22},{7,23},{8,24},{9,... | collective-permute-start | bytes 159752 | tf_op jit(solution)/shard_map/ppermute | solution.py:477
  48.4 0.0 collective-permute-done.10.refs_4_.refs_10_
  48.4 1.3 %collective-permute-start.11 = (bf16[192,128]{1,0:T(8,128)(2,1)S(1)}, bf16[192,128]{1,0:T(8,128)(2,1)S(1)}, u32[]{:S(2)}, u32[]{:S(2)}) collective-permute-start(bf16[192,128]{1,0:T(8,128)(2,1)S(1)} %add_chunk1_step4.1), channel_id=1, source_target_pairs={{0,16},{1,17},{2,18},{3,19},{4,20},{5,21},{6,22},{7,23},{8,24},{9,... | collective-permute-start | bytes 147464 | tf_op jit(solution)/shard_map/ppermute | solution.py:477
  49.6 0.0 collective-permute-done.5.refs_4_
  49.7 1.8 %collective-permute-start.6 = (bf16[192,128]{1,0:T(8,128)(2,1)S(1)}, bf16[192,128]{1,0:T(8,128)(2,1)S(1)}, u32[]{:S(2)}, u32[]{:S(2)}) collective-permute-start(bf16[192,128]{1,0:T(8,128)(2,1)S(1)} %add_chunk2_step4.1), channel_id=1, source_target_pairs={{0,16},{1,17},{2,18},{3,19},{4,20},{5,21},{6,22},{7,23},{8,24},{9,... | collective-permute-start | bytes 147464 | tf_op jit(solution)/shard_map/ppermute | solution.py:477
  51.5 2.0 %collective-permute-done.11.refs_11_ = bf16[192,128]{1,0:T(8,128)(2,1)S(1)} collective-permute-done((bf16[192,128]{1,0:T(8,128)(2,1)S(1)}, bf16[192,128]{1,0:T(8,128)(2,1)S(1)}, u32[]{:S(2)}, u32[]{:S(2)}) %collective-permute-start.11) | collective-permute-done | bytes 49184 | tf_op jit(solution)/shard_map/ppermute | solution.py:477
  53.4 0.0 collective-permute-done.16.refs_17_
  53.4 1.3 %collective-permute-done.6.refs_5_ = bf16[192,128]{1,0:T(8,128)(2,1)S(1)} collective-permute-done((bf16[192,128]{1,0:T(8,128)(2,1)S(1)}, bf16[192,128]{1,0:T(8,128)(2,1)S(1)}, u32[]{:S(2)}, u32[]{:S(2)}) %collective-permute-start.6) | collective-permute-done | bytes 49184 | tf_op jit(solution)/shard_map/ppermute | solution.py:477
  54.8 1.0 %scale_all.1 = (f32[512,256]{1,0:T(8,128)}, f32[6,64,128]{2,1,0:T(8,128)}, f32[6,32,128]{2,1,0:T(8,128)}) custom-call(bf16[2,2,2,2,192,128]{5,4,3,2,1,0:T(8,128)(2,1)S(1)} %get-tuple-element.42.refs_0_, bf16[2,2,2,2,192,128]{5,4,3,2,1,0:T(8,128)(2,1)S(1)} %collective-permute-done.2.refs_1_, bf16[2,2,2,192,128]{4,3,2,1,0:T(8,128)(2,1)S(1)} %collective-permute-done.3.refs_2_, ...), custom_call_target="tpu_custom_call" | custom-call | tf_op jit(solution)/shard_map/scale_all/pallas_call | solution.py:513
  (2 shorter events, 0.1 us)
Async XLA Ops:
  1.6 9.5 %collective-permute-start = (bf16[256,256]{1,0:T(8,128)(2,1)S(1)}, bf16[256,256]{1,0:T(8,128)(2,1)S(1)}, u32[]{:S(2)}, u32[]{:S(2)}) collective-permute-start(bf16[256,256]{1,0:T(8,128)(2,1)S(1)} %pack_borders.1._), channel_id=1, source_target_pairs={{0,4},{4,8},{8,12},{12,16},{16,20},{20,24},{24,28},{28,0},{1,5},{5... | collective-permute-start | bytes 393224 | tf_op jit(solution)/shard_map/ppermute | solution.py:30
  16.6 2.6 %collective-permute-start.1 = (bf16[2,2,2,2,208,128]{5,4,3,2,1,0:T(8,128)(2,1)S(1)}, bf16[2,2,2,2,208,128]{5,4,3,2,1,0:T(8,128)(2,1)S(1)}, u32[]{:S(2)}, u32[]{:S(2)}) collective-permute-start(bf16[2,2,2,2,208,128]{5,4,3,2,1,0:T(8,128)(2,1)S(1)} %get-tuple-element.41), channel_id=1, source_target_pairs={{0,1},{1,0},{2,3},{3,2},{4,5},{5,4},{6,7},{7,6},{8,9},{9,8},{10,11... | collective-permute-start | bytes 2555912 | tf_op jit(solution)/shard_map/ppermute | solution.py:477
  18.6 4.3 %collective-permute-start.7 = (bf16[2,2,2,2,192,128]{5,4,3,2,1,0:T(8,128)(2,1)S(1)}, bf16[2,2,2,2,192,128]{5,4,3,2,1,0:T(8,128)(2,1)S(1)}, u32[]{:S(2)}, u32[]{:S(2)}) collective-permute-start(bf16[2,2,2,2,192,128]{5,4,3,2,1,0:T(8,128)(2,1)S(1)} %get-tuple-element.45), channel_id=1, source_target_pairs={{0,1},{1,0},{2,3},{3,2},{4,5},{5,4},{6,7},{7,6},{8,9},{9,8},{10,11... | collective-permute-start | bytes 2359304 | tf_op jit(solution)/shard_map/ppermute | solution.py:477
  21.2 2.4 %collective-permute-start.2 = (bf16[2,2,2,2,192,128]{5,4,3,2,1,0:T(8,128)(2,1)S(1)}, bf16[2,2,2,2,192,128]{5,4,3,2,1,0:T(8,128)(2,1)S(1)}, u32[]{:S(2)}, u32[]{:S(2)}) collective-permute-start(bf16[2,2,2,2,192,128]{5,4,3,2,1,0:T(8,128)(2,1)S(1)} %get-tuple-element.43), channel_id=1, source_target_pairs={{0,1},{1,0},{2,3},{3,2},{4,5},{5,4},{6,7},{7,6},{8,9},{9,8},{10,11... | collective-permute-start | bytes 2359304 | tf_op jit(solution)/shard_map/ppermute | solution.py:477
  21.3 13.6 %collective-permute-start.12 = (bf16[2,2,2,208,128]{4,3,2,1,0:T(8,128)(2,1)S(1)}, bf16[2,2,2,208,128]{4,3,2,1,0:T(8,128)(2,1)S(1)}, u32[]{:S(2)}, u32[]{:S(2)}) collective-permute-start(bf16[2,2,2,208,128]{4,3,2,1,0:T(8,128)(2,1)S(1)} %add_chunk0_step1.1.rest_0_), channel_id=1, source_target_pairs={{0,2},{1,3},{2,0},{3,1},{4,6},{5,7},{6,4},{7,5},{8,10},{9,11},{10,... | collective-permute-start | bytes 1277960 | tf_op jit(solution)/shard_map/ppermute | solution.py:477
  23.0 14.2 %collective-permute-start.8 = (bf16[2,2,2,192,128]{4,3,2,1,0:T(8,128)(2,1)S(1)}, bf16[2,2,2,192,128]{4,3,2,1,0:T(8,128)(2,1)S(1)}, u32[]{:S(2)}, u32[]{:S(2)}) collective-permute-start(bf16[2,2,2,192,128]{4,3,2,1,0:T(8,128)(2,1)S(1)} %add_chunk1_step1.1), channel_id=1, source_target_pairs={{0,4},{1,5},{2,6},{3,7},{4,0},{5,1},{6,2},{7,3},{8,12},{9,13},{10,... | collective-permute-start | bytes 1179656 | tf_op jit(solution)/shard_map/ppermute | solution.py:477
  23.7 13.7 %collective-permute-start.3 = (bf16[2,2,2,192,128]{4,3,2,1,0:T(8,128)(2,1)S(1)}, bf16[2,2,2,192,128]{4,3,2,1,0:T(8,128)(2,1)S(1)}, u32[]{:S(2)}, u32[]{:S(2)}) collective-permute-start(bf16[2,2,2,192,128]{4,3,2,1,0:T(8,128)(2,1)S(1)} %add_chunk2_step1.1), channel_id=1, source_target_pairs={{0,8},{1,9},{2,10},{3,11},{4,12},{5,13},{6,14},{7,15},{8,0},{9,1},... | collective-permute-start | bytes 1179656 | tf_op jit(solution)/shard_map/ppermute | solution.py:477
  23.7 11.2 %collective-permute-start.13 = (bf16[64,256]{1,0:T(8,128)(2,1)S(1)}, bf16[64,256]{1,0:T(8,128)(2,1)S(1)}, u32[]{:S(2)}, u32[]{:S(2)}) collective-permute-start(bf16[64,256]{1,0:T(8,128)(2,1)S(1)} %get-tuple-element.46), channel_id=1, source_target_pairs={{0,28},{4,0},{8,4},{12,8},{16,12},{20,16},{24,20},{28,24},{1,29},{... | collective-permute-start | bytes 98312 | tf_op jit(solution)/shard_map/ppermute | solution.py:30
  35.0 6.6 %collective-permute-start.14 = (bf16[2,2,208,128]{3,2,1,0:T(8,128)(2,1)S(1)}, bf16[2,2,208,128]{3,2,1,0:T(8,128)(2,1)S(1)}, u32[]{:S(2)}, u32[]{:S(2)}) collective-permute-start(bf16[2,2,208,128]{3,2,1,0:T(8,128)(2,1)S(1)} %add_chunk0_step2.1), channel_id=1, source_target_pairs={{0,4},{1,5},{2,6},{3,7},{4,0},{5,1},{6,2},{7,3},{8,12},{9,13},{10,... | collective-permute-start | bytes 638984 | tf_op jit(solution)/shard_map/ppermute | solution.py:477
  37.3 6.0 %collective-permute-start.9 = (bf16[2,2,192,128]{3,2,1,0:T(8,128)(2,1)S(1)}, bf16[2,2,192,128]{3,2,1,0:T(8,128)(2,1)S(1)}, u32[]{:S(2)}, u32[]{:S(2)}) collective-permute-start(bf16[2,2,192,128]{3,2,1,0:T(8,128)(2,1)S(1)} %add_chunk1_step2.1), channel_id=1, source_target_pairs={{0,8},{1,9},{2,10},{3,11},{4,12},{5,13},{6,14},{7,15},{8,0},{9,1},... | collective-permute-start | bytes 589832 | tf_op jit(solution)/shard_map/ppermute | solution.py:477
  37.5 7.4 %collective-permute-start.4 = (bf16[2,2,192,128]{3,2,1,0:T(8,128)(2,1)S(1)}, bf16[2,2,192,128]{3,2,1,0:T(8,128)(2,1)S(1)}, u32[]{:S(2)}, u32[]{:S(2)}) collective-permute-start(bf16[2,2,192,128]{3,2,1,0:T(8,128)(2,1)S(1)} %add_chunk2_step2.1), channel_id=1, source_target_pairs={{0,2},{1,3},{2,0},{3,1},{4,6},{5,7},{6,4},{7,5},{8,10},{9,11},{10,... | collective-permute-start | bytes 589832 | tf_op jit(solution)/shard_map/ppermute | solution.py:477
  41.7 4.8 %collective-permute-start.15 = (bf16[2,208,128]{2,1,0:T(8,128)(2,1)S(1)}, bf16[2,208,128]{2,1,0:T(8,128)(2,1)S(1)}, u32[]{:S(2)}, u32[]{:S(2)}) collective-permute-start(bf16[2,208,128]{2,1,0:T(8,128)(2,1)S(1)} %add_chunk0_step3.1), channel_id=1, source_target_pairs={{0,8},{1,9},{2,10},{3,11},{4,12},{5,13},{6,14},{7,15},{8,0},{9,1},... | collective-permute-start | bytes 319496 | tf_op jit(solution)/shard_map/ppermute | solution.py:477
  43.3 5.1 %collective-permute-start.10 = (bf16[2,192,128]{2,1,0:T(8,128)(2,1)S(1)}, bf16[2,192,128]{2,1,0:T(8,128)(2,1)S(1)}, u32[]{:S(2)}, u32[]{:S(2)}) collective-permute-start(bf16[2,192,128]{2,1,0:T(8,128)(2,1)S(1)} %add_chunk1_step3.1), channel_id=1, source_target_pairs={{0,2},{1,3},{2,0},{3,1},{4,6},{5,7},{6,4},{7,5},{8,10},{9,11},{10,... | collective-permute-start | bytes 294920 | tf_op jit(solution)/shard_map/ppermute | solution.py:477
  44.9 4.7 %collective-permute-start.5 = (bf16[2,192,128]{2,1,0:T(8,128)(2,1)S(1)}, bf16[2,192,128]{2,1,0:T(8,128)(2,1)S(1)}, u32[]{:S(2)}, u32[]{:S(2)}) collective-permute-start(bf16[2,192,128]{2,1,0:T(8,128)(2,1)S(1)} %add_chunk2_step3.1), channel_id=1, source_target_pairs={{0,4},{1,5},{2,6},{3,7},{4,0},{5,1},{6,2},{7,3},{8,12},{9,13},{10,... | collective-permute-start | bytes 294920 | tf_op jit(solution)/shard_map/ppermute | solution.py:477
  46.5 6.9 %collective-permute-start.16 = (bf16[208,128]{1,0:T(8,128)(2,1)S(1)}, bf16[208,128]{1,0:T(8,128)(2,1)S(1)}, u32[]{:S(2)}, u32[]{:S(2)}) collective-permute-start(bf16[208,128]{1,0:T(8,128)(2,1)S(1)} %add_chunk0_step4.1), channel_id=1, source_target_pairs={{0,16},{1,17},{2,18},{3,19},{4,20},{5,21},{6,22},{7,23},{8,24},{9,... | collective-permute-start | bytes 159752 | tf_op jit(solution)/shard_map/ppermute | solution.py:477
  48.4 5.1 %collective-permute-start.11 = (bf16[192,128]{1,0:T(8,128)(2,1)S(1)}, bf16[192,128]{1,0:T(8,128)(2,1)S(1)}, u32[]{:S(2)}, u32[]{:S(2)}) collective-permute-start(bf16[192,128]{1,0:T(8,128)(2,1)S(1)} %add_chunk1_step4.1), channel_id=1, source_target_pairs={{0,16},{1,17},{2,18},{3,19},{4,20},{5,21},{6,22},{7,23},{8,24},{9,... | collective-permute-start | bytes 147464 | tf_op jit(solution)/shard_map/ppermute | solution.py:477
  49.7 5.1 %collective-permute-start.6 = (bf16[192,128]{1,0:T(8,128)(2,1)S(1)}, bf16[192,128]{1,0:T(8,128)(2,1)S(1)}, u32[]{:S(2)}, u32[]{:S(2)}) collective-permute-start(bf16[192,128]{1,0:T(8,128)(2,1)S(1)} %add_chunk2_step4.1), channel_id=1, source_target_pairs={{0,16},{1,17},{2,18},{3,19},{4,20},{5,21},{6,22},{7,23},{8,24},{9,... | collective-permute-start | bytes 147464 | tf_op jit(solution)/shard_map/ppermute | solution.py:477

commit v13 on v12

--- a/solution.py
+++ b/solution.py
@@ -38,30 +38,30 @@
     return pl.CostEstimate(flops=flops, bytes_accessed=moved, transcendentals=0)
 
 
-def pack_kernel(tail_x, tail_gs, tail_gk, weight, message):
-    halo, channels = tail_gs.shape
-    by_row = column(weight[...], LANES)[LANES - halo :]
+def pack_kernel(head_x, tail_x, head_gs, head_gk, weight, for_next, for_prev):
+    halo, channels = head_x.shape
+    by_row = column(weight[...], LANES)[:halo]
     by_row = jnp.concatenate([by_row] * (channels // LANES), axis=1)
-    message[0 : 2 * halo] = tail_x[...]
-    message[2 * halo : 3 * halo] = (tail_gs[...].astype(jnp.float32) * by_row).astype(jnp.bfloat16)
-    message[3 * halo :] = (tail_gk[...].astype(jnp.float32) * by_row).astype(jnp.bfloat16)
+    for_next[...] = tail_x[...]
+    for_prev[0:halo] = head_x[...]
+    for_prev[halo : 2 * halo] = (head_gs[...].astype(jnp.float32) * by_row).astype(jnp.bfloat16)
+    for_prev[2 * halo :] = (head_gk[...].astype(jnp.float32) * by_row).astype(jnp.bfloat16)
 
 
 def pack(halo, x, grad_stream_out, grad_skip_out, weight):
     length, channels = x.shape
-
-    def last(rows):
-        return pl.BlockSpec((rows, channels), lambda i: (length // rows - 1, 0))
-
+    first = pl.BlockSpec((halo, channels), lambda i: (0, 0))
+    last = pl.BlockSpec((halo, channels), lambda i: (length // halo - 1, 0))
+    shapes = [(halo, channels), (3 * halo, channels)]
     return pl.pallas_call(
         pack_kernel,
         grid=(1,),
-        in_specs=[last(2 * halo), last(halo), last(halo), pl.BlockSpec((1, LANES), lambda i: (0, length // LANES - 1))],
-        out_specs=pl.BlockSpec((4 * halo, channels), lambda i: (0, 0)),
-        out_shape=jax.ShapeDtypeStruct((4 * halo, channels), jnp.bfloat16),
+        in_specs=[first, last, first, first, pl.BlockSpec((1, LANES), lambda i: (0, 0))],
+        out_specs=[pl.BlockSpec(shape, lambda i: (0, 0)) for shape in shapes],
+        out_shape=[jax.ShapeDtypeStruct(shape, jnp.bfloat16) for shape in shapes],
         compiler_params=pltpu.CompilerParams(vmem_limit_bytes=ADD_BYTES),
         name="pack_borders",
-    )(*held((x, grad_stream_out, grad_skip_out, weight), pltpu.HBM))
+    )(*held((x, x, grad_stream_out, grad_skip_out, weight), pltpu.HBM))
 
 
 def load_kernel(
@@ -125,21 +125,10 @@
     return jnp.sum(rows.astype(jnp.float32), axis=0, keepdims=True)
 
 
-def cut_off(rows, dilation):
-    row = lax.broadcasted_iota(jnp.int32, rows.shape, 0)
-    return jnp.where(jnp.logical_and(row < dilation, lax.axis_index("tm") == 0), 0.0, rows)
-
-
 def items_of(layers, chunk):
     third = layers // len(CHAINS)
     high = layers - chunk * third
     return [(index, is_out) for index in reversed(range(high - third, high)) for is_out in (False, True)]
-
-
-def earlier_rows(plan, index, present, first, last):
-    dilation, begin = 2**index, 2 * plan["halo"]
-    cut = cut_off(present[begin - dilation : begin], dilation)
-    return jnp.concatenate([present[first - dilation : begin - dilation], cut, present[begin : last - dilation]])
 
 
 def backward(plan, layers, refs_of, conv_w, out_w, grad_proj, grad_stream, past_part, grad_parts):
@@ -160,17 +149,15 @@
         ).astype(jnp.bfloat16)
         spread = dot(grad_preact, conv_w[index], NT)
         past_part[0:count] = spread[:, channels:]
-        cut = slice(halo, halo + max(dilation, 8))
-        past_part[cut] = cut_off(past_part[cut], dilation)
         rows = plan["counts"][index - 1] if index else length
         grad_stream[0:rows] += spread[0:rows, :channels] + past_part[dilation : dilation + rows]
-        past = earlier_rows(plan, index, present, halo, halo + length) if earlier is None else earlier[own]
+        past = present[halo - dilation : halo + length - dilation] if earlier is None else earlier[own]
         total = dot(jnp.concatenate([present[own], past], axis=1), grad_preact[0:length], TN)
         plan["store"](total, items.index((index, False)), grad_parts)
 
 
 def first_kernel(
-    plan, prev_rows, own_x, own_grad, own_skip, sums, conv_w, out_w,
+    plan, prev_rows, next_rows, own_x, own_grad, own_skip, sums, conv_w, out_w,
     low_present, low_earlier, low_factors, low_gates, grad_stream, grad_skip, *rest,
 ):
     *grad_parts, stream, high_present, high_factors, high_gates, grad_proj, past_part = rest
@@ -178,10 +165,17 @@
     layers, low = conv_w.shape[0], low_gates.shape[0]
     pad = 2 ** (layers - 1)
     extent = length + 2 * halo
-    begin = 2 * halo
+    at = lax.axis_index("tm")
+
+    def unless(is_end, rows):
+        return jnp.where(is_end, jnp.zeros_like(rows), rows)
+
+    before = unless(at == 0, prev_rows[...])
+    after = unless(at == lax.axis_size("tm") - 1, next_rows[...])
     stream[0:pad] = jnp.zeros((pad, channels), jnp.float32)
-    stream[pad : pad + begin] = prev_rows[0:begin].astype(jnp.float32)
-    stream[pad + begin :] = own_x[...].astype(jnp.float32)
+    stream[pad : pad + halo] = before.astype(jnp.float32)
+    stream[pad + halo : pad + halo + length] = own_x[...].astype(jnp.float32)
+    stream[pad + halo + length :] = after[0:halo].astype(jnp.float32)
 
     def refs_of(index):
         if index < low:
@@ -189,17 +183,16 @@
         at = index - low
         return high_present.at[at], None, high_factors.at[at], high_gates.at[at]
 
-    refs_of(0)[0][0:begin] = prev_rows[0:begin]
-    refs_of(0)[0][begin:] = own_x[...]
+    refs_of(0)[0][0:halo] = before
+    refs_of(0)[0][halo : halo + length] = own_x[...]
+    refs_of(0)[0][halo + length :] = after[0:halo]
     for index in range(layers):
         dilation, start = 2**index, plan["starts"][index]
         present, earlier, factor, gate = refs_of(index)
         if earlier is None:
-            past = earlier_rows(plan, index, present, start, extent)
+            past = present[start - dilation : extent - dilation]
         else:
-            past = stream[pad + start - dilation : pad + extent - dilation]
-            cut = cut_off(past[begin - start : begin - start + 16], dilation)
-            past = jnp.concatenate([past[: begin - start], cut, past[begin - start + 16 :]]).astype(jnp.bfloat16)
+            past = stream[pad + start - dilation : pad + extent - dilation].astype(jnp.bfloat16)
             earlier[start:] = past
         preact = dot(jnp.concatenate([present[start:], past], axis=1), conv_w[index], NN)
         filtered = jnp.tanh(preact[:, :channels])
@@ -210,15 +203,15 @@
         factor[start:, :channels] = (opening - filtered * product).astype(jnp.bfloat16)
         factor[start:, channels:] = (product * (1.0 - opening)).astype(jnp.bfloat16)
         if index < layers - 1:
-            after = stream[pad + start :] + dot(gated, out_w[index, :, :channels], NN)
-            refs_of(index + 1)[0][start:] = after.astype(jnp.bfloat16)
+            moved_on = stream[pad + start :] + dot(gated, out_w[index, :, :channels], NN)
+            refs_of(index + 1)[0][start:] = moved_on.astype(jnp.bfloat16)
             if index < layers - 2:
-                stream[pad + start :] = after
-
-    grad_stream[0:halo] = prev_rows[2 * halo : 3 * halo].astype(jnp.float32)
-    grad_stream[halo:] = own_grad[...]
-    grad_skip[0:halo] = prev_rows[3 * halo :]
-    grad_skip[halo:] = own_skip[...]
+                stream[pad + start :] = moved_on
+
+    grad_stream[0:length] = own_grad[...]
+    grad_stream[length:] = after[halo : 2 * halo].astype(jnp.float32)
+    grad_skip[0:length] = own_skip[...]
+    grad_skip[length:] = after[2 * halo :]
     grad_proj[:, channels:] = grad_skip[...]
     backward(
         plan, list(reversed(range(low, layers))), refs_of, conv_w, out_w, grad_proj, grad_stream, past_part, grad_parts
@@ -229,7 +222,7 @@
 def later_kernel(
     plan, first, third, present, earlier, factors, gates, grad_before, grad_skip, conv_w, out_w, *rest
 ):
-    *outs, keep, send, grad_stream, grad_proj, past_part = rest[plan["unused"] :]
+    grad_after, keep, send, grad_stream, grad_proj, past_part = rest[plan["unused"] :]
     channels = plan["channels"]
     grad_stream[...] = grad_before[...]
     grad_proj[:, channels:] = grad_skip[...]
@@ -241,10 +234,7 @@
         plan, list(reversed(range(first, first + third))), refs_of, conv_w, out_w,
         grad_proj, grad_stream, past_part, (keep, send),
     )
-    at = 0
-    for out in outs:
-        out[...] = grad_stream[at : at + out.shape[0]].astype(out.dtype)
-        at += out.shape[0]
+    grad_after[...] = grad_stream[0 : grad_after.shape[0]]
 
 
 def store_whole(items, total, item, grad_parts):
@@ -296,7 +286,7 @@
     return ends[:-1], ends[-1]
 
 
-def run_layers(in_shards, tm, dp, halo, prev_rows, loaded):
+def run_layers(in_shards, tm, dp, halo, borders, loaded):
     own_x, own_grad, own_skip, sums, conv_w, out_w = loaded
     length, channels = own_x.shape
     layers = conv_w.shape[0]
@@ -327,7 +317,7 @@
     flops = 2 * length * channels * channels
     *kept, grad_stream, grad_skip, keep, send = pl.pallas_call(
         functools.partial(first_kernel, plans[0]),
-        in_specs=[vmem] * 7,
+        in_specs=[vmem] * 8,
         out_specs=[vmem] * 8,
         out_shape=[
             pltpu.VMEM((low, extent, channels), jnp.bfloat16),
@@ -349,14 +339,14 @@
         compiler_params=pltpu.CompilerParams(vmem_limit_bytes=VMEM_BYTES),
         cost_estimate=cost(flops * (5 * layers + 12 * third), weight_bytes),
         name="forward_and_last_third",
-    )(*held((prev_rows, *loaded)))
-
-    def later(step, outs, after):
+    )(*held((*borders, *loaded)))
+
+    def later(step, rows, after):
         return pl.pallas_call(
             functools.partial(later_kernel, plans[step] | {"unused": len(after)}, layers - (step + 1) * third, third),
             in_specs=[vmem] * 8 + [anywhere] * len(after),
-            out_specs=[vmem] * (len(outs) + 2),
-            out_shape=[pltpu.VMEM((rows, channels), kind) for rows, kind in outs]
+            out_specs=[vmem] * 3,
+            out_shape=[pltpu.VMEM((rows, channels), jnp.float32)]
             + [pltpu.VMEM(shape, jnp.bfloat16) for shape in shapes[step]],
             scratch_shapes=[
                 pltpu.VMEM((border, channels), jnp.float32),
@@ -371,15 +361,13 @@
     parts = [(keep, send)]
     if in_shards:
         parts[0] = Chunk(tm, dp, 0, keep, send)
-    grad_stream, *middle = later(1, [(border, jnp.float32)], [])
-    other, own, *last = later(
-        2, [(halo, jnp.bfloat16), (length - halo, jnp.float32)], [parts[0].next_message()] if in_shards else []
-    )
+    grad_stream, *middle = later(1, border, [])
+    grad_in, *last = later(2, length, [parts[0].next_message()] if in_shards else [])
     parts += [middle, last]
     if in_shards:
         for step in (1, 2):
             parts[step] = Chunk(tm, dp, step, *parts[step])
-    return other, own, parts
+    return grad_in, parts
 
 
 def add_kernel(count, groups, *refs):
@@ -401,16 +389,16 @@
                 out[lead + (slice(first + body, first + rows),)] = jnp.broadcast_to(slab, out.shape[:-2] + slab.shape)
 
 
-def add_up(arrays, groups, shapes, after, name):
+def add_up(arrays, groups, shapes, name):
     vmem = pl.BlockSpec(memory_space=pltpu.VMEM)
     return pl.pallas_call(
         functools.partial(add_kernel, len(arrays), groups),
-        in_specs=[vmem] * len(arrays) + [pl.BlockSpec(memory_space=pl.ANY)] * len(after),
+        in_specs=[vmem] * len(arrays),
         out_specs=[vmem] * len(groups),
         out_shape=[pltpu.VMEM(shape, jnp.bfloat16) for shape in shapes],
         compiler_params=pltpu.CompilerParams(vmem_limit_bytes=ADD_BYTES),
         name=name,
-    )(*held(arrays), *held(after))
+    )(*held(arrays))
 
 
 def first_block(array, first, rows):
@@ -426,8 +414,8 @@
     for count in counts:
         chunks.insert(0, refs[:count])
         refs = refs[count:]
-    other, own, grad_inputs, grad_conv, grad_out = refs
-    layers, channels = grad_conv.shape[0], own.shape[1]
+    grad_in, grad_inputs, grad_conv, grad_out = refs
+    layers, channels = grad_conv.shape[0], grad_in.shape[1]
     total = 0.0
     for term in chunks[0]:
         total = total + jnp.sum(first_block(term, term.shape[-2] - 16, 16), axis=0, keepdims=True)
@@ -442,8 +430,7 @@
             out[index] = value * scale
     for first in range(0, channels, LANES):
         lanes = slice(first, first + LANES)
-        grad_inputs[0 : own.shape[0], lanes] = own[:, lanes] * scale
-        grad_inputs[own.shape[0] :, lanes] = other[:, lanes].astype(jnp.float32) * scale
+        grad_inputs[:, lanes] = grad_in[:, lanes] * scale
 
 
 class Chunk:
@@ -452,21 +439,21 @@
         self.message = None
         self.terms = [keep, swapped(tm, dp, send, "core")]
 
-    def next_message(self, after=()):
+    def next_message(self):
         if self.message is None:
             left = len(CHAINS[self.chunk]) + 2 - len(self.terms)
             pieces = []
             for i, v in enumerate(self.terms):
                 pieces.append((i, (0,) * (len(v.shape) - 2 - left) + (1,), 0))
             (self.message,) = add_up(
-                self.terms, [[(0, self.rows, EXTRA[self.chunk] > 0, pieces)]], [(2,) * (left - 1) + (self.rows, LANES)], after,
+                self.terms, [[(0, self.rows, EXTRA[self.chunk] > 0, pieces)]], [(2,) * (left - 1) + (self.rows, LANES)],
                 "add_chunk%d_step%d" % (self.chunk, len(self.terms) - 1),
             )
         return self.message
 
-    def run_chain(self, after=()):
-        for step, name in enumerate(CHAINS[self.chunk]):
-            self.terms.append(swapped(self.tm, self.dp, self.next_message(after if step == 1 else ()), name))
+    def run_chain(self):
+        for name in CHAINS[self.chunk]:
+            self.terms.append(swapped(self.tm, self.dp, self.next_message(), name))
             self.message = None
         return self.terms
 
@@ -490,12 +477,11 @@
     halo = 2**layers
     samples_all = batch * length * tm * dp
     x, gs, gk = inputs[0], grad_stream_out[0], grad_skip_out[0]
-    message = pack(halo, x, gs, gk, sample_weight)
-    prev_rows = around(message, "tm", 1)
-    loaded = load_all(x, gs, gk, sample_weight, conv_weight, out_weight, message)
+    for_next, for_prev = pack(halo, x, gs, gk, sample_weight)
+    borders = [around(for_next, "tm", 1), around(for_prev, "tm", -1)]
+    loaded = load_all(x, gs, gk, sample_weight, conv_weight, out_weight, for_next)
     in_shards = tm == 8 and dp == 4 and channels // tm % 16 == 0 and 2 * channels == dp * LANES
-    other, own, parts = run_layers(in_shards, tm, dp, halo, prev_rows, loaded)
-    other = around(other, "tm", -1)
+    grad_in, parts = run_layers(in_shards, tm, dp, halo, borders, loaded)
     if not in_shards:
         scale = samples_all / lax.psum(jnp.sum(sample_weight), ("tm", "dp"))
         found = {}
@@ -507,8 +493,8 @@
         grad_conv, grad_out = (
             scattered(jnp.stack([found[index, is_out] for index in range(layers)])) * scale for is_out in (False, True)
         )
-        return (jnp.concatenate([own, other]) * scale)[None], grad_conv, grad_out
-    chunks = [part.run_chain([other] if part is parts[0] else ()) for part in parts]
+        return (grad_in * scale)[None], grad_conv, grad_out
+    chunks = [part.run_chain() for part in parts]
     conv_rows, out_rows = 2 * channels // tm, channels // tm
     grad_inputs, grad_conv, grad_out = pl.pallas_call(
         functools.partial(last_kernel, [len(terms) for terms in reversed(chunks)], float(samples_all), tm),
@@ -519,7 +505,7 @@
         ],
         compiler_params=pltpu.CompilerParams(vmem_limit_bytes=ADD_BYTES),
         name="scale_all",
-    )(*held([term for terms in reversed(chunks) for term in terms]), *held([other, own]))
+    )(*held([term for terms in reversed(chunks) for term in terms]), *held([grad_in]))
     return grad_inputs[None], grad_conv, grad_out
 
 

time: 55.9 us -> 58.3 us (1.043)
  waiting for transfers between devices: 20.9 us -> 26.2 us
  starting transfers between devices: 19.3 us -> 16.5 us
    ppermute x15, waiting for transfers between devices: 8.93 us -> 22.2 us  [swapped(): return lax.ppermute(value, ('tm', 'dp'), pairs)]
    ppermute x2, waiting for transfers between devices: 12 us -> 3.93 us  [around(): return lax.ppermute(x, axis, [(i, (i + by) % count) for i in range(count)])]
    ppermute x15, starting transfers between devices: 13.3 us -> 10.5 us  [swapped(): return lax.ppermute(value, ('tm', 'dp'), pairs)]
  transfers between devices with their start and end apart: 17 -> 17, of which waited for: 8 -> 9; matrix products, arithmetic and copies ran while one was open for 0% -> 0% of each run, Pallas kernels for 13% -> 13%
where the time goes in v13:
time: 58.3 us; the launch traced here: 58.1 us
  waiting for transfers between devices  26.2 us (45%)
  starting transfers between devices  16.5 us (28%)
  Pallas kernels  14.7 us (25%)
  between operations  0.79 us (1%)
    ppermute x15, waiting for transfers between devices, swapped(): return lax.ppermute(value, ('tm', 'dp'), pairs)  22.2 us
    ppermute x15, starting transfers between devices, swapped(): return lax.ppermute(value, ('tm', 'dp'), pairs)  10.5 us
    ppermute x2, starting transfers between devices, around(): return lax.ppermute(x, axis, [(i, (i + by) % count) for i in range(count)])  6.03 us
    pallas_call x1, Pallas kernels, run_layers(): pl.pallas_call(functools.partial(first_kernel, plans[0]), in_specs=[vmem]...  5.46 us
    ppermute x2, waiting for transfers between devices, around(): return lax.ppermute(x, axis, [(i, (i + by) % count) for i in range(count)])  3.93 us
    pallas_call x2, Pallas kernels, later(): pl.pallas_call(functools.partial(later_kernel, plans[step] | {'unused': l...  3.85 us
    pallas_call x1, Pallas kernels, load_all(): pl.pallas_call(load_kernel, in_specs=[anywhere] * 7, out_specs=[vmem] * 6...  2.67 us
  transfers between devices with their start and end apart: 17, of which 9 were waited for; matrix products, arithmetic and copies ran while one was open for 0% of the time, Pallas kernels for 13%

profile of v13, /device:TPU:0, one launch (start us, length us, event | category | flops | bytes accessed | tf_op | source)
XLA Modules:
  0.0 58.1 jit_solution(3229707609124784965)
XLA Ops:
  0.6 0.9 %pack_borders.1 = (bf16[64,256]{1,0:T(8,128)(2,1)S(1)}, bf16[192,256]{1,0:T(8,128)(2,1)S(1)}) custom-call(bf16[512,256]{1,0:T(8,128)(2,1)} %bitcast.4, bf16[512,256]{1,0:T(8,128)(2,1)} %bitcast.5, bf16[512,256]{1,0:T(8,128)(2,1)} %bitcast.7, bf16[512,256]{1,0:T(8,128)(2,1)} %bitcast.9, f32[1,512]{1,0:T(1,128)} %weight.3), custom_call_target="tpu_custom_call" | custom-call | tf_op jit(solution)/shard_map/pack_borders/pallas_call | solution.py:56
  1.5 6.0 %collective-permute-start.1 = (bf16[192,256]{1,0:T(8,128)(2,1)S(1)}, bf16[192,256]{1,0:T(8,128)(2,1)S(1)}, u32[]{:S(2)}, u32[]{:S(2)}) collective-permute-start(bf16[192,256]{1,0:T(8,128)(2,1)S(1)} %get-tuple-element.29), channel_id=1, source_target_pairs={{0,28},{4,0},{8,4},{12,8},{16,12},{20,16},{24,20},{28,24},{1,29},{... | collective-permute-start | bytes 294920 | tf_op jit(solution)/shard_map/ppermute | solution.py:30
  7.6 0.0 collective-permute-start
  7.6 2.7 %load_all.1 = (bf16[512,256]{1,0:T(8,128)(2,1)S(1)}, f32[512,256]{1,0:T(8,128)S(1)}, bf16[512,256]{1,0:T(8,128)(2,1)S(1)}, bf16[16,128]{1,0:T(8,128)(2,1)S(1)}, ...) custom-call(bf16[512,256]{1,0:T(8,128)(2,1)} %bitcast.6, bf16[512,256]{1,0:T(8,128)(2,1)} %bitcast.8, ...), custom_call_target="tpu_custom_call" | custom-call | flops 10000000 | bytes 6000000 | tf_op jit(solution)/shard_map/load_all/pallas_call | solution.py:91
  10.3 3.9 %collective-permute-done.prev_rows = bf16[64,256]{1,0:T(8,128)(2,1)S(1)} collective-permute-done((bf16[64,256]{1,0:T(8,128)(2,1)S(1)}, bf16[64,256]{1,0:T(8,128)(2,1)S(1)}, u32[]{:S(2)}, u32[]{:S(2)}) %collective-permute-start) | collective-permute-done | bytes 32800 | tf_op jit(solution)/shard_map/ppermute | solution.py:30
  14.2 0.0 collective-permute-done.1.next_rows
  14.2 5.5 %forward_and_last_third.1 = (bf16[4,640,256]{2,1,0:T(8,128)(2,1)S(1)}, bf16[4,640,256]{2,1,0:T(8,128)(2,1)S(1)}, bf16[4,640,512]{2,1,0:T(8,128)(2,1)S(1)}, bf16[...) custom-call(bf16[64,256]{1,0:T(8,128)(2,1)S(1)} %collective-permute-, ...), custom_call_target="tpu_custom_call" | custom-call | flops 3623878656 | bytes 4718592 | tf_op jit(solution)/shard_map/forward_and_last_third/pallas_call | solution.py:318
  19.7 0.1 collective-permute-start.2
  19.7 1.9 %middle_third.1 = (f32[576,256]{1,0:T(8,128)S(1)}, bf16[2,2,2,2,192,128]{5,4,3,2,1,0:T(8,128)(2,1)S(1)}, bf16[2,2,2,2,192,128]{5,4,3,2,1,0:T(8,128)(2,1)S(1)}) custom-call(bf16[4,640,256]{2,1,0:T(8,128)(2,1)S(1)} %get-tuple-element.36.present, bf16[4,640,256]{2,1,0:T(8,128)(2,1)S(1)} %get-tuple-element.37.earlier, ...), custom_call_target="tpu_custom_call" | custom-call | flops 1610612736 | bytes 4718592 | tf_op jit(solution)/shard_map/middle_third/pallas_call | solution.py:345
  21.7 0.6 collective-permute-start.8
  22.2 0.0 collective-permute-done.2.refs_1_.refs_13_
  22.2 0.1 add_chunk0_step1.1.rest_0_
  22.3 1.9 %first_third.1 = (f32[512,256]{1,0:T(8,128)S(1)}, bf16[2,2,2,2,192,128]{5,4,3,2,1,0:T(8,128)(2,1)S(1)}, bf16[2,2,2,2,192,128]{5,4,3,2,1,0:T(8,128)(2,1)S(1)}) custom-call(bf16[4,640,256]{2,1,0:T(8,128)(2,1)S(1)} %get-tuple-element.36.present, bf16[4,640,256]{2,1,0:T(8,128)(2,1)S(1)} %get-tuple-element.37.earlier, ...), custom_call_target="tpu_custom_call" | custom-call | flops 1610612736 | bytes 4718592 | tf_op jit(solution)/shard_map/first_third/pallas_call | solution.py:345
  24.3 0.1 collective-permute-start.3
  24.4 1.6 %collective-permute-start.13 = (bf16[2,2,2,208,128]{4,3,2,1,0:T(8,128)(2,1)S(1)}, bf16[2,2,2,208,128]{4,3,2,1,0:T(8,128)(2,1)S(1)}, u32[]{:S(2)}, u32[]{:S(2)}) collective-permute-start(bf16[2,2,2,208,128]{4,3,2,1,0:T(8,128)(2,1)S(1)} %add_chunk0_step1.1.rest_0_), channel_id=1, source_target_pairs={{0,2},{1,3},{2,0},{3,1},{4,6},{5,7},{6,4},{7,5},{8,10},{9,11},{10,... | collective-permute-start | bytes 1277960 | tf_op jit(solution)/shard_map/ppermute | solution.py:464
  26.0 0.0 collective-permute-done.8.refs_1_.refs_7_
  26.0 0.1 add_chunk1_step1.1
  26.1 0.1 collective-permute-start.9
  26.1 0.5 collective-permute-done.3.refs_1_
  26.6 0.1 add_chunk2_step1.1
  26.7 0.1 collective-permute-start.4
  26.8 9.8 %collective-permute-done.13.refs_2_.refs_14_ = bf16[2,2,2,208,128]{4,3,2,1,0:T(8,128)(2,1)S(1)} collective-permute-done((bf16[2,2,2,208,128]{4,3,2,1,0:T(8,128)(2,1)S(1)}, bf16[2,2,2,208,128]{4,3,2,1,0:T(8,128)(2,1)S(1)}, u32[]{:S(2)}, u32[]{:S(2)}) %collective-permute-start.13) | collective-permute-done | bytes 426016 | tf_op jit(solution)/shard_map/ppermute | solution.py:464
  36.6 0.1 add_chunk0_step2.1
  36.7 0.1 collective-permute-start.14
  36.7 0.6 collective-permute-done.9.refs_2_.refs_8_
  37.3 0.1 add_chunk1_step2.1
  37.4 0.1 collective-permute-start.10
  37.5 0.5 collective-permute-done.4.refs_2_
  37.9 0.1 add_chunk2_step2.1
  38.0 1.6 %collective-permute-start.5 = (bf16[2,2,192,128]{3,2,1,0:T(8,128)(2,1)S(1)}, bf16[2,2,192,128]{3,2,1,0:T(8,128)(2,1)S(1)}, u32[]{:S(2)}, u32[]{:S(2)}) collective-permute-start(bf16[2,2,192,128]{3,2,1,0:T(8,128)(2,1)S(1)} %add_chunk2_step2.1), channel_id=1, source_target_pairs={{0,2},{1,3},{2,0},{3,1},{4,6},{5,7},{6,4},{7,5},{8,10},{9,11},{10,... | collective-permute-start | bytes 589832 | tf_op jit(solution)/shard_map/ppermute | solution.py:464
  39.6 3.9 %collective-permute-done.14.refs_3_.refs_15_ = bf16[2,2,208,128]{3,2,1,0:T(8,128)(2,1)S(1)} collective-permute-done((bf16[2,2,208,128]{3,2,1,0:T(8,128)(2,1)S(1)}, bf16[2,2,208,128]{3,2,1,0:T(8,128)(2,1)S(1)}, u32[]{:S(2)}, u32[]{:S(2)}) %collective-permute-start.14) | collective-permute-done | bytes 213024 | tf_op jit(solution)/shard_map/ppermute | solution.py:464
  43.6 0.1 add_chunk0_step3.1
  43.6 0.1 collective-permute-start.15
  43.7 0.0 collective-permute-done.10.refs_3_.refs_9_
  43.7 0.1 add_chunk1_step3.1
  43.8 1.6 %collective-permute-start.11 = (bf16[2,192,128]{2,1,0:T(8,128)(2,1)S(1)}, bf16[2,192,128]{2,1,0:T(8,128)(2,1)S(1)}, u32[]{:S(2)}, u32[]{:S(2)}) collective-permute-start(bf16[2,192,128]{2,1,0:T(8,128)(2,1)S(1)} %add_chunk1_step3.1), channel_id=1, source_target_pairs={{0,2},{1,3},{2,0},{3,1},{4,6},{5,7},{6,4},{7,5},{8,10},{9,11},{10,... | collective-permute-start | bytes 294920 | tf_op jit(solution)/shard_map/ppermute | solution.py:464
  45.4 0.0 collective-permute-done.5.refs_3_
  45.4 0.1 add_chunk2_step3.1
  45.4 1.4 %collective-permute-start.6 = (bf16[2,192,128]{2,1,0:T(8,128)(2,1)S(1)}, bf16[2,192,128]{2,1,0:T(8,128)(2,1)S(1)}, u32[]{:S(2)}, u32[]{:S(2)}) collective-permute-start(bf16[2,192,128]{2,1,0:T(8,128)(2,1)S(1)} %add_chunk2_step3.1), channel_id=1, source_target_pairs={{0,4},{1,5},{2,6},{3,7},{4,0},{5,1},{6,2},{7,3},{8,12},{9,13},{10,... | collective-permute-start | bytes 294920 | tf_op jit(solution)/shard_map/ppermute | solution.py:464
  46.9 1.5 %collective-permute-done.15.refs_4_.refs_16_ = bf16[2,208,128]{2,1,0:T(8,128)(2,1)S(1)} collective-permute-done((bf16[2,208,128]{2,1,0:T(8,128)(2,1)S(1)}, bf16[2,208,128]{2,1,0:T(8,128)(2,1)S(1)}, u32[]{:S(2)}, u32[]{:S(2)}) %collective-permute-start.15) | collective-permute-done | bytes 106528 | tf_op jit(solution)/shard_map/ppermute | solution.py:464
  48.4 0.1 add_chunk0_step4.1
  48.4 0.1 collective-permute-start.16
  48.5 0.0 collective-permute-done.11.refs_4_.refs_10_
  48.6 3.0 %collective-permute-start.12 = (bf16[192,128]{1,0:T(8,128)(2,1)S(1)}, bf16[192,128]{1,0:T(8,128)(2,1)S(1)}, u32[]{:S(2)}, u32[]{:S(2)}) collective-permute-start(bf16[192,128]{1,0:T(8,128)(2,1)S(1)} %add_chunk1_step4.1), channel_id=1, source_target_pairs={{0,16},{1,17},{2,18},{3,19},{4,20},{5,21},{6,22},{7,23},{8,24},{9,... | collective-permute-start | bytes 147464 | tf_op jit(solution)/shard_map/ppermute | solution.py:464
  51.5 0.0 collective-permute-done.6.refs_4_
  51.6 0.1 collective-permute-start.7
  51.7 3.8 %collective-permute-done.12.refs_11_ = bf16[192,128]{1,0:T(8,128)(2,1)S(1)} collective-permute-done((bf16[192,128]{1,0:T(8,128)(2,1)S(1)}, bf16[192,128]{1,0:T(8,128)(2,1)S(1)}, u32[]{:S(2)}, u32[]{:S(2)}) %collective-permute-start.12) | collective-permute-done | bytes 49184 | tf_op jit(solution)/shard_map/ppermute | solution.py:464
  55.4 0.0 collective-permute-done.16.refs_17_
  55.4 1.7 %collective-permute-done.7.refs_5_ = bf16[192,128]{1,0:T(8,128)(2,1)S(1)} collective-permute-done((bf16[192,128]{1,0:T(8,128)(2,1)S(1)}, bf16[192,128]{1,0:T(8,128)(2,1)S(1)}, u32[]{:S(2)}, u32[]{:S(2)}) %collective-permute-start.7) | collective-permute-done | bytes 49184 | tf_op jit(solution)/shard_map/ppermute | solution.py:464
  57.2 1.0 %scale_all.1 = (f32[512,256]{1,0:T(8,128)}, f32[6,64,128]{2,1,0:T(8,128)}, f32[6,32,128]{2,1,0:T(8,128)}) custom-call(bf16[2,2,2,2,192,128]{5,4,3,2,1,0:T(8,128)(2,1)S(1)} %get-tuple-element.45.refs_0_, bf16[2,2,2,2,192,128]{5,4,3,2,1,0:T(8,128)(2,1)S(1)} %collective-permute-done.3.refs_1_, bf16[2,2,2,192,128]{4,3,2,1,0:T(8,128)(2,1)S(1)} %collective-permute-done.4.refs_2_, ...), custom_call_target="tpu_custom_call" | custom-call | tf_op jit(solution)/shard_map/scale_all/pallas_call | solution.py:499
  (2 shorter events, 0.1 us)
Async XLA Ops:
  1.5 12.6 %collective-permute-start.1 = (bf16[192,256]{1,0:T(8,128)(2,1)S(1)}, bf16[192,256]{1,0:T(8,128)(2,1)S(1)}, u32[]{:S(2)}, u32[]{:S(2)}) collective-permute-start(bf16[192,256]{1,0:T(8,128)(2,1)S(1)} %get-tuple-element.29), channel_id=1, source_target_pairs={{0,28},{4,0},{8,4},{12,8},{16,12},{20,16},{24,20},{28,24},{1,29},{... | collective-permute-start | bytes 294920 | tf_op jit(solution)/shard_map/ppermute | solution.py:30
  7.6 6.6 %collective-permute-start = (bf16[64,256]{1,0:T(8,128)(2,1)S(1)}, bf16[64,256]{1,0:T(8,128)(2,1)S(1)}, u32[]{:S(2)}, u32[]{:S(2)}) collective-permute-start(bf16[64,256]{1,0:T(8,128)(2,1)S(1)} %get-tuple-element.28._), channel_id=1, source_target_pairs={{0,4},{4,8},{8,12},{12,16},{16,20},{20,24},{24,28},{28,0},{1,5},{5... | collective-permute-start | bytes 98312 | tf_op jit(solution)/shard_map/ppermute | solution.py:30
  19.7 2.6 %collective-permute-start.2 = (bf16[2,2,2,2,208,128]{5,4,3,2,1,0:T(8,128)(2,1)S(1)}, bf16[2,2,2,2,208,128]{5,4,3,2,1,0:T(8,128)(2,1)S(1)}, u32[]{:S(2)}, u32[]{:S(2)}) collective-permute-start(bf16[2,2,2,2,208,128]{5,4,3,2,1,0:T(8,128)(2,1)S(1)} %get-tuple-element.44), channel_id=1, source_target_pairs={{0,1},{1,0},{2,3},{3,2},{4,5},{5,4},{6,7},{7,6},{8,9},{9,8},{10,11... | collective-permute-start | bytes 2555912 | tf_op jit(solution)/shard_map/ppermute | solution.py:464
  21.7 4.3 %collective-permute-start.8 = (bf16[2,2,2,2,192,128]{5,4,3,2,1,0:T(8,128)(2,1)S(1)}, bf16[2,2,2,2,192,128]{5,4,3,2,1,0:T(8,128)(2,1)S(1)}, u32[]{:S(2)}, u32[]{:S(2)}) collective-permute-start(bf16[2,2,2,2,192,128]{5,4,3,2,1,0:T(8,128)(2,1)S(1)} %get-tuple-element.48), channel_id=1, source_target_pairs={{0,1},{1,0},{2,3},{3,2},{4,5},{5,4},{6,7},{7,6},{8,9},{9,8},{10,11... | collective-permute-start | bytes 2359304 | tf_op jit(solution)/shard_map/ppermute | solution.py:464
  24.3 2.4 %collective-permute-start.3 = (bf16[2,2,2,2,192,128]{5,4,3,2,1,0:T(8,128)(2,1)S(1)}, bf16[2,2,2,2,192,128]{5,4,3,2,1,0:T(8,128)(2,1)S(1)}, u32[]{:S(2)}, u32[]{:S(2)}) collective-permute-start(bf16[2,2,2,2,192,128]{5,4,3,2,1,0:T(8,128)(2,1)S(1)} %get-tuple-element.46), channel_id=1, source_target_pairs={{0,1},{1,0},{2,3},{3,2},{4,5},{5,4},{6,7},{7,6},{8,9},{9,8},{10,11... | collective-permute-start | bytes 2359304 | tf_op jit(solution)/shard_map/ppermute | solution.py:464
  24.4 12.2 %collective-permute-start.13 = (bf16[2,2,2,208,128]{4,3,2,1,0:T(8,128)(2,1)S(1)}, bf16[2,2,2,208,128]{4,3,2,1,0:T(8,128)(2,1)S(1)}, u32[]{:S(2)}, u32[]{:S(2)}) collective-permute-start(bf16[2,2,2,208,128]{4,3,2,1,0:T(8,128)(2,1)S(1)} %add_chunk0_step1.1.rest_0_), channel_id=1, source_target_pairs={{0,2},{1,3},{2,0},{3,1},{4,6},{5,7},{6,4},{7,5},{8,10},{9,11},{10,... | collective-permute-start | bytes 1277960 | tf_op jit(solution)/shard_map/ppermute | solution.py:464
  26.1 11.3 %collective-permute-start.9 = (bf16[2,2,2,192,128]{4,3,2,1,0:T(8,128)(2,1)S(1)}, bf16[2,2,2,192,128]{4,3,2,1,0:T(8,128)(2,1)S(1)}, u32[]{:S(2)}, u32[]{:S(2)}) collective-permute-start(bf16[2,2,2,192,128]{4,3,2,1,0:T(8,128)(2,1)S(1)} %add_chunk1_step1.1), channel_id=1, source_target_pairs={{0,4},{1,5},{2,6},{3,7},{4,0},{5,1},{6,2},{7,3},{8,12},{9,13},{10,... | collective-permute-start | bytes 1179656 | tf_op jit(solution)/shard_map/ppermute | solution.py:464
  26.7 11.2 %collective-permute-start.4 = (bf16[2,2,2,192,128]{4,3,2,1,0:T(8,128)(2,1)S(1)}, bf16[2,2,2,192,128]{4,3,2,1,0:T(8,128)(2,1)S(1)}, u32[]{:S(2)}, u32[]{:S(2)}) collective-permute-start(bf16[2,2,2,192,128]{4,3,2,1,0:T(8,128)(2,1)S(1)} %add_chunk2_step1.1), channel_id=1, source_target_pairs={{0,8},{1,9},{2,10},{3,11},{4,12},{5,13},{6,14},{7,15},{8,0},{9,1},... | collective-permute-start | bytes 1179656 | tf_op jit(solution)/shard_map/ppermute | solution.py:464
  36.7 6.9 %collective-permute-start.14 = (bf16[2,2,208,128]{3,2,1,0:T(8,128)(2,1)S(1)}, bf16[2,2,208,128]{3,2,1,0:T(8,128)(2,1)S(1)}, u32[]{:S(2)}, u32[]{:S(2)}) collective-permute-start(bf16[2,2,208,128]{3,2,1,0:T(8,128)(2,1)S(1)} %add_chunk0_step2.1), channel_id=1, source_target_pairs={{0,4},{1,5},{2,6},{3,7},{4,0},{5,1},{6,2},{7,3},{8,12},{9,13},{10,... | collective-permute-start | bytes 638984 | tf_op jit(solution)/shard_map/ppermute | solution.py:464
  37.4 6.3 %collective-permute-start.10 = (bf16[2,2,192,128]{3,2,1,0:T(8,128)(2,1)S(1)}, bf16[2,2,192,128]{3,2,1,0:T(8,128)(2,1)S(1)}, u32[]{:S(2)}, u32[]{:S(2)}) collective-permute-start(bf16[2,2,192,128]{3,2,1,0:T(8,128)(2,1)S(1)} %add_chunk1_step2.1), channel_id=1, source_target_pairs={{0,8},{1,9},{2,10},{3,11},{4,12},{5,13},{6,14},{7,15},{8,0},{9,1},... | collective-permute-start | bytes 589832 | tf_op jit(solution)/shard_map/ppermute | solution.py:464
  38.0 7.4 %collective-permute-start.5 = (bf16[2,2,192,128]{3,2,1,0:T(8,128)(2,1)S(1)}, bf16[2,2,192,128]{3,2,1,0:T(8,128)(2,1)S(1)}, u32[]{:S(2)}, u32[]{:S(2)}) collective-permute-start(bf16[2,2,192,128]{3,2,1,0:T(8,128)(2,1)S(1)} %add_chunk2_step2.1), channel_id=1, source_target_pairs={{0,2},{1,3},{2,0},{3,1},{4,6},{5,7},{6,4},{7,5},{8,10},{9,11},{10,... | collective-permute-start | bytes 589832 | tf_op jit(solution)/shard_map/ppermute | solution.py:464
  43.6 4.8 %collective-permute-start.15 = (bf16[2,208,128]{2,1,0:T(8,128)(2,1)S(1)}, bf16[2,208,128]{2,1,0:T(8,128)(2,1)S(1)}, u32[]{:S(2)}, u32[]{:S(2)}) collective-permute-start(bf16[2,208,128]{2,1,0:T(8,128)(2,1)S(1)} %add_chunk0_step3.1), channel_id=1, source_target_pairs={{0,8},{1,9},{2,10},{3,11},{4,12},{5,13},{6,14},{7,15},{8,0},{9,1},... | collective-permute-start | bytes 319496 | tf_op jit(solution)/shard_map/ppermute | solution.py:464
  43.8 4.8 %collective-permute-start.11 = (bf16[2,192,128]{2,1,0:T(8,128)(2,1)S(1)}, bf16[2,192,128]{2,1,0:T(8,128)(2,1)S(1)}, u32[]{:S(2)}, u32[]{:S(2)}) collective-permute-start(bf16[2,192,128]{2,1,0:T(8,128)(2,1)S(1)} %add_chunk1_step3.1), channel_id=1, source_target_pairs={{0,2},{1,3},{2,0},{3,1},{4,6},{5,7},{6,4},{7,5},{8,10},{9,11},{10,... | collective-permute-start | bytes 294920 | tf_op jit(solution)/shard_map/ppermute | solution.py:464
  45.4 6.1 %collective-permute-start.6 = (bf16[2,192,128]{2,1,0:T(8,128)(2,1)S(1)}, bf16[2,192,128]{2,1,0:T(8,128)(2,1)S(1)}, u32[]{:S(2)}, u32[]{:S(2)}) collective-permute-start(bf16[2,192,128]{2,1,0:T(8,128)(2,1)S(1)} %add_chunk2_step3.1), channel_id=1, source_target_pairs={{0,4},{1,5},{2,6},{3,7},{4,0},{5,1},{6,2},{7,3},{8,12},{9,13},{10,... | collective-permute-start | bytes 294920 | tf_op jit(solution)/shard_map/ppermute | solution.py:464
  48.4 7.0 %collective-permute-start.16 = (bf16[208,128]{1,0:T(8,128)(2,1)S(1)}, bf16[208,128]{1,0:T(8,128)(2,1)S(1)}, u32[]{:S(2)}, u32[]{:S(2)}) collective-permute-start(bf16[208,128]{1,0:T(8,128)(2,1)S(1)} %add_chunk0_step4.1), channel_id=1, source_target_pairs={{0,16},{1,17},{2,18},{3,19},{4,20},{5,21},{6,22},{7,23},{8,24},{9,... | collective-permute-start | bytes 159752 | tf_op jit(solution)/shard_map/ppermute | solution.py:464
  48.6 6.9 %collective-permute-start.12 = (bf16[192,128]{1,0:T(8,128)(2,1)S(1)}, bf16[192,128]{1,0:T(8,128)(2,1)S(1)}, u32[]{:S(2)}, u32[]{:S(2)}) collective-permute-start(bf16[192,128]{1,0:T(8,128)(2,1)S(1)} %add_chunk1_step4.1), channel_id=1, source_target_pairs={{0,16},{1,17},{2,18},{3,19},{4,20},{5,21},{6,22},{7,23},{8,24},{9,... | collective-permute-start | bytes 147464 | tf_op jit(solution)/shard_map/ppermute | solution.py:464
  51.6 5.6 %collective-permute-start.7 = (bf16[192,128]{1,0:T(8,128)(2,1)S(1)}, bf16[192,128]{1,0:T(8,128)(2,1)S(1)}, u32[]{:S(2)}, u32[]{:S(2)}) collective-permute-start(bf16[192,128]{1,0:T(8,128)(2,1)S(1)} %add_chunk2_step4.1), channel_id=1, source_target_pairs={{0,16},{1,17},{2,18},{3,19},{4,20},{5,21},{6,22},{7,23},{8,24},{9,... | collective-permute-start | bytes 147464 | tf_op jit(solution)/shard_map/ppermute | solution.py:464

commit v14 on v12

--- a/solution.py
+++ b/solution.py
@@ -38,13 +38,13 @@
     return pl.CostEstimate(flops=flops, bytes_accessed=moved, transcendentals=0)
 
 
-def pack_kernel(tail_x, tail_gs, tail_gk, weight, message):
+def pack_kernel(tail_x, tail_gs, tail_gk, weight, x_rows, grad_rows):
     halo, channels = tail_gs.shape
     by_row = column(weight[...], LANES)[LANES - halo :]
     by_row = jnp.concatenate([by_row] * (channels // LANES), axis=1)
-    message[0 : 2 * halo] = tail_x[...]
-    message[2 * halo : 3 * halo] = (tail_gs[...].astype(jnp.float32) * by_row).astype(jnp.bfloat16)
-    message[3 * halo :] = (tail_gk[...].astype(jnp.float32) * by_row).astype(jnp.bfloat16)
+    x_rows[...] = tail_x[...]
+    grad_rows[0:halo] = (tail_gs[...].astype(jnp.float32) * by_row).astype(jnp.bfloat16)
+    grad_rows[halo:] = (tail_gk[...].astype(jnp.float32) * by_row).astype(jnp.bfloat16)
 
 
 def pack(halo, x, grad_stream_out, grad_skip_out, weight):
@@ -53,12 +53,13 @@
     def last(rows):
         return pl.BlockSpec((rows, channels), lambda i: (length // rows - 1, 0))
 
+    message = jax.ShapeDtypeStruct((2 * halo, channels), jnp.bfloat16)
     return pl.pallas_call(
         pack_kernel,
         grid=(1,),
         in_specs=[last(2 * halo), last(halo), last(halo), pl.BlockSpec((1, LANES), lambda i: (0, length // LANES - 1))],
-        out_specs=pl.BlockSpec((4 * halo, channels), lambda i: (0, 0)),
-        out_shape=jax.ShapeDtypeStruct((4 * halo, channels), jnp.bfloat16),
+        out_specs=[pl.BlockSpec(message.shape, lambda i: (0, 0))] * 2,
+        out_shape=[message] * 2,
         compiler_params=pltpu.CompilerParams(vmem_limit_bytes=ADD_BYTES),
         name="pack_borders",
     )(*held((x, grad_stream_out, grad_skip_out, weight), pltpu.HBM))
@@ -169,73 +170,61 @@
         plan["store"](total, items.index((index, False)), grad_parts)
 
 
-def first_kernel(
-    plan, prev_rows, own_x, own_grad, own_skip, sums, conv_w, out_w,
-    low_present, low_earlier, low_factors, low_gates, grad_stream, grad_skip, *rest,
-):
-    *grad_parts, stream, high_present, high_factors, high_gates, grad_proj, past_part = rest
+def forward_kernel(plan, prev_x, own_x, conv_w, out_w, all_present, all_earlier, all_factors, all_gates, stream):
     halo, (length, channels) = plan["halo"], own_x.shape
-    layers, low = conv_w.shape[0], low_gates.shape[0]
+    layers, low = conv_w.shape[0], all_earlier.shape[0]
     pad = 2 ** (layers - 1)
     extent = length + 2 * halo
     begin = 2 * halo
     stream[0:pad] = jnp.zeros((pad, channels), jnp.float32)
-    stream[pad : pad + begin] = prev_rows[0:begin].astype(jnp.float32)
+    stream[pad : pad + begin] = prev_x[...].astype(jnp.float32)
     stream[pad + begin :] = own_x[...].astype(jnp.float32)
-
-    def refs_of(index):
-        if index < low:
-            return low_present.at[index], low_earlier.at[index], low_factors.at[index], low_gates.at[index]
-        at = index - low
-        return high_present.at[at], None, high_factors.at[at], high_gates.at[at]
-
-    refs_of(0)[0][0:begin] = prev_rows[0:begin]
-    refs_of(0)[0][begin:] = own_x[...]
+    all_present[0, 0:begin] = prev_x[...]
+    all_present[0, begin:] = own_x[...]
     for index in range(layers):
         dilation, start = 2**index, plan["starts"][index]
-        present, earlier, factor, gate = refs_of(index)
-        if earlier is None:
+        present = all_present.at[index]
+        if index >= low:
             past = earlier_rows(plan, index, present, start, extent)
         else:
             past = stream[pad + start - dilation : pad + extent - dilation]
             cut = cut_off(past[begin - start : begin - start + 16], dilation)
             past = jnp.concatenate([past[: begin - start], cut, past[begin - start + 16 :]]).astype(jnp.bfloat16)
-            earlier[start:] = past
+            all_earlier[index, start:] = past
         preact = dot(jnp.concatenate([present[start:], past], axis=1), conv_w[index], NN)
         filtered = jnp.tanh(preact[:, :channels])
         opening = 0.5 + 0.5 * jnp.tanh(0.5 * preact[:, channels:])
         product = filtered * opening
         gated = product.astype(jnp.bfloat16)
-        gate[start:] = gated
-        factor[start:, :channels] = (opening - filtered * product).astype(jnp.bfloat16)
-        factor[start:, channels:] = (product * (1.0 - opening)).astype(jnp.bfloat16)
+        all_gates[index, start:] = gated
+        all_factors[index, start:, :channels] = (opening - filtered * product).astype(jnp.bfloat16)
+        all_factors[index, start:, channels:] = (product * (1.0 - opening)).astype(jnp.bfloat16)
         if index < layers - 1:
             after = stream[pad + start :] + dot(gated, out_w[index, :, :channels], NN)
-            refs_of(index + 1)[0][start:] = after.astype(jnp.bfloat16)
+            all_present[index + 1, start:] = after.astype(jnp.bfloat16)
             if index < layers - 2:
                 stream[pad + start :] = after
 
-    grad_stream[0:halo] = prev_rows[2 * halo : 3 * halo].astype(jnp.float32)
-    grad_stream[halo:] = own_grad[...]
-    grad_skip[0:halo] = prev_rows[3 * halo :]
-    grad_skip[halo:] = own_skip[...]
+
+def backward_kernel(plan, first, third, all_present, all_earlier, all_factors, all_gates, conv_w, out_w, *rest):
+    refs = rest[: plan["inputs"]]
+    *outs, keep, send, grad_stream, grad_proj, past_part = rest[plan["inputs"] + plan["unused"] :]
+    halo, length, channels, low = plan["halo"], plan["length"], plan["channels"], all_earlier.shape[0]
+    if plan["inputs"] == 4:
+        prev_rows, own_grad, own_skip, sums = refs
+        *outs, grad_skip = outs
+        grad_stream[0:halo] = prev_rows[0:halo].astype(jnp.float32)
+        grad_stream[halo:] = own_grad[...]
+        grad_skip[0:halo] = prev_rows[halo:]
+        grad_skip[halo:] = own_skip[...]
+    else:
+        grad_before, grad_skip = refs
+        grad_stream[...] = grad_before[...]
     grad_proj[:, channels:] = grad_skip[...]
-    backward(
-        plan, list(reversed(range(low, layers))), refs_of, conv_w, out_w, grad_proj, grad_stream, past_part, grad_parts
-    )
-    plan["finish"](sums, grad_parts)
-
-
-def later_kernel(
-    plan, first, third, present, earlier, factors, gates, grad_before, grad_skip, conv_w, out_w, *rest
-):
-    *outs, keep, send, grad_stream, grad_proj, past_part = rest[plan["unused"] :]
-    channels = plan["channels"]
-    grad_stream[...] = grad_before[...]
-    grad_proj[:, channels:] = grad_skip[...]
 
     def refs_of(index):
-        return present.at[index], earlier.at[index], factors.at[index], gates.at[index]
+        earlier = all_earlier.at[index] if index < low else None
+        return all_present.at[index], earlier, all_factors.at[index], all_gates.at[index]
 
     backward(
         plan, list(reversed(range(first, first + third))), refs_of, conv_w, out_w,
@@ -245,6 +234,8 @@
     for out in outs:
         out[...] = grad_stream[at : at + out.shape[0]].astype(out.dtype)
         at += out.shape[0]
+    if plan["inputs"] == 4:
+        plan["finish"](sums, (keep, send))
 
 
 def store_whole(items, total, item, grad_parts):
@@ -296,7 +287,7 @@
     return ends[:-1], ends[-1]
 
 
-def run_layers(in_shards, tm, dp, halo, prev_rows, loaded):
+def run_layers(in_shards, tm, dp, halo, borders, loaded):
     own_x, own_grad, own_skip, sums, conv_w, out_w = loaded
     length, channels = own_x.shape
     layers = conv_w.shape[0]
@@ -325,36 +316,27 @@
     vmem, anywhere = pl.BlockSpec(memory_space=pltpu.VMEM), pl.BlockSpec(memory_space=pl.ANY)
     weight_bytes = 2 * (conv_w.size + out_w.size)
     flops = 2 * length * channels * channels
-    *kept, grad_stream, grad_skip, keep, send = pl.pallas_call(
-        functools.partial(first_kernel, plans[0]),
-        in_specs=[vmem] * 7,
-        out_specs=[vmem] * 8,
+    kept = pl.pallas_call(
+        functools.partial(forward_kernel, plan),
+        in_specs=[vmem] * 4,
+        out_specs=[vmem] * 4,
         out_shape=[
+            pltpu.VMEM((layers, extent, channels), jnp.bfloat16),
             pltpu.VMEM((low, extent, channels), jnp.bfloat16),
-            pltpu.VMEM((low, extent, channels), jnp.bfloat16),
-            pltpu.VMEM((low, extent, 2 * channels), jnp.bfloat16),
-            pltpu.VMEM((low, extent, channels), jnp.bfloat16),
-            pltpu.VMEM((border, channels), jnp.float32),
-            pltpu.VMEM((border, channels), jnp.bfloat16),
-        ]
-        + [pltpu.VMEM(shape, jnp.bfloat16) for shape in shapes[0]],
-        scratch_shapes=[
-            pltpu.VMEM((2 ** (layers - 1) + extent, channels), jnp.float32),
-            pltpu.VMEM((third, extent, channels), jnp.bfloat16),
-            pltpu.VMEM((third, extent, 2 * channels), jnp.bfloat16),
-            pltpu.VMEM((third, extent, channels), jnp.bfloat16),
-            pltpu.VMEM((border, 2 * channels), jnp.bfloat16),
-            pltpu.VMEM((border, channels), jnp.float32),
+            pltpu.VMEM((layers, extent, 2 * channels), jnp.bfloat16),
+            pltpu.VMEM((layers, extent, channels), jnp.bfloat16),
         ],
+        scratch_shapes=[pltpu.VMEM((2 ** (layers - 1) + extent, channels), jnp.float32)],
         compiler_params=pltpu.CompilerParams(vmem_limit_bytes=VMEM_BYTES),
-        cost_estimate=cost(flops * (5 * layers + 12 * third), weight_bytes),
-        name="forward_and_last_third",
-    )(*held((prev_rows, *loaded)))
-
-    def later(step, outs, after):
+        cost_estimate=cost(flops * 5 * layers, weight_bytes),
+        name="forward",
+    )(*held((borders[0], own_x, conv_w, out_w)))
+
+    def backward_of(step, inputs, outs, after):
+        more = {"inputs": len(inputs), "unused": len(after)}
         return pl.pallas_call(
-            functools.partial(later_kernel, plans[step] | {"unused": len(after)}, layers - (step + 1) * third, third),
-            in_specs=[vmem] * 8 + [anywhere] * len(after),
+            functools.partial(backward_kernel, plans[step] | more, layers - (step + 1) * third, third),
+            in_specs=[vmem] * (6 + len(inputs)) + [anywhere] * len(after),
             out_specs=[vmem] * (len(outs) + 2),
             out_shape=[pltpu.VMEM((rows, channels), kind) for rows, kind in outs]
             + [pltpu.VMEM(shape, jnp.bfloat16) for shape in shapes[step]],
@@ -365,17 +347,22 @@
             ],
             compiler_params=pltpu.CompilerParams(vmem_limit_bytes=VMEM_BYTES),
             cost_estimate=cost(flops * 12 * third, weight_bytes),
-            name="middle_third" if step == 1 else "first_third",
-        )(*held((*kept, grad_stream, grad_skip, conv_w, out_w, *after)))
-
-    parts = [(keep, send)]
+            name=("last_third", "middle_third", "first_third")[step],
+        )(*held((*kept, conv_w, out_w, *inputs, *after)))
+
+    whole = (border, jnp.float32)
+    grad_stream, grad_skip, *last = backward_of(
+        0, (borders[1], own_grad, own_skip, sums), [whole, (border, jnp.bfloat16)], []
+    )
+    parts = [last]
     if in_shards:
-        parts[0] = Chunk(tm, dp, 0, keep, send)
-    grad_stream, *middle = later(1, [(border, jnp.float32)], [])
-    other, own, *last = later(
-        2, [(halo, jnp.bfloat16), (length - halo, jnp.float32)], [parts[0].next_message()] if in_shards else []
+        parts[0] = Chunk(tm, dp, 0, *last)
+    grad_stream, *middle = backward_of(1, (grad_stream, grad_skip), [whole], [])
+    other, own, *first = backward_of(
+        2, (grad_stream, grad_skip), [(halo, jnp.bfloat16), (length - halo, jnp.float32)],
+        [parts[0].next_message()] if in_shards else [],
     )
-    parts += [middle, last]
+    parts += [middle, first]
     if in_shards:
         for step in (1, 2):
             parts[step] = Chunk(tm, dp, step, *parts[step])
@@ -490,11 +477,11 @@
     halo = 2**layers
     samples_all = batch * length * tm * dp
     x, gs, gk = inputs[0], grad_stream_out[0], grad_skip_out[0]
-    message = pack(halo, x, gs, gk, sample_weight)
-    prev_rows = around(message, "tm", 1)
-    loaded = load_all(x, gs, gk, sample_weight, conv_weight, out_weight, message)
+    x_rows, grad_rows = pack(halo, x, gs, gk, sample_weight)
+    borders = [around(x_rows, "tm", 1), around(grad_rows, "tm", 1)]
+    loaded = load_all(x, gs, gk, sample_weight, conv_weight, out_weight, x_rows)
     in_shards = tm == 8 and dp == 4 and channels // tm % 16 == 0 and 2 * channels == dp * LANES
-    other, own, parts = run_layers(in_shards, tm, dp, halo, prev_rows, loaded)
+    other, own, parts = run_layers(in_shards, tm, dp, halo, borders, loaded)
     other = around(other, "tm", -1)
     if not in_shards:
         scale = samples_all / lax.psum(jnp.sum(sample_weight), ("tm", "dp"))

time: 55.9 us -> 56.2 us (level)
  starting transfers between devices: 19.3 us -> 22.3 us
  waiting for transfers between devices: 20.9 us -> 18 us
    ppermute x2 -> x3, waiting for transfers between devices: 12 us -> 9.5 us  [around(): return lax.ppermute(x, axis, [(i, (i + by) % count) for i in range(count)])]
    ppermute x15, starting transfers between devices: 13.3 us -> 15.3 us  [swapped(): return lax.ppermute(value, ('tm', 'dp'), pairs)]
    ppermute x2 -> x3, starting transfers between devices: 6.07 us -> 7.04 us  [around(): return lax.ppermute(x, axis, [(i, (i + by) % count) for i in range(count)])]
    pallas_call x3 -> x4, Pallas kernels: 9.3 us -> 9.51 us  [the longest x3 5.84 us: backward_of(): pl.pallas_call(functools.partial(backward_kernel, plans[step] | more, lay...]
  transfers between devices with their start and end apart: 17 -> 18, of which waited for: 8 -> 8; matrix products, arithmetic and copies ran while one was open for 0% -> 0% of each run, Pallas kernels for 13% -> 20%
where the time goes in v14:
time: 56.2 us; the launch traced here: 56 us
  starting transfers between devices  22.3 us (40%)
  waiting for transfers between devices  18 us (32%)
  Pallas kernels  15 us (27%)
  between operations  0.77 us (1%)
    ppermute x15, starting transfers between devices, swapped(): return lax.ppermute(value, ('tm', 'dp'), pairs)  15.3 us
    ppermute x3, waiting for transfers between devices, around(): return lax.ppermute(x, axis, [(i, (i + by) % count) for i in range(count)])  9.5 us
    ppermute x15, waiting for transfers between devices, swapped(): return lax.ppermute(value, ('tm', 'dp'), pairs)  8.46 us
    ppermute x3, starting transfers between devices, around(): return lax.ppermute(x, axis, [(i, (i + by) % count) for i in range(count)])  7.04 us
    pallas_call x3, Pallas kernels, backward_of(): pl.pallas_call(functools.partial(backward_kernel, plans[step] | more, lay...  5.84 us
    pallas_call x1, Pallas kernels, run_layers(): pl.pallas_call(functools.partial(forward_kernel, plan), in_specs=[vmem] *...  3.67 us
    pallas_call x1, Pallas kernels, load_all(): pl.pallas_call(load_kernel, in_specs=[anywhere] * 7, out_specs=[vmem] * 6...  2.67 us
  transfers between devices with their start and end apart: 18, of which 8 were waited for; matrix products, arithmetic and copies ran while one was open for 0% of the time, Pallas kernels for 20%

profile of v14, /device:TPU:0, one launch (start us, length us, event | category | flops | bytes accessed | tf_op | source)
XLA Modules:
  0.0 56.0 jit_solution(197788999984767315)
XLA Ops:
  0.6 1.0 %pack_borders.1 = (bf16[128,256]{1,0:T(8,128)(2,1)S(1)}, bf16[128,256]{1,0:T(8,128)(2,1)S(1)}) custom-call(bf16[512,256]{1,0:T(8,128)(2,1)} %bitcast.4, bf16[512,256]{1,0:T(8,128)(2,1)} %bitcast.6, bf16[512,256]{1,0:T(8,128)(2,1)} %bitcast.8, f32[1,512]{1,0:T(1,128)} %weight.3), custom_call_target="tpu_custom_call" | custom-call | tf_op jit(solution)/shard_map/pack_borders/pallas_call | solution.py:57
  1.6 3.0 %collective-permute-start = (bf16[128,256]{1,0:T(8,128)(2,1)S(1)}, bf16[128,256]{1,0:T(8,128)(2,1)S(1)}, u32[]{:S(2)}, u32[]{:S(2)}) collective-permute-start(bf16[128,256]{1,0:T(8,128)(2,1)S(1)} %get-tuple-element.29._), channel_id=1, source_target_pairs={{0,4},{4,8},{8,12},{12,16},{16,20},{20,24},{24,28},{28,0},{1,5},{5... | collective-permute-start | bytes 196616 | tf_op jit(solution)/shard_map/ppermute | solution.py:30
  4.6 1.5 %collective-permute-start.1 = (bf16[128,256]{1,0:T(8,128)(2,1)S(1)}, bf16[128,256]{1,0:T(8,128)(2,1)S(1)}, u32[]{:S(2)}, u32[]{:S(2)}) collective-permute-start(bf16[128,256]{1,0:T(8,128)(2,1)S(1)} %get-tuple-element.37), channel_id=1, source_target_pairs={{0,4},{4,8},{8,12},{12,16},{16,20},{20,24},{24,28},{28,0},{1,5},{5... | collective-permute-start | bytes 196616 | tf_op jit(solution)/shard_map/ppermute | solution.py:30
  6.1 2.7 %load_all.1 = (bf16[512,256]{1,0:T(8,128)(2,1)S(1)}, f32[512,256]{1,0:T(8,128)S(1)}, bf16[512,256]{1,0:T(8,128)(2,1)S(1)}, bf16[16,128]{1,0:T(8,128)(2,1)S(1)}, ...) custom-call(bf16[512,256]{1,0:T(8,128)(2,1)} %bitcast.5, bf16[512,256]{1,0:T(8,128)(2,1)} %bitcast.7, ...), custom_call_target="tpu_custom_call" | custom-call | flops 10000000 | bytes 6000000 | tf_op jit(solution)/shard_map/load_all/pallas_call | solution.py:92
  8.8 1.5 %collective-permute-done.prev_x = bf16[128,256]{1,0:T(8,128)(2,1)S(1)} collective-permute-done((bf16[128,256]{1,0:T(8,128)(2,1)S(1)}, bf16[128,256]{1,0:T(8,128)(2,1)S(1)}, u32[]{:S(2)}, u32[]{:S(2)}) %collective-permute-start) | collective-permute-done | bytes 65568 | tf_op jit(solution)/shard_map/ppermute | solution.py:30
  10.3 3.7 %forward.1 = (bf16[6,640,256]{2,1,0:T(8,128)(2,1)S(1)}, bf16[4,640,256]{2,1,0:T(8,128)(2,1)S(1)}, bf16[6,640,512]{2,1,0:T(8,128)(2,1)S(1)}, bf16[6,640,256]{2,1,0:T(8,128)(2,1)S(1)}) custom-call(bf16[128,256]{1,0:T(8,128)(2,1)S(1)} %collective-permute-done.prev_x, bf16[512,256]{1,0:T(8,128)(2,1)S(1)} %get-tuple-element.30.own_x, ...), custom_call_target="tpu_custom_call" | custom-call | flops 2013265920 | bytes 4718592 | tf_op jit(solution)/shard_map/forward/pallas_call | solution.py:319
  14.0 0.0 collective-permute-done.1.rest_0_
  14.0 2.0 %last_third.1 = (f32[576,256]{1,0:T(8,128)S(1)}, bf16[576,256]{1,0:T(8,128)(2,1)S(1)}, bf16[2,2,2,2,208,128]{5,4,3,2,1,0:T(8,128)(2,1)S(1)}, bf16[2,2,2,2,208,128]{5,4,3,2,1,0:T(8,128)(2,1)S(1)}) custom-call(bf16[6,640,256]{2,1,0:T(8,128)(2,1)S(1)} %get-tuple-element.33.all_present, bf16[4,640,256]{2,1,0:T(8,128)(2,1)S(1)} %get-tuple-element.34.all_earlier, ...), custom_call_target="tpu_custom_call" | custom-call | flops 1610612736 | bytes 4718592 | tf_op jit(solution)/shard_map/last_third/pallas_call | solution.py:337
  16.0 0.1 collective-permute-start.2
  16.1 1.9 %middle_third.1 = (f32[576,256]{1,0:T(8,128)S(1)}, bf16[2,2,2,2,192,128]{5,4,3,2,1,0:T(8,128)(2,1)S(1)}, bf16[2,2,2,2,192,128]{5,4,3,2,1,0:T(8,128)(2,1)S(1)}) custom-call(bf16[6,640,256]{2,1,0:T(8,128)(2,1)S(1)} %get-tuple-element.33.all_present, bf16[4,640,256]{2,1,0:T(8,128)(2,1)S(1)} %get-tuple-element.34.all_earlier, ...), custom_call_target="tpu_custom_call" | custom-call | flops 1610612736 | bytes 4718592 | tf_op jit(solution)/shard_map/middle_third/pallas_call | solution.py:337
  18.0 0.6 collective-permute-start.8
  18.6 0.0 collective-permute-done.2.refs_1_.refs_13_
  18.6 0.1 add_chunk0_step1.1.rest_2_
  18.7 1.9 %first_third.1 = (bf16[64,256]{1,0:T(8,128)(2,1)S(1)}, f32[448,256]{1,0:T(8,128)S(1)}, bf16[2,2,2,2,192,128]{5,4,3,2,1,0:T(8,128)(2,1)S(1)}, bf16[2,2,2,2,192,128]{5,4,3,2,1,0:T(8,128)(2,1)S(1)}) custom-call(bf16[6,640,256]{2,1,0:T(8,128)(2,1)S(1)} %get-tuple-element.33.all_present, bf16[4,640,256]{2,1,0:T(8,128)(2,1)S(1)} %get-tuple-element.34.all_earlier, ...), custom_call_target="tpu_custom_call" | custom-call | flops 1610612736 | bytes 4718592 | tf_op jit(solution)/shard_map/first_third/pallas_call | solution.py:337
  20.6 0.1 collective-permute-start.3
  20.7 1.9 %collective-permute-start.13 = (bf16[2,2,2,208,128]{4,3,2,1,0:T(8,128)(2,1)S(1)}, bf16[2,2,2,208,128]{4,3,2,1,0:T(8,128)(2,1)S(1)}, u32[]{:S(2)}, u32[]{:S(2)}) collective-permute-start(bf16[2,2,2,208,128]{4,3,2,1,0:T(8,128)(2,1)S(1)} %add_chunk0_step1.1.rest_2_), channel_id=1, source_target_pairs={{0,2},{1,3},{2,0},{3,1},{4,6},{5,7},{6,4},{7,5},{8,10},{9,11},{10,... | collective-permute-start | bytes 1277960 | tf_op jit(solution)/shard_map/ppermute | solution.py:464
  22.7 0.0 collective-permute-done.8.refs_1_.refs_7_
  22.7 0.1 add_chunk1_step1.1
  22.8 0.1 collective-permute-start.9
  22.8 0.1 collective-permute-done.3.refs_1_
  23.0 0.1 add_chunk2_step1.1
  23.1 1.1 %collective-permute-start.4 = (bf16[2,2,2,192,128]{4,3,2,1,0:T(8,128)(2,1)S(1)}, bf16[2,2,2,192,128]{4,3,2,1,0:T(8,128)(2,1)S(1)}, u32[]{:S(2)}, u32[]{:S(2)}) collective-permute-start(bf16[2,2,2,192,128]{4,3,2,1,0:T(8,128)(2,1)S(1)} %add_chunk2_step1.1), channel_id=1, source_target_pairs={{0,8},{1,9},{2,10},{3,11},{4,12},{5,13},{6,14},{7,15},{8,0},{9,1},... | collective-permute-start | bytes 1179656 | tf_op jit(solution)/shard_map/ppermute | solution.py:464
  24.2 2.5 %collective-permute-start.14 = (bf16[64,256]{1,0:T(8,128)(2,1)S(1)}, bf16[64,256]{1,0:T(8,128)(2,1)S(1)}, u32[]{:S(2)}, u32[]{:S(2)}) collective-permute-start(bf16[64,256]{1,0:T(8,128)(2,1)S(1)} %get-tuple-element.50), channel_id=1, source_target_pairs={{0,28},{4,0},{8,4},{12,8},{16,12},{20,16},{24,20},{28,24},{1,29},{... | collective-permute-start | bytes 98312 | tf_op jit(solution)/shard_map/ppermute | solution.py:30
  26.7 8.0 %collective-permute-done.14.refs_3_.refs_18_ = bf16[64,256]{1,0:T(8,128)(2,1)S(1)} collective-permute-done((bf16[64,256]{1,0:T(8,128)(2,1)S(1)}, bf16[64,256]{1,0:T(8,128)(2,1)S(1)}, u32[]{:S(2)}, u32[]{:S(2)}) %collective-permute-start.14) | collective-permute-done | bytes 32800 | tf_op jit(solution)/shard_map/ppermute | solution.py:30
  34.7 0.0 collective-permute-done.13.refs_2_.refs_14_
  34.7 0.1 add_chunk0_step2.1
  34.8 1.8 %collective-permute-start.15 = (bf16[2,2,208,128]{3,2,1,0:T(8,128)(2,1)S(1)}, bf16[2,2,208,128]{3,2,1,0:T(8,128)(2,1)S(1)}, u32[]{:S(2)}, u32[]{:S(2)}) collective-permute-start(bf16[2,2,208,128]{3,2,1,0:T(8,128)(2,1)S(1)} %add_chunk0_step2.1), channel_id=1, source_target_pairs={{0,4},{1,5},{2,6},{3,7},{4,0},{5,1},{6,2},{7,3},{8,12},{9,13},{10,... | collective-permute-start | bytes 638984 | tf_op jit(solution)/shard_map/ppermute | solution.py:464
  36.6 0.0 collective-permute-done.9.refs_2_.refs_8_
  36.6 0.1 add_chunk1_step2.1
  36.7 0.1 collective-permute-start.10
  36.8 0.0 collective-permute-done.4.refs_2_
  36.8 0.1 add_chunk2_step2.1
  36.9 2.0 %collective-permute-start.5 = (bf16[2,2,192,128]{3,2,1,0:T(8,128)(2,1)S(1)}, bf16[2,2,192,128]{3,2,1,0:T(8,128)(2,1)S(1)}, u32[]{:S(2)}, u32[]{:S(2)}) collective-permute-start(bf16[2,2,192,128]{3,2,1,0:T(8,128)(2,1)S(1)} %add_chunk2_step2.1), channel_id=1, source_target_pairs={{0,2},{1,3},{2,0},{3,1},{4,6},{5,7},{6,4},{7,5},{8,10},{9,11},{10,... | collective-permute-start | bytes 589832 | tf_op jit(solution)/shard_map/ppermute | solution.py:464
  38.8 2.5 %collective-permute-done.15.refs_3_.refs_15_ = bf16[2,2,208,128]{3,2,1,0:T(8,128)(2,1)S(1)} collective-permute-done((bf16[2,2,208,128]{3,2,1,0:T(8,128)(2,1)S(1)}, bf16[2,2,208,128]{3,2,1,0:T(8,128)(2,1)S(1)}, u32[]{:S(2)}, u32[]{:S(2)}) %collective-permute-start.15) | collective-permute-done | bytes 213024 | tf_op jit(solution)/shard_map/ppermute | solution.py:464
  41.4 0.1 add_chunk0_step3.1
  41.4 0.1 collective-permute-start.16
  41.5 0.9 %collective-permute-done.10.refs_3_.refs_9_ = bf16[2,2,192,128]{3,2,1,0:T(8,128)(2,1)S(1)} collective-permute-done((bf16[2,2,192,128]{3,2,1,0:T(8,128)(2,1)S(1)}, bf16[2,2,192,128]{3,2,1,0:T(8,128)(2,1)S(1)}, u32[]{:S(2)}, u32[]{:S(2)}) %collective-permute-start.10) | collective-permute-done | bytes 196640 | tf_op jit(solution)/shard_map/ppermute | solution.py:464
  42.4 0.1 add_chunk1_step3.1
  42.5 2.2 %collective-permute-start.11 = (bf16[2,192,128]{2,1,0:T(8,128)(2,1)S(1)}, bf16[2,192,128]{2,1,0:T(8,128)(2,1)S(1)}, u32[]{:S(2)}, u32[]{:S(2)}) collective-permute-start(bf16[2,192,128]{2,1,0:T(8,128)(2,1)S(1)} %add_chunk1_step3.1), channel_id=1, source_target_pairs={{0,2},{1,3},{2,0},{3,1},{4,6},{5,7},{6,4},{7,5},{8,10},{9,11},{10,... | collective-permute-start | bytes 294920 | tf_op jit(solution)/shard_map/ppermute | solution.py:464
  44.7 0.0 collective-permute-done.5.refs_3_
  44.7 0.1 add_chunk2_step3.1
  44.7 0.4 collective-permute-start.6
  45.1 1.1 %collective-permute-done.16.refs_4_.refs_16_ = bf16[2,208,128]{2,1,0:T(8,128)(2,1)S(1)} collective-permute-done((bf16[2,208,128]{2,1,0:T(8,128)(2,1)S(1)}, bf16[2,208,128]{2,1,0:T(8,128)(2,1)S(1)}, u32[]{:S(2)}, u32[]{:S(2)}) %collective-permute-start.16) | collective-permute-done | bytes 106528 | tf_op jit(solution)/shard_map/ppermute | solution.py:464
  46.2 0.1 add_chunk0_step4.1
  46.3 1.9 %collective-permute-start.17 = (bf16[208,128]{1,0:T(8,128)(2,1)S(1)}, bf16[208,128]{1,0:T(8,128)(2,1)S(1)}, u32[]{:S(2)}, u32[]{:S(2)}) collective-permute-start(bf16[208,128]{1,0:T(8,128)(2,1)S(1)} %add_chunk0_step4.1), channel_id=1, source_target_pairs={{0,16},{1,17},{2,18},{3,19},{4,20},{5,21},{6,22},{7,23},{8,24},{9,... | collective-permute-start | bytes 159752 | tf_op jit(solution)/shard_map/ppermute | solution.py:464
  48.2 0.0 collective-permute-done.11.refs_4_.refs_10_
  48.2 1.7 %collective-permute-start.12 = (bf16[192,128]{1,0:T(8,128)(2,1)S(1)}, bf16[192,128]{1,0:T(8,128)(2,1)S(1)}, u32[]{:S(2)}, u32[]{:S(2)}) collective-permute-start(bf16[192,128]{1,0:T(8,128)(2,1)S(1)} %add_chunk1_step4.1), channel_id=1, source_target_pairs={{0,16},{1,17},{2,18},{3,19},{4,20},{5,21},{6,22},{7,23},{8,24},{9,... | collective-permute-start | bytes 147464 | tf_op jit(solution)/shard_map/ppermute | solution.py:464
  49.9 0.0 collective-permute-done.6.refs_4_
  50.0 1.3 %collective-permute-start.7 = (bf16[192,128]{1,0:T(8,128)(2,1)S(1)}, bf16[192,128]{1,0:T(8,128)(2,1)S(1)}, u32[]{:S(2)}, u32[]{:S(2)}) collective-permute-start(bf16[192,128]{1,0:T(8,128)(2,1)S(1)} %add_chunk2_step4.1), channel_id=1, source_target_pairs={{0,16},{1,17},{2,18},{3,19},{4,20},{5,21},{6,22},{7,23},{8,24},{9,... | collective-permute-start | bytes 147464 | tf_op jit(solution)/shard_map/ppermute | solution.py:464
  51.3 2.5 %collective-permute-done.12.refs_11_ = bf16[192,128]{1,0:T(8,128)(2,1)S(1)} collective-permute-done((bf16[192,128]{1,0:T(8,128)(2,1)S(1)}, bf16[192,128]{1,0:T(8,128)(2,1)S(1)}, u32[]{:S(2)}, u32[]{:S(2)}) %collective-permute-start.12) | collective-permute-done | bytes 49184 | tf_op jit(solution)/shard_map/ppermute | solution.py:464
  53.8 0.0 collective-permute-done.17.refs_17_
  53.8 1.3 %collective-permute-done.7.refs_5_ = bf16[192,128]{1,0:T(8,128)(2,1)S(1)} collective-permute-done((bf16[192,128]{1,0:T(8,128)(2,1)S(1)}, bf16[192,128]{1,0:T(8,128)(2,1)S(1)}, u32[]{:S(2)}, u32[]{:S(2)}) %collective-permute-start.7) | collective-permute-done | bytes 49184 | tf_op jit(solution)/shard_map/ppermute | solution.py:464
  55.0 1.0 %scale_all.1 = (f32[512,256]{1,0:T(8,128)}, f32[6,64,128]{2,1,0:T(8,128)}, f32[6,32,128]{2,1,0:T(8,128)}) custom-call(bf16[2,2,2,2,192,128]{5,4,3,2,1,0:T(8,128)(2,1)S(1)} %get-tuple-element.46.refs_0_, bf16[2,2,2,2,192,128]{5,4,3,2,1,0:T(8,128)(2,1)S(1)} %collective-permute-done.3.refs_1_, bf16[2,2,2,192,128]{4,3,2,1,0:T(8,128)(2,1)S(1)} %collective-permute-done.4.refs_2_, ...), custom_call_target="tpu_custom_call" | custom-call | tf_op jit(solution)/shard_map/scale_all/pallas_call | solution.py:500
  (2 shorter events, 0.1 us)
Async XLA Ops:
  1.6 8.7 %collective-permute-start = (bf16[128,256]{1,0:T(8,128)(2,1)S(1)}, bf16[128,256]{1,0:T(8,128)(2,1)S(1)}, u32[]{:S(2)}, u32[]{:S(2)}) collective-permute-start(bf16[128,256]{1,0:T(8,128)(2,1)S(1)} %get-tuple-element.29._), channel_id=1, source_target_pairs={{0,4},{4,8},{8,12},{12,16},{16,20},{20,24},{24,28},{28,0},{1,5},{5... | collective-permute-start | bytes 196616 | tf_op jit(solution)/shard_map/ppermute | solution.py:30
  4.6 9.4 %collective-permute-start.1 = (bf16[128,256]{1,0:T(8,128)(2,1)S(1)}, bf16[128,256]{1,0:T(8,128)(2,1)S(1)}, u32[]{:S(2)}, u32[]{:S(2)}) collective-permute-start(bf16[128,256]{1,0:T(8,128)(2,1)S(1)} %get-tuple-element.37), channel_id=1, source_target_pairs={{0,4},{4,8},{8,12},{12,16},{16,20},{20,24},{24,28},{28,0},{1,5},{5... | collective-permute-start | bytes 196616 | tf_op jit(solution)/shard_map/ppermute | solution.py:30
  16.0 2.6 %collective-permute-start.2 = (bf16[2,2,2,2,208,128]{5,4,3,2,1,0:T(8,128)(2,1)S(1)}, bf16[2,2,2,2,208,128]{5,4,3,2,1,0:T(8,128)(2,1)S(1)}, u32[]{:S(2)}, u32[]{:S(2)}) collective-permute-start(bf16[2,2,2,2,208,128]{5,4,3,2,1,0:T(8,128)(2,1)S(1)} %get-tuple-element.45), channel_id=1, source_target_pairs={{0,1},{1,0},{2,3},{3,2},{4,5},{5,4},{6,7},{7,6},{8,9},{9,8},{10,11... | collective-permute-start | bytes 2555912 | tf_op jit(solution)/shard_map/ppermute | solution.py:464
  18.0 4.6 %collective-permute-start.8 = (bf16[2,2,2,2,192,128]{5,4,3,2,1,0:T(8,128)(2,1)S(1)}, bf16[2,2,2,2,192,128]{5,4,3,2,1,0:T(8,128)(2,1)S(1)}, u32[]{:S(2)}, u32[]{:S(2)}) collective-permute-start(bf16[2,2,2,2,192,128]{5,4,3,2,1,0:T(8,128)(2,1)S(1)} %get-tuple-element.49), channel_id=1, source_target_pairs={{0,1},{1,0},{2,3},{3,2},{4,5},{5,4},{6,7},{7,6},{8,9},{9,8},{10,11... | collective-permute-start | bytes 2359304 | tf_op jit(solution)/shard_map/ppermute | solution.py:464
  20.6 2.4 %collective-permute-start.3 = (bf16[2,2,2,2,192,128]{5,4,3,2,1,0:T(8,128)(2,1)S(1)}, bf16[2,2,2,2,192,128]{5,4,3,2,1,0:T(8,128)(2,1)S(1)}, u32[]{:S(2)}, u32[]{:S(2)}) collective-permute-start(bf16[2,2,2,2,192,128]{5,4,3,2,1,0:T(8,128)(2,1)S(1)} %get-tuple-element.47), channel_id=1, source_target_pairs={{0,1},{1,0},{2,3},{3,2},{4,5},{5,4},{6,7},{7,6},{8,9},{9,8},{10,11... | collective-permute-start | bytes 2359304 | tf_op jit(solution)/shard_map/ppermute | solution.py:464
  20.7 14.0 %collective-permute-start.13 = (bf16[2,2,2,208,128]{4,3,2,1,0:T(8,128)(2,1)S(1)}, bf16[2,2,2,208,128]{4,3,2,1,0:T(8,128)(2,1)S(1)}, u32[]{:S(2)}, u32[]{:S(2)}) collective-permute-start(bf16[2,2,2,208,128]{4,3,2,1,0:T(8,128)(2,1)S(1)} %add_chunk0_step1.1.rest_2_), channel_id=1, source_target_pairs={{0,2},{1,3},{2,0},{3,1},{4,6},{5,7},{6,4},{7,5},{8,10},{9,11},{10,... | collective-permute-start | bytes 1277960 | tf_op jit(solution)/shard_map/ppermute | solution.py:464
  22.8 13.9 %collective-permute-start.9 = (bf16[2,2,2,192,128]{4,3,2,1,0:T(8,128)(2,1)S(1)}, bf16[2,2,2,192,128]{4,3,2,1,0:T(8,128)(2,1)S(1)}, u32[]{:S(2)}, u32[]{:S(2)}) collective-permute-start(bf16[2,2,2,192,128]{4,3,2,1,0:T(8,128)(2,1)S(1)} %add_chunk1_step1.1), channel_id=1, source_target_pairs={{0,4},{1,5},{2,6},{3,7},{4,0},{5,1},{6,2},{7,3},{8,12},{9,13},{10,... | collective-permute-start | bytes 1179656 | tf_op jit(solution)/shard_map/ppermute | solution.py:464
  23.1 13.7 %collective-permute-start.4 = (bf16[2,2,2,192,128]{4,3,2,1,0:T(8,128)(2,1)S(1)}, bf16[2,2,2,192,128]{4,3,2,1,0:T(8,128)(2,1)S(1)}, u32[]{:S(2)}, u32[]{:S(2)}) collective-permute-start(bf16[2,2,2,192,128]{4,3,2,1,0:T(8,128)(2,1)S(1)} %add_chunk2_step1.1), channel_id=1, source_target_pairs={{0,8},{1,9},{2,10},{3,11},{4,12},{5,13},{6,14},{7,15},{8,0},{9,1},... | collective-permute-start | bytes 1179656 | tf_op jit(solution)/shard_map/ppermute | solution.py:464
  24.2 10.5 %collective-permute-start.14 = (bf16[64,256]{1,0:T(8,128)(2,1)S(1)}, bf16[64,256]{1,0:T(8,128)(2,1)S(1)}, u32[]{:S(2)}, u32[]{:S(2)}) collective-permute-start(bf16[64,256]{1,0:T(8,128)(2,1)S(1)} %get-tuple-element.50), channel_id=1, source_target_pairs={{0,28},{4,0},{8,4},{12,8},{16,12},{20,16},{24,20},{28,24},{1,29},{... | collective-permute-start | bytes 98312 | tf_op jit(solution)/shard_map/ppermute | solution.py:30
  34.8 6.6 %collective-permute-start.15 = (bf16[2,2,208,128]{3,2,1,0:T(8,128)(2,1)S(1)}, bf16[2,2,208,128]{3,2,1,0:T(8,128)(2,1)S(1)}, u32[]{:S(2)}, u32[]{:S(2)}) collective-permute-start(bf16[2,2,208,128]{3,2,1,0:T(8,128)(2,1)S(1)} %add_chunk0_step2.1), channel_id=1, source_target_pairs={{0,4},{1,5},{2,6},{3,7},{4,0},{5,1},{6,2},{7,3},{8,12},{9,13},{10,... | collective-permute-start | bytes 638984 | tf_op jit(solution)/shard_map/ppermute | solution.py:464
  36.7 5.7 %collective-permute-start.10 = (bf16[2,2,192,128]{3,2,1,0:T(8,128)(2,1)S(1)}, bf16[2,2,192,128]{3,2,1,0:T(8,128)(2,1)S(1)}, u32[]{:S(2)}, u32[]{:S(2)}) collective-permute-start(bf16[2,2,192,128]{3,2,1,0:T(8,128)(2,1)S(1)} %add_chunk1_step2.1), channel_id=1, source_target_pairs={{0,8},{1,9},{2,10},{3,11},{4,12},{5,13},{6,14},{7,15},{8,0},{9,1},... | collective-permute-start | bytes 589832 | tf_op jit(solution)/shard_map/ppermute | solution.py:464
  36.9 7.8 %collective-permute-start.5 = (bf16[2,2,192,128]{3,2,1,0:T(8,128)(2,1)S(1)}, bf16[2,2,192,128]{3,2,1,0:T(8,128)(2,1)S(1)}, u32[]{:S(2)}, u32[]{:S(2)}) collective-permute-start(bf16[2,2,192,128]{3,2,1,0:T(8,128)(2,1)S(1)} %add_chunk2_step2.1), channel_id=1, source_target_pairs={{0,2},{1,3},{2,0},{3,1},{4,6},{5,7},{6,4},{7,5},{8,10},{9,11},{10,... | collective-permute-start | bytes 589832 | tf_op jit(solution)/shard_map/ppermute | solution.py:464
  41.4 4.8 %collective-permute-start.16 = (bf16[2,208,128]{2,1,0:T(8,128)(2,1)S(1)}, bf16[2,208,128]{2,1,0:T(8,128)(2,1)S(1)}, u32[]{:S(2)}, u32[]{:S(2)}) collective-permute-start(bf16[2,208,128]{2,1,0:T(8,128)(2,1)S(1)} %add_chunk0_step3.1), channel_id=1, source_target_pairs={{0,8},{1,9},{2,10},{3,11},{4,12},{5,13},{6,14},{7,15},{8,0},{9,1},... | collective-permute-start | bytes 319496 | tf_op jit(solution)/shard_map/ppermute | solution.py:464
  42.5 5.7 %collective-permute-start.11 = (bf16[2,192,128]{2,1,0:T(8,128)(2,1)S(1)}, bf16[2,192,128]{2,1,0:T(8,128)(2,1)S(1)}, u32[]{:S(2)}, u32[]{:S(2)}) collective-permute-start(bf16[2,192,128]{2,1,0:T(8,128)(2,1)S(1)} %add_chunk1_step3.1), channel_id=1, source_target_pairs={{0,2},{1,3},{2,0},{3,1},{4,6},{5,7},{6,4},{7,5},{8,10},{9,11},{10,... | collective-permute-start | bytes 294920 | tf_op jit(solution)/shard_map/ppermute | solution.py:464
  44.7 5.2 %collective-permute-start.6 = (bf16[2,192,128]{2,1,0:T(8,128)(2,1)S(1)}, bf16[2,192,128]{2,1,0:T(8,128)(2,1)S(1)}, u32[]{:S(2)}, u32[]{:S(2)}) collective-permute-start(bf16[2,192,128]{2,1,0:T(8,128)(2,1)S(1)} %add_chunk2_step3.1), channel_id=1, source_target_pairs={{0,4},{1,5},{2,6},{3,7},{4,0},{5,1},{6,2},{7,3},{8,12},{9,13},{10,... | collective-permute-start | bytes 294920 | tf_op jit(solution)/shard_map/ppermute | solution.py:464
  46.3 7.5 %collective-permute-start.17 = (bf16[208,128]{1,0:T(8,128)(2,1)S(1)}, bf16[208,128]{1,0:T(8,128)(2,1)S(1)}, u32[]{:S(2)}, u32[]{:S(2)}) collective-permute-start(bf16[208,128]{1,0:T(8,128)(2,1)S(1)} %add_chunk0_step4.1), channel_id=1, source_target_pairs={{0,16},{1,17},{2,18},{3,19},{4,20},{5,21},{6,22},{7,23},{8,24},{9,... | collective-permute-start | bytes 159752 | tf_op jit(solution)/shard_map/ppermute | solution.py:464
  48.2 5.6 %collective-permute-start.12 = (bf16[192,128]{1,0:T(8,128)(2,1)S(1)}, bf16[192,128]{1,0:T(8,128)(2,1)S(1)}, u32[]{:S(2)}, u32[]{:S(2)}) collective-permute-start(bf16[192,128]{1,0:T(8,128)(2,1)S(1)} %add_chunk1_step4.1), channel_id=1, source_target_pairs={{0,16},{1,17},{2,18},{3,19},{4,20},{5,21},{6,22},{7,23},{8,24},{9,... | collective-permute-start | bytes 147464 | tf_op jit(solution)/shard_map/ppermute | solution.py:464
  50.0 5.1 %collective-permute-start.7 = (bf16[192,128]{1,0:T(8,128)(2,1)S(1)}, bf16[192,128]{1,0:T(8,128)(2,1)S(1)}, u32[]{:S(2)}, u32[]{:S(2)}) collective-permute-start(bf16[192,128]{1,0:T(8,128)(2,1)S(1)} %add_chunk2_step4.1), channel_id=1, source_target_pairs={{0,16},{1,17},{2,18},{3,19},{4,20},{5,21},{6,22},{7,23},{8,24},{9,... | collective-permute-start | bytes 147464 | tf_op jit(solution)/shard_map/ppermute | solution.py:464

commit v15 on v14

--- a/solution.py
+++ b/solution.py
@@ -10,7 +10,7 @@
 LANES = 128
 VMEM_BYTES = 24 * 1024 * 1024
 ADD_BYTES = 8 * 1024 * 1024
-CHAINS = (("y", "x", "z0", "z1"), ("x", "z0", "y", "z1"), ("z0", "y", "x", "z1"))
+CHAINS = (("x", "z0", "y", "z1"), ("z0", "y", "x", "z1"), ("y", "x", "z0", "z1"))
 EXTRA = (16, 0, 0)
 NN = (((1,), (0,)), ((), ()))
 NT = (((1,), (1,)), ((), ()))

time: 56.2 us -> 54.9 us (0.977)
  starting transfers between devices: 22.3 us -> 21.5 us
    ppermute x3, waiting for transfers between devices: 9.5 us -> 8.41 us  [around(): return lax.ppermute(x, axis, [(i, (i + by) % count) for i in range(count)])]
    ppermute x3, starting transfers between devices: 7.04 us -> 6.22 us  [around(): return lax.ppermute(x, axis, [(i, (i + by) % count) for i in range(count)])]
    ppermute x15, waiting for transfers between devices: 8.46 us -> 9.07 us  [swapped(): return lax.ppermute(value, ('tm', 'dp'), pairs)]
where the time goes in v15:
time: 54.9 us; the launch traced here: 54.7 us
  starting transfers between devices  21.5 us (39%)
  waiting for transfers between devices  17.5 us (32%)
  Pallas kernels  15 us (27%)
  between operations  0.75 us (1%)
    ppermute x15, starting transfers between devices, swapped(): return lax.ppermute(value, ('tm', 'dp'), pairs)  15.3 us
    ppermute x15, waiting for transfers between devices, swapped(): return lax.ppermute(value, ('tm', 'dp'), pairs)  9.07 us
    ppermute x3, waiting for transfers between devices, around(): return lax.ppermute(x, axis, [(i, (i + by) % count) for i in range(count)])  8.41 us
    ppermute x3, starting transfers between devices, around(): return lax.ppermute(x, axis, [(i, (i + by) % count) for i in range(count)])  6.22 us
    pallas_call x3, Pallas kernels, backward_of(): pl.pallas_call(functools.partial(backward_kernel, plans[step] | more, lay...  5.83 us
    pallas_call x1, Pallas kernels, run_layers(): pl.pallas_call(functools.partial(forward_kernel, plan), in_specs=[vmem] *...  3.67 us
    pallas_call x1, Pallas kernels, load_all(): pl.pallas_call(load_kernel, in_specs=[anywhere] * 7, out_specs=[vmem] * 6...  2.67 us
  transfers between devices with their start and end apart: 18, of which 8 were waited for; matrix products, arithmetic and copies ran while one was open for 0% of the time, Pallas kernels for 20%

profile of v15, /device:TPU:0, one launch (start us, length us, event | category | flops | bytes accessed | tf_op | source)
XLA Modules:
  0.0 54.7 jit_solution(5603655627005135573)
XLA Ops:
  0.6 1.0 %pack_borders.1 = (bf16[128,256]{1,0:T(8,128)(2,1)S(1)}, bf16[128,256]{1,0:T(8,128)(2,1)S(1)}) custom-call(bf16[512,256]{1,0:T(8,128)(2,1)} %bitcast.4, bf16[512,256]{1,0:T(8,128)(2,1)} %bitcast.6, bf16[512,256]{1,0:T(8,128)(2,1)} %bitcast.8, f32[1,512]{1,0:T(1,128)} %weight.3), custom_call_target="tpu_custom_call" | custom-call | tf_op jit(solution)/shard_map/pack_borders/pallas_call | solution.py:57
  1.6 3.0 %collective-permute-start = (bf16[128,256]{1,0:T(8,128)(2,1)S(1)}, bf16[128,256]{1,0:T(8,128)(2,1)S(1)}, u32[]{:S(2)}, u32[]{:S(2)}) collective-permute-start(bf16[128,256]{1,0:T(8,128)(2,1)S(1)} %get-tuple-element.29._), channel_id=1, source_target_pairs={{0,4},{4,8},{8,12},{12,16},{16,20},{20,24},{24,28},{28,0},{1,5},{5... | collective-permute-start | bytes 196616 | tf_op jit(solution)/shard_map/ppermute | solution.py:30
  4.6 1.5 %collective-permute-start.1 = (bf16[128,256]{1,0:T(8,128)(2,1)S(1)}, bf16[128,256]{1,0:T(8,128)(2,1)S(1)}, u32[]{:S(2)}, u32[]{:S(2)}) collective-permute-start(bf16[128,256]{1,0:T(8,128)(2,1)S(1)} %get-tuple-element.37), channel_id=1, source_target_pairs={{0,4},{4,8},{8,12},{12,16},{16,20},{20,24},{24,28},{28,0},{1,5},{5... | collective-permute-start | bytes 196616 | tf_op jit(solution)/shard_map/ppermute | solution.py:30
  6.1 2.7 %load_all.1 = (bf16[512,256]{1,0:T(8,128)(2,1)S(1)}, f32[512,256]{1,0:T(8,128)S(1)}, bf16[512,256]{1,0:T(8,128)(2,1)S(1)}, bf16[16,128]{1,0:T(8,128)(2,1)S(1)}, ...) custom-call(bf16[512,256]{1,0:T(8,128)(2,1)} %bitcast.5, bf16[512,256]{1,0:T(8,128)(2,1)} %bitcast.7, ...), custom_call_target="tpu_custom_call" | custom-call | flops 10000000 | bytes 6000000 | tf_op jit(solution)/shard_map/load_all/pallas_call | solution.py:92
  8.8 1.5 %collective-permute-done.prev_x = bf16[128,256]{1,0:T(8,128)(2,1)S(1)} collective-permute-done((bf16[128,256]{1,0:T(8,128)(2,1)S(1)}, bf16[128,256]{1,0:T(8,128)(2,1)S(1)}, u32[]{:S(2)}, u32[]{:S(2)}) %collective-permute-start) | collective-permute-done | bytes 65568 | tf_op jit(solution)/shard_map/ppermute | solution.py:30
  10.3 3.7 %forward.1 = (bf16[6,640,256]{2,1,0:T(8,128)(2,1)S(1)}, bf16[4,640,256]{2,1,0:T(8,128)(2,1)S(1)}, bf16[6,640,512]{2,1,0:T(8,128)(2,1)S(1)}, bf16[6,640,256]{2,1,0:T(8,128)(2,1)S(1)}) custom-call(bf16[128,256]{1,0:T(8,128)(2,1)S(1)} %collective-permute-done.prev_x, bf16[512,256]{1,0:T(8,128)(2,1)S(1)} %get-tuple-element.30.own_x, ...), custom_call_target="tpu_custom_call" | custom-call | flops 2013265920 | bytes 4718592 | tf_op jit(solution)/shard_map/forward/pallas_call | solution.py:319
  14.0 0.0 collective-permute-done.1.rest_0_
  14.0 2.0 %last_third.1 = (f32[576,256]{1,0:T(8,128)S(1)}, bf16[576,256]{1,0:T(8,128)(2,1)S(1)}, bf16[2,2,2,2,208,128]{5,4,3,2,1,0:T(8,128)(2,1)S(1)}, bf16[2,2,2,2,208,128]{5,4,3,2,1,0:T(8,128)(2,1)S(1)}) custom-call(bf16[6,640,256]{2,1,0:T(8,128)(2,1)S(1)} %get-tuple-element.33.all_present, bf16[4,640,256]{2,1,0:T(8,128)(2,1)S(1)} %get-tuple-element.34.all_earlier, ...), custom_call_target="tpu_custom_call" | custom-call | flops 1610612736 | bytes 4718592 | tf_op jit(solution)/shard_map/last_third/pallas_call | solution.py:337
  16.0 0.1 collective-permute-start.2
  16.1 1.9 %middle_third.1 = (f32[576,256]{1,0:T(8,128)S(1)}, bf16[2,2,2,2,192,128]{5,4,3,2,1,0:T(8,128)(2,1)S(1)}, bf16[2,2,2,2,192,128]{5,4,3,2,1,0:T(8,128)(2,1)S(1)}) custom-call(bf16[6,640,256]{2,1,0:T(8,128)(2,1)S(1)} %get-tuple-element.33.all_present, bf16[4,640,256]{2,1,0:T(8,128)(2,1)S(1)} %get-tuple-element.34.all_earlier, ...), custom_call_target="tpu_custom_call" | custom-call | flops 1610612736 | bytes 4718592 | tf_op jit(solution)/shard_map/middle_third/pallas_call | solution.py:337
  18.0 0.6 %collective-permute-start.8 = (bf16[2,2,2,2,192,128]{5,4,3,2,1,0:T(8,128)(2,1)S(1)}, bf16[2,2,2,2,192,128]{5,4,3,2,1,0:T(8,128)(2,1)S(1)}, u32[]{:S(2)}, u32[]{:S(2)}) collective-permute-start(bf16[2,2,2,2,192,128]{5,4,3,2,1,0:T(8,128)(2,1)S(1)} %get-tuple-element.49), channel_id=1, source_target_pairs={{0,1},{1,0},{2,3},{3,2},{4,5},{5,4},{6,7},{7,6},{8,9},{9,8},{10,11... | collective-permute-start | bytes 2359304 | tf_op jit(solution)/shard_map/ppermute | solution.py:464
  18.6 0.0 collective-permute-done.2.refs_1_.refs_13_
  18.6 0.1 add_chunk0_step1.1.rest_2_
  18.7 1.9 %first_third.1 = (bf16[64,256]{1,0:T(8,128)(2,1)S(1)}, f32[448,256]{1,0:T(8,128)S(1)}, bf16[2,2,2,2,192,128]{5,4,3,2,1,0:T(8,128)(2,1)S(1)}, bf16[2,2,2,2,192,128]{5,4,3,2,1,0:T(8,128)(2,1)S(1)}) custom-call(bf16[6,640,256]{2,1,0:T(8,128)(2,1)S(1)} %get-tuple-element.33.all_present, bf16[4,640,256]{2,1,0:T(8,128)(2,1)S(1)} %get-tuple-element.34.all_earlier, ...), custom_call_target="tpu_custom_call" | custom-call | flops 1610612736 | bytes 4718592 | tf_op jit(solution)/shard_map/first_third/pallas_call | solution.py:337
  20.6 0.1 collective-permute-start.3
  20.7 0.1 collective-permute-start.13
  20.8 0.0 collective-permute-done.8.refs_1_.refs_7_
  20.8 0.1 add_chunk1_step1.1
  20.9 1.6 %collective-permute-start.9 = (bf16[2,2,2,192,128]{4,3,2,1,0:T(8,128)(2,1)S(1)}, bf16[2,2,2,192,128]{4,3,2,1,0:T(8,128)(2,1)S(1)}, u32[]{:S(2)}, u32[]{:S(2)}) collective-permute-start(bf16[2,2,2,192,128]{4,3,2,1,0:T(8,128)(2,1)S(1)} %add_chunk1_step1.1), channel_id=1, source_target_pairs={{0,8},{1,9},{2,10},{3,11},{4,12},{5,13},{6,14},{7,15},{8,0},{9,1},... | collective-permute-start | bytes 1179656 | tf_op jit(solution)/shard_map/ppermute | solution.py:464
  22.5 0.5 collective-permute-done.3.refs_1_
  23.0 0.1 add_chunk2_step1.1
  23.1 2.0 %collective-permute-start.4 = (bf16[2,2,2,192,128]{4,3,2,1,0:T(8,128)(2,1)S(1)}, bf16[2,2,2,192,128]{4,3,2,1,0:T(8,128)(2,1)S(1)}, u32[]{:S(2)}, u32[]{:S(2)}) collective-permute-start(bf16[2,2,2,192,128]{4,3,2,1,0:T(8,128)(2,1)S(1)} %add_chunk2_step1.1), channel_id=1, source_target_pairs={{0,2},{1,3},{2,0},{3,1},{4,6},{5,7},{6,4},{7,5},{8,10},{9,11},{10,... | collective-permute-start | bytes 1179656 | tf_op jit(solution)/shard_map/ppermute | solution.py:464
  25.0 1.7 %collective-permute-start.14 = (bf16[64,256]{1,0:T(8,128)(2,1)S(1)}, bf16[64,256]{1,0:T(8,128)(2,1)S(1)}, u32[]{:S(2)}, u32[]{:S(2)}) collective-permute-start(bf16[64,256]{1,0:T(8,128)(2,1)S(1)} %get-tuple-element.50), channel_id=1, source_target_pairs={{0,28},{4,0},{8,4},{12,8},{16,12},{20,16},{24,20},{28,24},{1,29},{... | collective-permute-start | bytes 98312 | tf_op jit(solution)/shard_map/ppermute | solution.py:30
  26.7 6.9 %collective-permute-done.14.refs_3_.refs_18_ = bf16[64,256]{1,0:T(8,128)(2,1)S(1)} collective-permute-done((bf16[64,256]{1,0:T(8,128)(2,1)S(1)}, bf16[64,256]{1,0:T(8,128)(2,1)S(1)}, u32[]{:S(2)}, u32[]{:S(2)}) %collective-permute-start.14) | collective-permute-done | bytes 32800 | tf_op jit(solution)/shard_map/ppermute | solution.py:30
  33.6 0.0 collective-permute-done.13.refs_2_.refs_14_
  33.6 0.1 add_chunk0_step2.1
  33.7 0.2 collective-permute-start.15
  33.9 0.0 collective-permute-done.9.refs_2_.refs_8_
  34.0 0.1 add_chunk1_step2.1
  34.0 1.8 %collective-permute-start.10 = (bf16[2,2,192,128]{3,2,1,0:T(8,128)(2,1)S(1)}, bf16[2,2,192,128]{3,2,1,0:T(8,128)(2,1)S(1)}, u32[]{:S(2)}, u32[]{:S(2)}) collective-permute-start(bf16[2,2,192,128]{3,2,1,0:T(8,128)(2,1)S(1)} %add_chunk1_step2.1), channel_id=1, source_target_pairs={{0,2},{1,3},{2,0},{3,1},{4,6},{5,7},{6,4},{7,5},{8,10},{9,11},{10,... | collective-permute-start | bytes 589832 | tf_op jit(solution)/shard_map/ppermute | solution.py:464
  35.9 0.0 collective-permute-done.4.refs_2_
  35.9 0.1 add_chunk2_step2.1
  35.9 1.2 %collective-permute-start.5 = (bf16[2,2,192,128]{3,2,1,0:T(8,128)(2,1)S(1)}, bf16[2,2,192,128]{3,2,1,0:T(8,128)(2,1)S(1)}, u32[]{:S(2)}, u32[]{:S(2)}) collective-permute-start(bf16[2,2,192,128]{3,2,1,0:T(8,128)(2,1)S(1)} %add_chunk2_step2.1), channel_id=1, source_target_pairs={{0,4},{1,5},{2,6},{3,7},{4,0},{5,1},{6,2},{7,3},{8,12},{9,13},{10,... | collective-permute-start | bytes 589832 | tf_op jit(solution)/shard_map/ppermute | solution.py:464
  37.2 3.4 %collective-permute-done.15.refs_3_.refs_15_ = bf16[2,2,208,128]{3,2,1,0:T(8,128)(2,1)S(1)} collective-permute-done((bf16[2,2,208,128]{3,2,1,0:T(8,128)(2,1)S(1)}, bf16[2,2,208,128]{3,2,1,0:T(8,128)(2,1)S(1)}, u32[]{:S(2)}, u32[]{:S(2)}) %collective-permute-start.15) | collective-permute-done | bytes 213024 | tf_op jit(solution)/shard_map/ppermute | solution.py:464
  40.6 0.1 add_chunk0_step3.1
  40.7 2.0 %collective-permute-start.16 = (bf16[2,208,128]{2,1,0:T(8,128)(2,1)S(1)}, bf16[2,208,128]{2,1,0:T(8,128)(2,1)S(1)}, u32[]{:S(2)}, u32[]{:S(2)}) collective-permute-start(bf16[2,208,128]{2,1,0:T(8,128)(2,1)S(1)} %add_chunk0_step3.1), channel_id=1, source_target_pairs={{0,2},{1,3},{2,0},{3,1},{4,6},{5,7},{6,4},{7,5},{8,10},{9,11},{10,... | collective-permute-start | bytes 319496 | tf_op jit(solution)/shard_map/ppermute | solution.py:464
  42.6 0.0 collective-permute-done.10.refs_3_.refs_9_
  42.6 0.1 add_chunk1_step3.1
  42.7 0.7 %collective-permute-start.11 = (bf16[2,192,128]{2,1,0:T(8,128)(2,1)S(1)}, bf16[2,192,128]{2,1,0:T(8,128)(2,1)S(1)}, u32[]{:S(2)}, u32[]{:S(2)}) collective-permute-start(bf16[2,192,128]{2,1,0:T(8,128)(2,1)S(1)} %add_chunk1_step3.1), channel_id=1, source_target_pairs={{0,4},{1,5},{2,6},{3,7},{4,0},{5,1},{6,2},{7,3},{8,12},{9,13},{10,... | collective-permute-start | bytes 294920 | tf_op jit(solution)/shard_map/ppermute | solution.py:464
  43.4 0.0 collective-permute-done.5.refs_3_
  43.4 0.1 add_chunk2_step3.1
  43.4 0.7 %collective-permute-start.6 = (bf16[2,192,128]{2,1,0:T(8,128)(2,1)S(1)}, bf16[2,192,128]{2,1,0:T(8,128)(2,1)S(1)}, u32[]{:S(2)}, u32[]{:S(2)}) collective-permute-start(bf16[2,192,128]{2,1,0:T(8,128)(2,1)S(1)} %add_chunk2_step3.1), channel_id=1, source_target_pairs={{0,8},{1,9},{2,10},{3,11},{4,12},{5,13},{6,14},{7,15},{8,0},{9,1},... | collective-permute-start | bytes 294920 | tf_op jit(solution)/shard_map/ppermute | solution.py:464
  44.1 1.3 %collective-permute-done.16.refs_4_.refs_16_ = bf16[2,208,128]{2,1,0:T(8,128)(2,1)S(1)} collective-permute-done((bf16[2,208,128]{2,1,0:T(8,128)(2,1)S(1)}, bf16[2,208,128]{2,1,0:T(8,128)(2,1)S(1)}, u32[]{:S(2)}, u32[]{:S(2)}) %collective-permute-start.16) | collective-permute-done | bytes 106528 | tf_op jit(solution)/shard_map/ppermute | solution.py:464
  45.4 0.1 add_chunk0_step4.1
  45.5 1.2 %collective-permute-start.17 = (bf16[208,128]{1,0:T(8,128)(2,1)S(1)}, bf16[208,128]{1,0:T(8,128)(2,1)S(1)}, u32[]{:S(2)}, u32[]{:S(2)}) collective-permute-start(bf16[208,128]{1,0:T(8,128)(2,1)S(1)} %add_chunk0_step4.1), channel_id=1, source_target_pairs={{0,16},{1,17},{2,18},{3,19},{4,20},{5,21},{6,22},{7,23},{8,24},{9,... | collective-permute-start | bytes 159752 | tf_op jit(solution)/shard_map/ppermute | solution.py:464
  46.7 0.6 %collective-permute-done.11.refs_4_.refs_10_ = bf16[2,192,128]{2,1,0:T(8,128)(2,1)S(1)} collective-permute-done((bf16[2,192,128]{2,1,0:T(8,128)(2,1)S(1)}, bf16[2,192,128]{2,1,0:T(8,128)(2,1)S(1)}, u32[]{:S(2)}, u32[]{:S(2)}) %collective-permute-start.11) | collective-permute-done | bytes 98336 | tf_op jit(solution)/shard_map/ppermute | solution.py:464
  47.4 1.2 %collective-permute-start.12 = (bf16[192,128]{1,0:T(8,128)(2,1)S(1)}, bf16[192,128]{1,0:T(8,128)(2,1)S(1)}, u32[]{:S(2)}, u32[]{:S(2)}) collective-permute-start(bf16[192,128]{1,0:T(8,128)(2,1)S(1)} %add_chunk1_step4.1), channel_id=1, source_target_pairs={{0,16},{1,17},{2,18},{3,19},{4,20},{5,21},{6,22},{7,23},{8,24},{9,... | collective-permute-start | bytes 147464 | tf_op jit(solution)/shard_map/ppermute | solution.py:464
  48.6 0.0 collective-permute-done.6.refs_4_
  48.6 1.9 %collective-permute-start.7 = (bf16[192,128]{1,0:T(8,128)(2,1)S(1)}, bf16[192,128]{1,0:T(8,128)(2,1)S(1)}, u32[]{:S(2)}, u32[]{:S(2)}) collective-permute-start(bf16[192,128]{1,0:T(8,128)(2,1)S(1)} %add_chunk2_step4.1), channel_id=1, source_target_pairs={{0,16},{1,17},{2,18},{3,19},{4,20},{5,21},{6,22},{7,23},{8,24},{9,... | collective-permute-start | bytes 147464 | tf_op jit(solution)/shard_map/ppermute | solution.py:464
  50.5 2.5 %collective-permute-done.12.refs_11_ = bf16[192,128]{1,0:T(8,128)(2,1)S(1)} collective-permute-done((bf16[192,128]{1,0:T(8,128)(2,1)S(1)}, bf16[192,128]{1,0:T(8,128)(2,1)S(1)}, u32[]{:S(2)}, u32[]{:S(2)}) %collective-permute-start.12) | collective-permute-done | bytes 49184 | tf_op jit(solution)/shard_map/ppermute | solution.py:464
  53.0 0.0 collective-permute-done.17.refs_17_
  53.0 0.7 %collective-permute-done.7.refs_5_ = bf16[192,128]{1,0:T(8,128)(2,1)S(1)} collective-permute-done((bf16[192,128]{1,0:T(8,128)(2,1)S(1)}, bf16[192,128]{1,0:T(8,128)(2,1)S(1)}, u32[]{:S(2)}, u32[]{:S(2)}) %collective-permute-start.7) | collective-permute-done | bytes 49184 | tf_op jit(solution)/shard_map/ppermute | solution.py:464
  53.7 1.0 %scale_all.1 = (f32[512,256]{1,0:T(8,128)}, f32[6,64,128]{2,1,0:T(8,128)}, f32[6,32,128]{2,1,0:T(8,128)}) custom-call(bf16[2,2,2,2,192,128]{5,4,3,2,1,0:T(8,128)(2,1)S(1)} %get-tuple-element.46.refs_0_, bf16[2,2,2,2,192,128]{5,4,3,2,1,0:T(8,128)(2,1)S(1)} %collective-permute-done.3.refs_1_, bf16[2,2,2,192,128]{4,3,2,1,0:T(8,128)(2,1)S(1)} %collective-permute-done.4.refs_2_, ...), custom_call_target="tpu_custom_call" | custom-call | tf_op jit(solution)/shard_map/scale_all/pallas_call | solution.py:500
  (2 shorter events, 0.1 us)
Async XLA Ops:
  1.6 8.7 %collective-permute-start = (bf16[128,256]{1,0:T(8,128)(2,1)S(1)}, bf16[128,256]{1,0:T(8,128)(2,1)S(1)}, u32[]{:S(2)}, u32[]{:S(2)}) collective-permute-start(bf16[128,256]{1,0:T(8,128)(2,1)S(1)} %get-tuple-element.29._), channel_id=1, source_target_pairs={{0,4},{4,8},{8,12},{12,16},{16,20},{20,24},{24,28},{28,0},{1,5},{5... | collective-permute-start | bytes 196616 | tf_op jit(solution)/shard_map/ppermute | solution.py:30
  4.6 9.4 %collective-permute-start.1 = (bf16[128,256]{1,0:T(8,128)(2,1)S(1)}, bf16[128,256]{1,0:T(8,128)(2,1)S(1)}, u32[]{:S(2)}, u32[]{:S(2)}) collective-permute-start(bf16[128,256]{1,0:T(8,128)(2,1)S(1)} %get-tuple-element.37), channel_id=1, source_target_pairs={{0,4},{4,8},{8,12},{12,16},{16,20},{20,24},{24,28},{28,0},{1,5},{5... | collective-permute-start | bytes 196616 | tf_op jit(solution)/shard_map/ppermute | solution.py:30
  16.0 2.6 %collective-permute-start.2 = (bf16[2,2,2,2,208,128]{5,4,3,2,1,0:T(8,128)(2,1)S(1)}, bf16[2,2,2,2,208,128]{5,4,3,2,1,0:T(8,128)(2,1)S(1)}, u32[]{:S(2)}, u32[]{:S(2)}) collective-permute-start(bf16[2,2,2,2,208,128]{5,4,3,2,1,0:T(8,128)(2,1)S(1)} %get-tuple-element.45), channel_id=1, source_target_pairs={{0,1},{1,0},{2,3},{3,2},{4,5},{5,4},{6,7},{7,6},{8,9},{9,8},{10,11... | collective-permute-start | bytes 2555912 | tf_op jit(solution)/shard_map/ppermute | solution.py:464
  18.0 2.8 %collective-permute-start.8 = (bf16[2,2,2,2,192,128]{5,4,3,2,1,0:T(8,128)(2,1)S(1)}, bf16[2,2,2,2,192,128]{5,4,3,2,1,0:T(8,128)(2,1)S(1)}, u32[]{:S(2)}, u32[]{:S(2)}) collective-permute-start(bf16[2,2,2,2,192,128]{5,4,3,2,1,0:T(8,128)(2,1)S(1)} %get-tuple-element.49), channel_id=1, source_target_pairs={{0,1},{1,0},{2,3},{3,2},{4,5},{5,4},{6,7},{7,6},{8,9},{9,8},{10,11... | collective-permute-start | bytes 2359304 | tf_op jit(solution)/shard_map/ppermute | solution.py:464
  20.6 2.4 %collective-permute-start.3 = (bf16[2,2,2,2,192,128]{5,4,3,2,1,0:T(8,128)(2,1)S(1)}, bf16[2,2,2,2,192,128]{5,4,3,2,1,0:T(8,128)(2,1)S(1)}, u32[]{:S(2)}, u32[]{:S(2)}) collective-permute-start(bf16[2,2,2,2,192,128]{5,4,3,2,1,0:T(8,128)(2,1)S(1)} %get-tuple-element.47), channel_id=1, source_target_pairs={{0,1},{1,0},{2,3},{3,2},{4,5},{5,4},{6,7},{7,6},{8,9},{9,8},{10,11... | collective-permute-start | bytes 2359304 | tf_op jit(solution)/shard_map/ppermute | solution.py:464
  20.7 12.9 %collective-permute-start.13 = (bf16[2,2,2,208,128]{4,3,2,1,0:T(8,128)(2,1)S(1)}, bf16[2,2,2,208,128]{4,3,2,1,0:T(8,128)(2,1)S(1)}, u32[]{:S(2)}, u32[]{:S(2)}) collective-permute-start(bf16[2,2,2,208,128]{4,3,2,1,0:T(8,128)(2,1)S(1)} %add_chunk0_step1.1.rest_2_), channel_id=1, source_target_pairs={{0,4},{1,5},{2,6},{3,7},{4,0},{5,1},{6,2},{7,3},{8,12},{9,13},{10,... | collective-permute-start | bytes 1277960 | tf_op jit(solution)/shard_map/ppermute | solution.py:464
  20.9 13.1 %collective-permute-start.9 = (bf16[2,2,2,192,128]{4,3,2,1,0:T(8,128)(2,1)S(1)}, bf16[2,2,2,192,128]{4,3,2,1,0:T(8,128)(2,1)S(1)}, u32[]{:S(2)}, u32[]{:S(2)}) collective-permute-start(bf16[2,2,2,192,128]{4,3,2,1,0:T(8,128)(2,1)S(1)} %add_chunk1_step1.1), channel_id=1, source_target_pairs={{0,8},{1,9},{2,10},{3,11},{4,12},{5,13},{6,14},{7,15},{8,0},{9,1},... | collective-permute-start | bytes 1179656 | tf_op jit(solution)/shard_map/ppermute | solution.py:464
  23.1 12.8 %collective-permute-start.4 = (bf16[2,2,2,192,128]{4,3,2,1,0:T(8,128)(2,1)S(1)}, bf16[2,2,2,192,128]{4,3,2,1,0:T(8,128)(2,1)S(1)}, u32[]{:S(2)}, u32[]{:S(2)}) collective-permute-start(bf16[2,2,2,192,128]{4,3,2,1,0:T(8,128)(2,1)S(1)} %add_chunk2_step1.1), channel_id=1, source_target_pairs={{0,2},{1,3},{2,0},{3,1},{4,6},{5,7},{6,4},{7,5},{8,10},{9,11},{10,... | collective-permute-start | bytes 1179656 | tf_op jit(solution)/shard_map/ppermute | solution.py:464
  25.0 8.6 %collective-permute-start.14 = (bf16[64,256]{1,0:T(8,128)(2,1)S(1)}, bf16[64,256]{1,0:T(8,128)(2,1)S(1)}, u32[]{:S(2)}, u32[]{:S(2)}) collective-permute-start(bf16[64,256]{1,0:T(8,128)(2,1)S(1)} %get-tuple-element.50), channel_id=1, source_target_pairs={{0,28},{4,0},{8,4},{12,8},{16,12},{20,16},{24,20},{28,24},{1,29},{... | collective-permute-start | bytes 98312 | tf_op jit(solution)/shard_map/ppermute | solution.py:30
  33.7 6.9 %collective-permute-start.15 = (bf16[2,2,208,128]{3,2,1,0:T(8,128)(2,1)S(1)}, bf16[2,2,208,128]{3,2,1,0:T(8,128)(2,1)S(1)}, u32[]{:S(2)}, u32[]{:S(2)}) collective-permute-start(bf16[2,2,208,128]{3,2,1,0:T(8,128)(2,1)S(1)} %add_chunk0_step2.1), channel_id=1, source_target_pairs={{0,8},{1,9},{2,10},{3,11},{4,12},{5,13},{6,14},{7,15},{8,0},{9,1},... | collective-permute-start | bytes 638984 | tf_op jit(solution)/shard_map/ppermute | solution.py:464
  34.0 8.6 %collective-permute-start.10 = (bf16[2,2,192,128]{3,2,1,0:T(8,128)(2,1)S(1)}, bf16[2,2,192,128]{3,2,1,0:T(8,128)(2,1)S(1)}, u32[]{:S(2)}, u32[]{:S(2)}) collective-permute-start(bf16[2,2,192,128]{3,2,1,0:T(8,128)(2,1)S(1)} %add_chunk1_step2.1), channel_id=1, source_target_pairs={{0,2},{1,3},{2,0},{3,1},{4,6},{5,7},{6,4},{7,5},{8,10},{9,11},{10,... | collective-permute-start | bytes 589832 | tf_op jit(solution)/shard_map/ppermute | solution.py:464
  35.9 7.4 %collective-permute-start.5 = (bf16[2,2,192,128]{3,2,1,0:T(8,128)(2,1)S(1)}, bf16[2,2,192,128]{3,2,1,0:T(8,128)(2,1)S(1)}, u32[]{:S(2)}, u32[]{:S(2)}) collective-permute-start(bf16[2,2,192,128]{3,2,1,0:T(8,128)(2,1)S(1)} %add_chunk2_step2.1), channel_id=1, source_target_pairs={{0,4},{1,5},{2,6},{3,7},{4,0},{5,1},{6,2},{7,3},{8,12},{9,13},{10,... | collective-permute-start | bytes 589832 | tf_op jit(solution)/shard_map/ppermute | solution.py:464
  40.7 4.8 %collective-permute-start.16 = (bf16[2,208,128]{2,1,0:T(8,128)(2,1)S(1)}, bf16[2,208,128]{2,1,0:T(8,128)(2,1)S(1)}, u32[]{:S(2)}, u32[]{:S(2)}) collective-permute-start(bf16[2,208,128]{2,1,0:T(8,128)(2,1)S(1)} %add_chunk0_step3.1), channel_id=1, source_target_pairs={{0,2},{1,3},{2,0},{3,1},{4,6},{5,7},{6,4},{7,5},{8,10},{9,11},{10,... | collective-permute-start | bytes 319496 | tf_op jit(solution)/shard_map/ppermute | solution.py:464
  42.7 4.7 %collective-permute-start.11 = (bf16[2,192,128]{2,1,0:T(8,128)(2,1)S(1)}, bf16[2,192,128]{2,1,0:T(8,128)(2,1)S(1)}, u32[]{:S(2)}, u32[]{:S(2)}) collective-permute-start(bf16[2,192,128]{2,1,0:T(8,128)(2,1)S(1)} %add_chunk1_step3.1), channel_id=1, source_target_pairs={{0,4},{1,5},{2,6},{3,7},{4,0},{5,1},{6,2},{7,3},{8,12},{9,13},{10,... | collective-permute-start | bytes 294920 | tf_op jit(solution)/shard_map/ppermute | solution.py:464
  43.4 5.2 %collective-permute-start.6 = (bf16[2,192,128]{2,1,0:T(8,128)(2,1)S(1)}, bf16[2,192,128]{2,1,0:T(8,128)(2,1)S(1)}, u32[]{:S(2)}, u32[]{:S(2)}) collective-permute-start(bf16[2,192,128]{2,1,0:T(8,128)(2,1)S(1)} %add_chunk2_step3.1), channel_id=1, source_target_pairs={{0,8},{1,9},{2,10},{3,11},{4,12},{5,13},{6,14},{7,15},{8,0},{9,1},... | collective-permute-start | bytes 294920 | tf_op jit(solution)/shard_map/ppermute | solution.py:464
  45.5 7.5 %collective-permute-start.17 = (bf16[208,128]{1,0:T(8,128)(2,1)S(1)}, bf16[208,128]{1,0:T(8,128)(2,1)S(1)}, u32[]{:S(2)}, u32[]{:S(2)}) collective-permute-start(bf16[208,128]{1,0:T(8,128)(2,1)S(1)} %add_chunk0_step4.1), channel_id=1, source_target_pairs={{0,16},{1,17},{2,18},{3,19},{4,20},{5,21},{6,22},{7,23},{8,24},{9,... | collective-permute-start | bytes 159752 | tf_op jit(solution)/shard_map/ppermute | solution.py:464
  47.4 5.6 %collective-permute-start.12 = (bf16[192,128]{1,0:T(8,128)(2,1)S(1)}, bf16[192,128]{1,0:T(8,128)(2,1)S(1)}, u32[]{:S(2)}, u32[]{:S(2)}) collective-permute-start(bf16[192,128]{1,0:T(8,128)(2,1)S(1)} %add_chunk1_step4.1), channel_id=1, source_target_pairs={{0,16},{1,17},{2,18},{3,19},{4,20},{5,21},{6,22},{7,23},{8,24},{9,... | collective-permute-start | bytes 147464 | tf_op jit(solution)/shard_map/ppermute | solution.py:464
  48.6 5.1 %collective-permute-start.7 = (bf16[192,128]{1,0:T(8,128)(2,1)S(1)}, bf16[192,128]{1,0:T(8,128)(2,1)S(1)}, u32[]{:S(2)}, u32[]{:S(2)}) collective-permute-start(bf16[192,128]{1,0:T(8,128)(2,1)S(1)} %add_chunk2_step4.1), channel_id=1, source_target_pairs={{0,16},{1,17},{2,18},{3,19},{4,20},{5,21},{6,22},{7,23},{8,24},{9,... | collective-permute-start | bytes 147464 | tf_op jit(solution)/shard_map/ppermute | solution.py:464

commit v16 on v15

--- a/solution.py
+++ b/solution.py
@@ -38,35 +38,26 @@
     return pl.CostEstimate(flops=flops, bytes_accessed=moved, transcendentals=0)
 
 
-def pack_kernel(tail_x, tail_gs, tail_gk, weight, x_rows, grad_rows):
-    halo, channels = tail_gs.shape
-    by_row = column(weight[...], LANES)[LANES - halo :]
-    by_row = jnp.concatenate([by_row] * (channels // LANES), axis=1)
-    x_rows[...] = tail_x[...]
-    grad_rows[0:halo] = (tail_gs[...].astype(jnp.float32) * by_row).astype(jnp.bfloat16)
-    grad_rows[halo:] = (tail_gk[...].astype(jnp.float32) * by_row).astype(jnp.bfloat16)
-
-
-def pack(halo, x, grad_stream_out, grad_skip_out, weight):
-    length, channels = x.shape
-
-    def last(rows):
-        return pl.BlockSpec((rows, channels), lambda i: (length // rows - 1, 0))
-
-    message = jax.ShapeDtypeStruct((2 * halo, channels), jnp.bfloat16)
+def take_kernel(x, rows, sem):
+    copy = pltpu.make_async_copy(x.at[pl.ds(x.shape[0] - rows.shape[0], rows.shape[0])], rows, sem)
+    copy.start()
+    copy.wait()
+
+
+def last_rows(x, rows):
     return pl.pallas_call(
-        pack_kernel,
-        grid=(1,),
-        in_specs=[last(2 * halo), last(halo), last(halo), pl.BlockSpec((1, LANES), lambda i: (0, length // LANES - 1))],
-        out_specs=[pl.BlockSpec(message.shape, lambda i: (0, 0))] * 2,
-        out_shape=[message] * 2,
+        take_kernel,
+        in_specs=[pl.BlockSpec(memory_space=pl.ANY)],
+        out_specs=pl.BlockSpec(memory_space=pltpu.VMEM),
+        out_shape=pltpu.VMEM((rows, x.shape[1]), x.dtype),
+        scratch_shapes=[pltpu.SemaphoreType.DMA],
         compiler_params=pltpu.CompilerParams(vmem_limit_bytes=ADD_BYTES),
-        name="pack_borders",
-    )(*held((x, grad_stream_out, grad_skip_out, weight), pltpu.HBM))
+        name="take_border",
+    )(*held([x], pltpu.HBM))
 
 
 def load_kernel(
-    x, gs, gk, weight, conv_w, out_w, _, x_here, grad_stream, grad_skip, sums, conv_here, out_here,
+    x, gs, gk, weight, conv_w, out_w, _, x_here, grad_stream, grad_skip, sums, conv_here, out_here, grad_rows,
     gs_raw, gk_raw, weight_here, sems,
 ):
     pairs = ((weight, weight_here), (gs, gs_raw), (gk, gk_raw), (x, x_here), (conv_w, conv_here), (out_w, out_here))
@@ -80,19 +71,22 @@
     by_row = jnp.concatenate([by_row] * (channels // LANES), axis=1)
     grad_stream[...] = gs_raw[...].astype(jnp.float32) * by_row
     grad_skip[...] = (gk_raw[...].astype(jnp.float32) * by_row).astype(jnp.bfloat16)
+    halo = grad_rows.shape[0] // 2
+    grad_rows[0:halo] = grad_stream[length - halo :].astype(jnp.bfloat16)
+    grad_rows[halo:] = grad_skip[length - halo :]
     own_sum = jnp.broadcast_to(jnp.sum(weight_here[...], axis=1, keepdims=True), (1, LANES))
     sums[...] = split_rows(own_sum)
     for copy in copies[3:]:
         copy.wait()
 
 
-def load_all(x, gs, gk, weight, conv_w, out_w, after):
+def load_all(halo, x, gs, gk, weight, conv_w, out_w, after):
     shape = x.shape
     vmem, anywhere = pl.BlockSpec(memory_space=pltpu.VMEM), pl.BlockSpec(memory_space=pl.ANY)
     return pl.pallas_call(
         load_kernel,
         in_specs=[anywhere] * 7,
-        out_specs=[vmem] * 6,
+        out_specs=[vmem] * 7,
         out_shape=[
             pltpu.VMEM(shape, jnp.bfloat16),
             pltpu.VMEM(shape, jnp.float32),
@@ -100,6 +94,7 @@
             pltpu.VMEM((16, LANES), jnp.bfloat16),
             pltpu.VMEM(conv_w.shape, jnp.bfloat16),
             pltpu.VMEM(out_w.shape, jnp.bfloat16),
+            pltpu.VMEM((2 * halo, shape[1]), jnp.bfloat16),
         ],
         scratch_shapes=[
             pltpu.VMEM(shape, jnp.bfloat16),
@@ -413,12 +408,21 @@
     for count in counts:
         chunks.insert(0, refs[:count])
         refs = refs[count:]
-    other, own, grad_inputs, grad_conv, grad_out = refs
+    other, own, *results, grad_inputs, grad_conv, grad_out, sems = refs
     layers, channels = grad_conv.shape[0], own.shape[1]
     total = 0.0
     for term in chunks[0]:
         total = total + jnp.sum(first_block(term, term.shape[-2] - 16, 16), axis=0, keepdims=True)
     scale = samples_all / total
+    copies = [
+        pltpu.make_async_copy(here, result, sems.at[i])
+        for i, (here, result) in enumerate(zip((grad_inputs, grad_conv, grad_out), results))
+    ]
+    for first in range(0, channels, LANES):
+        lanes = slice(first, first + LANES)
+        grad_inputs[0 : own.shape[0], lanes] = own[:, lanes] * scale
+        grad_inputs[own.shape[0] :, lanes] = other[:, lanes].astype(jnp.float32) * scale
+    copies[0].start()
     for chunk, terms in enumerate(chunks):
         items = items_of(layers, chunk)
         for (index, is_out), base in zip(items, bases_of(items, tm, channels)[0]):
@@ -427,10 +431,10 @@
             for term in terms:
                 value = value + first_block(term, base, out.shape[1])
             out[index] = value * scale
-    for first in range(0, channels, LANES):
-        lanes = slice(first, first + LANES)
-        grad_inputs[0 : own.shape[0], lanes] = own[:, lanes] * scale
-        grad_inputs[own.shape[0] :, lanes] = other[:, lanes].astype(jnp.float32) * scale
+    for copy in copies[1:]:
+        copy.start()
+    for copy in copies:
+        copy.wait()
 
 
 class Chunk:
@@ -477,9 +481,10 @@
     halo = 2**layers
     samples_all = batch * length * tm * dp
     x, gs, gk = inputs[0], grad_stream_out[0], grad_skip_out[0]
-    x_rows, grad_rows = pack(halo, x, gs, gk, sample_weight)
-    borders = [around(x_rows, "tm", 1), around(grad_rows, "tm", 1)]
-    loaded = load_all(x, gs, gk, sample_weight, conv_weight, out_weight, x_rows)
+    x_rows = last_rows(x, 2 * halo)
+    prev_x = around(x_rows, "tm", 1)
+    *loaded, grad_rows = load_all(halo, x, gs, gk, sample_weight, conv_weight, out_weight, x_rows)
+    borders = [prev_x, around(grad_rows, "tm", 1)]
     in_shards = tm == 8 and dp == 4 and channels // tm % 16 == 0 and 2 * channels == dp * LANES
     other, own, parts = run_layers(in_shards, tm, dp, halo, borders, loaded)
     other = around(other, "tm", -1)
@@ -497,16 +502,17 @@
         return (jnp.concatenate([own, other]) * scale)[None], grad_conv, grad_out
     chunks = [part.run_chain([other] if part is parts[0] else ()) for part in parts]
     conv_rows, out_rows = 2 * channels // tm, channels // tm
+    shapes = [(length, channels), (layers, conv_rows, LANES), (layers, out_rows, LANES)]
+    terms = [term for group in reversed(chunks) for term in group]
     grad_inputs, grad_conv, grad_out = pl.pallas_call(
-        functools.partial(last_kernel, [len(terms) for terms in reversed(chunks)], float(samples_all), tm),
-        out_shape=[
-            jax.ShapeDtypeStruct((length, channels), jnp.float32),
-            jax.ShapeDtypeStruct((layers, conv_rows, LANES), jnp.float32),
-            jax.ShapeDtypeStruct((layers, out_rows, LANES), jnp.float32),
-        ],
+        functools.partial(last_kernel, [len(group) for group in reversed(chunks)], float(samples_all), tm),
+        in_specs=[pl.BlockSpec(memory_space=pltpu.VMEM)] * (len(terms) + 2),
+        out_specs=[pl.BlockSpec(memory_space=pl.ANY)] * len(shapes),
+        out_shape=[jax.ShapeDtypeStruct(shape, jnp.float32) for shape in shapes],
+        scratch_shapes=[pltpu.VMEM(shape, jnp.float32) for shape in shapes] + [pltpu.SemaphoreType.DMA((len(shapes),))],
         compiler_params=pltpu.CompilerParams(vmem_limit_bytes=ADD_BYTES),
         name="scale_all",
-    )(*held([term for terms in reversed(chunks) for term in terms]), *held([other, own]))
+    )(*held(terms), *held([other, own]))
     return grad_inputs[None], grad_conv, grad_out
 
 

time: 54.9 us -> 55.5 us (1.011)
  waiting for transfers between devices: 17.5 us -> 19.6 us
  starting transfers between devices: 21.5 us -> 20.2 us
    ppermute x15, waiting for transfers between devices: 9.07 us -> 10.6 us  [swapped(): return lax.ppermute(value, ('tm', 'dp'), pairs)]
    ppermute x15, starting transfers between devices: 15.3 us -> 13.8 us  [swapped(): return lax.ppermute(value, ('tm', 'dp'), pairs)]
  transfers between devices with their start and end apart: 18 -> 18, of which waited for: 8 -> 9; matrix products, arithmetic and copies ran while one was open for 0% -> 0% of each run, Pallas kernels for 20% -> 20%
where the time goes in v16:
time: 55.5 us; the launch traced here: 55.3 us
  starting transfers between devices  20.2 us (36%)
  waiting for transfers between devices  19.6 us (35%)
  Pallas kernels  14.8 us (27%)
  between operations  0.77 us (1%)
    ppermute x15, starting transfers between devices, swapped(): return lax.ppermute(value, ('tm', 'dp'), pairs)  13.8 us
    ppermute x15, waiting for transfers between devices, swapped(): return lax.ppermute(value, ('tm', 'dp'), pairs)  10.6 us
    ppermute x3, waiting for transfers between devices, around(): return lax.ppermute(x, axis, [(i, (i + by) % count) for i in range(count)])  8.96 us
    ppermute x3, starting transfers between devices, around(): return lax.ppermute(x, axis, [(i, (i + by) % count) for i in range(count)])  6.35 us
    pallas_call x3, Pallas kernels, backward_of(): pl.pallas_call(functools.partial(backward_kernel, plans[step] | more, lay...  5.83 us
    pallas_call x1, Pallas kernels, run_layers(): pl.pallas_call(functools.partial(forward_kernel, plan), in_specs=[vmem] *...  3.67 us
    pallas_call x1, Pallas kernels, load_all(): pl.pallas_call(load_kernel, in_specs=[anywhere] * 7, out_specs=[vmem] * 7...  2.67 us
  transfers between devices with their start and end apart: 18, of which 9 were waited for; matrix products, arithmetic and copies ran while one was open for 0% of the time, Pallas kernels for 20%

profile of v16, /device:TPU:0, one launch (start us, length us, event | category | flops | bytes accessed | tf_op | source)
XLA Modules:
  0.0 55.3 jit_solution(9819242486547150457)
XLA Ops:
  0.6 0.9 %take_border.1._ = bf16[128,256]{1,0:T(8,128)(2,1)S(1)} custom-call(bf16[512,256]{1,0:T(8,128)(2,1)} %bitcast.4), custom_call_target="tpu_custom_call" | custom-call | tf_op jit(solution)/shard_map/take_border/pallas_call | solution.py:48
  1.5 3.0 %collective-permute-start = (bf16[128,256]{1,0:T(8,128)(2,1)S(1)}, bf16[128,256]{1,0:T(8,128)(2,1)S(1)}, u32[]{:S(2)}, u32[]{:S(2)}) collective-permute-start(bf16[128,256]{1,0:T(8,128)(2,1)S(1)} %take_border.1._), channel_id=1, source_target_pairs={{0,4},{4,8},{8,12},{12,16},{16,20},{20,24},{24,28},{28,0},{1,5},{5... | collective-permute-start | bytes 196616 | tf_op jit(solution)/shard_map/ppermute | solution.py:30
  4.5 2.7 %load_all.1 = (bf16[512,256]{1,0:T(8,128)(2,1)S(1)}, f32[512,256]{1,0:T(8,128)S(1)}, bf16[512,256]{1,0:T(8,128)(2,1)S(1)}, bf16[16,128]{1,0:T(8,128)(2,1)S(1)}, ...) custom-call(bf16[512,256]{1,0:T(8,128)(2,1)} %bitcast.5, ...), custom_call_target="tpu_custom_call" | custom-call | flops 10000000 | bytes 6000000 | tf_op jit(solution)/shard_map/load_all/pallas_call | solution.py:86
  7.2 1.6 %collective-permute-start.1 = (bf16[128,256]{1,0:T(8,128)(2,1)S(1)}, bf16[128,256]{1,0:T(8,128)(2,1)S(1)}, u32[]{:S(2)}, u32[]{:S(2)}) collective-permute-start(bf16[128,256]{1,0:T(8,128)(2,1)S(1)} %get-tuple-element.35), channel_id=1, source_target_pairs={{0,4},{4,8},{8,12},{12,16},{16,20},{20,24},{24,28},{28,0},{1,5},{5... | collective-permute-start | bytes 196616 | tf_op jit(solution)/shard_map/ppermute | solution.py:30
  8.8 1.0 %collective-permute-done.prev_x = bf16[128,256]{1,0:T(8,128)(2,1)S(1)} collective-permute-done((bf16[128,256]{1,0:T(8,128)(2,1)S(1)}, bf16[128,256]{1,0:T(8,128)(2,1)S(1)}, u32[]{:S(2)}, u32[]{:S(2)}) %collective-permute-start) | collective-permute-done | bytes 65568 | tf_op jit(solution)/shard_map/ppermute | solution.py:30
  9.8 3.7 %forward.1 = (bf16[6,640,256]{2,1,0:T(8,128)(2,1)S(1)}, bf16[4,640,256]{2,1,0:T(8,128)(2,1)S(1)}, bf16[6,640,512]{2,1,0:T(8,128)(2,1)S(1)}, bf16[6,640,256]{2,1,0:T(8,128)(2,1)S(1)}) custom-call(bf16[128,256]{1,0:T(8,128)(2,1)S(1)} %collective-permute-done.prev_x, bf16[512,256]{1,0:T(8,128)(2,1)S(1)} %get-tuple-element.28.own_x, ...), custom_call_target="tpu_custom_call" | custom-call | flops 2013265920 | bytes 4718592 | tf_op jit(solution)/shard_map/forward/pallas_call | solution.py:314
  13.4 0.7 %collective-permute-done.1.rest_0_ = bf16[128,256]{1,0:T(8,128)(2,1)S(1)} collective-permute-done((bf16[128,256]{1,0:T(8,128)(2,1)S(1)}, bf16[128,256]{1,0:T(8,128)(2,1)S(1)}, u32[]{:S(2)}, u32[]{:S(2)}) %collective-permute-start.1) | collective-permute-done | bytes 65568 | tf_op jit(solution)/shard_map/ppermute | solution.py:30
  14.2 2.0 %last_third.1 = (f32[576,256]{1,0:T(8,128)S(1)}, bf16[576,256]{1,0:T(8,128)(2,1)S(1)}, bf16[2,2,2,2,208,128]{5,4,3,2,1,0:T(8,128)(2,1)S(1)}, bf16[2,2,2,2,208,128]{5,4,3,2,1,0:T(8,128)(2,1)S(1)}) custom-call(bf16[6,640,256]{2,1,0:T(8,128)(2,1)S(1)} %get-tuple-element.31.all_present, bf16[4,640,256]{2,1,0:T(8,128)(2,1)S(1)} %get-tuple-element.32.all_earlier, ...), custom_call_target="tpu_custom_call" | custom-call | flops 1610612736 | bytes 4718592 | tf_op jit(solution)/shard_map/last_third/pallas_call | solution.py:332
  16.2 0.1 collective-permute-start.2
  16.3 1.9 %middle_third.1 = (f32[576,256]{1,0:T(8,128)S(1)}, bf16[2,2,2,2,192,128]{5,4,3,2,1,0:T(8,128)(2,1)S(1)}, bf16[2,2,2,2,192,128]{5,4,3,2,1,0:T(8,128)(2,1)S(1)}) custom-call(bf16[6,640,256]{2,1,0:T(8,128)(2,1)S(1)} %get-tuple-element.31.all_present, bf16[4,640,256]{2,1,0:T(8,128)(2,1)S(1)} %get-tuple-element.32.all_earlier, ...), custom_call_target="tpu_custom_call" | custom-call | flops 1610612736 | bytes 4718592 | tf_op jit(solution)/shard_map/middle_third/pallas_call | solution.py:332
  18.2 0.6 %collective-permute-start.8 = (bf16[2,2,2,2,192,128]{5,4,3,2,1,0:T(8,128)(2,1)S(1)}, bf16[2,2,2,2,192,128]{5,4,3,2,1,0:T(8,128)(2,1)S(1)}, u32[]{:S(2)}, u32[]{:S(2)}) collective-permute-start(bf16[2,2,2,2,192,128]{5,4,3,2,1,0:T(8,128)(2,1)S(1)} %get-tuple-element.47), channel_id=1, source_target_pairs={{0,1},{1,0},{2,3},{3,2},{4,5},{5,4},{6,7},{7,6},{8,9},{9,8},{10,11... | collective-permute-start | bytes 2359304 | tf_op jit(solution)/shard_map/ppermute | solution.py:468
  18.7 0.0 collective-permute-done.2.refs_1_.refs_13_
  18.7 0.1 add_chunk0_step1.1.rest_2_
  18.9 1.9 %first_third.1 = (bf16[64,256]{1,0:T(8,128)(2,1)S(1)}, f32[448,256]{1,0:T(8,128)S(1)}, bf16[2,2,2,2,192,128]{5,4,3,2,1,0:T(8,128)(2,1)S(1)}, bf16[2,2,2,2,192,128]{5,4,3,2,1,0:T(8,128)(2,1)S(1)}) custom-call(bf16[6,640,256]{2,1,0:T(8,128)(2,1)S(1)} %get-tuple-element.31.all_present, bf16[4,640,256]{2,1,0:T(8,128)(2,1)S(1)} %get-tuple-element.32.all_earlier, ...), custom_call_target="tpu_custom_call" | custom-call | flops 1610612736 | bytes 4718592 | tf_op jit(solution)/shard_map/first_third/pallas_call | solution.py:332
  20.8 0.1 collective-permute-start.3
  20.9 0.1 collective-permute-start.13
  20.9 0.0 collective-permute-done.8.refs_1_.refs_7_
  20.9 0.1 add_chunk1_step1.1
  21.0 1.4 %collective-permute-start.9 = (bf16[2,2,2,192,128]{4,3,2,1,0:T(8,128)(2,1)S(1)}, bf16[2,2,2,192,128]{4,3,2,1,0:T(8,128)(2,1)S(1)}, u32[]{:S(2)}, u32[]{:S(2)}) collective-permute-start(bf16[2,2,2,192,128]{4,3,2,1,0:T(8,128)(2,1)S(1)} %add_chunk1_step1.1), channel_id=1, source_target_pairs={{0,8},{1,9},{2,10},{3,11},{4,12},{5,13},{6,14},{7,15},{8,0},{9,1},... | collective-permute-start | bytes 1179656 | tf_op jit(solution)/shard_map/ppermute | solution.py:468
  22.4 0.7 %collective-permute-done.3.refs_1_ = bf16[2,2,2,2,192,128]{5,4,3,2,1,0:T(8,128)(2,1)S(1)} collective-permute-done((bf16[2,2,2,2,192,128]{5,4,3,2,1,0:T(8,128)(2,1)S(1)}, bf16[2,2,2,2,192,128]{5,4,3,2,1,0:T(8,128)(2,1)S(1)}, u32[]{:S(2)}, u32[]{:S(2)}) %collective-permute-start.3) | collective-permute-done | bytes 786464 | tf_op jit(solution)/shard_map/ppermute | solution.py:468
  23.1 0.1 add_chunk2_step1.1
  23.2 1.6 %collective-permute-start.4 = (bf16[2,2,2,192,128]{4,3,2,1,0:T(8,128)(2,1)S(1)}, bf16[2,2,2,192,128]{4,3,2,1,0:T(8,128)(2,1)S(1)}, u32[]{:S(2)}, u32[]{:S(2)}) collective-permute-start(bf16[2,2,2,192,128]{4,3,2,1,0:T(8,128)(2,1)S(1)} %add_chunk2_step1.1), channel_id=1, source_target_pairs={{0,2},{1,3},{2,0},{3,1},{4,6},{5,7},{6,4},{7,5},{8,10},{9,11},{10,... | collective-permute-start | bytes 1179656 | tf_op jit(solution)/shard_map/ppermute | solution.py:468
  24.8 1.8 %collective-permute-start.14 = (bf16[64,256]{1,0:T(8,128)(2,1)S(1)}, bf16[64,256]{1,0:T(8,128)(2,1)S(1)}, u32[]{:S(2)}, u32[]{:S(2)}) collective-permute-start(bf16[64,256]{1,0:T(8,128)(2,1)S(1)} %get-tuple-element.48), channel_id=1, source_target_pairs={{0,28},{4,0},{8,4},{12,8},{16,12},{20,16},{24,20},{28,24},{1,29},{... | collective-permute-start | bytes 98312 | tf_op jit(solution)/shard_map/ppermute | solution.py:30
  26.6 7.2 %collective-permute-done.14.refs_3_.refs_18_ = bf16[64,256]{1,0:T(8,128)(2,1)S(1)} collective-permute-done((bf16[64,256]{1,0:T(8,128)(2,1)S(1)}, bf16[64,256]{1,0:T(8,128)(2,1)S(1)}, u32[]{:S(2)}, u32[]{:S(2)}) %collective-permute-start.14) | collective-permute-done | bytes 32800 | tf_op jit(solution)/shard_map/ppermute | solution.py:30
  33.8 0.0 collective-permute-done.13.refs_2_.refs_14_
  33.8 0.1 add_chunk0_step2.1
  33.9 0.1 collective-permute-start.15
  34.0 0.0 collective-permute-done.9.refs_2_.refs_8_
  34.0 0.1 add_chunk1_step2.1
  34.1 1.6 %collective-permute-start.10 = (bf16[2,2,192,128]{3,2,1,0:T(8,128)(2,1)S(1)}, bf16[2,2,192,128]{3,2,1,0:T(8,128)(2,1)S(1)}, u32[]{:S(2)}, u32[]{:S(2)}) collective-permute-start(bf16[2,2,192,128]{3,2,1,0:T(8,128)(2,1)S(1)} %add_chunk1_step2.1), channel_id=1, source_target_pairs={{0,2},{1,3},{2,0},{3,1},{4,6},{5,7},{6,4},{7,5},{8,10},{9,11},{10,... | collective-permute-start | bytes 589832 | tf_op jit(solution)/shard_map/ppermute | solution.py:468
  35.6 0.0 collective-permute-done.4.refs_2_
  35.6 0.1 add_chunk2_step2.1
  35.7 1.4 %collective-permute-start.5 = (bf16[2,2,192,128]{3,2,1,0:T(8,128)(2,1)S(1)}, bf16[2,2,192,128]{3,2,1,0:T(8,128)(2,1)S(1)}, u32[]{:S(2)}, u32[]{:S(2)}) collective-permute-start(bf16[2,2,192,128]{3,2,1,0:T(8,128)(2,1)S(1)} %add_chunk2_step2.1), channel_id=1, source_target_pairs={{0,4},{1,5},{2,6},{3,7},{4,0},{5,1},{6,2},{7,3},{8,12},{9,13},{10,... | collective-permute-start | bytes 589832 | tf_op jit(solution)/shard_map/ppermute | solution.py:468
  37.1 3.7 %collective-permute-done.15.refs_3_.refs_15_ = bf16[2,2,208,128]{3,2,1,0:T(8,128)(2,1)S(1)} collective-permute-done((bf16[2,2,208,128]{3,2,1,0:T(8,128)(2,1)S(1)}, bf16[2,2,208,128]{3,2,1,0:T(8,128)(2,1)S(1)}, u32[]{:S(2)}, u32[]{:S(2)}) %collective-permute-start.15) | collective-permute-done | bytes 213024 | tf_op jit(solution)/shard_map/ppermute | solution.py:468
  40.8 0.1 add_chunk0_step3.1
  40.8 1.6 %collective-permute-start.16 = (bf16[2,208,128]{2,1,0:T(8,128)(2,1)S(1)}, bf16[2,208,128]{2,1,0:T(8,128)(2,1)S(1)}, u32[]{:S(2)}, u32[]{:S(2)}) collective-permute-start(bf16[2,208,128]{2,1,0:T(8,128)(2,1)S(1)} %add_chunk0_step3.1), channel_id=1, source_target_pairs={{0,2},{1,3},{2,0},{3,1},{4,6},{5,7},{6,4},{7,5},{8,10},{9,11},{10,... | collective-permute-start | bytes 319496 | tf_op jit(solution)/shard_map/ppermute | solution.py:468
  42.4 0.0 collective-permute-done.10.refs_3_.refs_9_
  42.4 0.1 add_chunk1_step3.1
  42.5 0.7 %collective-permute-start.11 = (bf16[2,192,128]{2,1,0:T(8,128)(2,1)S(1)}, bf16[2,192,128]{2,1,0:T(8,128)(2,1)S(1)}, u32[]{:S(2)}, u32[]{:S(2)}) collective-permute-start(bf16[2,192,128]{2,1,0:T(8,128)(2,1)S(1)} %add_chunk1_step3.1), channel_id=1, source_target_pairs={{0,4},{1,5},{2,6},{3,7},{4,0},{5,1},{6,2},{7,3},{8,12},{9,13},{10,... | collective-permute-start | bytes 294920 | tf_op jit(solution)/shard_map/ppermute | solution.py:468
  43.2 0.0 collective-permute-done.5.refs_3_
  43.2 0.1 add_chunk2_step3.1
  43.2 0.8 %collective-permute-start.6 = (bf16[2,192,128]{2,1,0:T(8,128)(2,1)S(1)}, bf16[2,192,128]{2,1,0:T(8,128)(2,1)S(1)}, u32[]{:S(2)}, u32[]{:S(2)}) collective-permute-start(bf16[2,192,128]{2,1,0:T(8,128)(2,1)S(1)} %add_chunk2_step3.1), channel_id=1, source_target_pairs={{0,8},{1,9},{2,10},{3,11},{4,12},{5,13},{6,14},{7,15},{8,0},{9,1},... | collective-permute-start | bytes 294920 | tf_op jit(solution)/shard_map/ppermute | solution.py:468
  44.0 1.6 %collective-permute-done.16.refs_4_.refs_16_ = bf16[2,208,128]{2,1,0:T(8,128)(2,1)S(1)} collective-permute-done((bf16[2,208,128]{2,1,0:T(8,128)(2,1)S(1)}, bf16[2,208,128]{2,1,0:T(8,128)(2,1)S(1)}, u32[]{:S(2)}, u32[]{:S(2)}) %collective-permute-start.16) | collective-permute-done | bytes 106528 | tf_op jit(solution)/shard_map/ppermute | solution.py:468
  45.6 0.1 add_chunk0_step4.1
  45.7 0.9 %collective-permute-start.17 = (bf16[208,128]{1,0:T(8,128)(2,1)S(1)}, bf16[208,128]{1,0:T(8,128)(2,1)S(1)}, u32[]{:S(2)}, u32[]{:S(2)}) collective-permute-start(bf16[208,128]{1,0:T(8,128)(2,1)S(1)} %add_chunk0_step4.1), channel_id=1, source_target_pairs={{0,16},{1,17},{2,18},{3,19},{4,20},{5,21},{6,22},{7,23},{8,24},{9,... | collective-permute-start | bytes 159752 | tf_op jit(solution)/shard_map/ppermute | solution.py:468
  46.6 0.6 %collective-permute-done.11.refs_4_.refs_10_ = bf16[2,192,128]{2,1,0:T(8,128)(2,1)S(1)} collective-permute-done((bf16[2,192,128]{2,1,0:T(8,128)(2,1)S(1)}, bf16[2,192,128]{2,1,0:T(8,128)(2,1)S(1)}, u32[]{:S(2)}, u32[]{:S(2)}) %collective-permute-start.11) | collective-permute-done | bytes 98336 | tf_op jit(solution)/shard_map/ppermute | solution.py:468
  47.2 1.6 %collective-permute-start.12 = (bf16[192,128]{1,0:T(8,128)(2,1)S(1)}, bf16[192,128]{1,0:T(8,128)(2,1)S(1)}, u32[]{:S(2)}, u32[]{:S(2)}) collective-permute-start(bf16[192,128]{1,0:T(8,128)(2,1)S(1)} %add_chunk1_step4.1), channel_id=1, source_target_pairs={{0,16},{1,17},{2,18},{3,19},{4,20},{5,21},{6,22},{7,23},{8,24},{9,... | collective-permute-start | bytes 147464 | tf_op jit(solution)/shard_map/ppermute | solution.py:468
  48.8 0.0 collective-permute-done.6.refs_4_
  48.8 1.5 %collective-permute-start.7 = (bf16[192,128]{1,0:T(8,128)(2,1)S(1)}, bf16[192,128]{1,0:T(8,128)(2,1)S(1)}, u32[]{:S(2)}, u32[]{:S(2)}) collective-permute-start(bf16[192,128]{1,0:T(8,128)(2,1)S(1)} %add_chunk2_step4.1), channel_id=1, source_target_pairs={{0,16},{1,17},{2,18},{3,19},{4,20},{5,21},{6,22},{7,23},{8,24},{9,... | collective-permute-start | bytes 147464 | tf_op jit(solution)/shard_map/ppermute | solution.py:468
  50.3 2.5 %collective-permute-done.12.refs_11_ = bf16[192,128]{1,0:T(8,128)(2,1)S(1)} collective-permute-done((bf16[192,128]{1,0:T(8,128)(2,1)S(1)}, bf16[192,128]{1,0:T(8,128)(2,1)S(1)}, u32[]{:S(2)}, u32[]{:S(2)}) %collective-permute-start.12) | collective-permute-done | bytes 49184 | tf_op jit(solution)/shard_map/ppermute | solution.py:468
  52.8 0.0 collective-permute-done.17.refs_17_
  52.8 1.6 %collective-permute-done.7.refs_5_ = bf16[192,128]{1,0:T(8,128)(2,1)S(1)} collective-permute-done((bf16[192,128]{1,0:T(8,128)(2,1)S(1)}, bf16[192,128]{1,0:T(8,128)(2,1)S(1)}, u32[]{:S(2)}, u32[]{:S(2)}) %collective-permute-start.7) | collective-permute-done | bytes 49184 | tf_op jit(solution)/shard_map/ppermute | solution.py:468
  54.4 1.0 %scale_all.1 = (f32[512,256]{1,0:T(8,128)}, f32[6,64,128]{2,1,0:T(8,128)}, f32[6,32,128]{2,1,0:T(8,128)}) custom-call(bf16[2,2,2,2,192,128]{5,4,3,2,1,0:T(8,128)(2,1)S(1)} %get-tuple-element.44.refs_0_, bf16[2,2,2,2,192,128]{5,4,3,2,1,0:T(8,128)(2,1)S(1)} %collective-permute-done.3.refs_1_, bf16[2,2,2,192,128]{4,3,2,1,0:T(8,128)(2,1)S(1)} %collective-permute-done.4.refs_2_, ...), custom_call_target="tpu_custom_call" | custom-call | tf_op jit(solution)/shard_map/scale_all/pallas_call | solution.py:507
  (2 shorter events, 0.1 us)
Async XLA Ops:
  1.5 8.3 %collective-permute-start = (bf16[128,256]{1,0:T(8,128)(2,1)S(1)}, bf16[128,256]{1,0:T(8,128)(2,1)S(1)}, u32[]{:S(2)}, u32[]{:S(2)}) collective-permute-start(bf16[128,256]{1,0:T(8,128)(2,1)S(1)} %take_border.1._), channel_id=1, source_target_pairs={{0,4},{4,8},{8,12},{12,16},{16,20},{20,24},{24,28},{28,0},{1,5},{5... | collective-permute-start | bytes 196616 | tf_op jit(solution)/shard_map/ppermute | solution.py:30
  7.2 7.0 %collective-permute-start.1 = (bf16[128,256]{1,0:T(8,128)(2,1)S(1)}, bf16[128,256]{1,0:T(8,128)(2,1)S(1)}, u32[]{:S(2)}, u32[]{:S(2)}) collective-permute-start(bf16[128,256]{1,0:T(8,128)(2,1)S(1)} %get-tuple-element.35), channel_id=1, source_target_pairs={{0,4},{4,8},{8,12},{12,16},{16,20},{20,24},{24,28},{28,0},{1,5},{5... | collective-permute-start | bytes 196616 | tf_op jit(solution)/shard_map/ppermute | solution.py:30
  16.2 2.6 %collective-permute-start.2 = (bf16[2,2,2,2,208,128]{5,4,3,2,1,0:T(8,128)(2,1)S(1)}, bf16[2,2,2,2,208,128]{5,4,3,2,1,0:T(8,128)(2,1)S(1)}, u32[]{:S(2)}, u32[]{:S(2)}) collective-permute-start(bf16[2,2,2,2,208,128]{5,4,3,2,1,0:T(8,128)(2,1)S(1)} %get-tuple-element.43), channel_id=1, source_target_pairs={{0,1},{1,0},{2,3},{3,2},{4,5},{5,4},{6,7},{7,6},{8,9},{9,8},{10,11... | collective-permute-start | bytes 2555912 | tf_op jit(solution)/shard_map/ppermute | solution.py:468
  18.2 2.8 %collective-permute-start.8 = (bf16[2,2,2,2,192,128]{5,4,3,2,1,0:T(8,128)(2,1)S(1)}, bf16[2,2,2,2,192,128]{5,4,3,2,1,0:T(8,128)(2,1)S(1)}, u32[]{:S(2)}, u32[]{:S(2)}) collective-permute-start(bf16[2,2,2,2,192,128]{5,4,3,2,1,0:T(8,128)(2,1)S(1)} %get-tuple-element.47), channel_id=1, source_target_pairs={{0,1},{1,0},{2,3},{3,2},{4,5},{5,4},{6,7},{7,6},{8,9},{9,8},{10,11... | collective-permute-start | bytes 2359304 | tf_op jit(solution)/shard_map/ppermute | solution.py:468
  20.8 2.4 %collective-permute-start.3 = (bf16[2,2,2,2,192,128]{5,4,3,2,1,0:T(8,128)(2,1)S(1)}, bf16[2,2,2,2,192,128]{5,4,3,2,1,0:T(8,128)(2,1)S(1)}, u32[]{:S(2)}, u32[]{:S(2)}) collective-permute-start(bf16[2,2,2,2,192,128]{5,4,3,2,1,0:T(8,128)(2,1)S(1)} %get-tuple-element.45), channel_id=1, source_target_pairs={{0,1},{1,0},{2,3},{3,2},{4,5},{5,4},{6,7},{7,6},{8,9},{9,8},{10,11... | collective-permute-start | bytes 2359304 | tf_op jit(solution)/shard_map/ppermute | solution.py:468
  20.9 12.9 %collective-permute-start.13 = (bf16[2,2,2,208,128]{4,3,2,1,0:T(8,128)(2,1)S(1)}, bf16[2,2,2,208,128]{4,3,2,1,0:T(8,128)(2,1)S(1)}, u32[]{:S(2)}, u32[]{:S(2)}) collective-permute-start(bf16[2,2,2,208,128]{4,3,2,1,0:T(8,128)(2,1)S(1)} %add_chunk0_step1.1.rest_2_), channel_id=1, source_target_pairs={{0,4},{1,5},{2,6},{3,7},{4,0},{5,1},{6,2},{7,3},{8,12},{9,13},{10,... | collective-permute-start | bytes 1277960 | tf_op jit(solution)/shard_map/ppermute | solution.py:468
  21.0 12.9 %collective-permute-start.9 = (bf16[2,2,2,192,128]{4,3,2,1,0:T(8,128)(2,1)S(1)}, bf16[2,2,2,192,128]{4,3,2,1,0:T(8,128)(2,1)S(1)}, u32[]{:S(2)}, u32[]{:S(2)}) collective-permute-start(bf16[2,2,2,192,128]{4,3,2,1,0:T(8,128)(2,1)S(1)} %add_chunk1_step1.1), channel_id=1, source_target_pairs={{0,8},{1,9},{2,10},{3,11},{4,12},{5,13},{6,14},{7,15},{8,0},{9,1},... | collective-permute-start | bytes 1179656 | tf_op jit(solution)/shard_map/ppermute | solution.py:468
  23.2 12.4 %collective-permute-start.4 = (bf16[2,2,2,192,128]{4,3,2,1,0:T(8,128)(2,1)S(1)}, bf16[2,2,2,192,128]{4,3,2,1,0:T(8,128)(2,1)S(1)}, u32[]{:S(2)}, u32[]{:S(2)}) collective-permute-start(bf16[2,2,2,192,128]{4,3,2,1,0:T(8,128)(2,1)S(1)} %add_chunk2_step1.1), channel_id=1, source_target_pairs={{0,2},{1,3},{2,0},{3,1},{4,6},{5,7},{6,4},{7,5},{8,10},{9,11},{10,... | collective-permute-start | bytes 1179656 | tf_op jit(solution)/shard_map/ppermute | solution.py:468
  24.8 9.0 %collective-permute-start.14 = (bf16[64,256]{1,0:T(8,128)(2,1)S(1)}, bf16[64,256]{1,0:T(8,128)(2,1)S(1)}, u32[]{:S(2)}, u32[]{:S(2)}) collective-permute-start(bf16[64,256]{1,0:T(8,128)(2,1)S(1)} %get-tuple-element.48), channel_id=1, source_target_pairs={{0,28},{4,0},{8,4},{12,8},{16,12},{20,16},{24,20},{28,24},{1,29},{... | collective-permute-start | bytes 98312 | tf_op jit(solution)/shard_map/ppermute | solution.py:30
  33.9 6.9 %collective-permute-start.15 = (bf16[2,2,208,128]{3,2,1,0:T(8,128)(2,1)S(1)}, bf16[2,2,208,128]{3,2,1,0:T(8,128)(2,1)S(1)}, u32[]{:S(2)}, u32[]{:S(2)}) collective-permute-start(bf16[2,2,208,128]{3,2,1,0:T(8,128)(2,1)S(1)} %add_chunk0_step2.1), channel_id=1, source_target_pairs={{0,8},{1,9},{2,10},{3,11},{4,12},{5,13},{6,14},{7,15},{8,0},{9,1},... | collective-permute-start | bytes 638984 | tf_op jit(solution)/shard_map/ppermute | solution.py:468
  34.1 8.4 %collective-permute-start.10 = (bf16[2,2,192,128]{3,2,1,0:T(8,128)(2,1)S(1)}, bf16[2,2,192,128]{3,2,1,0:T(8,128)(2,1)S(1)}, u32[]{:S(2)}, u32[]{:S(2)}) collective-permute-start(bf16[2,2,192,128]{3,2,1,0:T(8,128)(2,1)S(1)} %add_chunk1_step2.1), channel_id=1, source_target_pairs={{0,2},{1,3},{2,0},{3,1},{4,6},{5,7},{6,4},{7,5},{8,10},{9,11},{10,... | collective-permute-start | bytes 589832 | tf_op jit(solution)/shard_map/ppermute | solution.py:468
  35.7 7.4 %collective-permute-start.5 = (bf16[2,2,192,128]{3,2,1,0:T(8,128)(2,1)S(1)}, bf16[2,2,192,128]{3,2,1,0:T(8,128)(2,1)S(1)}, u32[]{:S(2)}, u32[]{:S(2)}) collective-permute-start(bf16[2,2,192,128]{3,2,1,0:T(8,128)(2,1)S(1)} %add_chunk2_step2.1), channel_id=1, source_target_pairs={{0,4},{1,5},{2,6},{3,7},{4,0},{5,1},{6,2},{7,3},{8,12},{9,13},{10,... | collective-permute-start | bytes 589832 | tf_op jit(solution)/shard_map/ppermute | solution.py:468
  40.8 4.8 %collective-permute-start.16 = (bf16[2,208,128]{2,1,0:T(8,128)(2,1)S(1)}, bf16[2,208,128]{2,1,0:T(8,128)(2,1)S(1)}, u32[]{:S(2)}, u32[]{:S(2)}) collective-permute-start(bf16[2,208,128]{2,1,0:T(8,128)(2,1)S(1)} %add_chunk0_step3.1), channel_id=1, source_target_pairs={{0,2},{1,3},{2,0},{3,1},{4,6},{5,7},{6,4},{7,5},{8,10},{9,11},{10,... | collective-permute-start | bytes 319496 | tf_op jit(solution)/shard_map/ppermute | solution.py:468
  42.5 4.7 %collective-permute-start.11 = (bf16[2,192,128]{2,1,0:T(8,128)(2,1)S(1)}, bf16[2,192,128]{2,1,0:T(8,128)(2,1)S(1)}, u32[]{:S(2)}, u32[]{:S(2)}) collective-permute-start(bf16[2,192,128]{2,1,0:T(8,128)(2,1)S(1)} %add_chunk1_step3.1), channel_id=1, source_target_pairs={{0,4},{1,5},{2,6},{3,7},{4,0},{5,1},{6,2},{7,3},{8,12},{9,13},{10,... | collective-permute-start | bytes 294920 | tf_op jit(solution)/shard_map/ppermute | solution.py:468
  43.2 5.5 %collective-permute-start.6 = (bf16[2,192,128]{2,1,0:T(8,128)(2,1)S(1)}, bf16[2,192,128]{2,1,0:T(8,128)(2,1)S(1)}, u32[]{:S(2)}, u32[]{:S(2)}) collective-permute-start(bf16[2,192,128]{2,1,0:T(8,128)(2,1)S(1)} %add_chunk2_step3.1), channel_id=1, source_target_pairs={{0,8},{1,9},{2,10},{3,11},{4,12},{5,13},{6,14},{7,15},{8,0},{9,1},... | collective-permute-start | bytes 294920 | tf_op jit(solution)/shard_map/ppermute | solution.py:468
  45.7 7.1 %collective-permute-start.17 = (bf16[208,128]{1,0:T(8,128)(2,1)S(1)}, bf16[208,128]{1,0:T(8,128)(2,1)S(1)}, u32[]{:S(2)}, u32[]{:S(2)}) collective-permute-start(bf16[208,128]{1,0:T(8,128)(2,1)S(1)} %add_chunk0_step4.1), channel_id=1, source_target_pairs={{0,16},{1,17},{2,18},{3,19},{4,20},{5,21},{6,22},{7,23},{8,24},{9,... | collective-permute-start | bytes 159752 | tf_op jit(solution)/shard_map/ppermute | solution.py:468
  47.2 5.6 %collective-permute-start.12 = (bf16[192,128]{1,0:T(8,128)(2,1)S(1)}, bf16[192,128]{1,0:T(8,128)(2,1)S(1)}, u32[]{:S(2)}, u32[]{:S(2)}) collective-permute-start(bf16[192,128]{1,0:T(8,128)(2,1)S(1)} %add_chunk1_step4.1), channel_id=1, source_target_pairs={{0,16},{1,17},{2,18},{3,19},{4,20},{5,21},{6,22},{7,23},{8,24},{9,... | collective-permute-start | bytes 147464 | tf_op jit(solution)/shard_map/ppermute | solution.py:468
  48.8 5.6 %collective-permute-start.7 = (bf16[192,128]{1,0:T(8,128)(2,1)S(1)}, bf16[192,128]{1,0:T(8,128)(2,1)S(1)}, u32[]{:S(2)}, u32[]{:S(2)}) collective-permute-start(bf16[192,128]{1,0:T(8,128)(2,1)S(1)} %add_chunk2_step4.1), channel_id=1, source_target_pairs={{0,16},{1,17},{2,18},{3,19},{4,20},{5,21},{6,22},{7,23},{8,24},{9,... | collective-permute-start | bytes 147464 | tf_op jit(solution)/shard_map/ppermute | solution.py:468

commit v17 on v15

--- a/solution.py
+++ b/solution.py
@@ -143,7 +143,22 @@
     return jnp.concatenate([present[first - dilation : begin - dilation], cut, present[begin : last - dilation]])
 
 
-def backward(plan, layers, refs_of, conv_w, out_w, grad_proj, grad_stream, past_part, grad_parts):
+def moved_on(dilation, spread, past_part, grad_stream, halo, rows):
+    count, channels = spread.shape[0], grad_stream.shape[1]
+    past_part[0:count] = spread[:, channels:]
+    cut = slice(halo, halo + max(dilation, 8))
+    past_part[cut] = cut_off(past_part[cut], dilation)
+    grad_stream[0:rows] += spread[0:rows, :channels] + past_part[dilation : dilation + rows]
+
+
+def inputs_kernel(halo, preact, grad_before, conv_w, other, own, grad_stream, past_part):
+    grad_stream[...] = grad_before[...]
+    moved_on(1, dot(preact[...], conv_w[0], NT), past_part, grad_stream, halo, grad_stream.shape[0])
+    other[...] = grad_stream[0:halo].astype(other.dtype)
+    own[...] = grad_stream[halo:]
+
+
+def backward(plan, layers, refs_of, conv_w, out_w, grad_proj, grad_stream, past_part, grad_parts, last_preact):
     halo, length, channels = plan["halo"], plan["length"], plan["channels"]
     own = slice(halo, halo + length)
     items = plan["items"]
@@ -153,18 +168,16 @@
         present, earlier, factors, gates = refs_of(index)
         grad_proj[0:count, :channels] = grad_stream[0:count].astype(jnp.bfloat16)
         grad_gated = dot(grad_proj[0:count], out_w[index], NT)
-        total = dot(gates[own], grad_proj[0:length], TN)
-        plan["store"](total, items.index((index, True)), grad_parts)
         both = factors[halo : halo + count].astype(jnp.float32)
         grad_preact = jnp.concatenate(
             [grad_gated * both[:, :channels], grad_gated * both[:, channels:]], axis=1
         ).astype(jnp.bfloat16)
-        spread = dot(grad_preact, conv_w[index], NT)
-        past_part[0:count] = spread[:, channels:]
-        cut = slice(halo, halo + max(dilation, 8))
-        past_part[cut] = cut_off(past_part[cut], dilation)
-        rows = plan["counts"][index - 1] if index else length
-        grad_stream[0:rows] += spread[0:rows, :channels] + past_part[dilation : dilation + rows]
+        if index:
+            moved_on(dilation, dot(grad_preact, conv_w[index], NT), past_part, grad_stream, halo, plan["counts"][index - 1])
+        else:
+            last_preact[...] = grad_preact
+        total = dot(gates[own], grad_proj[0:length], TN)
+        plan["store"](total, items.index((index, True)), grad_parts)
         past = earlier_rows(plan, index, present, halo, halo + length) if earlier is None else earlier[own]
         total = dot(jnp.concatenate([present[own], past], axis=1), grad_preact[0:length], TN)
         plan["store"](total, items.index((index, False)), grad_parts)
@@ -228,12 +241,9 @@
 
     backward(
         plan, list(reversed(range(first, first + third))), refs_of, conv_w, out_w,
-        grad_proj, grad_stream, past_part, (keep, send),
+        grad_proj, grad_stream, past_part, (keep, send), outs[-1],
     )
-    at = 0
-    for out in outs:
-        out[...] = grad_stream[at : at + out.shape[0]].astype(out.dtype)
-        at += out.shape[0]
+    outs[0][...] = grad_stream[0 : outs[0].shape[0]]
     if plan["inputs"] == 4:
         plan["finish"](sums, (keep, send))
 
@@ -338,7 +348,7 @@
             functools.partial(backward_kernel, plans[step] | more, layers - (step + 1) * third, third),
             in_specs=[vmem] * (6 + len(inputs)) + [anywhere] * len(after),
             out_specs=[vmem] * (len(outs) + 2),
-            out_shape=[pltpu.VMEM((rows, channels), kind) for rows, kind in outs]
+            out_shape=[pltpu.VMEM((rows, wide), kind) for rows, wide, kind in outs]
             + [pltpu.VMEM(shape, jnp.bfloat16) for shape in shapes[step]],
             scratch_shapes=[
                 pltpu.VMEM((border, channels), jnp.float32),
@@ -350,18 +360,28 @@
             name=("last_third", "middle_third", "first_third")[step],
         )(*held((*kept, conv_w, out_w, *inputs, *after)))
 
-    whole = (border, jnp.float32)
+    whole = (border, channels, jnp.float32)
     grad_stream, grad_skip, *last = backward_of(
-        0, (borders[1], own_grad, own_skip, sums), [whole, (border, jnp.bfloat16)], []
+        0, (borders[1], own_grad, own_skip, sums), [whole, (border, channels, jnp.bfloat16)], []
     )
     parts = [last]
     if in_shards:
         parts[0] = Chunk(tm, dp, 0, *last)
     grad_stream, *middle = backward_of(1, (grad_stream, grad_skip), [whole], [])
-    other, own, *first = backward_of(
-        2, (grad_stream, grad_skip), [(halo, jnp.bfloat16), (length - halo, jnp.float32)],
+    grad_stream, preact, *first = backward_of(
+        2, (grad_stream, grad_skip), [(length, channels, jnp.float32), (counts[0], 2 * channels, jnp.bfloat16)],
         [parts[0].next_message()] if in_shards else [],
     )
+    other, own = pl.pallas_call(
+        functools.partial(inputs_kernel, halo),
+        in_specs=[vmem] * 3,
+        out_specs=[vmem] * 2,
+        out_shape=[pltpu.VMEM((halo, channels), jnp.bfloat16), pltpu.VMEM((length - halo, channels), jnp.float32)],
+        scratch_shapes=[pltpu.VMEM((length, channels), jnp.float32), pltpu.VMEM((counts[0], channels), jnp.float32)],
+        compiler_params=pltpu.CompilerParams(vmem_limit_bytes=ADD_BYTES),
+        cost_estimate=cost(flops * 4, weight_bytes // layers),
+        name="to_inputs",
+    )(*held((preact, grad_stream, conv_w)))
     parts += [middle, first]
     if in_shards:
         for step in (1, 2):

time: 54.9 us -> 55.6 us (1.013)
  Pallas kernels: 15 us -> 16.2 us
  waiting for transfers between devices: 17.5 us -> 16.9 us
    pallas_call x3, Pallas kernels: 5.83 us -> 6.62 us  [backward_of(): pl.pallas_call(functools.partial(backward_kernel, plans[step] | more, lay...]
  transfers between devices with their start and end apart: 18 -> 18, of which waited for: 8 -> 8; matrix products, arithmetic and copies ran while one was open for 0% -> 0% of each run, Pallas kernels for 20% -> 22%
where the time goes in v17:
time: 55.6 us; the launch traced here: 55.4 us
  starting transfers between devices  21.6 us (39%)
  waiting for transfers between devices  16.9 us (30%)
  Pallas kernels  16.2 us (29%)
  between operations  0.75 us (1%)
    ppermute x15, starting transfers between devices, swapped(): return lax.ppermute(value, ('tm', 'dp'), pairs)  15.3 us
    ppermute x15, waiting for transfers between devices, swapped(): return lax.ppermute(value, ('tm', 'dp'), pairs)  9.06 us
    ppermute x3, waiting for transfers between devices, around(): return lax.ppermute(x, axis, [(i, (i + by) % count) for i in range(count)])  7.87 us
    pallas_call x3, Pallas kernels, backward_of(): pl.pallas_call(functools.partial(backward_kernel, plans[step] | more, lay...  6.62 us
    ppermute x3, starting transfers between devices, around(): return lax.ppermute(x, axis, [(i, (i + by) % count) for i in range(count)])  6.27 us
    pallas_call x1, Pallas kernels, run_layers(): pl.pallas_call(functools.partial(forward_kernel, plan), in_specs=[vmem] *...  3.6 us
    pallas_call x1, Pallas kernels, load_all(): pl.pallas_call(load_kernel, in_specs=[anywhere] * 7, out_specs=[vmem] * 6...  2.67 us
  transfers between devices with their start and end apart: 18, of which 8 were waited for; matrix products, arithmetic and copies ran while one was open for 0% of the time, Pallas kernels for 22%

profile of v17, /device:TPU:0, one launch (start us, length us, event | category | flops | bytes accessed | tf_op | source)
XLA Modules:
  0.0 55.4 jit_solution(12366124654679135780)
XLA Ops:
  0.6 1.0 %pack_borders.1 = (bf16[128,256]{1,0:T(8,128)(2,1)S(1)}, bf16[128,256]{1,0:T(8,128)(2,1)S(1)}) custom-call(bf16[512,256]{1,0:T(8,128)(2,1)} %bitcast.4, bf16[512,256]{1,0:T(8,128)(2,1)} %bitcast.6, bf16[512,256]{1,0:T(8,128)(2,1)} %bitcast.8, f32[1,512]{1,0:T(1,128)} %weight.3), custom_call_target="tpu_custom_call" | custom-call | tf_op jit(solution)/shard_map/pack_borders/pallas_call | solution.py:57
  1.6 3.0 %collective-permute-start = (bf16[128,256]{1,0:T(8,128)(2,1)S(1)}, bf16[128,256]{1,0:T(8,128)(2,1)S(1)}, u32[]{:S(2)}, u32[]{:S(2)}) collective-permute-start(bf16[128,256]{1,0:T(8,128)(2,1)S(1)} %get-tuple-element.31._), channel_id=1, source_target_pairs={{0,4},{4,8},{8,12},{12,16},{16,20},{20,24},{24,28},{28,0},{1,5},{5... | collective-permute-start | bytes 196616 | tf_op jit(solution)/shard_map/ppermute | solution.py:30
  4.6 1.5 %collective-permute-start.1 = (bf16[128,256]{1,0:T(8,128)(2,1)S(1)}, bf16[128,256]{1,0:T(8,128)(2,1)S(1)}, u32[]{:S(2)}, u32[]{:S(2)}) collective-permute-start(bf16[128,256]{1,0:T(8,128)(2,1)S(1)} %get-tuple-element.39), channel_id=1, source_target_pairs={{0,4},{4,8},{8,12},{12,16},{16,20},{20,24},{24,28},{28,0},{1,5},{5... | collective-permute-start | bytes 196616 | tf_op jit(solution)/shard_map/ppermute | solution.py:30
  6.1 2.7 %load_all.1 = (bf16[512,256]{1,0:T(8,128)(2,1)S(1)}, f32[512,256]{1,0:T(8,128)S(1)}, bf16[512,256]{1,0:T(8,128)(2,1)S(1)}, bf16[16,128]{1,0:T(8,128)(2,1)S(1)}, ...) custom-call(bf16[512,256]{1,0:T(8,128)(2,1)} %bitcast.5, bf16[512,256]{1,0:T(8,128)(2,1)} %bitcast.7, ...), custom_call_target="tpu_custom_call" | custom-call | flops 10000000 | bytes 6000000 | tf_op jit(solution)/shard_map/load_all/pallas_call | solution.py:92
  8.8 1.5 %collective-permute-done.prev_x = bf16[128,256]{1,0:T(8,128)(2,1)S(1)} collective-permute-done((bf16[128,256]{1,0:T(8,128)(2,1)S(1)}, bf16[128,256]{1,0:T(8,128)(2,1)S(1)}, u32[]{:S(2)}, u32[]{:S(2)}) %collective-permute-start) | collective-permute-done | bytes 65568 | tf_op jit(solution)/shard_map/ppermute | solution.py:30
  10.3 3.6 %forward.1 = (bf16[6,640,256]{2,1,0:T(8,128)(2,1)S(1)}, bf16[4,640,256]{2,1,0:T(8,128)(2,1)S(1)}, bf16[6,640,512]{2,1,0:T(8,128)(2,1)S(1)}, bf16[6,640,256]{2,1,0:T(8,128)(2,1)S(1)}) custom-call(bf16[128,256]{1,0:T(8,128)(2,1)S(1)} %collective-permute-done.prev_x, bf16[512,256]{1,0:T(8,128)(2,1)S(1)} %get-tuple-element.32.own_x, ...), custom_call_target="tpu_custom_call" | custom-call | flops 2013265920 | bytes 4718592 | tf_op jit(solution)/shard_map/forward/pallas_call | solution.py:329
  13.9 0.0 collective-permute-done.1.rest_0_
  13.9 2.2 %last_third.1 = (f32[576,256]{1,0:T(8,128)S(1)}, bf16[576,256]{1,0:T(8,128)(2,1)S(1)}, bf16[2,2,2,2,208,128]{5,4,3,2,1,0:T(8,128)(2,1)S(1)}, bf16[2,2,2,2,208,128]{5,4,3,2,1,0:T(8,128)(2,1)S(1)}) custom-call(bf16[6,640,256]{2,1,0:T(8,128)(2,1)S(1)} %get-tuple-element.35.all_present, bf16[4,640,256]{2,1,0:T(8,128)(2,1)S(1)} %get-tuple-element.36.all_earlier, ...), custom_call_target="tpu_custom_call" | custom-call | flops 1610612736 | bytes 4718592 | tf_op jit(solution)/shard_map/last_third/pallas_call | solution.py:347
  16.1 0.1 collective-permute-start.2
  16.2 2.4 %middle_third.1 = (f32[576,256]{1,0:T(8,128)S(1)}, bf16[2,2,2,2,192,128]{5,4,3,2,1,0:T(8,128)(2,1)S(1)}, bf16[2,2,2,2,192,128]{5,4,3,2,1,0:T(8,128)(2,1)S(1)}) custom-call(bf16[6,640,256]{2,1,0:T(8,128)(2,1)S(1)} %get-tuple-element.35.all_present, bf16[4,640,256]{2,1,0:T(8,128)(2,1)S(1)} %get-tuple-element.36.all_earlier, ...), custom_call_target="tpu_custom_call" | custom-call | flops 1610612736 | bytes 4718592 | tf_op jit(solution)/shard_map/middle_third/pallas_call | solution.py:347
  18.6 0.6 %collective-permute-start.8 = (bf16[2,2,2,2,192,128]{5,4,3,2,1,0:T(8,128)(2,1)S(1)}, bf16[2,2,2,2,192,128]{5,4,3,2,1,0:T(8,128)(2,1)S(1)}, u32[]{:S(2)}, u32[]{:S(2)}) collective-permute-start(bf16[2,2,2,2,192,128]{5,4,3,2,1,0:T(8,128)(2,1)S(1)} %get-tuple-element.51), channel_id=1, source_target_pairs={{0,1},{1,0},{2,3},{3,2},{4,5},{5,4},{6,7},{7,6},{8,9},{9,8},{10,11... | collective-permute-start | bytes 2359304 | tf_op jit(solution)/shard_map/ppermute | solution.py:484
  19.2 0.0 collective-permute-done.2.refs_1_.refs_13_
  19.2 0.1 add_chunk0_step1.1.rest_2_
  19.3 2.0 %first_third.1 = (f32[512,256]{1,0:T(8,128)S(1)}, bf16[528,512]{1,0:T(8,128)(2,1)S(1)}, bf16[2,2,2,2,192,128]{5,4,3,2,1,0:T(8,128)(2,1)S(1)}, bf16[2,2,2,2,192,128]{5,4,3,2,1,0:T(8,128)(2,1)S(1)}) custom-call(bf16[6,640,256]{2,1,0:T(8,128)(2,1)S(1)} %get-tuple-element.35.all_present, bf16[4,640,256]{2,1,0:T(8,128)(2,1)S(1)} %get-tuple-element.36.all_earlier, ...), custom_call_target="tpu_custom_call" | custom-call | flops 1610612736 | bytes 4718592 | tf_op jit(solution)/shard_map/first_third/pallas_call | solution.py:347
  21.3 0.1 collective-permute-start.3
  21.4 0.1 collective-permute-start.13
  21.5 0.0 collective-permute-done.8.refs_1_.refs_7_
  21.5 0.1 add_chunk1_step1.1
  21.6 1.6 %collective-permute-start.9 = (bf16[2,2,2,192,128]{4,3,2,1,0:T(8,128)(2,1)S(1)}, bf16[2,2,2,192,128]{4,3,2,1,0:T(8,128)(2,1)S(1)}, u32[]{:S(2)}, u32[]{:S(2)}) collective-permute-start(bf16[2,2,2,192,128]{4,3,2,1,0:T(8,128)(2,1)S(1)} %add_chunk1_step1.1), channel_id=1, source_target_pairs={{0,8},{1,9},{2,10},{3,11},{4,12},{5,13},{6,14},{7,15},{8,0},{9,1},... | collective-permute-start | bytes 1179656 | tf_op jit(solution)/shard_map/ppermute | solution.py:484
  23.2 0.4 collective-permute-done.3.refs_1_
  23.7 0.1 add_chunk2_step1.1
  23.8 2.0 %collective-permute-start.4 = (bf16[2,2,2,192,128]{4,3,2,1,0:T(8,128)(2,1)S(1)}, bf16[2,2,2,192,128]{4,3,2,1,0:T(8,128)(2,1)S(1)}, u32[]{:S(2)}, u32[]{:S(2)}) collective-permute-start(bf16[2,2,2,192,128]{4,3,2,1,0:T(8,128)(2,1)S(1)} %add_chunk2_step1.1), channel_id=1, source_target_pairs={{0,2},{1,3},{2,0},{3,1},{4,6},{5,7},{6,4},{7,5},{8,10},{9,11},{10,... | collective-permute-start | bytes 1179656 | tf_op jit(solution)/shard_map/ppermute | solution.py:484
  25.7 0.5 to_inputs.1
  26.2 1.7 %collective-permute-start.14 = (bf16[64,256]{1,0:T(8,128)(2,1)S(1)}, bf16[64,256]{1,0:T(8,128)(2,1)S(1)}, u32[]{:S(2)}, u32[]{:S(2)}) collective-permute-start(bf16[64,256]{1,0:T(8,128)(2,1)S(1)} %get-tuple-element.54), channel_id=1, source_target_pairs={{0,28},{4,0},{8,4},{12,8},{16,12},{20,16},{24,20},{28,24},{1,29},{... | collective-permute-start | bytes 98312 | tf_op jit(solution)/shard_map/ppermute | solution.py:30
  28.0 6.4 %collective-permute-done.14.refs_3_.refs_18_ = bf16[64,256]{1,0:T(8,128)(2,1)S(1)} collective-permute-done((bf16[64,256]{1,0:T(8,128)(2,1)S(1)}, bf16[64,256]{1,0:T(8,128)(2,1)S(1)}, u32[]{:S(2)}, u32[]{:S(2)}) %collective-permute-start.14) | collective-permute-done | bytes 32800 | tf_op jit(solution)/shard_map/ppermute | solution.py:30
  34.3 0.0 collective-permute-done.13.refs_2_.refs_14_
  34.3 0.1 add_chunk0_step2.1
  34.4 0.2 collective-permute-start.15
  34.7 0.0 collective-permute-done.9.refs_2_.refs_8_
  34.7 0.1 add_chunk1_step2.1
  34.7 1.8 %collective-permute-start.10 = (bf16[2,2,192,128]{3,2,1,0:T(8,128)(2,1)S(1)}, bf16[2,2,192,128]{3,2,1,0:T(8,128)(2,1)S(1)}, u32[]{:S(2)}, u32[]{:S(2)}) collective-permute-start(bf16[2,2,192,128]{3,2,1,0:T(8,128)(2,1)S(1)} %add_chunk1_step2.1), channel_id=1, source_target_pairs={{0,2},{1,3},{2,0},{3,1},{4,6},{5,7},{6,4},{7,5},{8,10},{9,11},{10,... | collective-permute-start | bytes 589832 | tf_op jit(solution)/shard_map/ppermute | solution.py:484
  36.6 0.0 collective-permute-done.4.refs_2_
  36.6 0.1 add_chunk2_step2.1
  36.7 1.2 %collective-permute-start.5 = (bf16[2,2,192,128]{3,2,1,0:T(8,128)(2,1)S(1)}, bf16[2,2,192,128]{3,2,1,0:T(8,128)(2,1)S(1)}, u32[]{:S(2)}, u32[]{:S(2)}) collective-permute-start(bf16[2,2,192,128]{3,2,1,0:T(8,128)(2,1)S(1)} %add_chunk2_step2.1), channel_id=1, source_target_pairs={{0,4},{1,5},{2,6},{3,7},{4,0},{5,1},{6,2},{7,3},{8,12},{9,13},{10,... | collective-permute-start | bytes 589832 | tf_op jit(solution)/shard_map/ppermute | solution.py:484
  37.9 3.4 %collective-permute-done.15.refs_3_.refs_15_ = bf16[2,2,208,128]{3,2,1,0:T(8,128)(2,1)S(1)} collective-permute-done((bf16[2,2,208,128]{3,2,1,0:T(8,128)(2,1)S(1)}, bf16[2,2,208,128]{3,2,1,0:T(8,128)(2,1)S(1)}, u32[]{:S(2)}, u32[]{:S(2)}) %collective-permute-start.15) | collective-permute-done | bytes 213024 | tf_op jit(solution)/shard_map/ppermute | solution.py:484
  41.3 0.1 add_chunk0_step3.1
  41.4 2.0 %collective-permute-start.16 = (bf16[2,208,128]{2,1,0:T(8,128)(2,1)S(1)}, bf16[2,208,128]{2,1,0:T(8,128)(2,1)S(1)}, u32[]{:S(2)}, u32[]{:S(2)}) collective-permute-start(bf16[2,208,128]{2,1,0:T(8,128)(2,1)S(1)} %add_chunk0_step3.1), channel_id=1, source_target_pairs={{0,2},{1,3},{2,0},{3,1},{4,6},{5,7},{6,4},{7,5},{8,10},{9,11},{10,... | collective-permute-start | bytes 319496 | tf_op jit(solution)/shard_map/ppermute | solution.py:484
  43.4 0.0 collective-permute-done.10.refs_3_.refs_9_
  43.4 0.1 add_chunk1_step3.1
  43.4 0.7 %collective-permute-start.11 = (bf16[2,192,128]{2,1,0:T(8,128)(2,1)S(1)}, bf16[2,192,128]{2,1,0:T(8,128)(2,1)S(1)}, u32[]{:S(2)}, u32[]{:S(2)}) collective-permute-start(bf16[2,192,128]{2,1,0:T(8,128)(2,1)S(1)} %add_chunk1_step3.1), channel_id=1, source_target_pairs={{0,4},{1,5},{2,6},{3,7},{4,0},{5,1},{6,2},{7,3},{8,12},{9,13},{10,... | collective-permute-start | bytes 294920 | tf_op jit(solution)/shard_map/ppermute | solution.py:484
  44.1 0.0 collective-permute-done.5.refs_3_
  44.1 0.1 add_chunk2_step3.1
  44.2 0.7 %collective-permute-start.6 = (bf16[2,192,128]{2,1,0:T(8,128)(2,1)S(1)}, bf16[2,192,128]{2,1,0:T(8,128)(2,1)S(1)}, u32[]{:S(2)}, u32[]{:S(2)}) collective-permute-start(bf16[2,192,128]{2,1,0:T(8,128)(2,1)S(1)} %add_chunk2_step3.1), channel_id=1, source_target_pairs={{0,8},{1,9},{2,10},{3,11},{4,12},{5,13},{6,14},{7,15},{8,0},{9,1},... | collective-permute-start | bytes 294920 | tf_op jit(solution)/shard_map/ppermute | solution.py:484
  44.8 1.3 %collective-permute-done.16.refs_4_.refs_16_ = bf16[2,208,128]{2,1,0:T(8,128)(2,1)S(1)} collective-permute-done((bf16[2,208,128]{2,1,0:T(8,128)(2,1)S(1)}, bf16[2,208,128]{2,1,0:T(8,128)(2,1)S(1)}, u32[]{:S(2)}, u32[]{:S(2)}) %collective-permute-start.16) | collective-permute-done | bytes 106528 | tf_op jit(solution)/shard_map/ppermute | solution.py:484
  46.2 0.1 add_chunk0_step4.1
  46.2 1.2 %collective-permute-start.17 = (bf16[208,128]{1,0:T(8,128)(2,1)S(1)}, bf16[208,128]{1,0:T(8,128)(2,1)S(1)}, u32[]{:S(2)}, u32[]{:S(2)}) collective-permute-start(bf16[208,128]{1,0:T(8,128)(2,1)S(1)} %add_chunk0_step4.1), channel_id=1, source_target_pairs={{0,16},{1,17},{2,18},{3,19},{4,20},{5,21},{6,22},{7,23},{8,24},{9,... | collective-permute-start | bytes 159752 | tf_op jit(solution)/shard_map/ppermute | solution.py:484
  47.4 0.6 %collective-permute-done.11.refs_4_.refs_10_ = bf16[2,192,128]{2,1,0:T(8,128)(2,1)S(1)} collective-permute-done((bf16[2,192,128]{2,1,0:T(8,128)(2,1)S(1)}, bf16[2,192,128]{2,1,0:T(8,128)(2,1)S(1)}, u32[]{:S(2)}, u32[]{:S(2)}) %collective-permute-start.11) | collective-permute-done | bytes 98336 | tf_op jit(solution)/shard_map/ppermute | solution.py:484
  48.1 1.2 %collective-permute-start.12 = (bf16[192,128]{1,0:T(8,128)(2,1)S(1)}, bf16[192,128]{1,0:T(8,128)(2,1)S(1)}, u32[]{:S(2)}, u32[]{:S(2)}) collective-permute-start(bf16[192,128]{1,0:T(8,128)(2,1)S(1)} %add_chunk1_step4.1), channel_id=1, source_target_pairs={{0,16},{1,17},{2,18},{3,19},{4,20},{5,21},{6,22},{7,23},{8,24},{9,... | collective-permute-start | bytes 147464 | tf_op jit(solution)/shard_map/ppermute | solution.py:484
  49.3 0.0 collective-permute-done.6.refs_4_
  49.4 1.9 %collective-permute-start.7 = (bf16[192,128]{1,0:T(8,128)(2,1)S(1)}, bf16[192,128]{1,0:T(8,128)(2,1)S(1)}, u32[]{:S(2)}, u32[]{:S(2)}) collective-permute-start(bf16[192,128]{1,0:T(8,128)(2,1)S(1)} %add_chunk2_step4.1), channel_id=1, source_target_pairs={{0,16},{1,17},{2,18},{3,19},{4,20},{5,21},{6,22},{7,23},{8,24},{9,... | collective-permute-start | bytes 147464 | tf_op jit(solution)/shard_map/ppermute | solution.py:484
  51.2 2.5 %collective-permute-done.12.refs_11_ = bf16[192,128]{1,0:T(8,128)(2,1)S(1)} collective-permute-done((bf16[192,128]{1,0:T(8,128)(2,1)S(1)}, bf16[192,128]{1,0:T(8,128)(2,1)S(1)}, u32[]{:S(2)}, u32[]{:S(2)}) %collective-permute-start.12) | collective-permute-done | bytes 49184 | tf_op jit(solution)/shard_map/ppermute | solution.py:484
  53.7 0.0 collective-permute-done.17.refs_17_
  53.7 0.7 %collective-permute-done.7.refs_5_ = bf16[192,128]{1,0:T(8,128)(2,1)S(1)} collective-permute-done((bf16[192,128]{1,0:T(8,128)(2,1)S(1)}, bf16[192,128]{1,0:T(8,128)(2,1)S(1)}, u32[]{:S(2)}, u32[]{:S(2)}) %collective-permute-start.7) | collective-permute-done | bytes 49184 | tf_op jit(solution)/shard_map/ppermute | solution.py:484
  54.4 1.0 %scale_all.1 = (f32[512,256]{1,0:T(8,128)}, f32[6,64,128]{2,1,0:T(8,128)}, f32[6,32,128]{2,1,0:T(8,128)}) custom-call(bf16[2,2,2,2,192,128]{5,4,3,2,1,0:T(8,128)(2,1)S(1)} %get-tuple-element.48.refs_0_, bf16[2,2,2,2,192,128]{5,4,3,2,1,0:T(8,128)(2,1)S(1)} %collective-permute-done.3.refs_1_, bf16[2,2,2,192,128]{4,3,2,1,0:T(8,128)(2,1)S(1)} %collective-permute-done.4.refs_2_, ...), custom_call_target="tpu_custom_call" | custom-call | tf_op jit(solution)/shard_map/scale_all/pallas_call | solution.py:520
  (2 shorter events, 0.1 us)
Async XLA Ops:
  1.6 8.7 %collective-permute-start = (bf16[128,256]{1,0:T(8,128)(2,1)S(1)}, bf16[128,256]{1,0:T(8,128)(2,1)S(1)}, u32[]{:S(2)}, u32[]{:S(2)}) collective-permute-start(bf16[128,256]{1,0:T(8,128)(2,1)S(1)} %get-tuple-element.31._), channel_id=1, source_target_pairs={{0,4},{4,8},{8,12},{12,16},{16,20},{20,24},{24,28},{28,0},{1,5},{5... | collective-permute-start | bytes 196616 | tf_op jit(solution)/shard_map/ppermute | solution.py:30
  4.6 9.3 %collective-permute-start.1 = (bf16[128,256]{1,0:T(8,128)(2,1)S(1)}, bf16[128,256]{1,0:T(8,128)(2,1)S(1)}, u32[]{:S(2)}, u32[]{:S(2)}) collective-permute-start(bf16[128,256]{1,0:T(8,128)(2,1)S(1)} %get-tuple-element.39), channel_id=1, source_target_pairs={{0,4},{4,8},{8,12},{12,16},{16,20},{20,24},{24,28},{28,0},{1,5},{5... | collective-permute-start | bytes 196616 | tf_op jit(solution)/shard_map/ppermute | solution.py:30
  16.1 3.1 %collective-permute-start.2 = (bf16[2,2,2,2,208,128]{5,4,3,2,1,0:T(8,128)(2,1)S(1)}, bf16[2,2,2,2,208,128]{5,4,3,2,1,0:T(8,128)(2,1)S(1)}, u32[]{:S(2)}, u32[]{:S(2)}) collective-permute-start(bf16[2,2,2,2,208,128]{5,4,3,2,1,0:T(8,128)(2,1)S(1)} %get-tuple-element.47), channel_id=1, source_target_pairs={{0,1},{1,0},{2,3},{3,2},{4,5},{5,4},{6,7},{7,6},{8,9},{9,8},{10,11... | collective-permute-start | bytes 2555912 | tf_op jit(solution)/shard_map/ppermute | solution.py:484
  18.6 2.8 %collective-permute-start.8 = (bf16[2,2,2,2,192,128]{5,4,3,2,1,0:T(8,128)(2,1)S(1)}, bf16[2,2,2,2,192,128]{5,4,3,2,1,0:T(8,128)(2,1)S(1)}, u32[]{:S(2)}, u32[]{:S(2)}) collective-permute-start(bf16[2,2,2,2,192,128]{5,4,3,2,1,0:T(8,128)(2,1)S(1)} %get-tuple-element.51), channel_id=1, source_target_pairs={{0,1},{1,0},{2,3},{3,2},{4,5},{5,4},{6,7},{7,6},{8,9},{9,8},{10,11... | collective-permute-start | bytes 2359304 | tf_op jit(solution)/shard_map/ppermute | solution.py:484
  21.3 2.4 %collective-permute-start.3 = (bf16[2,2,2,2,192,128]{5,4,3,2,1,0:T(8,128)(2,1)S(1)}, bf16[2,2,2,2,192,128]{5,4,3,2,1,0:T(8,128)(2,1)S(1)}, u32[]{:S(2)}, u32[]{:S(2)}) collective-permute-start(bf16[2,2,2,2,192,128]{5,4,3,2,1,0:T(8,128)(2,1)S(1)} %get-tuple-element.49), channel_id=1, source_target_pairs={{0,1},{1,0},{2,3},{3,2},{4,5},{5,4},{6,7},{7,6},{8,9},{9,8},{10,11... | collective-permute-start | bytes 2359304 | tf_op jit(solution)/shard_map/ppermute | solution.py:484
  21.4 12.9 %collective-permute-start.13 = (bf16[2,2,2,208,128]{4,3,2,1,0:T(8,128)(2,1)S(1)}, bf16[2,2,2,208,128]{4,3,2,1,0:T(8,128)(2,1)S(1)}, u32[]{:S(2)}, u32[]{:S(2)}) collective-permute-start(bf16[2,2,2,208,128]{4,3,2,1,0:T(8,128)(2,1)S(1)} %add_chunk0_step1.1.rest_2_), channel_id=1, source_target_pairs={{0,4},{1,5},{2,6},{3,7},{4,0},{5,1},{6,2},{7,3},{8,12},{9,13},{10,... | collective-permute-start | bytes 1277960 | tf_op jit(solution)/shard_map/ppermute | solution.py:484
  21.6 13.1 %collective-permute-start.9 = (bf16[2,2,2,192,128]{4,3,2,1,0:T(8,128)(2,1)S(1)}, bf16[2,2,2,192,128]{4,3,2,1,0:T(8,128)(2,1)S(1)}, u32[]{:S(2)}, u32[]{:S(2)}) collective-permute-start(bf16[2,2,2,192,128]{4,3,2,1,0:T(8,128)(2,1)S(1)} %add_chunk1_step1.1), channel_id=1, source_target_pairs={{0,8},{1,9},{2,10},{3,11},{4,12},{5,13},{6,14},{7,15},{8,0},{9,1},... | collective-permute-start | bytes 1179656 | tf_op jit(solution)/shard_map/ppermute | solution.py:484
  23.8 12.8 %collective-permute-start.4 = (bf16[2,2,2,192,128]{4,3,2,1,0:T(8,128)(2,1)S(1)}, bf16[2,2,2,192,128]{4,3,2,1,0:T(8,128)(2,1)S(1)}, u32[]{:S(2)}, u32[]{:S(2)}) collective-permute-start(bf16[2,2,2,192,128]{4,3,2,1,0:T(8,128)(2,1)S(1)} %add_chunk2_step1.1), channel_id=1, source_target_pairs={{0,2},{1,3},{2,0},{3,1},{4,6},{5,7},{6,4},{7,5},{8,10},{9,11},{10,... | collective-permute-start | bytes 1179656 | tf_op jit(solution)/shard_map/ppermute | solution.py:484
  26.2 8.1 %collective-permute-start.14 = (bf16[64,256]{1,0:T(8,128)(2,1)S(1)}, bf16[64,256]{1,0:T(8,128)(2,1)S(1)}, u32[]{:S(2)}, u32[]{:S(2)}) collective-permute-start(bf16[64,256]{1,0:T(8,128)(2,1)S(1)} %get-tuple-element.54), channel_id=1, source_target_pairs={{0,28},{4,0},{8,4},{12,8},{16,12},{20,16},{24,20},{28,24},{1,29},{... | collective-permute-start | bytes 98312 | tf_op jit(solution)/shard_map/ppermute | solution.py:30
  34.4 6.9 %collective-permute-start.15 = (bf16[2,2,208,128]{3,2,1,0:T(8,128)(2,1)S(1)}, bf16[2,2,208,128]{3,2,1,0:T(8,128)(2,1)S(1)}, u32[]{:S(2)}, u32[]{:S(2)}) collective-permute-start(bf16[2,2,208,128]{3,2,1,0:T(8,128)(2,1)S(1)} %add_chunk0_step2.1), channel_id=1, source_target_pairs={{0,8},{1,9},{2,10},{3,11},{4,12},{5,13},{6,14},{7,15},{8,0},{9,1},... | collective-permute-start | bytes 638984 | tf_op jit(solution)/shard_map/ppermute | solution.py:484
  34.7 8.6 %collective-permute-start.10 = (bf16[2,2,192,128]{3,2,1,0:T(8,128)(2,1)S(1)}, bf16[2,2,192,128]{3,2,1,0:T(8,128)(2,1)S(1)}, u32[]{:S(2)}, u32[]{:S(2)}) collective-permute-start(bf16[2,2,192,128]{3,2,1,0:T(8,128)(2,1)S(1)} %add_chunk1_step2.1), channel_id=1, source_target_pairs={{0,2},{1,3},{2,0},{3,1},{4,6},{5,7},{6,4},{7,5},{8,10},{9,11},{10,... | collective-permute-start | bytes 589832 | tf_op jit(solution)/shard_map/ppermute | solution.py:484
  36.7 7.4 %collective-permute-start.5 = (bf16[2,2,192,128]{3,2,1,0:T(8,128)(2,1)S(1)}, bf16[2,2,192,128]{3,2,1,0:T(8,128)(2,1)S(1)}, u32[]{:S(2)}, u32[]{:S(2)}) collective-permute-start(bf16[2,2,192,128]{3,2,1,0:T(8,128)(2,1)S(1)} %add_chunk2_step2.1), channel_id=1, source_target_pairs={{0,4},{1,5},{2,6},{3,7},{4,0},{5,1},{6,2},{7,3},{8,12},{9,13},{10,... | collective-permute-start | bytes 589832 | tf_op jit(solution)/shard_map/ppermute | solution.py:484
  41.4 4.8 %collective-permute-start.16 = (bf16[2,208,128]{2,1,0:T(8,128)(2,1)S(1)}, bf16[2,208,128]{2,1,0:T(8,128)(2,1)S(1)}, u32[]{:S(2)}, u32[]{:S(2)}) collective-permute-start(bf16[2,208,128]{2,1,0:T(8,128)(2,1)S(1)} %add_chunk0_step3.1), channel_id=1, source_target_pairs={{0,2},{1,3},{2,0},{3,1},{4,6},{5,7},{6,4},{7,5},{8,10},{9,11},{10,... | collective-permute-start | bytes 319496 | tf_op jit(solution)/shard_map/ppermute | solution.py:484
  43.4 4.7 %collective-permute-start.11 = (bf16[2,192,128]{2,1,0:T(8,128)(2,1)S(1)}, bf16[2,192,128]{2,1,0:T(8,128)(2,1)S(1)}, u32[]{:S(2)}, u32[]{:S(2)}) collective-permute-start(bf16[2,192,128]{2,1,0:T(8,128)(2,1)S(1)} %add_chunk1_step3.1), channel_id=1, source_target_pairs={{0,4},{1,5},{2,6},{3,7},{4,0},{5,1},{6,2},{7,3},{8,12},{9,13},{10,... | collective-permute-start | bytes 294920 | tf_op jit(solution)/shard_map/ppermute | solution.py:484
  44.2 5.2 %collective-permute-start.6 = (bf16[2,192,128]{2,1,0:T(8,128)(2,1)S(1)}, bf16[2,192,128]{2,1,0:T(8,128)(2,1)S(1)}, u32[]{:S(2)}, u32[]{:S(2)}) collective-permute-start(bf16[2,192,128]{2,1,0:T(8,128)(2,1)S(1)} %add_chunk2_step3.1), channel_id=1, source_target_pairs={{0,8},{1,9},{2,10},{3,11},{4,12},{5,13},{6,14},{7,15},{8,0},{9,1},... | collective-permute-start | bytes 294920 | tf_op jit(solution)/shard_map/ppermute | solution.py:484
  46.2 7.5 %collective-permute-start.17 = (bf16[208,128]{1,0:T(8,128)(2,1)S(1)}, bf16[208,128]{1,0:T(8,128)(2,1)S(1)}, u32[]{:S(2)}, u32[]{:S(2)}) collective-permute-start(bf16[208,128]{1,0:T(8,128)(2,1)S(1)} %add_chunk0_step4.1), channel_id=1, source_target_pairs={{0,16},{1,17},{2,18},{3,19},{4,20},{5,21},{6,22},{7,23},{8,24},{9,... | collective-permute-start | bytes 159752 | tf_op jit(solution)/shard_map/ppermute | solution.py:484
  48.1 5.6 %collective-permute-start.12 = (bf16[192,128]{1,0:T(8,128)(2,1)S(1)}, bf16[192,128]{1,0:T(8,128)(2,1)S(1)}, u32[]{:S(2)}, u32[]{:S(2)}) collective-permute-start(bf16[192,128]{1,0:T(8,128)(2,1)S(1)} %add_chunk1_step4.1), channel_id=1, source_target_pairs={{0,16},{1,17},{2,18},{3,19},{4,20},{5,21},{6,22},{7,23},{8,24},{9,... | collective-permute-start | bytes 147464 | tf_op jit(solution)/shard_map/ppermute | solution.py:484
  49.4 5.1 %collective-permute-start.7 = (bf16[192,128]{1,0:T(8,128)(2,1)S(1)}, bf16[192,128]{1,0:T(8,128)(2,1)S(1)}, u32[]{:S(2)}, u32[]{:S(2)}) collective-permute-start(bf16[192,128]{1,0:T(8,128)(2,1)S(1)} %add_chunk2_step4.1), channel_id=1, source_target_pairs={{0,16},{1,17},{2,18},{3,19},{4,20},{5,21},{6,22},{7,23},{8,24},{9,... | collective-permute-start | bytes 147464 | tf_op jit(solution)/shard_map/ppermute | solution.py:484

commit v18 on v17

--- a/solution.py
+++ b/solution.py
@@ -168,6 +168,8 @@
         present, earlier, factors, gates = refs_of(index)
         grad_proj[0:count, :channels] = grad_stream[0:count].astype(jnp.bfloat16)
         grad_gated = dot(grad_proj[0:count], out_w[index], NT)
+        total = dot(gates[own], grad_proj[0:length], TN)
+        plan["store"](total, items.index((index, True)), grad_parts)
         both = factors[halo : halo + count].astype(jnp.float32)
         grad_preact = jnp.concatenate(
             [grad_gated * both[:, :channels], grad_gated * both[:, channels:]], axis=1
@@ -176,8 +178,6 @@
             moved_on(dilation, dot(grad_preact, conv_w[index], NT), past_part, grad_stream, halo, plan["counts"][index - 1])
         else:
             last_preact[...] = grad_preact
-        total = dot(gates[own], grad_proj[0:length], TN)
-        plan["store"](total, items.index((index, True)), grad_parts)
         past = earlier_rows(plan, index, present, halo, halo + length) if earlier is None else earlier[own]
         total = dot(jnp.concatenate([present[own], past], axis=1), grad_preact[0:length], TN)
         plan["store"](total, items.index((index, False)), grad_parts)

time: 55.6 us -> 54.6 us (0.982)
  Pallas kernels: 16.2 us -> 15.2 us
    pallas_call x3, Pallas kernels: 6.62 us -> 5.62 us  [backward_of(): pl.pallas_call(functools.partial(backward_kernel, plans[step] | more, lay...]
  transfers between devices with their start and end apart: 18 -> 18, of which waited for: 8 -> 8; matrix products, arithmetic and copies ran while one was open for 0% -> 0% of each run, Pallas kernels for 22% -> 21%
where the time goes in v18:
time: 54.6 us; the launch traced here: 54.4 us
  starting transfers between devices  21.6 us (40%)
  waiting for transfers between devices  16.9 us (31%)
  Pallas kernels  15.2 us (28%)
  between operations  0.75 us (1%)
    ppermute x15, starting transfers between devices, swapped(): return lax.ppermute(value, ('tm', 'dp'), pairs)  15.3 us
    ppermute x15, waiting for transfers between devices, swapped(): return lax.ppermute(value, ('tm', 'dp'), pairs)  9.06 us
    ppermute x3, waiting for transfers between devices, around(): return lax.ppermute(x, axis, [(i, (i + by) % count) for i in range(count)])  7.87 us
    ppermute x3, starting transfers between devices, around(): return lax.ppermute(x, axis, [(i, (i + by) % count) for i in range(count)])  6.27 us
    pallas_call x3, Pallas kernels, backward_of(): pl.pallas_call(functools.partial(backward_kernel, plans[step] | more, lay...  5.62 us
    pallas_call x1, Pallas kernels, run_layers(): pl.pallas_call(functools.partial(forward_kernel, plan), in_specs=[vmem] *...  3.6 us
    pallas_call x1, Pallas kernels, load_all(): pl.pallas_call(load_kernel, in_specs=[anywhere] * 7, out_specs=[vmem] * 6...  2.67 us
  transfers between devices with their start and end apart: 18, of which 8 were waited for; matrix products, arithmetic and copies ran while one was open for 0% of the time, Pallas kernels for 21%

profile of v18, /device:TPU:0, one launch (start us, length us, event | category | flops | bytes accessed | tf_op | source)
XLA Modules:
  0.0 54.4 jit_solution(5330155687817172064)
XLA Ops:
  0.6 1.0 %pack_borders.1 = (bf16[128,256]{1,0:T(8,128)(2,1)S(1)}, bf16[128,256]{1,0:T(8,128)(2,1)S(1)}) custom-call(bf16[512,256]{1,0:T(8,128)(2,1)} %bitcast.4, bf16[512,256]{1,0:T(8,128)(2,1)} %bitcast.6, bf16[512,256]{1,0:T(8,128)(2,1)} %bitcast.8, f32[1,512]{1,0:T(1,128)} %weight.3), custom_call_target="tpu_custom_call" | custom-call | tf_op jit(solution)/shard_map/pack_borders/pallas_call | solution.py:57
  1.6 3.0 %collective-permute-start = (bf16[128,256]{1,0:T(8,128)(2,1)S(1)}, bf16[128,256]{1,0:T(8,128)(2,1)S(1)}, u32[]{:S(2)}, u32[]{:S(2)}) collective-permute-start(bf16[128,256]{1,0:T(8,128)(2,1)S(1)} %get-tuple-element.31._), channel_id=1, source_target_pairs={{0,4},{4,8},{8,12},{12,16},{16,20},{20,24},{24,28},{28,0},{1,5},{5... | collective-permute-start | bytes 196616 | tf_op jit(solution)/shard_map/ppermute | solution.py:30
  4.6 1.5 %collective-permute-start.1 = (bf16[128,256]{1,0:T(8,128)(2,1)S(1)}, bf16[128,256]{1,0:T(8,128)(2,1)S(1)}, u32[]{:S(2)}, u32[]{:S(2)}) collective-permute-start(bf16[128,256]{1,0:T(8,128)(2,1)S(1)} %get-tuple-element.39), channel_id=1, source_target_pairs={{0,4},{4,8},{8,12},{12,16},{16,20},{20,24},{24,28},{28,0},{1,5},{5... | collective-permute-start | bytes 196616 | tf_op jit(solution)/shard_map/ppermute | solution.py:30
  6.1 2.7 %load_all.1 = (bf16[512,256]{1,0:T(8,128)(2,1)S(1)}, f32[512,256]{1,0:T(8,128)S(1)}, bf16[512,256]{1,0:T(8,128)(2,1)S(1)}, bf16[16,128]{1,0:T(8,128)(2,1)S(1)}, ...) custom-call(bf16[512,256]{1,0:T(8,128)(2,1)} %bitcast.5, bf16[512,256]{1,0:T(8,128)(2,1)} %bitcast.7, ...), custom_call_target="tpu_custom_call" | custom-call | flops 10000000 | bytes 6000000 | tf_op jit(solution)/shard_map/load_all/pallas_call | solution.py:92
  8.8 1.5 %collective-permute-done.prev_x = bf16[128,256]{1,0:T(8,128)(2,1)S(1)} collective-permute-done((bf16[128,256]{1,0:T(8,128)(2,1)S(1)}, bf16[128,256]{1,0:T(8,128)(2,1)S(1)}, u32[]{:S(2)}, u32[]{:S(2)}) %collective-permute-start) | collective-permute-done | bytes 65568 | tf_op jit(solution)/shard_map/ppermute | solution.py:30
  10.3 3.6 %forward.1 = (bf16[6,640,256]{2,1,0:T(8,128)(2,1)S(1)}, bf16[4,640,256]{2,1,0:T(8,128)(2,1)S(1)}, bf16[6,640,512]{2,1,0:T(8,128)(2,1)S(1)}, bf16[6,640,256]{2,1,0:T(8,128)(2,1)S(1)}) custom-call(bf16[128,256]{1,0:T(8,128)(2,1)S(1)} %collective-permute-done.prev_x, bf16[512,256]{1,0:T(8,128)(2,1)S(1)} %get-tuple-element.32.own_x, ...), custom_call_target="tpu_custom_call" | custom-call | flops 2013265920 | bytes 4718592 | tf_op jit(solution)/shard_map/forward/pallas_call | solution.py:329
  13.9 0.0 collective-permute-done.1.rest_0_
  13.9 2.0 %last_third.1 = (f32[576,256]{1,0:T(8,128)S(1)}, bf16[576,256]{1,0:T(8,128)(2,1)S(1)}, bf16[2,2,2,2,208,128]{5,4,3,2,1,0:T(8,128)(2,1)S(1)}, bf16[2,2,2,2,208,128]{5,4,3,2,1,0:T(8,128)(2,1)S(1)}) custom-call(bf16[6,640,256]{2,1,0:T(8,128)(2,1)S(1)} %get-tuple-element.35.all_present, bf16[4,640,256]{2,1,0:T(8,128)(2,1)S(1)} %get-tuple-element.36.all_earlier, ...), custom_call_target="tpu_custom_call" | custom-call | flops 1610612736 | bytes 4718592 | tf_op jit(solution)/shard_map/last_third/pallas_call | solution.py:347
  15.9 0.1 collective-permute-start.2
  16.0 1.9 %middle_third.1 = (f32[576,256]{1,0:T(8,128)S(1)}, bf16[2,2,2,2,192,128]{5,4,3,2,1,0:T(8,128)(2,1)S(1)}, bf16[2,2,2,2,192,128]{5,4,3,2,1,0:T(8,128)(2,1)S(1)}) custom-call(bf16[6,640,256]{2,1,0:T(8,128)(2,1)S(1)} %get-tuple-element.35.all_present, bf16[4,640,256]{2,1,0:T(8,128)(2,1)S(1)} %get-tuple-element.36.all_earlier, ...), custom_call_target="tpu_custom_call" | custom-call | flops 1610612736 | bytes 4718592 | tf_op jit(solution)/shard_map/middle_third/pallas_call | solution.py:347
  17.9 0.6 %collective-permute-start.8 = (bf16[2,2,2,2,192,128]{5,4,3,2,1,0:T(8,128)(2,1)S(1)}, bf16[2,2,2,2,192,128]{5,4,3,2,1,0:T(8,128)(2,1)S(1)}, u32[]{:S(2)}, u32[]{:S(2)}) collective-permute-start(bf16[2,2,2,2,192,128]{5,4,3,2,1,0:T(8,128)(2,1)S(1)} %get-tuple-element.51), channel_id=1, source_target_pairs={{0,1},{1,0},{2,3},{3,2},{4,5},{5,4},{6,7},{7,6},{8,9},{9,8},{10,11... | collective-permute-start | bytes 2359304 | tf_op jit(solution)/shard_map/ppermute | solution.py:484
  18.5 0.0 collective-permute-done.2.refs_1_.refs_13_
  18.5 0.1 add_chunk0_step1.1.rest_2_
  18.6 1.7 %first_third.1 = (f32[512,256]{1,0:T(8,128)S(1)}, bf16[528,512]{1,0:T(8,128)(2,1)S(1)}, bf16[2,2,2,2,192,128]{5,4,3,2,1,0:T(8,128)(2,1)S(1)}, bf16[2,2,2,2,192,128]{5,4,3,2,1,0:T(8,128)(2,1)S(1)}) custom-call(bf16[6,640,256]{2,1,0:T(8,128)(2,1)S(1)} %get-tuple-element.35.all_present, bf16[4,640,256]{2,1,0:T(8,128)(2,1)S(1)} %get-tuple-element.36.all_earlier, ...), custom_call_target="tpu_custom_call" | custom-call | flops 1610612736 | bytes 4718592 | tf_op jit(solution)/shard_map/first_third/pallas_call | solution.py:347
  20.3 0.1 collective-permute-start.3
  20.4 0.1 collective-permute-start.13
  20.5 0.0 collective-permute-done.8.refs_1_.refs_7_
  20.5 0.1 add_chunk1_step1.1
  20.6 1.6 %collective-permute-start.9 = (bf16[2,2,2,192,128]{4,3,2,1,0:T(8,128)(2,1)S(1)}, bf16[2,2,2,192,128]{4,3,2,1,0:T(8,128)(2,1)S(1)}, u32[]{:S(2)}, u32[]{:S(2)}) collective-permute-start(bf16[2,2,2,192,128]{4,3,2,1,0:T(8,128)(2,1)S(1)} %add_chunk1_step1.1), channel_id=1, source_target_pairs={{0,8},{1,9},{2,10},{3,11},{4,12},{5,13},{6,14},{7,15},{8,0},{9,1},... | collective-permute-start | bytes 1179656 | tf_op jit(solution)/shard_map/ppermute | solution.py:484
  22.2 0.4 collective-permute-done.3.refs_1_
  22.7 0.1 add_chunk2_step1.1
  22.8 2.0 %collective-permute-start.4 = (bf16[2,2,2,192,128]{4,3,2,1,0:T(8,128)(2,1)S(1)}, bf16[2,2,2,192,128]{4,3,2,1,0:T(8,128)(2,1)S(1)}, u32[]{:S(2)}, u32[]{:S(2)}) collective-permute-start(bf16[2,2,2,192,128]{4,3,2,1,0:T(8,128)(2,1)S(1)} %add_chunk2_step1.1), channel_id=1, source_target_pairs={{0,2},{1,3},{2,0},{3,1},{4,6},{5,7},{6,4},{7,5},{8,10},{9,11},{10,... | collective-permute-start | bytes 1179656 | tf_op jit(solution)/shard_map/ppermute | solution.py:484
  24.7 0.5 to_inputs.1
  25.2 1.7 %collective-permute-start.14 = (bf16[64,256]{1,0:T(8,128)(2,1)S(1)}, bf16[64,256]{1,0:T(8,128)(2,1)S(1)}, u32[]{:S(2)}, u32[]{:S(2)}) collective-permute-start(bf16[64,256]{1,0:T(8,128)(2,1)S(1)} %get-tuple-element.54), channel_id=1, source_target_pairs={{0,28},{4,0},{8,4},{12,8},{16,12},{20,16},{24,20},{28,24},{1,29},{... | collective-permute-start | bytes 98312 | tf_op jit(solution)/shard_map/ppermute | solution.py:30
  27.0 6.4 %collective-permute-done.14.refs_3_.refs_18_ = bf16[64,256]{1,0:T(8,128)(2,1)S(1)} collective-permute-done((bf16[64,256]{1,0:T(8,128)(2,1)S(1)}, bf16[64,256]{1,0:T(8,128)(2,1)S(1)}, u32[]{:S(2)}, u32[]{:S(2)}) %collective-permute-start.14) | collective-permute-done | bytes 32800 | tf_op jit(solution)/shard_map/ppermute | solution.py:30
  33.3 0.0 collective-permute-done.13.refs_2_.refs_14_
  33.3 0.1 add_chunk0_step2.1
  33.4 0.2 collective-permute-start.15
  33.7 0.0 collective-permute-done.9.refs_2_.refs_8_
  33.7 0.1 add_chunk1_step2.1
  33.7 1.8 %collective-permute-start.10 = (bf16[2,2,192,128]{3,2,1,0:T(8,128)(2,1)S(1)}, bf16[2,2,192,128]{3,2,1,0:T(8,128)(2,1)S(1)}, u32[]{:S(2)}, u32[]{:S(2)}) collective-permute-start(bf16[2,2,192,128]{3,2,1,0:T(8,128)(2,1)S(1)} %add_chunk1_step2.1), channel_id=1, source_target_pairs={{0,2},{1,3},{2,0},{3,1},{4,6},{5,7},{6,4},{7,5},{8,10},{9,11},{10,... | collective-permute-start | bytes 589832 | tf_op jit(solution)/shard_map/ppermute | solution.py:484
  35.6 0.0 collective-permute-done.4.refs_2_
  35.6 0.1 add_chunk2_step2.1
  35.7 1.2 %collective-permute-start.5 = (bf16[2,2,192,128]{3,2,1,0:T(8,128)(2,1)S(1)}, bf16[2,2,192,128]{3,2,1,0:T(8,128)(2,1)S(1)}, u32[]{:S(2)}, u32[]{:S(2)}) collective-permute-start(bf16[2,2,192,128]{3,2,1,0:T(8,128)(2,1)S(1)} %add_chunk2_step2.1), channel_id=1, source_target_pairs={{0,4},{1,5},{2,6},{3,7},{4,0},{5,1},{6,2},{7,3},{8,12},{9,13},{10,... | collective-permute-start | bytes 589832 | tf_op jit(solution)/shard_map/ppermute | solution.py:484
  36.9 3.4 %collective-permute-done.15.refs_3_.refs_15_ = bf16[2,2,208,128]{3,2,1,0:T(8,128)(2,1)S(1)} collective-permute-done((bf16[2,2,208,128]{3,2,1,0:T(8,128)(2,1)S(1)}, bf16[2,2,208,128]{3,2,1,0:T(8,128)(2,1)S(1)}, u32[]{:S(2)}, u32[]{:S(2)}) %collective-permute-start.15) | collective-permute-done | bytes 213024 | tf_op jit(solution)/shard_map/ppermute | solution.py:484
  40.3 0.1 add_chunk0_step3.1
  40.4 2.0 %collective-permute-start.16 = (bf16[2,208,128]{2,1,0:T(8,128)(2,1)S(1)}, bf16[2,208,128]{2,1,0:T(8,128)(2,1)S(1)}, u32[]{:S(2)}, u32[]{:S(2)}) collective-permute-start(bf16[2,208,128]{2,1,0:T(8,128)(2,1)S(1)} %add_chunk0_step3.1), channel_id=1, source_target_pairs={{0,2},{1,3},{2,0},{3,1},{4,6},{5,7},{6,4},{7,5},{8,10},{9,11},{10,... | collective-permute-start | bytes 319496 | tf_op jit(solution)/shard_map/ppermute | solution.py:484
  42.4 0.0 collective-permute-done.10.refs_3_.refs_9_
  42.4 0.1 add_chunk1_step3.1
  42.4 0.7 %collective-permute-start.11 = (bf16[2,192,128]{2,1,0:T(8,128)(2,1)S(1)}, bf16[2,192,128]{2,1,0:T(8,128)(2,1)S(1)}, u32[]{:S(2)}, u32[]{:S(2)}) collective-permute-start(bf16[2,192,128]{2,1,0:T(8,128)(2,1)S(1)} %add_chunk1_step3.1), channel_id=1, source_target_pairs={{0,4},{1,5},{2,6},{3,7},{4,0},{5,1},{6,2},{7,3},{8,12},{9,13},{10,... | collective-permute-start | bytes 294920 | tf_op jit(solution)/shard_map/ppermute | solution.py:484
  43.1 0.0 collective-permute-done.5.refs_3_
  43.1 0.1 add_chunk2_step3.1
  43.2 0.6 %collective-permute-start.6 = (bf16[2,192,128]{2,1,0:T(8,128)(2,1)S(1)}, bf16[2,192,128]{2,1,0:T(8,128)(2,1)S(1)}, u32[]{:S(2)}, u32[]{:S(2)}) collective-permute-start(bf16[2,192,128]{2,1,0:T(8,128)(2,1)S(1)} %add_chunk2_step3.1), channel_id=1, source_target_pairs={{0,8},{1,9},{2,10},{3,11},{4,12},{5,13},{6,14},{7,15},{8,0},{9,1},... | collective-permute-start | bytes 294920 | tf_op jit(solution)/shard_map/ppermute | solution.py:484
  43.8 1.3 %collective-permute-done.16.refs_4_.refs_16_ = bf16[2,208,128]{2,1,0:T(8,128)(2,1)S(1)} collective-permute-done((bf16[2,208,128]{2,1,0:T(8,128)(2,1)S(1)}, bf16[2,208,128]{2,1,0:T(8,128)(2,1)S(1)}, u32[]{:S(2)}, u32[]{:S(2)}) %collective-permute-start.16) | collective-permute-done | bytes 106528 | tf_op jit(solution)/shard_map/ppermute | solution.py:484
  45.2 0.1 add_chunk0_step4.1
  45.2 1.2 %collective-permute-start.17 = (bf16[208,128]{1,0:T(8,128)(2,1)S(1)}, bf16[208,128]{1,0:T(8,128)(2,1)S(1)}, u32[]{:S(2)}, u32[]{:S(2)}) collective-permute-start(bf16[208,128]{1,0:T(8,128)(2,1)S(1)} %add_chunk0_step4.1), channel_id=1, source_target_pairs={{0,16},{1,17},{2,18},{3,19},{4,20},{5,21},{6,22},{7,23},{8,24},{9,... | collective-permute-start | bytes 159752 | tf_op jit(solution)/shard_map/ppermute | solution.py:484
  46.5 0.6 %collective-permute-done.11.refs_4_.refs_10_ = bf16[2,192,128]{2,1,0:T(8,128)(2,1)S(1)} collective-permute-done((bf16[2,192,128]{2,1,0:T(8,128)(2,1)S(1)}, bf16[2,192,128]{2,1,0:T(8,128)(2,1)S(1)}, u32[]{:S(2)}, u32[]{:S(2)}) %collective-permute-start.11) | collective-permute-done | bytes 98336 | tf_op jit(solution)/shard_map/ppermute | solution.py:484
  47.1 1.2 %collective-permute-start.12 = (bf16[192,128]{1,0:T(8,128)(2,1)S(1)}, bf16[192,128]{1,0:T(8,128)(2,1)S(1)}, u32[]{:S(2)}, u32[]{:S(2)}) collective-permute-start(bf16[192,128]{1,0:T(8,128)(2,1)S(1)} %add_chunk1_step4.1), channel_id=1, source_target_pairs={{0,16},{1,17},{2,18},{3,19},{4,20},{5,21},{6,22},{7,23},{8,24},{9,... | collective-permute-start | bytes 147464 | tf_op jit(solution)/shard_map/ppermute | solution.py:484
  48.3 0.0 collective-permute-done.6.refs_4_
  48.4 1.9 %collective-permute-start.7 = (bf16[192,128]{1,0:T(8,128)(2,1)S(1)}, bf16[192,128]{1,0:T(8,128)(2,1)S(1)}, u32[]{:S(2)}, u32[]{:S(2)}) collective-permute-start(bf16[192,128]{1,0:T(8,128)(2,1)S(1)} %add_chunk2_step4.1), channel_id=1, source_target_pairs={{0,16},{1,17},{2,18},{3,19},{4,20},{5,21},{6,22},{7,23},{8,24},{9,... | collective-permute-start | bytes 147464 | tf_op jit(solution)/shard_map/ppermute | solution.py:484
  50.2 2.5 %collective-permute-done.12.refs_11_ = bf16[192,128]{1,0:T(8,128)(2,1)S(1)} collective-permute-done((bf16[192,128]{1,0:T(8,128)(2,1)S(1)}, bf16[192,128]{1,0:T(8,128)(2,1)S(1)}, u32[]{:S(2)}, u32[]{:S(2)}) %collective-permute-start.12) | collective-permute-done | bytes 49184 | tf_op jit(solution)/shard_map/ppermute | solution.py:484
  52.7 0.0 collective-permute-done.17.refs_17_
  52.7 0.7 %collective-permute-done.7.refs_5_ = bf16[192,128]{1,0:T(8,128)(2,1)S(1)} collective-permute-done((bf16[192,128]{1,0:T(8,128)(2,1)S(1)}, bf16[192,128]{1,0:T(8,128)(2,1)S(1)}, u32[]{:S(2)}, u32[]{:S(2)}) %collective-permute-start.7) | collective-permute-done | bytes 49184 | tf_op jit(solution)/shard_map/ppermute | solution.py:484
  53.4 1.0 %scale_all.1 = (f32[512,256]{1,0:T(8,128)}, f32[6,64,128]{2,1,0:T(8,128)}, f32[6,32,128]{2,1,0:T(8,128)}) custom-call(bf16[2,2,2,2,192,128]{5,4,3,2,1,0:T(8,128)(2,1)S(1)} %get-tuple-element.48.refs_0_, bf16[2,2,2,2,192,128]{5,4,3,2,1,0:T(8,128)(2,1)S(1)} %collective-permute-done.3.refs_1_, bf16[2,2,2,192,128]{4,3,2,1,0:T(8,128)(2,1)S(1)} %collective-permute-done.4.refs_2_, ...), custom_call_target="tpu_custom_call" | custom-call | tf_op jit(solution)/shard_map/scale_all/pallas_call | solution.py:520
  (2 shorter events, 0.1 us)
Async XLA Ops:
  1.6 8.7 %collective-permute-start = (bf16[128,256]{1,0:T(8,128)(2,1)S(1)}, bf16[128,256]{1,0:T(8,128)(2,1)S(1)}, u32[]{:S(2)}, u32[]{:S(2)}) collective-permute-start(bf16[128,256]{1,0:T(8,128)(2,1)S(1)} %get-tuple-element.31._), channel_id=1, source_target_pairs={{0,4},{4,8},{8,12},{12,16},{16,20},{20,24},{24,28},{28,0},{1,5},{5... | collective-permute-start | bytes 196616 | tf_op jit(solution)/shard_map/ppermute | solution.py:30
  4.6 9.3 %collective-permute-start.1 = (bf16[128,256]{1,0:T(8,128)(2,1)S(1)}, bf16[128,256]{1,0:T(8,128)(2,1)S(1)}, u32[]{:S(2)}, u32[]{:S(2)}) collective-permute-start(bf16[128,256]{1,0:T(8,128)(2,1)S(1)} %get-tuple-element.39), channel_id=1, source_target_pairs={{0,4},{4,8},{8,12},{12,16},{16,20},{20,24},{24,28},{28,0},{1,5},{5... | collective-permute-start | bytes 196616 | tf_op jit(solution)/shard_map/ppermute | solution.py:30
  15.9 2.5 %collective-permute-start.2 = (bf16[2,2,2,2,208,128]{5,4,3,2,1,0:T(8,128)(2,1)S(1)}, bf16[2,2,2,2,208,128]{5,4,3,2,1,0:T(8,128)(2,1)S(1)}, u32[]{:S(2)}, u32[]{:S(2)}) collective-permute-start(bf16[2,2,2,2,208,128]{5,4,3,2,1,0:T(8,128)(2,1)S(1)} %get-tuple-element.47), channel_id=1, source_target_pairs={{0,1},{1,0},{2,3},{3,2},{4,5},{5,4},{6,7},{7,6},{8,9},{9,8},{10,11... | collective-permute-start | bytes 2555912 | tf_op jit(solution)/shard_map/ppermute | solution.py:484
  17.9 2.6 %collective-permute-start.8 = (bf16[2,2,2,2,192,128]{5,4,3,2,1,0:T(8,128)(2,1)S(1)}, bf16[2,2,2,2,192,128]{5,4,3,2,1,0:T(8,128)(2,1)S(1)}, u32[]{:S(2)}, u32[]{:S(2)}) collective-permute-start(bf16[2,2,2,2,192,128]{5,4,3,2,1,0:T(8,128)(2,1)S(1)} %get-tuple-element.51), channel_id=1, source_target_pairs={{0,1},{1,0},{2,3},{3,2},{4,5},{5,4},{6,7},{7,6},{8,9},{9,8},{10,11... | collective-permute-start | bytes 2359304 | tf_op jit(solution)/shard_map/ppermute | solution.py:484
  20.3 2.4 %collective-permute-start.3 = (bf16[2,2,2,2,192,128]{5,4,3,2,1,0:T(8,128)(2,1)S(1)}, bf16[2,2,2,2,192,128]{5,4,3,2,1,0:T(8,128)(2,1)S(1)}, u32[]{:S(2)}, u32[]{:S(2)}) collective-permute-start(bf16[2,2,2,2,192,128]{5,4,3,2,1,0:T(8,128)(2,1)S(1)} %get-tuple-element.49), channel_id=1, source_target_pairs={{0,1},{1,0},{2,3},{3,2},{4,5},{5,4},{6,7},{7,6},{8,9},{9,8},{10,11... | collective-permute-start | bytes 2359304 | tf_op jit(solution)/shard_map/ppermute | solution.py:484
  20.4 12.9 %collective-permute-start.13 = (bf16[2,2,2,208,128]{4,3,2,1,0:T(8,128)(2,1)S(1)}, bf16[2,2,2,208,128]{4,3,2,1,0:T(8,128)(2,1)S(1)}, u32[]{:S(2)}, u32[]{:S(2)}) collective-permute-start(bf16[2,2,2,208,128]{4,3,2,1,0:T(8,128)(2,1)S(1)} %add_chunk0_step1.1.rest_2_), channel_id=1, source_target_pairs={{0,4},{1,5},{2,6},{3,7},{4,0},{5,1},{6,2},{7,3},{8,12},{9,13},{10,... | collective-permute-start | bytes 1277960 | tf_op jit(solution)/shard_map/ppermute | solution.py:484
  20.6 13.1 %collective-permute-start.9 = (bf16[2,2,2,192,128]{4,3,2,1,0:T(8,128)(2,1)S(1)}, bf16[2,2,2,192,128]{4,3,2,1,0:T(8,128)(2,1)S(1)}, u32[]{:S(2)}, u32[]{:S(2)}) collective-permute-start(bf16[2,2,2,192,128]{4,3,2,1,0:T(8,128)(2,1)S(1)} %add_chunk1_step1.1), channel_id=1, source_target_pairs={{0,8},{1,9},{2,10},{3,11},{4,12},{5,13},{6,14},{7,15},{8,0},{9,1},... | collective-permute-start | bytes 1179656 | tf_op jit(solution)/shard_map/ppermute | solution.py:484
  22.8 12.8 %collective-permute-start.4 = (bf16[2,2,2,192,128]{4,3,2,1,0:T(8,128)(2,1)S(1)}, bf16[2,2,2,192,128]{4,3,2,1,0:T(8,128)(2,1)S(1)}, u32[]{:S(2)}, u32[]{:S(2)}) collective-permute-start(bf16[2,2,2,192,128]{4,3,2,1,0:T(8,128)(2,1)S(1)} %add_chunk2_step1.1), channel_id=1, source_target_pairs={{0,2},{1,3},{2,0},{3,1},{4,6},{5,7},{6,4},{7,5},{8,10},{9,11},{10,... | collective-permute-start | bytes 1179656 | tf_op jit(solution)/shard_map/ppermute | solution.py:484
  25.2 8.1 %collective-permute-start.14 = (bf16[64,256]{1,0:T(8,128)(2,1)S(1)}, bf16[64,256]{1,0:T(8,128)(2,1)S(1)}, u32[]{:S(2)}, u32[]{:S(2)}) collective-permute-start(bf16[64,256]{1,0:T(8,128)(2,1)S(1)} %get-tuple-element.54), channel_id=1, source_target_pairs={{0,28},{4,0},{8,4},{12,8},{16,12},{20,16},{24,20},{28,24},{1,29},{... | collective-permute-start | bytes 98312 | tf_op jit(solution)/shard_map/ppermute | solution.py:30
  33.4 6.9 %collective-permute-start.15 = (bf16[2,2,208,128]{3,2,1,0:T(8,128)(2,1)S(1)}, bf16[2,2,208,128]{3,2,1,0:T(8,128)(2,1)S(1)}, u32[]{:S(2)}, u32[]{:S(2)}) collective-permute-start(bf16[2,2,208,128]{3,2,1,0:T(8,128)(2,1)S(1)} %add_chunk0_step2.1), channel_id=1, source_target_pairs={{0,8},{1,9},{2,10},{3,11},{4,12},{5,13},{6,14},{7,15},{8,0},{9,1},... | collective-permute-start | bytes 638984 | tf_op jit(solution)/shard_map/ppermute | solution.py:484
  33.7 8.6 %collective-permute-start.10 = (bf16[2,2,192,128]{3,2,1,0:T(8,128)(2,1)S(1)}, bf16[2,2,192,128]{3,2,1,0:T(8,128)(2,1)S(1)}, u32[]{:S(2)}, u32[]{:S(2)}) collective-permute-start(bf16[2,2,192,128]{3,2,1,0:T(8,128)(2,1)S(1)} %add_chunk1_step2.1), channel_id=1, source_target_pairs={{0,2},{1,3},{2,0},{3,1},{4,6},{5,7},{6,4},{7,5},{8,10},{9,11},{10,... | collective-permute-start | bytes 589832 | tf_op jit(solution)/shard_map/ppermute | solution.py:484
  35.7 7.4 %collective-permute-start.5 = (bf16[2,2,192,128]{3,2,1,0:T(8,128)(2,1)S(1)}, bf16[2,2,192,128]{3,2,1,0:T(8,128)(2,1)S(1)}, u32[]{:S(2)}, u32[]{:S(2)}) collective-permute-start(bf16[2,2,192,128]{3,2,1,0:T(8,128)(2,1)S(1)} %add_chunk2_step2.1), channel_id=1, source_target_pairs={{0,4},{1,5},{2,6},{3,7},{4,0},{5,1},{6,2},{7,3},{8,12},{9,13},{10,... | collective-permute-start | bytes 589832 | tf_op jit(solution)/shard_map/ppermute | solution.py:484
  40.4 4.8 %collective-permute-start.16 = (bf16[2,208,128]{2,1,0:T(8,128)(2,1)S(1)}, bf16[2,208,128]{2,1,0:T(8,128)(2,1)S(1)}, u32[]{:S(2)}, u32[]{:S(2)}) collective-permute-start(bf16[2,208,128]{2,1,0:T(8,128)(2,1)S(1)} %add_chunk0_step3.1), channel_id=1, source_target_pairs={{0,2},{1,3},{2,0},{3,1},{4,6},{5,7},{6,4},{7,5},{8,10},{9,11},{10,... | collective-permute-start | bytes 319496 | tf_op jit(solution)/shard_map/ppermute | solution.py:484
  42.4 4.7 %collective-permute-start.11 = (bf16[2,192,128]{2,1,0:T(8,128)(2,1)S(1)}, bf16[2,192,128]{2,1,0:T(8,128)(2,1)S(1)}, u32[]{:S(2)}, u32[]{:S(2)}) collective-permute-start(bf16[2,192,128]{2,1,0:T(8,128)(2,1)S(1)} %add_chunk1_step3.1), channel_id=1, source_target_pairs={{0,4},{1,5},{2,6},{3,7},{4,0},{5,1},{6,2},{7,3},{8,12},{9,13},{10,... | collective-permute-start | bytes 294920 | tf_op jit(solution)/shard_map/ppermute | solution.py:484
  43.2 5.2 %collective-permute-start.6 = (bf16[2,192,128]{2,1,0:T(8,128)(2,1)S(1)}, bf16[2,192,128]{2,1,0:T(8,128)(2,1)S(1)}, u32[]{:S(2)}, u32[]{:S(2)}) collective-permute-start(bf16[2,192,128]{2,1,0:T(8,128)(2,1)S(1)} %add_chunk2_step3.1), channel_id=1, source_target_pairs={{0,8},{1,9},{2,10},{3,11},{4,12},{5,13},{6,14},{7,15},{8,0},{9,1},... | collective-permute-start | bytes 294920 | tf_op jit(solution)/shard_map/ppermute | solution.py:484
  45.2 7.5 %collective-permute-start.17 = (bf16[208,128]{1,0:T(8,128)(2,1)S(1)}, bf16[208,128]{1,0:T(8,128)(2,1)S(1)}, u32[]{:S(2)}, u32[]{:S(2)}) collective-permute-start(bf16[208,128]{1,0:T(8,128)(2,1)S(1)} %add_chunk0_step4.1), channel_id=1, source_target_pairs={{0,16},{1,17},{2,18},{3,19},{4,20},{5,21},{6,22},{7,23},{8,24},{9,... | collective-permute-start | bytes 159752 | tf_op jit(solution)/shard_map/ppermute | solution.py:484
  47.1 5.6 %collective-permute-start.12 = (bf16[192,128]{1,0:T(8,128)(2,1)S(1)}, bf16[192,128]{1,0:T(8,128)(2,1)S(1)}, u32[]{:S(2)}, u32[]{:S(2)}) collective-permute-start(bf16[192,128]{1,0:T(8,128)(2,1)S(1)} %add_chunk1_step4.1), channel_id=1, source_target_pairs={{0,16},{1,17},{2,18},{3,19},{4,20},{5,21},{6,22},{7,23},{8,24},{9,... | collective-permute-start | bytes 147464 | tf_op jit(solution)/shard_map/ppermute | solution.py:484
  48.4 5.1 %collective-permute-start.7 = (bf16[192,128]{1,0:T(8,128)(2,1)S(1)}, bf16[192,128]{1,0:T(8,128)(2,1)S(1)}, u32[]{:S(2)}, u32[]{:S(2)}) collective-permute-start(bf16[192,128]{1,0:T(8,128)(2,1)S(1)} %add_chunk2_step4.1), channel_id=1, source_target_pairs={{0,16},{1,17},{2,18},{3,19},{4,20},{5,21},{6,22},{7,23},{8,24},{9,... | collective-permute-start | bytes 147464 | tf_op jit(solution)/shard_map/ppermute | solution.py:484

commit v19 on v18

--- a/solution.py
+++ b/solution.py
@@ -210,10 +210,12 @@
         product = filtered * opening
         gated = product.astype(jnp.bfloat16)
         all_gates[index, start:] = gated
+        if index < layers - 1:
+            projected = dot(gated, out_w[index, :, :channels], NN)
         all_factors[index, start:, :channels] = (opening - filtered * product).astype(jnp.bfloat16)
         all_factors[index, start:, channels:] = (product * (1.0 - opening)).astype(jnp.bfloat16)
         if index < layers - 1:
-            after = stream[pad + start :] + dot(gated, out_w[index, :, :channels], NN)
+            after = stream[pad + start :] + projected
             all_present[index + 1, start:] = after.astype(jnp.bfloat16)
             if index < layers - 2:
                 stream[pad + start :] = after

time: 54.6 us -> 54.6 us (level)
  no operation moved by 1% of the time
where the time goes in v19:
time: 54.6 us; the launch traced here: 54.4 us
  starting transfers between devices  21.6 us (40%)
  waiting for transfers between devices  16.9 us (31%)
  Pallas kernels  15.2 us (28%)
  between operations  0.75 us (1%)
    ppermute x15, starting transfers between devices, swapped(): return lax.ppermute(value, ('tm', 'dp'), pairs)  15.3 us
    ppermute x15, waiting for transfers between devices, swapped(): return lax.ppermute(value, ('tm', 'dp'), pairs)  9.07 us
    ppermute x3, waiting for transfers between devices, around(): return lax.ppermute(x, axis, [(i, (i + by) % count) for i in range(count)])  7.87 us
    ppermute x3, starting transfers between devices, around(): return lax.ppermute(x, axis, [(i, (i + by) % count) for i in range(count)])  6.27 us
    pallas_call x3, Pallas kernels, backward_of(): pl.pallas_call(functools.partial(backward_kernel, plans[step] | more, lay...  5.62 us
    pallas_call x1, Pallas kernels, run_layers(): pl.pallas_call(functools.partial(forward_kernel, plan), in_specs=[vmem] *...  3.6 us
    pallas_call x1, Pallas kernels, load_all(): pl.pallas_call(load_kernel, in_specs=[anywhere] * 7, out_specs=[vmem] * 6...  2.67 us
  transfers between devices with their start and end apart: 18, of which 8 were waited for; matrix products, arithmetic and copies ran while one was open for 0% of the time, Pallas kernels for 21%

profile of v19, /device:TPU:0, one launch (start us, length us, event | category | flops | bytes accessed | tf_op | source)
XLA Modules:
  0.0 54.4 jit_solution(13157487559986988839)
XLA Ops:
  0.6 1.0 %pack_borders.1 = (bf16[128,256]{1,0:T(8,128)(2,1)S(1)}, bf16[128,256]{1,0:T(8,128)(2,1)S(1)}) custom-call(bf16[512,256]{1,0:T(8,128)(2,1)} %bitcast.4, bf16[512,256]{1,0:T(8,128)(2,1)} %bitcast.6, bf16[512,256]{1,0:T(8,128)(2,1)} %bitcast.8, f32[1,512]{1,0:T(1,128)} %weight.3), custom_call_target="tpu_custom_call" | custom-call | tf_op jit(solution)/shard_map/pack_borders/pallas_call | solution.py:57
  1.6 3.0 %collective-permute-start = (bf16[128,256]{1,0:T(8,128)(2,1)S(1)}, bf16[128,256]{1,0:T(8,128)(2,1)S(1)}, u32[]{:S(2)}, u32[]{:S(2)}) collective-permute-start(bf16[128,256]{1,0:T(8,128)(2,1)S(1)} %get-tuple-element.31._), channel_id=1, source_target_pairs={{0,4},{4,8},{8,12},{12,16},{16,20},{20,24},{24,28},{28,0},{1,5},{5... | collective-permute-start | bytes 196616 | tf_op jit(solution)/shard_map/ppermute | solution.py:30
  4.6 1.5 %collective-permute-start.1 = (bf16[128,256]{1,0:T(8,128)(2,1)S(1)}, bf16[128,256]{1,0:T(8,128)(2,1)S(1)}, u32[]{:S(2)}, u32[]{:S(2)}) collective-permute-start(bf16[128,256]{1,0:T(8,128)(2,1)S(1)} %get-tuple-element.39), channel_id=1, source_target_pairs={{0,4},{4,8},{8,12},{12,16},{16,20},{20,24},{24,28},{28,0},{1,5},{5... | collective-permute-start | bytes 196616 | tf_op jit(solution)/shard_map/ppermute | solution.py:30
  6.1 2.7 %load_all.1 = (bf16[512,256]{1,0:T(8,128)(2,1)S(1)}, f32[512,256]{1,0:T(8,128)S(1)}, bf16[512,256]{1,0:T(8,128)(2,1)S(1)}, bf16[16,128]{1,0:T(8,128)(2,1)S(1)}, ...) custom-call(bf16[512,256]{1,0:T(8,128)(2,1)} %bitcast.5, bf16[512,256]{1,0:T(8,128)(2,1)} %bitcast.7, ...), custom_call_target="tpu_custom_call" | custom-call | flops 10000000 | bytes 6000000 | tf_op jit(solution)/shard_map/load_all/pallas_call | solution.py:92
  8.8 1.5 %collective-permute-done.prev_x = bf16[128,256]{1,0:T(8,128)(2,1)S(1)} collective-permute-done((bf16[128,256]{1,0:T(8,128)(2,1)S(1)}, bf16[128,256]{1,0:T(8,128)(2,1)S(1)}, u32[]{:S(2)}, u32[]{:S(2)}) %collective-permute-start) | collective-permute-done | bytes 65568 | tf_op jit(solution)/shard_map/ppermute | solution.py:30
  10.3 3.6 %forward.1 = (bf16[6,640,256]{2,1,0:T(8,128)(2,1)S(1)}, bf16[4,640,256]{2,1,0:T(8,128)(2,1)S(1)}, bf16[6,640,512]{2,1,0:T(8,128)(2,1)S(1)}, bf16[6,640,256]{2,1,0:T(8,128)(2,1)S(1)}) custom-call(bf16[128,256]{1,0:T(8,128)(2,1)S(1)} %collective-permute-done.prev_x, bf16[512,256]{1,0:T(8,128)(2,1)S(1)} %get-tuple-element.32.own_x, ...), custom_call_target="tpu_custom_call" | custom-call | flops 2013265920 | bytes 4718592 | tf_op jit(solution)/shard_map/forward/pallas_call | solution.py:331
  13.9 0.0 collective-permute-done.1.rest_0_
  13.9 2.0 %last_third.1 = (f32[576,256]{1,0:T(8,128)S(1)}, bf16[576,256]{1,0:T(8,128)(2,1)S(1)}, bf16[2,2,2,2,208,128]{5,4,3,2,1,0:T(8,128)(2,1)S(1)}, bf16[2,2,2,2,208,128]{5,4,3,2,1,0:T(8,128)(2,1)S(1)}) custom-call(bf16[6,640,256]{2,1,0:T(8,128)(2,1)S(1)} %get-tuple-element.35.all_present, bf16[4,640,256]{2,1,0:T(8,128)(2,1)S(1)} %get-tuple-element.36.all_earlier, ...), custom_call_target="tpu_custom_call" | custom-call | flops 1610612736 | bytes 4718592 | tf_op jit(solution)/shard_map/last_third/pallas_call | solution.py:349
  15.9 0.1 collective-permute-start.2
  16.0 1.9 %middle_third.1 = (f32[576,256]{1,0:T(8,128)S(1)}, bf16[2,2,2,2,192,128]{5,4,3,2,1,0:T(8,128)(2,1)S(1)}, bf16[2,2,2,2,192,128]{5,4,3,2,1,0:T(8,128)(2,1)S(1)}) custom-call(bf16[6,640,256]{2,1,0:T(8,128)(2,1)S(1)} %get-tuple-element.35.all_present, bf16[4,640,256]{2,1,0:T(8,128)(2,1)S(1)} %get-tuple-element.36.all_earlier, ...), custom_call_target="tpu_custom_call" | custom-call | flops 1610612736 | bytes 4718592 | tf_op jit(solution)/shard_map/middle_third/pallas_call | solution.py:349
  17.9 0.6 %collective-permute-start.8 = (bf16[2,2,2,2,192,128]{5,4,3,2,1,0:T(8,128)(2,1)S(1)}, bf16[2,2,2,2,192,128]{5,4,3,2,1,0:T(8,128)(2,1)S(1)}, u32[]{:S(2)}, u32[]{:S(2)}) collective-permute-start(bf16[2,2,2,2,192,128]{5,4,3,2,1,0:T(8,128)(2,1)S(1)} %get-tuple-element.51), channel_id=1, source_target_pairs={{0,1},{1,0},{2,3},{3,2},{4,5},{5,4},{6,7},{7,6},{8,9},{9,8},{10,11... | collective-permute-start | bytes 2359304 | tf_op jit(solution)/shard_map/ppermute | solution.py:486
  18.5 0.0 collective-permute-done.2.refs_1_.refs_13_
  18.5 0.1 add_chunk0_step1.1.rest_2_
  18.6 1.7 %first_third.1 = (f32[512,256]{1,0:T(8,128)S(1)}, bf16[528,512]{1,0:T(8,128)(2,1)S(1)}, bf16[2,2,2,2,192,128]{5,4,3,2,1,0:T(8,128)(2,1)S(1)}, bf16[2,2,2,2,192,128]{5,4,3,2,1,0:T(8,128)(2,1)S(1)}) custom-call(bf16[6,640,256]{2,1,0:T(8,128)(2,1)S(1)} %get-tuple-element.35.all_present, bf16[4,640,256]{2,1,0:T(8,128)(2,1)S(1)} %get-tuple-element.36.all_earlier, ...), custom_call_target="tpu_custom_call" | custom-call | flops 1610612736 | bytes 4718592 | tf_op jit(solution)/shard_map/first_third/pallas_call | solution.py:349
  20.3 0.1 collective-permute-start.3
  20.4 0.0 collective-permute-start.13
  20.5 0.0 collective-permute-done.8.refs_1_.refs_7_
  20.5 0.1 add_chunk1_step1.1
  20.6 1.6 %collective-permute-start.9 = (bf16[2,2,2,192,128]{4,3,2,1,0:T(8,128)(2,1)S(1)}, bf16[2,2,2,192,128]{4,3,2,1,0:T(8,128)(2,1)S(1)}, u32[]{:S(2)}, u32[]{:S(2)}) collective-permute-start(bf16[2,2,2,192,128]{4,3,2,1,0:T(8,128)(2,1)S(1)} %add_chunk1_step1.1), channel_id=1, source_target_pairs={{0,8},{1,9},{2,10},{3,11},{4,12},{5,13},{6,14},{7,15},{8,0},{9,1},... | collective-permute-start | bytes 1179656 | tf_op jit(solution)/shard_map/ppermute | solution.py:486
  22.2 0.4 collective-permute-done.3.refs_1_
  22.7 0.1 add_chunk2_step1.1
  22.8 2.0 %collective-permute-start.4 = (bf16[2,2,2,192,128]{4,3,2,1,0:T(8,128)(2,1)S(1)}, bf16[2,2,2,192,128]{4,3,2,1,0:T(8,128)(2,1)S(1)}, u32[]{:S(2)}, u32[]{:S(2)}) collective-permute-start(bf16[2,2,2,192,128]{4,3,2,1,0:T(8,128)(2,1)S(1)} %add_chunk2_step1.1), channel_id=1, source_target_pairs={{0,2},{1,3},{2,0},{3,1},{4,6},{5,7},{6,4},{7,5},{8,10},{9,11},{10,... | collective-permute-start | bytes 1179656 | tf_op jit(solution)/shard_map/ppermute | solution.py:486
  24.7 0.5 to_inputs.1
  25.2 1.7 %collective-permute-start.14 = (bf16[64,256]{1,0:T(8,128)(2,1)S(1)}, bf16[64,256]{1,0:T(8,128)(2,1)S(1)}, u32[]{:S(2)}, u32[]{:S(2)}) collective-permute-start(bf16[64,256]{1,0:T(8,128)(2,1)S(1)} %get-tuple-element.54), channel_id=1, source_target_pairs={{0,28},{4,0},{8,4},{12,8},{16,12},{20,16},{24,20},{28,24},{1,29},{... | collective-permute-start | bytes 98312 | tf_op jit(solution)/shard_map/ppermute | solution.py:30
  27.0 6.4 %collective-permute-done.14.refs_3_.refs_18_ = bf16[64,256]{1,0:T(8,128)(2,1)S(1)} collective-permute-done((bf16[64,256]{1,0:T(8,128)(2,1)S(1)}, bf16[64,256]{1,0:T(8,128)(2,1)S(1)}, u32[]{:S(2)}, u32[]{:S(2)}) %collective-permute-start.14) | collective-permute-done | bytes 32800 | tf_op jit(solution)/shard_map/ppermute | solution.py:30
  33.3 0.0 collective-permute-done.13.refs_2_.refs_14_
  33.3 0.1 add_chunk0_step2.1
  33.4 0.2 collective-permute-start.15
  33.7 0.0 collective-permute-done.9.refs_2_.refs_8_
  33.7 0.1 add_chunk1_step2.1
  33.7 1.8 %collective-permute-start.10 = (bf16[2,2,192,128]{3,2,1,0:T(8,128)(2,1)S(1)}, bf16[2,2,192,128]{3,2,1,0:T(8,128)(2,1)S(1)}, u32[]{:S(2)}, u32[]{:S(2)}) collective-permute-start(bf16[2,2,192,128]{3,2,1,0:T(8,128)(2,1)S(1)} %add_chunk1_step2.1), channel_id=1, source_target_pairs={{0,2},{1,3},{2,0},{3,1},{4,6},{5,7},{6,4},{7,5},{8,10},{9,11},{10,... | collective-permute-start | bytes 589832 | tf_op jit(solution)/shard_map/ppermute | solution.py:486
  35.6 0.0 collective-permute-done.4.refs_2_
  35.6 0.1 add_chunk2_step2.1
  35.7 1.2 %collective-permute-start.5 = (bf16[2,2,192,128]{3,2,1,0:T(8,128)(2,1)S(1)}, bf16[2,2,192,128]{3,2,1,0:T(8,128)(2,1)S(1)}, u32[]{:S(2)}, u32[]{:S(2)}) collective-permute-start(bf16[2,2,192,128]{3,2,1,0:T(8,128)(2,1)S(1)} %add_chunk2_step2.1), channel_id=1, source_target_pairs={{0,4},{1,5},{2,6},{3,7},{4,0},{5,1},{6,2},{7,3},{8,12},{9,13},{10,... | collective-permute-start | bytes 589832 | tf_op jit(solution)/shard_map/ppermute | solution.py:486
  36.9 3.4 %collective-permute-done.15.refs_3_.refs_15_ = bf16[2,2,208,128]{3,2,1,0:T(8,128)(2,1)S(1)} collective-permute-done((bf16[2,2,208,128]{3,2,1,0:T(8,128)(2,1)S(1)}, bf16[2,2,208,128]{3,2,1,0:T(8,128)(2,1)S(1)}, u32[]{:S(2)}, u32[]{:S(2)}) %collective-permute-start.15) | collective-permute-done | bytes 213024 | tf_op jit(solution)/shard_map/ppermute | solution.py:486
  40.3 0.1 add_chunk0_step3.1
  40.4 2.0 %collective-permute-start.16 = (bf16[2,208,128]{2,1,0:T(8,128)(2,1)S(1)}, bf16[2,208,128]{2,1,0:T(8,128)(2,1)S(1)}, u32[]{:S(2)}, u32[]{:S(2)}) collective-permute-start(bf16[2,208,128]{2,1,0:T(8,128)(2,1)S(1)} %add_chunk0_step3.1), channel_id=1, source_target_pairs={{0,2},{1,3},{2,0},{3,1},{4,6},{5,7},{6,4},{7,5},{8,10},{9,11},{10,... | collective-permute-start | bytes 319496 | tf_op jit(solution)/shard_map/ppermute | solution.py:486
  42.4 0.0 collective-permute-done.10.refs_3_.refs_9_
  42.4 0.1 add_chunk1_step3.1
  42.4 0.7 %collective-permute-start.11 = (bf16[2,192,128]{2,1,0:T(8,128)(2,1)S(1)}, bf16[2,192,128]{2,1,0:T(8,128)(2,1)S(1)}, u32[]{:S(2)}, u32[]{:S(2)}) collective-permute-start(bf16[2,192,128]{2,1,0:T(8,128)(2,1)S(1)} %add_chunk1_step3.1), channel_id=1, source_target_pairs={{0,4},{1,5},{2,6},{3,7},{4,0},{5,1},{6,2},{7,3},{8,12},{9,13},{10,... | collective-permute-start | bytes 294920 | tf_op jit(solution)/shard_map/ppermute | solution.py:486
  43.1 0.0 collective-permute-done.5.refs_3_
  43.1 0.1 add_chunk2_step3.1
  43.2 0.6 %collective-permute-start.6 = (bf16[2,192,128]{2,1,0:T(8,128)(2,1)S(1)}, bf16[2,192,128]{2,1,0:T(8,128)(2,1)S(1)}, u32[]{:S(2)}, u32[]{:S(2)}) collective-permute-start(bf16[2,192,128]{2,1,0:T(8,128)(2,1)S(1)} %add_chunk2_step3.1), channel_id=1, source_target_pairs={{0,8},{1,9},{2,10},{3,11},{4,12},{5,13},{6,14},{7,15},{8,0},{9,1},... | collective-permute-start | bytes 294920 | tf_op jit(solution)/shard_map/ppermute | solution.py:486
  43.8 1.3 %collective-permute-done.16.refs_4_.refs_16_ = bf16[2,208,128]{2,1,0:T(8,128)(2,1)S(1)} collective-permute-done((bf16[2,208,128]{2,1,0:T(8,128)(2,1)S(1)}, bf16[2,208,128]{2,1,0:T(8,128)(2,1)S(1)}, u32[]{:S(2)}, u32[]{:S(2)}) %collective-permute-start.16) | collective-permute-done | bytes 106528 | tf_op jit(solution)/shard_map/ppermute | solution.py:486
  45.2 0.1 add_chunk0_step4.1
  45.2 1.2 %collective-permute-start.17 = (bf16[208,128]{1,0:T(8,128)(2,1)S(1)}, bf16[208,128]{1,0:T(8,128)(2,1)S(1)}, u32[]{:S(2)}, u32[]{:S(2)}) collective-permute-start(bf16[208,128]{1,0:T(8,128)(2,1)S(1)} %add_chunk0_step4.1), channel_id=1, source_target_pairs={{0,16},{1,17},{2,18},{3,19},{4,20},{5,21},{6,22},{7,23},{8,24},{9,... | collective-permute-start | bytes 159752 | tf_op jit(solution)/shard_map/ppermute | solution.py:486
  46.5 0.6 %collective-permute-done.11.refs_4_.refs_10_ = bf16[2,192,128]{2,1,0:T(8,128)(2,1)S(1)} collective-permute-done((bf16[2,192,128]{2,1,0:T(8,128)(2,1)S(1)}, bf16[2,192,128]{2,1,0:T(8,128)(2,1)S(1)}, u32[]{:S(2)}, u32[]{:S(2)}) %collective-permute-start.11) | collective-permute-done | bytes 98336 | tf_op jit(solution)/shard_map/ppermute | solution.py:486
  47.1 1.2 %collective-permute-start.12 = (bf16[192,128]{1,0:T(8,128)(2,1)S(1)}, bf16[192,128]{1,0:T(8,128)(2,1)S(1)}, u32[]{:S(2)}, u32[]{:S(2)}) collective-permute-start(bf16[192,128]{1,0:T(8,128)(2,1)S(1)} %add_chunk1_step4.1), channel_id=1, source_target_pairs={{0,16},{1,17},{2,18},{3,19},{4,20},{5,21},{6,22},{7,23},{8,24},{9,... | collective-permute-start | bytes 147464 | tf_op jit(solution)/shard_map/ppermute | solution.py:486
  48.3 0.0 collective-permute-done.6.refs_4_
  48.4 1.9 %collective-permute-start.7 = (bf16[192,128]{1,0:T(8,128)(2,1)S(1)}, bf16[192,128]{1,0:T(8,128)(2,1)S(1)}, u32[]{:S(2)}, u32[]{:S(2)}) collective-permute-start(bf16[192,128]{1,0:T(8,128)(2,1)S(1)} %add_chunk2_step4.1), channel_id=1, source_target_pairs={{0,16},{1,17},{2,18},{3,19},{4,20},{5,21},{6,22},{7,23},{8,24},{9,... | collective-permute-start | bytes 147464 | tf_op jit(solution)/shard_map/ppermute | solution.py:486
  50.2 2.5 %collective-permute-done.12.refs_11_ = bf16[192,128]{1,0:T(8,128)(2,1)S(1)} collective-permute-done((bf16[192,128]{1,0:T(8,128)(2,1)S(1)}, bf16[192,128]{1,0:T(8,128)(2,1)S(1)}, u32[]{:S(2)}, u32[]{:S(2)}) %collective-permute-start.12) | collective-permute-done | bytes 49184 | tf_op jit(solution)/shard_map/ppermute | solution.py:486
  52.7 0.0 collective-permute-done.17.refs_17_
  52.7 0.7 %collective-permute-done.7.refs_5_ = bf16[192,128]{1,0:T(8,128)(2,1)S(1)} collective-permute-done((bf16[192,128]{1,0:T(8,128)(2,1)S(1)}, bf16[192,128]{1,0:T(8,128)(2,1)S(1)}, u32[]{:S(2)}, u32[]{:S(2)}) %collective-permute-start.7) | collective-permute-done | bytes 49184 | tf_op jit(solution)/shard_map/ppermute | solution.py:486
  53.4 1.0 %scale_all.1 = (f32[512,256]{1,0:T(8,128)}, f32[6,64,128]{2,1,0:T(8,128)}, f32[6,32,128]{2,1,0:T(8,128)}) custom-call(bf16[2,2,2,2,192,128]{5,4,3,2,1,0:T(8,128)(2,1)S(1)} %get-tuple-element.48.refs_0_, bf16[2,2,2,2,192,128]{5,4,3,2,1,0:T(8,128)(2,1)S(1)} %collective-permute-done.3.refs_1_, bf16[2,2,2,192,128]{4,3,2,1,0:T(8,128)(2,1)S(1)} %collective-permute-done.4.refs_2_, ...), custom_call_target="tpu_custom_call" | custom-call | tf_op jit(solution)/shard_map/scale_all/pallas_call | solution.py:522
  (2 shorter events, 0.1 us)
Async XLA Ops:
  1.6 8.7 %collective-permute-start = (bf16[128,256]{1,0:T(8,128)(2,1)S(1)}, bf16[128,256]{1,0:T(8,128)(2,1)S(1)}, u32[]{:S(2)}, u32[]{:S(2)}) collective-permute-start(bf16[128,256]{1,0:T(8,128)(2,1)S(1)} %get-tuple-element.31._), channel_id=1, source_target_pairs={{0,4},{4,8},{8,12},{12,16},{16,20},{20,24},{24,28},{28,0},{1,5},{5... | collective-permute-start | bytes 196616 | tf_op jit(solution)/shard_map/ppermute | solution.py:30
  4.6 9.3 %collective-permute-start.1 = (bf16[128,256]{1,0:T(8,128)(2,1)S(1)}, bf16[128,256]{1,0:T(8,128)(2,1)S(1)}, u32[]{:S(2)}, u32[]{:S(2)}) collective-permute-start(bf16[128,256]{1,0:T(8,128)(2,1)S(1)} %get-tuple-element.39), channel_id=1, source_target_pairs={{0,4},{4,8},{8,12},{12,16},{16,20},{20,24},{24,28},{28,0},{1,5},{5... | collective-permute-start | bytes 196616 | tf_op jit(solution)/shard_map/ppermute | solution.py:30
  15.9 2.5 %collective-permute-start.2 = (bf16[2,2,2,2,208,128]{5,4,3,2,1,0:T(8,128)(2,1)S(1)}, bf16[2,2,2,2,208,128]{5,4,3,2,1,0:T(8,128)(2,1)S(1)}, u32[]{:S(2)}, u32[]{:S(2)}) collective-permute-start(bf16[2,2,2,2,208,128]{5,4,3,2,1,0:T(8,128)(2,1)S(1)} %get-tuple-element.47), channel_id=1, source_target_pairs={{0,1},{1,0},{2,3},{3,2},{4,5},{5,4},{6,7},{7,6},{8,9},{9,8},{10,11... | collective-permute-start | bytes 2555912 | tf_op jit(solution)/shard_map/ppermute | solution.py:486
  17.9 2.6 %collective-permute-start.8 = (bf16[2,2,2,2,192,128]{5,4,3,2,1,0:T(8,128)(2,1)S(1)}, bf16[2,2,2,2,192,128]{5,4,3,2,1,0:T(8,128)(2,1)S(1)}, u32[]{:S(2)}, u32[]{:S(2)}) collective-permute-start(bf16[2,2,2,2,192,128]{5,4,3,2,1,0:T(8,128)(2,1)S(1)} %get-tuple-element.51), channel_id=1, source_target_pairs={{0,1},{1,0},{2,3},{3,2},{4,5},{5,4},{6,7},{7,6},{8,9},{9,8},{10,11... | collective-permute-start | bytes 2359304 | tf_op jit(solution)/shard_map/ppermute | solution.py:486
  20.3 2.4 %collective-permute-start.3 = (bf16[2,2,2,2,192,128]{5,4,3,2,1,0:T(8,128)(2,1)S(1)}, bf16[2,2,2,2,192,128]{5,4,3,2,1,0:T(8,128)(2,1)S(1)}, u32[]{:S(2)}, u32[]{:S(2)}) collective-permute-start(bf16[2,2,2,2,192,128]{5,4,3,2,1,0:T(8,128)(2,1)S(1)} %get-tuple-element.49), channel_id=1, source_target_pairs={{0,1},{1,0},{2,3},{3,2},{4,5},{5,4},{6,7},{7,6},{8,9},{9,8},{10,11... | collective-permute-start | bytes 2359304 | tf_op jit(solution)/shard_map/ppermute | solution.py:486
  20.4 12.9 %collective-permute-start.13 = (bf16[2,2,2,208,128]{4,3,2,1,0:T(8,128)(2,1)S(1)}, bf16[2,2,2,208,128]{4,3,2,1,0:T(8,128)(2,1)S(1)}, u32[]{:S(2)}, u32[]{:S(2)}) collective-permute-start(bf16[2,2,2,208,128]{4,3,2,1,0:T(8,128)(2,1)S(1)} %add_chunk0_step1.1.rest_2_), channel_id=1, source_target_pairs={{0,4},{1,5},{2,6},{3,7},{4,0},{5,1},{6,2},{7,3},{8,12},{9,13},{10,... | collective-permute-start | bytes 1277960 | tf_op jit(solution)/shard_map/ppermute | solution.py:486
  20.6 13.1 %collective-permute-start.9 = (bf16[2,2,2,192,128]{4,3,2,1,0:T(8,128)(2,1)S(1)}, bf16[2,2,2,192,128]{4,3,2,1,0:T(8,128)(2,1)S(1)}, u32[]{:S(2)}, u32[]{:S(2)}) collective-permute-start(bf16[2,2,2,192,128]{4,3,2,1,0:T(8,128)(2,1)S(1)} %add_chunk1_step1.1), channel_id=1, source_target_pairs={{0,8},{1,9},{2,10},{3,11},{4,12},{5,13},{6,14},{7,15},{8,0},{9,1},... | collective-permute-start | bytes 1179656 | tf_op jit(solution)/shard_map/ppermute | solution.py:486
  22.8 12.8 %collective-permute-start.4 = (bf16[2,2,2,192,128]{4,3,2,1,0:T(8,128)(2,1)S(1)}, bf16[2,2,2,192,128]{4,3,2,1,0:T(8,128)(2,1)S(1)}, u32[]{:S(2)}, u32[]{:S(2)}) collective-permute-start(bf16[2,2,2,192,128]{4,3,2,1,0:T(8,128)(2,1)S(1)} %add_chunk2_step1.1), channel_id=1, source_target_pairs={{0,2},{1,3},{2,0},{3,1},{4,6},{5,7},{6,4},{7,5},{8,10},{9,11},{10,... | collective-permute-start | bytes 1179656 | tf_op jit(solution)/shard_map/ppermute | solution.py:486
  25.2 8.1 %collective-permute-start.14 = (bf16[64,256]{1,0:T(8,128)(2,1)S(1)}, bf16[64,256]{1,0:T(8,128)(2,1)S(1)}, u32[]{:S(2)}, u32[]{:S(2)}) collective-permute-start(bf16[64,256]{1,0:T(8,128)(2,1)S(1)} %get-tuple-element.54), channel_id=1, source_target_pairs={{0,28},{4,0},{8,4},{12,8},{16,12},{20,16},{24,20},{28,24},{1,29},{... | collective-permute-start | bytes 98312 | tf_op jit(solution)/shard_map/ppermute | solution.py:30
  33.4 6.9 %collective-permute-start.15 = (bf16[2,2,208,128]{3,2,1,0:T(8,128)(2,1)S(1)}, bf16[2,2,208,128]{3,2,1,0:T(8,128)(2,1)S(1)}, u32[]{:S(2)}, u32[]{:S(2)}) collective-permute-start(bf16[2,2,208,128]{3,2,1,0:T(8,128)(2,1)S(1)} %add_chunk0_step2.1), channel_id=1, source_target_pairs={{0,8},{1,9},{2,10},{3,11},{4,12},{5,13},{6,14},{7,15},{8,0},{9,1},... | collective-permute-start | bytes 638984 | tf_op jit(solution)/shard_map/ppermute | solution.py:486
  33.7 8.6 %collective-permute-start.10 = (bf16[2,2,192,128]{3,2,1,0:T(8,128)(2,1)S(1)}, bf16[2,2,192,128]{3,2,1,0:T(8,128)(2,1)S(1)}, u32[]{:S(2)}, u32[]{:S(2)}) collective-permute-start(bf16[2,2,192,128]{3,2,1,0:T(8,128)(2,1)S(1)} %add_chunk1_step2.1), channel_id=1, source_target_pairs={{0,2},{1,3},{2,0},{3,1},{4,6},{5,7},{6,4},{7,5},{8,10},{9,11},{10,... | collective-permute-start | bytes 589832 | tf_op jit(solution)/shard_map/ppermute | solution.py:486
  35.7 7.4 %collective-permute-start.5 = (bf16[2,2,192,128]{3,2,1,0:T(8,128)(2,1)S(1)}, bf16[2,2,192,128]{3,2,1,0:T(8,128)(2,1)S(1)}, u32[]{:S(2)}, u32[]{:S(2)}) collective-permute-start(bf16[2,2,192,128]{3,2,1,0:T(8,128)(2,1)S(1)} %add_chunk2_step2.1), channel_id=1, source_target_pairs={{0,4},{1,5},{2,6},{3,7},{4,0},{5,1},{6,2},{7,3},{8,12},{9,13},{10,... | collective-permute-start | bytes 589832 | tf_op jit(solution)/shard_map/ppermute | solution.py:486
  40.4 4.8 %collective-permute-start.16 = (bf16[2,208,128]{2,1,0:T(8,128)(2,1)S(1)}, bf16[2,208,128]{2,1,0:T(8,128)(2,1)S(1)}, u32[]{:S(2)}, u32[]{:S(2)}) collective-permute-start(bf16[2,208,128]{2,1,0:T(8,128)(2,1)S(1)} %add_chunk0_step3.1), channel_id=1, source_target_pairs={{0,2},{1,3},{2,0},{3,1},{4,6},{5,7},{6,4},{7,5},{8,10},{9,11},{10,... | collective-permute-start | bytes 319496 | tf_op jit(solution)/shard_map/ppermute | solution.py:486
  42.4 4.7 %collective-permute-start.11 = (bf16[2,192,128]{2,1,0:T(8,128)(2,1)S(1)}, bf16[2,192,128]{2,1,0:T(8,128)(2,1)S(1)}, u32[]{:S(2)}, u32[]{:S(2)}) collective-permute-start(bf16[2,192,128]{2,1,0:T(8,128)(2,1)S(1)} %add_chunk1_step3.1), channel_id=1, source_target_pairs={{0,4},{1,5},{2,6},{3,7},{4,0},{5,1},{6,2},{7,3},{8,12},{9,13},{10,... | collective-permute-start | bytes 294920 | tf_op jit(solution)/shard_map/ppermute | solution.py:486
  43.2 5.2 %collective-permute-start.6 = (bf16[2,192,128]{2,1,0:T(8,128)(2,1)S(1)}, bf16[2,192,128]{2,1,0:T(8,128)(2,1)S(1)}, u32[]{:S(2)}, u32[]{:S(2)}) collective-permute-start(bf16[2,192,128]{2,1,0:T(8,128)(2,1)S(1)} %add_chunk2_step3.1), channel_id=1, source_target_pairs={{0,8},{1,9},{2,10},{3,11},{4,12},{5,13},{6,14},{7,15},{8,0},{9,1},... | collective-permute-start | bytes 294920 | tf_op jit(solution)/shard_map/ppermute | solution.py:486
  45.2 7.5 %collective-permute-start.17 = (bf16[208,128]{1,0:T(8,128)(2,1)S(1)}, bf16[208,128]{1,0:T(8,128)(2,1)S(1)}, u32[]{:S(2)}, u32[]{:S(2)}) collective-permute-start(bf16[208,128]{1,0:T(8,128)(2,1)S(1)} %add_chunk0_step4.1), channel_id=1, source_target_pairs={{0,16},{1,17},{2,18},{3,19},{4,20},{5,21},{6,22},{7,23},{8,24},{9,... | collective-permute-start | bytes 159752 | tf_op jit(solution)/shard_map/ppermute | solution.py:486
  47.1 5.6 %collective-permute-start.12 = (bf16[192,128]{1,0:T(8,128)(2,1)S(1)}, bf16[192,128]{1,0:T(8,128)(2,1)S(1)}, u32[]{:S(2)}, u32[]{:S(2)}) collective-permute-start(bf16[192,128]{1,0:T(8,128)(2,1)S(1)} %add_chunk1_step4.1), channel_id=1, source_target_pairs={{0,16},{1,17},{2,18},{3,19},{4,20},{5,21},{6,22},{7,23},{8,24},{9,... | collective-permute-start | bytes 147464 | tf_op jit(solution)/shard_map/ppermute | solution.py:486
  48.4 5.1 %collective-permute-start.7 = (bf16[192,128]{1,0:T(8,128)(2,1)S(1)}, bf16[192,128]{1,0:T(8,128)(2,1)S(1)}, u32[]{:S(2)}, u32[]{:S(2)}) collective-permute-start(bf16[192,128]{1,0:T(8,128)(2,1)S(1)} %add_chunk2_step4.1), channel_id=1, source_target_pairs={{0,16},{1,17},{2,18},{3,19},{4,20},{5,21},{6,22},{7,23},{8,24},{9,... | collective-permute-start | bytes 147464 | tf_op jit(solution)/shard_map/ppermute | solution.py:486

commit v20 on v18

--- a/solution.py
+++ b/solution.py
@@ -175,11 +175,13 @@
             [grad_gated * both[:, :channels], grad_gated * both[:, channels:]], axis=1
         ).astype(jnp.bfloat16)
         if index:
-            moved_on(dilation, dot(grad_preact, conv_w[index], NT), past_part, grad_stream, halo, plan["counts"][index - 1])
+            spread = dot(grad_preact, conv_w[index], NT)
         else:
             last_preact[...] = grad_preact
         past = earlier_rows(plan, index, present, halo, halo + length) if earlier is None else earlier[own]
         total = dot(jnp.concatenate([present[own], past], axis=1), grad_preact[0:length], TN)
+        if index:
+            moved_on(dilation, spread, past_part, grad_stream, halo, plan["counts"][index - 1])
         plan["store"](total, items.index((index, False)), grad_parts)
 
 

time: 54.6 us -> 54.6 us (level)
  no operation moved by 1% of the time
where the time goes in v20:
time: 54.6 us; the launch traced here: 54.4 us
  starting transfers between devices  21.6 us (40%)
  waiting for transfers between devices  16.9 us (31%)
  Pallas kernels  15.2 us (28%)
  between operations  0.75 us (1%)
    ppermute x15, starting transfers between devices, swapped(): return lax.ppermute(value, ('tm', 'dp'), pairs)  15.3 us
    ppermute x15, waiting for transfers between devices, swapped(): return lax.ppermute(value, ('tm', 'dp'), pairs)  9.06 us
    ppermute x3, waiting for transfers between devices, around(): return lax.ppermute(x, axis, [(i, (i + by) % count) for i in range(count)])  7.87 us
    ppermute x3, starting transfers between devices, around(): return lax.ppermute(x, axis, [(i, (i + by) % count) for i in range(count)])  6.27 us
    pallas_call x3, Pallas kernels, backward_of(): pl.pallas_call(functools.partial(backward_kernel, plans[step] | more, lay...  5.63 us
    pallas_call x1, Pallas kernels, run_layers(): pl.pallas_call(functools.partial(forward_kernel, plan), in_specs=[vmem] *...  3.6 us
    pallas_call x1, Pallas kernels, load_all(): pl.pallas_call(load_kernel, in_specs=[anywhere] * 7, out_specs=[vmem] * 6...  2.67 us
  transfers between devices with their start and end apart: 18, of which 8 were waited for; matrix products, arithmetic and copies ran while one was open for 0% of the time, Pallas kernels for 21%

profile of v20, /device:TPU:0, one launch (start us, length us, event | category | flops | bytes accessed | tf_op | source)
XLA Modules:
  0.0 54.4 jit_solution(9499574593481199889)
XLA Ops:
  0.6 1.0 %pack_borders.1 = (bf16[128,256]{1,0:T(8,128)(2,1)S(1)}, bf16[128,256]{1,0:T(8,128)(2,1)S(1)}) custom-call(bf16[512,256]{1,0:T(8,128)(2,1)} %bitcast.4, bf16[512,256]{1,0:T(8,128)(2,1)} %bitcast.6, bf16[512,256]{1,0:T(8,128)(2,1)} %bitcast.8, f32[1,512]{1,0:T(1,128)} %weight.3), custom_call_target="tpu_custom_call" | custom-call | tf_op jit(solution)/shard_map/pack_borders/pallas_call | solution.py:57
  1.6 3.0 %collective-permute-start = (bf16[128,256]{1,0:T(8,128)(2,1)S(1)}, bf16[128,256]{1,0:T(8,128)(2,1)S(1)}, u32[]{:S(2)}, u32[]{:S(2)}) collective-permute-start(bf16[128,256]{1,0:T(8,128)(2,1)S(1)} %get-tuple-element.31._), channel_id=1, source_target_pairs={{0,4},{4,8},{8,12},{12,16},{16,20},{20,24},{24,28},{28,0},{1,5},{5... | collective-permute-start | bytes 196616 | tf_op jit(solution)/shard_map/ppermute | solution.py:30
  4.6 1.5 %collective-permute-start.1 = (bf16[128,256]{1,0:T(8,128)(2,1)S(1)}, bf16[128,256]{1,0:T(8,128)(2,1)S(1)}, u32[]{:S(2)}, u32[]{:S(2)}) collective-permute-start(bf16[128,256]{1,0:T(8,128)(2,1)S(1)} %get-tuple-element.39), channel_id=1, source_target_pairs={{0,4},{4,8},{8,12},{12,16},{16,20},{20,24},{24,28},{28,0},{1,5},{5... | collective-permute-start | bytes 196616 | tf_op jit(solution)/shard_map/ppermute | solution.py:30
  6.1 2.7 %load_all.1 = (bf16[512,256]{1,0:T(8,128)(2,1)S(1)}, f32[512,256]{1,0:T(8,128)S(1)}, bf16[512,256]{1,0:T(8,128)(2,1)S(1)}, bf16[16,128]{1,0:T(8,128)(2,1)S(1)}, ...) custom-call(bf16[512,256]{1,0:T(8,128)(2,1)} %bitcast.5, bf16[512,256]{1,0:T(8,128)(2,1)} %bitcast.7, ...), custom_call_target="tpu_custom_call" | custom-call | flops 10000000 | bytes 6000000 | tf_op jit(solution)/shard_map/load_all/pallas_call | solution.py:92
  8.8 1.5 %collective-permute-done.prev_x = bf16[128,256]{1,0:T(8,128)(2,1)S(1)} collective-permute-done((bf16[128,256]{1,0:T(8,128)(2,1)S(1)}, bf16[128,256]{1,0:T(8,128)(2,1)S(1)}, u32[]{:S(2)}, u32[]{:S(2)}) %collective-permute-start) | collective-permute-done | bytes 65568 | tf_op jit(solution)/shard_map/ppermute | solution.py:30
  10.3 3.6 %forward.1 = (bf16[6,640,256]{2,1,0:T(8,128)(2,1)S(1)}, bf16[4,640,256]{2,1,0:T(8,128)(2,1)S(1)}, bf16[6,640,512]{2,1,0:T(8,128)(2,1)S(1)}, bf16[6,640,256]{2,1,0:T(8,128)(2,1)S(1)}) custom-call(bf16[128,256]{1,0:T(8,128)(2,1)S(1)} %collective-permute-done.prev_x, bf16[512,256]{1,0:T(8,128)(2,1)S(1)} %get-tuple-element.32.own_x, ...), custom_call_target="tpu_custom_call" | custom-call | flops 2013265920 | bytes 4718592 | tf_op jit(solution)/shard_map/forward/pallas_call | solution.py:331
  13.9 0.0 collective-permute-done.1.rest_0_
  13.9 2.0 %last_third.1 = (f32[576,256]{1,0:T(8,128)S(1)}, bf16[576,256]{1,0:T(8,128)(2,1)S(1)}, bf16[2,2,2,2,208,128]{5,4,3,2,1,0:T(8,128)(2,1)S(1)}, bf16[2,2,2,2,208,128]{5,4,3,2,1,0:T(8,128)(2,1)S(1)}) custom-call(bf16[6,640,256]{2,1,0:T(8,128)(2,1)S(1)} %get-tuple-element.35.all_present, bf16[4,640,256]{2,1,0:T(8,128)(2,1)S(1)} %get-tuple-element.36.all_earlier, ...), custom_call_target="tpu_custom_call" | custom-call | flops 1610612736 | bytes 4718592 | tf_op jit(solution)/shard_map/last_third/pallas_call | solution.py:349
  15.9 0.1 collective-permute-start.2
  16.0 1.9 %middle_third.1 = (f32[576,256]{1,0:T(8,128)S(1)}, bf16[2,2,2,2,192,128]{5,4,3,2,1,0:T(8,128)(2,1)S(1)}, bf16[2,2,2,2,192,128]{5,4,3,2,1,0:T(8,128)(2,1)S(1)}) custom-call(bf16[6,640,256]{2,1,0:T(8,128)(2,1)S(1)} %get-tuple-element.35.all_present, bf16[4,640,256]{2,1,0:T(8,128)(2,1)S(1)} %get-tuple-element.36.all_earlier, ...), custom_call_target="tpu_custom_call" | custom-call | flops 1610612736 | bytes 4718592 | tf_op jit(solution)/shard_map/middle_third/pallas_call | solution.py:349
  17.9 0.6 %collective-permute-start.8 = (bf16[2,2,2,2,192,128]{5,4,3,2,1,0:T(8,128)(2,1)S(1)}, bf16[2,2,2,2,192,128]{5,4,3,2,1,0:T(8,128)(2,1)S(1)}, u32[]{:S(2)}, u32[]{:S(2)}) collective-permute-start(bf16[2,2,2,2,192,128]{5,4,3,2,1,0:T(8,128)(2,1)S(1)} %get-tuple-element.51), channel_id=1, source_target_pairs={{0,1},{1,0},{2,3},{3,2},{4,5},{5,4},{6,7},{7,6},{8,9},{9,8},{10,11... | collective-permute-start | bytes 2359304 | tf_op jit(solution)/shard_map/ppermute | solution.py:486
  18.5 0.0 collective-permute-done.2.refs_1_.refs_13_
  18.5 0.1 add_chunk0_step1.1.rest_2_
  18.6 1.7 %first_third.1 = (f32[512,256]{1,0:T(8,128)S(1)}, bf16[528,512]{1,0:T(8,128)(2,1)S(1)}, bf16[2,2,2,2,192,128]{5,4,3,2,1,0:T(8,128)(2,1)S(1)}, bf16[2,2,2,2,192,128]{5,4,3,2,1,0:T(8,128)(2,1)S(1)}) custom-call(bf16[6,640,256]{2,1,0:T(8,128)(2,1)S(1)} %get-tuple-element.35.all_present, bf16[4,640,256]{2,1,0:T(8,128)(2,1)S(1)} %get-tuple-element.36.all_earlier, ...), custom_call_target="tpu_custom_call" | custom-call | flops 1610612736 | bytes 4718592 | tf_op jit(solution)/shard_map/first_third/pallas_call | solution.py:349
  20.3 0.1 collective-permute-start.3
  20.4 0.1 collective-permute-start.13
  20.5 0.0 collective-permute-done.8.refs_1_.refs_7_
  20.5 0.1 add_chunk1_step1.1
  20.6 1.6 %collective-permute-start.9 = (bf16[2,2,2,192,128]{4,3,2,1,0:T(8,128)(2,1)S(1)}, bf16[2,2,2,192,128]{4,3,2,1,0:T(8,128)(2,1)S(1)}, u32[]{:S(2)}, u32[]{:S(2)}) collective-permute-start(bf16[2,2,2,192,128]{4,3,2,1,0:T(8,128)(2,1)S(1)} %add_chunk1_step1.1), channel_id=1, source_target_pairs={{0,8},{1,9},{2,10},{3,11},{4,12},{5,13},{6,14},{7,15},{8,0},{9,1},... | collective-permute-start | bytes 1179656 | tf_op jit(solution)/shard_map/ppermute | solution.py:486
  22.2 0.4 collective-permute-done.3.refs_1_
  22.7 0.1 add_chunk2_step1.1
  22.8 2.0 %collective-permute-start.4 = (bf16[2,2,2,192,128]{4,3,2,1,0:T(8,128)(2,1)S(1)}, bf16[2,2,2,192,128]{4,3,2,1,0:T(8,128)(2,1)S(1)}, u32[]{:S(2)}, u32[]{:S(2)}) collective-permute-start(bf16[2,2,2,192,128]{4,3,2,1,0:T(8,128)(2,1)S(1)} %add_chunk2_step1.1), channel_id=1, source_target_pairs={{0,2},{1,3},{2,0},{3,1},{4,6},{5,7},{6,4},{7,5},{8,10},{9,11},{10,... | collective-permute-start | bytes 1179656 | tf_op jit(solution)/shard_map/ppermute | solution.py:486
  24.8 0.5 to_inputs.1
  25.2 1.7 %collective-permute-start.14 = (bf16[64,256]{1,0:T(8,128)(2,1)S(1)}, bf16[64,256]{1,0:T(8,128)(2,1)S(1)}, u32[]{:S(2)}, u32[]{:S(2)}) collective-permute-start(bf16[64,256]{1,0:T(8,128)(2,1)S(1)} %get-tuple-element.54), channel_id=1, source_target_pairs={{0,28},{4,0},{8,4},{12,8},{16,12},{20,16},{24,20},{28,24},{1,29},{... | collective-permute-start | bytes 98312 | tf_op jit(solution)/shard_map/ppermute | solution.py:30
  27.0 6.4 %collective-permute-done.14.refs_3_.refs_18_ = bf16[64,256]{1,0:T(8,128)(2,1)S(1)} collective-permute-done((bf16[64,256]{1,0:T(8,128)(2,1)S(1)}, bf16[64,256]{1,0:T(8,128)(2,1)S(1)}, u32[]{:S(2)}, u32[]{:S(2)}) %collective-permute-start.14) | collective-permute-done | bytes 32800 | tf_op jit(solution)/shard_map/ppermute | solution.py:30
  33.3 0.0 collective-permute-done.13.refs_2_.refs_14_
  33.4 0.1 add_chunk0_step2.1
  33.4 0.2 collective-permute-start.15
  33.7 0.0 collective-permute-done.9.refs_2_.refs_8_
  33.7 0.1 add_chunk1_step2.1
  33.8 1.8 %collective-permute-start.10 = (bf16[2,2,192,128]{3,2,1,0:T(8,128)(2,1)S(1)}, bf16[2,2,192,128]{3,2,1,0:T(8,128)(2,1)S(1)}, u32[]{:S(2)}, u32[]{:S(2)}) collective-permute-start(bf16[2,2,192,128]{3,2,1,0:T(8,128)(2,1)S(1)} %add_chunk1_step2.1), channel_id=1, source_target_pairs={{0,2},{1,3},{2,0},{3,1},{4,6},{5,7},{6,4},{7,5},{8,10},{9,11},{10,... | collective-permute-start | bytes 589832 | tf_op jit(solution)/shard_map/ppermute | solution.py:486
  35.6 0.0 collective-permute-done.4.refs_2_
  35.6 0.1 add_chunk2_step2.1
  35.7 1.2 %collective-permute-start.5 = (bf16[2,2,192,128]{3,2,1,0:T(8,128)(2,1)S(1)}, bf16[2,2,192,128]{3,2,1,0:T(8,128)(2,1)S(1)}, u32[]{:S(2)}, u32[]{:S(2)}) collective-permute-start(bf16[2,2,192,128]{3,2,1,0:T(8,128)(2,1)S(1)} %add_chunk2_step2.1), channel_id=1, source_target_pairs={{0,4},{1,5},{2,6},{3,7},{4,0},{5,1},{6,2},{7,3},{8,12},{9,13},{10,... | collective-permute-start | bytes 589832 | tf_op jit(solution)/shard_map/ppermute | solution.py:486
  36.9 3.4 %collective-permute-done.15.refs_3_.refs_15_ = bf16[2,2,208,128]{3,2,1,0:T(8,128)(2,1)S(1)} collective-permute-done((bf16[2,2,208,128]{3,2,1,0:T(8,128)(2,1)S(1)}, bf16[2,2,208,128]{3,2,1,0:T(8,128)(2,1)S(1)}, u32[]{:S(2)}, u32[]{:S(2)}) %collective-permute-start.15) | collective-permute-done | bytes 213024 | tf_op jit(solution)/shard_map/ppermute | solution.py:486
  40.3 0.1 add_chunk0_step3.1
  40.4 2.0 %collective-permute-start.16 = (bf16[2,208,128]{2,1,0:T(8,128)(2,1)S(1)}, bf16[2,208,128]{2,1,0:T(8,128)(2,1)S(1)}, u32[]{:S(2)}, u32[]{:S(2)}) collective-permute-start(bf16[2,208,128]{2,1,0:T(8,128)(2,1)S(1)} %add_chunk0_step3.1), channel_id=1, source_target_pairs={{0,2},{1,3},{2,0},{3,1},{4,6},{5,7},{6,4},{7,5},{8,10},{9,11},{10,... | collective-permute-start | bytes 319496 | tf_op jit(solution)/shard_map/ppermute | solution.py:486
  42.4 0.0 collective-permute-done.10.refs_3_.refs_9_
  42.4 0.1 add_chunk1_step3.1
  42.4 0.7 %collective-permute-start.11 = (bf16[2,192,128]{2,1,0:T(8,128)(2,1)S(1)}, bf16[2,192,128]{2,1,0:T(8,128)(2,1)S(1)}, u32[]{:S(2)}, u32[]{:S(2)}) collective-permute-start(bf16[2,192,128]{2,1,0:T(8,128)(2,1)S(1)} %add_chunk1_step3.1), channel_id=1, source_target_pairs={{0,4},{1,5},{2,6},{3,7},{4,0},{5,1},{6,2},{7,3},{8,12},{9,13},{10,... | collective-permute-start | bytes 294920 | tf_op jit(solution)/shard_map/ppermute | solution.py:486
  43.1 0.0 collective-permute-done.5.refs_3_
  43.1 0.1 add_chunk2_step3.1
  43.2 0.7 %collective-permute-start.6 = (bf16[2,192,128]{2,1,0:T(8,128)(2,1)S(1)}, bf16[2,192,128]{2,1,0:T(8,128)(2,1)S(1)}, u32[]{:S(2)}, u32[]{:S(2)}) collective-permute-start(bf16[2,192,128]{2,1,0:T(8,128)(2,1)S(1)} %add_chunk2_step3.1), channel_id=1, source_target_pairs={{0,8},{1,9},{2,10},{3,11},{4,12},{5,13},{6,14},{7,15},{8,0},{9,1},... | collective-permute-start | bytes 294920 | tf_op jit(solution)/shard_map/ppermute | solution.py:486
  43.8 1.3 %collective-permute-done.16.refs_4_.refs_16_ = bf16[2,208,128]{2,1,0:T(8,128)(2,1)S(1)} collective-permute-done((bf16[2,208,128]{2,1,0:T(8,128)(2,1)S(1)}, bf16[2,208,128]{2,1,0:T(8,128)(2,1)S(1)}, u32[]{:S(2)}, u32[]{:S(2)}) %collective-permute-start.16) | collective-permute-done | bytes 106528 | tf_op jit(solution)/shard_map/ppermute | solution.py:486
  45.2 0.1 add_chunk0_step4.1
  45.2 1.2 %collective-permute-start.17 = (bf16[208,128]{1,0:T(8,128)(2,1)S(1)}, bf16[208,128]{1,0:T(8,128)(2,1)S(1)}, u32[]{:S(2)}, u32[]{:S(2)}) collective-permute-start(bf16[208,128]{1,0:T(8,128)(2,1)S(1)} %add_chunk0_step4.1), channel_id=1, source_target_pairs={{0,16},{1,17},{2,18},{3,19},{4,20},{5,21},{6,22},{7,23},{8,24},{9,... | collective-permute-start | bytes 159752 | tf_op jit(solution)/shard_map/ppermute | solution.py:486
  46.5 0.6 %collective-permute-done.11.refs_4_.refs_10_ = bf16[2,192,128]{2,1,0:T(8,128)(2,1)S(1)} collective-permute-done((bf16[2,192,128]{2,1,0:T(8,128)(2,1)S(1)}, bf16[2,192,128]{2,1,0:T(8,128)(2,1)S(1)}, u32[]{:S(2)}, u32[]{:S(2)}) %collective-permute-start.11) | collective-permute-done | bytes 98336 | tf_op jit(solution)/shard_map/ppermute | solution.py:486
  47.1 1.2 %collective-permute-start.12 = (bf16[192,128]{1,0:T(8,128)(2,1)S(1)}, bf16[192,128]{1,0:T(8,128)(2,1)S(1)}, u32[]{:S(2)}, u32[]{:S(2)}) collective-permute-start(bf16[192,128]{1,0:T(8,128)(2,1)S(1)} %add_chunk1_step4.1), channel_id=1, source_target_pairs={{0,16},{1,17},{2,18},{3,19},{4,20},{5,21},{6,22},{7,23},{8,24},{9,... | collective-permute-start | bytes 147464 | tf_op jit(solution)/shard_map/ppermute | solution.py:486
  48.3 0.0 collective-permute-done.6.refs_4_
  48.4 1.9 %collective-permute-start.7 = (bf16[192,128]{1,0:T(8,128)(2,1)S(1)}, bf16[192,128]{1,0:T(8,128)(2,1)S(1)}, u32[]{:S(2)}, u32[]{:S(2)}) collective-permute-start(bf16[192,128]{1,0:T(8,128)(2,1)S(1)} %add_chunk2_step4.1), channel_id=1, source_target_pairs={{0,16},{1,17},{2,18},{3,19},{4,20},{5,21},{6,22},{7,23},{8,24},{9,... | collective-permute-start | bytes 147464 | tf_op jit(solution)/shard_map/ppermute | solution.py:486
  50.2 2.5 %collective-permute-done.12.refs_11_ = bf16[192,128]{1,0:T(8,128)(2,1)S(1)} collective-permute-done((bf16[192,128]{1,0:T(8,128)(2,1)S(1)}, bf16[192,128]{1,0:T(8,128)(2,1)S(1)}, u32[]{:S(2)}, u32[]{:S(2)}) %collective-permute-start.12) | collective-permute-done | bytes 49184 | tf_op jit(solution)/shard_map/ppermute | solution.py:486
  52.7 0.0 collective-permute-done.17.refs_17_
  52.7 0.7 %collective-permute-done.7.refs_5_ = bf16[192,128]{1,0:T(8,128)(2,1)S(1)} collective-permute-done((bf16[192,128]{1,0:T(8,128)(2,1)S(1)}, bf16[192,128]{1,0:T(8,128)(2,1)S(1)}, u32[]{:S(2)}, u32[]{:S(2)}) %collective-permute-start.7) | collective-permute-done | bytes 49184 | tf_op jit(solution)/shard_map/ppermute | solution.py:486
  53.4 1.0 %scale_all.1 = (f32[512,256]{1,0:T(8,128)}, f32[6,64,128]{2,1,0:T(8,128)}, f32[6,32,128]{2,1,0:T(8,128)}) custom-call(bf16[2,2,2,2,192,128]{5,4,3,2,1,0:T(8,128)(2,1)S(1)} %get-tuple-element.48.refs_0_, bf16[2,2,2,2,192,128]{5,4,3,2,1,0:T(8,128)(2,1)S(1)} %collective-permute-done.3.refs_1_, bf16[2,2,2,192,128]{4,3,2,1,0:T(8,128)(2,1)S(1)} %collective-permute-done.4.refs_2_, ...), custom_call_target="tpu_custom_call" | custom-call | tf_op jit(solution)/shard_map/scale_all/pallas_call | solution.py:522
  (2 shorter events, 0.1 us)
Async XLA Ops:
  1.6 8.7 %collective-permute-start = (bf16[128,256]{1,0:T(8,128)(2,1)S(1)}, bf16[128,256]{1,0:T(8,128)(2,1)S(1)}, u32[]{:S(2)}, u32[]{:S(2)}) collective-permute-start(bf16[128,256]{1,0:T(8,128)(2,1)S(1)} %get-tuple-element.31._), channel_id=1, source_target_pairs={{0,4},{4,8},{8,12},{12,16},{16,20},{20,24},{24,28},{28,0},{1,5},{5... | collective-permute-start | bytes 196616 | tf_op jit(solution)/shard_map/ppermute | solution.py:30
  4.6 9.3 %collective-permute-start.1 = (bf16[128,256]{1,0:T(8,128)(2,1)S(1)}, bf16[128,256]{1,0:T(8,128)(2,1)S(1)}, u32[]{:S(2)}, u32[]{:S(2)}) collective-permute-start(bf16[128,256]{1,0:T(8,128)(2,1)S(1)} %get-tuple-element.39), channel_id=1, source_target_pairs={{0,4},{4,8},{8,12},{12,16},{16,20},{20,24},{24,28},{28,0},{1,5},{5... | collective-permute-start | bytes 196616 | tf_op jit(solution)/shard_map/ppermute | solution.py:30
  15.9 2.5 %collective-permute-start.2 = (bf16[2,2,2,2,208,128]{5,4,3,2,1,0:T(8,128)(2,1)S(1)}, bf16[2,2,2,2,208,128]{5,4,3,2,1,0:T(8,128)(2,1)S(1)}, u32[]{:S(2)}, u32[]{:S(2)}) collective-permute-start(bf16[2,2,2,2,208,128]{5,4,3,2,1,0:T(8,128)(2,1)S(1)} %get-tuple-element.47), channel_id=1, source_target_pairs={{0,1},{1,0},{2,3},{3,2},{4,5},{5,4},{6,7},{7,6},{8,9},{9,8},{10,11... | collective-permute-start | bytes 2555912 | tf_op jit(solution)/shard_map/ppermute | solution.py:486
  17.9 2.6 %collective-permute-start.8 = (bf16[2,2,2,2,192,128]{5,4,3,2,1,0:T(8,128)(2,1)S(1)}, bf16[2,2,2,2,192,128]{5,4,3,2,1,0:T(8,128)(2,1)S(1)}, u32[]{:S(2)}, u32[]{:S(2)}) collective-permute-start(bf16[2,2,2,2,192,128]{5,4,3,2,1,0:T(8,128)(2,1)S(1)} %get-tuple-element.51), channel_id=1, source_target_pairs={{0,1},{1,0},{2,3},{3,2},{4,5},{5,4},{6,7},{7,6},{8,9},{9,8},{10,11... | collective-permute-start | bytes 2359304 | tf_op jit(solution)/shard_map/ppermute | solution.py:486
  20.3 2.4 %collective-permute-start.3 = (bf16[2,2,2,2,192,128]{5,4,3,2,1,0:T(8,128)(2,1)S(1)}, bf16[2,2,2,2,192,128]{5,4,3,2,1,0:T(8,128)(2,1)S(1)}, u32[]{:S(2)}, u32[]{:S(2)}) collective-permute-start(bf16[2,2,2,2,192,128]{5,4,3,2,1,0:T(8,128)(2,1)S(1)} %get-tuple-element.49), channel_id=1, source_target_pairs={{0,1},{1,0},{2,3},{3,2},{4,5},{5,4},{6,7},{7,6},{8,9},{9,8},{10,11... | collective-permute-start | bytes 2359304 | tf_op jit(solution)/shard_map/ppermute | solution.py:486
  20.4 12.9 %collective-permute-start.13 = (bf16[2,2,2,208,128]{4,3,2,1,0:T(8,128)(2,1)S(1)}, bf16[2,2,2,208,128]{4,3,2,1,0:T(8,128)(2,1)S(1)}, u32[]{:S(2)}, u32[]{:S(2)}) collective-permute-start(bf16[2,2,2,208,128]{4,3,2,1,0:T(8,128)(2,1)S(1)} %add_chunk0_step1.1.rest_2_), channel_id=1, source_target_pairs={{0,4},{1,5},{2,6},{3,7},{4,0},{5,1},{6,2},{7,3},{8,12},{9,13},{10,... | collective-permute-start | bytes 1277960 | tf_op jit(solution)/shard_map/ppermute | solution.py:486
  20.6 13.1 %collective-permute-start.9 = (bf16[2,2,2,192,128]{4,3,2,1,0:T(8,128)(2,1)S(1)}, bf16[2,2,2,192,128]{4,3,2,1,0:T(8,128)(2,1)S(1)}, u32[]{:S(2)}, u32[]{:S(2)}) collective-permute-start(bf16[2,2,2,192,128]{4,3,2,1,0:T(8,128)(2,1)S(1)} %add_chunk1_step1.1), channel_id=1, source_target_pairs={{0,8},{1,9},{2,10},{3,11},{4,12},{5,13},{6,14},{7,15},{8,0},{9,1},... | collective-permute-start | bytes 1179656 | tf_op jit(solution)/shard_map/ppermute | solution.py:486
  22.8 12.8 %collective-permute-start.4 = (bf16[2,2,2,192,128]{4,3,2,1,0:T(8,128)(2,1)S(1)}, bf16[2,2,2,192,128]{4,3,2,1,0:T(8,128)(2,1)S(1)}, u32[]{:S(2)}, u32[]{:S(2)}) collective-permute-start(bf16[2,2,2,192,128]{4,3,2,1,0:T(8,128)(2,1)S(1)} %add_chunk2_step1.1), channel_id=1, source_target_pairs={{0,2},{1,3},{2,0},{3,1},{4,6},{5,7},{6,4},{7,5},{8,10},{9,11},{10,... | collective-permute-start | bytes 1179656 | tf_op jit(solution)/shard_map/ppermute | solution.py:486
  25.2 8.1 %collective-permute-start.14 = (bf16[64,256]{1,0:T(8,128)(2,1)S(1)}, bf16[64,256]{1,0:T(8,128)(2,1)S(1)}, u32[]{:S(2)}, u32[]{:S(2)}) collective-permute-start(bf16[64,256]{1,0:T(8,128)(2,1)S(1)} %get-tuple-element.54), channel_id=1, source_target_pairs={{0,28},{4,0},{8,4},{12,8},{16,12},{20,16},{24,20},{28,24},{1,29},{... | collective-permute-start | bytes 98312 | tf_op jit(solution)/shard_map/ppermute | solution.py:30
  33.4 6.9 %collective-permute-start.15 = (bf16[2,2,208,128]{3,2,1,0:T(8,128)(2,1)S(1)}, bf16[2,2,208,128]{3,2,1,0:T(8,128)(2,1)S(1)}, u32[]{:S(2)}, u32[]{:S(2)}) collective-permute-start(bf16[2,2,208,128]{3,2,1,0:T(8,128)(2,1)S(1)} %add_chunk0_step2.1), channel_id=1, source_target_pairs={{0,8},{1,9},{2,10},{3,11},{4,12},{5,13},{6,14},{7,15},{8,0},{9,1},... | collective-permute-start | bytes 638984 | tf_op jit(solution)/shard_map/ppermute | solution.py:486
  33.8 8.6 %collective-permute-start.10 = (bf16[2,2,192,128]{3,2,1,0:T(8,128)(2,1)S(1)}, bf16[2,2,192,128]{3,2,1,0:T(8,128)(2,1)S(1)}, u32[]{:S(2)}, u32[]{:S(2)}) collective-permute-start(bf16[2,2,192,128]{3,2,1,0:T(8,128)(2,1)S(1)} %add_chunk1_step2.1), channel_id=1, source_target_pairs={{0,2},{1,3},{2,0},{3,1},{4,6},{5,7},{6,4},{7,5},{8,10},{9,11},{10,... | collective-permute-start | bytes 589832 | tf_op jit(solution)/shard_map/ppermute | solution.py:486
  35.7 7.4 %collective-permute-start.5 = (bf16[2,2,192,128]{3,2,1,0:T(8,128)(2,1)S(1)}, bf16[2,2,192,128]{3,2,1,0:T(8,128)(2,1)S(1)}, u32[]{:S(2)}, u32[]{:S(2)}) collective-permute-start(bf16[2,2,192,128]{3,2,1,0:T(8,128)(2,1)S(1)} %add_chunk2_step2.1), channel_id=1, source_target_pairs={{0,4},{1,5},{2,6},{3,7},{4,0},{5,1},{6,2},{7,3},{8,12},{9,13},{10,... | collective-permute-start | bytes 589832 | tf_op jit(solution)/shard_map/ppermute | solution.py:486
  40.4 4.8 %collective-permute-start.16 = (bf16[2,208,128]{2,1,0:T(8,128)(2,1)S(1)}, bf16[2,208,128]{2,1,0:T(8,128)(2,1)S(1)}, u32[]{:S(2)}, u32[]{:S(2)}) collective-permute-start(bf16[2,208,128]{2,1,0:T(8,128)(2,1)S(1)} %add_chunk0_step3.1), channel_id=1, source_target_pairs={{0,2},{1,3},{2,0},{3,1},{4,6},{5,7},{6,4},{7,5},{8,10},{9,11},{10,... | collective-permute-start | bytes 319496 | tf_op jit(solution)/shard_map/ppermute | solution.py:486
  42.4 4.7 %collective-permute-start.11 = (bf16[2,192,128]{2,1,0:T(8,128)(2,1)S(1)}, bf16[2,192,128]{2,1,0:T(8,128)(2,1)S(1)}, u32[]{:S(2)}, u32[]{:S(2)}) collective-permute-start(bf16[2,192,128]{2,1,0:T(8,128)(2,1)S(1)} %add_chunk1_step3.1), channel_id=1, source_target_pairs={{0,4},{1,5},{2,6},{3,7},{4,0},{5,1},{6,2},{7,3},{8,12},{9,13},{10,... | collective-permute-start | bytes 294920 | tf_op jit(solution)/shard_map/ppermute | solution.py:486
  43.2 5.2 %collective-permute-start.6 = (bf16[2,192,128]{2,1,0:T(8,128)(2,1)S(1)}, bf16[2,192,128]{2,1,0:T(8,128)(2,1)S(1)}, u32[]{:S(2)}, u32[]{:S(2)}) collective-permute-start(bf16[2,192,128]{2,1,0:T(8,128)(2,1)S(1)} %add_chunk2_step3.1), channel_id=1, source_target_pairs={{0,8},{1,9},{2,10},{3,11},{4,12},{5,13},{6,14},{7,15},{8,0},{9,1},... | collective-permute-start | bytes 294920 | tf_op jit(solution)/shard_map/ppermute | solution.py:486
  45.2 7.5 %collective-permute-start.17 = (bf16[208,128]{1,0:T(8,128)(2,1)S(1)}, bf16[208,128]{1,0:T(8,128)(2,1)S(1)}, u32[]{:S(2)}, u32[]{:S(2)}) collective-permute-start(bf16[208,128]{1,0:T(8,128)(2,1)S(1)} %add_chunk0_step4.1), channel_id=1, source_target_pairs={{0,16},{1,17},{2,18},{3,19},{4,20},{5,21},{6,22},{7,23},{8,24},{9,... | collective-permute-start | bytes 159752 | tf_op jit(solution)/shard_map/ppermute | solution.py:486
  47.1 5.6 %collective-permute-start.12 = (bf16[192,128]{1,0:T(8,128)(2,1)S(1)}, bf16[192,128]{1,0:T(8,128)(2,1)S(1)}, u32[]{:S(2)}, u32[]{:S(2)}) collective-permute-start(bf16[192,128]{1,0:T(8,128)(2,1)S(1)} %add_chunk1_step4.1), channel_id=1, source_target_pairs={{0,16},{1,17},{2,18},{3,19},{4,20},{5,21},{6,22},{7,23},{8,24},{9,... | collective-permute-start | bytes 147464 | tf_op jit(solution)/shard_map/ppermute | solution.py:486
  48.4 5.1 %collective-permute-start.7 = (bf16[192,128]{1,0:T(8,128)(2,1)S(1)}, bf16[192,128]{1,0:T(8,128)(2,1)S(1)}, u32[]{:S(2)}, u32[]{:S(2)}) collective-permute-start(bf16[192,128]{1,0:T(8,128)(2,1)S(1)} %add_chunk2_step4.1), channel_id=1, source_target_pairs={{0,16},{1,17},{2,18},{3,19},{4,20},{5,21},{6,22},{7,23},{8,24},{9,... | collective-permute-start | bytes 147464 | tf_op jit(solution)/shard_map/ppermute | solution.py:486
